TPU v7x, 32 devices: a whole 2x2x4 slice. The times are simulated.
32 devices in a mesh: gx: 2 (over x), gy: 4 (over y, core), gz: 4 (over z).
Axes of the slice: x: 2, y: 2, z: 4, core: 2. Of those that a mesh axis runs over, the one named last changes fastest.
Arguments:
- right_side: float32 [48, 128, 512], P('gx', 'gy', 'gz'), may hold values from -6 to 6
- conductance: float32 [48, 128, 512], P('gx', 'gy', 'gz'), may hold values from 0.05 to 10
- absorption: float32 [48, 128, 512], P('gx', 'gy', 'gz'), may hold values from 0.002 to 0.02
- block_agg: int32 [24, 64, 256], P('gx', 'gy', 'gz'), may hold values from 0 to 127, as said below
Outputs:
- solution: float32 [48, 128, 512], P('gx', 'gy', 'gz')
Inputs may be any that keep to these rules, and one draw needn't show every extreme that they name: `block_agg`: aggregates never leave their brick; in every brick each number 0 to 127 names at least one block.
All inputs are finite; a program needn't handle non-finite values.
Results may differ from a plain program's by a relative error of at most 0.0003.
Values sent between devices are 32-bit elements; how exact they have to be, the bound alone decides.
No kernel may reach another device: no remote copies, remote signals or barrier semaphores. Data moves between devices by JAX's collectives and lax.ppermute only.
A program may use at most 128 MiB of HBM per device.

v0:
```python
import jax
import jax.numpy as jnp
from jax import lax
from jax.sharding import PartitionSpec as P

AGG = 128
POST = 4
KC = 8


OMEGA_FINE = 0.8
OMEGA_COARSE = 0.7


def padded_2(cells, sides, width):
    for axis, dim in sides:
        count = lax.axis_size(axis)
        ends = count - 1
        head = lax.slice_in_dim(cells, 0, width, axis=dim)
        tail = lax.slice_in_dim(cells, cells.shape[dim] - width, cells.shape[dim], axis=dim)
        cells = jnp.concatenate(
            [
                lax.ppermute(tail, axis, [(i, (i + 1) % count) for i in range(ends)]),
                cells,
                lax.ppermute(head, axis, [((i + 1) % count, i) for i in range(ends)]),
            ],
            axis=dim,
        )
    return cells


def harmonic(one_side, other_side):
    summed = one_side + other_side
    return 2.0 * (one_side * other_side) / jnp.where(summed > 0.0, summed, 1.0)


def face_weights(cond_pad):
    face_x = harmonic(cond_pad[:-1, 1:-1, 1:-1], cond_pad[1:, 1:-1, 1:-1])
    face_y = harmonic(cond_pad[1:-1, :-1, 1:-1], cond_pad[1:-1, 1:, 1:-1])
    face_z = harmonic(cond_pad[1:-1, 1:-1, :-1], cond_pad[1:-1, 1:-1, 1:])
    return (face_x, face_y, face_z)


def diagonal_of(absorb, face_x, face_y, face_z):
    return (
        absorb
        + face_x[:-1]
        + face_x[1:]
        + face_y[:, :-1]
        + face_y[:, 1:]
        + face_z[:, :, :-1]
        + face_z[:, :, 1:]
    )


def stencil(padded, cell_diag, face_x, face_y, face_z):
    centre = padded[1:-1, 1:-1, 1:-1]
    beside = face_x[1:] * padded[2:, 1:-1, 1:-1] + face_x[:-1] * padded[:-2, 1:-1, 1:-1]
    beside = (
        beside + face_y[:, 1:] * padded[1:-1, 2:, 1:-1] + face_y[:, :-1] * padded[1:-1, :-2, 1:-1]
    )
    beside = (
        beside
        + face_z[:, :, 1:] * padded[1:-1, 1:-1, 2:]
        + face_z[:, :, :-1] * padded[1:-1, 1:-1, :-2]
    )
    return cell_diag * centre - beside


def fine_image(values, cell_diag, face_x, face_y, face_z):
    padded = padded_2(values, (("gx", 0), ("gy", 1), ("gz", 2)), 1)
    return stencil(padded, cell_diag, face_x, face_y, face_z)


def block_sum(values):
    size_a, size_b, size_c = values.shape
    return values.reshape(size_a // 2, 2, size_b // 2, 2, size_c // 2, 2).sum(axis=(1, 3, 5))


def upsample(values):
    size_a, size_b, size_c = values.shape
    spread = jnp.broadcast_to(values[:, None, :, None, :, None], (size_a, 2, size_b, 2, size_c, 2))
    return spread.reshape(2 * size_a, 2 * size_b, 2 * size_c)


def indicator(labels):
    return (labels[..., None] == jnp.arange(AGG, dtype=jnp.int32)).astype(jnp.float32)


def coupling(own_labels, peer_labels, weights):
    return -jnp.einsum(
        "abi,abj->ij",
        indicator(own_labels),
        weights[:, :, None] * indicator(peer_labels),
        precision=lax.Precision.HIGHEST,
    )


def body(right_side, conductance, absorption, block_agg):
    cond_wide = padded_2(conductance, (("gx", 0), ("gy", 1), ("gz", 2)), 3)
    cond_pad = cond_wide[2:-2, 2:-2, 2:-2]
    face_x, face_y, face_z = face_weights(cond_pad)
    cell_diag = diagonal_of(absorption, face_x, face_y, face_z)
    iterate = OMEGA_FINE * right_side / cell_diag
    iterate = (
        iterate
        + OMEGA_FINE
        * (right_side - fine_image(iterate, cell_diag, face_x, face_y, face_z))
        / cell_diag
    )
    residual = right_side - fine_image(iterate, cell_diag, face_x, face_y, face_z)
    blocks_x, blocks_y, blocks_z = block_agg.shape
    block_x = face_x[0::2].reshape(blocks_x + 1, blocks_y, 2, blocks_z, 2).sum(axis=(2, 4))
    block_y = face_y[:, 0::2].reshape(blocks_x, 2, blocks_y + 1, blocks_z, 2).sum(axis=(1, 4))
    block_z = face_z[:, :, 0::2].reshape(blocks_x, 2, blocks_y, 2, blocks_z + 1).sum(axis=(1, 3))
    block_diag = (
        block_sum(absorption)
        + block_x[:-1]
        + block_x[1:]
        + block_y[:, :-1]
        + block_y[:, 1:]
        + block_z[:, :, :-1]
        + block_z[:, :, 1:]
    )
    inner_x = block_x.at[0].set(0.0).at[-1].set(0.0)
    inner_y = block_y.at[:, 0].set(0.0).at[:, -1].set(0.0)
    inner_z = block_z.at[:, :, 0].set(0.0).at[:, :, -1].set(0.0)

    def tile_step(slab_no, running):
        this_slab = indicator(block_agg[slab_no])
        prev_slab = indicator(block_agg[jnp.maximum(slab_no - 1, 0)])
        next_slab = indicator(block_agg[jnp.minimum(slab_no + 1, blocks_x - 1)])
        applied = block_diag[slab_no][:, :, None] * this_slab
        applied = (
            applied
            - inner_x[slab_no][:, :, None] * prev_slab
            - inner_x[slab_no + 1][:, :, None] * next_slab
        )
        shift_y = jnp.pad(this_slab, ((1, 1), (0, 0), (0, 0)))
        applied = (
            applied
            - inner_y[slab_no, 1:][:, :, None] * shift_y[2:]
            - inner_y[slab_no, :-1][:, :, None] * shift_y[:-2]
        )
        shift_z = jnp.pad(this_slab, ((0, 0), (1, 1), (0, 0)))
        applied = (
            applied
            - inner_z[slab_no, :, 1:][:, :, None] * shift_z[:, 2:]
            - inner_z[slab_no, :, :-1][:, :, None] * shift_z[:, :-2]
        )
        return running + jnp.einsum(
            "abi,abj->ij", this_slab, applied, precision=lax.Precision.HIGHEST
        )

    own_tile = lax.fori_loop(0, blocks_x, tile_step, jnp.zeros((AGG, AGG), jnp.float32))
    ids_pad = padded_2(block_agg, (("gx", 0), ("gy", 1), ("gz", 2)), 1)
    face_tiles = jnp.stack(
        [
            coupling(block_agg[0], ids_pad[0, 1:-1, 1:-1], block_x[0]),
            coupling(block_agg[-1], ids_pad[-1, 1:-1, 1:-1], block_x[-1]),
            coupling(block_agg[:, 0], ids_pad[1:-1, 0, 1:-1], block_y[:, 0]),
            coupling(block_agg[:, -1], ids_pad[1:-1, -1, 1:-1], block_y[:, -1]),
            coupling(block_agg[:, :, 0], ids_pad[1:-1, 1:-1, 0], block_z[:, :, 0]),
            coupling(block_agg[:, :, -1], ids_pad[1:-1, 1:-1, -1], block_z[:, :, -1]),
        ]
    )
    block_res = block_sum(residual)

    def restrict_step(slab_no, running):
        return running + jnp.einsum(
            "abi,ab->i",
            indicator(block_agg[slab_no]),
            block_res[slab_no],
            precision=lax.Precision.HIGHEST,
        )

    coarse_rhs = lax.fori_loop(0, blocks_x, restrict_step, jnp.zeros((AGG,), jnp.float32))
    coarse_diag = jnp.diagonal(own_tile)
    correction = OMEGA_COARSE * coarse_rhs / coarse_diag
    for turn_no in range(KC - 1):
        padded = padded_2(correction[None, None, None], (("gx", 0), ("gy", 1), ("gz", 2)), 1)
        beside = jnp.stack(
            [
                padded[0, 1, 1],
                padded[2, 1, 1],
                padded[1, 0, 1],
                padded[1, 2, 1],
                padded[1, 1, 0],
                padded[1, 1, 2],
            ]
        )
        applied = jnp.dot(own_tile, correction, precision=lax.Precision.HIGHEST)
        applied = applied + jnp.einsum(
            "fij,fj->i", face_tiles, beside, precision=lax.Precision.HIGHEST
        )
        correction = correction + OMEGA_COARSE * (coarse_rhs - applied) / coarse_diag

    def lift_slab(slab_no):
        return jnp.dot(indicator(block_agg[slab_no]), correction, precision=lax.Precision.HIGHEST)

    block_corr = lax.map(lift_slab, jnp.arange(blocks_x, dtype=jnp.int32))
    iterate = iterate + upsample(block_corr)
    stacked = padded_2(jnp.stack([absorption, right_side]), (("gx", 1), ("gy", 2), ("gz", 3)), 2)
    absorb_wide = stacked[0]
    right_wide = stacked[1]
    wide_x, wide_y, wide_z = face_weights(cond_wide)
    diag_wide = diagonal_of(absorb_wide, wide_x, wide_y, wide_z)
    safe_diag = jnp.where(diag_wide > 0.0, diag_wide, 1.0)
    for pair_no in range(POST // 2):
        wide_iter = padded_2(iterate, (("gx", 0), ("gy", 1), ("gz", 2)), 2)
        for inner_no in range(2):
            applied = stencil(jnp.pad(wide_iter, 1), diag_wide, wide_x, wide_y, wide_z)
            wide_iter = wide_iter + OMEGA_FINE * (right_wide - applied) / safe_diag
        iterate = wide_iter[2:-2, 2:-2, 2:-2]
    return iterate


def solution(mesh):
    in_specs = (P("gx", "gy", "gz"), P("gx", "gy", "gz"), P("gx", "gy", "gz"), P("gx", "gy", "gz"))
    out_specs = P("gx", "gy", "gz")
    return jax.shard_map(body, mesh=mesh, in_specs=in_specs, out_specs=out_specs, check_vma=False)
```

profile of v0, /device:TPU:25, one launch (start us, length us, event | category | flops | bytes accessed | tf_op | source)
XLA Modules:
  0.0 629.1 jit_solution(17433992715146352944)
XLA Ops:
  14.7 5.7 collective-permute-start.20
  22.3 26.5 %reshape.194 = f32[12,2,16,2,64,2]{5,4,3,2,1,0:T(8,128)} reshape(f32[24,32,128]{2,1,0:T(8,128)S(1)} %copy-done.4) | data formatting | bytes 786432 | tf_op jit(solution)/shard_map/reshape | solution.py:77
  50.4 9.4 %reduce_sum.46 = f32[12,16,64]{2,1,0:T(8,128)S(1)} reduce(f32[12,2,16,2,64,2]{5,4,3,2,1,0:T(8,128)} %reshape.194, f32[]{:T(128)} %constant.302.clone.1), dimensions={1,3,5}, to_apply=%region_3.4 | reduce | flops 86016 | bytes 442372 | tf_op jit(solution)/shard_map/reduce_sum | solution.py:77
  72.2 4.8 collective-permute-start.2
  92.1 5.2 collective-permute-start.5
  117.4 5.0 collective-permute-start.9
  134.5 8.2 %slice.754 = f32[24,32,65]{2,1,0:T(8,128)S(1)} slice(f32[24,32,129]{2,1,0:T(8,128)S(1)} %fusion.120), slice={[0:24:1], [0:32:1], [0:129:2]} | slice | bytes 399360 | tf_op jit(solution)/shard_map/slice | solution.py:115
  170.1 4.6 collective-permute-start.15
  174.7 48.5 %while.48 = (s32[]{:T(128)}, f32[128,128]{1,0:T(8,128)S(1)}, s32[12,16,64]{2,1,0:T(8,128)S(1)}, f32[12,16,64]{2,1,0:T(8,128)}, f32[13,16,64]{2,1,0:T(8,128)}, /*...) while((s32[]{:T(128)}, f32[128,128]{1,0:T(8,128)S(1)}, ...), condition=%wide.region_8.9_spmd.clone, body=%wide.region_7.8_spmd.clone.sunk | while | flops 203849744 | bytes 1356047 | solution.py:155
  238.4 27.3 %reshape.193 = f32[12,2,16,2,64,2]{5,4,3,2,1,0:T(8,128)} reshape(f32[24,32,128]{2,1,0:T(8,128)} %fusion.131) | data formatting | bytes 786432 | tf_op jit(solution)/shard_map/reshape | solution.py:77
  265.7 9.4 %reduce_sum.45 = f32[12,16,64]{2,1,0:T(8,128)S(1)} reduce(f32[12,2,16,2,64,2]{5,4,3,2,1,0:T(8,128)} %reshape.193, f32[]{:T(128)} %constant.302.clone.1), dimensions={1,3,5}, to_apply=%region_0.1 | reduce | flops 86016 | bytes 442372 | tf_op jit(solution)/shard_map/reduce_sum | solution.py:77
  275.1 5.3 while.47
  288.2 5.2 collective-permute-start.26
  366.1 4.8 collective-permute-start.44
  388.7 4.8 collective-permute-start.50
  410.7 4.8 collective-permute-start.56
  433.4 4.8 collective-permute-start.62
  449.6 47.7 %while.46 = (s32[]{:T(128)}, f32[12,16,64]{2,1,0:T(8,128)}, s32[12]{0:T(128)S(1)}, s32[12,16,64]{2,1,0:T(8,128)S(1)}, f32[128]{0:T(128)S(1)}, /*index=5*/s32[]{:T(128)}, s32[]{:T(128)}, s32[]{:T(128)}) while((s32[]{:T(128)}, f32[12,16,64]{2,1,0:T(8,128)}, s32[12]{0:T(128)S(1)}, s32[12,16,64]{2,1,0:T(8,128)S(1)}, f32[128]{0:T(128)S(1)}, ...), condition=%wide.region_10.11_spmd, body=%wide.region_9.10_spmd.sunk | while | flops 1703941 | bytes 29831 | solution.py:201
  497.3 9.9 %broadcast_in_dim.106 = f32[12,2,16,2,64,2]{5,4,3,2,1,0:T(8,128)} broadcast(f32[12,16,64]{2,1,0:T(8,128)} %get-tuple-element.363), dimensions={0,2,4} | broadcast | bytes 442368 | tf_op jit(solution)/shard_map/broadcast_in_dim | solution.py:82
  507.2 18.4 %reshape.198 = f32[24,32,128]{2,1,0:T(8,128)S(1)} reshape(f32[12,2,16,2,64,2]{5,4,3,2,1,0:T(8,128)} %broadcast_in_dim.106) | data formatting | bytes 786432 | tf_op jit(solution)/shard_map/reshape | solution.py:83
  537.4 4.6 collective-permute-start.77
  563.3 4.6 collective-permute-start.71
  591.4 5.6 collective-permute-start.80
  608.7 4.6 collective-permute-start.83
  (581 shorter events, 424.0 us)
Async XLA Ops:
  0.9 67.2 %collective-permute-start = (f32[3,32,128]{2,1,0:T(8,128)S(1)}, f32[3,32,128]{2,1,0:T(8,128)S(1)}, u32[]{:S(2)}, u32[]{:S(2)}) collective-permute-start(f32[3,32,128]{2,1,0:T(8,128)S(1)} %get-tuple-element.528), channel_id=1, source_target_pairs={{0,16},{1,17},{2,18},{3,19},{4,20},{5,21},{6,22},{7,23},{8,24},{9,... | collective-permute-start | bytes 147464 | tf_op jit(solution)/shard_map/ppermute | solution.py:23
  4.0 64.1 %collective-permute-start.1 = (f32[3,32,128]{2,1,0:T(8,128)S(1)}, f32[3,32,128]{2,1,0:T(8,128)S(1)}, u32[]{:S(2)}, u32[]{:S(2)}) collective-permute-start(f32[3,32,128]{2,1,0:T(8,128)S(1)} %get-tuple-element.527), channel_id=1, source_target_pairs={{16,0},{17,1},{18,2},{19,3},{20,4},{21,5},{22,6},{23,7},{24,8},{25... | collective-permute-start | bytes 147464 | tf_op jit(solution)/shard_map/ppermute | solution.py:25
  14.7 45.1 %collective-permute-start.20 = (s32[14,1,64]{2,0,1:T(8,128)S(1)}, s32[14,1,64]{2,0,1:T(8,128)S(1)}, u32[]{:S(2)}, u32[]{:S(2)}) collective-permute-start(s32[14,1,64]{2,0,1:T(8,128)S(1)} %get-tuple-element.532), channel_id=1, source_target_pairs={{0,4},{4,8},{8,12},{1,5},{5,9},{9,13},{2,6},{6,10},{10,14},{3,7},{... | collective-permute-start | bytes 10760 | tf_op jit(solution)/shard_map/ppermute | solution.py:23
  20.4 39.4 %collective-permute-start.21 = (s32[14,1,64]{2,0,1:T(8,128)S(1)}, s32[14,1,64]{2,0,1:T(8,128)S(1)}, u32[]{:S(2)}, u32[]{:S(2)}) collective-permute-start(s32[14,1,64]{2,0,1:T(8,128)S(1)} %get-tuple-element.531), channel_id=1, source_target_pairs={{4,0},{8,4},{12,8},{5,1},{9,5},{13,9},{6,2},{10,6},{14,10},{7,3},{... | collective-permute-start | bytes 10760 | tf_op jit(solution)/shard_map/ppermute | solution.py:25
  72.2 14.5 %collective-permute-start.2 = (f32[30,3,128]{2,1,0:T(4,128)S(1)}, f32[30,3,128]{2,1,0:T(4,128)S(1)}, u32[]{:S(2)}, u32[]{:S(2)}) collective-permute-start(f32[30,3,128]{2,1,0:T(4,128)S(1)} %get-tuple-element.509), channel_id=1, source_target_pairs={{0,4},{4,8},{8,12},{1,5},{5,9},{9,13},{2,6},{6,10},{10,14},{3,7},{... | collective-permute-start | bytes 138248 | tf_op jit(solution)/shard_map/ppermute | solution.py:23
  89.4 14.4 %collective-permute-start.4 = (f32[30,38,3]{1,0,2:T(8,128)S(1)}, f32[30,38,3]{1,0,2:T(8,128)S(1)}, u32[]{:S(2)}, u32[]{:S(2)}) collective-permute-start(f32[30,38,3]{1,0,2:T(8,128)S(1)} %copy.84), channel_id=1, source_target_pairs={{0,1},{1,2},{2,3},{4,5},{5,6},{6,7},{8,9},{9,10},{10,11},{12,13},{... | collective-permute-start | bytes 41048 | tf_op jit(solution)/shard_map/ppermute | solution.py:23
  92.1 12.8 %collective-permute-start.5 = (f32[30,38,3]{1,0,2:T(8,128)S(1)}, f32[30,38,3]{1,0,2:T(8,128)S(1)}, u32[]{:S(2)}, u32[]{:S(2)}) collective-permute-start(f32[30,38,3]{1,0,2:T(8,128)S(1)} %copy.86), channel_id=1, source_target_pairs={{1,0},{2,1},{3,2},{5,4},{6,5},{7,6},{9,8},{10,9},{11,10},{13,12},{... | collective-permute-start | bytes 41048 | tf_op jit(solution)/shard_map/ppermute | solution.py:25
  115.4 27.5 %collective-permute-start.8 = (f32[26,1,128]{2,1,0:T(1,128)S(1)}, f32[26,1,128]{2,1,0:T(1,128)S(1)}, u32[]{:S(2)}, u32[]{:S(2)}) collective-permute-start(f32[26,1,128]{2,1,0:T(1,128)S(1)} %get-tuple-element.518), channel_id=1, source_target_pairs={{4,0},{8,4},{12,8},{5,1},{9,5},{13,9},{6,2},{10,6},{14,10},{7,3},{... | collective-permute-start | bytes 39944 | tf_op jit(solution)/shard_map/ppermute | solution.py:25
  117.4 25.6 %collective-permute-start.9 = (f32[26,1,128]{2,1,0:T(1,128)S(1)}, f32[26,1,128]{2,1,0:T(1,128)}, u32[]{:S(2)}, u32[]{:S(2)}) collective-permute-start(f32[26,1,128]{2,1,0:T(1,128)S(1)} %get-tuple-element.517), channel_id=1, source_target_pairs={{0,4},{4,8},{8,12},{1,5},{5,9},{9,13},{2,6},{6,10},{10,14},{3,7},{... | collective-permute-start | bytes 39944 | tf_op jit(solution)/shard_map/ppermute | solution.py:23
  168.2 55.0 %collective-permute-start.14 = (f32[26,1,128]{2,1,0:T(1,128)}, f32[26,1,128]{2,1,0:T(1,128)S(1)}, u32[]{:S(2)}, u32[]{:S(2)}) collective-permute-start(f32[26,1,128]{2,1,0:T(1,128)} %get-tuple-element.516), channel_id=1, source_target_pairs={{4,0},{8,4},{12,8},{5,1},{9,5},{13,9},{6,2},{10,6},{14,10},{7,3},{... | collective-permute-start | bytes 39944 | tf_op jit(solution)/shard_map/ppermute | solution.py:25
  170.1 53.1 %collective-permute-start.15 = (f32[26,1,128]{2,1,0:T(1,128)}, f32[26,1,128]{2,1,0:T(1,128)S(1)}, u32[]{:S(2)}, u32[]{:S(2)}) collective-permute-start(f32[26,1,128]{2,1,0:T(1,128)} %get-tuple-element.515), channel_id=1, source_target_pairs={{0,4},{4,8},{8,12},{1,5},{5,9},{9,13},{2,6},{6,10},{10,14},{3,7},{... | collective-permute-start | bytes 39944 | tf_op jit(solution)/shard_map/ppermute | solution.py:23
  308.7 26.8 %collective-permute-start.72 = (f32[2,2,32,128]{3,2,1,0:T(8,128)S(1)}, f32[2,2,32,128]{3,2,1,0:T(8,128)S(1)}, u32[]{:S(2)}, u32[]{:S(2)}) collective-permute-start(f32[2,2,32,128]{3,2,1,0:T(8,128)S(1)} %get-tuple-element.495), channel_id=1, source_target_pairs={{0,16},{1,17},{2,18},{3,19},{4,20},{5,21},{6,22},{7,23},{8,24},{9,... | collective-permute-start | bytes 196616 | tf_op jit(solution)/shard_map/ppermute | solution.py:23
  312.8 22.7 %collective-permute-start.73 = (f32[2,2,32,128]{3,2,1,0:T(8,128)S(1)}, f32[2,2,32,128]{3,2,1,0:T(8,128)S(1)}, u32[]{:S(2)}, u32[]{:S(2)}) collective-permute-start(f32[2,2,32,128]{3,2,1,0:T(8,128)S(1)} %get-tuple-element.496), channel_id=1, source_target_pairs={{16,0},{17,1},{18,2},{19,3},{20,4},{21,5},{22,6},{23,7},{24,8},{25... | collective-permute-start | bytes 196616 | tf_op jit(solution)/shard_map/ppermute | solution.py:25
  330.0 11.9 %collective-permute-start.36 = (f32[1,1,1,128]{3,2,1,0:T(1,128)S(1)}, f32[1,1,1,128]{3,2,1,0:T(1,128)S(1)}, u32[]{:S(2)}, u32[]{:S(2)}) collective-permute-start(f32[1,1,1,128]{3,2,1,0:T(1,128)S(1)} %bitcast.421), channel_id=1, source_target_pairs={{0,16},{1,17},{2,18},{3,19},{4,20},{5,21},{6,22},{7,23},{8,24},{9,... | collective-permute-start | bytes 1544 | tf_op jit(solution)/shard_map/ppermute | solution.py:23
  336.3 94.2 %collective-permute-start.74 = (f32[2,28,2,128]{3,2,1,0:T(2,128)}, f32[2,28,2,128]{3,2,1,0:T(2,128)S(1)}, u32[]{:S(2)}, u32[]{:S(2)}) collective-permute-start(f32[2,28,2,128]{3,2,1,0:T(2,128)} %get-tuple-element.493), channel_id=1, source_target_pairs={{0,4},{4,8},{8,12},{1,5},{5,9},{9,13},{2,6},{6,10},{10,14},{3,7},{... | collective-permute-start | bytes 172040 | tf_op jit(solution)/shard_map/ppermute | solution.py:23
  339.9 90.5 %collective-permute-start.75 = (f32[2,28,2,128]{3,2,1,0:T(2,128)}, f32[2,28,2,128]{3,2,1,0:T(2,128)}, u32[]{:S(2)}, u32[]{:S(2)}) collective-permute-start(f32[2,28,2,128]{3,2,1,0:T(2,128)} %get-tuple-element.494), channel_id=1, source_target_pairs={{4,0},{8,4},{12,8},{5,1},{9,5},{13,9},{6,2},{10,6},{14,10},{7,3},{... | collective-permute-start | bytes 172040 | tf_op jit(solution)/shard_map/ppermute | solution.py:25
  525.7 16.3 %collective-permute-start.66 = (f32[2,32,128]{2,1,0:T(8,128)S(1)}, f32[2,32,128]{2,1,0:T(8,128)S(1)}, u32[]{:S(2)}, u32[]{:S(2)}) collective-permute-start(f32[2,32,128]{2,1,0:T(8,128)S(1)} %get-tuple-element.519), channel_id=1, source_target_pairs={{0,16},{1,17},{2,18},{3,19},{4,20},{5,21},{6,22},{7,23},{8,24},{9,... | collective-permute-start | bytes 98312 | tf_op jit(solution)/shard_map/ppermute | solution.py:23
  528.3 13.7 %collective-permute-start.67 = (f32[2,32,128]{2,1,0:T(8,128)S(1)}, f32[2,32,128]{2,1,0:T(8,128)S(1)}, u32[]{:S(2)}, u32[]{:S(2)}) collective-permute-start(f32[2,32,128]{2,1,0:T(8,128)S(1)} %get-tuple-element.520), channel_id=1, source_target_pairs={{16,0},{17,1},{18,2},{19,3},{20,4},{21,5},{22,6},{23,7},{24,8},{25... | collective-permute-start | bytes 98312 | tf_op jit(solution)/shard_map/ppermute | solution.py:25
  533.7 17.4 %collective-permute-start.76 = (f32[2,28,36,2]{2,3,1,0:T(2,128)}, f32[2,28,36,2]{2,3,1,0:T(2,128)}, u32[]{:S(2)}, u32[]{:S(2)}) collective-permute-start(f32[2,28,36,2]{2,3,1,0:T(2,128)} %copy.117), channel_id=1, source_target_pairs={{0,1},{1,2},{2,3},{4,5},{5,6},{6,7},{8,9},{9,10},{10,11},{12,13},{... | collective-permute-start | bytes 48392 | tf_op jit(solution)/shard_map/ppermute | solution.py:23
  537.4 16.1 %collective-permute-start.77 = (f32[2,28,36,2]{2,3,1,0:T(2,128)}, f32[2,28,36,2]{2,3,1,0:T(2,128)}, u32[]{:S(2)}, u32[]{:S(2)}) collective-permute-start(f32[2,28,36,2]{2,3,1,0:T(2,128)} %copy.118), channel_id=1, source_target_pairs={{1,0},{2,1},{3,2},{5,4},{6,5},{7,6},{9,8},{10,9},{11,10},{13,12},{... | collective-permute-start | bytes 48392 | tf_op jit(solution)/shard_map/ppermute | solution.py:25
  542.6 13.2 %collective-permute-start.68 = (f32[28,2,128]{2,1,0:T(2,128)}, f32[28,2,128]{2,1,0:T(2,128)}, u32[]{:S(2)}, u32[]{:S(2)}) collective-permute-start(f32[28,2,128]{2,1,0:T(2,128)} %get-tuple-element.513), channel_id=1, source_target_pairs={{0,4},{4,8},{8,12},{1,5},{5,9},{9,13},{2,6},{6,10},{10,14},{3,7},{... | collective-permute-start | bytes 86024 | tf_op jit(solution)/shard_map/ppermute | solution.py:23
  560.1 12.3 %collective-permute-start.70 = (f32[28,36,2]{1,2,0:T(2,128)}, f32[28,36,2]{1,2,0:T(2,128)}, u32[]{:S(2)}, u32[]{:S(2)}) collective-permute-start(f32[28,36,2]{1,2,0:T(2,128)} %copy.113), channel_id=1, source_target_pairs={{0,1},{1,2},{2,3},{4,5},{5,6},{6,7},{8,9},{9,10},{10,11},{12,13},{... | collective-permute-start | bytes 24200 | tf_op jit(solution)/shard_map/ppermute | solution.py:23
  563.3 11.0 %collective-permute-start.71 = (f32[28,36,2]{1,2,0:T(2,128)}, f32[28,36,2]{1,2,0:T(2,128)}, u32[]{:S(2)}, u32[]{:S(2)}) collective-permute-start(f32[28,36,2]{1,2,0:T(2,128)} %copy.114), channel_id=1, source_target_pairs={{1,0},{2,1},{3,2},{5,4},{6,5},{7,6},{9,8},{10,9},{11,10},{13,12},{... | collective-permute-start | bytes 24200 | tf_op jit(solution)/shard_map/ppermute | solution.py:25
  605.5 10.2 %collective-permute-start.82 = (f32[28,36,2]{1,2,0:T(2,128)}, f32[28,36,2]{1,2,0:T(2,128)}, u32[]{:S(2)}, u32[]{:S(2)}) collective-permute-start(f32[28,36,2]{1,2,0:T(2,128)} %copy.123), channel_id=1, source_target_pairs={{0,1},{1,2},{2,3},{4,5},{5,6},{6,7},{8,9},{9,10},{10,11},{12,13},{... | collective-permute-start | bytes 24200 | tf_op jit(solution)/shard_map/ppermute | solution.py:23
  (106 other events, 996.9 us)
where the time goes:
time: 642 us; the launch traced here: 629 us
  starting transfers between devices  217 us (34%)
  local copies, waits for them, and re-layouts  208 us (32%)
  other arithmetic  70.4 us (11%)
  waiting for transfers between devices  57.8 us (9%)
  matrix products  48.8 us (8%)
  loops' own time  24.2 us (4%)
    ppermute x42, starting transfers between devices, padded_2(): lax.ppermute(tail, axis, [(i, (i + 1) % count) for i in range(ends)])  130 us
    ppermute x42, starting transfers between devices, padded_2(): lax.ppermute(head, axis, [((i + 1) % count, i) for i in range(ends)])  86.9 us
    reshape x2, local copies, waits for them, and re-layouts, block_sum(): values.reshape(size_a // 2, 2, size_b // 2, 2, size_c // 2, 2)  53.8 us
    ppermute x42, waiting for transfers between devices, padded_2(): lax.ppermute(head, axis, [((i + 1) % count, i) for i in range(ends)])  35.2 us
    dot_general x12, matrix products, tile_step(): jnp.einsum('abi,abj->ij', this_slab, applied, precision=lax.Precision.HIG...  26.1 us
    another operation x1, loops' own time, body(): block_corr = lax.map(lift_slab, jnp.arange(blocks_x, dtype=jnp.int32))  23 us
    ppermute x42, waiting for transfers between devices, padded_2(): lax.ppermute(tail, axis, [(i, (i + 1) % count) for i in range(ends)])  22.6 us
    reduce_sum x2, other arithmetic, block_sum(): values.reshape(size_a // 2, 2, size_b // 2, 2, size_c // 2, 2)  18.9 us
  transfers between devices with their start and end apart: 84, of which 25 were waited for; matrix products, arithmetic and copies ran while one was open for 28% of the time, Pallas kernels for 0%

commit v1 on v0

v1 whole, which is shorter than its diff:
```python
import functools

import jax
import jax.numpy as jnp
from jax import lax
from jax.experimental import pallas as pl
from jax.experimental.pallas import tpu as pltpu
from jax.sharding import PartitionSpec as P

AGG = 128
LANES = 128
HALO = 4
BLOCK_HALO = HALO // 2
POST = 4
KC = 8
OMEGA_FINE = 0.8
OMEGA_COARSE = 0.7
F32 = jnp.float32
BF16 = jnp.bfloat16
SMEM = pl.BlockSpec(memory_space=pltpu.SMEM)
VMEM = pl.BlockSpec(memory_space=pltpu.VMEM)
IX, PARITY, X_LOW, X_HIGH, Y_LOW, Y_HIGH, Z_LOW, Z_HIGH = range(8)


def call(kernel, outs, scratch=(), limit=16, flops=10**6):
    def run(flags, *arrays):
        return pl.pallas_call(
            kernel,
            out_shape=outs,
            in_specs=[SMEM] + [VMEM] * len(arrays),
            out_specs=jax.tree.map(lambda _: VMEM, outs),
            scratch_shapes=list(scratch),
            compiler_params=pltpu.CompilerParams(vmem_limit_bytes=limit * 2**20),
            cost_estimate=pl.CostEstimate(flops=flops, bytes_accessed=10**5, transcendentals=0),
        )(flags, *arrays)

    return run


def shaped(*shape):
    return jax.ShapeDtypeStruct(shape, F32)


def lane_no(shape):
    return lax.broadcasted_iota(jnp.int32, shape, len(shape) - 1)


def row_no(shape):
    return lax.broadcasted_iota(jnp.int32, shape, len(shape) - 2)


def turned(values, shift, axis):
    shift = shift % values.shape[axis]
    return values if shift == 0 else pltpu.roll(values, shift, axis)


def picked(values, index):
    return jnp.take_along_axis(values, index, axis=1, mode="promise_in_bounds")


def pack_x_kernel(count, fields, labels, flags, *refs):
    ins, outs = refs[: fields + labels], refs[fields + labels :]
    nx = ins[0].shape[0]

    def fill(out, fine_at, block_at):
        for f in range(fields):
            out[HALO * f : HALO * (f + 1)] = ins[f][pl.ds(fine_at, HALO)]
        if labels:
            last = HALO * fields
            out[last] = jnp.zeros(out.shape[1:], F32)
            rows = ins[-1].shape[1]
            for b in range(BLOCK_HALO):
                out[last, rows * b : rows * (b + 1), : ins[-1].shape[2]] = ins[-1][block_at + b].astype(F32)

    if count == 2:
        first = flags[IX] == 0
        fill(outs[0], jnp.where(first, nx - HALO, 0), jnp.where(first, nx // 2 - BLOCK_HALO, 0))
    else:
        fill(outs[0], nx - HALO, nx // 2 - BLOCK_HALO)
        fill(outs[1], 0, 0)


def slab_of(own, low, high, f, x):
    nx = own.shape[0]
    if x < HALO:
        return low[HALO * f + x]
    if x < HALO + nx:
        return own[x - HALO]
    return high[HALO * f + x - HALO - nx]


def label_slab(own, low, high, f, b):
    nb, rows, width = own.shape
    if b < BLOCK_HALO:
        return low[HALO * f, rows * b : rows * (b + 1), :width]
    if b < BLOCK_HALO + nb:
        return own[b - BLOCK_HALO].astype(F32)
    at = b - BLOCK_HALO - nb
    return high[HALO * f, rows * at : rows * (at + 1), :width]


def pack_y_kernel(fields, labels, flags, *refs):
    ins = refs[: fields + labels]
    low, high = refs[fields + labels : fields + labels + 2]
    to_high, to_low = refs[fields + labels + 2 :]
    nx, ny = ins[0].shape[0], ins[0].shape[1]
    wide = nx + 2 * HALO
    for f in range(fields):
        for x in range(wide):
            slab = slab_of(ins[f], low, high, f, x)
            at = (f * wide + x) * HALO
            to_high[at : at + HALO] = slab[ny - HALO :]
            to_low[at : at + HALO] = slab[:HALO]
    if labels:
        base = fields * wide * HALO
        nb, rows, width = ins[-1].shape
        to_high[base:] = jnp.zeros((to_high.shape[0] - base, LANES), F32)
        to_low[base:] = jnp.zeros((to_low.shape[0] - base, LANES), F32)
        for b in range(nb + 2 * BLOCK_HALO):
            slab = label_slab(ins[-1], low, high, fields, b)
            at = base + BLOCK_HALO * b
            to_high[at : at + BLOCK_HALO, :width] = slab[rows - BLOCK_HALO :]
            to_low[at : at + BLOCK_HALO, :width] = slab[:BLOCK_HALO]


def pack_z_kernel(fields, labels, flags, *refs):
    ins = refs[: fields + labels]
    x_low, x_high, y_low, y_high = refs[fields + labels : fields + labels + 4]
    outs = refs[fields + labels + 4 :]
    wide_ref, send = outs[0], outs[1]
    nx, ny = ins[0].shape[0], ins[0].shape[1]
    wide, tall = nx + 2 * HALO, ny + 2 * HALO
    group = LANES // (2 * HALO)
    lane = lane_no((tall, LANES))
    for f in range(fields):
        for g in range(wide // group):
            packed = jnp.zeros((tall, LANES), F32)
            for k in range(group):
                x = g * group + k
                at = (f * wide + x) * HALO
                wide_ref[f, x, HALO : HALO + ny] = slab_of(ins[f], x_low, x_high, f, x)
                wide_ref[f, x, :HALO] = y_low[at : at + HALO]
                wide_ref[f, x, HALO + ny :] = y_high[at : at + HALO]
                moved = turned(wide_ref[f, x], 2 * HALO * k + HALO, 1)
                packed = jnp.where(lane // (2 * HALO) == k, moved, packed)
            at = (f * (wide // group) + g) * tall
            send[at : at + tall] = packed
    if labels:
        base = fields * (wide // group) * tall
        label_ref = outs[2]
        nb, rows, width = ins[-1].shape
        span = rows + 2 * BLOCK_HALO
        label_ref[...] = jnp.zeros(label_ref.shape, F32)
        lane = lane_no((span, LANES))
        packed = jnp.zeros((span, LANES), F32)
        for b in range(nb + 2 * BLOCK_HALO):
            at = fields * wide * HALO + BLOCK_HALO * b
            label_ref[b, BLOCK_HALO : BLOCK_HALO + rows, :width] = label_slab(ins[-1], x_low, x_high, fields, b)
            label_ref[b, :BLOCK_HALO] = y_low[at : at + BLOCK_HALO]
            label_ref[b, BLOCK_HALO + rows : span] = y_high[at : at + BLOCK_HALO]
            slab = label_ref[b, :span]
            slab = jnp.where(lane < width, slab, turned(slab, width, 1))
            moved = turned(slab, 2 * BLOCK_HALO * b + BLOCK_HALO - width, 1)
            packed = jnp.where(lane // (2 * BLOCK_HALO) == b, moved, packed)
        send[base:] = jnp.zeros((send.shape[0] - base, LANES), F32)
        send[base : base + span] = packed


def permuted(values, axes, pairs):
    return lax.ppermute(values, axes, pairs)


class Links:
    def __init__(self, mesh):
        self.sizes = [mesh.shape[a] for a in ("gx", "gy", "gz")]
        n_x, n_y, n_z = self.sizes
        self.ring_x = [(i, (i + 1) % n_x) for i in range(n_x)]
        self.ring_y = [(i, (i + 1) % n_y) for i in range(n_y)]
        self.snake = []
        for i in range(n_x):
            for j in range(0, n_y, 2):
                nodes = [(i * n_y + j) * n_z + k for k in range(n_z)]
                nodes += [(i * n_y + j + 1) * n_z + k for k in reversed(range(n_z))]
                self.snake += [(nodes[m], nodes[(m + 1) % len(nodes)]) for m in range(len(nodes))]

    @staticmethod
    def back(pairs):
        return [(b, a) for a, b in pairs]

    def x(self, sends):
        if self.sizes[0] == 2:
            got = permuted(sends[0], "gx", self.ring_x)
            return got, got
        return permuted(sends[0], "gx", self.ring_x), permuted(sends[-1], "gx", self.back(self.ring_x))

    def y(self, to_high, to_low):
        return permuted(to_high, "gy", self.ring_y), permuted(to_low, "gy", self.back(self.ring_y))

    def z(self, send):
        axes = ("gx", "gy", "gz")
        return permuted(send, axes, self.snake), permuted(send, axes, self.back(self.snake))


def widened(links, flags, fields, labels=()):
    count = len(fields)
    has = len(labels)
    nx, ny, nz = fields[0].shape
    wide, tall = nx + 2 * HALO, ny + 2 * HALO
    blocks = nx // 2 + 2 * BLOCK_HALO
    arrays = tuple(fields) + tuple(labels)
    n_send = 1 if links.sizes[0] == 2 else 2
    sends = call(
        functools.partial(pack_x_kernel, links.sizes[0], count, has),
        [shaped(HALO * count + has, ny, nz)] * n_send,
    )(flags, *arrays)
    x_low, x_high = links.x(sends)
    rows = count * wide * HALO + has * blocks * BLOCK_HALO
    to_high, to_low = call(
        functools.partial(pack_y_kernel, count, has), [shaped(rows, nz)] * 2
    )(flags, *arrays, x_low, x_high)
    y_low, y_high = links.y(to_high, to_low)
    groups = wide // (LANES // (2 * HALO))
    rows = count * groups * tall + has * 24
    outs = [shaped(count, wide, tall, nz), shaped(rows, nz)]
    if has:
        outs.append(shaped(blocks, 24, LANES))
    got = call(functools.partial(pack_z_kernel, count, has), outs)(
        flags, *arrays, x_low, x_high, y_low, y_high
    )
    forth, back = links.z(got[1])
    return got[0], forth, back, (got[2] if has else None)


def lane_halo(flags, forth, back, at, rows):
    lane = lane_no((rows, LANES))
    one, two = forth[at : at + rows], back[at : at + rows]
    even = flags[PARITY] == 0
    low, high = jnp.where(even, one, two), jnp.where(even, two, one)
    return jnp.where(lane % (2 * HALO) < HALO, low, high)


def spread_lanes(flags, forth, back, wide_ref, f, out):
    wide, tall = out.shape[0], out.shape[2]
    group = LANES // (2 * HALO)
    for g in range(wide // group):
        packed = lane_halo(flags, forth, back, (f * (wide // group) + g) * tall, tall)
        for k in range(group):
            x = g * group + k
            out[x, 0] = wide_ref[f, x]
            out[x, 1] = turned(packed, -(2 * HALO * k + HALO), 1)


def get(ref, x):
    return jnp.concatenate([ref[x, 0], ref[x, 1]], axis=1)


def put(ref, x, values):
    ref[x, 0] = values[:, :LANES]
    ref[x, 1] = values[:, LANES:]


def weight(one, two):
    return 2.0 * (one * two) / (one + two)


def beside(field, x, wx, wy, wz):
    here, face_y, face_z = get(field, x), get(wy, x), get(wz, x)
    total = get(wx, x) * get(field, x + 1) + get(wx, x - 1) * get(field, x - 1)
    total = total + face_y * turned(here, -1, 0) + turned(face_y * here, 1, 0)
    return total + face_z * turned(here, -1, 1) + turned(face_z * here, 1, 1)


def pack_rows(values):
    half = values.shape[0] // 2
    lane = lane_no((half, LANES))
    return jnp.where(lane < LANES // 2, values[:half], turned(values[half:], LANES // 2, 1))


def fine_kernel(flags, wide_ref, forth, back, label_ref, *refs):
    (inv_diag, start, wx, wy, wz, pre, block_label, block_near, block_weight, face_label, face_near, face_weight,
     scaled_rhs, scale, cond, rhs, absorb, diag, once, res, side_rows, side_lanes) = refs
    wide, _, tall, _ = inv_diag.shape
    both = 2 * LANES
    nx, ny = pre.shape[0], pre.shape[1]
    last = HALO + nx
    for f, out in enumerate((cond, rhs, absorb)):
        spread_lanes(flags, forth, back, wide_ref, f, out)
    row, lane = row_no((tall, both)), lane_no((tall, both))
    keep_y = jnp.where(
        row == HALO - 1, flags[Y_LOW], jnp.where(row == HALO + ny - 1, flags[Y_HIGH], 1)
    ).astype(F32)
    keep_z = jnp.where(
        lane == both - 1, flags[Z_LOW], jnp.where(lane == LANES - 1, flags[Z_HIGH], 1)
    ).astype(F32)

    def fields(x, before):
        here = get(cond, x)
        keep = jnp.where(x == HALO - 1, flags[X_LOW], jnp.where(x == last - 1, flags[X_HIGH], 1)).astype(F32)
        face_x = keep * weight(here, get(cond, jnp.minimum(x + 1, wide - 1)))
        face_y = keep_y * weight(here, turned(here, -1, 0))
        face_z = keep_z * weight(here, turned(here, -1, 1))
        total = get(absorb, x) + face_x + before
        total = total + face_y + turned(face_y, 1, 0) + face_z + turned(face_z, 1, 1)
        inverse = OMEGA_FINE / total
        for ref, values in ((wx, face_x), (wy, face_y), (wz, face_z), (diag, total), (inv_diag, inverse)):
            put(ref, x, values)
        put(start, x, inverse * get(rhs, x))
        return face_x

    lax.fori_loop(0, wide, fields, jnp.zeros((tall, both), F32))

    @pl.loop(HALO - 1, last + 1)
    def _(x):
        put(once, x, (2.0 - OMEGA_FINE) * get(start, x) + get(inv_diag, x) * beside(start, x, wx, wy, wz))

    @pl.loop(HALO, last)
    def _(x):
        full = get(rhs, x) - get(diag, x) * get(once, x) + beside(once, x, wx, wy, wz)
        res[x, 0] = full[:, :LANES]
        pre[x - HALO] = once[x, 0, HALO : HALO + ny]

    nb, half, width = nx // 2, ny // 2, LANES // 2
    lane = lane_no((half, LANES))
    row = row_no((half, LANES))
    even = 2 * (lane % width)
    odd = even + 1
    iota = row_no((AGG, LANES)).astype(F32)
    side_rows[...] = jnp.zeros(side_rows.shape, F32)
    side_lanes[...] = jnp.zeros(side_lanes.shape, F32)

    def rows_at(ref, x, off):
        return ref[x, 0, pl.ds(off, half, stride=2)]

    def four(ref, x):
        return sum(rows_at(ref, x + a, HALO + b) for a in range(2) for b in range(2))

    def in_pairs(values):
        return picked(values + turned(values, -1, 1), even)

    def edge_x(x):
        return in_pairs(rows_at(wx, x, HALO) + rows_at(wx, x, HALO + 1))

    def block_step(b, carry):
        low_x, acc_r, acc_q = carry
        x = HALO + 2 * b
        at = b + BLOCK_HALO
        rows = pl.ds(BLOCK_HALO, half)
        own = label_ref[at, rows]
        near_x, past_x = label_ref[at + 1, rows], label_ref[at - 1, rows]
        high_x = edge_x(x + 1)
        high_y = in_pairs(rows_at(wy, x, HALO + 1) + rows_at(wy, x + 1, HALO + 1))
        low_y = in_pairs(rows_at(wy, x, HALO - 1) + rows_at(wy, x + 1, HALO - 1))
        side = four(wz, x)
        high_z = picked(side, odd)
        end = sum(
            wz[x + a, 1, pl.ds(HALO + c, half, stride=2)] for a in range(2) for c in range(2)
        )
        low_z = picked(jnp.where(lane == 0, turned(end, 1, 1), turned(side, 1, 1)), even)
        near_y, past_y = turned(own, -1, 0), turned(own, 1, 0)
        near_z, past_z = turned(own, -1, 1), turned(own, 1, 1)
        end_x, end_y, end_z = b == nb - 1, row == half - 1, lane == width - 1
        total = in_pairs(four(absorb, x))
        total = total + jnp.where((near_x != own) | end_x, high_x, 0.0)
        total = total + jnp.where((past_x != own) | (b == 0), low_x, 0.0)
        total = total + jnp.where((near_y != own) | end_y, high_y, 0.0)
        total = total + jnp.where((past_y != own) | (row == 0), low_y, 0.0)
        total = total + jnp.where((near_z != own) | end_z, high_z, 0.0)
        total = total + jnp.where((past_z != own) | (lane == 0), low_z, 0.0)
        packed = pack_rows(own)
        block_label[b] = packed
        block_near[0, b], block_near[1, b], block_near[2, b] = pack_rows(near_x), pack_rows(near_y), pack_rows(near_z)
        block_weight[0, b] = pack_rows(jnp.where(end_x, 0.0, high_x))
        block_weight[1, b] = pack_rows(jnp.where(end_y, 0.0, high_y))
        block_weight[2, b] = pack_rows(jnp.where(end_z, 0.0, high_z))
        sums, total = pack_rows(in_pairs(four(res, x))), pack_rows(total)
        for r in range(half // 2):
            hit = packed[r : r + 1] == iota
            acc_r = acc_r + jnp.where(hit, sums[r : r + 1], 0.0)
            acc_q = acc_q + jnp.where(hit, total[r : r + 1], 0.0)

        @pl.when(b == 0)
        def _():
            face_label[0] = packed
            face_near[0] = pack_rows(past_x)
            face_weight[0] = pack_rows(low_x)

        @pl.when(end_x)
        def _():
            face_label[1] = packed
            face_near[1] = pack_rows(near_x)
            face_weight[1] = pack_rows(high_x)

        here = pl.ds(b, 1)
        side_rows[0, here], side_rows[1, here] = own[:1], own[half - 1 :]
        side_rows[2, here] = label_ref[at, pl.ds(BLOCK_HALO - 1, 1)]
        side_rows[3, here] = label_ref[at, pl.ds(BLOCK_HALO + half, 1)]
        side_rows[4, here], side_rows[5, here] = low_y[:1], high_y[half - 1 :]
        mine = lane == b
        for s, (values, at_lane) in enumerate(((own, 0), (own, width - 1), (low_z, 0), (high_z, width - 1))):
            one = jnp.broadcast_to(values[:, at_lane : at_lane + 1], (half, LANES))
            side_lanes[s] = jnp.where(mine, one, side_lanes[s])
        return high_x, acc_r, acc_q

    nothing = jnp.zeros((AGG, LANES), F32)
    _, acc_r, acc_q = lax.fori_loop(0, nb, block_step, (edge_x(HALO - 1), nothing, nothing))
    for s in range(2):
        face_label[2 + s] = pack_rows(side_rows[s])
        face_near[2 + s] = pack_rows(side_rows[2 + s])
        face_weight[2 + s] = pack_rows(jnp.where(lane < width, side_rows[4 + s], 0.0))
        face_label[4 + s] = pack_rows(side_lanes[s])
        face_weight[4 + s] = pack_rows(side_lanes[2 + s])
    base = 3 * (wide // (LANES // (2 * HALO))) * tall
    even_place = flags[PARITY] == 0
    one, two = forth[pl.ds(base + BLOCK_HALO, half)], back[pl.ds(base + BLOCK_HALO, half)]
    below, above = jnp.where(even_place, one, two), jnp.where(even_place, two, one)
    span = 2 * BLOCK_HALO
    spot = span * jnp.minimum(lane + BLOCK_HALO, LANES // span - 1)
    face_near[4] = pack_rows(picked(below, spot + BLOCK_HALO - 1))
    face_near[5] = pack_rows(picked(above, spot + BLOCK_HALO))

    def lane_total(values):
        ones = jnp.ones((8, LANES), F32)
        return lax.dot_general(
            ones, values, (((1,), (1,)), ((), ())), precision=lax.Precision.HIGHEST, preferred_element_type=F32
        )

    scale[...] = OMEGA_COARSE / lane_total(acc_q)
    scaled_rhs[...] = scale[...] * lane_total(acc_r)


def tiles_kernel(flags, block_label, block_near, block_weight, face_label, face_near, face_weight, out, left, right):
    iota = row_no((AGG, LANES)).astype(F32)
    depth = block_label.shape[1]

    def product(labels, pairs):
        for r in range(depth):
            lanes = pl.ds(r * LANES, LANES)
            left[:, lanes] = jnp.where(labels[r : r + 1] == iota, 1.0, 0.0).astype(BF16)
            held = sum(jnp.where(near[r : r + 1] == iota, w[r : r + 1], 0.0) for near, w in pairs)
            high = held.astype(BF16)
            right[:AGG, lanes] = high
            right[AGG:, lanes] = (held - high.astype(F32)).astype(BF16)
        return lax.dot_general(
            left[...], right[...], (((1,), (1,)), ((), ())), preferred_element_type=F32
        )

    def own_step(b, total):
        return total + product(block_label[b], [(block_near[d, b], block_weight[d, b]) for d in range(3)])

    own = lax.fori_loop(0, block_label.shape[0], own_step, jnp.zeros((AGG, 2 * AGG), F32))
    own = own[:, :AGG] + own[:, AGG:]
    own = jnp.where(row_no((AGG, AGG)) == lane_no((AGG, AGG)), 0.0, own + own.T)

    def keep(t, tile):
        high = tile.astype(BF16)
        out[pl.ds(t * AGG, AGG), :AGG] = high
        out[pl.ds(t * AGG, AGG), AGG:] = (tile - high.astype(F32)).astype(BF16)

    keep(0, own)

    @pl.loop(0, 6)
    def _(s):
        tile = product(face_near[s], [(face_label[s], face_weight[s])])
        keep(s + 1, tile[:, :AGG] + tile[:, AGG:])


def turn_kernel(flags, tiles, scaled_rhs, scale, own, x_low, x_high, y_low, y_high, forth, back, out):
    even = flags[PARITY] == 0
    one, two = forth[...], back[...]
    vectors = [own[...], x_low[...], x_high[...], y_low[...], y_high[...]]
    vectors += [jnp.where(even, one, two), jnp.where(even, two, one)]
    row = row_no((8, AGG))
    parts = []
    for v in vectors:
        high = v.astype(BF16).astype(F32)
        parts.append(jnp.where(row == 0, high, jnp.where(row == 1, v - high, 0.0)).astype(BF16))
    got = jnp.dot(jnp.concatenate(parts, axis=1), tiles[...], preferred_element_type=F32)
    applied = jnp.sum(got[:, :AGG] + got[:, AGG:], axis=0, keepdims=True)
    out[...] = (1.0 - OMEGA_COARSE) * own[...] + scaled_rhs[...] + scale[...] * applied


def correct_kernel(flags, pre, label_ref, coarse, out):
    nb, half = pre.shape[0] // 2, pre.shape[1] // 2
    to_block = lane_no((half, LANES)) // 2
    table = jnp.broadcast_to(coarse[:1], (half, LANES))

    @pl.loop(0, nb)
    def _(b):
        labels = picked(label_ref[b + BLOCK_HALO, pl.ds(BLOCK_HALO, half)], to_block)
        values = picked(table, labels.astype(jnp.int32))
        for a in range(2):
            for c in range(2):
                rows = pl.ds(c, half, stride=2)
                out[2 * b + a, rows] = pre[2 * b + a, rows] + values


def post_kernel(flags, wide_ref, forth, back, inv_diag, start, wx, wy, wz, out, one, two):
    spread_lanes(flags, forth, back, wide_ref, 0, one)
    wide = one.shape[0]
    nx, ny = out.shape[0], out.shape[1]

    def sweep(src, x):
        kept = (1.0 - OMEGA_FINE) * get(src, x) + get(start, x)
        return kept + get(inv_diag, x) * beside(src, x, wx, wy, wz)

    buffers = (one, two)
    for s in range(POST - 1):
        src, dst = buffers[s % 2], buffers[(s + 1) % 2]

        @pl.loop(s + 1, wide - s - 1)
        def _(x):
            put(dst, x, sweep(src, x))

    src = buffers[(POST - 1) % 2]

    @pl.loop(HALO, HALO + nx)
    def _(x):
        out[x - HALO] = sweep(src, x)[HALO : HALO + ny, :LANES]


def body(links, right_side, conductance, absorption, block_agg):
    nx, ny, nz = right_side.shape
    wide, tall = nx + 2 * HALO, ny + 2 * HALO
    nb = nx // 2
    ix, iy, iz = (lax.axis_index(a) for a in ("gx", "gy", "gz"))
    n_x, n_y, n_z = links.sizes
    flags = jnp.stack(
        [ix, iy % 2, ix > 0, ix < n_x - 1, iy > 0, iy < n_y - 1, iz > 0, iz < n_z - 1]
    ).astype(jnp.int32)
    wide_fields, forth, back, labels = widened(links, flags, (conductance, right_side, absorption), (block_agg,))
    big = shaped(wide, 2, tall, nz)
    outs = [big] * 5 + [shaped(nx, ny, nz)]
    outs += [shaped(nb, 8, LANES), shaped(3, nb, 8, LANES), shaped(3, nb, 8, LANES)]
    outs += [shaped(6, 8, LANES)] * 3 + [shaped(8, AGG)] * 2
    scratch = [pltpu.VMEM((wide, 2, tall, nz), F32)] * 5 + [pltpu.VMEM((wide, 1, tall, nz), F32)]
    scratch += [pltpu.VMEM((6, 16, LANES), F32), pltpu.VMEM((4, 16, LANES), F32)]
    got = call(fine_kernel, outs, scratch, limit=40)(flags, wide_fields, forth, back, labels)
    inv_diag, start, wx, wy, wz, pre = got[:6]
    scaled_rhs, scale = got[12:]
    tiles = call(
        tiles_kernel,
        jax.ShapeDtypeStruct((7 * AGG, 2 * AGG), BF16),
        [pltpu.VMEM((AGG, 8 * LANES), BF16), pltpu.VMEM((2 * AGG, 8 * LANES), BF16)],
    )(flags, *got[6:12])
    coarse = scaled_rhs
    for _ in range(KC - 1):
        near = links.x([coarse] * (1 if n_x == 2 else 2)) + links.y(coarse, coarse) + links.z(coarse)
        coarse = call(turn_kernel, shaped(8, AGG))(flags, tiles, scaled_rhs, scale, coarse, *near)
    corrected = call(correct_kernel, shaped(nx, ny, nz))(flags, pre, labels, coarse)
    wide_iter, forth, back, _ = widened(links, flags, (corrected,))
    return call(post_kernel, shaped(nx, ny, nz), [pltpu.VMEM((wide, 2, tall, nz), F32)] * 2, limit=24)(
        flags, wide_iter, forth, back, inv_diag, start, wx, wy, wz
    )


def solution(mesh):
    spec = P("gx", "gy", "gz")
    return jax.shard_map(
        functools.partial(body, Links(mesh)), mesh=mesh, in_specs=(spec,) * 4, out_specs=spec, check_vma=False
    )
```

time: 642 us -> 131 us (0.20)
  the two profiles are of different devices: /device:TPU:25 before, /device:TPU:0 now
where the time goes in v1:
time: 131 us; the launch traced here: 130 us
  Pallas kernels  50.4 us (38%)
  waiting for transfers between devices  39.9 us (30%)
  starting transfers between devices  35.1 us (27%)
  local copies, waits for them, and re-layouts  3.97 us (3%)
    pallas_call x17, Pallas kernels, run(): pl.pallas_call(kernel, out_shape=outs, in_specs=[SMEM] + [VMEM] * len(arr...  50.4 us
    ppermute x45, waiting for transfers between devices, permuted(): return lax.ppermute(values, axes, pairs)  39.9 us
    ppermute x45, starting transfers between devices, permuted(): return lax.ppermute(values, axes, pairs)  35.1 us
    unnamed x8, local copies, waits for them, and re-layouts  3.88 us
  transfers between devices with their start and end apart: 45, of which 26 were waited for; matrix products, arithmetic and copies ran while one was open for 0% of the time, Pallas kernels for 7%

profile of v1, /device:TPU:0, one launch (start us, length us, event | category | flops | bytes accessed | tf_op | source)
XLA Modules:
  0.0 129.6 jit_solution(1772801173560232435)
XLA Ops:
  4.5 3.0 %collective-permute-start = (f32[13,32,128]{2,1,0:T(8,128)S(1)}, f32[13,32,128]{2,1,0:T(8,128)S(1)}, u32[]{:S(2)}, u32[]{:S(2)}) collective-permute-start(f32[13,32,128]{2,1,0:T(8,128)S(1)} %shard_map.46), channel_id=1, source_target_pairs={{0,16},{16,0},{1,17},{17,1},{2,18},{18,2},{3,19},{19,3},{4,20},{20... | collective-permute-start | bytes 638984 | tf_op jit(solution)/shard_map/ppermute | solution.py:170
  7.5 5.3 %collective-permute-done.refs_4_.refs_5_ = f32[13,32,128]{2,1,0:T(8,128)S(1)} collective-permute-done((f32[13,32,128]{2,1,0:T(8,128)S(1)}, f32[13,32,128]{2,1,0:T(8,128)S(1)}, u32[]{:S(2)}, u32[]{:S(2)}) %collective-permute-start) | collective-permute-done | bytes 213024 | tf_op jit(solution)/shard_map/ppermute | solution.py:170
  13.5 1.7 %collective-permute-start.2 = (f32[416,128]{1,0:T(8,128)S(1)}, f32[416,128]{1,0:T(8,128)S(1)}, u32[]{:S(2)}, u32[]{:S(2)}) collective-permute-start(f32[416,128]{1,0:T(8,128)S(1)} %get-tuple-element.29), channel_id=1, source_target_pairs={{4,0},{8,4},{12,8},{0,12},{5,1},{9,5},{13,9},{1,13},{6,2},{10,6},{... | collective-permute-start | bytes 638984 | tf_op jit(solution)/shard_map/ppermute | solution.py:170
  15.2 3.7 %collective-permute-done.1.refs_6_ = f32[416,128]{1,0:T(8,128)S(1)} collective-permute-done((f32[416,128]{1,0:T(8,128)S(1)}, f32[416,128]{1,0:T(8,128)S(1)}, u32[]{:S(2)}, u32[]{:S(2)}) %collective-permute-start.1) | collective-permute-done | bytes 213024 | tf_op jit(solution)/shard_map/ppermute | solution.py:170
  20.3 1.5 %shard_map.48 = (f32[3,32,40,128]{3,2,1,0:T(8,128)S(1)}, f32[264,128]{1,0:T(8,128)S(1)}, f32[16,24,128]{2,1,0:T(8,128)S(1)}) custom-call(s32[8]{0:T(128)S(1)} %stack.59.flags, f32[24,32,128]{2,1,0:T(8,128)S(1)} %copy-done, f32[24,32,128]{2,1,0:T(8,128)S(1)} %copy-done.1, f32[24,32,128]{2,1,0:T(8,128)S(1)} %copy-done.2, s32[12,16,64]{2,1,0:T(8,128)S(1)} %copy-done.3, ...), custom_call_target="tpu_custom_call" | custom-call | flops 1000000 | bytes 100000 | tf_op jit(solution)/shard_map/pallas_call | solution.py:27
  22.4 1.5 %collective-permute-start.3 = (f32[264,128]{1,0:T(8,128)S(1)}, f32[264,128]{1,0:T(8,128)S(1)}, u32[]{:S(2)}, u32[]{:S(2)}) collective-permute-start(f32[264,128]{1,0:T(8,128)S(1)} %get-tuple-element.31), channel_id=1, source_target_pairs={{0,1},{1,2},{2,3},{3,7},{7,6},{6,5},{5,4},{4,0},{8,9},{9,10},{10,1... | collective-permute-start | bytes 405512 | tf_op jit(solution)/shard_map/ppermute | solution.py:170
  23.9 3.3 %collective-permute-done.4.back = f32[264,128]{1,0:T(8,128)S(1)} collective-permute-done((f32[264,128]{1,0:T(8,128)S(1)}, f32[264,128]{1,0:T(8,128)S(1)}, u32[]{:S(2)}, u32[]{:S(2)}) %collective-permute-start.4) | collective-permute-done | bytes 135200 | tf_op jit(solution)/shard_map/ppermute | solution.py:170
  27.2 17.0 %shard_map.49 = (f32[32,2,40,128]{3,2,1,0:T(8,128)S(1)}, f32[32,2,40,128]{3,2,1,0:T(8,128)S(1)}, f32[32,2,40,128]{3,2,1,0:T(8,128)S(1)}, f32[32,2,40,128]{3,2,1,...) custom-call(s32[8]{0:T(128)S(1)} %stack.59.flags, ...), custom_call_target="tpu_custom_call" | custom-call | flops 1000000 | bytes 100000 | tf_op jit(solution)/shard_map/pallas_call | solution.py:27
  45.1 1.6 %collective-permute-start.8 = (f32[8,128]{1,0:T(8,128)S(1)}, f32[8,128]{1,0:T(8,128)S(1)}, u32[]{:S(2)}, u32[]{:S(2)}) collective-permute-start(f32[8,128]{1,0:T(8,128)S(1)} %get-tuple-element.40.scaled_rhs.own), channel_id=1, source_target_pairs={{0,1},{1,2},{2,3},{3,7},{7,6},{6,5},{5,4},{4,0},{8,9},{9,10},{10,1... | collective-permute-start | bytes 12296 | tf_op jit(solution)/shard_map/ppermute | solution.py:170
  47.7 1.5 %collective-permute-start.5 = (f32[8,128]{1,0:T(8,128)S(1)}, f32[8,128]{1,0:T(8,128)S(1)}, u32[]{:S(2)}, u32[]{:S(2)}) collective-permute-start(f32[8,128]{1,0:T(8,128)S(1)} %get-tuple-element.40.scaled_rhs.own), channel_id=1, source_target_pairs={{0,16},{16,0},{1,17},{17,1},{2,18},{18,2},{3,19},{19,3},{4,20},{20... | collective-permute-start | bytes 12296 | tf_op jit(solution)/shard_map/ppermute | solution.py:170
  49.2 9.4 %shard_map.50.tiles = bf16[896,256]{1,0:T(8,128)(2,1)S(1)} custom-call(s32[8]{0:T(128)S(1)} %stack.59.flags, f32[12,8,128]{2,1,0:T(8,128)S(1)} %get-tuple-element.34.block_label, f32[3,12,8,128]{3,2,1,0:T(8,128)S(1)} %get-tuple-element.35.block_near, f32[3,12,8,128]{3,2,1,0:T(8,128)S(1)} %get-tuple-element.36.block_weight, ...), custom_call_target="tpu_custom_call" | custom-call | flops 1000000 | bytes 100000 | tf_op jit(solution)/shard_map/pallas_call | solution.py:27
  59.8 1.7 %collective-permute-start.13 = (f32[8,128]{1,0:T(8,128)S(1)}, f32[8,128]{1,0:T(8,128)S(1)}, u32[]{:S(2)}, u32[]{:S(2)}) collective-permute-start(f32[8,128]{1,0:T(8,128)S(1)} %shard_map.51.own), channel_id=1, source_target_pairs={{0,1},{1,2},{2,3},{3,7},{7,6},{6,5},{5,4},{4,0},{8,9},{9,10},{10,1... | collective-permute-start | bytes 12296 | tf_op jit(solution)/shard_map/ppermute | solution.py:170
  63.7 1.7 %collective-permute-done.11.y_low = f32[8,128]{1,0:T(8,128)S(1)} collective-permute-done((f32[8,128]{1,0:T(8,128)S(1)}, f32[8,128]{1,0:T(8,128)S(1)}, u32[]{:S(2)}, u32[]{:S(2)}) %collective-permute-start.11) | collective-permute-done | bytes 4128 | tf_op jit(solution)/shard_map/ppermute | solution.py:170
  66.8 2.0 %collective-permute-start.18 = (f32[8,128]{1,0:T(8,128)S(1)}, f32[8,128]{1,0:T(8,128)S(1)}, u32[]{:S(2)}, u32[]{:S(2)}) collective-permute-start(f32[8,128]{1,0:T(8,128)S(1)} %shard_map.52.own), channel_id=1, source_target_pairs={{0,1},{1,2},{2,3},{3,7},{7,6},{6,5},{5,4},{4,0},{8,9},{9,10},{10,1... | collective-permute-start | bytes 12296 | tf_op jit(solution)/shard_map/ppermute | solution.py:170
  73.6 2.0 %collective-permute-start.23 = (f32[8,128]{1,0:T(8,128)S(1)}, f32[8,128]{1,0:T(8,128)S(1)}, u32[]{:S(2)}, u32[]{:S(2)}) collective-permute-start(f32[8,128]{1,0:T(8,128)S(1)} %shard_map.53.own), channel_id=1, source_target_pairs={{0,1},{1,2},{2,3},{3,7},{7,6},{6,5},{5,4},{4,0},{8,9},{9,10},{10,1... | collective-permute-start | bytes 12296 | tf_op jit(solution)/shard_map/ppermute | solution.py:170
  80.5 2.0 %collective-permute-start.28 = (f32[8,128]{1,0:T(8,128)S(1)}, f32[8,128]{1,0:T(8,128)S(1)}, u32[]{:S(2)}, u32[]{:S(2)}) collective-permute-start(f32[8,128]{1,0:T(8,128)S(1)} %shard_map.54.own), channel_id=1, source_target_pairs={{0,1},{1,2},{2,3},{3,7},{7,6},{6,5},{5,4},{4,0},{8,9},{9,10},{10,1... | collective-permute-start | bytes 12296 | tf_op jit(solution)/shard_map/ppermute | solution.py:170
  87.4 2.0 %collective-permute-start.33 = (f32[8,128]{1,0:T(8,128)S(1)}, f32[8,128]{1,0:T(8,128)S(1)}, u32[]{:S(2)}, u32[]{:S(2)}) collective-permute-start(f32[8,128]{1,0:T(8,128)S(1)} %shard_map.55.own), channel_id=1, source_target_pairs={{0,1},{1,2},{2,3},{3,7},{7,6},{6,5},{5,4},{4,0},{8,9},{9,10},{10,1... | collective-permute-start | bytes 12296 | tf_op jit(solution)/shard_map/ppermute | solution.py:170
  94.3 2.0 %collective-permute-start.38 = (f32[8,128]{1,0:T(8,128)S(1)}, f32[8,128]{1,0:T(8,128)S(1)}, u32[]{:S(2)}, u32[]{:S(2)}) collective-permute-start(f32[8,128]{1,0:T(8,128)S(1)} %shard_map.56.own), channel_id=1, source_target_pairs={{0,1},{1,2},{2,3},{3,7},{7,6},{6,5},{5,4},{4,0},{8,9},{9,10},{10,1... | collective-permute-start | bytes 12296 | tf_op jit(solution)/shard_map/ppermute | solution.py:170
  101.1 2.3 %shard_map.58.refs_0_ = f32[24,32,128]{2,1,0:T(8,128)S(1)} custom-call(s32[8]{0:T(128)S(1)} %stack.59.flags, f32[24,32,128]{2,1,0:T(8,128)S(1)} %get-tuple-element.33.pre, f32[16,24,128]{2,1,0:T(8,128)S(1)} %get-tuple-element.32.label_ref, f32[8,128]{1,0:T(8,128)S(1)} %shard_map.57.coarse), custom_call_target="tpu_custom_call" | custom-call | flops 1000000 | bytes 100000 | tf_op jit(solution)/shard_map/pallas_call | solution.py:27
  104.6 3.8 %collective-permute-done.40.refs_1_.refs_2_ = f32[4,32,128]{2,1,0:T(8,128)S(1)} collective-permute-done((f32[4,32,128]{2,1,0:T(8,128)S(1)}, f32[4,32,128]{2,1,0:T(8,128)S(1)}, u32[]{:S(2)}, u32[]{:S(2)}) %collective-permute-start.40) | collective-permute-done | bytes 65568 | tf_op jit(solution)/shard_map/ppermute | solution.py:170
  109.0 1.7 %collective-permute-start.42 = (f32[128,128]{1,0:T(8,128)S(1)}, f32[128,128]{1,0:T(8,128)S(1)}, u32[]{:S(2)}, u32[]{:S(2)}) collective-permute-start(f32[128,128]{1,0:T(8,128)S(1)} %get-tuple-element.43), channel_id=1, source_target_pairs={{4,0},{8,4},{12,8},{0,12},{5,1},{9,5},{13,9},{1,13},{6,2},{10,6},{... | collective-permute-start | bytes 196616 | tf_op jit(solution)/shard_map/ppermute | solution.py:170
  110.8 1.9 %collective-permute-done.41.refs_3_ = f32[128,128]{1,0:T(8,128)S(1)} collective-permute-done((f32[128,128]{1,0:T(8,128)S(1)}, f32[128,128]{1,0:T(8,128)S(1)}, u32[]{:S(2)}, u32[]{:S(2)}) %collective-permute-start.41) | collective-permute-done | bytes 65568 | tf_op jit(solution)/shard_map/ppermute | solution.py:170
  115.5 2.0 %collective-permute-done.44.back = f32[80,128]{1,0:T(8,128)S(1)} collective-permute-done((f32[80,128]{1,0:T(8,128)S(1)}, f32[80,128]{1,0:T(8,128)S(1)}, u32[]{:S(2)}, u32[]{:S(2)}) %collective-permute-start.44) | collective-permute-done | bytes 40992 | tf_op jit(solution)/shard_map/ppermute | solution.py:170
  117.5 12.1 %shard_map.62 = f32[24,32,128]{2,1,0:T(8,128)} custom-call(s32[8]{0:T(128)S(1)} %stack.59.flags, f32[1,32,40,128]{3,2,1,0:T(8,128)S(1)} %get-tuple-element.44.wide_ref, f32[80,128]{1,0:T(8,128)S(1)} %collective-permute-done.43.forth, f32[80,128]{1,0:T(8,128)S(1)} %collective-permute-done.44.back, f32[32,2,40,128]{3,2,1,0:T(8,128)S(1)} %get-tuple-element.46.inv_diag, ...), custom_call_target="tpu_custom_call" | custom-call | flops 1000000 | bytes 100000 | tf_op jit(solution)/shard_map/pallas_call | solution.py:27
  (92 shorter events, 42.6 us)
Async XLA Ops:
  4.5 8.3 %collective-permute-start = (f32[13,32,128]{2,1,0:T(8,128)S(1)}, f32[13,32,128]{2,1,0:T(8,128)S(1)}, u32[]{:S(2)}, u32[]{:S(2)}) collective-permute-start(f32[13,32,128]{2,1,0:T(8,128)S(1)} %shard_map.46), channel_id=1, source_target_pairs={{0,16},{16,0},{1,17},{17,1},{2,18},{18,2},{3,19},{19,3},{4,20},{20... | collective-permute-start | bytes 638984 | tf_op jit(solution)/shard_map/ppermute | solution.py:170
  13.4 5.5 %collective-permute-start.1 = (f32[416,128]{1,0:T(8,128)S(1)}, f32[416,128]{1,0:T(8,128)S(1)}, u32[]{:S(2)}, u32[]{:S(2)}) collective-permute-start(f32[416,128]{1,0:T(8,128)S(1)} %get-tuple-element.28), channel_id=1, source_target_pairs={{0,4},{4,8},{8,12},{12,0},{1,5},{5,9},{9,13},{13,1},{2,6},{6,10},{... | collective-permute-start | bytes 638984 | tf_op jit(solution)/shard_map/ppermute | solution.py:170
  13.5 6.8 %collective-permute-start.2 = (f32[416,128]{1,0:T(8,128)S(1)}, f32[416,128]{1,0:T(8,128)S(1)}, u32[]{:S(2)}, u32[]{:S(2)}) collective-permute-start(f32[416,128]{1,0:T(8,128)S(1)} %get-tuple-element.29), channel_id=1, source_target_pairs={{4,0},{8,4},{12,8},{0,12},{5,1},{9,5},{13,9},{1,13},{6,2},{10,6},{... | collective-permute-start | bytes 638984 | tf_op jit(solution)/shard_map/ppermute | solution.py:170
  21.8 5.4 %collective-permute-start.4 = (f32[264,128]{1,0:T(8,128)S(1)}, f32[264,128]{1,0:T(8,128)S(1)}, u32[]{:S(2)}, u32[]{:S(2)}) collective-permute-start(f32[264,128]{1,0:T(8,128)S(1)} %get-tuple-element.31), channel_id=1, source_target_pairs={{1,0},{2,1},{3,2},{7,3},{6,7},{5,6},{4,5},{0,4},{9,8},{10,9},{11,1... | collective-permute-start | bytes 405512 | tf_op jit(solution)/shard_map/ppermute | solution.py:170
  22.4 4.8 %collective-permute-start.3 = (f32[264,128]{1,0:T(8,128)S(1)}, f32[264,128]{1,0:T(8,128)S(1)}, u32[]{:S(2)}, u32[]{:S(2)}) collective-permute-start(f32[264,128]{1,0:T(8,128)S(1)} %get-tuple-element.31), channel_id=1, source_target_pairs={{0,1},{1,2},{2,3},{3,7},{7,6},{6,5},{5,4},{4,0},{8,9},{9,10},{10,1... | collective-permute-start | bytes 405512 | tf_op jit(solution)/shard_map/ppermute | solution.py:170
  44.2 14.5 %collective-permute-start.9 = (f32[8,128]{1,0:T(8,128)S(1)}, f32[8,128]{1,0:T(8,128)S(1)}, u32[]{:S(2)}, u32[]{:S(2)}) collective-permute-start(f32[8,128]{1,0:T(8,128)S(1)} %get-tuple-element.40.scaled_rhs.own), channel_id=1, source_target_pairs={{1,0},{2,1},{3,2},{7,3},{6,7},{5,6},{4,5},{0,4},{9,8},{10,9},{11,1... | collective-permute-start | bytes 12296 | tf_op jit(solution)/shard_map/ppermute | solution.py:170
  45.1 13.5 %collective-permute-start.8 = (f32[8,128]{1,0:T(8,128)S(1)}, f32[8,128]{1,0:T(8,128)S(1)}, u32[]{:S(2)}, u32[]{:S(2)}) collective-permute-start(f32[8,128]{1,0:T(8,128)S(1)} %get-tuple-element.40.scaled_rhs.own), channel_id=1, source_target_pairs={{0,1},{1,2},{2,3},{3,7},{7,6},{6,5},{5,4},{4,0},{8,9},{9,10},{10,1... | collective-permute-start | bytes 12296 | tf_op jit(solution)/shard_map/ppermute | solution.py:170
  46.7 12.0 %collective-permute-start.7 = (f32[8,128]{1,0:T(8,128)S(1)}, f32[8,128]{1,0:T(8,128)S(1)}, u32[]{:S(2)}, u32[]{:S(2)}) collective-permute-start(f32[8,128]{1,0:T(8,128)S(1)} %get-tuple-element.40.scaled_rhs.own), channel_id=1, source_target_pairs={{4,0},{8,4},{12,8},{0,12},{5,1},{9,5},{13,9},{1,13},{6,2},{10,6},{... | collective-permute-start | bytes 12296 | tf_op jit(solution)/shard_map/ppermute | solution.py:170
  47.7 11.0 %collective-permute-start.6 = (f32[8,128]{1,0:T(8,128)S(1)}, f32[8,128]{1,0:T(8,128)S(1)}, u32[]{:S(2)}, u32[]{:S(2)}) collective-permute-start(f32[8,128]{1,0:T(8,128)S(1)} %get-tuple-element.40.scaled_rhs.own), channel_id=1, source_target_pairs={{0,4},{4,8},{8,12},{12,0},{1,5},{5,9},{9,13},{13,1},{2,6},{6,10},{... | collective-permute-start | bytes 12296 | tf_op jit(solution)/shard_map/ppermute | solution.py:170
  47.7 11.0 %collective-permute-start.5 = (f32[8,128]{1,0:T(8,128)S(1)}, f32[8,128]{1,0:T(8,128)S(1)}, u32[]{:S(2)}, u32[]{:S(2)}) collective-permute-start(f32[8,128]{1,0:T(8,128)S(1)} %get-tuple-element.40.scaled_rhs.own), channel_id=1, source_target_pairs={{0,16},{16,0},{1,17},{17,1},{2,18},{18,2},{3,19},{19,3},{4,20},{20... | collective-permute-start | bytes 12296 | tf_op jit(solution)/shard_map/ppermute | solution.py:170
  59.4 3.6 %collective-permute-start.14 = (f32[8,128]{1,0:T(8,128)S(1)}, f32[8,128]{1,0:T(8,128)S(1)}, u32[]{:S(2)}, u32[]{:S(2)}) collective-permute-start(f32[8,128]{1,0:T(8,128)S(1)} %shard_map.51.own), channel_id=1, source_target_pairs={{1,0},{2,1},{3,2},{7,3},{6,7},{5,6},{4,5},{0,4},{9,8},{10,9},{11,1... | collective-permute-start | bytes 12296 | tf_op jit(solution)/shard_map/ppermute | solution.py:170
  62.4 3.6 %collective-permute-start.10 = (f32[8,128]{1,0:T(8,128)S(1)}, f32[8,128]{1,0:T(8,128)S(1)}, u32[]{:S(2)}, u32[]{:S(2)}) collective-permute-start(f32[8,128]{1,0:T(8,128)S(1)} %shard_map.51.own), channel_id=1, source_target_pairs={{0,16},{16,0},{1,17},{17,1},{2,18},{18,2},{3,19},{19,3},{4,20},{20... | collective-permute-start | bytes 12296 | tf_op jit(solution)/shard_map/ppermute | solution.py:170
  66.7 3.6 %collective-permute-start.19 = (f32[8,128]{1,0:T(8,128)S(1)}, f32[8,128]{1,0:T(8,128)S(1)}, u32[]{:S(2)}, u32[]{:S(2)}) collective-permute-start(f32[8,128]{1,0:T(8,128)S(1)} %shard_map.52.own), channel_id=1, source_target_pairs={{1,0},{2,1},{3,2},{7,3},{6,7},{5,6},{4,5},{0,4},{9,8},{10,9},{11,1... | collective-permute-start | bytes 12296 | tf_op jit(solution)/shard_map/ppermute | solution.py:170
  73.6 3.6 %collective-permute-start.24 = (f32[8,128]{1,0:T(8,128)S(1)}, f32[8,128]{1,0:T(8,128)S(1)}, u32[]{:S(2)}, u32[]{:S(2)}) collective-permute-start(f32[8,128]{1,0:T(8,128)S(1)} %shard_map.53.own), channel_id=1, source_target_pairs={{1,0},{2,1},{3,2},{7,3},{6,7},{5,6},{4,5},{0,4},{9,8},{10,9},{11,1... | collective-permute-start | bytes 12296 | tf_op jit(solution)/shard_map/ppermute | solution.py:170
  76.2 3.6 %collective-permute-start.20 = (f32[8,128]{1,0:T(8,128)S(1)}, f32[8,128]{1,0:T(8,128)S(1)}, u32[]{:S(2)}, u32[]{:S(2)}) collective-permute-start(f32[8,128]{1,0:T(8,128)S(1)} %shard_map.53.own), channel_id=1, source_target_pairs={{0,16},{16,0},{1,17},{17,1},{2,18},{18,2},{3,19},{19,3},{4,20},{20... | collective-permute-start | bytes 12296 | tf_op jit(solution)/shard_map/ppermute | solution.py:170
  80.5 3.6 %collective-permute-start.29 = (f32[8,128]{1,0:T(8,128)S(1)}, f32[8,128]{1,0:T(8,128)S(1)}, u32[]{:S(2)}, u32[]{:S(2)}) collective-permute-start(f32[8,128]{1,0:T(8,128)S(1)} %shard_map.54.own), channel_id=1, source_target_pairs={{1,0},{2,1},{3,2},{7,3},{6,7},{5,6},{4,5},{0,4},{9,8},{10,9},{11,1... | collective-permute-start | bytes 12296 | tf_op jit(solution)/shard_map/ppermute | solution.py:170
  87.4 3.6 %collective-permute-start.34 = (f32[8,128]{1,0:T(8,128)S(1)}, f32[8,128]{1,0:T(8,128)S(1)}, u32[]{:S(2)}, u32[]{:S(2)}) collective-permute-start(f32[8,128]{1,0:T(8,128)S(1)} %shard_map.55.own), channel_id=1, source_target_pairs={{1,0},{2,1},{3,2},{7,3},{6,7},{5,6},{4,5},{0,4},{9,8},{10,9},{11,1... | collective-permute-start | bytes 12296 | tf_op jit(solution)/shard_map/ppermute | solution.py:170
  89.9 3.6 %collective-permute-start.30 = (f32[8,128]{1,0:T(8,128)S(1)}, f32[8,128]{1,0:T(8,128)S(1)}, u32[]{:S(2)}, u32[]{:S(2)}) collective-permute-start(f32[8,128]{1,0:T(8,128)S(1)} %shard_map.55.own), channel_id=1, source_target_pairs={{0,16},{16,0},{1,17},{17,1},{2,18},{18,2},{3,19},{19,3},{4,20},{20... | collective-permute-start | bytes 12296 | tf_op jit(solution)/shard_map/ppermute | solution.py:170
  94.3 3.6 %collective-permute-start.39 = (f32[8,128]{1,0:T(8,128)S(1)}, f32[8,128]{1,0:T(8,128)S(1)}, u32[]{:S(2)}, u32[]{:S(2)}) collective-permute-start(f32[8,128]{1,0:T(8,128)S(1)} %shard_map.56.own), channel_id=1, source_target_pairs={{1,0},{2,1},{3,2},{7,3},{6,7},{5,6},{4,5},{0,4},{9,8},{10,9},{11,1... | collective-permute-start | bytes 12296 | tf_op jit(solution)/shard_map/ppermute | solution.py:170
  96.8 3.6 %collective-permute-start.35 = (f32[8,128]{1,0:T(8,128)S(1)}, f32[8,128]{1,0:T(8,128)S(1)}, u32[]{:S(2)}, u32[]{:S(2)}) collective-permute-start(f32[8,128]{1,0:T(8,128)S(1)} %shard_map.56.own), channel_id=1, source_target_pairs={{0,16},{16,0},{1,17},{17,1},{2,18},{18,2},{3,19},{19,3},{4,20},{20... | collective-permute-start | bytes 12296 | tf_op jit(solution)/shard_map/ppermute | solution.py:170
  104.1 4.3 %collective-permute-start.40 = (f32[4,32,128]{2,1,0:T(8,128)S(1)}, f32[4,32,128]{2,1,0:T(8,128)S(1)}, u32[]{:S(2)}, u32[]{:S(2)}) collective-permute-start(f32[4,32,128]{2,1,0:T(8,128)S(1)} %shard_map.59), channel_id=1, source_target_pairs={{0,16},{16,0},{1,17},{17,1},{2,18},{18,2},{3,19},{19,3},{4,20},{20... | collective-permute-start | bytes 196616 | tf_op jit(solution)/shard_map/ppermute | solution.py:170
  109.0 3.7 %collective-permute-start.41 = (f32[128,128]{1,0:T(8,128)S(1)}, f32[128,128]{1,0:T(8,128)S(1)}, u32[]{:S(2)}, u32[]{:S(2)}) collective-permute-start(f32[128,128]{1,0:T(8,128)S(1)} %get-tuple-element.42), channel_id=1, source_target_pairs={{0,4},{4,8},{8,12},{12,0},{1,5},{5,9},{9,13},{13,1},{2,6},{6,10},{... | collective-permute-start | bytes 196616 | tf_op jit(solution)/shard_map/ppermute | solution.py:170
  109.0 3.7 %collective-permute-start.42 = (f32[128,128]{1,0:T(8,128)S(1)}, f32[128,128]{1,0:T(8,128)S(1)}, u32[]{:S(2)}, u32[]{:S(2)}) collective-permute-start(f32[128,128]{1,0:T(8,128)S(1)} %get-tuple-element.43), channel_id=1, source_target_pairs={{4,0},{8,4},{12,8},{0,12},{5,1},{9,5},{13,9},{1,13},{6,2},{10,6},{... | collective-permute-start | bytes 196616 | tf_op jit(solution)/shard_map/ppermute | solution.py:170
  113.5 4.0 %collective-permute-start.44 = (f32[80,128]{1,0:T(8,128)S(1)}, f32[80,128]{1,0:T(8,128)S(1)}, u32[]{:S(2)}, u32[]{:S(2)}) collective-permute-start(f32[80,128]{1,0:T(8,128)S(1)} %get-tuple-element.45), channel_id=1, source_target_pairs={{1,0},{2,1},{3,2},{7,3},{6,7},{5,6},{4,5},{0,4},{9,8},{10,9},{11,1... | collective-permute-start | bytes 122888 | tf_op jit(solution)/shard_map/ppermute | solution.py:170
  (25 other events, 63.9 us)

commit v2 on v0

v2 whole, which is shorter than its diff:
```python
import functools

import jax
import jax.numpy as jnp
from jax import lax
from jax.experimental import pallas as pl
from jax.experimental.pallas import tpu as pltpu
from jax.sharding import PartitionSpec as P

AGG = 128
LANES = 128
SUB = 8
HALO = 4
WIDTHS = (4, 3, 3)
POST = 4
KC = 8
OMEGA_FINE = 0.8
OMEGA_COARSE = 0.7
F32 = jnp.float32
BF16 = jnp.bfloat16
SMEM = pl.BlockSpec(memory_space=pltpu.SMEM)
VMEM = pl.BlockSpec(memory_space=pltpu.VMEM)
IX, PARITY, X_LOW, X_HIGH, Y_LOW, Y_HIGH, Z_LOW, Z_HIGH = range(8)


def call(kernel, outs, scratch=(), limit=16, flops=10**6, in_specs=None):
    def run(flags, *arrays):
        return pl.pallas_call(
            kernel,
            out_shape=outs,
            in_specs=[SMEM] + (in_specs or [VMEM] * len(arrays)),
            out_specs=jax.tree.map(lambda _: VMEM, outs),
            scratch_shapes=list(scratch),
            compiler_params=pltpu.CompilerParams(vmem_limit_bytes=limit * 2**20),
            cost_estimate=pl.CostEstimate(flops=flops, bytes_accessed=10**5, transcendentals=0),
        )(flags, *arrays)

    return run


def shaped(*shape):
    return jax.ShapeDtypeStruct(shape, F32)


def lane_no(shape):
    return lax.broadcasted_iota(jnp.int32, shape, len(shape) - 1)


def row_no(shape):
    return lax.broadcasted_iota(jnp.int32, shape, len(shape) - 2)


def turned(values, shift, axis):
    if isinstance(shift, int):
        shift = shift % values.shape[axis]
        if shift == 0:
            return values
    return pltpu.roll(values, shift, axis)


def picked(values, index):
    return jnp.take_along_axis(values, index, axis=1, mode="promise_in_bounds")


class Frame:
    def __init__(self, nx, ny):
        self.nx, self.ny = nx, ny
        self.wide, self.tall = nx + 2 * HALO, ny + 2 * HALO
        self.rows = self.tall + 2 * SUB
        self.span = pl.ds(SUB, self.tall)
        self.own = SUB + HALO
        self.main = (self.wide, self.rows, LANES)
        self.ends = (2, self.rows, LANES)


def bases(widths):
    return [sum(widths[:f]) for f in range(len(widths) + 1)]


def pack_x_kernel(count, widths, flags, *refs):
    fields = len(widths)
    ins, labels, outs = refs[:fields], refs[fields], refs[fields + 1 : -2]
    near, sems = refs[-2:]
    nx, ny = ins[0].shape[0], ins[0].shape[1]
    base = bases(widths)
    copies = []
    for s, out in enumerate(outs):
        for f, (ref, width) in enumerate(zip(ins, widths)):
            if count == 2:
                at = jnp.where(flags[IX] == 0, nx - width, 0)
            else:
                at = (nx - width, 0)[s]
            copies.append(
                pltpu.make_async_copy(
                    ref.at[pl.ds(at, width)], out.at[pl.ds(base[f], width)], sems.at[len(copies)]
                )
            )
        if count == 2:
            at = jnp.where(flags[IX] == 0, nx // 2 - 1, 0)
        else:
            at = (nx // 2 - 1, 0)[s]
        copies.append(pltpu.make_async_copy(labels.at[at], near.at[s], sems.at[len(copies)]))
    for copy in copies:
        copy.start()
    for copy in copies:
        copy.wait()
    for s, out in enumerate(outs):
        out[base[-1]] = jnp.zeros(out.shape[1:], F32)
        out[base[-1], : ny // 2, : near.shape[2]] = near[s].astype(F32)


def slab_of(own, low, high, base, width, x):
    nx = own.shape[0]
    if HALO <= x < HALO + nx:
        return own[x - HALO]
    if x < HALO:
        at = x - (HALO - width)
        return low[base + at] if at >= 0 else None
    at = x - HALO - nx
    return high[base + at] if at < width else None


def pack_y_kernel(widths, labels, flags, *refs):
    fields = len(widths)
    ins = refs[:fields]
    low, high = refs[fields + labels : fields + labels + 2]
    to_high, to_low = refs[fields + labels + 2 :]
    nx, ny = ins[0].shape[0], ins[0].shape[1]
    frame = Frame(nx, ny)
    base = bases(widths)
    for f in range(fields):
        for x in range(frame.wide):
            slab = slab_of(ins[f], low, high, base[f], widths[f], x)
            at = (f * frame.wide + x) * HALO
            if slab is None:
                slab = jnp.ones((ny, LANES), F32)
            to_high[at : at + HALO] = slab[ny - HALO :]
            to_low[at : at + HALO] = slab[:HALO]
    if labels:
        at = fields * frame.wide * HALO
        nb, rows, width = refs[fields].shape
        for out, row in ((to_high, rows - 1), (to_low, 0)):
            out[at:] = jnp.zeros((out.shape[0] - at, LANES), F32)
            for b in range(nb):
                out[at + b : at + b + 1, :width] = refs[fields][b, row : row + 1].astype(F32)


def pack_z_kernel(widths, labels, flags, *refs):
    fields = len(widths)
    ins = refs[:fields]
    x_low, x_high, y_low, y_high = refs[fields + labels : fields + labels + 4]
    wide_ref, send_forth, send_back = refs[fields + labels + 4 :]
    nx, ny = ins[0].shape[0], ins[0].shape[1]
    frame = Frame(nx, ny)
    base = bases(widths)
    tall, own = frame.tall, frame.own
    even = flags[PARITY] == 0

    def send(at, count, to_high, to_low):
        send_forth[at : at + count] = jnp.where(even, to_high, to_low)
        send_back[at : at + count] = jnp.where(even, to_low, to_high)

    group = lane_no((tall, LANES)) // HALO
    spare = jnp.ones((SUB, LANES), F32)
    for f in range(fields):
        to_high = to_low = jnp.ones((tall, LANES), F32)
        for x in range(frame.wide):
            at = (f * frame.wide + x) * HALO
            slab = slab_of(ins[f], x_low, x_high, base[f], widths[f], x)
            wide_ref[f, x, own : own + ny] = jnp.ones((ny, LANES), F32) if slab is None else slab
            wide_ref[f, x, SUB:own] = y_low[at : at + HALO]
            wide_ref[f, x, own + ny : own + ny + HALO] = y_high[at : at + HALO]
            wide_ref[f, x, :SUB] = spare
            wide_ref[f, x, SUB + tall :] = spare
            moved = turned(wide_ref[f, x, SUB : SUB + tall], HALO * (x + 1), 1)
            to_high = jnp.where(group == x, moved, to_high)
            to_low = jnp.where(group == (x + 1) % frame.wide, moved, to_low)
        send(f * tall, tall, to_high, turned(to_low, -HALO, 1))
    if labels:
        nb, rows, width = refs[fields].shape
        lane = lane_no((rows, LANES))
        to_high = to_low = jnp.zeros((rows, LANES), F32)
        for b in range(nb):
            slab = refs[fields][b].astype(F32)
            to_high = jnp.where(lane == b, slab[:, width - 1 :], to_high)
            to_low = jnp.where(lane == b, slab[:, :1], to_low)
        send(fields * tall, rows, to_high, to_low)


class Links:
    def __init__(self, mesh):
        self.sizes = [mesh.shape[a] for a in ("gx", "gy", "gz")]
        n_x, n_y, n_z = self.sizes
        self.ring_x = [(i, (i + 1) % n_x) for i in range(n_x)]
        self.ring_y = [(i, (i + 1) % n_y) for i in range(n_y)]
        self.snake = []
        for i in range(n_x):
            for j in range(0, n_y, 2):
                nodes = [(i * n_y + j) * n_z + k for k in range(n_z)]
                nodes += [(i * n_y + j + 1) * n_z + k for k in reversed(range(n_z))]
                self.snake += [(nodes[m], nodes[(m + 1) % len(nodes)]) for m in range(len(nodes))]

    @staticmethod
    def back(pairs):
        return [(b, a) for a, b in pairs]

    def x(self, sends):
        if self.sizes[0] == 2:
            got = lax.ppermute(sends[0], "gx", self.ring_x)
            return got, got
        return lax.ppermute(sends[0], "gx", self.ring_x), lax.ppermute(sends[-1], "gx", self.back(self.ring_x))

    def y(self, to_high, to_low):
        return lax.ppermute(to_high, "gy", self.ring_y), lax.ppermute(to_low, "gy", self.back(self.ring_y))

    def z(self, forth, back):
        axes = ("gx", "gy", "gz")
        return lax.ppermute(forth, axes, self.snake), lax.ppermute(back, axes, self.back(self.snake))


def widened(links, flags, widths, arrays, from_x):
    fields, labels = len(widths), len(arrays) - len(widths)
    nx, ny, nz = arrays[0].shape
    frame = Frame(nx, ny)
    rows = fields * frame.wide * HALO + labels * ny // 2
    sends = call(functools.partial(pack_y_kernel, widths, labels), [shaped(rows, nz)] * 2)(flags, *arrays, *from_x)
    from_y = links.y(*sends)
    rows = fields * frame.tall + labels * ny // 2
    wide, *sends = call(
        functools.partial(pack_z_kernel, widths, labels), [shaped(fields, *frame.main)] + [shaped(rows, nz)] * 2
    )(flags, *arrays, *from_x, *from_y)
    return (wide, *links.z(*sends)), from_y


def sides(flags, forth, back):
    even = flags[PARITY] == 0
    return jnp.where(even, forth, back), jnp.where(even, back, forth)


def weight(one, two):
    return 2.0 * (one * two) / (one + two)


def lane_mask(x):
    return ((lane_no((1, LANES)) - (HALO * x + HALO - 1)) & (LANES - 1)) < 2


def edge_step(here, x, edges):
    return jnp.where(lane_mask(x), turned(here, HALO * x + HALO, 1), edges)


def joined(below, above):
    lane = lane_no(below.shape)
    return jnp.where(lane % HALO == HALO - 1, below, turned(above, HALO, 1))


def next_and_last(here, join, x):
    lane = lane_no((1, LANES))
    edge = turned(join, (LANES - HALO) - HALO * x, 1)
    upper = turned(jnp.where(lane == 0, edge, here), -1, 1)
    lower = turned(jnp.where(lane == LANES - 1, edge, here), 1, 1)
    return upper, lower


def ends_near(below, above, edges):
    layer = lane_no((1, LANES)) % HALO
    return (
        jnp.where(layer == HALO - 1, turned(edges, -1, 1), turned(below, -1, 1)),
        turned(below, 1, 1),
        turned(above, -1, 1),
        jnp.where(layer == 0, turned(edges, 1 - HALO, 1), turned(above, 1, 1)),
    )


def main_sum(frame, field, x, join, wx, wy, wz_up, wz_low):
    span = frame.span
    upper, lower = next_and_last(field[x, span], join, x)
    total = wx[x, span] * field[x + 1, span] + wx[x - 1, span] * field[x - 1, span]
    total = total + wy[x, span] * field[x, pl.ds(SUB + 1, frame.tall)]
    down = pl.ds(SUB - 1, frame.tall)
    total = total + wy[x, down] * field[x, down]
    return total + wz_up[x, span] * upper + wz_low[x, span] * lower


def ends_sum(frame, ends, s, upper, lower, wx, wy, wz_up, wz_low):
    span, down = frame.span, pl.ds(SUB - 1, frame.tall)
    here = ends[s, span]
    total = wx[s, span] * turned(here, -HALO, 1) + turned(wx[s, span] * here, HALO, 1)
    total = total + wy[s, span] * ends[s, pl.ds(SUB + 1, frame.tall)] + wy[s, down] * ends[s, down]
    return total + wz_up[s, span] * upper + wz_low[s, span] * lower


def clear_spares(ref, frame):
    for x in range(ref.shape[0]):
        ref[x, :SUB] = jnp.zeros((SUB, LANES), F32)
        ref[x, SUB + frame.tall :] = jnp.zeros((SUB, LANES), F32)


def pack_rows(values):
    half = values.shape[0] // 2
    lane = lane_no((half, LANES))
    return jnp.where(lane < LANES // 2, values[:half], turned(values[half:], LANES // 2, 1))


def lane_total(values):
    ones = jnp.ones((SUB, LANES), F32)
    return lax.dot_general(
        ones, values, (((1,), (1,)), ((), ())), precision=lax.Precision.HIGHEST, preferred_element_type=F32
    )


def paired(values):
    even = 2 * (lane_no(values.shape) % (LANES // 2))
    return picked(values + turned(values, -1, 1), even)


def fine_kernel(flags, wide_ref, forth, back, from_x_low, from_x_high, from_y_low, from_y_high, block_label,
                face_label, inner_diag, *refs):
    main, ends = refs[:6], refs[6:12]
    pre, face_near, face_weight, scaled_rhs, scale, once, once_ends, res = refs[12:]
    wx, wy, wz_up, wz_low, inv_diag, start = main
    ex, ey, ez_up, ez_low, inv_ends, start_ends = ends
    nx, ny = pre.shape[0], pre.shape[1]
    frame = Frame(nx, ny)
    wide, tall, span = frame.wide, frame.tall, frame.span
    last = HALO + nx
    got = [sides(flags, forth[f * tall : (f + 1) * tall], back[f * tall : (f + 1) * tall]) for f in range(3)]
    (cond_below, cond_above), rhs_ends, absorb_ends = got
    for ref in (wy, start, once):
        clear_spares(ref, frame)
    for ref in (ey, start_ends, once_ends):
        clear_spares(ref, frame)

    row = row_no((tall, LANES))
    lane = lane_no((1, LANES))
    keep_y = jnp.where(
        row == HALO - 1, flags[Y_LOW], jnp.where(row == HALO + ny - 1, flags[Y_HIGH], 1)
    ).astype(F32)
    keep_low, keep_high = flags[Z_LOW].astype(F32), flags[Z_HIGH].astype(F32)

    def cond_edges(x, edges):
        return edge_step(wide_ref[0, x, span], x, edges)

    edges = lax.fori_loop(0, wide, cond_edges, jnp.ones((tall, LANES), F32), unroll=4)
    near = ends_near(cond_below, cond_above, edges)
    slab = lane // HALO
    keep_x = jnp.where(
        slab == HALO - 1, flags[X_LOW], jnp.where(slab == last - 1, flags[X_HIGH], 1)
    ).astype(F32)
    layer = lane % HALO
    for s, here in enumerate((cond_below, cond_above)):
        up, low = weight(here, near[2 * s]), weight(here, near[2 * s + 1])
        if s == 0:
            up = up * jnp.where(layer == HALO - 1, keep_low, 1.0)
        else:
            low = low * jnp.where(layer == 0, keep_high, 1.0)
        face_x = keep_x * weight(here, turned(here, -HALO, 1))
        face_y = keep_y * weight(here, turned(here, -1, 0))
        ex[s, span], ey[s, span], ez_up[s, span], ez_low[s, span] = face_x, face_y, up, low
        total = absorb_ends[s] + face_x + turned(face_x, HALO, 1) + face_y + turned(face_y, 1, 0) + up + low
        inverse = OMEGA_FINE / total
        inv_ends[s, span] = inverse
        start_ends[s, span] = inverse * rhs_ends[s]

    join = joined(cond_below, cond_above)
    wz_under = ez_up[0, span]

    def fields(x, carry):
        before, edges = carry
        here = wide_ref[0, x, span]
        keep = jnp.where(x == HALO - 1, flags[X_LOW], jnp.where(x == last - 1, flags[X_HIGH], 1)).astype(F32)
        edge = turned(join, (LANES - HALO) - HALO * x, 1)
        upper = turned(jnp.where(lane == 0, edge, here), -1, 1)
        face_x = keep * weight(here, wide_ref[0, jnp.minimum(x + 1, wide - 1), span])
        face_y = keep_y * weight(here, wide_ref[0, x, pl.ds(SUB + 1, tall)])
        up = weight(here, upper) * jnp.where(lane == LANES - 1, keep_high, 1.0)
        under = turned(wz_under, (LANES - HALO) - HALO * x, 1)
        low = turned(jnp.where(lane == LANES - 1, under, up), 1, 1)
        total = wide_ref[2, x, span] + face_x + before + face_y + turned(face_y, 1, 0) + up + low
        inverse = OMEGA_FINE / total
        begin = inverse * wide_ref[1, x, span]
        for ref, values in zip(main, (face_x, face_y, up, low, inverse, begin)):
            ref[x, span] = values
        return face_x, edge_step(begin, x, edges)

    nothing = jnp.zeros((tall, LANES), F32)
    _, edges = lax.fori_loop(0, wide, fields, (nothing, nothing))

    join = joined(start_ends[0, span], start_ends[1, span])
    near = ends_near(start_ends[0, span], start_ends[1, span], edges)
    for s in range(2):
        total = ends_sum(frame, start_ends, s, near[2 * s], near[2 * s + 1], ex, ey, ez_up, ez_low)
        once_ends[s, span] = (2.0 - OMEGA_FINE) * start_ends[s, span] + inv_ends[s, span] * total

    @pl.loop(HALO - 1, last + 1)
    def _(x):
        total = main_sum(frame, start, x, join, wx, wy, wz_up, wz_low)
        once[x, span] = (2.0 - OMEGA_FINE) * start[x, span] + inv_diag[x, span] * total

    join2 = joined(once_ends[0, span], once_ends[1, span])

    @pl.loop(HALO, last)
    def _(x):
        total = main_sum(frame, once, x, join2, wx, wy, wz_up, wz_low)
        full = wide_ref[1, x, span] - (OMEGA_FINE / inv_diag[x, span]) * once[x, span] + total
        res[x - HALO, span] = full
        pre[x - HALO] = once[x, pl.ds(frame.own, ny)]

    nb, half, width = nx // 2, ny // 2, LANES // 2
    iota = row_no((AGG, LANES)).astype(F32)

    def rows_at(ref, x, off):
        return ref[x, pl.ds(frame.own + off, half, stride=2)]

    def add_rows(total, labels, values, rows):
        for r in range(rows):
            total = total + jnp.where(labels[r : r + 1] == iota, values[r : r + 1], 0.0)
        return total

    def restrict(b, total):
        four = sum(rows_at(res, 2 * b + a, c) for a in range(2) for c in range(2))
        return add_rows(total, block_label[b], pack_rows(paired(four)), SUB)

    zeros = jnp.zeros((AGG, LANES), F32)
    sums = lax.fori_loop(0, nb, restrict, zeros)

    blank = jnp.zeros((half - nb, LANES), F32)
    low_at, high_at = pl.ds(frame.own - 1, 1), pl.ds(frame.own + ny - 1, 1)
    face_weight[0] = pack_rows(paired(rows_at(wx, HALO - 1, 0) + rows_at(wx, HALO - 1, 1)))
    face_weight[1] = pack_rows(paired(rows_at(wx, last - 1, 0) + rows_at(wx, last - 1, 1)))
    for s, at in ((2, low_at), (3, high_at)):
        lines = [wy[HALO + 2 * b, at] + wy[HALO + 2 * b + 1, at] for b in range(nb)]
        face_weight[s] = pack_rows(paired(jnp.concatenate(lines + [blank], axis=0)))
    lane = lane_no((half, LANES))
    for s, (ref, side, layer_at) in ((4, (ez_up, 0, HALO - 1)), (5, (ez_low, 1, 0))):
        values = rows_at(ref, side, 0) + rows_at(ref, side, 1)
        values = values + turned(values, -HALO, 1)
        spot = jnp.minimum(2 * HALO * lane + HALO * HALO + layer_at, LANES - 1)
        face_weight[s] = pack_rows(jnp.where(lane < nb, picked(values, spot), 0.0))
    around = zeros
    for s in range(6):
        around = add_rows(around, face_label[s], face_weight[s], SUB)
    scale[...] = OMEGA_COARSE / (inner_diag[...] + lane_total(around))
    scaled_rhs[...] = scale[...] * lane_total(sums)

    at = sum(WIDTHS)
    face_near[0] = pack_rows(from_x_low[at, :half])
    face_near[1] = pack_rows(from_x_high[at, :half])
    at = 3 * wide * HALO
    face_near[2] = pack_rows(from_y_low[at : at + half])
    face_near[3] = pack_rows(from_y_high[at : at + half])
    below, above = sides(flags, forth[3 * tall : 3 * tall + half], back[3 * tall : 3 * tall + half])
    face_near[4] = pack_rows(below)
    face_near[5] = pack_rows(above)


def tile_product(left, right, labels, pairs):
    iota = row_no((AGG, LANES)).astype(F32)
    for r in range(SUB):
        lanes = pl.ds(r * LANES, LANES)
        left[:, lanes] = jnp.where(labels[r : r + 1] == iota, 1.0, 0.0).astype(BF16)
        held = sum(jnp.where(near[r : r + 1] == iota, w[r : r + 1], 0.0) for near, w in pairs)
        high = held.astype(BF16)
        right[:AGG, lanes] = high
        right[AGG:, lanes] = (held - high.astype(F32)).astype(BF16)
    return lax.dot_general(left[...], right[...], (((1,), (1,)), ((), ())), preferred_element_type=F32)


def keep_tile(out, at, tile):
    high = tile.astype(BF16)
    out[pl.ds(at, AGG), :AGG] = high
    out[pl.ds(at, AGG), AGG:] = (tile - high.astype(F32)).astype(BF16)


def own_kernel(flags, cond, absorb, block_agg, out, block_label, face_label, inner_diag, part, line, left, right):
    nx, ny = cond.shape[0], cond.shape[1]
    nb, half, width = nx // 2, ny // 2, LANES // 2
    lane, row = lane_no((half, LANES)), row_no((half, LANES))
    even = 2 * (lane % width)
    iota = row_no((AGG, LANES)).astype(F32)
    line[...] = jnp.zeros(line.shape, F32)

    def halves(values, slot):
        part[slot] = values
        return part[slot, pl.ds(0, half, stride=2)], part[slot, pl.ds(1, half, stride=2)]

    def label_at(b):
        values = block_agg[b].astype(F32)
        return jnp.concatenate([values, values], axis=1)

    def step(b, carry):
        low_x, tile, around = carry
        x = 2 * b
        one, two, three = cond[x], cond[x + 1], cond[jnp.minimum(x + 2, nx - 1)]
        faces_x = sum(halves(weight(two, three), 0))
        both_y = weight(one, turned(one, -1, 0)) + weight(two, turned(two, -1, 0))
        both_z = weight(one, turned(one, -1, 1)) + weight(two, turned(two, -1, 1))
        end_x, end_y, end_z = b == nb - 1, row == half - 1, lane % width == width - 1
        high_x = jnp.where(end_x, 0.0, paired(faces_x))
        high_y = jnp.where(end_y, 0.0, paired(halves(both_y, 1)[1]))
        high_z = jnp.where(end_z, 0.0, picked(sum(halves(both_z, 2)), even + 1))
        low_y = turned(high_y, 1, 0)
        low_z = turned(high_z, 1, 1)
        own = label_at(b)
        near_x, past_x = label_at(jnp.minimum(b + 1, nb - 1)), label_at(jnp.maximum(b - 1, 0))
        near_y, past_y = turned(own, -1, 0), turned(own, 1, 0)
        near_z, past_z = turned(own, -1, 1), turned(own, 1, 1)
        total = paired(sum(halves(absorb[x] + absorb[x + 1], 3)))
        for near, values in (
            (near_x, high_x), (past_x, low_x), (near_y, high_y), (past_y, low_y), (near_z, high_z), (past_z, low_z)
        ):
            total = total + jnp.where(near != own, values, 0.0)
        packed, total = pack_rows(own), pack_rows(total)
        block_label[b] = packed
        pairs = [
            (pack_rows(near_x), pack_rows(high_x)),
            (pack_rows(near_y), pack_rows(high_y)),
            (pack_rows(near_z), pack_rows(high_z)),
        ]
        tile = tile + tile_product(left, right, packed, pairs)
        for r in range(SUB):
            around = around + jnp.where(packed[r : r + 1] == iota, total[r : r + 1], 0.0)
        line[0, pl.ds(b, 1)], line[1, pl.ds(b, 1)] = own[:1], own[half - 1 :]
        line[2] = jnp.where(lane == b, own[:, :1], line[2])
        line[3] = jnp.where(lane == b, own[:, width - 1 : width], line[3])
        return high_x, tile, around

    nothing = jnp.zeros((half, LANES), F32)
    _, tile, around = lax.fori_loop(
        0, nb, step, (nothing, jnp.zeros((AGG, 2 * AGG), F32), jnp.zeros((AGG, LANES), F32))
    )
    tile = tile[:, :AGG] + tile[:, AGG:]
    keep_tile(out, 0, jnp.where(row_no((AGG, AGG)) == lane_no((AGG, AGG)), 0.0, tile + tile.T))
    inner_diag[...] = lane_total(around)
    face_label[0], face_label[1] = block_label[0], block_label[nb - 1]
    for s in range(4):
        face_label[2 + s] = pack_rows(line[s])


def faces_kernel(flags, own, face_label, face_near, face_weight, out, left, right):
    out[:AGG] = own[...]

    @pl.loop(0, 6)
    def _(s):
        tile = tile_product(left, right, face_near[s], [(face_label[s], face_weight[s])])
        keep_tile(out, (s + 1) * AGG, tile[:, :AGG] + tile[:, AGG:])


def turn_kernel(flags, tiles, scaled_rhs, scale, own, x_low, x_high, y_low, y_high, forth, back, out):
    vectors = [own[...], x_low[...], x_high[...], y_low[...], y_high[...], *sides(flags, forth[...], back[...])]
    row = row_no((SUB, AGG))
    parts = []
    for v in vectors:
        high = v.astype(BF16).astype(F32)
        parts.append(jnp.where(row == 0, high, jnp.where(row == 1, v - high, 0.0)).astype(BF16))
    got = jnp.dot(jnp.concatenate(parts, axis=1), tiles[...], preferred_element_type=F32)
    applied = jnp.sum(got[:, :AGG] + got[:, AGG:], axis=0, keepdims=True)
    out[...] = (1.0 - OMEGA_COARSE) * own[...] + scaled_rhs[...] + scale[...] * applied


def lifted(pre, block_agg, table, out, b, at):
    half = pre.shape[1] // 2
    labels = block_agg[b]
    labels = jnp.concatenate([labels, labels], axis=1)
    labels = picked(labels, lane_no((half, LANES)) // 2)
    values = picked(table, labels)
    for a in range(2):
        for c in range(2):
            rows = pl.ds(c, half, stride=2)
            out[at + a, rows] = pre[2 * b + a, rows] + values


def send_kernel(count, flags, pre, block_agg, coarse, *outs):
    nb, half = pre.shape[0] // 2, pre.shape[1] // 2
    table = jnp.broadcast_to(coarse[:1], (half, LANES))
    for s, out in enumerate(outs):
        for h in range(HALO // 2):
            if count == 2:
                b = jnp.where(flags[IX] == 0, nb - HALO // 2 + h, h)
            else:
                b = (nb - HALO // 2 + h, h)[s]
            lifted(pre, block_agg, table, out, b, 2 * h)


def correct_kernel(flags, pre, block_agg, coarse, out):
    table = jnp.broadcast_to(coarse[:1], (pre.shape[1] // 2, LANES))

    @pl.loop(0, pre.shape[0] // 2)
    def _(b):
        lifted(pre, block_agg, table, out, b, 2 * b)


def post_kernel(flags, wide_ref, forth, back, *refs):
    main, ends = refs[:6], refs[6:12]
    out, one, two, one_ends, two_ends = refs[12:]
    nx, ny = out.shape[0], out.shape[1]
    frame = Frame(nx, ny)
    wide, tall, span = frame.wide, frame.tall, frame.span
    wx, wy, wz_up, wz_low, inv_diag, start = main
    ex, ey, ez_up, ez_low, inv_ends, start_ends = ends
    for ref in (one, two, one_ends, two_ends):
        clear_spares(ref, frame)
    below, above = sides(flags, forth[...], back[...])
    two_ends[0, span], two_ends[1, span] = below, above
    kept = 1.0 - OMEGA_FINE
    buffers = ((wide_ref.at[0], two_ends), (one, one_ends), (two, two_ends), (one, one_ends))
    for s in range(POST):
        src, src_ends = buffers[s]
        join = joined(src_ends[0, span], src_ends[1, span])
        final = s == POST - 1
        dst, dst_ends = (None, None) if final else buffers[s + 1]

        def step(x, edges, src=src, join=join, dst=dst, final=final):
            here = src[x, span]
            total = main_sum(frame, src, x, join, wx, wy, wz_up, wz_low)
            new = kept * here + start[x, span] + inv_diag[x, span] * total
            if final:
                out[x - HALO] = new[HALO : HALO + ny]
                return edges
            dst[x, span] = new
            return edge_step(here, x, edges)

        edges = jnp.zeros((tall, LANES), F32)
        edges = lax.fori_loop(s + 1, wide - s - 1, step, edges)
        if not final:
            near = ends_near(src_ends[0, span], src_ends[1, span], edges)
            news = []
            for e in range(2):
                total = ends_sum(frame, src_ends, e, near[2 * e], near[2 * e + 1], ex, ey, ez_up, ez_low)
                news.append(kept * src_ends[e, span] + start_ends[e, span] + inv_ends[e, span] * total)
            dst_ends[0, span], dst_ends[1, span] = news


def body(links, right_side, conductance, absorption, block_agg):
    nx, ny, nz = right_side.shape
    frame = Frame(nx, ny)
    nb = nx // 2
    ix, iy, iz = (lax.axis_index(a) for a in ("gx", "gy", "gz"))
    n_x, n_y, n_z = links.sizes
    flags = jnp.stack(
        [ix, iy % 2, ix > 0, ix < n_x - 1, iy > 0, iy < n_y - 1, iz > 0, iz < n_z - 1]
    ).astype(jnp.int32)
    arrays = (conductance, right_side, absorption, block_agg)
    n_send = 1 if n_x == 2 else 2
    x_sends = call(
        functools.partial(pack_x_kernel, n_x, WIDTHS),
        [shaped(sum(WIDTHS) + 1, ny, nz)] * n_send,
        [pltpu.VMEM((n_send, ny // 2, nz // 2), jnp.int32), pltpu.SemaphoreType.DMA((n_send * 4,))],
        in_specs=[pl.BlockSpec(memory_space=pl.ANY)] * 4,
    )(flags, *arrays)
    from_x = links.x(x_sends)
    pair = [pltpu.VMEM((AGG, SUB * LANES), BF16), pltpu.VMEM((2 * AGG, SUB * LANES), BF16)]
    own_tile, block_label, face_label, inner_diag = call(
        own_kernel,
        [jax.ShapeDtypeStruct((AGG, 2 * AGG), BF16), shaped(nb, SUB, LANES), shaped(6, SUB, LANES), shaped(SUB, AGG)],
        [pltpu.VMEM((4, ny, LANES), F32), pltpu.VMEM((4, ny // 2, LANES), F32)] + pair,
    )(flags, conductance, absorption, block_agg)
    halo, from_y = widened(links, flags, WIDTHS, arrays, from_x)
    outs = [shaped(*frame.main)] * 6 + [shaped(*frame.ends)] * 6 + [shaped(nx, ny, nz)]
    outs += [shaped(6, SUB, LANES)] * 2 + [shaped(SUB, AGG)] * 2
    scratch = [pltpu.VMEM(frame.main, F32), pltpu.VMEM(frame.ends, F32), pltpu.VMEM((nx, frame.rows, LANES), F32)]
    got = call(fine_kernel, outs, scratch, limit=28)(
        flags, *halo, *from_x, *from_y, block_label, face_label, inner_diag
    )
    fields, pre = got[:12], got[12]
    face_near, face_weight, scaled_rhs, scale = got[13:]
    tiles = call(faces_kernel, jax.ShapeDtypeStruct((7 * AGG, 2 * AGG), BF16), pair)(
        flags, own_tile, face_label, face_near, face_weight
    )
    coarse = scaled_rhs
    for _ in range(KC - 1):
        near = links.x([coarse] * n_send) + links.y(coarse, coarse) + links.z(coarse, coarse)
        coarse = call(turn_kernel, shaped(SUB, AGG))(flags, tiles, scaled_rhs, scale, coarse, *near)
    x_sends = call(functools.partial(send_kernel, n_x), [shaped(HALO, ny, nz)] * n_send)(
        flags, pre, block_agg, coarse
    )
    from_x = links.x(x_sends)
    corrected = call(correct_kernel, shaped(nx, ny, nz))(flags, pre, block_agg, coarse)
    halo, _ = widened(links, flags, (HALO,), (corrected,), from_x)
    scratch = [pltpu.VMEM(frame.main, F32)] * 2 + [pltpu.VMEM(frame.ends, F32)] * 2
    return call(post_kernel, shaped(nx, ny, nz), scratch, limit=24)(flags, *halo, *fields)


def solution(mesh):
    spec = P("gx", "gy", "gz")
    return jax.shard_map(
        functools.partial(body, Links(mesh)), mesh=mesh, in_specs=(spec,) * 4, out_specs=spec, check_vma=False
    )
```

time: 642 us -> 140 us (0.22)
  the two profiles are of different devices: /device:TPU:25 before, /device:TPU:0 now
where the time goes in v2:
time: 140 us
  Pallas kernels  67.7 us (48%)
  waiting for transfers between devices  34.5 us (25%)
  starting transfers between devices  33.8 us (24%)
  local copies, waits for them, and re-layouts  3.98 us (3%)
    pallas_call x18, Pallas kernels, run(): pl.pallas_call(kernel, out_shape=outs, in_specs=[SMEM] + (in_specs or [VM...  67.7 us
    ppermute x9, starting transfers between devices, z(): lax.ppermute(forth, axes, self.snake)  16.3 us
    ppermute x9, waiting for transfers between devices, y(): lax.ppermute(to_high, 'gy', self.ring_y)  14.5 us
    ppermute x9, waiting for transfers between devices, x(): got = lax.ppermute(sends[0], 'gx', self.ring_x)  11.1 us
    ppermute x9, starting transfers between devices, x(): got = lax.ppermute(sends[0], 'gx', self.ring_x)  8.03 us
    ppermute x9, starting transfers between devices, y(): lax.ppermute(to_low, 'gy', self.back(self.ring_y))  5.62 us
    ppermute x9, waiting for transfers between devices, z(): lax.ppermute(back, axes, self.back(self.snake))  5.29 us
    unnamed x12, local copies, waits for them, and re-layouts  3.9 us
  transfers between devices with their start and end apart: 45, of which 26 were waited for; matrix products, arithmetic and copies ran while one was open for 0% of the time, Pallas kernels for 12%

profile of v2, /device:TPU:0, one launch (start us, length us, event | category | flops | bytes accessed | tf_op | source)
XLA Modules:
  0.0 140.2 jit_solution(6966609828939367793)
XLA Ops:
  4.8 3.0 %collective-permute-start = (f32[11,32,128]{2,1,0:T(8,128)S(1)}, f32[11,32,128]{2,1,0:T(8,128)S(1)}, u32[]{:S(2)}, u32[]{:S(2)}) collective-permute-start(f32[11,32,128]{2,1,0:T(8,128)S(1)} %shard_map.46), channel_id=1, source_target_pairs={{0,16},{16,0},{1,17},{17,1},{2,18},{18,2},{3,19},{19,3},{4,20},{20... | collective-permute-start | bytes 540680 | tf_op jit(solution)/shard_map/ppermute | solution.py:209
  7.8 4.5 %collective-permute-done.refs_4_.refs_5_.from_x_low.from_x_high = f32[11,32,128]{2,1,0:T(8,128)S(1)} collective-permute-done((f32[11,32,128]{2,1,0:T(8,128)S(1)}, f32[11,32,128]{2,1,0:T(8,128)S(1)}, u32[]{:S(2)}, u32[]{:S(2)}) %collective-permute-start) | collective-permute-done | bytes 180256 | tf_op jit(solution)/shard_map/ppermute | solution.py:209
  13.0 1.7 %collective-permute-start.2 = (f32[400,128]{1,0:T(8,128)S(1)}, f32[400,128]{1,0:T(8,128)S(1)}, u32[]{:S(2)}, u32[]{:S(2)}) collective-permute-start(f32[400,128]{1,0:T(8,128)S(1)} %get-tuple-element.37), channel_id=1, source_target_pairs={{4,0},{8,4},{12,8},{0,12},{5,1},{9,5},{13,9},{1,13},{6,2},{10,6},{... | collective-permute-start | bytes 614408 | tf_op jit(solution)/shard_map/ppermute | solution.py:214
  14.8 3.5 %collective-permute-done.1.refs_6_.from_y_low = f32[400,128]{1,0:T(8,128)S(1)} collective-permute-done((f32[400,128]{1,0:T(8,128)S(1)}, f32[400,128]{1,0:T(8,128)S(1)}, u32[]{:S(2)}, u32[]{:S(2)}) %collective-permute-start.1) | collective-permute-done | bytes 204832 | tf_op jit(solution)/shard_map/ppermute | solution.py:214
  19.7 1.5 %shard_map.48 = (f32[3,32,56,128]{3,2,1,0:T(8,128)S(1)}, f32[136,128]{1,0:T(8,128)S(1)}, f32[136,128]{1,0:T(8,128)S(1)}) custom-call(s32[8]{0:T(128)S(1)} %stack.59.flags, f32[24,32,128]{2,1,0:T(8,128)S(1)} %copy-done, f32[24,32,128]{2,1,0:T(8,128)S(1)} %copy-done.5, f32[24,32,128]{2,1,0:T(8,128)S(1)} %copy-done.1, s32[12,16,64]{2,1,0:T(8,128)S(1)} %copy-done.3, ...), custom_call_target="tpu_custom_call" | custom-call | flops 1000000 | bytes 100000 | tf_op jit(solution)/shard_map/pallas_call | solution.py:28
  21.2 1.6 %collective-permute-start.3 = (f32[136,128]{1,0:T(8,128)S(1)}, f32[136,128]{1,0:T(8,128)S(1)}, u32[]{:S(2)}, u32[]{:S(2)}) collective-permute-start(f32[136,128]{1,0:T(8,128)S(1)} %get-tuple-element.39), channel_id=1, source_target_pairs={{0,1},{1,2},{2,3},{3,7},{7,6},{6,5},{5,4},{4,0},{8,9},{9,10},{10,1... | collective-permute-start | bytes 208904 | tf_op jit(solution)/shard_map/ppermute | solution.py:218
  22.8 10.5 %shard_map.49 = (bf16[128,256]{1,0:T(8,128)(2,1)S(1)}, f32[12,8,128]{2,1,0:T(8,128)S(1)}, f32[6,8,128]{2,1,0:T(8,128)S(1)}, f32[8,128]{1,0:T(8,128)S(1)}) custom-call(s32[8]{0:T(128)S(1)} %stack.59.flags, f32[24,32,128]{2,1,0:T(8,128)S(1)} %copy-done, f32[24,32,128]{2,1,0:T(8,128)S(1)} %copy-done.2, s32[12,16,64]{2,1,0:T(8,128)S(1)} %copy-done.3), custom_call_target="tpu_custom_call" | custom-call | flops 1000000 | bytes 100000 | tf_op jit(solution)/shard_map/pallas_call | solution.py:28
  33.3 22.6 %shard_map.50 = (f32[32,56,128]{2,1,0:T(8,128)S(1)}, f32[32,56,128]{2,1,0:T(8,128)S(1)}, f32[32,56,128]{2,1,0:T(8,128)S(1)}, f32[32,56,128]{2,1,0:T(8,128)S(1)},...) custom-call(s32[8]{0:T(128)S(1)} %stack.59.flags, ...), custom_call_target="tpu_custom_call" | custom-call | flops 1000000 | bytes 100000 | tf_op jit(solution)/shard_map/pallas_call | solution.py:28
  56.5 1.5 %collective-permute-start.8 = (f32[8,128]{1,0:T(8,128)S(1)}, f32[8,128]{1,0:T(8,128)S(1)}, u32[]{:S(2)}, u32[]{:S(2)}) collective-permute-start(f32[8,128]{1,0:T(8,128)S(1)} %get-tuple-element.48.scaled_rhs.own), channel_id=1, source_target_pairs={{0,1},{1,2},{2,3},{3,7},{7,6},{6,5},{5,4},{4,0},{8,9},{9,10},{10,1... | collective-permute-start | bytes 12296 | tf_op jit(solution)/shard_map/ppermute | solution.py:218
  60.6 3.0 %shard_map.51.tiles = bf16[896,256]{1,0:T(8,128)(2,1)S(1)} custom-call(s32[8]{0:T(128)S(1)} %stack.59.flags, bf16[128,256]{1,0:T(8,128)(2,1)S(1)} %get-tuple-element.45.own, f32[6,8,128]{2,1,0:T(8,128)S(1)} %get-tuple-element.42.face_label, f32[6,8,128]{2,1,0:T(8,128)S(1)} %get-tuple-element.46.face_near, f32[6,8,128]{2,1,0:T(8,128)S(1)} %get-tuple-element.47.face_weight), custom_call_target="tpu_custom_call" | custom-call | flops 1000000 | bytes 100000 | tf_op jit(solution)/shard_map/pallas_call | solution.py:28
  64.9 1.5 %collective-permute-start.13 = (f32[8,128]{1,0:T(8,128)S(1)}, f32[8,128]{1,0:T(8,128)S(1)}, u32[]{:S(2)}, u32[]{:S(2)}) collective-permute-start(f32[8,128]{1,0:T(8,128)S(1)} %shard_map.52.own), channel_id=1, source_target_pairs={{0,1},{1,2},{2,3},{3,7},{7,6},{6,5},{5,4},{4,0},{8,9},{9,10},{10,1... | collective-permute-start | bytes 12296 | tf_op jit(solution)/shard_map/ppermute | solution.py:218
  68.7 1.7 %collective-permute-done.11.y_low = f32[8,128]{1,0:T(8,128)S(1)} collective-permute-done((f32[8,128]{1,0:T(8,128)S(1)}, f32[8,128]{1,0:T(8,128)S(1)}, u32[]{:S(2)}, u32[]{:S(2)}) %collective-permute-start.11) | collective-permute-done | bytes 4128 | tf_op jit(solution)/shard_map/ppermute | solution.py:214
  71.8 1.9 %collective-permute-start.18 = (f32[8,128]{1,0:T(8,128)S(1)}, f32[8,128]{1,0:T(8,128)S(1)}, u32[]{:S(2)}, u32[]{:S(2)}) collective-permute-start(f32[8,128]{1,0:T(8,128)S(1)} %shard_map.53.own), channel_id=1, source_target_pairs={{0,1},{1,2},{2,3},{3,7},{7,6},{6,5},{5,4},{4,0},{8,9},{9,10},{10,1... | collective-permute-start | bytes 12296 | tf_op jit(solution)/shard_map/ppermute | solution.py:218
  75.3 1.6 %collective-permute-done.16.y_low = f32[8,128]{1,0:T(8,128)S(1)} collective-permute-done((f32[8,128]{1,0:T(8,128)S(1)}, f32[8,128]{1,0:T(8,128)S(1)}, u32[]{:S(2)}, u32[]{:S(2)}) %collective-permute-start.16) | collective-permute-done | bytes 4128 | tf_op jit(solution)/shard_map/ppermute | solution.py:214
  78.6 2.0 %collective-permute-start.23 = (f32[8,128]{1,0:T(8,128)S(1)}, f32[8,128]{1,0:T(8,128)S(1)}, u32[]{:S(2)}, u32[]{:S(2)}) collective-permute-start(f32[8,128]{1,0:T(8,128)S(1)} %shard_map.54.own), channel_id=1, source_target_pairs={{0,1},{1,2},{2,3},{3,7},{7,6},{6,5},{5,4},{4,0},{8,9},{9,10},{10,1... | collective-permute-start | bytes 12296 | tf_op jit(solution)/shard_map/ppermute | solution.py:218
  85.5 2.0 %collective-permute-start.28 = (f32[8,128]{1,0:T(8,128)S(1)}, f32[8,128]{1,0:T(8,128)S(1)}, u32[]{:S(2)}, u32[]{:S(2)}) collective-permute-start(f32[8,128]{1,0:T(8,128)S(1)} %shard_map.55.own), channel_id=1, source_target_pairs={{0,1},{1,2},{2,3},{3,7},{7,6},{6,5},{5,4},{4,0},{8,9},{9,10},{10,1... | collective-permute-start | bytes 12296 | tf_op jit(solution)/shard_map/ppermute | solution.py:218
  92.3 2.0 %collective-permute-start.33 = (f32[8,128]{1,0:T(8,128)S(1)}, f32[8,128]{1,0:T(8,128)S(1)}, u32[]{:S(2)}, u32[]{:S(2)}) collective-permute-start(f32[8,128]{1,0:T(8,128)S(1)} %shard_map.56.own), channel_id=1, source_target_pairs={{0,1},{1,2},{2,3},{3,7},{7,6},{6,5},{5,4},{4,0},{8,9},{9,10},{10,1... | collective-permute-start | bytes 12296 | tf_op jit(solution)/shard_map/ppermute | solution.py:218
  99.2 2.0 %collective-permute-start.38 = (f32[8,128]{1,0:T(8,128)S(1)}, f32[8,128]{1,0:T(8,128)S(1)}, u32[]{:S(2)}, u32[]{:S(2)}) collective-permute-start(f32[8,128]{1,0:T(8,128)S(1)} %shard_map.57.own), channel_id=1, source_target_pairs={{0,1},{1,2},{2,3},{3,7},{7,6},{6,5},{5,4},{4,0},{8,9},{9,10},{10,1... | collective-permute-start | bytes 12296 | tf_op jit(solution)/shard_map/ppermute | solution.py:218
  107.4 3.1 %shard_map.59.refs_0_ = f32[24,32,128]{2,1,0:T(8,128)S(1)} custom-call(s32[8]{0:T(128)S(1)} %stack.59.flags, f32[24,32,128]{2,1,0:T(8,128)S(1)} %get-tuple-element.44.pre, s32[12,16,64]{2,1,0:T(8,128)S(1)} %copy-done.4, f32[8,128]{1,0:T(8,128)S(1)} %shard_map.58.coarse), custom_call_target="tpu_custom_call" | custom-call | flops 1000000 | bytes 100000 | tf_op jit(solution)/shard_map/pallas_call | solution.py:28
  111.8 1.7 %collective-permute-start.42 = (f32[128,128]{1,0:T(8,128)S(1)}, f32[128,128]{1,0:T(8,128)S(1)}, u32[]{:S(2)}, u32[]{:S(2)}) collective-permute-start(f32[128,128]{1,0:T(8,128)S(1)} %get-tuple-element.51), channel_id=1, source_target_pairs={{4,0},{8,4},{12,8},{0,12},{5,1},{9,5},{13,9},{1,13},{6,2},{10,6},{... | collective-permute-start | bytes 196616 | tf_op jit(solution)/shard_map/ppermute | solution.py:214
  113.5 1.9 %collective-permute-done.41.refs_3_ = f32[128,128]{1,0:T(8,128)S(1)} collective-permute-done((f32[128,128]{1,0:T(8,128)S(1)}, f32[128,128]{1,0:T(8,128)S(1)}, u32[]{:S(2)}, u32[]{:S(2)}) %collective-permute-start.41) | collective-permute-done | bytes 65568 | tf_op jit(solution)/shard_map/ppermute | solution.py:214
  116.3 1.7 %collective-permute-start.43 = (f32[40,128]{1,0:T(8,128)S(1)}, f32[40,128]{1,0:T(8,128)S(1)}, u32[]{:S(2)}, u32[]{:S(2)}) collective-permute-start(f32[40,128]{1,0:T(8,128)S(1)} %get-tuple-element.53), channel_id=1, source_target_pairs={{0,1},{1,2},{2,3},{3,7},{7,6},{6,5},{5,4},{4,0},{8,9},{9,10},{10,1... | collective-permute-start | bytes 61448 | tf_op jit(solution)/shard_map/ppermute | solution.py:218
  119.5 2.3 %collective-permute-done.44.back = f32[40,128]{1,0:T(8,128)S(1)} collective-permute-done((f32[40,128]{1,0:T(8,128)S(1)}, f32[40,128]{1,0:T(8,128)S(1)}, u32[]{:S(2)}, u32[]{:S(2)}) %collective-permute-start.44) | collective-permute-done | bytes 20512 | tf_op jit(solution)/shard_map/ppermute | solution.py:218
  121.8 18.4 %shard_map.63 = f32[24,32,128]{2,1,0:T(8,128)} custom-call(s32[8]{0:T(128)S(1)} %stack.59.flags, f32[1,32,56,128]{3,2,1,0:T(8,128)S(1)} %get-tuple-element.52.wide_ref, f32[40,128]{1,0:T(8,128)S(1)} %collective-permute-done.43.forth, f32[40,128]{1,0:T(8,128)S(1)} %collective-permute-done.44.back, f32[32,56,128]{2,1,0:T(8,128)S(1)} %get-tuple-element.55.refs_0_, ...), custom_call_target="tpu_custom_call" | custom-call | flops 1000000 | bytes 100000 | tf_op jit(solution)/shard_map/pallas_call | solution.py:28
  (97 shorter events, 42.5 us)
Async XLA Ops:
  4.8 7.6 %collective-permute-start = (f32[11,32,128]{2,1,0:T(8,128)S(1)}, f32[11,32,128]{2,1,0:T(8,128)S(1)}, u32[]{:S(2)}, u32[]{:S(2)}) collective-permute-start(f32[11,32,128]{2,1,0:T(8,128)S(1)} %shard_map.46), channel_id=1, source_target_pairs={{0,16},{16,0},{1,17},{17,1},{2,18},{18,2},{3,19},{19,3},{4,20},{20... | collective-permute-start | bytes 540680 | tf_op jit(solution)/shard_map/ppermute | solution.py:209
  13.0 5.3 %collective-permute-start.1 = (f32[400,128]{1,0:T(8,128)S(1)}, f32[400,128]{1,0:T(8,128)S(1)}, u32[]{:S(2)}, u32[]{:S(2)}) collective-permute-start(f32[400,128]{1,0:T(8,128)S(1)} %get-tuple-element.36), channel_id=1, source_target_pairs={{0,4},{4,8},{8,12},{12,0},{1,5},{5,9},{9,13},{13,1},{2,6},{6,10},{... | collective-permute-start | bytes 614408 | tf_op jit(solution)/shard_map/ppermute | solution.py:214
  13.0 6.7 %collective-permute-start.2 = (f32[400,128]{1,0:T(8,128)S(1)}, f32[400,128]{1,0:T(8,128)S(1)}, u32[]{:S(2)}, u32[]{:S(2)}) collective-permute-start(f32[400,128]{1,0:T(8,128)S(1)} %get-tuple-element.37), channel_id=1, source_target_pairs={{4,0},{8,4},{12,8},{0,12},{5,1},{9,5},{13,9},{1,13},{6,2},{10,6},{... | collective-permute-start | bytes 614408 | tf_op jit(solution)/shard_map/ppermute | solution.py:214
  21.2 12.1 %collective-permute-start.3 = (f32[136,128]{1,0:T(8,128)S(1)}, f32[136,128]{1,0:T(8,128)S(1)}, u32[]{:S(2)}, u32[]{:S(2)}) collective-permute-start(f32[136,128]{1,0:T(8,128)S(1)} %get-tuple-element.39), channel_id=1, source_target_pairs={{0,1},{1,2},{2,3},{3,7},{7,6},{6,5},{5,4},{4,0},{8,9},{9,10},{10,1... | collective-permute-start | bytes 208904 | tf_op jit(solution)/shard_map/ppermute | solution.py:218
  22.8 10.5 %collective-permute-start.4 = (f32[136,128]{1,0:T(8,128)S(1)}, f32[136,128]{1,0:T(8,128)S(1)}, u32[]{:S(2)}, u32[]{:S(2)}) collective-permute-start(f32[136,128]{1,0:T(8,128)S(1)} %get-tuple-element.40), channel_id=1, source_target_pairs={{1,0},{2,1},{3,2},{7,3},{6,7},{5,6},{4,5},{0,4},{9,8},{10,9},{11,1... | collective-permute-start | bytes 208904 | tf_op jit(solution)/shard_map/ppermute | solution.py:218
  55.9 7.6 %collective-permute-start.9 = (f32[8,128]{1,0:T(8,128)S(1)}, f32[8,128]{1,0:T(8,128)S(1)}, u32[]{:S(2)}, u32[]{:S(2)}) collective-permute-start(f32[8,128]{1,0:T(8,128)S(1)} %get-tuple-element.48.scaled_rhs.own), channel_id=1, source_target_pairs={{1,0},{2,1},{3,2},{7,3},{6,7},{5,6},{4,5},{0,4},{9,8},{10,9},{11,1... | collective-permute-start | bytes 12296 | tf_op jit(solution)/shard_map/ppermute | solution.py:218
  56.5 7.1 %collective-permute-start.8 = (f32[8,128]{1,0:T(8,128)S(1)}, f32[8,128]{1,0:T(8,128)S(1)}, u32[]{:S(2)}, u32[]{:S(2)}) collective-permute-start(f32[8,128]{1,0:T(8,128)S(1)} %get-tuple-element.48.scaled_rhs.own), channel_id=1, source_target_pairs={{0,1},{1,2},{2,3},{3,7},{7,6},{6,5},{5,4},{4,0},{8,9},{9,10},{10,1... | collective-permute-start | bytes 12296 | tf_op jit(solution)/shard_map/ppermute | solution.py:218
  58.0 5.6 %collective-permute-start.7 = (f32[8,128]{1,0:T(8,128)S(1)}, f32[8,128]{1,0:T(8,128)S(1)}, u32[]{:S(2)}, u32[]{:S(2)}) collective-permute-start(f32[8,128]{1,0:T(8,128)S(1)} %get-tuple-element.48.scaled_rhs.own), channel_id=1, source_target_pairs={{4,0},{8,4},{12,8},{0,12},{5,1},{9,5},{13,9},{1,13},{6,2},{10,6},{... | collective-permute-start | bytes 12296 | tf_op jit(solution)/shard_map/ppermute | solution.py:214
  59.1 4.5 %collective-permute-start.6 = (f32[8,128]{1,0:T(8,128)S(1)}, f32[8,128]{1,0:T(8,128)S(1)}, u32[]{:S(2)}, u32[]{:S(2)}) collective-permute-start(f32[8,128]{1,0:T(8,128)S(1)} %get-tuple-element.48.scaled_rhs.own), channel_id=1, source_target_pairs={{0,4},{4,8},{8,12},{12,0},{1,5},{5,9},{9,13},{13,1},{2,6},{6,10},{... | collective-permute-start | bytes 12296 | tf_op jit(solution)/shard_map/ppermute | solution.py:214
  59.1 4.6 %collective-permute-start.5 = (f32[8,128]{1,0:T(8,128)S(1)}, f32[8,128]{1,0:T(8,128)S(1)}, u32[]{:S(2)}, u32[]{:S(2)}) collective-permute-start(f32[8,128]{1,0:T(8,128)S(1)} %get-tuple-element.48.scaled_rhs.own), channel_id=1, source_target_pairs={{0,16},{16,0},{1,17},{17,1},{2,18},{18,2},{3,19},{19,3},{4,20},{20... | collective-permute-start | bytes 12296 | tf_op jit(solution)/shard_map/ppermute | solution.py:209
  64.4 3.6 %collective-permute-start.14 = (f32[8,128]{1,0:T(8,128)S(1)}, f32[8,128]{1,0:T(8,128)S(1)}, u32[]{:S(2)}, u32[]{:S(2)}) collective-permute-start(f32[8,128]{1,0:T(8,128)S(1)} %shard_map.52.own), channel_id=1, source_target_pairs={{1,0},{2,1},{3,2},{7,3},{6,7},{5,6},{4,5},{0,4},{9,8},{10,9},{11,1... | collective-permute-start | bytes 12296 | tf_op jit(solution)/shard_map/ppermute | solution.py:218
  67.3 3.6 %collective-permute-start.10 = (f32[8,128]{1,0:T(8,128)S(1)}, f32[8,128]{1,0:T(8,128)S(1)}, u32[]{:S(2)}, u32[]{:S(2)}) collective-permute-start(f32[8,128]{1,0:T(8,128)S(1)} %shard_map.52.own), channel_id=1, source_target_pairs={{0,16},{16,0},{1,17},{17,1},{2,18},{18,2},{3,19},{19,3},{4,20},{20... | collective-permute-start | bytes 12296 | tf_op jit(solution)/shard_map/ppermute | solution.py:209
  71.7 3.6 %collective-permute-start.19 = (f32[8,128]{1,0:T(8,128)S(1)}, f32[8,128]{1,0:T(8,128)S(1)}, u32[]{:S(2)}, u32[]{:S(2)}) collective-permute-start(f32[8,128]{1,0:T(8,128)S(1)} %shard_map.53.own), channel_id=1, source_target_pairs={{1,0},{2,1},{3,2},{7,3},{6,7},{5,6},{4,5},{0,4},{9,8},{10,9},{11,1... | collective-permute-start | bytes 12296 | tf_op jit(solution)/shard_map/ppermute | solution.py:218
  78.5 3.6 %collective-permute-start.24 = (f32[8,128]{1,0:T(8,128)S(1)}, f32[8,128]{1,0:T(8,128)S(1)}, u32[]{:S(2)}, u32[]{:S(2)}) collective-permute-start(f32[8,128]{1,0:T(8,128)S(1)} %shard_map.54.own), channel_id=1, source_target_pairs={{1,0},{2,1},{3,2},{7,3},{6,7},{5,6},{4,5},{0,4},{9,8},{10,9},{11,1... | collective-permute-start | bytes 12296 | tf_op jit(solution)/shard_map/ppermute | solution.py:218
  81.1 3.6 %collective-permute-start.20 = (f32[8,128]{1,0:T(8,128)S(1)}, f32[8,128]{1,0:T(8,128)S(1)}, u32[]{:S(2)}, u32[]{:S(2)}) collective-permute-start(f32[8,128]{1,0:T(8,128)S(1)} %shard_map.54.own), channel_id=1, source_target_pairs={{0,16},{16,0},{1,17},{17,1},{2,18},{18,2},{3,19},{19,3},{4,20},{20... | collective-permute-start | bytes 12296 | tf_op jit(solution)/shard_map/ppermute | solution.py:209
  85.4 3.6 %collective-permute-start.29 = (f32[8,128]{1,0:T(8,128)S(1)}, f32[8,128]{1,0:T(8,128)S(1)}, u32[]{:S(2)}, u32[]{:S(2)}) collective-permute-start(f32[8,128]{1,0:T(8,128)S(1)} %shard_map.55.own), channel_id=1, source_target_pairs={{1,0},{2,1},{3,2},{7,3},{6,7},{5,6},{4,5},{0,4},{9,8},{10,9},{11,1... | collective-permute-start | bytes 12296 | tf_op jit(solution)/shard_map/ppermute | solution.py:218
  92.3 3.6 %collective-permute-start.34 = (f32[8,128]{1,0:T(8,128)S(1)}, f32[8,128]{1,0:T(8,128)S(1)}, u32[]{:S(2)}, u32[]{:S(2)}) collective-permute-start(f32[8,128]{1,0:T(8,128)S(1)} %shard_map.56.own), channel_id=1, source_target_pairs={{1,0},{2,1},{3,2},{7,3},{6,7},{5,6},{4,5},{0,4},{9,8},{10,9},{11,1... | collective-permute-start | bytes 12296 | tf_op jit(solution)/shard_map/ppermute | solution.py:218
  94.9 3.6 %collective-permute-start.30 = (f32[8,128]{1,0:T(8,128)S(1)}, f32[8,128]{1,0:T(8,128)S(1)}, u32[]{:S(2)}, u32[]{:S(2)}) collective-permute-start(f32[8,128]{1,0:T(8,128)S(1)} %shard_map.56.own), channel_id=1, source_target_pairs={{0,16},{16,0},{1,17},{17,1},{2,18},{18,2},{3,19},{19,3},{4,20},{20... | collective-permute-start | bytes 12296 | tf_op jit(solution)/shard_map/ppermute | solution.py:209
  99.2 3.6 %collective-permute-start.39 = (f32[8,128]{1,0:T(8,128)S(1)}, f32[8,128]{1,0:T(8,128)S(1)}, u32[]{:S(2)}, u32[]{:S(2)}) collective-permute-start(f32[8,128]{1,0:T(8,128)S(1)} %shard_map.57.own), channel_id=1, source_target_pairs={{1,0},{2,1},{3,2},{7,3},{6,7},{5,6},{4,5},{0,4},{9,8},{10,9},{11,1... | collective-permute-start | bytes 12296 | tf_op jit(solution)/shard_map/ppermute | solution.py:218
  101.7 3.6 %collective-permute-start.35 = (f32[8,128]{1,0:T(8,128)S(1)}, f32[8,128]{1,0:T(8,128)S(1)}, u32[]{:S(2)}, u32[]{:S(2)}) collective-permute-start(f32[8,128]{1,0:T(8,128)S(1)} %shard_map.57.own), channel_id=1, source_target_pairs={{0,16},{16,0},{1,17},{17,1},{2,18},{18,2},{3,19},{19,3},{4,20},{20... | collective-permute-start | bytes 12296 | tf_op jit(solution)/shard_map/ppermute | solution.py:209
  106.8 4.3 %collective-permute-start.40 = (f32[4,32,128]{2,1,0:T(8,128)S(1)}, f32[4,32,128]{2,1,0:T(8,128)S(1)}, u32[]{:S(2)}, u32[]{:S(2)}) collective-permute-start(f32[4,32,128]{2,1,0:T(8,128)S(1)} %shard_map.60), channel_id=1, source_target_pairs={{0,16},{16,0},{1,17},{17,1},{2,18},{18,2},{3,19},{19,3},{4,20},{20... | collective-permute-start | bytes 196616 | tf_op jit(solution)/shard_map/ppermute | solution.py:209
  111.7 3.7 %collective-permute-start.41 = (f32[128,128]{1,0:T(8,128)S(1)}, f32[128,128]{1,0:T(8,128)S(1)}, u32[]{:S(2)}, u32[]{:S(2)}) collective-permute-start(f32[128,128]{1,0:T(8,128)S(1)} %get-tuple-element.50), channel_id=1, source_target_pairs={{0,4},{4,8},{8,12},{12,0},{1,5},{5,9},{9,13},{13,1},{2,6},{6,10},{... | collective-permute-start | bytes 196616 | tf_op jit(solution)/shard_map/ppermute | solution.py:214
  111.8 3.7 %collective-permute-start.42 = (f32[128,128]{1,0:T(8,128)S(1)}, f32[128,128]{1,0:T(8,128)S(1)}, u32[]{:S(2)}, u32[]{:S(2)}) collective-permute-start(f32[128,128]{1,0:T(8,128)S(1)} %get-tuple-element.51), channel_id=1, source_target_pairs={{4,0},{8,4},{12,8},{0,12},{5,1},{9,5},{13,9},{1,13},{6,2},{10,6},{... | collective-permute-start | bytes 196616 | tf_op jit(solution)/shard_map/ppermute | solution.py:214
  118.1 3.8 %collective-permute-start.44 = (f32[40,128]{1,0:T(8,128)S(1)}, f32[40,128]{1,0:T(8,128)S(1)}, u32[]{:S(2)}, u32[]{:S(2)}) collective-permute-start(f32[40,128]{1,0:T(8,128)S(1)} %get-tuple-element.54), channel_id=1, source_target_pairs={{1,0},{2,1},{3,2},{7,3},{6,7},{5,6},{4,5},{0,4},{9,8},{10,9},{11,1... | collective-permute-start | bytes 61448 | tf_op jit(solution)/shard_map/ppermute | solution.py:218
  (27 other events, 132.7 us)

commit v3 on v2

--- a/solution.py
+++ b/solution.py
@@ -56,6 +56,15 @@
         if shift == 0:
             return values
     return pltpu.roll(values, shift, axis)
+
+
+def batched(low, high, step, carry, size=6):
+    def some(i, carry):
+        return step([low + i * size + k for k in range(size)], carry)
+
+    carry = lax.fori_loop(0, (high - low) // size, some, carry)
+    rest = (high - low) % size
+    return step(list(range(high - rest, high)), carry) if rest else carry
 
 
 def picked(values, index):
@@ -218,17 +227,21 @@
         return lax.ppermute(forth, axes, self.snake), lax.ppermute(back, axes, self.back(self.snake))
 
 
-def widened(links, flags, widths, arrays, from_x):
+def widened(links, flags, widths, arrays, from_x, beside_y=None, beside_z=None):
     fields, labels = len(widths), len(arrays) - len(widths)
     nx, ny, nz = arrays[0].shape
     frame = Frame(nx, ny)
     rows = fields * frame.wide * HALO + labels * ny // 2
     sends = call(functools.partial(pack_y_kernel, widths, labels), [shaped(rows, nz)] * 2)(flags, *arrays, *from_x)
+    work = beside_y(sends[0]) if beside_y else ()
     from_y = links.y(*sends)
+    from_y = lax.optimization_barrier((*from_y, *work))[:2] if work else from_y
     rows = fields * frame.tall + labels * ny // 2
     wide, *sends = call(
         functools.partial(pack_z_kernel, widths, labels), [shaped(fields, *frame.main)] + [shaped(rows, nz)] * 2
     )(flags, *arrays, *from_x, *from_y)
+    if beside_z:
+        beside_z(sends[0])
     return (wide, *links.z(*sends)), from_y
 
 
@@ -251,14 +264,14 @@
 
 def joined(below, above):
     lane = lane_no(below.shape)
-    return jnp.where(lane % HALO == HALO - 1, below, turned(above, HALO, 1))
+    return jnp.where(lane % HALO == HALO - 1, turned(above, HALO - 1, 1), turned(below, 1, 1))
 
 
 def next_and_last(here, join, x):
     lane = lane_no((1, LANES))
     edge = turned(join, (LANES - HALO) - HALO * x, 1)
-    upper = turned(jnp.where(lane == 0, edge, here), -1, 1)
-    lower = turned(jnp.where(lane == LANES - 1, edge, here), 1, 1)
+    upper = jnp.where(lane == LANES - 1, edge, turned(here, -1, 1))
+    lower = jnp.where(lane == 0, edge, turned(here, 1, 1))
     return upper, lower
 
 
@@ -317,7 +330,7 @@
 def fine_kernel(flags, wide_ref, forth, back, from_x_low, from_x_high, from_y_low, from_y_high, block_label,
                 face_label, inner_diag, *refs):
     main, ends = refs[:6], refs[6:12]
-    pre, face_near, face_weight, scaled_rhs, scale, once, once_ends, res = refs[12:]
+    pre, face_near, face_weight, scaled_rhs, scale, once, once_ends, res, diag = refs[12:]
     wx, wy, wz_up, wz_low, inv_diag, start = main
     ex, ey, ez_up, ez_low, inv_ends, start_ends = ends
     nx, ny = pre.shape[0], pre.shape[1]
@@ -338,10 +351,12 @@
     ).astype(F32)
     keep_low, keep_high = flags[Z_LOW].astype(F32), flags[Z_HIGH].astype(F32)
 
-    def cond_edges(x, edges):
-        return edge_step(wide_ref[0, x, span], x, edges)
-
-    edges = lax.fori_loop(0, wide, cond_edges, jnp.ones((tall, LANES), F32), unroll=4)
+    def cond_edges(xs, edges):
+        for x in xs:
+            edges = edge_step(wide_ref[0, x, span], x, edges)
+        return edges
+
+    edges = batched(0, wide, cond_edges, jnp.ones((tall, LANES), F32), 8)
     near = ends_near(cond_below, cond_above, edges)
     slab = lane // HALO
     keep_x = jnp.where(
@@ -365,26 +380,31 @@
     join = joined(cond_below, cond_above)
     wz_under = ez_up[0, span]
 
-    def fields(x, carry):
+    def fields(xs, carry):
         before, edges = carry
-        here = wide_ref[0, x, span]
-        keep = jnp.where(x == HALO - 1, flags[X_LOW], jnp.where(x == last - 1, flags[X_HIGH], 1)).astype(F32)
-        edge = turned(join, (LANES - HALO) - HALO * x, 1)
-        upper = turned(jnp.where(lane == 0, edge, here), -1, 1)
-        face_x = keep * weight(here, wide_ref[0, jnp.minimum(x + 1, wide - 1), span])
-        face_y = keep_y * weight(here, wide_ref[0, x, pl.ds(SUB + 1, tall)])
-        up = weight(here, upper) * jnp.where(lane == LANES - 1, keep_high, 1.0)
-        under = turned(wz_under, (LANES - HALO) - HALO * x, 1)
-        low = turned(jnp.where(lane == LANES - 1, under, up), 1, 1)
-        total = wide_ref[2, x, span] + face_x + before + face_y + turned(face_y, 1, 0) + up + low
-        inverse = OMEGA_FINE / total
-        begin = inverse * wide_ref[1, x, span]
-        for ref, values in zip(main, (face_x, face_y, up, low, inverse, begin)):
-            ref[x, span] = values
-        return face_x, edge_step(begin, x, edges)
+        stores = []
+        for x in xs:
+            here = wide_ref[0, x, span]
+            keep = jnp.where(x == HALO - 1, flags[X_LOW], jnp.where(x == last - 1, flags[X_HIGH], 1)).astype(F32)
+            upper = next_and_last(here, join, x)[0]
+            face_x = keep * weight(here, wide_ref[0, jnp.minimum(x + 1, wide - 1), span])
+            face_y = keep_y * weight(here, wide_ref[0, x, pl.ds(SUB + 1, tall)])
+            up = weight(here, upper) * jnp.where(lane == LANES - 1, keep_high, 1.0)
+            under = turned(wz_under, (LANES - HALO + 1) - HALO * x, 1)
+            low = jnp.where(lane == 0, under, turned(up, 1, 1))
+            total = wide_ref[2, x, span] + face_x + before + face_y + turned(face_y, 1, 0) + up + low
+            inverse = OMEGA_FINE / total
+            begin = inverse * wide_ref[1, x, span]
+            stores.append((x, (face_x, face_y, up, low, inverse, begin, total)))
+            edges = edge_step(begin, x, edges)
+            before = face_x
+        for x, values in stores:
+            for ref, value in zip((*main, diag), values):
+                ref[x, span] = value
+        return before, edges
 
     nothing = jnp.zeros((tall, LANES), F32)
-    _, edges = lax.fori_loop(0, wide, fields, (nothing, nothing))
+    _, edges = batched(0, wide, fields, (nothing, nothing), 4)
 
     join = joined(start_ends[0, span], start_ends[1, span])
     near = ends_near(start_ends[0, span], start_ends[1, span], edges)
@@ -392,19 +412,30 @@
         total = ends_sum(frame, start_ends, s, near[2 * s], near[2 * s + 1], ex, ey, ez_up, ez_low)
         once_ends[s, span] = (2.0 - OMEGA_FINE) * start_ends[s, span] + inv_ends[s, span] * total
 
-    @pl.loop(HALO - 1, last + 1)
-    def _(x):
-        total = main_sum(frame, start, x, join, wx, wy, wz_up, wz_low)
-        once[x, span] = (2.0 - OMEGA_FINE) * start[x, span] + inv_diag[x, span] * total
-
+    def second(xs, carry):
+        news = []
+        for x in xs:
+            total = main_sum(frame, start, x, join, wx, wy, wz_up, wz_low)
+            news.append((2.0 - OMEGA_FINE) * start[x, span] + inv_diag[x, span] * total)
+        for x, new in zip(xs, news):
+            once[x, span] = new
+        return carry
+
+    batched(HALO - 1, last + 1, second, 0)
     join2 = joined(once_ends[0, span], once_ends[1, span])
 
-    @pl.loop(HALO, last)
-    def _(x):
-        total = main_sum(frame, once, x, join2, wx, wy, wz_up, wz_low)
-        full = wide_ref[1, x, span] - (OMEGA_FINE / inv_diag[x, span]) * once[x, span] + total
-        res[x - HALO, span] = full
-        pre[x - HALO] = once[x, pl.ds(frame.own, ny)]
+    def remainder(xs, carry):
+        news = []
+        for x in xs:
+            total = main_sum(frame, once, x, join2, wx, wy, wz_up, wz_low)
+            news.append(wide_ref[1, x, span] - diag[x, span] * once[x, span] + total)
+        for x, new in zip(xs, news):
+            res[x - HALO, span] = new
+        for x in xs:
+            pre[x - HALO] = once[x, pl.ds(frame.own, ny)]
+        return carry
+
+    batched(HALO, last, remainder, 0)
 
     nb, half, width = nx // 2, ny // 2, LANES // 2
     iota = row_no((AGG, LANES)).astype(F32)
@@ -472,13 +503,18 @@
     out[pl.ds(at, AGG), AGG:] = (tile - high.astype(F32)).astype(BF16)
 
 
-def own_kernel(flags, cond, absorb, block_agg, out, block_label, face_label, inner_diag, part, line, left, right):
+def own_kernel(first, count, last, flags, cond, absorb, block_agg, *refs):
+    if last:
+        tile_in, around_in, _, out, block_label, face_label, inner_diag, part, line, left, right = refs
+    elif first:
+        tile_in, around_in, _, tile_out, around_out, part, line, left, right = refs
+    else:
+        _, tile_out, around_out, part, line, left, right = refs
     nx, ny = cond.shape[0], cond.shape[1]
     nb, half, width = nx // 2, ny // 2, LANES // 2
     lane, row = lane_no((half, LANES)), row_no((half, LANES))
     even = 2 * (lane % width)
     iota = row_no((AGG, LANES)).astype(F32)
-    line[...] = jnp.zeros(line.shape, F32)
 
     def halves(values, slot):
         part[slot] = values
@@ -488,17 +524,20 @@
         values = block_agg[b].astype(F32)
         return jnp.concatenate([values, values], axis=1)
 
+    def upper_x(b):
+        x = 2 * b
+        faces = weight(cond[x + 1], cond[jnp.minimum(x + 2, nx - 1)])
+        return jnp.where(b == nb - 1, 0.0, paired(sum(halves(faces, 0))))
+
     def step(b, carry):
         low_x, tile, around = carry
         x = 2 * b
-        one, two, three = cond[x], cond[x + 1], cond[jnp.minimum(x + 2, nx - 1)]
-        faces_x = sum(halves(weight(two, three), 0))
+        one, two = cond[x], cond[x + 1]
         both_y = weight(one, turned(one, -1, 0)) + weight(two, turned(two, -1, 0))
         both_z = weight(one, turned(one, -1, 1)) + weight(two, turned(two, -1, 1))
-        end_x, end_y, end_z = b == nb - 1, row == half - 1, lane % width == width - 1
-        high_x = jnp.where(end_x, 0.0, paired(faces_x))
-        high_y = jnp.where(end_y, 0.0, paired(halves(both_y, 1)[1]))
-        high_z = jnp.where(end_z, 0.0, picked(sum(halves(both_z, 2)), even + 1))
+        high_x = upper_x(b)
+        high_y = jnp.where(row == half - 1, 0.0, paired(halves(both_y, 1)[1]))
+        high_z = jnp.where(lane % width == width - 1, 0.0, picked(sum(halves(both_z, 2)), even + 1))
         low_y = turned(high_y, 1, 0)
         low_z = turned(high_z, 1, 1)
         own = label_at(b)
@@ -511,7 +550,6 @@
         ):
             total = total + jnp.where(near != own, values, 0.0)
         packed, total = pack_rows(own), pack_rows(total)
-        block_label[b] = packed
         pairs = [
             (pack_rows(near_x), pack_rows(high_x)),
             (pack_rows(near_y), pack_rows(high_y)),
@@ -520,18 +558,26 @@
         tile = tile + tile_product(left, right, packed, pairs)
         for r in range(SUB):
             around = around + jnp.where(packed[r : r + 1] == iota, total[r : r + 1], 0.0)
-        line[0, pl.ds(b, 1)], line[1, pl.ds(b, 1)] = own[:1], own[half - 1 :]
-        line[2] = jnp.where(lane == b, own[:, :1], line[2])
-        line[3] = jnp.where(lane == b, own[:, width - 1 : width], line[3])
         return high_x, tile, around
 
-    nothing = jnp.zeros((half, LANES), F32)
-    _, tile, around = lax.fori_loop(
-        0, nb, step, (nothing, jnp.zeros((AGG, 2 * AGG), F32), jnp.zeros((AGG, LANES), F32))
-    )
+    if first:
+        start = (upper_x(first - 1), tile_in[...], around_in[...])
+    else:
+        start = tuple(jnp.zeros(shape, F32) for shape in ((half, LANES), (AGG, 2 * AGG), (AGG, LANES)))
+    _, tile, around = lax.fori_loop(first, first + count, step, start)
+    if not last:
+        tile_out[...], around_out[...] = tile, around
+        return
     tile = tile[:, :AGG] + tile[:, AGG:]
     keep_tile(out, 0, jnp.where(row_no((AGG, AGG)) == lane_no((AGG, AGG)), 0.0, tile + tile.T))
     inner_diag[...] = lane_total(around)
+    line[...] = jnp.zeros(line.shape, F32)
+    for b in range(nb):
+        own = label_at(b)
+        block_label[b] = pack_rows(own)
+        line[0, b : b + 1], line[1, b : b + 1] = own[:1], own[half - 1 :]
+        line[2] = jnp.where(lane == b, own[:, :1], line[2])
+        line[3] = jnp.where(lane == b, own[:, width - 1 : width], line[3])
     face_label[0], face_label[1] = block_label[0], block_label[nb - 1]
     for s in range(4):
         face_label[2 + s] = pack_rows(line[s])
@@ -610,18 +656,22 @@
         final = s == POST - 1
         dst, dst_ends = (None, None) if final else buffers[s + 1]
 
-        def step(x, edges, src=src, join=join, dst=dst, final=final):
-            here = src[x, span]
-            total = main_sum(frame, src, x, join, wx, wy, wz_up, wz_low)
-            new = kept * here + start[x, span] + inv_diag[x, span] * total
-            if final:
-                out[x - HALO] = new[HALO : HALO + ny]
-                return edges
-            dst[x, span] = new
-            return edge_step(here, x, edges)
-
-        edges = jnp.zeros((tall, LANES), F32)
-        edges = lax.fori_loop(s + 1, wide - s - 1, step, edges)
+        def step(xs, edges, src=src, join=join, dst=dst, final=final):
+            news = []
+            for x in xs:
+                here = src[x, span]
+                total = main_sum(frame, src, x, join, wx, wy, wz_up, wz_low)
+                news.append(kept * here + start[x, span] + inv_diag[x, span] * total)
+                if not final:
+                    edges = edge_step(here, x, edges)
+            for x, new in zip(xs, news):
+                if final:
+                    out[x - HALO] = new[HALO : HALO + ny]
+                else:
+                    dst[x, span] = new
+            return edges
+
+        edges = batched(s + 1, wide - s - 1, step, jnp.zeros((tall, LANES), F32))
         if not final:
             near = ends_near(src_ends[0, span], src_ends[1, span], edges)
             news = []
@@ -646,19 +696,37 @@
         functools.partial(pack_x_kernel, n_x, WIDTHS),
         [shaped(sum(WIDTHS) + 1, ny, nz)] * n_send,
         [pltpu.VMEM((n_send, ny // 2, nz // 2), jnp.int32), pltpu.SemaphoreType.DMA((n_send * 4,))],
-        in_specs=[pl.BlockSpec(memory_space=pl.ANY)] * 4,
-    )(flags, *arrays)
+        in_specs=[pl.BlockSpec(memory_space=pltpu.HBM)] * 4,
+    )(flags, *(pltpu.with_memory_space_constraint(a, pltpu.HBM) for a in arrays))
+    pair = [pltpu.VMEM((AGG, SUB * LANES), BF16), pltpu.VMEM((2 * AGG, SUB * LANES), BF16)]
+    scratch = [pltpu.VMEM((4, ny, LANES), F32), pltpu.VMEM((4, ny // 2, LANES), F32)] + pair
+    bounds = [nb * p // 3 for p in range(4)]
+
+    def own_part(p, *more):
+        outs = [shaped(AGG, 2 * AGG), shaped(AGG, LANES)]
+        if p == 2:
+            outs = [jax.ShapeDtypeStruct((AGG, 2 * AGG), BF16), shaped(nb, SUB, LANES)]
+            outs += [shaped(6, SUB, LANES), shaped(SUB, AGG)]
+        kernel = functools.partial(own_kernel, bounds[p], bounds[p + 1] - bounds[p], p == 2)
+        return call(kernel, outs, scratch)(flags, conductance, absorption, block_agg, *more)
+
+    parts = [own_part(0, x_sends[0])]
     from_x = links.x(x_sends)
-    pair = [pltpu.VMEM((AGG, SUB * LANES), BF16), pltpu.VMEM((2 * AGG, SUB * LANES), BF16)]
-    own_tile, block_label, face_label, inner_diag = call(
-        own_kernel,
-        [jax.ShapeDtypeStruct((AGG, 2 * AGG), BF16), shaped(nb, SUB, LANES), shaped(6, SUB, LANES), shaped(SUB, AGG)],
-        [pltpu.VMEM((4, ny, LANES), F32), pltpu.VMEM((4, ny // 2, LANES), F32)] + pair,
-    )(flags, conductance, absorption, block_agg)
-    halo, from_y = widened(links, flags, WIDTHS, arrays, from_x)
+    from_x = lax.optimization_barrier((*from_x, *parts[0]))[:2]
+
+    def beside(p):
+        def run(sent):
+            parts.append(own_part(p, *parts[-1], sent))
+            return parts[-1]
+
+        return run
+
+    halo, from_y = widened(links, flags, WIDTHS, arrays, from_x, beside(1), beside(2))
+    own_tile, block_label, face_label, inner_diag = parts[-1]
     outs = [shaped(*frame.main)] * 6 + [shaped(*frame.ends)] * 6 + [shaped(nx, ny, nz)]
     outs += [shaped(6, SUB, LANES)] * 2 + [shaped(SUB, AGG)] * 2
     scratch = [pltpu.VMEM(frame.main, F32), pltpu.VMEM(frame.ends, F32), pltpu.VMEM((nx, frame.rows, LANES), F32)]
+    scratch += [pltpu.VMEM(frame.main, F32)]
     got = call(fine_kernel, outs, scratch, limit=28)(
         flags, *halo, *from_x, *from_y, block_label, face_label, inner_diag
     )

time: 140 us -> 106 us (0.76)
  Pallas kernels: 67.7 us -> 43.5 us
  waiting for transfers between devices: 34.5 us -> 21.3 us
  starting transfers between devices: 33.8 us -> 38 us
    pallas_call x18 -> x20, Pallas kernels: 67.7 us -> 43.5 us  [run(): pl.pallas_call(kernel, out_shape=outs, in_specs=[SMEM] + (in_specs or [VM...]
    ppermute x9, starting transfers between devices: 8.03 us -> 14 us  [x(): got = lax.ppermute(sends[0], 'gx', self.ring_x)]
    ppermute x9, waiting for transfers between devices: 11.1 us -> 6.28 us  [x(): got = lax.ppermute(sends[0], 'gx', self.ring_x)]
    ppermute x9, waiting for transfers between devices: 14.5 us -> 9.93 us  [y(): lax.ppermute(to_high, 'gy', self.ring_y)]
    ppermute x9, waiting for transfers between devices: 5.29 us -> 2.32 us  [z(): lax.ppermute(back, axes, self.back(self.snake))]
    ppermute x9, starting transfers between devices: 5.62 us -> 2.71 us  [y(): lax.ppermute(to_low, 'gy', self.back(self.ring_y))]
  transfers between devices with their start and end apart: 45 -> 45, of which waited for: 26 -> 17; matrix products, arithmetic and copies ran while one was open for 0% -> 0% of each run, Pallas kernels for 12% -> 17%
where the time goes in v3:
time: 106 us
  Pallas kernels  43.5 us (41%)
  starting transfers between devices  38 us (36%)
  waiting for transfers between devices  21.3 us (20%)
  local copies, waits for them, and re-layouts  2.99 us (3%)
    pallas_call x20, Pallas kernels, run(): pl.pallas_call(kernel, out_shape=outs, in_specs=[SMEM] + (in_specs or [VM...  43.5 us
    ppermute x9, starting transfers between devices, z(): lax.ppermute(forth, axes, self.snake)  17.1 us
    ppermute x9, starting transfers between devices, x(): got = lax.ppermute(sends[0], 'gx', self.ring_x)  14 us
    ppermute x9, waiting for transfers between devices, y(): lax.ppermute(to_high, 'gy', self.ring_y)  9.93 us
    ppermute x9, waiting for transfers between devices, x(): got = lax.ppermute(sends[0], 'gx', self.ring_x)  6.28 us
    ppermute x9, starting transfers between devices, y(): lax.ppermute(to_high, 'gy', self.ring_y)  3.38 us
    unnamed x12, local copies, waits for them, and re-layouts  2.9 us
    ppermute x9, starting transfers between devices, y(): lax.ppermute(to_low, 'gy', self.back(self.ring_y))  2.71 us
  transfers between devices with their start and end apart: 45, of which 17 were waited for; matrix products, arithmetic and copies ran while one was open for 0% of the time, Pallas kernels for 17%

profile of v3, /device:TPU:0, one launch (start us, length us, event | category | flops | bytes accessed | tf_op | source)
XLA Modules:
  0.0 106.0 jit_solution(17379982495096231238)
XLA Ops:
  1.5 3.0 %collective-permute-start = (f32[11,32,128]{2,1,0:T(8,128)S(1)}, f32[11,32,128]{2,1,0:T(8,128)S(1)}, u32[]{:S(2)}, u32[]{:S(2)}) collective-permute-start(f32[11,32,128]{2,1,0:T(8,128)S(1)} %shard_map.46.refs_0_), channel_id=1, source_target_pairs={{0,16},{16,0},{1,17},{17,1},{2,18},{18,2},{3,19},{19,3},{4,20},{20... | collective-permute-start | bytes 540680 | tf_op jit(solution)/shard_map/ppermute | solution.py:218
  7.4 3.8 %shard_map.47 = (f32[128,256]{1,0:T(8,128)S(1)}, f32[128,128]{1,0:T(8,128)S(1)}) custom-call(s32[8]{0:T(128)S(1)} %stack.59.flags, f32[24,32,128]{2,1,0:T(8,128)S(1)} %copy-done, f32[24,32,128]{2,1,0:T(8,128)S(1)} %copy-done.1, s32[12,16,64]{2,1,0:T(8,128)S(1)} %copy-done.3, f32[11,32,128]{2,1,0:T(8,128)S(1)} %shard_map.46.refs_0_), custom_call_target="tpu_custom_call" | custom-call | flops 1000000 | bytes 100000 | tf_op jit(solution)/shard_map/pallas_call | solution.py:28
  12.6 3.9 %shard_map.49 = (f32[128,256]{1,0:T(8,128)S(1)}, f32[128,128]{1,0:T(8,128)S(1)}) custom-call(s32[8]{0:T(128)S(1)} %stack.59.flags, f32[24,32,128]{2,1,0:T(8,128)S(1)} %copy-done, f32[24,32,128]{2,1,0:T(8,128)S(1)} %copy-done.2, s32[12,16,64]{2,1,0:T(8,128)S(1)} %copy-done.3, f32[128,256]{1,0:T(8,128)S(1)} %get-tuple-element.44.refs_0_, ...), custom_call_target="tpu_custom_call" | custom-call | flops 1000000 | bytes 100000 | tf_op jit(solution)/shard_map/pallas_call | solution.py:28
  17.7 1.6 %collective-permute-done.1.refs_6_.from_y_low = f32[400,128]{1,0:T(8,128)S(1)} collective-permute-done((f32[400,128]{1,0:T(8,128)S(1)}, f32[400,128]{1,0:T(8,128)S(1)}, u32[]{:S(2)}, u32[]{:S(2)}) %collective-permute-start.1) | collective-permute-done | bytes 204832 | tf_op jit(solution)/shard_map/ppermute | solution.py:223
  19.4 1.5 %shard_map.50 = (f32[3,32,56,128]{3,2,1,0:T(8,128)S(1)}, f32[136,128]{1,0:T(8,128)S(1)}, f32[136,128]{1,0:T(8,128)S(1)}) custom-call(s32[8]{0:T(128)S(1)} %stack.59.flags, f32[24,32,128]{2,1,0:T(8,128)S(1)} %copy-done, f32[24,32,128]{2,1,0:T(8,128)S(1)} %copy-done.5, f32[24,32,128]{2,1,0:T(8,128)S(1)} %copy-done.2, s32[12,16,64]{2,1,0:T(8,128)S(1)} %copy-done.3, ...), custom_call_target="tpu_custom_call" | custom-call | flops 1000000 | bytes 100000 | tf_op jit(solution)/shard_map/pallas_call | solution.py:28
  20.9 2.0 %collective-permute-start.3 = (f32[136,128]{1,0:T(8,128)S(1)}, f32[136,128]{1,0:T(8,128)S(1)}, u32[]{:S(2)}, u32[]{:S(2)}) collective-permute-start(f32[136,128]{1,0:T(8,128)S(1)} %get-tuple-element.55.refs_2_), channel_id=1, source_target_pairs={{0,1},{1,2},{2,3},{3,7},{7,6},{6,5},{5,4},{4,0},{8,9},{9,10},{10,1... | collective-permute-start | bytes 208904 | tf_op jit(solution)/shard_map/ppermute | solution.py:227
  22.9 4.2 %shard_map.51 = (bf16[128,256]{1,0:T(8,128)(2,1)S(1)}, f32[12,8,128]{2,1,0:T(8,128)S(1)}, f32[6,8,128]{2,1,0:T(8,128)S(1)}, f32[8,128]{1,0:T(8,128)S(1)}) custom-call(s32[8]{0:T(128)S(1)} %stack.59.flags, f32[24,32,128]{2,1,0:T(8,128)S(1)} %copy-done, f32[24,32,128]{2,1,0:T(8,128)S(1)} %copy-done.2, s32[12,16,64]{2,1,0:T(8,128)S(1)} %copy-done.3, ...), custom_call_target="tpu_custom_call" | custom-call | flops 1000000 | bytes 100000 | tf_op jit(solution)/shard_map/pallas_call | solution.py:28
  27.2 9.1 %shard_map.52 = (f32[32,56,128]{2,1,0:T(8,128)S(1)}, f32[32,56,128]{2,1,0:T(8,128)S(1)}, f32[32,56,128]{2,1,0:T(8,128)S(1)}, f32[32,56,128]{2,1,0:T(8,128)S(1)},...) custom-call(s32[8]{0:T(128)S(1)} %stack.59.flags, ...), custom_call_target="tpu_custom_call" | custom-call | flops 1000000 | bytes 100000 | tf_op jit(solution)/shard_map/pallas_call | solution.py:28
  36.3 2.0 %collective-permute-start.8 = (f32[8,128]{1,0:T(8,128)S(1)}, f32[8,128]{1,0:T(8,128)S(1)}, u32[]{:S(2)}, u32[]{:S(2)}) collective-permute-start(f32[8,128]{1,0:T(8,128)S(1)} %get-tuple-element.64.scaled_rhs.own), channel_id=1, source_target_pairs={{0,1},{1,2},{2,3},{3,7},{7,6},{6,5},{5,4},{4,0},{8,9},{9,10},{10,1... | collective-permute-start | bytes 12296 | tf_op jit(solution)/shard_map/ppermute | solution.py:227
  39.4 3.0 %shard_map.53.tiles = bf16[896,256]{1,0:T(8,128)(2,1)S(1)} custom-call(s32[8]{0:T(128)S(1)} %stack.59.flags, bf16[128,256]{1,0:T(8,128)(2,1)S(1)} %get-tuple-element.61.own, f32[6,8,128]{2,1,0:T(8,128)S(1)} %get-tuple-element.58.face_label, f32[6,8,128]{2,1,0:T(8,128)S(1)} %get-tuple-element.62.face_near, f32[6,8,128]{2,1,0:T(8,128)S(1)} %get-tuple-element.63.face_weight), custom_call_target="tpu_custom_call" | custom-call | flops 1000000 | bytes 100000 | tf_op jit(solution)/shard_map/pallas_call | solution.py:28
  43.7 1.5 %collective-permute-start.13 = (f32[8,128]{1,0:T(8,128)S(1)}, f32[8,128]{1,0:T(8,128)S(1)}, u32[]{:S(2)}, u32[]{:S(2)}) collective-permute-start(f32[8,128]{1,0:T(8,128)S(1)} %shard_map.54.own), channel_id=1, source_target_pairs={{0,1},{1,2},{2,3},{3,7},{7,6},{6,5},{5,4},{4,0},{8,9},{9,10},{10,1... | collective-permute-start | bytes 12296 | tf_op jit(solution)/shard_map/ppermute | solution.py:227
  45.7 1.5 %collective-permute-start.10 = (f32[8,128]{1,0:T(8,128)S(1)}, f32[8,128]{1,0:T(8,128)S(1)}, u32[]{:S(2)}, u32[]{:S(2)}) collective-permute-start(f32[8,128]{1,0:T(8,128)S(1)} %shard_map.54.own), channel_id=1, source_target_pairs={{0,16},{16,0},{1,17},{17,1},{2,18},{18,2},{3,19},{19,3},{4,20},{20... | collective-permute-start | bytes 12296 | tf_op jit(solution)/shard_map/ppermute | solution.py:218
  50.2 1.9 %collective-permute-start.18 = (f32[8,128]{1,0:T(8,128)S(1)}, f32[8,128]{1,0:T(8,128)S(1)}, u32[]{:S(2)}, u32[]{:S(2)}) collective-permute-start(f32[8,128]{1,0:T(8,128)S(1)} %shard_map.55.own), channel_id=1, source_target_pairs={{0,1},{1,2},{2,3},{3,7},{7,6},{6,5},{5,4},{4,0},{8,9},{9,10},{10,1... | collective-permute-start | bytes 12296 | tf_op jit(solution)/shard_map/ppermute | solution.py:227
  56.9 2.0 %collective-permute-start.23 = (f32[8,128]{1,0:T(8,128)S(1)}, f32[8,128]{1,0:T(8,128)S(1)}, u32[]{:S(2)}, u32[]{:S(2)}) collective-permute-start(f32[8,128]{1,0:T(8,128)S(1)} %shard_map.56.own), channel_id=1, source_target_pairs={{0,1},{1,2},{2,3},{3,7},{7,6},{6,5},{5,4},{4,0},{8,9},{9,10},{10,1... | collective-permute-start | bytes 12296 | tf_op jit(solution)/shard_map/ppermute | solution.py:227
  63.8 2.0 %collective-permute-start.28 = (f32[8,128]{1,0:T(8,128)S(1)}, f32[8,128]{1,0:T(8,128)S(1)}, u32[]{:S(2)}, u32[]{:S(2)}) collective-permute-start(f32[8,128]{1,0:T(8,128)S(1)} %shard_map.57.own), channel_id=1, source_target_pairs={{0,1},{1,2},{2,3},{3,7},{7,6},{6,5},{5,4},{4,0},{8,9},{9,10},{10,1... | collective-permute-start | bytes 12296 | tf_op jit(solution)/shard_map/ppermute | solution.py:227
  70.7 2.0 %collective-permute-start.33 = (f32[8,128]{1,0:T(8,128)S(1)}, f32[8,128]{1,0:T(8,128)S(1)}, u32[]{:S(2)}, u32[]{:S(2)}) collective-permute-start(f32[8,128]{1,0:T(8,128)S(1)} %shard_map.58.own), channel_id=1, source_target_pairs={{0,1},{1,2},{2,3},{3,7},{7,6},{6,5},{5,4},{4,0},{8,9},{9,10},{10,1... | collective-permute-start | bytes 12296 | tf_op jit(solution)/shard_map/ppermute | solution.py:227
  77.6 2.0 %collective-permute-start.38 = (f32[8,128]{1,0:T(8,128)S(1)}, f32[8,128]{1,0:T(8,128)S(1)}, u32[]{:S(2)}, u32[]{:S(2)}) collective-permute-start(f32[8,128]{1,0:T(8,128)S(1)} %shard_map.59.own), channel_id=1, source_target_pairs={{0,1},{1,2},{2,3},{3,7},{7,6},{6,5},{5,4},{4,0},{8,9},{9,10},{10,1... | collective-permute-start | bytes 12296 | tf_op jit(solution)/shard_map/ppermute | solution.py:227
  85.2 1.5 %collective-permute-start.40 = (f32[4,32,128]{2,1,0:T(8,128)S(1)}, f32[4,32,128]{2,1,0:T(8,128)S(1)}, u32[]{:S(2)}, u32[]{:S(2)}) collective-permute-start(f32[4,32,128]{2,1,0:T(8,128)S(1)} %shard_map.62), channel_id=1, source_target_pairs={{0,16},{16,0},{1,17},{17,1},{2,18},{18,2},{3,19},{19,3},{4,20},{20... | collective-permute-start | bytes 196616 | tf_op jit(solution)/shard_map/ppermute | solution.py:218
  86.7 3.1 %shard_map.61.refs_0_ = f32[24,32,128]{2,1,0:T(8,128)S(1)} custom-call(s32[8]{0:T(128)S(1)} %stack.59.flags, f32[24,32,128]{2,1,0:T(8,128)S(1)} %get-tuple-element.60.pre, s32[12,16,64]{2,1,0:T(8,128)S(1)} %copy-done.4, f32[8,128]{1,0:T(8,128)S(1)} %shard_map.60.coarse), custom_call_target="tpu_custom_call" | custom-call | flops 1000000 | bytes 100000 | tf_op jit(solution)/shard_map/pallas_call | solution.py:28
  90.5 1.7 %collective-permute-start.42 = (f32[128,128]{1,0:T(8,128)S(1)}, f32[128,128]{1,0:T(8,128)S(1)}, u32[]{:S(2)}, u32[]{:S(2)}) collective-permute-start(f32[128,128]{1,0:T(8,128)S(1)} %get-tuple-element.67), channel_id=1, source_target_pairs={{4,0},{8,4},{12,8},{0,12},{5,1},{9,5},{13,9},{1,13},{6,2},{10,6},{... | collective-permute-start | bytes 196616 | tf_op jit(solution)/shard_map/ppermute | solution.py:223
  92.2 1.9 %collective-permute-done.41.refs_3_ = f32[128,128]{1,0:T(8,128)S(1)} collective-permute-done((f32[128,128]{1,0:T(8,128)S(1)}, f32[128,128]{1,0:T(8,128)S(1)}, u32[]{:S(2)}, u32[]{:S(2)}) %collective-permute-start.41) | collective-permute-done | bytes 65568 | tf_op jit(solution)/shard_map/ppermute | solution.py:223
  95.0 1.6 %collective-permute-start.43 = (f32[40,128]{1,0:T(8,128)S(1)}, f32[40,128]{1,0:T(8,128)S(1)}, u32[]{:S(2)}, u32[]{:S(2)}) collective-permute-start(f32[40,128]{1,0:T(8,128)S(1)} %get-tuple-element.69), channel_id=1, source_target_pairs={{0,1},{1,2},{2,3},{3,7},{7,6},{6,5},{5,4},{4,0},{8,9},{9,10},{10,1... | collective-permute-start | bytes 61448 | tf_op jit(solution)/shard_map/ppermute | solution.py:227
  98.1 2.3 %collective-permute-done.44.back = f32[40,128]{1,0:T(8,128)S(1)} collective-permute-done((f32[40,128]{1,0:T(8,128)S(1)}, f32[40,128]{1,0:T(8,128)S(1)}, u32[]{:S(2)}, u32[]{:S(2)}) %collective-permute-start.44) | collective-permute-done | bytes 20512 | tf_op jit(solution)/shard_map/ppermute | solution.py:227
  100.4 5.6 %shard_map.65 = f32[24,32,128]{2,1,0:T(8,128)} custom-call(s32[8]{0:T(128)S(1)} %stack.59.flags, f32[1,32,56,128]{3,2,1,0:T(8,128)S(1)} %get-tuple-element.68.wide_ref, f32[40,128]{1,0:T(8,128)S(1)} %collective-permute-done.43.forth, f32[40,128]{1,0:T(8,128)S(1)} %collective-permute-done.44.back, f32[32,56,128]{2,1,0:T(8,128)S(1)} %get-tuple-element.71.refs_0_, ...), custom_call_target="tpu_custom_call" | custom-call | flops 1000000 | bytes 100000 | tf_op jit(solution)/shard_map/pallas_call | solution.py:28
  (99 shorter events, 40.7 us)
Async XLA Ops:
  1.5 9.7 %collective-permute-start = (f32[11,32,128]{2,1,0:T(8,128)S(1)}, f32[11,32,128]{2,1,0:T(8,128)S(1)}, u32[]{:S(2)}, u32[]{:S(2)}) collective-permute-start(f32[11,32,128]{2,1,0:T(8,128)S(1)} %shard_map.46.refs_0_), channel_id=1, source_target_pairs={{0,16},{16,0},{1,17},{17,1},{2,18},{18,2},{3,19},{19,3},{4,20},{20... | collective-permute-start | bytes 540680 | tf_op jit(solution)/shard_map/ppermute | solution.py:218
  11.9 5.9 %collective-permute-start.2 = (f32[400,128]{1,0:T(8,128)S(1)}, f32[400,128]{1,0:T(8,128)S(1)}, u32[]{:S(2)}, u32[]{:S(2)}) collective-permute-start(f32[400,128]{1,0:T(8,128)S(1)} %get-tuple-element.49), channel_id=1, source_target_pairs={{4,0},{8,4},{12,8},{0,12},{5,1},{9,5},{13,9},{1,13},{6,2},{10,6},{... | collective-permute-start | bytes 614408 | tf_op jit(solution)/shard_map/ppermute | solution.py:223
  12.6 6.8 %collective-permute-start.1 = (f32[400,128]{1,0:T(8,128)S(1)}, f32[400,128]{1,0:T(8,128)S(1)}, u32[]{:S(2)}, u32[]{:S(2)}) collective-permute-start(f32[400,128]{1,0:T(8,128)S(1)} %get-tuple-element.48.refs_2_), channel_id=1, source_target_pairs={{0,4},{4,8},{8,12},{12,0},{1,5},{5,9},{9,13},{13,1},{2,6},{6,10},{... | collective-permute-start | bytes 614408 | tf_op jit(solution)/shard_map/ppermute | solution.py:223
  20.9 6.3 %collective-permute-start.4 = (f32[136,128]{1,0:T(8,128)S(1)}, f32[136,128]{1,0:T(8,128)S(1)}, u32[]{:S(2)}, u32[]{:S(2)}) collective-permute-start(f32[136,128]{1,0:T(8,128)S(1)} %get-tuple-element.56), channel_id=1, source_target_pairs={{1,0},{2,1},{3,2},{7,3},{6,7},{5,6},{4,5},{0,4},{9,8},{10,9},{11,1... | collective-permute-start | bytes 208904 | tf_op jit(solution)/shard_map/ppermute | solution.py:227
  20.9 6.3 %collective-permute-start.3 = (f32[136,128]{1,0:T(8,128)S(1)}, f32[136,128]{1,0:T(8,128)S(1)}, u32[]{:S(2)}, u32[]{:S(2)}) collective-permute-start(f32[136,128]{1,0:T(8,128)S(1)} %get-tuple-element.55.refs_2_), channel_id=1, source_target_pairs={{0,1},{1,2},{2,3},{3,7},{7,6},{6,5},{5,4},{4,0},{8,9},{9,10},{10,1... | collective-permute-start | bytes 208904 | tf_op jit(solution)/shard_map/ppermute | solution.py:227
  36.3 6.1 %collective-permute-start.9 = (f32[8,128]{1,0:T(8,128)S(1)}, f32[8,128]{1,0:T(8,128)S(1)}, u32[]{:S(2)}, u32[]{:S(2)}) collective-permute-start(f32[8,128]{1,0:T(8,128)S(1)} %get-tuple-element.64.scaled_rhs.own), channel_id=1, source_target_pairs={{1,0},{2,1},{3,2},{7,3},{6,7},{5,6},{4,5},{0,4},{9,8},{10,9},{11,1... | collective-permute-start | bytes 12296 | tf_op jit(solution)/shard_map/ppermute | solution.py:227
  36.3 6.1 %collective-permute-start.8 = (f32[8,128]{1,0:T(8,128)S(1)}, f32[8,128]{1,0:T(8,128)S(1)}, u32[]{:S(2)}, u32[]{:S(2)}) collective-permute-start(f32[8,128]{1,0:T(8,128)S(1)} %get-tuple-element.64.scaled_rhs.own), channel_id=1, source_target_pairs={{0,1},{1,2},{2,3},{3,7},{7,6},{6,5},{5,4},{4,0},{8,9},{9,10},{10,1... | collective-permute-start | bytes 12296 | tf_op jit(solution)/shard_map/ppermute | solution.py:227
  38.3 4.1 %collective-permute-start.7 = (f32[8,128]{1,0:T(8,128)S(1)}, f32[8,128]{1,0:T(8,128)S(1)}, u32[]{:S(2)}, u32[]{:S(2)}) collective-permute-start(f32[8,128]{1,0:T(8,128)S(1)} %get-tuple-element.64.scaled_rhs.own), channel_id=1, source_target_pairs={{4,0},{8,4},{12,8},{0,12},{5,1},{9,5},{13,9},{1,13},{6,2},{10,6},{... | collective-permute-start | bytes 12296 | tf_op jit(solution)/shard_map/ppermute | solution.py:223
  38.3 4.1 %collective-permute-start.6 = (f32[8,128]{1,0:T(8,128)S(1)}, f32[8,128]{1,0:T(8,128)S(1)}, u32[]{:S(2)}, u32[]{:S(2)}) collective-permute-start(f32[8,128]{1,0:T(8,128)S(1)} %get-tuple-element.64.scaled_rhs.own), channel_id=1, source_target_pairs={{0,4},{4,8},{8,12},{12,0},{1,5},{5,9},{9,13},{13,1},{2,6},{6,10},{... | collective-permute-start | bytes 12296 | tf_op jit(solution)/shard_map/ppermute | solution.py:223
  43.2 4.1 %collective-permute-start.14 = (f32[8,128]{1,0:T(8,128)S(1)}, f32[8,128]{1,0:T(8,128)S(1)}, u32[]{:S(2)}, u32[]{:S(2)}) collective-permute-start(f32[8,128]{1,0:T(8,128)S(1)} %shard_map.54.own), channel_id=1, source_target_pairs={{1,0},{2,1},{3,2},{7,3},{6,7},{5,6},{4,5},{0,4},{9,8},{10,9},{11,1... | collective-permute-start | bytes 12296 | tf_op jit(solution)/shard_map/ppermute | solution.py:227
  50.0 4.1 %collective-permute-start.19 = (f32[8,128]{1,0:T(8,128)S(1)}, f32[8,128]{1,0:T(8,128)S(1)}, u32[]{:S(2)}, u32[]{:S(2)}) collective-permute-start(f32[8,128]{1,0:T(8,128)S(1)} %shard_map.55.own), channel_id=1, source_target_pairs={{1,0},{2,1},{3,2},{7,3},{6,7},{5,6},{4,5},{0,4},{9,8},{10,9},{11,1... | collective-permute-start | bytes 12296 | tf_op jit(solution)/shard_map/ppermute | solution.py:227
  50.2 3.9 %collective-permute-start.18 = (f32[8,128]{1,0:T(8,128)S(1)}, f32[8,128]{1,0:T(8,128)S(1)}, u32[]{:S(2)}, u32[]{:S(2)}) collective-permute-start(f32[8,128]{1,0:T(8,128)S(1)} %shard_map.55.own), channel_id=1, source_target_pairs={{0,1},{1,2},{2,3},{3,7},{7,6},{6,5},{5,4},{4,0},{8,9},{9,10},{10,1... | collective-permute-start | bytes 12296 | tf_op jit(solution)/shard_map/ppermute | solution.py:227
  56.9 4.1 %collective-permute-start.24 = (f32[8,128]{1,0:T(8,128)S(1)}, f32[8,128]{1,0:T(8,128)S(1)}, u32[]{:S(2)}, u32[]{:S(2)}) collective-permute-start(f32[8,128]{1,0:T(8,128)S(1)} %shard_map.56.own), channel_id=1, source_target_pairs={{1,0},{2,1},{3,2},{7,3},{6,7},{5,6},{4,5},{0,4},{9,8},{10,9},{11,1... | collective-permute-start | bytes 12296 | tf_op jit(solution)/shard_map/ppermute | solution.py:227
  56.9 4.0 %collective-permute-start.23 = (f32[8,128]{1,0:T(8,128)S(1)}, f32[8,128]{1,0:T(8,128)S(1)}, u32[]{:S(2)}, u32[]{:S(2)}) collective-permute-start(f32[8,128]{1,0:T(8,128)S(1)} %shard_map.56.own), channel_id=1, source_target_pairs={{0,1},{1,2},{2,3},{3,7},{7,6},{6,5},{5,4},{4,0},{8,9},{9,10},{10,1... | collective-permute-start | bytes 12296 | tf_op jit(solution)/shard_map/ppermute | solution.py:227
  63.8 4.1 %collective-permute-start.29 = (f32[8,128]{1,0:T(8,128)S(1)}, f32[8,128]{1,0:T(8,128)S(1)}, u32[]{:S(2)}, u32[]{:S(2)}) collective-permute-start(f32[8,128]{1,0:T(8,128)S(1)} %shard_map.57.own), channel_id=1, source_target_pairs={{1,0},{2,1},{3,2},{7,3},{6,7},{5,6},{4,5},{0,4},{9,8},{10,9},{11,1... | collective-permute-start | bytes 12296 | tf_op jit(solution)/shard_map/ppermute | solution.py:227
  63.8 4.0 %collective-permute-start.28 = (f32[8,128]{1,0:T(8,128)S(1)}, f32[8,128]{1,0:T(8,128)S(1)}, u32[]{:S(2)}, u32[]{:S(2)}) collective-permute-start(f32[8,128]{1,0:T(8,128)S(1)} %shard_map.57.own), channel_id=1, source_target_pairs={{0,1},{1,2},{2,3},{3,7},{7,6},{6,5},{5,4},{4,0},{8,9},{9,10},{10,1... | collective-permute-start | bytes 12296 | tf_op jit(solution)/shard_map/ppermute | solution.py:227
  70.7 4.1 %collective-permute-start.34 = (f32[8,128]{1,0:T(8,128)S(1)}, f32[8,128]{1,0:T(8,128)S(1)}, u32[]{:S(2)}, u32[]{:S(2)}) collective-permute-start(f32[8,128]{1,0:T(8,128)S(1)} %shard_map.58.own), channel_id=1, source_target_pairs={{1,0},{2,1},{3,2},{7,3},{6,7},{5,6},{4,5},{0,4},{9,8},{10,9},{11,1... | collective-permute-start | bytes 12296 | tf_op jit(solution)/shard_map/ppermute | solution.py:227
  70.7 4.0 %collective-permute-start.33 = (f32[8,128]{1,0:T(8,128)S(1)}, f32[8,128]{1,0:T(8,128)S(1)}, u32[]{:S(2)}, u32[]{:S(2)}) collective-permute-start(f32[8,128]{1,0:T(8,128)S(1)} %shard_map.58.own), channel_id=1, source_target_pairs={{0,1},{1,2},{2,3},{3,7},{7,6},{6,5},{5,4},{4,0},{8,9},{9,10},{10,1... | collective-permute-start | bytes 12296 | tf_op jit(solution)/shard_map/ppermute | solution.py:227
  77.6 4.1 %collective-permute-start.39 = (f32[8,128]{1,0:T(8,128)S(1)}, f32[8,128]{1,0:T(8,128)S(1)}, u32[]{:S(2)}, u32[]{:S(2)}) collective-permute-start(f32[8,128]{1,0:T(8,128)S(1)} %shard_map.59.own), channel_id=1, source_target_pairs={{1,0},{2,1},{3,2},{7,3},{6,7},{5,6},{4,5},{0,4},{9,8},{10,9},{11,1... | collective-permute-start | bytes 12296 | tf_op jit(solution)/shard_map/ppermute | solution.py:227
  77.6 4.0 %collective-permute-start.38 = (f32[8,128]{1,0:T(8,128)S(1)}, f32[8,128]{1,0:T(8,128)S(1)}, u32[]{:S(2)}, u32[]{:S(2)}) collective-permute-start(f32[8,128]{1,0:T(8,128)S(1)} %shard_map.59.own), channel_id=1, source_target_pairs={{0,1},{1,2},{2,3},{3,7},{7,6},{6,5},{5,4},{4,0},{8,9},{9,10},{10,1... | collective-permute-start | bytes 12296 | tf_op jit(solution)/shard_map/ppermute | solution.py:227
  85.2 4.6 %collective-permute-start.40 = (f32[4,32,128]{2,1,0:T(8,128)S(1)}, f32[4,32,128]{2,1,0:T(8,128)S(1)}, u32[]{:S(2)}, u32[]{:S(2)}) collective-permute-start(f32[4,32,128]{2,1,0:T(8,128)S(1)} %shard_map.62), channel_id=1, source_target_pairs={{0,16},{16,0},{1,17},{17,1},{2,18},{18,2},{3,19},{19,3},{4,20},{20... | collective-permute-start | bytes 196616 | tf_op jit(solution)/shard_map/ppermute | solution.py:218
  90.4 3.7 %collective-permute-start.41 = (f32[128,128]{1,0:T(8,128)S(1)}, f32[128,128]{1,0:T(8,128)S(1)}, u32[]{:S(2)}, u32[]{:S(2)}) collective-permute-start(f32[128,128]{1,0:T(8,128)S(1)} %get-tuple-element.66), channel_id=1, source_target_pairs={{0,4},{4,8},{8,12},{12,0},{1,5},{5,9},{9,13},{13,1},{2,6},{6,10},{... | collective-permute-start | bytes 196616 | tf_op jit(solution)/shard_map/ppermute | solution.py:223
  90.5 3.7 %collective-permute-start.42 = (f32[128,128]{1,0:T(8,128)S(1)}, f32[128,128]{1,0:T(8,128)S(1)}, u32[]{:S(2)}, u32[]{:S(2)}) collective-permute-start(f32[128,128]{1,0:T(8,128)S(1)} %get-tuple-element.67), channel_id=1, source_target_pairs={{4,0},{8,4},{12,8},{0,12},{5,1},{9,5},{13,9},{1,13},{6,2},{10,6},{... | collective-permute-start | bytes 196616 | tf_op jit(solution)/shard_map/ppermute | solution.py:223
  96.6 3.8 %collective-permute-start.44 = (f32[40,128]{1,0:T(8,128)S(1)}, f32[40,128]{1,0:T(8,128)S(1)}, u32[]{:S(2)}, u32[]{:S(2)}) collective-permute-start(f32[40,128]{1,0:T(8,128)S(1)} %get-tuple-element.70), channel_id=1, source_target_pairs={{1,0},{2,1},{3,2},{7,3},{6,7},{5,6},{4,5},{0,4},{9,8},{10,9},{11,1... | collective-permute-start | bytes 61448 | tf_op jit(solution)/shard_map/ppermute | solution.py:227
  (27 other events, 135.6 us)

commit v4 on v3

--- a/solution.py
+++ b/solution.py
@@ -88,33 +88,31 @@
 
 def pack_x_kernel(count, widths, flags, *refs):
     fields = len(widths)
-    ins, labels, outs = refs[:fields], refs[fields], refs[fields + 1 : -2]
+    ins, refs = refs[: fields + 1], refs[fields + 1 :]
+    kept, outs = refs[: fields + 1], refs[fields + 1 : -2]
     near, sems = refs[-2:]
     nx, ny = ins[0].shape[0], ins[0].shape[1]
     base = bases(widths)
-    copies = []
+    pairs = []
     for s, out in enumerate(outs):
+
+        def place(size, width, s=s):
+            if count == 2:
+                return jnp.where(flags[IX] == 0, size - width, 0)
+            return (size - width, 0)[s]
+
         for f, (ref, width) in enumerate(zip(ins, widths)):
-            if count == 2:
-                at = jnp.where(flags[IX] == 0, nx - width, 0)
-            else:
-                at = (nx - width, 0)[s]
-            copies.append(
-                pltpu.make_async_copy(
-                    ref.at[pl.ds(at, width)], out.at[pl.ds(base[f], width)], sems.at[len(copies)]
-                )
-            )
-        if count == 2:
-            at = jnp.where(flags[IX] == 0, nx // 2 - 1, 0)
-        else:
-            at = (nx // 2 - 1, 0)[s]
-        copies.append(pltpu.make_async_copy(labels.at[at], near.at[s], sems.at[len(copies)]))
+            pairs.append((ref.at[pl.ds(place(nx, width), width)], out.at[pl.ds(base[f], width)]))
+        pairs.append((ins[-1].at[place(nx // 2, 1)], near.at[s]))
+    pairs += list(zip(ins, kept))
+    copies = [pltpu.make_async_copy(src, dst, sems.at[n]) for n, (src, dst) in enumerate(pairs)]
     for copy in copies:
         copy.start()
+    for out in outs:
+        out[base[-1]] = jnp.zeros(out.shape[1:], F32)
     for copy in copies:
         copy.wait()
     for s, out in enumerate(outs):
-        out[base[-1]] = jnp.zeros(out.shape[1:], F32)
         out[base[-1], : ny // 2, : near.shape[2]] = near[s].astype(F32)
 
 
@@ -133,31 +131,38 @@
     fields = len(widths)
     ins = refs[:fields]
     low, high = refs[fields + labels : fields + labels + 2]
-    to_high, to_low = refs[fields + labels + 2 :]
+    inner, outer = refs[fields + labels + 2 :]
     nx, ny = ins[0].shape[0], ins[0].shape[1]
     frame = Frame(nx, ny)
     base = bases(widths)
+    even = flags[PARITY] == 0
+
+    def send(at, count, to_high, to_low):
+        inner[at : at + count] = jnp.where(even, to_high, to_low)
+        outer[at : at + count] = jnp.where(even, to_low, to_high)
+
     for f in range(fields):
         for x in range(frame.wide):
             slab = slab_of(ins[f], low, high, base[f], widths[f], x)
             at = (f * frame.wide + x) * HALO
             if slab is None:
                 slab = jnp.ones((ny, LANES), F32)
-            to_high[at : at + HALO] = slab[ny - HALO :]
-            to_low[at : at + HALO] = slab[:HALO]
+            send(at, HALO, slab[ny - HALO :], slab[:HALO])
     if labels:
         at = fields * frame.wide * HALO
         nb, rows, width = refs[fields].shape
-        for out, row in ((to_high, rows - 1), (to_low, 0)):
+        for out in (inner, outer):
             out[at:] = jnp.zeros((out.shape[0] - at, LANES), F32)
-            for b in range(nb):
-                out[at + b : at + b + 1, :width] = refs[fields][b, row : row + 1].astype(F32)
+        for b in range(nb):
+            high, low = (refs[fields][b, row : row + 1].astype(F32) for row in (rows - 1, 0))
+            inner[at + b : at + b + 1, :width] = jnp.where(even, high, low)
+            outer[at + b : at + b + 1, :width] = jnp.where(even, low, high)
 
 
 def pack_z_kernel(widths, labels, flags, *refs):
     fields = len(widths)
     ins = refs[:fields]
-    x_low, x_high, y_low, y_high = refs[fields + labels : fields + labels + 4]
+    x_low, x_high, inner, outer = refs[fields + labels : fields + labels + 4]
     wide_ref, send_forth, send_back = refs[fields + labels + 4 :]
     nx, ny = ins[0].shape[0], ins[0].shape[1]
     frame = Frame(nx, ny)
@@ -177,8 +182,9 @@
             at = (f * frame.wide + x) * HALO
             slab = slab_of(ins[f], x_low, x_high, base[f], widths[f], x)
             wide_ref[f, x, own : own + ny] = jnp.ones((ny, LANES), F32) if slab is None else slab
-            wide_ref[f, x, SUB:own] = y_low[at : at + HALO]
-            wide_ref[f, x, own + ny : own + ny + HALO] = y_high[at : at + HALO]
+            low, high = sides(flags, outer[at : at + HALO], inner[at : at + HALO])
+            wide_ref[f, x, SUB:own] = low
+            wide_ref[f, x, own + ny : own + ny + HALO] = high
             wide_ref[f, x, :SUB] = spare
             wide_ref[f, x, SUB + tall :] = spare
             moved = turned(wide_ref[f, x, SUB : SUB + tall], HALO * (x + 1), 1)
@@ -200,31 +206,41 @@
     def __init__(self, mesh):
         self.sizes = [mesh.shape[a] for a in ("gx", "gy", "gz")]
         n_x, n_y, n_z = self.sizes
+
+        def at(i, j, k):
+            return (i * n_y + j) * n_z + k
+
         self.ring_x = [(i, (i + 1) % n_x) for i in range(n_x)]
-        self.ring_y = [(i, (i + 1) % n_y) for i in range(n_y)]
-        self.snake = []
+        self.inner, self.outer, self.snake = [], [], []
         for i in range(n_x):
+            for j in range(n_y):
+                for k in range(n_z):
+                    self.inner.append((at(i, j, k), at(i, j ^ 1, k)))
+                    over = (i, j + 1) if j % 2 else (i, j - 1)
+                    over = over if 0 <= over[1] < n_y else (i ^ 1, j)
+                    self.outer.append((at(i, j, k), at(*over, k)))
             for j in range(0, n_y, 2):
-                nodes = [(i * n_y + j) * n_z + k for k in range(n_z)]
-                nodes += [(i * n_y + j + 1) * n_z + k for k in reversed(range(n_z))]
+                nodes = [at(i, j, k) for k in range(n_z)] + [at(i, j + 1, k) for k in reversed(range(n_z))]
                 self.snake += [(nodes[m], nodes[(m + 1) % len(nodes)]) for m in range(len(nodes))]
 
     @staticmethod
     def back(pairs):
         return [(b, a) for a, b in pairs]
 
+    @staticmethod
+    def send(values, pairs):
+        return lax.ppermute(values, ("gx", "gy", "gz"), pairs)
+
     def x(self, sends):
         if self.sizes[0] == 2:
-            got = lax.ppermute(sends[0], "gx", self.ring_x)
-            return got, got
-        return lax.ppermute(sends[0], "gx", self.ring_x), lax.ppermute(sends[-1], "gx", self.back(self.ring_x))
-
-    def y(self, to_high, to_low):
-        return lax.ppermute(to_high, "gy", self.ring_y), lax.ppermute(to_low, "gy", self.back(self.ring_y))
+            return (lax.ppermute(sends[0], "gx", self.ring_x),)
+        return lax.ppermute(sends[0], "gx", self.ring_x), lax.ppermute(sends[1], "gx", self.back(self.ring_x))
+
+    def y(self, inner, outer):
+        return self.send(inner, self.inner), self.send(outer, self.outer)
 
     def z(self, forth, back):
-        axes = ("gx", "gy", "gz")
-        return lax.ppermute(forth, axes, self.snake), lax.ppermute(back, axes, self.back(self.snake))
+        return self.send(forth, self.snake), self.send(back, self.back(self.snake))
 
 
 def widened(links, flags, widths, arrays, from_x, beside_y=None, beside_z=None):
@@ -232,14 +248,14 @@
     nx, ny, nz = arrays[0].shape
     frame = Frame(nx, ny)
     rows = fields * frame.wide * HALO + labels * ny // 2
-    sends = call(functools.partial(pack_y_kernel, widths, labels), [shaped(rows, nz)] * 2)(flags, *arrays, *from_x)
+    sends = call(functools.partial(pack_y_kernel, widths, labels), [shaped(rows, nz)] * 2)(flags, *arrays, from_x[0], from_x[-1])
     work = beside_y(sends[0]) if beside_y else ()
     from_y = links.y(*sends)
     from_y = lax.optimization_barrier((*from_y, *work))[:2] if work else from_y
     rows = fields * frame.tall + labels * ny // 2
     wide, *sends = call(
         functools.partial(pack_z_kernel, widths, labels), [shaped(fields, *frame.main)] + [shaped(rows, nz)] * 2
-    )(flags, *arrays, *from_x, *from_y)
+    )(flags, *arrays, from_x[0], from_x[-1], *from_y)
     if beside_z:
         beside_z(sends[0])
     return (wide, *links.z(*sends)), from_y
@@ -316,10 +332,7 @@
 
 
 def lane_total(values):
-    ones = jnp.ones((SUB, LANES), F32)
-    return lax.dot_general(
-        ones, values, (((1,), (1,)), ((), ())), precision=lax.Precision.HIGHEST, preferred_element_type=F32
-    )
+    return jnp.broadcast_to(jnp.sum(values.T, axis=0, keepdims=True), (SUB, LANES))
 
 
 def paired(values):
@@ -327,10 +340,10 @@
     return picked(values + turned(values, -1, 1), even)
 
 
-def fine_kernel(flags, wide_ref, forth, back, from_x_low, from_x_high, from_y_low, from_y_high, block_label,
+def fine_kernel(flags, wide_ref, forth, back, from_x_low, from_x_high, inner, outer, block_label,
                 face_label, inner_diag, *refs):
     main, ends = refs[:6], refs[6:12]
-    pre, face_near, face_weight, scaled_rhs, scale, once, once_ends, res, diag = refs[12:]
+    pre, face_near, face_weight, scaled_rhs, scale, once, once_ends, res, diag, block_res = refs[12:]
     wx, wy, wz_up, wz_low, inv_diag, start = main
     ex, ey, ez_up, ez_low, inv_ends, start_ends = ends
     nx, ny = pre.shape[0], pre.shape[1]
@@ -443,16 +456,23 @@
     def rows_at(ref, x, off):
         return ref[x, pl.ds(frame.own + off, half, stride=2)]
 
-    def add_rows(total, labels, values, rows):
-        for r in range(rows):
-            total = total + jnp.where(labels[r : r + 1] == iota, values[r : r + 1], 0.0)
+    def add_rows(total, labels, b, values, c):
+        for r in range(SUB):
+            total = total + jnp.where(labels[b, r : r + 1] == iota, values[c, r : r + 1], 0.0)
         return total
 
+    def to_blocks(bs, carry):
+        for b in bs:
+            four = sum(rows_at(res, 2 * b + a, c) for a in range(2) for c in range(2))
+            block_res[b] = pack_rows(paired(four))
+        return carry
+
+    batched(0, nb, to_blocks, 0)
+    zeros = jnp.zeros((AGG, LANES), F32)
+
     def restrict(b, total):
-        four = sum(rows_at(res, 2 * b + a, c) for a in range(2) for c in range(2))
-        return add_rows(total, block_label[b], pack_rows(paired(four)), SUB)
-
-    zeros = jnp.zeros((AGG, LANES), F32)
+        return add_rows(total, block_label, b, block_res, b)
+
     sums = lax.fori_loop(0, nb, restrict, zeros)
 
     blank = jnp.zeros((half - nb, LANES), F32)
@@ -470,7 +490,7 @@
         face_weight[s] = pack_rows(jnp.where(lane < nb, picked(values, spot), 0.0))
     around = zeros
     for s in range(6):
-        around = add_rows(around, face_label[s], face_weight[s], SUB)
+        around = add_rows(around, face_label, s, face_weight, s)
     scale[...] = OMEGA_COARSE / (inner_diag[...] + lane_total(around))
     scaled_rhs[...] = scale[...] * lane_total(sums)
 
@@ -478,43 +498,44 @@
     face_near[0] = pack_rows(from_x_low[at, :half])
     face_near[1] = pack_rows(from_x_high[at, :half])
     at = 3 * wide * HALO
-    face_near[2] = pack_rows(from_y_low[at : at + half])
-    face_near[3] = pack_rows(from_y_high[at : at + half])
+    for s, values in enumerate(sides(flags, outer[at : at + half], inner[at : at + half])):
+        face_near[2 + s] = pack_rows(values)
     below, above = sides(flags, forth[3 * tall : 3 * tall + half], back[3 * tall : 3 * tall + half])
     face_near[4] = pack_rows(below)
     face_near[5] = pack_rows(above)
 
 
-def tile_product(left, right, labels, pairs):
+def fill(left, right, labels, b, pairs):
     iota = row_no((AGG, LANES)).astype(F32)
     for r in range(SUB):
         lanes = pl.ds(r * LANES, LANES)
-        left[:, lanes] = jnp.where(labels[r : r + 1] == iota, 1.0, 0.0).astype(BF16)
-        held = sum(jnp.where(near[r : r + 1] == iota, w[r : r + 1], 0.0) for near, w in pairs)
+        row = pl.ds(r, 1)
+        left[:, lanes] = jnp.where(labels[b, row] == iota, 1.0, 0.0).astype(BF16)
+        held = sum(jnp.where(near[row] == iota, w[row], 0.0) for near, w in pairs)
         high = held.astype(BF16)
         right[:AGG, lanes] = high
         right[AGG:, lanes] = (held - high.astype(F32)).astype(BF16)
+
+
+def product(left, right):
     return lax.dot_general(left[...], right[...], (((1,), (1,)), ((), ())), preferred_element_type=F32)
 
 
-def keep_tile(out, at, tile):
+def both_halves(tile):
+    return tile[:, :AGG] + tile[:, AGG:]
+
+
+def keep_tile(out, t, tile):
     high = tile.astype(BF16)
-    out[pl.ds(at, AGG), :AGG] = high
-    out[pl.ds(at, AGG), AGG:] = (tile - high.astype(F32)).astype(BF16)
-
-
-def own_kernel(first, count, last, flags, cond, absorb, block_agg, *refs):
-    if last:
-        tile_in, around_in, _, out, block_label, face_label, inner_diag, part, line, left, right = refs
-    elif first:
-        tile_in, around_in, _, tile_out, around_out, part, line, left, right = refs
-    else:
-        _, tile_out, around_out, part, line, left, right = refs
+    rows = pl.ds(t * AGG, AGG)
+    out[rows, :AGG] = high
+    out[rows, AGG:] = (tile - high.astype(F32)).astype(BF16)
+
+
+def blocks_kernel(flags, cond, absorb, block_agg, _, block_label, near, weights, inner, face_label, lift, part, line):
     nx, ny = cond.shape[0], cond.shape[1]
     nb, half, width = nx // 2, ny // 2, LANES // 2
     lane, row = lane_no((half, LANES)), row_no((half, LANES))
-    even = 2 * (lane % width)
-    iota = row_no((AGG, LANES)).astype(F32)
 
     def halves(values, slot):
         part[slot] = values
@@ -524,76 +545,97 @@
         values = block_agg[b].astype(F32)
         return jnp.concatenate([values, values], axis=1)
 
-    def upper_x(b):
-        x = 2 * b
+    def upper_x(b, slot):
+        x = jnp.maximum(2 * b, 0)
         faces = weight(cond[x + 1], cond[jnp.minimum(x + 2, nx - 1)])
-        return jnp.where(b == nb - 1, 0.0, paired(sum(halves(faces, 0))))
-
-    def step(b, carry):
-        low_x, tile, around = carry
-        x = 2 * b
-        one, two = cond[x], cond[x + 1]
-        both_y = weight(one, turned(one, -1, 0)) + weight(two, turned(two, -1, 0))
-        both_z = weight(one, turned(one, -1, 1)) + weight(two, turned(two, -1, 1))
-        high_x = upper_x(b)
-        high_y = jnp.where(row == half - 1, 0.0, paired(halves(both_y, 1)[1]))
-        high_z = jnp.where(lane % width == width - 1, 0.0, picked(sum(halves(both_z, 2)), even + 1))
-        low_y = turned(high_y, 1, 0)
-        low_z = turned(high_z, 1, 1)
-        own = label_at(b)
-        near_x, past_x = label_at(jnp.minimum(b + 1, nb - 1)), label_at(jnp.maximum(b - 1, 0))
-        near_y, past_y = turned(own, -1, 0), turned(own, 1, 0)
-        near_z, past_z = turned(own, -1, 1), turned(own, 1, 1)
-        total = paired(sum(halves(absorb[x] + absorb[x + 1], 3)))
-        for near, values in (
-            (near_x, high_x), (past_x, low_x), (near_y, high_y), (past_y, low_y), (near_z, high_z), (past_z, low_z)
-        ):
-            total = total + jnp.where(near != own, values, 0.0)
-        packed, total = pack_rows(own), pack_rows(total)
-        pairs = [
-            (pack_rows(near_x), pack_rows(high_x)),
-            (pack_rows(near_y), pack_rows(high_y)),
-            (pack_rows(near_z), pack_rows(high_z)),
-        ]
-        tile = tile + tile_product(left, right, packed, pairs)
-        for r in range(SUB):
-            around = around + jnp.where(packed[r : r + 1] == iota, total[r : r + 1], 0.0)
-        return high_x, tile, around
-
-    if first:
-        start = (upper_x(first - 1), tile_in[...], around_in[...])
-    else:
-        start = tuple(jnp.zeros(shape, F32) for shape in ((half, LANES), (AGG, 2 * AGG), (AGG, LANES)))
-    _, tile, around = lax.fori_loop(first, first + count, step, start)
-    if not last:
-        tile_out[...], around_out[...] = tile, around
-        return
-    tile = tile[:, :AGG] + tile[:, AGG:]
-    keep_tile(out, 0, jnp.where(row_no((AGG, AGG)) == lane_no((AGG, AGG)), 0.0, tile + tile.T))
-    inner_diag[...] = lane_total(around)
+        return jnp.where((b == nb - 1) | (b < 0), 0.0, paired(sum(halves(faces, slot))))
+
+    def step(bs, carry):
+        low_x = upper_x(bs[0] - 1, 0)
+        for k, b in enumerate(bs):
+            x = 2 * b
+            slot = 4 * k + 1
+            one, two = cond[x], cond[x + 1]
+            both_y = weight(one, turned(one, -1, 0)) + weight(two, turned(two, -1, 0))
+            both_z = weight(one, turned(one, -1, 1)) + weight(two, turned(two, -1, 1))
+            high_x = upper_x(b, slot)
+            high_y = jnp.where(row == half - 1, 0.0, paired(halves(both_y, slot + 1)[1]))
+            high_z = picked(sum(halves(both_z, slot + 2)), 2 * (lane % width) + 1)
+            high_z = jnp.where(lane % width == width - 1, 0.0, high_z)
+            low_y, low_z = turned(high_y, 1, 0), turned(high_z, 1, 1)
+            own = label_at(b)
+            near_x, past_x = label_at(jnp.minimum(b + 1, nb - 1)), label_at(jnp.maximum(b - 1, 0))
+            near_y, past_y = turned(own, -1, 0), turned(own, 1, 0)
+            near_z, past_z = turned(own, -1, 1), turned(own, 1, 1)
+            total = paired(sum(halves(absorb[x] + absorb[x + 1], slot + 3)))
+            for beside, values in (
+                (near_x, high_x), (past_x, low_x), (near_y, high_y), (past_y, low_y), (near_z, high_z), (past_z, low_z)
+            ):
+                total = total + jnp.where(beside != own, values, 0.0)
+            block_label[b] = pack_rows(own)
+            inner[b] = pack_rows(total)
+            for d, (beside, values) in enumerate(((near_x, high_x), (near_y, high_y), (near_z, high_z))):
+                near[d, b], weights[d, b] = pack_rows(beside), pack_rows(values)
+            lift[b] = picked(own, lane // 2).astype(jnp.int32)
+            low_x = high_x
+        return carry
+
+    batched(0, nb, step, 0, 4)
     line[...] = jnp.zeros(line.shape, F32)
+    low, high = jnp.zeros((half, LANES), F32), jnp.zeros((half, LANES), F32)
     for b in range(nb):
         own = label_at(b)
-        block_label[b] = pack_rows(own)
         line[0, b : b + 1], line[1, b : b + 1] = own[:1], own[half - 1 :]
-        line[2] = jnp.where(lane == b, own[:, :1], line[2])
-        line[3] = jnp.where(lane == b, own[:, width - 1 : width], line[3])
+        low = jnp.where(lane == b, own[:, :1], low)
+        high = jnp.where(lane == b, own[:, width - 1 : width], high)
     face_label[0], face_label[1] = block_label[0], block_label[nb - 1]
-    for s in range(4):
-        face_label[2 + s] = pack_rows(line[s])
-
-
-def faces_kernel(flags, own, face_label, face_near, face_weight, out, left, right):
+    for s, values in enumerate((line[0], line[1], low, high)):
+        face_label[2 + s] = pack_rows(values)
+
+
+def own_kernel(first, last, total, flags, block_label, near, weights, inner, *refs):
+    so_far, refs = (refs[0], refs[1:]) if first else (None, refs)
+    refs = refs[1:]
+    iota = row_no((AGG, LANES)).astype(F32)
+
+    def step(bs, tile):
+        for k, b in enumerate(bs):
+            left, right = refs[-4 + 2 * (k % 2) :][:2]
+            fill(left, right, block_label, b, [(near.at[d, b], weights.at[d, b]) for d in range(3)])
+            tile = tile + product(left, right)
+        return tile
+
+    tile = so_far[...] if first else jnp.zeros((AGG, 2 * AGG), F32)
+    tile = batched(first, last, step, tile, 2)
+    if last < total:
+        refs[0][...] = tile
+        return
+    out, inner_diag = refs[:2]
+    tile = both_halves(tile)
+    keep_tile(out, 0, jnp.where(row_no((AGG, AGG)) == lane_no((AGG, AGG)), 0.0, tile + tile.T))
+
+    def gather(b, around):
+        for r in range(SUB):
+            around = around + jnp.where(block_label[b, r : r + 1] == iota, inner[b, r : r + 1], 0.0)
+        return around
+
+    inner_diag[...] = lane_total(lax.fori_loop(0, total, gather, jnp.zeros((AGG, LANES), F32)))
+
+
+def faces_kernel(count, flags, own, face_label, face_near, face_weight, out, *factors):
     out[:AGG] = own[...]
-
-    @pl.loop(0, 6)
-    def _(s):
-        tile = tile_product(left, right, face_near[s], [(face_label[s], face_weight[s])])
-        keep_tile(out, (s + 1) * AGG, tile[:, :AGG] + tile[:, AGG:])
-
-
-def turn_kernel(flags, tiles, scaled_rhs, scale, own, x_low, x_high, y_low, y_high, forth, back, out):
-    vectors = [own[...], x_low[...], x_high[...], y_low[...], y_high[...], *sides(flags, forth[...], back[...])]
+    s = jnp.where(flags[IX] == 0, 1, 0)
+    faces = ([s] if count == 2 else [0, 1]) + [2, 3, 4, 5]
+    for t, s in enumerate(faces):
+        left, right = factors[2 * (t % 2) :][:2]
+        fill(left, right, face_near, s, [(face_label.at[s], face_weight.at[s])])
+        keep_tile(out, t + 1, both_halves(product(left, right)))
+
+
+def turn_kernel(flags, tiles, scaled_rhs, scale, own, *refs):
+    *from_x, inner, outer, forth, back, out = refs
+    vectors = [own[...]] + [ref[...] for ref in from_x]
+    vectors += [*sides(flags, outer[...], inner[...]), *sides(flags, forth[...], back[...])]
     row = row_no((SUB, AGG))
     parts = []
     for v in vectors:
@@ -604,36 +646,35 @@
     out[...] = (1.0 - OMEGA_COARSE) * own[...] + scaled_rhs[...] + scale[...] * applied
 
 
-def lifted(pre, block_agg, table, out, b, at):
+def lifted(pre, lift, table, out, bs, at):
     half = pre.shape[1] // 2
-    labels = block_agg[b]
-    labels = jnp.concatenate([labels, labels], axis=1)
-    labels = picked(labels, lane_no((half, LANES)) // 2)
-    values = picked(table, labels)
-    for a in range(2):
-        for c in range(2):
-            rows = pl.ds(c, half, stride=2)
-            out[at + a, rows] = pre[2 * b + a, rows] + values
-
-
-def send_kernel(count, flags, pre, block_agg, coarse, *outs):
+    for n, b in enumerate(bs):
+        values = picked(table, lift[b])
+        for a in range(2):
+            for c in range(2):
+                rows = pl.ds(c, half, stride=2)
+                out[at + 2 * n + a, rows] = pre[2 * b + a, rows] + values
+
+
+def send_kernel(count, flags, pre, lift, coarse, *outs):
     nb, half = pre.shape[0] // 2, pre.shape[1] // 2
     table = jnp.broadcast_to(coarse[:1], (half, LANES))
     for s, out in enumerate(outs):
-        for h in range(HALO // 2):
-            if count == 2:
-                b = jnp.where(flags[IX] == 0, nb - HALO // 2 + h, h)
-            else:
-                b = (nb - HALO // 2 + h, h)[s]
-            lifted(pre, block_agg, table, out, b, 2 * h)
-
-
-def correct_kernel(flags, pre, block_agg, coarse, out):
+        if count == 2:
+            b = jnp.where(flags[IX] == 0, nb - HALO // 2, 0)
+        else:
+            b = (nb - HALO // 2, 0)[s]
+        lifted(pre, lift, table, out, [b + h for h in range(HALO // 2)], 0)
+
+
+def correct_kernel(flags, pre, lift, coarse, out):
     table = jnp.broadcast_to(coarse[:1], (pre.shape[1] // 2, LANES))
 
-    @pl.loop(0, pre.shape[0] // 2)
-    def _(b):
-        lifted(pre, block_agg, table, out, b, 2 * b)
+    def step(bs, carry):
+        lifted(pre, lift, table, out, bs, 2 * bs[0])
+        return carry
+
+    batched(0, pre.shape[0] // 2, step, 0)
 
 
 def post_kernel(flags, wide_ref, forth, back, *refs):
@@ -692,58 +733,57 @@
     ).astype(jnp.int32)
     arrays = (conductance, right_side, absorption, block_agg)
     n_send = 1 if n_x == 2 else 2
-    x_sends = call(
+    got = call(
         functools.partial(pack_x_kernel, n_x, WIDTHS),
-        [shaped(sum(WIDTHS) + 1, ny, nz)] * n_send,
-        [pltpu.VMEM((n_send, ny // 2, nz // 2), jnp.int32), pltpu.SemaphoreType.DMA((n_send * 4,))],
+        [jax.ShapeDtypeStruct(a.shape, a.dtype) for a in arrays] + [shaped(sum(WIDTHS) + 1, ny, nz)] * n_send,
+        [pltpu.VMEM((n_send, ny // 2, nz // 2), jnp.int32), pltpu.SemaphoreType.DMA((n_send * 4 + 4,))],
         in_specs=[pl.BlockSpec(memory_space=pltpu.HBM)] * 4,
     )(flags, *(pltpu.with_memory_space_constraint(a, pltpu.HBM) for a in arrays))
+    arrays, x_sends = got[:4], got[4:]
+    blocks = (nb, SUB, LANES)
+    outs = [shaped(*blocks), shaped(3, *blocks), shaped(3, *blocks), shaped(*blocks), shaped(6, SUB, LANES)]
+    outs += [jax.ShapeDtypeStruct((nb, ny // 2, LANES), jnp.int32)]
+    scratch = [pltpu.VMEM((17, ny, LANES), F32), pltpu.VMEM((2, ny // 2, LANES), F32)]
     pair = [pltpu.VMEM((AGG, SUB * LANES), BF16), pltpu.VMEM((2 * AGG, SUB * LANES), BF16)]
-    scratch = [pltpu.VMEM((4, ny, LANES), F32), pltpu.VMEM((4, ny // 2, LANES), F32)] + pair
-    bounds = [nb * p // 3 for p in range(4)]
-
-    def own_part(p, *more):
-        outs = [shaped(AGG, 2 * AGG), shaped(AGG, LANES)]
-        if p == 2:
-            outs = [jax.ShapeDtypeStruct((AGG, 2 * AGG), BF16), shaped(nb, SUB, LANES)]
-            outs += [shaped(6, SUB, LANES), shaped(SUB, AGG)]
-        kernel = functools.partial(own_kernel, bounds[p], bounds[p + 1] - bounds[p], p == 2)
-        return call(kernel, outs, scratch)(flags, conductance, absorption, block_agg, *more)
-
-    parts = [own_part(0, x_sends[0])]
+    *rows, face_label, lift = call(blocks_kernel, outs, scratch)(flags, arrays[0], arrays[2], arrays[3], x_sends[0])
+    block_label = rows[0]
+    first = call(functools.partial(own_kernel, 0, nb // 2, nb), [shaped(AGG, 2 * AGG)], pair * 2)(
+        flags, *rows, x_sends[0]
+    )[0]
     from_x = links.x(x_sends)
-    from_x = lax.optimization_barrier((*from_x, *parts[0]))[:2]
-
-    def beside(p):
-        def run(sent):
-            parts.append(own_part(p, *parts[-1], sent))
-            return parts[-1]
-
-        return run
-
-    halo, from_y = widened(links, flags, WIDTHS, arrays, from_x, beside(1), beside(2))
-    own_tile, block_label, face_label, inner_diag = parts[-1]
+    from_x = lax.optimization_barrier((*from_x, first))[:-1]
+    later = []
+
+    def second_half(sent):
+        outs = [jax.ShapeDtypeStruct((AGG, 2 * AGG), BF16), shaped(SUB, AGG)]
+        later.extend(
+            call(functools.partial(own_kernel, nb // 2, nb, nb), outs, pair * 2)(flags, *rows, first, sent)
+        )
+        return later
+
+    halo, from_y = widened(links, flags, WIDTHS, arrays, from_x, second_half)
+    own_tile, inner_diag = later
     outs = [shaped(*frame.main)] * 6 + [shaped(*frame.ends)] * 6 + [shaped(nx, ny, nz)]
     outs += [shaped(6, SUB, LANES)] * 2 + [shaped(SUB, AGG)] * 2
     scratch = [pltpu.VMEM(frame.main, F32), pltpu.VMEM(frame.ends, F32), pltpu.VMEM((nx, frame.rows, LANES), F32)]
-    scratch += [pltpu.VMEM(frame.main, F32)]
+    scratch += [pltpu.VMEM(frame.main, F32), pltpu.VMEM((nb, SUB, LANES), F32)]
     got = call(fine_kernel, outs, scratch, limit=28)(
-        flags, *halo, *from_x, *from_y, block_label, face_label, inner_diag
+        flags, *halo, from_x[0], from_x[-1], *from_y, block_label, face_label, inner_diag
     )
     fields, pre = got[:12], got[12]
     face_near, face_weight, scaled_rhs, scale = got[13:]
-    tiles = call(faces_kernel, jax.ShapeDtypeStruct((7 * AGG, 2 * AGG), BF16), pair)(
-        flags, own_tile, face_label, face_near, face_weight
-    )
+    tiles = call(
+        functools.partial(faces_kernel, n_x),
+        jax.ShapeDtypeStruct(((n_send + 5) * AGG, 2 * AGG), BF16),
+        pair * 2,
+    )(flags, own_tile, face_label, face_near, face_weight)
     coarse = scaled_rhs
     for _ in range(KC - 1):
         near = links.x([coarse] * n_send) + links.y(coarse, coarse) + links.z(coarse, coarse)
         coarse = call(turn_kernel, shaped(SUB, AGG))(flags, tiles, scaled_rhs, scale, coarse, *near)
-    x_sends = call(functools.partial(send_kernel, n_x), [shaped(HALO, ny, nz)] * n_send)(
-        flags, pre, block_agg, coarse
-    )
+    x_sends = call(functools.partial(send_kernel, n_x), [shaped(HALO, ny, nz)] * n_send)(flags, pre, lift, coarse)
     from_x = links.x(x_sends)
-    corrected = call(correct_kernel, shaped(nx, ny, nz))(flags, pre, block_agg, coarse)
+    corrected = call(correct_kernel, shaped(nx, ny, nz))(flags, pre, lift, coarse)
     halo, _ = widened(links, flags, (HALO,), (corrected,), from_x)
     scratch = [pltpu.VMEM(frame.main, F32)] * 2 + [pltpu.VMEM(frame.ends, F32)] * 2
     return call(post_kernel, shaped(nx, ny, nz), scratch, limit=24)(flags, *halo, *fields)

time: 106 us -> 105 us (level)
  waiting for transfers between devices: 21.3 us -> 29.5 us
  Pallas kernels: 43.5 us -> 36.2 us
  local copies, waits for them, and re-layouts: 2.99 us -> 0.08 us
    ppermute x45, waiting for transfers between devices: 21.3 us -> 29.5 us  [the longest x36 20.8 us: send(): return lax.ppermute(values, ('gx', 'gy', 'gz'), pairs)]
    pallas_call x20, Pallas kernels: 43.5 us -> 36.2 us  [run(): pl.pallas_call(kernel, out_shape=outs, in_specs=[SMEM] + (in_specs or [VM...]
    unnamed x12 -> x0, local copies, waits for them, and re-layouts: 2.9 us -> none
  transfers between devices with their start and end apart: 45 -> 45, of which waited for: 17 -> 20; matrix products, arithmetic and copies ran while one was open for 0% -> 0% of each run, Pallas kernels for 17% -> 12%
where the time goes in v4:
time: 105 us
  starting transfers between devices  38.7 us (37%)
  Pallas kernels  36.2 us (34%)
  waiting for transfers between devices  29.5 us (28%)
    pallas_call x20, Pallas kernels, run(): pl.pallas_call(kernel, out_shape=outs, in_specs=[SMEM] + (in_specs or [VM...  36.2 us
    ppermute x36, starting transfers between devices, send(): return lax.ppermute(values, ('gx', 'gy', 'gz'), pairs)  27.5 us
    ppermute x36, waiting for transfers between devices, send(): return lax.ppermute(values, ('gx', 'gy', 'gz'), pairs)  20.8 us
    ppermute x9, starting transfers between devices, x(): return (lax.ppermute(sends[0], 'gx', self.ring_x),)  11.2 us
    ppermute x9, waiting for transfers between devices, x(): return (lax.ppermute(sends[0], 'gx', self.ring_x),)  8.77 us
  transfers between devices with their start and end apart: 45, of which 20 were waited for; matrix products, arithmetic and copies ran while one was open for 0% of the time, Pallas kernels for 12%

profile of v4, /device:TPU:0, one launch (start us, length us, event | category | flops | bytes accessed | tf_op | source)
XLA Modules:
  0.0 104.8 jit_solution(6229550661493462808)
XLA Ops:
  0.1 2.0 %shard_map.46 = (f32[24,32,128]{2,1,0:T(8,128)S(1)}, f32[24,32,128]{2,1,0:T(8,128)S(1)}, f32[24,32,128]{2,1,0:T(8,128)S(1)}, s32[12,16,64]{2,1,0:T(8,128)S(1)}, f32[11,32,128]{2,1,0:T(8,128)S(1)}) custom-call(s32[8]{0:T(128)S(1)} %stack.59.flags, f32[24,32,128]{2,1,0:T(8,128)} %refs_0_.1, f32[24,32,128]{2,1,0:T(8,128)} %refs_1_.1, f32[24,32,128]{2,1,0:T(8,128)} %refs_2_.1, ...), custom_call_target="tpu_custom_call" | custom-call | flops 1000000 | bytes 100000 | tf_op jit(solution)/shard_map/pallas_call | solution.py:28
  2.1 3.0 %collective-permute-start = (f32[11,32,128]{2,1,0:T(8,128)S(1)}, f32[11,32,128]{2,1,0:T(8,128)S(1)}, u32[]{:S(2)}, u32[]{:S(2)}) collective-permute-start(f32[11,32,128]{2,1,0:T(8,128)S(1)} %get-tuple-element.52._.refs_0_), channel_id=1, source_target_pairs={{0,16},{16,0},{1,17},{17,1},{2,18},{18,2},{3,19},{19,3},{4,20},{20... | collective-permute-start | bytes 540680 | tf_op jit(solution)/shard_map/ppermute | solution.py:236
  5.1 2.1 %shard_map.47 = (f32[12,8,128]{2,1,0:T(8,128)S(1)}, f32[3,12,8,128]{3,2,1,0:T(8,128)S(1)}, f32[3,12,8,128]{3,2,1,0:T(8,128)S(1)}, f32[12,8,128]{2,1,0:T(8,128)S(...) custom-call(s32[8]{0:T(128)S(1)} %stack.59.flags, f32[24,32,128]{2,1,0:T(8,128)S(1)} %get-tuple-element.48.cond.refs_0_, ...), custom_call_target="tpu_custom_call" | custom-call | flops 1000000 | bytes 100000 | tf_op jit(solution)/shard_map/pallas_call | solution.py:28
  7.2 3.3 %shard_map.48.refs_0_ = f32[128,256]{1,0:T(8,128)S(1)} custom-call(s32[8]{0:T(128)S(1)} %stack.59.flags, f32[12,8,128]{2,1,0:T(8,128)S(1)} %get-tuple-element.53.block_label, f32[3,12,8,128]{3,2,1,0:T(8,128)S(1)} %get-tuple-element.54.near, f32[3,12,8,128]{3,2,1,0:T(8,128)S(1)} %get-tuple-element.55.weights, f32[12,8,128]{2,1,0:T(8,128)S(1)} %get-tuple-element.56.inner, ...), custom_call_target="tpu_custom_call" | custom-call | flops 1000000 | bytes 100000 | tf_op jit(solution)/shard_map/pallas_call | solution.py:28
  12.9 4.2 %shard_map.50 = (bf16[128,256]{1,0:T(8,128)(2,1)S(1)}, f32[8,128]{1,0:T(8,128)S(1)}) custom-call(s32[8]{0:T(128)S(1)} %stack.59.flags, f32[12,8,128]{2,1,0:T(8,128)S(1)} %get-tuple-element.53.block_label, f32[3,12,8,128]{3,2,1,0:T(8,128)S(1)} %get-tuple-element.54.near, f32[3,12,8,128]{3,2,1,0:T(8,128)S(1)} %get-tuple-element.55.weights, ...), custom_call_target="tpu_custom_call" | custom-call | flops 1000000 | bytes 100000 | tf_op jit(solution)/shard_map/pallas_call | solution.py:28
  18.7 1.6 %collective-permute-start.3 = (f32[136,128]{1,0:T(8,128)S(1)}, f32[136,128]{1,0:T(8,128)S(1)}, u32[]{:S(2)}, u32[]{:S(2)}) collective-permute-start(f32[136,128]{1,0:T(8,128)S(1)} %get-tuple-element.65), channel_id=1, source_target_pairs={{0,1},{1,2},{2,3},{3,7},{7,6},{6,5},{5,4},{4,0},{8,9},{9,10},{10,1... | collective-permute-start | bytes 208904 | tf_op jit(solution)/shard_map/ppermute | solution.py:232
  20.3 1.9 %collective-permute-done.3.forth = f32[136,128]{1,0:T(8,128)S(1)} collective-permute-done((f32[136,128]{1,0:T(8,128)S(1)}, f32[136,128]{1,0:T(8,128)S(1)}, u32[]{:S(2)}, u32[]{:S(2)}) %collective-permute-start.3) | collective-permute-done | bytes 69664 | tf_op jit(solution)/shard_map/ppermute | solution.py:232
  22.2 2.4 %collective-permute-done.4.back = f32[136,128]{1,0:T(8,128)S(1)} collective-permute-done((f32[136,128]{1,0:T(8,128)S(1)}, f32[136,128]{1,0:T(8,128)S(1)}, u32[]{:S(2)}, u32[]{:S(2)}) %collective-permute-start.4) | collective-permute-done | bytes 69664 | tf_op jit(solution)/shard_map/ppermute | solution.py:232
  24.6 6.8 %shard_map.52 = (f32[32,56,128]{2,1,0:T(8,128)S(1)}, f32[32,56,128]{2,1,0:T(8,128)S(1)}, f32[32,56,128]{2,1,0:T(8,128)S(1)}, f32[32,56,128]{2,1,0:T(8,128)S(1)},...) custom-call(s32[8]{0:T(128)S(1)} %stack.59.flags, ...), custom_call_target="tpu_custom_call" | custom-call | flops 1000000 | bytes 100000 | tf_op jit(solution)/shard_map/pallas_call | solution.py:28
  31.4 2.0 %collective-permute-start.8 = (f32[8,128]{1,0:T(8,128)S(1)}, f32[8,128]{1,0:T(8,128)S(1)}, u32[]{:S(2)}, u32[]{:S(2)}) collective-permute-start(f32[8,128]{1,0:T(8,128)S(1)} %get-tuple-element.72.scaled_rhs.own), channel_id=1, source_target_pairs={{0,1},{1,2},{2,3},{3,7},{7,6},{6,5},{5,4},{4,0},{8,9},{9,10},{10,1... | collective-permute-start | bytes 12296 | tf_op jit(solution)/shard_map/ppermute | solution.py:232
  35.5 2.3 %shard_map.53.tiles = bf16[768,256]{1,0:T(8,128)(2,1)S(1)} custom-call(s32[8]{0:T(128)S(1)} %stack.59.flags, bf16[128,256]{1,0:T(8,128)(2,1)S(1)} %get-tuple-element.60.own, f32[6,8,128]{2,1,0:T(8,128)S(1)} %get-tuple-element.67.face_label, f32[6,8,128]{2,1,0:T(8,128)S(1)} %get-tuple-element.70.face_near, f32[6,8,128]{2,1,0:T(8,128)S(1)} %get-tuple-element.71.face_weight), custom_call_target="tpu_custom_call" | custom-call | flops 1000000 | bytes 100000 | tf_op jit(solution)/shard_map/pallas_call | solution.py:28
  38.8 2.0 %collective-permute-start.13 = (f32[8,128]{1,0:T(8,128)S(1)}, f32[8,128]{1,0:T(8,128)S(1)}, u32[]{:S(2)}, u32[]{:S(2)}) collective-permute-start(f32[8,128]{1,0:T(8,128)S(1)} %shard_map.54.own), channel_id=1, source_target_pairs={{0,1},{1,2},{2,3},{3,7},{7,6},{6,5},{5,4},{4,0},{8,9},{9,10},{10,1... | collective-permute-start | bytes 12296 | tf_op jit(solution)/shard_map/ppermute | solution.py:232
  42.8 1.6 %collective-permute-done.12.refs_2_ = f32[8,128]{1,0:T(8,128)S(1)} collective-permute-done((f32[8,128]{1,0:T(8,128)S(1)}, f32[8,128]{1,0:T(8,128)S(1)}, u32[]{:S(2)}, u32[]{:S(2)}) %collective-permute-start.12) | collective-permute-done | bytes 4128 | tf_op jit(solution)/shard_map/ppermute | solution.py:232
  46.2 2.0 %collective-permute-start.18 = (f32[8,128]{1,0:T(8,128)S(1)}, f32[8,128]{1,0:T(8,128)S(1)}, u32[]{:S(2)}, u32[]{:S(2)}) collective-permute-start(f32[8,128]{1,0:T(8,128)S(1)} %shard_map.55.own), channel_id=1, source_target_pairs={{0,1},{1,2},{2,3},{3,7},{7,6},{6,5},{5,4},{4,0},{8,9},{9,10},{10,1... | collective-permute-start | bytes 12296 | tf_op jit(solution)/shard_map/ppermute | solution.py:232
  50.3 1.6 %collective-permute-done.17.refs_2_ = f32[8,128]{1,0:T(8,128)S(1)} collective-permute-done((f32[8,128]{1,0:T(8,128)S(1)}, f32[8,128]{1,0:T(8,128)S(1)}, u32[]{:S(2)}, u32[]{:S(2)}) %collective-permute-start.17) | collective-permute-done | bytes 4128 | tf_op jit(solution)/shard_map/ppermute | solution.py:232
  53.5 2.0 %collective-permute-start.23 = (f32[8,128]{1,0:T(8,128)S(1)}, f32[8,128]{1,0:T(8,128)S(1)}, u32[]{:S(2)}, u32[]{:S(2)}) collective-permute-start(f32[8,128]{1,0:T(8,128)S(1)} %shard_map.56.own), channel_id=1, source_target_pairs={{0,1},{1,2},{2,3},{3,7},{7,6},{6,5},{5,4},{4,0},{8,9},{9,10},{10,1... | collective-permute-start | bytes 12296 | tf_op jit(solution)/shard_map/ppermute | solution.py:232
  61.0 2.0 %collective-permute-start.28 = (f32[8,128]{1,0:T(8,128)S(1)}, f32[8,128]{1,0:T(8,128)S(1)}, u32[]{:S(2)}, u32[]{:S(2)}) collective-permute-start(f32[8,128]{1,0:T(8,128)S(1)} %shard_map.57.own), channel_id=1, source_target_pairs={{0,1},{1,2},{2,3},{3,7},{7,6},{6,5},{5,4},{4,0},{8,9},{9,10},{10,1... | collective-permute-start | bytes 12296 | tf_op jit(solution)/shard_map/ppermute | solution.py:232
  68.3 2.0 %collective-permute-start.33 = (f32[8,128]{1,0:T(8,128)S(1)}, f32[8,128]{1,0:T(8,128)S(1)}, u32[]{:S(2)}, u32[]{:S(2)}) collective-permute-start(f32[8,128]{1,0:T(8,128)S(1)} %shard_map.58.own), channel_id=1, source_target_pairs={{0,1},{1,2},{2,3},{3,7},{7,6},{6,5},{5,4},{4,0},{8,9},{9,10},{10,1... | collective-permute-start | bytes 12296 | tf_op jit(solution)/shard_map/ppermute | solution.py:232
  75.7 2.0 %collective-permute-start.38 = (f32[8,128]{1,0:T(8,128)S(1)}, f32[8,128]{1,0:T(8,128)S(1)}, u32[]{:S(2)}, u32[]{:S(2)}) collective-permute-start(f32[8,128]{1,0:T(8,128)S(1)} %shard_map.59.own), channel_id=1, source_target_pairs={{0,1},{1,2},{2,3},{3,7},{7,6},{6,5},{5,4},{4,0},{8,9},{9,10},{10,1... | collective-permute-start | bytes 12296 | tf_op jit(solution)/shard_map/ppermute | solution.py:232
  85.5 2.5 %collective-permute-done.40.refs_1_.refs_2_ = f32[4,32,128]{2,1,0:T(8,128)S(1)} collective-permute-done((f32[4,32,128]{2,1,0:T(8,128)S(1)}, f32[4,32,128]{2,1,0:T(8,128)S(1)}, u32[]{:S(2)}, u32[]{:S(2)}) %collective-permute-start.40) | collective-permute-done | bytes 65568 | tf_op jit(solution)/shard_map/ppermute | solution.py:236
  89.9 3.1 %collective-permute-done.42.refs_4_ = f32[128,128]{1,0:T(8,128)S(1)} collective-permute-done((f32[128,128]{1,0:T(8,128)S(1)}, f32[128,128]{1,0:T(8,128)S(1)}, u32[]{:S(2)}, u32[]{:S(2)}) %collective-permute-start.42) | collective-permute-done | bytes 65568 | tf_op jit(solution)/shard_map/ppermute | solution.py:232
  93.8 1.6 %collective-permute-start.43 = (f32[40,128]{1,0:T(8,128)S(1)}, f32[40,128]{1,0:T(8,128)S(1)}, u32[]{:S(2)}, u32[]{:S(2)}) collective-permute-start(f32[40,128]{1,0:T(8,128)S(1)} %get-tuple-element.77), channel_id=1, source_target_pairs={{0,1},{1,2},{2,3},{3,7},{7,6},{6,5},{5,4},{4,0},{8,9},{9,10},{10,1... | collective-permute-start | bytes 61448 | tf_op jit(solution)/shard_map/ppermute | solution.py:232
  96.9 2.3 %collective-permute-done.44.back = f32[40,128]{1,0:T(8,128)S(1)} collective-permute-done((f32[40,128]{1,0:T(8,128)S(1)}, f32[40,128]{1,0:T(8,128)S(1)}, u32[]{:S(2)}, u32[]{:S(2)}) %collective-permute-start.44) | collective-permute-done | bytes 20512 | tf_op jit(solution)/shard_map/ppermute | solution.py:232
  99.2 5.6 %shard_map.65 = f32[24,32,128]{2,1,0:T(8,128)} custom-call(s32[8]{0:T(128)S(1)} %stack.59.flags, f32[1,32,56,128]{3,2,1,0:T(8,128)S(1)} %get-tuple-element.76.wide_ref, f32[40,128]{1,0:T(8,128)S(1)} %collective-permute-done.43.forth, f32[40,128]{1,0:T(8,128)S(1)} %collective-permute-done.44.back, f32[32,56,128]{2,1,0:T(8,128)S(1)} %get-tuple-element.79.refs_0_, ...), custom_call_target="tpu_custom_call" | custom-call | flops 1000000 | bytes 100000 | tf_op jit(solution)/shard_map/pallas_call | solution.py:28
  (87 shorter events, 42.6 us)
Async XLA Ops:
  2.1 8.5 %collective-permute-start = (f32[11,32,128]{2,1,0:T(8,128)S(1)}, f32[11,32,128]{2,1,0:T(8,128)S(1)}, u32[]{:S(2)}, u32[]{:S(2)}) collective-permute-start(f32[11,32,128]{2,1,0:T(8,128)S(1)} %get-tuple-element.52._.refs_0_), channel_id=1, source_target_pairs={{0,16},{16,0},{1,17},{17,1},{2,18},{18,2},{3,19},{19,3},{4,20},{20... | collective-permute-start | bytes 540680 | tf_op jit(solution)/shard_map/ppermute | solution.py:236
  11.2 5.9 %collective-permute-start.2 = (f32[400,128]{1,0:T(8,128)S(1)}, f32[400,128]{1,0:T(8,128)S(1)}, u32[]{:S(2)}, u32[]{:S(2)}) collective-permute-start(f32[400,128]{1,0:T(8,128)S(1)} %get-tuple-element.59), channel_id=1, source_target_pairs={{0,16},{1,17},{2,18},{3,19},{4,8},{5,9},{6,10},{7,11},{8,4},{9,5},... | collective-permute-start | bytes 614408 | tf_op jit(solution)/shard_map/ppermute | solution.py:232
  12.1 5.0 %collective-permute-start.1 = (f32[400,128]{1,0:T(8,128)S(1)}, f32[400,128]{1,0:T(8,128)S(1)}, u32[]{:S(2)}, u32[]{:S(2)}) collective-permute-start(f32[400,128]{1,0:T(8,128)S(1)} %get-tuple-element.58.refs_1_), channel_id=1, source_target_pairs={{0,4},{1,5},{2,6},{3,7},{4,0},{5,1},{6,2},{7,3},{8,12},{9,13},{10,... | collective-permute-start | bytes 614408 | tf_op jit(solution)/shard_map/ppermute | solution.py:232
  20.3 4.3 %collective-permute-start.4 = (f32[136,128]{1,0:T(8,128)S(1)}, f32[136,128]{1,0:T(8,128)S(1)}, u32[]{:S(2)}, u32[]{:S(2)}) collective-permute-start(f32[136,128]{1,0:T(8,128)S(1)} %get-tuple-element.66), channel_id=1, source_target_pairs={{1,0},{2,1},{3,2},{7,3},{6,7},{5,6},{4,5},{0,4},{9,8},{10,9},{11,1... | collective-permute-start | bytes 208904 | tf_op jit(solution)/shard_map/ppermute | solution.py:232
  31.4 6.4 %collective-permute-start.9 = (f32[8,128]{1,0:T(8,128)S(1)}, f32[8,128]{1,0:T(8,128)S(1)}, u32[]{:S(2)}, u32[]{:S(2)}) collective-permute-start(f32[8,128]{1,0:T(8,128)S(1)} %get-tuple-element.72.scaled_rhs.own), channel_id=1, source_target_pairs={{1,0},{2,1},{3,2},{7,3},{6,7},{5,6},{4,5},{0,4},{9,8},{10,9},{11,1... | collective-permute-start | bytes 12296 | tf_op jit(solution)/shard_map/ppermute | solution.py:232
  31.4 6.3 %collective-permute-start.8 = (f32[8,128]{1,0:T(8,128)S(1)}, f32[8,128]{1,0:T(8,128)S(1)}, u32[]{:S(2)}, u32[]{:S(2)}) collective-permute-start(f32[8,128]{1,0:T(8,128)S(1)} %get-tuple-element.72.scaled_rhs.own), channel_id=1, source_target_pairs={{0,1},{1,2},{2,3},{3,7},{7,6},{6,5},{5,4},{4,0},{8,9},{9,10},{10,1... | collective-permute-start | bytes 12296 | tf_op jit(solution)/shard_map/ppermute | solution.py:232
  33.4 4.3 %collective-permute-start.7 = (f32[8,128]{1,0:T(8,128)S(1)}, f32[8,128]{1,0:T(8,128)S(1)}, u32[]{:S(2)}, u32[]{:S(2)}) collective-permute-start(f32[8,128]{1,0:T(8,128)S(1)} %get-tuple-element.72.scaled_rhs.own), channel_id=1, source_target_pairs={{0,16},{1,17},{2,18},{3,19},{4,8},{5,9},{6,10},{7,11},{8,4},{9,5},... | collective-permute-start | bytes 12296 | tf_op jit(solution)/shard_map/ppermute | solution.py:232
  38.7 4.1 %collective-permute-start.14 = (f32[8,128]{1,0:T(8,128)S(1)}, f32[8,128]{1,0:T(8,128)S(1)}, u32[]{:S(2)}, u32[]{:S(2)}) collective-permute-start(f32[8,128]{1,0:T(8,128)S(1)} %shard_map.54.own), channel_id=1, source_target_pairs={{1,0},{2,1},{3,2},{7,3},{6,7},{5,6},{4,5},{0,4},{9,8},{10,9},{11,1... | collective-permute-start | bytes 12296 | tf_op jit(solution)/shard_map/ppermute | solution.py:232
  38.8 4.0 %collective-permute-start.13 = (f32[8,128]{1,0:T(8,128)S(1)}, f32[8,128]{1,0:T(8,128)S(1)}, u32[]{:S(2)}, u32[]{:S(2)}) collective-permute-start(f32[8,128]{1,0:T(8,128)S(1)} %shard_map.54.own), channel_id=1, source_target_pairs={{0,1},{1,2},{2,3},{3,7},{7,6},{6,5},{5,4},{4,0},{8,9},{9,10},{10,1... | collective-permute-start | bytes 12296 | tf_op jit(solution)/shard_map/ppermute | solution.py:232
  40.8 3.6 %collective-permute-start.12 = (f32[8,128]{1,0:T(8,128)S(1)}, f32[8,128]{1,0:T(8,128)S(1)}, u32[]{:S(2)}, u32[]{:S(2)}) collective-permute-start(f32[8,128]{1,0:T(8,128)S(1)} %shard_map.54.own), channel_id=1, source_target_pairs={{0,16},{1,17},{2,18},{3,19},{4,8},{5,9},{6,10},{7,11},{8,4},{9,5},... | collective-permute-start | bytes 12296 | tf_op jit(solution)/shard_map/ppermute | solution.py:232
  46.2 4.1 %collective-permute-start.19 = (f32[8,128]{1,0:T(8,128)S(1)}, f32[8,128]{1,0:T(8,128)S(1)}, u32[]{:S(2)}, u32[]{:S(2)}) collective-permute-start(f32[8,128]{1,0:T(8,128)S(1)} %shard_map.55.own), channel_id=1, source_target_pairs={{1,0},{2,1},{3,2},{7,3},{6,7},{5,6},{4,5},{0,4},{9,8},{10,9},{11,1... | collective-permute-start | bytes 12296 | tf_op jit(solution)/shard_map/ppermute | solution.py:232
  46.2 4.1 %collective-permute-start.18 = (f32[8,128]{1,0:T(8,128)S(1)}, f32[8,128]{1,0:T(8,128)S(1)}, u32[]{:S(2)}, u32[]{:S(2)}) collective-permute-start(f32[8,128]{1,0:T(8,128)S(1)} %shard_map.55.own), channel_id=1, source_target_pairs={{0,1},{1,2},{2,3},{3,7},{7,6},{6,5},{5,4},{4,0},{8,9},{9,10},{10,1... | collective-permute-start | bytes 12296 | tf_op jit(solution)/shard_map/ppermute | solution.py:232
  48.2 3.6 %collective-permute-start.17 = (f32[8,128]{1,0:T(8,128)S(1)}, f32[8,128]{1,0:T(8,128)S(1)}, u32[]{:S(2)}, u32[]{:S(2)}) collective-permute-start(f32[8,128]{1,0:T(8,128)S(1)} %shard_map.55.own), channel_id=1, source_target_pairs={{0,16},{1,17},{2,18},{3,19},{4,8},{5,9},{6,10},{7,11},{8,4},{9,5},... | collective-permute-start | bytes 12296 | tf_op jit(solution)/shard_map/ppermute | solution.py:232
  53.5 4.1 %collective-permute-start.24 = (f32[8,128]{1,0:T(8,128)S(1)}, f32[8,128]{1,0:T(8,128)S(1)}, u32[]{:S(2)}, u32[]{:S(2)}) collective-permute-start(f32[8,128]{1,0:T(8,128)S(1)} %shard_map.56.own), channel_id=1, source_target_pairs={{1,0},{2,1},{3,2},{7,3},{6,7},{5,6},{4,5},{0,4},{9,8},{10,9},{11,1... | collective-permute-start | bytes 12296 | tf_op jit(solution)/shard_map/ppermute | solution.py:232
  53.5 4.1 %collective-permute-start.23 = (f32[8,128]{1,0:T(8,128)S(1)}, f32[8,128]{1,0:T(8,128)S(1)}, u32[]{:S(2)}, u32[]{:S(2)}) collective-permute-start(f32[8,128]{1,0:T(8,128)S(1)} %shard_map.56.own), channel_id=1, source_target_pairs={{0,1},{1,2},{2,3},{3,7},{7,6},{6,5},{5,4},{4,0},{8,9},{9,10},{10,1... | collective-permute-start | bytes 12296 | tf_op jit(solution)/shard_map/ppermute | solution.py:232
  60.9 4.1 %collective-permute-start.29 = (f32[8,128]{1,0:T(8,128)S(1)}, f32[8,128]{1,0:T(8,128)S(1)}, u32[]{:S(2)}, u32[]{:S(2)}) collective-permute-start(f32[8,128]{1,0:T(8,128)S(1)} %shard_map.57.own), channel_id=1, source_target_pairs={{1,0},{2,1},{3,2},{7,3},{6,7},{5,6},{4,5},{0,4},{9,8},{10,9},{11,1... | collective-permute-start | bytes 12296 | tf_op jit(solution)/shard_map/ppermute | solution.py:232
  61.0 4.1 %collective-permute-start.28 = (f32[8,128]{1,0:T(8,128)S(1)}, f32[8,128]{1,0:T(8,128)S(1)}, u32[]{:S(2)}, u32[]{:S(2)}) collective-permute-start(f32[8,128]{1,0:T(8,128)S(1)} %shard_map.57.own), channel_id=1, source_target_pairs={{0,1},{1,2},{2,3},{3,7},{7,6},{6,5},{5,4},{4,0},{8,9},{9,10},{10,1... | collective-permute-start | bytes 12296 | tf_op jit(solution)/shard_map/ppermute | solution.py:232
  68.3 4.1 %collective-permute-start.34 = (f32[8,128]{1,0:T(8,128)S(1)}, f32[8,128]{1,0:T(8,128)S(1)}, u32[]{:S(2)}, u32[]{:S(2)}) collective-permute-start(f32[8,128]{1,0:T(8,128)S(1)} %shard_map.58.own), channel_id=1, source_target_pairs={{1,0},{2,1},{3,2},{7,3},{6,7},{5,6},{4,5},{0,4},{9,8},{10,9},{11,1... | collective-permute-start | bytes 12296 | tf_op jit(solution)/shard_map/ppermute | solution.py:232
  68.3 4.1 %collective-permute-start.33 = (f32[8,128]{1,0:T(8,128)S(1)}, f32[8,128]{1,0:T(8,128)S(1)}, u32[]{:S(2)}, u32[]{:S(2)}) collective-permute-start(f32[8,128]{1,0:T(8,128)S(1)} %shard_map.58.own), channel_id=1, source_target_pairs={{0,1},{1,2},{2,3},{3,7},{7,6},{6,5},{5,4},{4,0},{8,9},{9,10},{10,1... | collective-permute-start | bytes 12296 | tf_op jit(solution)/shard_map/ppermute | solution.py:232
  75.7 4.1 %collective-permute-start.39 = (f32[8,128]{1,0:T(8,128)S(1)}, f32[8,128]{1,0:T(8,128)S(1)}, u32[]{:S(2)}, u32[]{:S(2)}) collective-permute-start(f32[8,128]{1,0:T(8,128)S(1)} %shard_map.59.own), channel_id=1, source_target_pairs={{1,0},{2,1},{3,2},{7,3},{6,7},{5,6},{4,5},{0,4},{9,8},{10,9},{11,1... | collective-permute-start | bytes 12296 | tf_op jit(solution)/shard_map/ppermute | solution.py:232
  75.7 4.1 %collective-permute-start.38 = (f32[8,128]{1,0:T(8,128)S(1)}, f32[8,128]{1,0:T(8,128)S(1)}, u32[]{:S(2)}, u32[]{:S(2)}) collective-permute-start(f32[8,128]{1,0:T(8,128)S(1)} %shard_map.59.own), channel_id=1, source_target_pairs={{0,1},{1,2},{2,3},{3,7},{7,6},{6,5},{5,4},{4,0},{8,9},{9,10},{10,1... | collective-permute-start | bytes 12296 | tf_op jit(solution)/shard_map/ppermute | solution.py:232
  83.7 4.3 %collective-permute-start.40 = (f32[4,32,128]{2,1,0:T(8,128)S(1)}, f32[4,32,128]{2,1,0:T(8,128)S(1)}, u32[]{:S(2)}, u32[]{:S(2)}) collective-permute-start(f32[4,32,128]{2,1,0:T(8,128)S(1)} %shard_map.62), channel_id=1, source_target_pairs={{0,16},{16,0},{1,17},{17,1},{2,18},{18,2},{3,19},{19,3},{4,20},{20... | collective-permute-start | bytes 196616 | tf_op jit(solution)/shard_map/ppermute | solution.py:236
  88.6 4.3 %collective-permute-start.42 = (f32[128,128]{1,0:T(8,128)S(1)}, f32[128,128]{1,0:T(8,128)S(1)}, u32[]{:S(2)}, u32[]{:S(2)}) collective-permute-start(f32[128,128]{1,0:T(8,128)S(1)} %get-tuple-element.75), channel_id=1, source_target_pairs={{0,16},{1,17},{2,18},{3,19},{4,8},{5,9},{6,10},{7,11},{8,4},{9,5},... | collective-permute-start | bytes 196616 | tf_op jit(solution)/shard_map/ppermute | solution.py:232
  95.4 3.8 %collective-permute-start.44 = (f32[40,128]{1,0:T(8,128)S(1)}, f32[40,128]{1,0:T(8,128)S(1)}, u32[]{:S(2)}, u32[]{:S(2)}) collective-permute-start(f32[40,128]{1,0:T(8,128)S(1)} %get-tuple-element.78), channel_id=1, source_target_pairs={{1,0},{2,1},{3,2},{7,3},{6,7},{5,6},{4,5},{0,4},{9,8},{10,9},{11,1... | collective-permute-start | bytes 61448 | tf_op jit(solution)/shard_map/ppermute | solution.py:232
  (21 other events, 66.7 us)

commit v5 on v4

--- a/solution.py
+++ b/solution.py
@@ -23,7 +23,7 @@
 IX, PARITY, X_LOW, X_HIGH, Y_LOW, Y_HIGH, Z_LOW, Z_HIGH = range(8)
 
 
-def call(kernel, outs, scratch=(), limit=16, flops=10**6, in_specs=None):
+def call(kernel, outs, scratch=(), limit=16, flops=10**6, in_specs=None, aliases=None):
     def run(flags, *arrays):
         return pl.pallas_call(
             kernel,
@@ -31,6 +31,7 @@
             in_specs=[SMEM] + (in_specs or [VMEM] * len(arrays)),
             out_specs=jax.tree.map(lambda _: VMEM, outs),
             scratch_shapes=list(scratch),
+            input_output_aliases=aliases or {},
             compiler_params=pltpu.CompilerParams(vmem_limit_bytes=limit * 2**20),
             cost_estimate=pl.CostEstimate(flops=flops, bytes_accessed=10**5, transcendentals=0),
         )(flags, *arrays)
@@ -86,10 +87,16 @@
     return [sum(widths[:f]) for f in range(len(widths) + 1)]
 
 
+def copied(pairs, sems):
+    copies = [pltpu.make_async_copy(src, dst, sems.at[n]) for n, (src, dst) in enumerate(pairs)]
+    for copy in copies:
+        copy.start()
+    return copies
+
+
 def pack_x_kernel(count, widths, flags, *refs):
     fields = len(widths)
-    ins, refs = refs[: fields + 1], refs[fields + 1 :]
-    kept, outs = refs[: fields + 1], refs[fields + 1 : -2]
+    ins, outs = refs[: fields + 1], refs[fields + 1 : -2]
     near, sems = refs[-2:]
     nx, ny = ins[0].shape[0], ins[0].shape[1]
     base = bases(widths)
@@ -104,16 +111,19 @@
         for f, (ref, width) in enumerate(zip(ins, widths)):
             pairs.append((ref.at[pl.ds(place(nx, width), width)], out.at[pl.ds(base[f], width)]))
         pairs.append((ins[-1].at[place(nx // 2, 1)], near.at[s]))
-    pairs += list(zip(ins, kept))
-    copies = [pltpu.make_async_copy(src, dst, sems.at[n]) for n, (src, dst) in enumerate(pairs)]
-    for copy in copies:
-        copy.start()
+    copies = copied(pairs, sems)
     for out in outs:
         out[base[-1]] = jnp.zeros(out.shape[1:], F32)
     for copy in copies:
         copy.wait()
     for s, out in enumerate(outs):
         out[base[-1], : ny // 2, : near.shape[2]] = near[s].astype(F32)
+
+
+def load_kernel(flags, *refs):
+    count = (len(refs) - 2) // 2
+    for copy in copied(list(zip(refs[:count], refs[count + 1 : -1])), refs[-1]):
+        copy.wait()
 
 
 def slab_of(own, low, high, base, width, x):
@@ -159,47 +169,66 @@
             outer[at + b : at + b + 1, :width] = jnp.where(even, low, high)
 
 
-def pack_z_kernel(widths, labels, flags, *refs):
+def packed_lanes(wide_ref, f, frame, rows, to_high, to_low):
+    group = lane_no((1, LANES)) // HALO
+    nothing = jnp.ones((rows.size, LANES), F32)
+    high, low = nothing, nothing
+    for x in range(frame.wide):
+        moved = turned(wide_ref[f, x, rows], HALO * (x + 1), 1)
+        high = jnp.where(group == x, moved, high)
+        low = jnp.where(group == (x + 1) % frame.wide, moved, low)
+    at = pl.ds(f * frame.tall + rows.start - SUB, rows.size)
+    to_high[at] = high
+    to_low[at] = turned(low, -HALO, 1)
+
+
+def frame_kernel(widths, labels, flags, *refs):
     fields = len(widths)
     ins = refs[:fields]
-    x_low, x_high, inner, outer = refs[fields + labels : fields + labels + 4]
-    wide_ref, send_forth, send_back = refs[fields + labels + 4 :]
+    x_low, x_high, _ = refs[fields : fields + 3]
+    wide_ref, to_high, to_low = refs[fields + 3 :]
     nx, ny = ins[0].shape[0], ins[0].shape[1]
     frame = Frame(nx, ny)
     base = bases(widths)
     tall, own = frame.tall, frame.own
-    even = flags[PARITY] == 0
-
-    def send(at, count, to_high, to_low):
-        send_forth[at : at + count] = jnp.where(even, to_high, to_low)
-        send_back[at : at + count] = jnp.where(even, to_low, to_high)
-
-    group = lane_no((tall, LANES)) // HALO
     spare = jnp.ones((SUB, LANES), F32)
     for f in range(fields):
-        to_high = to_low = jnp.ones((tall, LANES), F32)
+        for x in range(frame.wide):
+            slab = slab_of(ins[f], x_low, x_high, base[f], widths[f], x)
+            wide_ref[f, x, own : own + ny] = jnp.ones((ny, LANES), F32) if slab is None else slab
+            wide_ref[f, x, :SUB] = spare
+            wide_ref[f, x, SUB + tall :] = spare
+        packed_lanes(wide_ref, f, frame, pl.ds(2 * SUB, tall - 2 * SUB), to_high, to_low)
+
+
+def pack_z_kernel(widths, labels, flags, wide_in, high_in, low_in, inner, outer, *refs):
+    fields = len(widths)
+    wide_ref, send_forth, send_back, to_high, to_low = refs[labels:]
+    frame = Frame(wide_ref.shape[1] - 2 * HALO, wide_ref.shape[2] - 2 * (SUB + HALO))
+    ny, tall, own = frame.ny, frame.tall, frame.own
+    even = flags[PARITY] == 0
+    for f in range(fields):
         for x in range(frame.wide):
             at = (f * frame.wide + x) * HALO
-            slab = slab_of(ins[f], x_low, x_high, base[f], widths[f], x)
-            wide_ref[f, x, own : own + ny] = jnp.ones((ny, LANES), F32) if slab is None else slab
             low, high = sides(flags, outer[at : at + HALO], inner[at : at + HALO])
             wide_ref[f, x, SUB:own] = low
             wide_ref[f, x, own + ny : own + ny + HALO] = high
-            wide_ref[f, x, :SUB] = spare
-            wide_ref[f, x, SUB + tall :] = spare
-            moved = turned(wide_ref[f, x, SUB : SUB + tall], HALO * (x + 1), 1)
-            to_high = jnp.where(group == x, moved, to_high)
-            to_low = jnp.where(group == (x + 1) % frame.wide, moved, to_low)
-        send(f * tall, tall, to_high, turned(to_low, -HALO, 1))
+    size = fields * tall
+    to_high[...], to_low[...] = high_in[...], low_in[...]
+    for f in range(fields):
+        for start in (SUB, tall):
+            packed_lanes(wide_ref, f, frame, pl.ds(start, SUB), to_high, to_low)
+    high, low = to_high[...], to_low[...]
+    send_forth[:size], send_back[:size] = jnp.where(even, high, low), jnp.where(even, low, high)
     if labels:
-        nb, rows, width = refs[fields].shape
+        nb, rows, width = refs[0].shape
         lane = lane_no((rows, LANES))
-        to_high = to_low = jnp.zeros((rows, LANES), F32)
+        high = low = jnp.zeros((rows, LANES), F32)
         for b in range(nb):
-            slab = refs[fields][b].astype(F32)
-            to_high = jnp.where(lane == b, slab[:, width - 1 :], to_high)
-            to_low = jnp.where(lane == b, slab[:, :1], to_low)
-        send(fields * tall, rows, to_high, to_low)
+            slab = refs[0][b].astype(F32)
+            high = jnp.where(lane == b, slab[:, width - 1 :], high)
+            low = jnp.where(lane == b, slab[:, :1], low)
+        send_forth[size:], send_back[size:] = jnp.where(even, high, low), jnp.where(even, low, high)
 
 
 class Links:
@@ -236,6 +265,13 @@
             return (lax.ppermute(sends[0], "gx", self.ring_x),)
         return lax.ppermute(sends[0], "gx", self.ring_x), lax.ppermute(sends[1], "gx", self.back(self.ring_x))
 
+    def near(self, values):
+        ring = [(j, (j + 1) % self.sizes[1]) for j in range(self.sizes[1])]
+        forth, back = self.z(values, values)
+        from_x = self.x([values, values])
+        low, high = lax.ppermute(values, "gy", ring), lax.ppermute(values, "gy", self.back(ring))
+        return (forth, back, *from_x, low, high)
+
     def y(self, inner, outer):
         return self.send(inner, self.inner), self.send(outer, self.outer)
 
@@ -248,16 +284,26 @@
     nx, ny, nz = arrays[0].shape
     frame = Frame(nx, ny)
     rows = fields * frame.wide * HALO + labels * ny // 2
-    sends = call(functools.partial(pack_y_kernel, widths, labels), [shaped(rows, nz)] * 2)(flags, *arrays, from_x[0], from_x[-1])
+    sends = call(functools.partial(pack_y_kernel, widths, labels), [shaped(rows, nz)] * 2)(
+        flags, *arrays, from_x[0], from_x[-1]
+    )
+    size = fields * frame.tall
+    framed = call(
+        functools.partial(frame_kernel, widths, labels), [shaped(fields, *frame.main)] + [shaped(size, nz)] * 2
+    )(flags, *arrays[:fields], from_x[0], from_x[-1], sends[0])
     work = beside_y(sends[0]) if beside_y else ()
     from_y = links.y(*sends)
-    from_y = lax.optimization_barrier((*from_y, *work))[:2] if work else from_y
-    rows = fields * frame.tall + labels * ny // 2
+    if work:
+        from_y = lax.optimization_barrier((*from_y, *work))[:2]
+    rows = size + labels * ny // 2
     wide, *sends = call(
-        functools.partial(pack_z_kernel, widths, labels), [shaped(fields, *frame.main)] + [shaped(rows, nz)] * 2
-    )(flags, *arrays, from_x[0], from_x[-1], *from_y)
+        functools.partial(pack_z_kernel, widths, labels),
+        [shaped(fields, *frame.main)] + [shaped(rows, nz)] * 2,
+        [pltpu.VMEM((size, nz), F32)] * 2,
+        aliases={1: 0},
+    )(flags, *framed, *from_y, *arrays[fields:])
     if beside_z:
-        beside_z(sends[0])
+        beside_z(wide, sends[0])
     return (wide, *links.z(*sends)), from_y
 
 
@@ -279,16 +325,13 @@
 
 
 def joined(below, above):
-    lane = lane_no(below.shape)
+    lane = lane_no((1, LANES))
     return jnp.where(lane % HALO == HALO - 1, turned(above, HALO - 1, 1), turned(below, 1, 1))
 
 
-def next_and_last(here, join, x):
+def at_edges(join, x):
     lane = lane_no((1, LANES))
-    edge = turned(join, (LANES - HALO) - HALO * x, 1)
-    upper = jnp.where(lane == LANES - 1, edge, turned(here, -1, 1))
-    lower = jnp.where(lane == 0, edge, turned(here, 1, 1))
-    return upper, lower
+    return jnp.where((lane == 0) | (lane == LANES - 1), turned(join, (LANES - HALO) - HALO * x, 1), 0.0)
 
 
 def ends_near(below, above, edges):
@@ -301,14 +344,13 @@
     )
 
 
-def main_sum(frame, field, x, join, wx, wy, wz_up, wz_low):
-    span = frame.span
-    upper, lower = next_and_last(field[x, span], join, x)
+def main_sum(frame, field, x, join, wx, wy, wz):
+    span, down = frame.span, pl.ds(SUB - 1, frame.tall)
+    here, face_z = field[x, span], wz[x, span]
     total = wx[x, span] * field[x + 1, span] + wx[x - 1, span] * field[x - 1, span]
-    total = total + wy[x, span] * field[x, pl.ds(SUB + 1, frame.tall)]
-    down = pl.ds(SUB - 1, frame.tall)
-    total = total + wy[x, down] * field[x, down]
-    return total + wz_up[x, span] * upper + wz_low[x, span] * lower
+    total = total + wy[x, span] * field[x, pl.ds(SUB + 1, frame.tall)] + wy[x, down] * field[x, down]
+    total = total + face_z * turned(here, -1, 1) + turned(face_z * here, 1, 1)
+    return total + at_edges(join, x)
 
 
 def ends_sum(frame, ends, s, upper, lower, wx, wy, wz_up, wz_low):
@@ -340,11 +382,48 @@
     return picked(values + turned(values, -1, 1), even)
 
 
-def fine_kernel(flags, wide_ref, forth, back, from_x_low, from_x_high, inner, outer, block_label,
-                face_label, inner_diag, *refs):
-    main, ends = refs[:6], refs[6:12]
-    pre, face_near, face_weight, scaled_rhs, scale, once, once_ends, res, diag, block_res = refs[12:]
-    wx, wy, wz_up, wz_low, inv_diag, start = main
+def faces_y_kept(flags, frame):
+    row = row_no((frame.tall, LANES))
+    at_low, at_high = row == HALO - 1, row == HALO + frame.ny - 1
+    return jnp.where(at_low, flags[Y_LOW], jnp.where(at_high, flags[Y_HIGH], 1)).astype(F32)
+
+
+def fields_kernel(flags, wide_ref, _, wx, wy, wz, partial, cond_edges):
+    frame = Frame(wx.shape[0] - 2 * HALO, wx.shape[1] - 2 * (SUB + HALO))
+    wide, tall, span = frame.wide, frame.tall, frame.span
+    last = HALO + frame.nx
+    keep_y = faces_y_kept(flags, frame)
+    inside = jnp.where(lane_no((1, LANES)) == LANES - 1, 0.0, 1.0)
+    clear_spares(wy, frame)
+
+    def fields(xs, carry):
+        before, edges = carry
+        stores = []
+        for x in xs:
+            here = wide_ref[0, x, span]
+            keep = jnp.where(x == HALO - 1, flags[X_LOW], jnp.where(x == last - 1, flags[X_HIGH], 1)).astype(F32)
+            face_x = keep * weight(here, wide_ref[0, jnp.minimum(x + 1, wide - 1), span])
+            face_y = keep_y * weight(here, wide_ref[0, x, pl.ds(SUB + 1, tall)])
+            face_z = inside * weight(here, turned(here, -1, 1))
+            total = wide_ref[2, x, span] + face_x + before + face_y + turned(face_y, 1, 0)
+            total = total + face_z + turned(face_z, 1, 1)
+            stores.append((x, (face_x, face_y, face_z, total)))
+            edges = edge_step(here, x, edges)
+            before = face_x
+        for x, values in stores:
+            for ref, value in zip((wx, wy, wz, partial), values):
+                ref[x, span] = value
+        return before, edges
+
+    nothing = jnp.zeros((tall, LANES), F32)
+    cond_edges[...] = batched(0, wide, fields, (nothing, nothing + 1.0), 4)[1]
+
+
+def fine_kernel(flags, wide_ref, forth, back, from_x_low, from_x_high, inner, outer, wx, wy, wz, partial, cond_edges,
+                block_label, face_label, inner_diag, *refs):
+    inv_diag, start = refs[:2]
+    ends = refs[2:8]
+    pre, face_near, face_weight, scaled_rhs, scale, once, once_ends, res, diag, block_res = refs[8:]
     ex, ey, ez_up, ez_low, inv_ends, start_ends = ends
     nx, ny = pre.shape[0], pre.shape[1]
     frame = Frame(nx, ny)
@@ -352,25 +431,13 @@
     last = HALO + nx
     got = [sides(flags, forth[f * tall : (f + 1) * tall], back[f * tall : (f + 1) * tall]) for f in range(3)]
     (cond_below, cond_above), rhs_ends, absorb_ends = got
-    for ref in (wy, start, once):
+    for ref in (start, once, ey, start_ends, once_ends):
         clear_spares(ref, frame)
-    for ref in (ey, start_ends, once_ends):
-        clear_spares(ref, frame)
-
-    row = row_no((tall, LANES))
+
     lane = lane_no((1, LANES))
-    keep_y = jnp.where(
-        row == HALO - 1, flags[Y_LOW], jnp.where(row == HALO + ny - 1, flags[Y_HIGH], 1)
-    ).astype(F32)
+    keep_y = faces_y_kept(flags, frame)
     keep_low, keep_high = flags[Z_LOW].astype(F32), flags[Z_HIGH].astype(F32)
-
-    def cond_edges(xs, edges):
-        for x in xs:
-            edges = edge_step(wide_ref[0, x, span], x, edges)
-        return edges
-
-    edges = batched(0, wide, cond_edges, jnp.ones((tall, LANES), F32), 8)
-    near = ends_near(cond_below, cond_above, edges)
+    near = ends_near(cond_below, cond_above, cond_edges[...])
     slab = lane // HALO
     keep_x = jnp.where(
         slab == HALO - 1, flags[X_LOW], jnp.where(slab == last - 1, flags[X_HIGH], 1)
@@ -390,36 +457,25 @@
         inv_ends[s, span] = inverse
         start_ends[s, span] = inverse * rhs_ends[s]
 
-    join = joined(cond_below, cond_above)
-    wz_under = ez_up[0, span]
-
-    def fields(xs, carry):
-        before, edges = carry
+    end_low, end_high = ez_up[0, span], ez_low[1, span]
+    join_faces = joined(end_low, end_high)
+
+    def first_sweep(xs, edges):
         stores = []
         for x in xs:
-            here = wide_ref[0, x, span]
-            keep = jnp.where(x == HALO - 1, flags[X_LOW], jnp.where(x == last - 1, flags[X_HIGH], 1)).astype(F32)
-            upper = next_and_last(here, join, x)[0]
-            face_x = keep * weight(here, wide_ref[0, jnp.minimum(x + 1, wide - 1), span])
-            face_y = keep_y * weight(here, wide_ref[0, x, pl.ds(SUB + 1, tall)])
-            up = weight(here, upper) * jnp.where(lane == LANES - 1, keep_high, 1.0)
-            under = turned(wz_under, (LANES - HALO + 1) - HALO * x, 1)
-            low = jnp.where(lane == 0, under, turned(up, 1, 1))
-            total = wide_ref[2, x, span] + face_x + before + face_y + turned(face_y, 1, 0) + up + low
+            total = partial[x, span] + at_edges(join_faces, x)
             inverse = OMEGA_FINE / total
             begin = inverse * wide_ref[1, x, span]
-            stores.append((x, (face_x, face_y, up, low, inverse, begin, total)))
+            stores.append((x, (total, inverse, begin)))
             edges = edge_step(begin, x, edges)
-            before = face_x
         for x, values in stores:
-            for ref, value in zip((*main, diag), values):
+            for ref, value in zip((diag, inv_diag, start), values):
                 ref[x, span] = value
-        return before, edges
-
-    nothing = jnp.zeros((tall, LANES), F32)
-    _, edges = batched(0, wide, fields, (nothing, nothing), 4)
-
-    join = joined(start_ends[0, span], start_ends[1, span])
+        return edges
+
+    edges = batched(0, wide, first_sweep, jnp.zeros((tall, LANES), F32), 4)
+
+    join = joined(end_low * start_ends[0, span], end_high * start_ends[1, span])
     near = ends_near(start_ends[0, span], start_ends[1, span], edges)
     for s in range(2):
         total = ends_sum(frame, start_ends, s, near[2 * s], near[2 * s + 1], ex, ey, ez_up, ez_low)
@@ -428,19 +484,19 @@
     def second(xs, carry):
         news = []
         for x in xs:
-            total = main_sum(frame, start, x, join, wx, wy, wz_up, wz_low)
+            total = main_sum(frame, start, x, join, wx, wy, wz)
             news.append((2.0 - OMEGA_FINE) * start[x, span] + inv_diag[x, span] * total)
         for x, new in zip(xs, news):
             once[x, span] = new
         return carry
 
     batched(HALO - 1, last + 1, second, 0)
-    join2 = joined(once_ends[0, span], once_ends[1, span])
+    join2 = joined(end_low * once_ends[0, span], end_high * once_ends[1, span])
 
     def remainder(xs, carry):
         news = []
         for x in xs:
-            total = main_sum(frame, once, x, join2, wx, wy, wz_up, wz_low)
+            total = main_sum(frame, once, x, join2, wx, wy, wz)
             news.append(wide_ref[1, x, span] - diag[x, span] * once[x, span] + total)
         for x, new in zip(xs, news):
             res[x - HALO, span] = new
@@ -633,9 +689,8 @@
 
 
 def turn_kernel(flags, tiles, scaled_rhs, scale, own, *refs):
-    *from_x, inner, outer, forth, back, out = refs
-    vectors = [own[...]] + [ref[...] for ref in from_x]
-    vectors += [*sides(flags, outer[...], inner[...]), *sides(flags, forth[...], back[...])]
+    forth, back, *others, out = refs
+    vectors = [own[...]] + [ref[...] for ref in others] + [*sides(flags, forth[...], back[...])]
     row = row_no((SUB, AGG))
     parts = []
     for v in vectors:
@@ -678,12 +733,11 @@
 
 
 def post_kernel(flags, wide_ref, forth, back, *refs):
-    main, ends = refs[:6], refs[6:12]
-    out, one, two, one_ends, two_ends = refs[12:]
+    (wx, wy, wz, inv_diag, start), ends = refs[:5], refs[5:11]
+    out, one, two, one_ends, two_ends = refs[11:]
     nx, ny = out.shape[0], out.shape[1]
     frame = Frame(nx, ny)
     wide, tall, span = frame.wide, frame.tall, frame.span
-    wx, wy, wz_up, wz_low, inv_diag, start = main
     ex, ey, ez_up, ez_low, inv_ends, start_ends = ends
     for ref in (one, two, one_ends, two_ends):
         clear_spares(ref, frame)
@@ -693,7 +747,7 @@
     buffers = ((wide_ref.at[0], two_ends), (one, one_ends), (two, two_ends), (one, one_ends))
     for s in range(POST):
         src, src_ends = buffers[s]
-        join = joined(src_ends[0, span], src_ends[1, span])
+        join = joined(ez_up[0, span] * src_ends[0, span], ez_low[1, span] * src_ends[1, span])
         final = s == POST - 1
         dst, dst_ends = (None, None) if final else buffers[s + 1]
 
@@ -701,7 +755,7 @@
             news = []
             for x in xs:
                 here = src[x, span]
-                total = main_sum(frame, src, x, join, wx, wy, wz_up, wz_low)
+                total = main_sum(frame, src, x, join, wx, wy, wz)
                 news.append(kept * here + start[x, span] + inv_diag[x, span] * total)
                 if not final:
                     edges = edge_step(here, x, edges)
@@ -733,13 +787,20 @@
     ).astype(jnp.int32)
     arrays = (conductance, right_side, absorption, block_agg)
     n_send = 1 if n_x == 2 else 2
-    got = call(
+    pinned = [pltpu.with_memory_space_constraint(a, pltpu.HBM) for a in arrays]
+    hbm = pl.BlockSpec(memory_space=pltpu.HBM)
+    x_sends = call(
         functools.partial(pack_x_kernel, n_x, WIDTHS),
-        [jax.ShapeDtypeStruct(a.shape, a.dtype) for a in arrays] + [shaped(sum(WIDTHS) + 1, ny, nz)] * n_send,
-        [pltpu.VMEM((n_send, ny // 2, nz // 2), jnp.int32), pltpu.SemaphoreType.DMA((n_send * 4 + 4,))],
-        in_specs=[pl.BlockSpec(memory_space=pltpu.HBM)] * 4,
-    )(flags, *(pltpu.with_memory_space_constraint(a, pltpu.HBM) for a in arrays))
-    arrays, x_sends = got[:4], got[4:]
+        [shaped(sum(WIDTHS) + 1, ny, nz)] * n_send,
+        [pltpu.VMEM((n_send, ny // 2, nz // 2), jnp.int32), pltpu.SemaphoreType.DMA((n_send * 4,))],
+        in_specs=[hbm] * 4,
+    )(flags, *pinned)
+    arrays = call(
+        load_kernel,
+        [jax.ShapeDtypeStruct(a.shape, a.dtype) for a in arrays],
+        [pltpu.SemaphoreType.DMA((4,))],
+        in_specs=[hbm] * 4 + [VMEM],
+    )(flags, *pinned, x_sends[0])
     blocks = (nb, SUB, LANES)
     outs = [shaped(*blocks), shaped(3, *blocks), shaped(3, *blocks), shaped(*blocks), shaped(6, SUB, LANES)]
     outs += [jax.ShapeDtypeStruct((nb, ny // 2, LANES), jnp.int32)]
@@ -747,31 +808,39 @@
     pair = [pltpu.VMEM((AGG, SUB * LANES), BF16), pltpu.VMEM((2 * AGG, SUB * LANES), BF16)]
     *rows, face_label, lift = call(blocks_kernel, outs, scratch)(flags, arrays[0], arrays[2], arrays[3], x_sends[0])
     block_label = rows[0]
-    first = call(functools.partial(own_kernel, 0, nb // 2, nb), [shaped(AGG, 2 * AGG)], pair * 2)(
-        flags, *rows, x_sends[0]
-    )[0]
+    bounds = (0, nb // 6, nb * 7 // 12, nb)
+    parts = []
+
+    def own_part(p, sent):
+        outs = [shaped(AGG, 2 * AGG)]
+        if p == 2:
+            outs = [jax.ShapeDtypeStruct((AGG, 2 * AGG), BF16), shaped(SUB, AGG)]
+        kernel = functools.partial(own_kernel, bounds[p], bounds[p + 1], nb)
+        parts.append(call(kernel, outs, pair * 2)(flags, *rows, *(parts[-1] if p else ()), sent))
+        return parts[-1]
+
+    first = own_part(0, x_sends[0])
     from_x = links.x(x_sends)
-    from_x = lax.optimization_barrier((*from_x, first))[:-1]
-    later = []
-
-    def second_half(sent):
-        outs = [jax.ShapeDtypeStruct((AGG, 2 * AGG), BF16), shaped(SUB, AGG)]
-        later.extend(
-            call(functools.partial(own_kernel, nb // 2, nb, nb), outs, pair * 2)(flags, *rows, first, sent)
+    from_x = lax.optimization_barrier((*from_x, *first))[:-1]
+    fields = []
+
+    def beside_z(wide, sent):
+        fields.extend(
+            call(fields_kernel, [shaped(*frame.main)] * 4 + [shaped(frame.tall, nz)], limit=24)(flags, wide, sent)
         )
-        return later
-
-    halo, from_y = widened(links, flags, WIDTHS, arrays, from_x, second_half)
-    own_tile, inner_diag = later
-    outs = [shaped(*frame.main)] * 6 + [shaped(*frame.ends)] * 6 + [shaped(nx, ny, nz)]
+        own_part(2, sent)
+
+    halo, from_y = widened(links, flags, WIDTHS, arrays, from_x, lambda sent: own_part(1, sent), beside_z)
+    own_tile, inner_diag = parts[-1]
+    outs = [shaped(*frame.main)] * 2 + [shaped(*frame.ends)] * 6 + [shaped(nx, ny, nz)]
     outs += [shaped(6, SUB, LANES)] * 2 + [shaped(SUB, AGG)] * 2
     scratch = [pltpu.VMEM(frame.main, F32), pltpu.VMEM(frame.ends, F32), pltpu.VMEM((nx, frame.rows, LANES), F32)]
-    scratch += [pltpu.VMEM(frame.main, F32), pltpu.VMEM((nb, SUB, LANES), F32)]
+    scratch += [pltpu.VMEM(frame.main, F32), pltpu.VMEM(blocks, F32)]
     got = call(fine_kernel, outs, scratch, limit=28)(
-        flags, *halo, from_x[0], from_x[-1], *from_y, block_label, face_label, inner_diag
+        flags, *halo, from_x[0], from_x[-1], *from_y, *fields, block_label, face_label, inner_diag
     )
-    fields, pre = got[:12], got[12]
-    face_near, face_weight, scaled_rhs, scale = got[13:]
+    fields, pre = (*fields[:3], *got[:8]), got[8]
+    face_near, face_weight, scaled_rhs, scale = got[9:]
     tiles = call(
         functools.partial(faces_kernel, n_x),
         jax.ShapeDtypeStruct(((n_send + 5) * AGG, 2 * AGG), BF16),
@@ -779,8 +848,7 @@
     )(flags, own_tile, face_label, face_near, face_weight)
     coarse = scaled_rhs
     for _ in range(KC - 1):
-        near = links.x([coarse] * n_send) + links.y(coarse, coarse) + links.z(coarse, coarse)
-        coarse = call(turn_kernel, shaped(SUB, AGG))(flags, tiles, scaled_rhs, scale, coarse, *near)
+        coarse = call(turn_kernel, shaped(SUB, AGG))(flags, tiles, scaled_rhs, scale, coarse, *links.near(coarse))
     x_sends = call(functools.partial(send_kernel, n_x), [shaped(HALO, ny, nz)] * n_send)(flags, pre, lift, coarse)
     from_x = links.x(x_sends)
     corrected = call(correct_kernel, shaped(nx, ny, nz))(flags, pre, lift, coarse)

time: 105 us -> 99.5 us (0.948)
  waiting for transfers between devices: 29.5 us -> 18.3 us
  Pallas kernels: 36.2 us -> 40.5 us
  starting transfers between devices: 38.7 us -> 40.2 us
    ppermute x36 -> x22, waiting for transfers between devices: 20.8 us -> 12.1 us  [send(): return lax.ppermute(values, ('gx', 'gy', 'gz'), pairs)]
    ppermute x0 -> x14, starting transfers between devices: none -> 7.99 us  [the longest x7 7.27 us: near(): lax.ppermute(values, 'gy', self.back(ring))]
    ppermute x36 -> x22, starting transfers between devices: 27.5 us -> 21.1 us  [send(): return lax.ppermute(values, ('gx', 'gy', 'gz'), pairs)]
    pallas_call x20 -> x25, Pallas kernels: 36.2 us -> 40.5 us  [run(): pl.pallas_call(kernel, out_shape=outs, in_specs=[SMEM] + (in_specs or [VM...]
    ppermute x9, waiting for transfers between devices: 8.77 us -> 5.92 us  [x(): return (lax.ppermute(sends[0], 'gx', self.ring_x),)]
  transfers between devices with their start and end apart: 45 -> 45, of which waited for: 20 -> 18; matrix products, arithmetic and copies ran while one was open for 0% -> 0% of each run, Pallas kernels for 12% -> 19%
where the time goes in v5:
time: 99.5 us; the launch traced here: 99.3 us
  Pallas kernels  40.5 us (41%)
  starting transfers between devices  40.2 us (40%)
  waiting for transfers between devices  18.3 us (18%)
    pallas_call x25, Pallas kernels, run(): pl.pallas_call(kernel, out_shape=outs, in_specs=[SMEM] + (in_specs or [VM...  40.5 us
    ppermute x22, starting transfers between devices, send(): return lax.ppermute(values, ('gx', 'gy', 'gz'), pairs)  21.1 us
    ppermute x22, waiting for transfers between devices, send(): return lax.ppermute(values, ('gx', 'gy', 'gz'), pairs)  12.1 us
    ppermute x9, starting transfers between devices, x(): return (lax.ppermute(sends[0], 'gx', self.ring_x),)  11.1 us
    ppermute x7, starting transfers between devices, near(): lax.ppermute(values, 'gy', self.back(ring))  7.27 us
    ppermute x9, waiting for transfers between devices, x(): return (lax.ppermute(sends[0], 'gx', self.ring_x),)  5.92 us
  transfers between devices with their start and end apart: 45, of which 18 were waited for; matrix products, arithmetic and copies ran while one was open for 0% of the time, Pallas kernels for 19%

profile of v5, /device:TPU:0, one launch (start us, length us, event | category | flops | bytes accessed | tf_op | source)
XLA Modules:
  0.0 99.3 jit_solution(14722848150544002301)
XLA Ops:
  0.1 1.4 %shard_map.46.refs_4_._.refs_0_ = f32[11,32,128]{2,1,0:T(8,128)S(1)} custom-call(s32[8]{0:T(128)S(1)} %stack.59.flags, f32[24,32,128]{2,1,0:T(8,128)} %refs_0_.3, f32[24,32,128]{2,1,0:T(8,128)} %refs_1_.3, f32[24,32,128]{2,1,0:T(8,128)} %refs_2_.3, s32[12,16,64]{2,1,0:T(8,128)} %refs_3_.3), custom_call_target="tpu_custom_call" | custom-call | flops 1000000 | bytes 100000 | tf_op jit(solution)/shard_map/pallas_call | solution.py:28
  1.5 3.0 %collective-permute-start = (f32[11,32,128]{2,1,0:T(8,128)S(1)}, f32[11,32,128]{2,1,0:T(8,128)S(1)}, u32[]{:S(2)}, u32[]{:S(2)}) collective-permute-start(f32[11,32,128]{2,1,0:T(8,128)S(1)} %shard_map.46.refs_4_._.refs_0_), channel_id=1, source_target_pairs={{0,16},{16,0},{1,17},{17,1},{2,18},{18,2},{3,19},{19,3},{4,20},{20... | collective-permute-start | bytes 540680 | tf_op jit(solution)/shard_map/ppermute | solution.py:265
  4.5 1.8 %shard_map.47 = (f32[24,32,128]{2,1,0:T(8,128)S(1)}, f32[24,32,128]{2,1,0:T(8,128)S(1)}, f32[24,32,128]{2,1,0:T(8,128)S(1)}, s32[12,16,64]{2,1,0:T(8,128)S(1)}) custom-call(s32[8]{0:T(128)S(1)} %stack.59.flags, f32[24,32,128]{2,1,0:T(8,128)} %refs_0_.3, f32[24,32,128]{2,1,0:T(8,128)} %refs_1_.3, f32[24,32,128]{2,1,0:T(8,128)} %refs_2_.3, ...), custom_call_target="tpu_custom_call" | custom-call | flops 1000000 | bytes 100000 | tf_op jit(solution)/shard_map/pallas_call | solution.py:28
  6.4 2.1 %shard_map.48 = (f32[12,8,128]{2,1,0:T(8,128)S(1)}, f32[3,12,8,128]{3,2,1,0:T(8,128)S(1)}, f32[3,12,8,128]{3,2,1,0:T(8,128)S(1)}, f32[12,8,128]{2,1,0:T(8,128)S(...) custom-call(s32[8]{0:T(128)S(1)} %stack.59.flags, f32[24,32,128]{2,1,0:T(8,128)S(1)} %get-tuple-element.54.cond.refs_0_, ...), custom_call_target="tpu_custom_call" | custom-call | flops 1000000 | bytes 100000 | tf_op jit(solution)/shard_map/pallas_call | solution.py:28
  8.5 1.5 %shard_map.49.refs_0_ = f32[128,256]{1,0:T(8,128)S(1)} custom-call(s32[8]{0:T(128)S(1)} %stack.59.flags, f32[12,8,128]{2,1,0:T(8,128)S(1)} %get-tuple-element.58.block_label, f32[3,12,8,128]{3,2,1,0:T(8,128)S(1)} %get-tuple-element.59.near, f32[3,12,8,128]{3,2,1,0:T(8,128)S(1)} %get-tuple-element.60.weights, f32[12,8,128]{2,1,0:T(8,128)S(1)} %get-tuple-element.61.inner, ...), custom_call_target="tpu_custom_call" | custom-call | flops 1000000 | bytes 100000 | tf_op jit(solution)/shard_map/pallas_call | solution.py:28
  12.3 2.9 %shard_map.52.refs_0_ = f32[128,256]{1,0:T(8,128)S(1)} custom-call(s32[8]{0:T(128)S(1)} %stack.59.flags, f32[12,8,128]{2,1,0:T(8,128)S(1)} %get-tuple-element.58.block_label, f32[3,12,8,128]{3,2,1,0:T(8,128)S(1)} %get-tuple-element.59.near, f32[3,12,8,128]{3,2,1,0:T(8,128)S(1)} %get-tuple-element.60.weights, f32[12,8,128]{2,1,0:T(8,128)S(1)} %get-tuple-element.61.inner, ...), custom_call_target="tpu_custom_call" | custom-call | flops 1000000 | bytes 100000 | tf_op jit(solution)/shard_map/pallas_call | solution.py:28
  17.7 2.0 %collective-permute-start.3 = (f32[136,128]{1,0:T(8,128)S(1)}, f32[136,128]{1,0:T(8,128)S(1)}, u32[]{:S(2)}, u32[]{:S(2)}) collective-permute-start(f32[136,128]{1,0:T(8,128)S(1)} %get-tuple-element.71._.refs_1_), channel_id=1, source_target_pairs={{0,1},{1,2},{2,3},{3,7},{7,6},{6,5},{5,4},{4,0},{8,9},{9,10},{10,1... | collective-permute-start | bytes 208904 | tf_op jit(solution)/shard_map/ppermute | solution.py:261
  19.7 3.8 %shard_map.55 = (bf16[128,256]{1,0:T(8,128)(2,1)S(1)}, f32[8,128]{1,0:T(8,128)S(1)}) custom-call(s32[8]{0:T(128)S(1)} %stack.59.flags, f32[12,8,128]{2,1,0:T(8,128)S(1)} %get-tuple-element.58.block_label, f32[3,12,8,128]{3,2,1,0:T(8,128)S(1)} %get-tuple-element.59.near, f32[3,12,8,128]{3,2,1,0:T(8,128)S(1)} %get-tuple-element.60.weights, ...), custom_call_target="tpu_custom_call" | custom-call | flops 1000000 | bytes 100000 | tf_op jit(solution)/shard_map/pallas_call | solution.py:28
  23.5 1.9 %shard_map.54 = (f32[32,56,128]{2,1,0:T(8,128)S(1)}, f32[32,56,128]{2,1,0:T(8,128)S(1)}, f32[32,56,128]{2,1,0:T(8,128)S(1)}, f32[32,56,128]{2,1,0:T(8,128)S(1)}, f32[40,128]{1,0:T(8,128)S(1)}) custom-call(s32[8]{0:T(128)S(1)} %stack.59.flags, f32[3,32,56,128]{3,2,1,0:T(8,128)S(1)} %get-tuple-element.70.wide_ref, f32[136,128]{1,0:T(8,128)S(1)} %get-tuple-element.71._.refs_1_), custom_call_target="tpu_custom_call" | custom-call | flops 1000000 | bytes 100000 | tf_op jit(solution)/shard_map/pallas_call | solution.py:28
  25.4 5.6 %shard_map.56 = (f32[32,56,128]{2,1,0:T(8,128)S(1)}, f32[32,56,128]{2,1,0:T(8,128)S(1)}, f32[2,56,128]{2,1,0:T(8,128)S(1)}, f32[2,56,128]{2,1,0:T(8,128)S(1)}, f...) custom-call(s32[8]{0:T(128)S(1)} %stack.59.flags, ...), custom_call_target="tpu_custom_call" | custom-call | flops 1000000 | bytes 100000 | tf_op jit(solution)/shard_map/pallas_call | solution.py:28
  32.8 1.7 %collective-permute-start.5 = (f32[8,128]{1,0:T(8,128)S(1)}, f32[8,128]{1,0:T(8,128)S(1)}, u32[]{:S(2)}, u32[]{:S(2)}) collective-permute-start(f32[8,128]{1,0:T(8,128)S(1)} %get-tuple-element.85.scaled_rhs.own), channel_id=1, source_target_pairs={{0,1},{1,2},{2,3},{3,7},{7,6},{6,5},{5,4},{4,0},{8,9},{9,10},{10,1... | collective-permute-start | bytes 12296 | tf_op jit(solution)/shard_map/ppermute | solution.py:261
  34.5 2.3 %shard_map.57.tiles = bf16[768,256]{1,0:T(8,128)(2,1)S(1)} custom-call(s32[8]{0:T(128)S(1)} %stack.59.flags, bf16[128,256]{1,0:T(8,128)(2,1)S(1)} %get-tuple-element.82.own, f32[6,8,128]{2,1,0:T(8,128)S(1)} %get-tuple-element.78.face_label, f32[6,8,128]{2,1,0:T(8,128)S(1)} %get-tuple-element.83.face_near, f32[6,8,128]{2,1,0:T(8,128)S(1)} %get-tuple-element.84.face_weight), custom_call_target="tpu_custom_call" | custom-call | flops 1000000 | bytes 100000 | tf_op jit(solution)/shard_map/pallas_call | solution.py:28
  40.0 1.3 %collective-permute-start.10 = (f32[8,128]{1,0:T(8,128)S(1)}, f32[8,128]{1,0:T(8,128)S(1)}, u32[]{:S(2)}, u32[]{:S(2)}) collective-permute-start(f32[8,128]{1,0:T(8,128)S(1)} %shard_map.58.own), channel_id=1, source_target_pairs={{0,1},{1,2},{2,3},{3,7},{7,6},{6,5},{5,4},{4,0},{8,9},{9,10},{10,1... | collective-permute-start | bytes 12296 | tf_op jit(solution)/shard_map/ppermute | solution.py:261
  43.6 1.6 %collective-permute-start.19 = (f32[8,128]{1,0:T(8,128)S(1)}, f32[8,128]{1,0:T(8,128)S(1)}, u32[]{:S(2)}, u32[]{:S(2)}) collective-permute-start(f32[8,128]{1,0:T(8,128)S(1)} %shard_map.59.own), channel_id=1, source_target_pairs={{4,0},{8,4},{12,8},{0,12},{5,1},{9,5},{13,9},{1,13},{6,2},{10,6},{... | collective-permute-start | bytes 12296 | tf_op jit(solution)/shard_map/ppermute | solution.py:272
  50.4 1.6 %collective-permute-start.24 = (f32[8,128]{1,0:T(8,128)S(1)}, f32[8,128]{1,0:T(8,128)S(1)}, u32[]{:S(2)}, u32[]{:S(2)}) collective-permute-start(f32[8,128]{1,0:T(8,128)S(1)} %shard_map.60.own), channel_id=1, source_target_pairs={{4,0},{8,4},{12,8},{0,12},{5,1},{9,5},{13,9},{1,13},{6,2},{10,6},{... | collective-permute-start | bytes 12296 | tf_op jit(solution)/shard_map/ppermute | solution.py:272
  59.7 1.3 %collective-permute-start.26 = (f32[8,128]{1,0:T(8,128)S(1)}, f32[8,128]{1,0:T(8,128)S(1)}, u32[]{:S(2)}, u32[]{:S(2)}) collective-permute-start(f32[8,128]{1,0:T(8,128)S(1)} %shard_map.61.own), channel_id=1, source_target_pairs={{1,0},{2,1},{3,2},{7,3},{6,7},{5,6},{4,5},{0,4},{9,8},{10,9},{11,1... | collective-permute-start | bytes 12296 | tf_op jit(solution)/shard_map/ppermute | solution.py:261
  67.0 1.3 %collective-permute-start.30 = (f32[8,128]{1,0:T(8,128)S(1)}, f32[8,128]{1,0:T(8,128)S(1)}, u32[]{:S(2)}, u32[]{:S(2)}) collective-permute-start(f32[8,128]{1,0:T(8,128)S(1)} %shard_map.62.own), channel_id=1, source_target_pairs={{0,1},{1,2},{2,3},{3,7},{7,6},{6,5},{5,4},{4,0},{8,9},{9,10},{10,1... | collective-permute-start | bytes 12296 | tf_op jit(solution)/shard_map/ppermute | solution.py:261
  72.7 1.4 %collective-permute-start.36 = (f32[8,128]{1,0:T(8,128)S(1)}, f32[8,128]{1,0:T(8,128)S(1)}, u32[]{:S(2)}, u32[]{:S(2)}) collective-permute-start(f32[8,128]{1,0:T(8,128)S(1)} %shard_map.63.own), channel_id=1, source_target_pairs={{1,0},{2,1},{3,2},{7,3},{6,7},{5,6},{4,5},{0,4},{9,8},{10,9},{11,1... | collective-permute-start | bytes 12296 | tf_op jit(solution)/shard_map/ppermute | solution.py:261
  79.5 2.8 %collective-permute-done.40.refs_1_.refs_2_ = f32[4,32,128]{2,1,0:T(8,128)S(1)} collective-permute-done((f32[4,32,128]{2,1,0:T(8,128)S(1)}, f32[4,32,128]{2,1,0:T(8,128)S(1)}, u32[]{:S(2)}, u32[]{:S(2)}) %collective-permute-start.40) | collective-permute-done | bytes 65568 | tf_op jit(solution)/shard_map/ppermute | solution.py:265
  85.2 2.1 %collective-permute-done.42.outer = f32[128,128]{1,0:T(8,128)S(1)} collective-permute-done((f32[128,128]{1,0:T(8,128)S(1)}, f32[128,128]{1,0:T(8,128)S(1)}, u32[]{:S(2)}, u32[]{:S(2)}) %collective-permute-start.42) | collective-permute-done | bytes 65568 | tf_op jit(solution)/shard_map/ppermute | solution.py:261
  88.1 1.8 %collective-permute-start.43 = (f32[40,128]{1,0:T(8,128)S(1)}, f32[40,128]{1,0:T(8,128)S(1)}, u32[]{:S(2)}, u32[]{:S(2)}) collective-permute-start(f32[40,128]{1,0:T(8,128)S(1)} %get-tuple-element.93), channel_id=1, source_target_pairs={{0,1},{1,2},{2,3},{3,7},{7,6},{6,5},{5,4},{4,0},{8,9},{9,10},{10,1... | collective-permute-start | bytes 61448 | tf_op jit(solution)/shard_map/ppermute | solution.py:261
  89.8 1.5 %collective-permute-done.43.forth = f32[40,128]{1,0:T(8,128)S(1)} collective-permute-done((f32[40,128]{1,0:T(8,128)S(1)}, f32[40,128]{1,0:T(8,128)S(1)}, u32[]{:S(2)}, u32[]{:S(2)}) %collective-permute-start.43) | collective-permute-done | bytes 20512 | tf_op jit(solution)/shard_map/ppermute | solution.py:261
  91.3 2.3 %collective-permute-done.44.back = f32[40,128]{1,0:T(8,128)S(1)} collective-permute-done((f32[40,128]{1,0:T(8,128)S(1)}, f32[40,128]{1,0:T(8,128)S(1)}, u32[]{:S(2)}, u32[]{:S(2)}) %collective-permute-start.44) | collective-permute-done | bytes 20512 | tf_op jit(solution)/shard_map/ppermute | solution.py:261
  93.6 5.7 %shard_map.70 = f32[24,32,128]{2,1,0:T(8,128)} custom-call(s32[8]{0:T(128)S(1)} %stack.59.flags, f32[1,32,56,128]{3,2,1,0:T(8,128)S(1)} %get-tuple-element.92.wide_ref, f32[40,128]{1,0:T(8,128)S(1)} %collective-permute-done.43.forth, f32[40,128]{1,0:T(8,128)S(1)} %collective-permute-done.44.back, f32[32,56,128]{2,1,0:T(8,128)S(1)} %get-tuple-element.73.wx.refs_0_, ...), custom_call_target="tpu_custom_call" | custom-call | flops 1000000 | bytes 100000 | tf_op jit(solution)/shard_map/pallas_call | solution.py:28
  (92 shorter events, 44.1 us)
Async XLA Ops:
  1.5 8.4 %collective-permute-start = (f32[11,32,128]{2,1,0:T(8,128)S(1)}, f32[11,32,128]{2,1,0:T(8,128)S(1)}, u32[]{:S(2)}, u32[]{:S(2)}) collective-permute-start(f32[11,32,128]{2,1,0:T(8,128)S(1)} %shard_map.46.refs_4_._.refs_0_), channel_id=1, source_target_pairs={{0,16},{16,0},{1,17},{17,1},{2,18},{18,2},{3,19},{19,3},{4,20},{20... | collective-permute-start | bytes 540680 | tf_op jit(solution)/shard_map/ppermute | solution.py:265
  10.6 5.8 %collective-permute-start.2 = (f32[400,128]{1,0:T(8,128)S(1)}, f32[400,128]{1,0:T(8,128)S(1)}, u32[]{:S(2)}, u32[]{:S(2)}) collective-permute-start(f32[400,128]{1,0:T(8,128)S(1)} %get-tuple-element.67), channel_id=1, source_target_pairs={{0,16},{1,17},{2,18},{3,19},{4,8},{5,9},{6,10},{7,11},{8,4},{9,5},... | collective-permute-start | bytes 614408 | tf_op jit(solution)/shard_map/ppermute | solution.py:261
  11.5 4.9 %collective-permute-start.1 = (f32[400,128]{1,0:T(8,128)S(1)}, f32[400,128]{1,0:T(8,128)S(1)}, u32[]{:S(2)}, u32[]{:S(2)}) collective-permute-start(f32[400,128]{1,0:T(8,128)S(1)} %get-tuple-element.63.refs_5_.refs_1_), channel_id=1, source_target_pairs={{0,4},{1,5},{2,6},{3,7},{4,0},{5,1},{6,2},{7,3},{8,12},{9,13},{10,... | collective-permute-start | bytes 614408 | tf_op jit(solution)/shard_map/ppermute | solution.py:261
  17.7 7.7 %collective-permute-start.4 = (f32[136,128]{1,0:T(8,128)S(1)}, f32[136,128]{1,0:T(8,128)S(1)}, u32[]{:S(2)}, u32[]{:S(2)}) collective-permute-start(f32[136,128]{1,0:T(8,128)S(1)} %get-tuple-element.72), channel_id=1, source_target_pairs={{1,0},{2,1},{3,2},{7,3},{6,7},{5,6},{4,5},{0,4},{9,8},{10,9},{11,1... | collective-permute-start | bytes 208904 | tf_op jit(solution)/shard_map/ppermute | solution.py:261
  17.7 7.7 %collective-permute-start.3 = (f32[136,128]{1,0:T(8,128)S(1)}, f32[136,128]{1,0:T(8,128)S(1)}, u32[]{:S(2)}, u32[]{:S(2)}) collective-permute-start(f32[136,128]{1,0:T(8,128)S(1)} %get-tuple-element.71._.refs_1_), channel_id=1, source_target_pairs={{0,1},{1,2},{2,3},{3,7},{7,6},{6,5},{5,4},{4,0},{8,9},{9,10},{10,1... | collective-permute-start | bytes 208904 | tf_op jit(solution)/shard_map/ppermute | solution.py:261
  31.1 5.7 %collective-permute-start.9 = (f32[8,128]{1,0:T(8,128)S(1)}, f32[8,128]{1,0:T(8,128)S(1)}, u32[]{:S(2)}, u32[]{:S(2)}) collective-permute-start(f32[8,128]{1,0:T(8,128)S(1)} %get-tuple-element.85.scaled_rhs.own), channel_id=1, source_target_pairs={{4,0},{8,4},{12,8},{0,12},{5,1},{9,5},{13,9},{1,13},{6,2},{10,6},{... | collective-permute-start | bytes 12296 | tf_op jit(solution)/shard_map/ppermute | solution.py:272
  31.1 5.7 %collective-permute-start.8 = (f32[8,128]{1,0:T(8,128)S(1)}, f32[8,128]{1,0:T(8,128)S(1)}, u32[]{:S(2)}, u32[]{:S(2)}) collective-permute-start(f32[8,128]{1,0:T(8,128)S(1)} %get-tuple-element.85.scaled_rhs.own), channel_id=1, source_target_pairs={{0,4},{4,8},{8,12},{12,0},{1,5},{5,9},{9,13},{13,1},{2,6},{6,10},{... | collective-permute-start | bytes 12296 | tf_op jit(solution)/shard_map/ppermute | solution.py:272
  31.6 5.2 %collective-permute-start.7 = (f32[8,128]{1,0:T(8,128)S(1)}, f32[8,128]{1,0:T(8,128)S(1)}, u32[]{:S(2)}, u32[]{:S(2)}) collective-permute-start(f32[8,128]{1,0:T(8,128)S(1)} %get-tuple-element.85.scaled_rhs.own), channel_id=1, source_target_pairs={{0,16},{16,0},{1,17},{17,1},{2,18},{18,2},{3,19},{19,3},{4,20},{20... | collective-permute-start | bytes 12296 | tf_op jit(solution)/shard_map/ppermute | solution.py:265
  32.5 4.3 %collective-permute-start.6 = (f32[8,128]{1,0:T(8,128)S(1)}, f32[8,128]{1,0:T(8,128)S(1)}, u32[]{:S(2)}, u32[]{:S(2)}) collective-permute-start(f32[8,128]{1,0:T(8,128)S(1)} %get-tuple-element.85.scaled_rhs.own), channel_id=1, source_target_pairs={{1,0},{2,1},{3,2},{7,3},{6,7},{5,6},{4,5},{0,4},{9,8},{10,9},{11,1... | collective-permute-start | bytes 12296 | tf_op jit(solution)/shard_map/ppermute | solution.py:261
  32.8 4.0 %collective-permute-start.5 = (f32[8,128]{1,0:T(8,128)S(1)}, f32[8,128]{1,0:T(8,128)S(1)}, u32[]{:S(2)}, u32[]{:S(2)}) collective-permute-start(f32[8,128]{1,0:T(8,128)S(1)} %get-tuple-element.85.scaled_rhs.own), channel_id=1, source_target_pairs={{0,1},{1,2},{2,3},{3,7},{7,6},{6,5},{5,4},{4,0},{8,9},{9,10},{10,1... | collective-permute-start | bytes 12296 | tf_op jit(solution)/shard_map/ppermute | solution.py:261
  37.5 3.8 %collective-permute-start.14 = (f32[8,128]{1,0:T(8,128)S(1)}, f32[8,128]{1,0:T(8,128)S(1)}, u32[]{:S(2)}, u32[]{:S(2)}) collective-permute-start(f32[8,128]{1,0:T(8,128)S(1)} %shard_map.58.own), channel_id=1, source_target_pairs={{4,0},{8,4},{12,8},{0,12},{5,1},{9,5},{13,9},{1,13},{6,2},{10,6},{... | collective-permute-start | bytes 12296 | tf_op jit(solution)/shard_map/ppermute | solution.py:272
  38.1 3.6 %collective-permute-start.12 = (f32[8,128]{1,0:T(8,128)S(1)}, f32[8,128]{1,0:T(8,128)S(1)}, u32[]{:S(2)}, u32[]{:S(2)}) collective-permute-start(f32[8,128]{1,0:T(8,128)S(1)} %shard_map.58.own), channel_id=1, source_target_pairs={{0,16},{16,0},{1,17},{17,1},{2,18},{18,2},{3,19},{19,3},{4,20},{20... | collective-permute-start | bytes 12296 | tf_op jit(solution)/shard_map/ppermute | solution.py:265
  43.6 4.5 %collective-permute-start.19 = (f32[8,128]{1,0:T(8,128)S(1)}, f32[8,128]{1,0:T(8,128)S(1)}, u32[]{:S(2)}, u32[]{:S(2)}) collective-permute-start(f32[8,128]{1,0:T(8,128)S(1)} %shard_map.59.own), channel_id=1, source_target_pairs={{4,0},{8,4},{12,8},{0,12},{5,1},{9,5},{13,9},{1,13},{6,2},{10,6},{... | collective-permute-start | bytes 12296 | tf_op jit(solution)/shard_map/ppermute | solution.py:272
  45.3 3.6 %collective-permute-start.17 = (f32[8,128]{1,0:T(8,128)S(1)}, f32[8,128]{1,0:T(8,128)S(1)}, u32[]{:S(2)}, u32[]{:S(2)}) collective-permute-start(f32[8,128]{1,0:T(8,128)S(1)} %shard_map.59.own), channel_id=1, source_target_pairs={{0,16},{16,0},{1,17},{17,1},{2,18},{18,2},{3,19},{19,3},{4,20},{20... | collective-permute-start | bytes 12296 | tf_op jit(solution)/shard_map/ppermute | solution.py:265
  50.4 4.9 %collective-permute-start.24 = (f32[8,128]{1,0:T(8,128)S(1)}, f32[8,128]{1,0:T(8,128)S(1)}, u32[]{:S(2)}, u32[]{:S(2)}) collective-permute-start(f32[8,128]{1,0:T(8,128)S(1)} %shard_map.60.own), channel_id=1, source_target_pairs={{4,0},{8,4},{12,8},{0,12},{5,1},{9,5},{13,9},{1,13},{6,2},{10,6},{... | collective-permute-start | bytes 12296 | tf_op jit(solution)/shard_map/ppermute | solution.py:272
  52.1 3.6 %collective-permute-start.22 = (f32[8,128]{1,0:T(8,128)S(1)}, f32[8,128]{1,0:T(8,128)S(1)}, u32[]{:S(2)}, u32[]{:S(2)}) collective-permute-start(f32[8,128]{1,0:T(8,128)S(1)} %shard_map.60.own), channel_id=1, source_target_pairs={{0,16},{16,0},{1,17},{17,1},{2,18},{18,2},{3,19},{19,3},{4,20},{20... | collective-permute-start | bytes 12296 | tf_op jit(solution)/shard_map/ppermute | solution.py:265
  57.6 4.1 %collective-permute-start.29 = (f32[8,128]{1,0:T(8,128)S(1)}, f32[8,128]{1,0:T(8,128)S(1)}, u32[]{:S(2)}, u32[]{:S(2)}) collective-permute-start(f32[8,128]{1,0:T(8,128)S(1)} %shard_map.61.own), channel_id=1, source_target_pairs={{4,0},{8,4},{12,8},{0,12},{5,1},{9,5},{13,9},{1,13},{6,2},{10,6},{... | collective-permute-start | bytes 12296 | tf_op jit(solution)/shard_map/ppermute | solution.py:272
  58.8 3.6 %collective-permute-start.27 = (f32[8,128]{1,0:T(8,128)S(1)}, f32[8,128]{1,0:T(8,128)S(1)}, u32[]{:S(2)}, u32[]{:S(2)}) collective-permute-start(f32[8,128]{1,0:T(8,128)S(1)} %shard_map.61.own), channel_id=1, source_target_pairs={{0,16},{16,0},{1,17},{17,1},{2,18},{18,2},{3,19},{19,3},{4,20},{20... | collective-permute-start | bytes 12296 | tf_op jit(solution)/shard_map/ppermute | solution.py:265
  64.0 4.4 %collective-permute-start.34 = (f32[8,128]{1,0:T(8,128)S(1)}, f32[8,128]{1,0:T(8,128)S(1)}, u32[]{:S(2)}, u32[]{:S(2)}) collective-permute-start(f32[8,128]{1,0:T(8,128)S(1)} %shard_map.62.own), channel_id=1, source_target_pairs={{4,0},{8,4},{12,8},{0,12},{5,1},{9,5},{13,9},{1,13},{6,2},{10,6},{... | collective-permute-start | bytes 12296 | tf_op jit(solution)/shard_map/ppermute | solution.py:272
  65.2 3.6 %collective-permute-start.32 = (f32[8,128]{1,0:T(8,128)S(1)}, f32[8,128]{1,0:T(8,128)S(1)}, u32[]{:S(2)}, u32[]{:S(2)}) collective-permute-start(f32[8,128]{1,0:T(8,128)S(1)} %shard_map.62.own), channel_id=1, source_target_pairs={{0,16},{16,0},{1,17},{17,1},{2,18},{18,2},{3,19},{19,3},{4,20},{20... | collective-permute-start | bytes 12296 | tf_op jit(solution)/shard_map/ppermute | solution.py:265
  70.6 4.1 %collective-permute-start.39 = (f32[8,128]{1,0:T(8,128)S(1)}, f32[8,128]{1,0:T(8,128)S(1)}, u32[]{:S(2)}, u32[]{:S(2)}) collective-permute-start(f32[8,128]{1,0:T(8,128)S(1)} %shard_map.63.own), channel_id=1, source_target_pairs={{4,0},{8,4},{12,8},{0,12},{5,1},{9,5},{13,9},{1,13},{6,2},{10,6},{... | collective-permute-start | bytes 12296 | tf_op jit(solution)/shard_map/ppermute | solution.py:272
  77.7 4.7 %collective-permute-start.40 = (f32[4,32,128]{2,1,0:T(8,128)S(1)}, f32[4,32,128]{2,1,0:T(8,128)S(1)}, u32[]{:S(2)}, u32[]{:S(2)}) collective-permute-start(f32[4,32,128]{2,1,0:T(8,128)S(1)} %shard_map.66), channel_id=1, source_target_pairs={{0,16},{16,0},{1,17},{17,1},{2,18},{18,2},{3,19},{19,3},{4,20},{20... | collective-permute-start | bytes 196616 | tf_op jit(solution)/shard_map/ppermute | solution.py:265
  83.0 4.3 %collective-permute-start.42 = (f32[128,128]{1,0:T(8,128)S(1)}, f32[128,128]{1,0:T(8,128)S(1)}, u32[]{:S(2)}, u32[]{:S(2)}) collective-permute-start(f32[128,128]{1,0:T(8,128)S(1)} %get-tuple-element.91), channel_id=1, source_target_pairs={{0,16},{1,17},{2,18},{3,19},{4,8},{5,9},{6,10},{7,11},{8,4},{9,5},... | collective-permute-start | bytes 196616 | tf_op jit(solution)/shard_map/ppermute | solution.py:261
  89.8 3.8 %collective-permute-start.44 = (f32[40,128]{1,0:T(8,128)S(1)}, f32[40,128]{1,0:T(8,128)S(1)}, u32[]{:S(2)}, u32[]{:S(2)}) collective-permute-start(f32[40,128]{1,0:T(8,128)S(1)} %get-tuple-element.94), channel_id=1, source_target_pairs={{1,0},{2,1},{3,2},{7,3},{6,7},{5,6},{4,5},{0,4},{9,8},{10,9},{11,1... | collective-permute-start | bytes 61448 | tf_op jit(solution)/shard_map/ppermute | solution.py:261
  (21 other events, 66.4 us)

commit v6 on v5

--- a/solution.py
+++ b/solution.py
@@ -18,23 +18,31 @@
 OMEGA_COARSE = 0.7
 F32 = jnp.float32
 BF16 = jnp.bfloat16
-SMEM = pl.BlockSpec(memory_space=pltpu.SMEM)
 VMEM = pl.BlockSpec(memory_space=pltpu.VMEM)
 IX, PARITY, X_LOW, X_HIGH, Y_LOW, Y_HIGH, Z_LOW, Z_HIGH = range(8)
 
 
+def places():
+    (ix, n_x), (iy, n_y), (iz, n_z) = ((lax.axis_index(a), lax.axis_size(a)) for a in ("gx", "gy", "gz"))
+    flags = [ix, iy % 2, ix > 0, ix < n_x - 1, iy > 0, iy < n_y - 1, iz > 0, iz < n_z - 1]
+    return [jnp.asarray(flag, jnp.int32) for flag in flags]
+
+
 def call(kernel, outs, scratch=(), limit=16, flops=10**6, in_specs=None, aliases=None):
-    def run(flags, *arrays):
+    def placed(*refs):
+        kernel(places(), *refs)
+
+    def run(*arrays):
         return pl.pallas_call(
-            kernel,
+            placed,
             out_shape=outs,
-            in_specs=[SMEM] + (in_specs or [VMEM] * len(arrays)),
+            in_specs=in_specs or [VMEM] * len(arrays),
             out_specs=jax.tree.map(lambda _: VMEM, outs),
             scratch_shapes=list(scratch),
             input_output_aliases=aliases or {},
             compiler_params=pltpu.CompilerParams(vmem_limit_bytes=limit * 2**20),
             cost_estimate=pl.CostEstimate(flops=flops, bytes_accessed=10**5, transcendentals=0),
-        )(flags, *arrays)
+        )(*arrays)
 
     return run
 
@@ -279,18 +287,18 @@
         return self.send(forth, self.snake), self.send(back, self.back(self.snake))
 
 
-def widened(links, flags, widths, arrays, from_x, beside_y=None, beside_z=None):
+def widened(links, widths, arrays, from_x, beside_y=None, beside_z=None):
     fields, labels = len(widths), len(arrays) - len(widths)
     nx, ny, nz = arrays[0].shape
     frame = Frame(nx, ny)
     rows = fields * frame.wide * HALO + labels * ny // 2
     sends = call(functools.partial(pack_y_kernel, widths, labels), [shaped(rows, nz)] * 2)(
-        flags, *arrays, from_x[0], from_x[-1]
+        *arrays, from_x[0], from_x[-1]
     )
     size = fields * frame.tall
     framed = call(
         functools.partial(frame_kernel, widths, labels), [shaped(fields, *frame.main)] + [shaped(size, nz)] * 2
-    )(flags, *arrays[:fields], from_x[0], from_x[-1], sends[0])
+    )(*arrays[:fields], from_x[0], from_x[-1], sends[0])
     work = beside_y(sends[0]) if beside_y else ()
     from_y = links.y(*sends)
     if work:
@@ -300,8 +308,8 @@
         functools.partial(pack_z_kernel, widths, labels),
         [shaped(fields, *frame.main)] + [shaped(rows, nz)] * 2,
         [pltpu.VMEM((size, nz), F32)] * 2,
-        aliases={1: 0},
-    )(flags, *framed, *from_y, *arrays[fields:])
+        aliases={0: 0},
+    )(*framed, *from_y, *arrays[fields:])
     if beside_z:
         beside_z(wide, sends[0])
     return (wide, *links.z(*sends)), from_y
@@ -780,11 +788,7 @@
     nx, ny, nz = right_side.shape
     frame = Frame(nx, ny)
     nb = nx // 2
-    ix, iy, iz = (lax.axis_index(a) for a in ("gx", "gy", "gz"))
-    n_x, n_y, n_z = links.sizes
-    flags = jnp.stack(
-        [ix, iy % 2, ix > 0, ix < n_x - 1, iy > 0, iy < n_y - 1, iz > 0, iz < n_z - 1]
-    ).astype(jnp.int32)
+    n_x = links.sizes[0]
     arrays = (conductance, right_side, absorption, block_agg)
     n_send = 1 if n_x == 2 else 2
     pinned = [pltpu.with_memory_space_constraint(a, pltpu.HBM) for a in arrays]
@@ -794,19 +798,19 @@
         [shaped(sum(WIDTHS) + 1, ny, nz)] * n_send,
         [pltpu.VMEM((n_send, ny // 2, nz // 2), jnp.int32), pltpu.SemaphoreType.DMA((n_send * 4,))],
         in_specs=[hbm] * 4,
-    )(flags, *pinned)
+    )(*pinned)
     arrays = call(
         load_kernel,
         [jax.ShapeDtypeStruct(a.shape, a.dtype) for a in arrays],
         [pltpu.SemaphoreType.DMA((4,))],
         in_specs=[hbm] * 4 + [VMEM],
-    )(flags, *pinned, x_sends[0])
+    )(*pinned, x_sends[0])
     blocks = (nb, SUB, LANES)
     outs = [shaped(*blocks), shaped(3, *blocks), shaped(3, *blocks), shaped(*blocks), shaped(6, SUB, LANES)]
     outs += [jax.ShapeDtypeStruct((nb, ny // 2, LANES), jnp.int32)]
     scratch = [pltpu.VMEM((17, ny, LANES), F32), pltpu.VMEM((2, ny // 2, LANES), F32)]
     pair = [pltpu.VMEM((AGG, SUB * LANES), BF16), pltpu.VMEM((2 * AGG, SUB * LANES), BF16)]
-    *rows, face_label, lift = call(blocks_kernel, outs, scratch)(flags, arrays[0], arrays[2], arrays[3], x_sends[0])
+    *rows, face_label, lift = call(blocks_kernel, outs, scratch)(arrays[0], arrays[2], arrays[3], x_sends[0])
     block_label = rows[0]
     bounds = (0, nb // 6, nb * 7 // 12, nb)
     parts = []
@@ -816,7 +820,7 @@
         if p == 2:
             outs = [jax.ShapeDtypeStruct((AGG, 2 * AGG), BF16), shaped(SUB, AGG)]
         kernel = functools.partial(own_kernel, bounds[p], bounds[p + 1], nb)
-        parts.append(call(kernel, outs, pair * 2)(flags, *rows, *(parts[-1] if p else ()), sent))
+        parts.append(call(kernel, outs, pair * 2)(*rows, *(parts[-1] if p else ()), sent))
         return parts[-1]
 
     first = own_part(0, x_sends[0])
@@ -826,18 +830,18 @@
 
     def beside_z(wide, sent):
         fields.extend(
-            call(fields_kernel, [shaped(*frame.main)] * 4 + [shaped(frame.tall, nz)], limit=24)(flags, wide, sent)
+            call(fields_kernel, [shaped(*frame.main)] * 4 + [shaped(frame.tall, nz)], limit=24)(wide, sent)
         )
         own_part(2, sent)
 
-    halo, from_y = widened(links, flags, WIDTHS, arrays, from_x, lambda sent: own_part(1, sent), beside_z)
+    halo, from_y = widened(links, WIDTHS, arrays, from_x, lambda sent: own_part(1, sent), beside_z)
     own_tile, inner_diag = parts[-1]
     outs = [shaped(*frame.main)] * 2 + [shaped(*frame.ends)] * 6 + [shaped(nx, ny, nz)]
     outs += [shaped(6, SUB, LANES)] * 2 + [shaped(SUB, AGG)] * 2
     scratch = [pltpu.VMEM(frame.main, F32), pltpu.VMEM(frame.ends, F32), pltpu.VMEM((nx, frame.rows, LANES), F32)]
     scratch += [pltpu.VMEM(frame.main, F32), pltpu.VMEM(blocks, F32)]
     got = call(fine_kernel, outs, scratch, limit=28)(
-        flags, *halo, from_x[0], from_x[-1], *from_y, *fields, block_label, face_label, inner_diag
+        *halo, from_x[0], from_x[-1], *from_y, *fields, block_label, face_label, inner_diag
     )
     fields, pre = (*fields[:3], *got[:8]), got[8]
     face_near, face_weight, scaled_rhs, scale = got[9:]
@@ -845,16 +849,16 @@
         functools.partial(faces_kernel, n_x),
         jax.ShapeDtypeStruct(((n_send + 5) * AGG, 2 * AGG), BF16),
         pair * 2,
-    )(flags, own_tile, face_label, face_near, face_weight)
+    )(own_tile, face_label, face_near, face_weight)
     coarse = scaled_rhs
     for _ in range(KC - 1):
-        coarse = call(turn_kernel, shaped(SUB, AGG))(flags, tiles, scaled_rhs, scale, coarse, *links.near(coarse))
-    x_sends = call(functools.partial(send_kernel, n_x), [shaped(HALO, ny, nz)] * n_send)(flags, pre, lift, coarse)
+        coarse = call(turn_kernel, shaped(SUB, AGG))(tiles, scaled_rhs, scale, coarse, *links.near(coarse))
+    x_sends = call(functools.partial(send_kernel, n_x), [shaped(HALO, ny, nz)] * n_send)(pre, lift, coarse)
     from_x = links.x(x_sends)
-    corrected = call(correct_kernel, shaped(nx, ny, nz))(flags, pre, lift, coarse)
-    halo, _ = widened(links, flags, (HALO,), (corrected,), from_x)
+    corrected = call(correct_kernel, shaped(nx, ny, nz))(pre, lift, coarse)
+    halo, _ = widened(links, (HALO,), (corrected,), from_x)
     scratch = [pltpu.VMEM(frame.main, F32)] * 2 + [pltpu.VMEM(frame.ends, F32)] * 2
-    return call(post_kernel, shaped(nx, ny, nz), scratch, limit=24)(flags, *halo, *fields)
+    return call(post_kernel, shaped(nx, ny, nz), scratch, limit=24)(*halo, *fields)
 
 
 def solution(mesh):

time: 99.5 us -> 89.5 us (0.90)
  Pallas kernels: 40.5 us -> 26.6 us
  waiting for transfers between devices: 18.3 us -> 21.8 us
    pallas_call x25, Pallas kernels: 40.5 us -> 26.6 us  [run(): pl.pallas_call(placed, out_shape=outs, in_specs=in_specs or [VMEM] * len(...]
    ppermute x22, waiting for transfers between devices: 12.1 us -> 13.8 us  [send(): return lax.ppermute(values, ('gx', 'gy', 'gz'), pairs)]
    ppermute x7, waiting for transfers between devices: 0.29 us -> 1.4 us  [near(): lax.ppermute(values, 'gy', ring)]
  transfers between devices with their start and end apart: 45 -> 45, of which waited for: 18 -> 19; matrix products, arithmetic and copies ran while one was open for 0% -> 0% of each run, Pallas kernels for 19% -> 15%
where the time goes in v6:
time: 89.5 us; the launch traced here: 89.3 us
  starting transfers between devices  40.7 us (45%)
  Pallas kernels  26.6 us (30%)
  waiting for transfers between devices  21.8 us (24%)
    pallas_call x25, Pallas kernels, run(): pl.pallas_call(placed, out_shape=outs, in_specs=in_specs or [VMEM] * len(...  26.6 us
    ppermute x22, starting transfers between devices, send(): return lax.ppermute(values, ('gx', 'gy', 'gz'), pairs)  21 us
    ppermute x22, waiting for transfers between devices, send(): return lax.ppermute(values, ('gx', 'gy', 'gz'), pairs)  13.8 us
    ppermute x9, starting transfers between devices, x(): return (lax.ppermute(sends[0], 'gx', self.ring_x),)  11.5 us
    ppermute x7, starting transfers between devices, near(): lax.ppermute(values, 'gy', self.back(ring))  7.62 us
    ppermute x9, waiting for transfers between devices, x(): return (lax.ppermute(sends[0], 'gx', self.ring_x),)  6.67 us
  transfers between devices with their start and end apart: 45, of which 19 were waited for; matrix products, arithmetic and copies ran while one was open for 0% of the time, Pallas kernels for 15%

profile of v6, /device:TPU:0, one launch (start us, length us, event | category | flops | bytes accessed | tf_op | source)
XLA Modules:
  0.0 89.3 jit_solution(6832605548902517088)
XLA Ops:
  0.9 3.0 %collective-permute-start = (f32[11,32,128]{2,1,0:T(8,128)S(1)}, f32[11,32,128]{2,1,0:T(8,128)S(1)}, u32[]{:S(2)}, u32[]{:S(2)}) collective-permute-start(f32[11,32,128]{2,1,0:T(8,128)S(1)} %shard_map.46.refs_4_.refs_3_), channel_id=1, source_target_pairs={{0,16},{16,0},{1,17},{17,1},{2,18},{18,2},{3,19},{19,3},{4,20},{20... | collective-permute-start | bytes 540680 | tf_op jit(solution)/shard_map/ppermute | solution.py:273
  5.2 1.6 %shard_map.48 = (f32[12,8,128]{2,1,0:T(8,128)S(1)}, f32[3,12,8,128]{3,2,1,0:T(8,128)S(1)}, f32[3,12,8,128]{3,2,1,0:T(8,128)S(1)}, f32[12,8,128]{2,1,0:T(8,128)S(...) custom-call(f32[24,32,128]{2,1,0:T(8,128)S(1)} %get-tuple-element.54.refs_0_, ...), custom_call_target="tpu_custom_call" | custom-call | flops 1000000 | bytes 100000 | tf_op jit(solution)/shard_map/pallas_call | solution.py:36
  8.6 1.8 %collective-permute-start.2 = (f32[400,128]{1,0:T(8,128)S(1)}, f32[400,128]{1,0:T(8,128)S(1)}, u32[]{:S(2)}, u32[]{:S(2)}) collective-permute-start(f32[400,128]{1,0:T(8,128)S(1)} %get-tuple-element.67), channel_id=1, source_target_pairs={{0,16},{1,17},{2,18},{3,19},{4,8},{5,9},{6,10},{7,11},{8,4},{9,5},... | collective-permute-start | bytes 614408 | tf_op jit(solution)/shard_map/ppermute | solution.py:269
  10.5 2.4 %shard_map.52.refs_4_ = f32[128,256]{1,0:T(8,128)S(1)} custom-call(f32[12,8,128]{2,1,0:T(8,128)S(1)} %get-tuple-element.58.refs_0_.refs_12_, f32[3,12,8,128]{3,2,1,0:T(8,128)S(1)} %get-tuple-element.59.refs_1_, f32[3,12,8,128]{3,2,1,0:T(8,128)S(1)} %get-tuple-element.60.refs_2_, f32[12,8,128]{2,1,0:T(8,128)S(1)} %get-tuple-element.61.refs_3_, ...), custom_call_target="tpu_custom_call" | custom-call | flops 1000000 | bytes 100000 | tf_op jit(solution)/shard_map/pallas_call | solution.py:36
  15.1 2.0 %collective-permute-start.3 = (f32[136,128]{1,0:T(8,128)S(1)}, f32[136,128]{1,0:T(8,128)S(1)}, u32[]{:S(2)}, u32[]{:S(2)}) collective-permute-start(f32[136,128]{1,0:T(8,128)S(1)} %get-tuple-element.71.refs_1_.refs_5_), channel_id=1, source_target_pairs={{0,1},{1,2},{2,3},{3,7},{7,6},{6,5},{5,4},{4,0},{8,9},{9,10},{10,1... | collective-permute-start | bytes 208904 | tf_op jit(solution)/shard_map/ppermute | solution.py:269
  17.1 3.2 %shard_map.55 = (bf16[128,256]{1,0:T(8,128)(2,1)S(1)}, f32[8,128]{1,0:T(8,128)S(1)}) custom-call(f32[12,8,128]{2,1,0:T(8,128)S(1)} %get-tuple-element.58.refs_0_.refs_12_, f32[3,12,8,128]{3,2,1,0:T(8,128)S(1)} %get-tuple-element.59.refs_1_, f32[3,12,8,128]{3,2,1,0:T(8,128)S(1)} %get-tuple-element.60.refs_2_, f32[12,8,128]{2,1,0:T(8,128)S(1)} %get-tuple-element.61.refs_3_, ...), custom_call_target="tpu_custom_call" | custom-call | flops 1000000 | bytes 100000 | tf_op jit(solution)/shard_map/pallas_call | solution.py:36
  21.7 5.0 %shard_map.56 = (f32[32,56,128]{2,1,0:T(8,128)S(1)}, f32[32,56,128]{2,1,0:T(8,128)S(1)}, f32[2,56,128]{2,1,0:T(8,128)S(1)}, f32[2,56,128]{2,1,0:T(8,128)S(1)}, f...) custom-call(f32[3,32,56,128]{3,2,1,0:T(8,128)S(1)} %get-tuple-elemen, ...), custom_call_target="tpu_custom_call" | custom-call | flops 1000000 | bytes 100000 | tf_op jit(solution)/shard_map/pallas_call | solution.py:36
  27.3 1.7 %collective-permute-start.7 = (f32[8,128]{1,0:T(8,128)S(1)}, f32[8,128]{1,0:T(8,128)S(1)}, u32[]{:S(2)}, u32[]{:S(2)}) collective-permute-start(f32[8,128]{1,0:T(8,128)S(1)} %get-tuple-element.85.refs_1_.refs_3_), channel_id=1, source_target_pairs={{0,16},{16,0},{1,17},{17,1},{2,18},{18,2},{3,19},{19,3},{4,20},{20... | collective-permute-start | bytes 12296 | tf_op jit(solution)/shard_map/ppermute | solution.py:273
  29.3 1.7 %collective-permute-start.5 = (f32[8,128]{1,0:T(8,128)S(1)}, f32[8,128]{1,0:T(8,128)S(1)}, u32[]{:S(2)}, u32[]{:S(2)}) collective-permute-start(f32[8,128]{1,0:T(8,128)S(1)} %get-tuple-element.85.refs_1_.refs_3_), channel_id=1, source_target_pairs={{0,1},{1,2},{2,3},{3,7},{7,6},{6,5},{5,4},{4,0},{8,9},{9,10},{10,1... | collective-permute-start | bytes 12296 | tf_op jit(solution)/shard_map/ppermute | solution.py:269
  31.0 1.7 %shard_map.57.refs_0_ = bf16[768,256]{1,0:T(8,128)(2,1)S(1)} custom-call(bf16[128,256]{1,0:T(8,128)(2,1)S(1)} %get-tuple-element.82.refs_0_, f32[6,8,128]{2,1,0:T(8,128)S(1)} %get-tuple-element.78.refs_13_.refs_1_, f32[6,8,128]{2,1,0:T(8,128)S(1)} %get-tuple-element.83.refs_2_, f32[6,8,128]{2,1,0:T(8,128)S(1)} %get-tuple-element.84.refs_3_), custom_call_target="tpu_custom_call" | custom-call | flops 1000000 | bytes 100000 | tf_op jit(solution)/shard_map/pallas_call | solution.py:36
  38.3 1.7 %collective-permute-start.19 = (f32[8,128]{1,0:T(8,128)S(1)}, f32[8,128]{1,0:T(8,128)S(1)}, u32[]{:S(2)}, u32[]{:S(2)}) collective-permute-start(f32[8,128]{1,0:T(8,128)S(1)} %shard_map.59.refs_3_), channel_id=1, source_target_pairs={{4,0},{8,4},{12,8},{0,12},{5,1},{9,5},{13,9},{1,13},{6,2},{10,6},{... | collective-permute-start | bytes 12296 | tf_op jit(solution)/shard_map/ppermute | solution.py:280
  40.0 1.5 %collective-permute-start.17 = (f32[8,128]{1,0:T(8,128)S(1)}, f32[8,128]{1,0:T(8,128)S(1)}, u32[]{:S(2)}, u32[]{:S(2)}) collective-permute-start(f32[8,128]{1,0:T(8,128)S(1)} %shard_map.59.refs_3_), channel_id=1, source_target_pairs={{0,16},{16,0},{1,17},{17,1},{2,18},{18,2},{3,19},{19,3},{4,20},{20... | collective-permute-start | bytes 12296 | tf_op jit(solution)/shard_map/ppermute | solution.py:273
  43.6 1.5 %collective-permute-done.16.refs_5_ = f32[8,128]{1,0:T(8,128)S(1)} collective-permute-done((f32[8,128]{1,0:T(8,128)S(1)}, f32[8,128]{1,0:T(8,128)S(1)}, u32[]{:S(2)}, u32[]{:S(2)}) %collective-permute-start.16) | collective-permute-done | bytes 4128 | tf_op jit(solution)/shard_map/ppermute | solution.py:269
  50.7 1.6 %collective-permute-start.29 = (f32[8,128]{1,0:T(8,128)S(1)}, f32[8,128]{1,0:T(8,128)S(1)}, u32[]{:S(2)}, u32[]{:S(2)}) collective-permute-start(f32[8,128]{1,0:T(8,128)S(1)} %shard_map.61.refs_3_), channel_id=1, source_target_pairs={{4,0},{8,4},{12,8},{0,12},{5,1},{9,5},{13,9},{1,13},{6,2},{10,6},{... | collective-permute-start | bytes 12296 | tf_op jit(solution)/shard_map/ppermute | solution.py:280
  52.4 1.6 %collective-permute-start.27 = (f32[8,128]{1,0:T(8,128)S(1)}, f32[8,128]{1,0:T(8,128)S(1)}, u32[]{:S(2)}, u32[]{:S(2)}) collective-permute-start(f32[8,128]{1,0:T(8,128)S(1)} %shard_map.61.refs_3_), channel_id=1, source_target_pairs={{0,16},{16,0},{1,17},{17,1},{2,18},{18,2},{3,19},{19,3},{4,20},{20... | collective-permute-start | bytes 12296 | tf_op jit(solution)/shard_map/ppermute | solution.py:273
  56.0 1.6 %collective-permute-done.26.refs_5_ = f32[8,128]{1,0:T(8,128)S(1)} collective-permute-done((f32[8,128]{1,0:T(8,128)S(1)}, f32[8,128]{1,0:T(8,128)S(1)}, u32[]{:S(2)}, u32[]{:S(2)}) %collective-permute-start.26) | collective-permute-done | bytes 4128 | tf_op jit(solution)/shard_map/ppermute | solution.py:269
  64.1 1.6 %collective-permute-start.37 = (f32[8,128]{1,0:T(8,128)S(1)}, f32[8,128]{1,0:T(8,128)S(1)}, u32[]{:S(2)}, u32[]{:S(2)}) collective-permute-start(f32[8,128]{1,0:T(8,128)S(1)} %shard_map.63.refs_3_), channel_id=1, source_target_pairs={{0,16},{16,0},{1,17},{17,1},{2,18},{18,2},{3,19},{19,3},{4,20},{20... | collective-permute-start | bytes 12296 | tf_op jit(solution)/shard_map/ppermute | solution.py:273
  67.8 1.6 %collective-permute-done.36.refs_5_ = f32[8,128]{1,0:T(8,128)S(1)} collective-permute-done((f32[8,128]{1,0:T(8,128)S(1)}, f32[8,128]{1,0:T(8,128)S(1)}, u32[]{:S(2)}, u32[]{:S(2)}) %collective-permute-start.36) | collective-permute-done | bytes 4128 | tf_op jit(solution)/shard_map/ppermute | solution.py:269
  70.3 4.1 %collective-permute-done.40.refs_1_.refs_2_ = f32[4,32,128]{2,1,0:T(8,128)S(1)} collective-permute-done((f32[4,32,128]{2,1,0:T(8,128)S(1)}, f32[4,32,128]{2,1,0:T(8,128)S(1)}, u32[]{:S(2)}, u32[]{:S(2)}) %collective-permute-start.40) | collective-permute-done | bytes 65568 | tf_op jit(solution)/shard_map/ppermute | solution.py:273
  75.9 2.8 %collective-permute-done.42.refs_4_ = f32[128,128]{1,0:T(8,128)S(1)} collective-permute-done((f32[128,128]{1,0:T(8,128)S(1)}, f32[128,128]{1,0:T(8,128)S(1)}, u32[]{:S(2)}, u32[]{:S(2)}) %collective-permute-start.42) | collective-permute-done | bytes 65568 | tf_op jit(solution)/shard_map/ppermute | solution.py:269
  79.0 1.6 %collective-permute-start.43 = (f32[40,128]{1,0:T(8,128)S(1)}, f32[40,128]{1,0:T(8,128)S(1)}, u32[]{:S(2)}, u32[]{:S(2)}) collective-permute-start(f32[40,128]{1,0:T(8,128)S(1)} %get-tuple-element.93), channel_id=1, source_target_pairs={{0,1},{1,2},{2,3},{3,7},{7,6},{6,5},{5,4},{4,0},{8,9},{9,10},{10,1... | collective-permute-start | bytes 61448 | tf_op jit(solution)/shard_map/ppermute | solution.py:269
  80.6 1.5 %collective-permute-done.43.refs_1_ = f32[40,128]{1,0:T(8,128)S(1)} collective-permute-done((f32[40,128]{1,0:T(8,128)S(1)}, f32[40,128]{1,0:T(8,128)S(1)}, u32[]{:S(2)}, u32[]{:S(2)}) %collective-permute-start.43) | collective-permute-done | bytes 20512 | tf_op jit(solution)/shard_map/ppermute | solution.py:269
  82.0 2.3 %collective-permute-done.44.refs_2_ = f32[40,128]{1,0:T(8,128)S(1)} collective-permute-done((f32[40,128]{1,0:T(8,128)S(1)}, f32[40,128]{1,0:T(8,128)S(1)}, u32[]{:S(2)}, u32[]{:S(2)}) %collective-permute-start.44) | collective-permute-done | bytes 20512 | tf_op jit(solution)/shard_map/ppermute | solution.py:269
  84.3 5.0 %shard_map.70 = f32[24,32,128]{2,1,0:T(8,128)} custom-call(f32[1,32,56,128]{3,2,1,0:T(8,128)S(1)} %get-tuple-element.92.refs_0_, f32[40,128]{1,0:T(8,128)S(1)} %collective-permute-done.43.refs_1_, f32[40,128]{1,0:T(8,128)S(1)} %collective-permute-done.44.refs_2_, f32[32,56,128]{2,1,0:T(8,128)S(1)} %get-tuple-element.73.refs_7_.refs_3_, ...), custom_call_target="tpu_custom_call" | custom-call | flops 1000000 | bytes 100000 | tf_op jit(solution)/shard_map/pallas_call | solution.py:36
  (91 shorter events, 35.0 us)
Async XLA Ops:
  0.9 7.6 %collective-permute-start = (f32[11,32,128]{2,1,0:T(8,128)S(1)}, f32[11,32,128]{2,1,0:T(8,128)S(1)}, u32[]{:S(2)}, u32[]{:S(2)}) collective-permute-start(f32[11,32,128]{2,1,0:T(8,128)S(1)} %shard_map.46.refs_4_.refs_3_), channel_id=1, source_target_pairs={{0,16},{16,0},{1,17},{17,1},{2,18},{18,2},{3,19},{19,3},{4,20},{20... | collective-permute-start | bytes 540680 | tf_op jit(solution)/shard_map/ppermute | solution.py:273
  8.6 5.8 %collective-permute-start.2 = (f32[400,128]{1,0:T(8,128)S(1)}, f32[400,128]{1,0:T(8,128)S(1)}, u32[]{:S(2)}, u32[]{:S(2)}) collective-permute-start(f32[400,128]{1,0:T(8,128)S(1)} %get-tuple-element.67), channel_id=1, source_target_pairs={{0,16},{1,17},{2,18},{3,19},{4,8},{5,9},{6,10},{7,11},{8,4},{9,5},... | collective-permute-start | bytes 614408 | tf_op jit(solution)/shard_map/ppermute | solution.py:269
  10.4 4.0 %collective-permute-start.1 = (f32[400,128]{1,0:T(8,128)S(1)}, f32[400,128]{1,0:T(8,128)S(1)}, u32[]{:S(2)}, u32[]{:S(2)}) collective-permute-start(f32[400,128]{1,0:T(8,128)S(1)} %get-tuple-element.63.refs_5_), channel_id=1, source_target_pairs={{0,4},{1,5},{2,6},{3,7},{4,0},{5,1},{6,2},{7,3},{8,12},{9,13},{10,... | collective-permute-start | bytes 614408 | tf_op jit(solution)/shard_map/ppermute | solution.py:269
  15.0 6.7 %collective-permute-start.4 = (f32[136,128]{1,0:T(8,128)S(1)}, f32[136,128]{1,0:T(8,128)S(1)}, u32[]{:S(2)}, u32[]{:S(2)}) collective-permute-start(f32[136,128]{1,0:T(8,128)S(1)} %get-tuple-element.72), channel_id=1, source_target_pairs={{1,0},{2,1},{3,2},{7,3},{6,7},{5,6},{4,5},{0,4},{9,8},{10,9},{11,1... | collective-permute-start | bytes 208904 | tf_op jit(solution)/shard_map/ppermute | solution.py:269
  15.1 6.6 %collective-permute-start.3 = (f32[136,128]{1,0:T(8,128)S(1)}, f32[136,128]{1,0:T(8,128)S(1)}, u32[]{:S(2)}, u32[]{:S(2)}) collective-permute-start(f32[136,128]{1,0:T(8,128)S(1)} %get-tuple-element.71.refs_1_.refs_5_), channel_id=1, source_target_pairs={{0,1},{1,2},{2,3},{3,7},{7,6},{6,5},{5,4},{4,0},{8,9},{9,10},{10,1... | collective-permute-start | bytes 208904 | tf_op jit(solution)/shard_map/ppermute | solution.py:269
  26.7 6.1 %collective-permute-start.9 = (f32[8,128]{1,0:T(8,128)S(1)}, f32[8,128]{1,0:T(8,128)S(1)}, u32[]{:S(2)}, u32[]{:S(2)}) collective-permute-start(f32[8,128]{1,0:T(8,128)S(1)} %get-tuple-element.85.refs_1_.refs_3_), channel_id=1, source_target_pairs={{4,0},{8,4},{12,8},{0,12},{5,1},{9,5},{13,9},{1,13},{6,2},{10,6},{... | collective-permute-start | bytes 12296 | tf_op jit(solution)/shard_map/ppermute | solution.py:280
  26.8 6.0 %collective-permute-start.8 = (f32[8,128]{1,0:T(8,128)S(1)}, f32[8,128]{1,0:T(8,128)S(1)}, u32[]{:S(2)}, u32[]{:S(2)}) collective-permute-start(f32[8,128]{1,0:T(8,128)S(1)} %get-tuple-element.85.refs_1_.refs_3_), channel_id=1, source_target_pairs={{0,4},{4,8},{8,12},{12,0},{1,5},{5,9},{9,13},{13,1},{2,6},{6,10},{... | collective-permute-start | bytes 12296 | tf_op jit(solution)/shard_map/ppermute | solution.py:280
  27.3 5.5 %collective-permute-start.7 = (f32[8,128]{1,0:T(8,128)S(1)}, f32[8,128]{1,0:T(8,128)S(1)}, u32[]{:S(2)}, u32[]{:S(2)}) collective-permute-start(f32[8,128]{1,0:T(8,128)S(1)} %get-tuple-element.85.refs_1_.refs_3_), channel_id=1, source_target_pairs={{0,16},{16,0},{1,17},{17,1},{2,18},{18,2},{3,19},{19,3},{4,20},{20... | collective-permute-start | bytes 12296 | tf_op jit(solution)/shard_map/ppermute | solution.py:273
  29.0 3.8 %collective-permute-start.6 = (f32[8,128]{1,0:T(8,128)S(1)}, f32[8,128]{1,0:T(8,128)S(1)}, u32[]{:S(2)}, u32[]{:S(2)}) collective-permute-start(f32[8,128]{1,0:T(8,128)S(1)} %get-tuple-element.85.refs_1_.refs_3_), channel_id=1, source_target_pairs={{1,0},{2,1},{3,2},{7,3},{6,7},{5,6},{4,5},{0,4},{9,8},{10,9},{11,1... | collective-permute-start | bytes 12296 | tf_op jit(solution)/shard_map/ppermute | solution.py:269
  34.0 3.6 %collective-permute-start.12 = (f32[8,128]{1,0:T(8,128)S(1)}, f32[8,128]{1,0:T(8,128)S(1)}, u32[]{:S(2)}, u32[]{:S(2)}) collective-permute-start(f32[8,128]{1,0:T(8,128)S(1)} %shard_map.58.refs_3_), channel_id=1, source_target_pairs={{0,16},{16,0},{1,17},{17,1},{2,18},{18,2},{3,19},{19,3},{4,20},{20... | collective-permute-start | bytes 12296 | tf_op jit(solution)/shard_map/ppermute | solution.py:273
  34.5 3.6 %collective-permute-start.11 = (f32[8,128]{1,0:T(8,128)S(1)}, f32[8,128]{1,0:T(8,128)S(1)}, u32[]{:S(2)}, u32[]{:S(2)}) collective-permute-start(f32[8,128]{1,0:T(8,128)S(1)} %shard_map.58.refs_3_), channel_id=1, source_target_pairs={{1,0},{2,1},{3,2},{7,3},{6,7},{5,6},{4,5},{0,4},{9,8},{10,9},{11,1... | collective-permute-start | bytes 12296 | tf_op jit(solution)/shard_map/ppermute | solution.py:269
  38.3 5.2 %collective-permute-start.19 = (f32[8,128]{1,0:T(8,128)S(1)}, f32[8,128]{1,0:T(8,128)S(1)}, u32[]{:S(2)}, u32[]{:S(2)}) collective-permute-start(f32[8,128]{1,0:T(8,128)S(1)} %shard_map.59.refs_3_), channel_id=1, source_target_pairs={{4,0},{8,4},{12,8},{0,12},{5,1},{9,5},{13,9},{1,13},{6,2},{10,6},{... | collective-permute-start | bytes 12296 | tf_op jit(solution)/shard_map/ppermute | solution.py:280
  40.0 3.6 %collective-permute-start.17 = (f32[8,128]{1,0:T(8,128)S(1)}, f32[8,128]{1,0:T(8,128)S(1)}, u32[]{:S(2)}, u32[]{:S(2)}) collective-permute-start(f32[8,128]{1,0:T(8,128)S(1)} %shard_map.59.refs_3_), channel_id=1, source_target_pairs={{0,16},{16,0},{1,17},{17,1},{2,18},{18,2},{3,19},{19,3},{4,20},{20... | collective-permute-start | bytes 12296 | tf_op jit(solution)/shard_map/ppermute | solution.py:273
  45.2 3.7 %collective-permute-start.24 = (f32[8,128]{1,0:T(8,128)S(1)}, f32[8,128]{1,0:T(8,128)S(1)}, u32[]{:S(2)}, u32[]{:S(2)}) collective-permute-start(f32[8,128]{1,0:T(8,128)S(1)} %shard_map.60.refs_3_), channel_id=1, source_target_pairs={{4,0},{8,4},{12,8},{0,12},{5,1},{9,5},{13,9},{1,13},{6,2},{10,6},{... | collective-permute-start | bytes 12296 | tf_op jit(solution)/shard_map/ppermute | solution.py:280
  50.7 5.3 %collective-permute-start.29 = (f32[8,128]{1,0:T(8,128)S(1)}, f32[8,128]{1,0:T(8,128)S(1)}, u32[]{:S(2)}, u32[]{:S(2)}) collective-permute-start(f32[8,128]{1,0:T(8,128)S(1)} %shard_map.61.refs_3_), channel_id=1, source_target_pairs={{4,0},{8,4},{12,8},{0,12},{5,1},{9,5},{13,9},{1,13},{6,2},{10,6},{... | collective-permute-start | bytes 12296 | tf_op jit(solution)/shard_map/ppermute | solution.py:280
  52.3 3.7 %collective-permute-start.28 = (f32[8,128]{1,0:T(8,128)S(1)}, f32[8,128]{1,0:T(8,128)S(1)}, u32[]{:S(2)}, u32[]{:S(2)}) collective-permute-start(f32[8,128]{1,0:T(8,128)S(1)} %shard_map.61.refs_3_), channel_id=1, source_target_pairs={{0,4},{4,8},{8,12},{12,0},{1,5},{5,9},{9,13},{13,1},{2,6},{6,10},{... | collective-permute-start | bytes 12296 | tf_op jit(solution)/shard_map/ppermute | solution.py:280
  52.4 3.7 %collective-permute-start.27 = (f32[8,128]{1,0:T(8,128)S(1)}, f32[8,128]{1,0:T(8,128)S(1)}, u32[]{:S(2)}, u32[]{:S(2)}) collective-permute-start(f32[8,128]{1,0:T(8,128)S(1)} %shard_map.61.refs_3_), channel_id=1, source_target_pairs={{0,16},{16,0},{1,17},{17,1},{2,18},{18,2},{3,19},{19,3},{4,20},{20... | collective-permute-start | bytes 12296 | tf_op jit(solution)/shard_map/ppermute | solution.py:273
  62.8 5.0 %collective-permute-start.39 = (f32[8,128]{1,0:T(8,128)S(1)}, f32[8,128]{1,0:T(8,128)S(1)}, u32[]{:S(2)}, u32[]{:S(2)}) collective-permute-start(f32[8,128]{1,0:T(8,128)S(1)} %shard_map.63.refs_3_), channel_id=1, source_target_pairs={{4,0},{8,4},{12,8},{0,12},{5,1},{9,5},{13,9},{1,13},{6,2},{10,6},{... | collective-permute-start | bytes 12296 | tf_op jit(solution)/shard_map/ppermute | solution.py:280
  64.1 3.7 %collective-permute-start.38 = (f32[8,128]{1,0:T(8,128)S(1)}, f32[8,128]{1,0:T(8,128)S(1)}, u32[]{:S(2)}, u32[]{:S(2)}) collective-permute-start(f32[8,128]{1,0:T(8,128)S(1)} %shard_map.63.refs_3_), channel_id=1, source_target_pairs={{0,4},{4,8},{8,12},{12,0},{1,5},{5,9},{9,13},{13,1},{2,6},{6,10},{... | collective-permute-start | bytes 12296 | tf_op jit(solution)/shard_map/ppermute | solution.py:280
  64.1 3.7 %collective-permute-start.37 = (f32[8,128]{1,0:T(8,128)S(1)}, f32[8,128]{1,0:T(8,128)S(1)}, u32[]{:S(2)}, u32[]{:S(2)}) collective-permute-start(f32[8,128]{1,0:T(8,128)S(1)} %shard_map.63.refs_3_), channel_id=1, source_target_pairs={{0,16},{16,0},{1,17},{17,1},{2,18},{18,2},{3,19},{19,3},{4,20},{20... | collective-permute-start | bytes 12296 | tf_op jit(solution)/shard_map/ppermute | solution.py:273
  69.6 4.7 %collective-permute-start.40 = (f32[4,32,128]{2,1,0:T(8,128)S(1)}, f32[4,32,128]{2,1,0:T(8,128)S(1)}, u32[]{:S(2)}, u32[]{:S(2)}) collective-permute-start(f32[4,32,128]{2,1,0:T(8,128)S(1)} %shard_map.66), channel_id=1, source_target_pairs={{0,16},{16,0},{1,17},{17,1},{2,18},{18,2},{3,19},{19,3},{4,20},{20... | collective-permute-start | bytes 196616 | tf_op jit(solution)/shard_map/ppermute | solution.py:273
  74.4 4.3 %collective-permute-start.42 = (f32[128,128]{1,0:T(8,128)S(1)}, f32[128,128]{1,0:T(8,128)S(1)}, u32[]{:S(2)}, u32[]{:S(2)}) collective-permute-start(f32[128,128]{1,0:T(8,128)S(1)} %get-tuple-element.91), channel_id=1, source_target_pairs={{0,16},{1,17},{2,18},{3,19},{4,8},{5,9},{6,10},{7,11},{8,4},{9,5},... | collective-permute-start | bytes 196616 | tf_op jit(solution)/shard_map/ppermute | solution.py:269
  75.0 3.7 %collective-permute-start.41 = (f32[128,128]{1,0:T(8,128)S(1)}, f32[128,128]{1,0:T(8,128)S(1)}, u32[]{:S(2)}, u32[]{:S(2)}) collective-permute-start(f32[128,128]{1,0:T(8,128)S(1)} %get-tuple-element.87.refs_3_), channel_id=1, source_target_pairs={{0,4},{1,5},{2,6},{3,7},{4,0},{5,1},{6,2},{7,3},{8,12},{9,13},{10,... | collective-permute-start | bytes 196616 | tf_op jit(solution)/shard_map/ppermute | solution.py:269
  80.6 3.8 %collective-permute-start.44 = (f32[40,128]{1,0:T(8,128)S(1)}, f32[40,128]{1,0:T(8,128)S(1)}, u32[]{:S(2)}, u32[]{:S(2)}) collective-permute-start(f32[40,128]{1,0:T(8,128)S(1)} %get-tuple-element.94), channel_id=1, source_target_pairs={{1,0},{2,1},{3,2},{7,3},{6,7},{5,6},{4,5},{0,4},{9,8},{10,9},{11,1... | collective-permute-start | bytes 61448 | tf_op jit(solution)/shard_map/ppermute | solution.py:269
  (21 other events, 68.0 us)

commit v7 on v6

--- a/solution.py
+++ b/solution.py
@@ -1,4 +1,5 @@
 import functools
+import math
 
 import jax
 import jax.numpy as jnp
@@ -145,19 +146,19 @@
     return high[base + at] if at < width else None
 
 
-def pack_y_kernel(widths, labels, flags, *refs):
+def pack_y_kernel(widths, labels, ring, flags, *refs):
     fields = len(widths)
     ins = refs[:fields]
-    low, high = refs[fields + labels : fields + labels + 2]
-    inner, outer = refs[fields + labels + 2 :]
+    low, high = refs[fields + 1 : fields + 3]
+    one, two = refs[fields + 3 :]
     nx, ny = ins[0].shape[0], ins[0].shape[1]
     frame = Frame(nx, ny)
     base = bases(widths)
     even = flags[PARITY] == 0
 
     def send(at, count, to_high, to_low):
-        inner[at : at + count] = jnp.where(even, to_high, to_low)
-        outer[at : at + count] = jnp.where(even, to_low, to_high)
+        one[at : at + count] = to_high if ring else jnp.where(even, to_high, to_low)
+        two[at : at + count] = to_low if ring else jnp.where(even, to_low, to_high)
 
     for f in range(fields):
         for x in range(frame.wide):
@@ -166,15 +167,17 @@
             if slab is None:
                 slab = jnp.ones((ny, LANES), F32)
             send(at, HALO, slab[ny - HALO :], slab[:HALO])
+    at = fields * frame.wide * HALO
+    if ring:
+        one[at:], two[at:] = refs[fields][...], refs[fields][...]
     if labels:
-        at = fields * frame.wide * HALO
         nb, rows, width = refs[fields].shape
-        for out in (inner, outer):
+        for out in (one, two):
             out[at:] = jnp.zeros((out.shape[0] - at, LANES), F32)
         for b in range(nb):
-            high, low = (refs[fields][b, row : row + 1].astype(F32) for row in (rows - 1, 0))
-            inner[at + b : at + b + 1, :width] = jnp.where(even, high, low)
-            outer[at + b : at + b + 1, :width] = jnp.where(even, low, high)
+            top, bottom = (refs[fields][b, row : row + 1].astype(F32) for row in (rows - 1, 0))
+            one[at + b : at + b + 1, :width] = jnp.where(even, top, bottom)
+            two[at + b : at + b + 1, :width] = jnp.where(even, bottom, top)
 
 
 def packed_lanes(wide_ref, f, frame, rows, to_high, to_low):
@@ -190,7 +193,7 @@
     to_low[at] = turned(low, -HALO, 1)
 
 
-def frame_kernel(widths, labels, flags, *refs):
+def frame_kernel(widths, flags, *refs):
     fields = len(widths)
     ins = refs[:fields]
     x_low, x_high, _ = refs[fields : fields + 3]
@@ -209,16 +212,18 @@
         packed_lanes(wide_ref, f, frame, pl.ds(2 * SUB, tall - 2 * SUB), to_high, to_low)
 
 
-def pack_z_kernel(widths, labels, flags, wide_in, high_in, low_in, inner, outer, *refs):
+def pack_z_kernel(widths, labels, ring, flags, wide_in, high_in, low_in, from_low, from_high, rider, *refs):
     fields = len(widths)
-    wide_ref, send_forth, send_back, to_high, to_low = refs[labels:]
+    wide_ref, send_forth, send_back, to_high, to_low = refs
     frame = Frame(wide_ref.shape[1] - 2 * HALO, wide_ref.shape[2] - 2 * (SUB + HALO))
     ny, tall, own = frame.ny, frame.tall, frame.own
     even = flags[PARITY] == 0
     for f in range(fields):
         for x in range(frame.wide):
             at = (f * frame.wide + x) * HALO
-            low, high = sides(flags, outer[at : at + HALO], inner[at : at + HALO])
+            low, high = from_low[at : at + HALO], from_high[at : at + HALO]
+            if not ring:
+                low, high = jnp.where(even, high, low), jnp.where(even, low, high)
             wide_ref[f, x, SUB:own] = low
             wide_ref[f, x, own + ny : own + ny + HALO] = high
     size = fields * tall
@@ -228,12 +233,14 @@
             packed_lanes(wide_ref, f, frame, pl.ds(start, SUB), to_high, to_low)
     high, low = to_high[...], to_low[...]
     send_forth[:size], send_back[:size] = jnp.where(even, high, low), jnp.where(even, low, high)
+    if ring:
+        send_forth[size:], send_back[size:] = rider[...], rider[...]
     if labels:
-        nb, rows, width = refs[0].shape
+        nb, rows, width = rider.shape
         lane = lane_no((rows, LANES))
         high = low = jnp.zeros((rows, LANES), F32)
         for b in range(nb):
-            slab = refs[0][b].astype(F32)
+            slab = rider[b].astype(F32)
             high = jnp.where(lane == b, slab[:, width - 1 :], high)
             low = jnp.where(lane == b, slab[:, :1], low)
         send_forth[size:], send_back[size:] = jnp.where(even, high, low), jnp.where(even, low, high)
@@ -273,12 +280,18 @@
             return (lax.ppermute(sends[0], "gx", self.ring_x),)
         return lax.ppermute(sends[0], "gx", self.ring_x), lax.ppermute(sends[1], "gx", self.back(self.ring_x))
 
-    def near(self, values):
+    def near(self, values, x=None, y=None, z=None):
         ring = [(j, (j + 1) % self.sizes[1]) for j in range(self.sizes[1])]
-        forth, back = self.z(values, values)
-        from_x = self.x([values, values])
-        low, high = lax.ppermute(values, "gy", ring), lax.ppermute(values, "gy", self.back(ring))
+        forth, back = self.z(*(z or (values, values)))
+        from_x = self.x(x or (values, values))
+        to_high, to_low = y or (values, values)
+        low, high = lax.ppermute(to_high, "gy", ring), lax.ppermute(to_low, "gy", self.back(ring))
         return (forth, back, *from_x, low, high)
+
+    def all(self, values):
+        total = math.prod(self.sizes)
+        copies = jnp.broadcast_to(values, (total, *values.shape))
+        return lax.all_to_all(copies, ("gx", "gy", "gz"), 0, 0, tiled=True)
 
     def y(self, inner, outer):
         return self.send(inner, self.inner), self.send(outer, self.outer)
@@ -287,32 +300,29 @@
         return self.send(forth, self.snake), self.send(back, self.back(self.snake))
 
 
-def widened(links, widths, arrays, from_x, beside_y=None, beside_z=None):
-    fields, labels = len(widths), len(arrays) - len(widths)
+def send_y(widths, arrays, rider, from_x, ring):
     nx, ny, nz = arrays[0].shape
-    frame = Frame(nx, ny)
-    rows = fields * frame.wide * HALO + labels * ny // 2
-    sends = call(functools.partial(pack_y_kernel, widths, labels), [shaped(rows, nz)] * 2)(
-        *arrays, from_x[0], from_x[-1]
-    )
-    size = fields * frame.tall
-    framed = call(
-        functools.partial(frame_kernel, widths, labels), [shaped(fields, *frame.main)] + [shaped(size, nz)] * 2
-    )(*arrays[:fields], from_x[0], from_x[-1], sends[0])
-    work = beside_y(sends[0]) if beside_y else ()
-    from_y = links.y(*sends)
-    if work:
-        from_y = lax.optimization_barrier((*from_y, *work))[:2]
-    rows = size + labels * ny // 2
-    wide, *sends = call(
-        functools.partial(pack_z_kernel, widths, labels),
-        [shaped(fields, *frame.main)] + [shaped(rows, nz)] * 2,
-        [pltpu.VMEM((size, nz), F32)] * 2,
+    rows = len(widths) * Frame(nx, ny).wide * HALO + (SUB if ring else ny // 2)
+    kernel = functools.partial(pack_y_kernel, widths, not ring, ring)
+    return call(kernel, [shaped(rows, nz)] * 2)(*arrays, rider, from_x[0], from_x[-1])
+
+
+def framed(widths, arrays, from_x, sent):
+    nx, ny, nz = arrays[0].shape
+    frame, fields = Frame(nx, ny), len(widths)
+    outs = [shaped(fields, *frame.main)] + [shaped(fields * frame.tall, nz)] * 2
+    return call(functools.partial(frame_kernel, widths), outs)(*arrays, from_x[0], from_x[-1], sent)
+
+
+def send_z(widths, frames, from_y, rider, ring):
+    wide, high, _ = frames
+    rows = high.shape[0] + (SUB if ring else rider.shape[1])
+    return call(
+        functools.partial(pack_z_kernel, widths, not ring, ring),
+        [shaped(*wide.shape)] + [shaped(rows, LANES)] * 2,
+        [pltpu.VMEM(high.shape, F32)] * 2,
         aliases={0: 0},
-    )(*framed, *from_y, *arrays[fields:])
-    if beside_z:
-        beside_z(wide, sends[0])
-    return (wide, *links.z(*sends)), from_y
+    )(*frames, *from_y, rider)
 
 
 def sides(flags, forth, back):
@@ -596,7 +606,8 @@
     out[rows, AGG:] = (tile - high.astype(F32)).astype(BF16)
 
 
-def blocks_kernel(flags, cond, absorb, block_agg, _, block_label, near, weights, inner, face_label, lift, part, line):
+def blocks_kernel(flags, cond, absorb, block_agg, _, block_label, near, weights, inner, face_label, fine_label,
+                  part, line):
     nx, ny = cond.shape[0], cond.shape[1]
     nb, half, width = nx // 2, ny // 2, LANES // 2
     lane, row = lane_no((half, LANES)), row_no((half, LANES))
@@ -640,7 +651,10 @@
             inner[b] = pack_rows(total)
             for d, (beside, values) in enumerate(((near_x, high_x), (near_y, high_y), (near_z, high_z))):
                 near[d, b], weights[d, b] = pack_rows(beside), pack_rows(values)
-            lift[b] = picked(own, lane // 2).astype(jnp.int32)
+            spread = picked(own, lane // 2)
+            for a in range(2):
+                for c in range(2):
+                    fine_label[x + a, pl.ds(c, half, stride=2)] = spread
             low_x = high_x
         return carry
 
@@ -698,7 +712,8 @@
 
 def turn_kernel(flags, tiles, scaled_rhs, scale, own, *refs):
     forth, back, *others, out = refs
-    vectors = [own[...]] + [ref[...] for ref in others] + [*sides(flags, forth[...], back[...])]
+    got = [ref[ref.shape[0] - 1, :SUB] if len(ref.shape) == 3 else ref[ref.shape[0] - SUB :] for ref in (*others, forth, back)]
+    vectors = [own[...], *got[:-2], *sides(flags, *got[-2:])]
     row = row_no((SUB, AGG))
     parts = []
     for v in vectors:
@@ -709,38 +724,28 @@
     out[...] = (1.0 - OMEGA_COARSE) * own[...] + scaled_rhs[...] + scale[...] * applied
 
 
-def lifted(pre, lift, table, out, bs, at):
-    half = pre.shape[1] // 2
-    for n, b in enumerate(bs):
-        values = picked(table, lift[b])
-        for a in range(2):
-            for c in range(2):
-                rows = pl.ds(c, half, stride=2)
-                out[at + 2 * n + a, rows] = pre[2 * b + a, rows] + values
-
-
-def send_kernel(count, flags, pre, lift, coarse, *outs):
-    nb, half = pre.shape[0] // 2, pre.shape[1] // 2
-    table = jnp.broadcast_to(coarse[:1], (half, LANES))
+def ride_kernel(count, flags, pre, fine_label, coarse, *outs):
+    nx = pre.shape[0]
     for s, out in enumerate(outs):
-        if count == 2:
-            b = jnp.where(flags[IX] == 0, nb - HALO // 2, 0)
-        else:
-            b = (nb - HALO // 2, 0)[s]
-        lifted(pre, lift, table, out, [b + h for h in range(HALO // 2)], 0)
-
-
-def correct_kernel(flags, pre, lift, coarse, out):
-    table = jnp.broadcast_to(coarse[:1], (pre.shape[1] // 2, LANES))
-
-    def step(bs, carry):
-        lifted(pre, lift, table, out, bs, 2 * bs[0])
-        return carry
-
-    batched(0, pre.shape[0] // 2, step, 0)
-
-
-def post_kernel(flags, wide_ref, forth, back, *refs):
+        at = jnp.where(flags[IX] == 0, nx - HALO, 0) if count == 2 else (nx - HALO, 0)[s]
+        for f, field in enumerate((pre, fine_label)):
+            for x in range(HALO):
+                out[HALO * f + x] = field[at + x]
+        out[2 * HALO] = jnp.zeros(out.shape[1:], F32)
+        out[2 * HALO, :SUB] = coarse[...]
+
+
+def lift_kernel(flags, wide_ref, forth, back, main, ends):
+    frame = Frame(wide_ref.shape[1] - 2 * HALO, wide_ref.shape[2] - 2 * (SUB + HALO))
+    tall = frame.tall
+    for b in range(frame.wide // 2):
+        main[b] = wide_ref[1, 2 * b, frame.span].astype(jnp.int32)
+    rows = pl.ds(tall, tall)
+    for s, values in enumerate(sides(flags, forth[rows], back[rows])):
+        ends[s] = values.astype(jnp.int32)
+
+
+def post_kernel(sizes, flags, table, labels, end_labels, wide_ref, forth, back, *refs):
     (wx, wy, wz, inv_diag, start), ends = refs[:5], refs[5:11]
     out, one, two, one_ends, two_ends = refs[11:]
     nx, ny = out.shape[0], out.shape[1]
@@ -749,10 +754,34 @@
     ex, ey, ez_up, ez_low, inv_ends, start_ends = ends
     for ref in (one, two, one_ends, two_ends):
         clear_spares(ref, frame)
-    below, above = sides(flags, forth[...], back[...])
-    two_ends[0, span], two_ends[1, span] = below, above
+    place = [lax.axis_index(a) for a in ("gx", "gy", "gz")]
+    row, lane = row_no((tall, LANES)), lane_no((tall, LANES))
+
+    def table_at(dx, dz):
+        tables = []
+        for dy in (-1, 0, 1):
+            at = [jnp.clip(p + d, 0, n - 1) for p, d, n in zip(place, (dx, dy, dz), sizes)]
+            tables.append(table[(at[0] * sizes[1] + at[1]) * sizes[2] + at[2]])
+        return jnp.where(row < HALO, tables[0], jnp.where(row < HALO + ny, tables[1], tables[2]))
+
+    for x_from, x_to, dx in ((0, HALO, -1), (HALO, HALO + nx, 0), (HALO + nx, wide, 1)):
+        values = table_at(dx, 0)
+
+        def lift(bs, carry, values=values):
+            news = [picked(values, labels[b]) for b in bs]
+            for b, new in zip(bs, news):
+                for a in range(2):
+                    two[2 * b + a, span] = wide_ref[0, 2 * b + a, span] + new
+            return carry
+
+        batched(x_from // 2, x_to // 2, lift, 0, 4)
+    for s, (dz, base) in enumerate(zip((-1, 1), sides(flags, forth[:tall], back[:tall]))):
+        below, inside, above = (picked(table_at(dx, dz), end_labels[s]) for dx in (-1, 0, 1))
+        spot = lane // HALO
+        lifted = jnp.where(spot < HALO, below, jnp.where(spot < HALO + nx, inside, above))
+        two_ends[s, span] = base + lifted
     kept = 1.0 - OMEGA_FINE
-    buffers = ((wide_ref.at[0], two_ends), (one, one_ends), (two, two_ends), (one, one_ends))
+    buffers = ((two, two_ends), (one, one_ends), (two, two_ends), (one, one_ends))
     for s in range(POST):
         src, src_ends = buffers[s]
         join = joined(ez_up[0, span] * src_ends[0, span], ez_low[1, span] * src_ends[1, span])
@@ -807,12 +836,12 @@
     )(*pinned, x_sends[0])
     blocks = (nb, SUB, LANES)
     outs = [shaped(*blocks), shaped(3, *blocks), shaped(3, *blocks), shaped(*blocks), shaped(6, SUB, LANES)]
-    outs += [jax.ShapeDtypeStruct((nb, ny // 2, LANES), jnp.int32)]
+    outs += [shaped(nx, ny, nz)]
     scratch = [pltpu.VMEM((17, ny, LANES), F32), pltpu.VMEM((2, ny // 2, LANES), F32)]
     pair = [pltpu.VMEM((AGG, SUB * LANES), BF16), pltpu.VMEM((2 * AGG, SUB * LANES), BF16)]
-    *rows, face_label, lift = call(blocks_kernel, outs, scratch)(arrays[0], arrays[2], arrays[3], x_sends[0])
+    *rows, face_label, fine_label = call(blocks_kernel, outs, scratch)(arrays[0], arrays[2], arrays[3], x_sends[0])
     block_label = rows[0]
-    bounds = (0, nb // 6, nb * 7 // 12, nb)
+    bounds = (0, nb // 4, nb * 5 // 6, nb)
     parts = []
 
     def own_part(p, sent):
@@ -826,16 +855,16 @@
     first = own_part(0, x_sends[0])
     from_x = links.x(x_sends)
     from_x = lax.optimization_barrier((*from_x, *first))[:-1]
-    fields = []
-
-    def beside_z(wide, sent):
-        fields.extend(
-            call(fields_kernel, [shaped(*frame.main)] * 4 + [shaped(frame.tall, nz)], limit=24)(wide, sent)
-        )
-        own_part(2, sent)
-
-    halo, from_y = widened(links, WIDTHS, arrays, from_x, lambda sent: own_part(1, sent), beside_z)
-    own_tile, inner_diag = parts[-1]
+
+    sends = send_y(WIDTHS, arrays[:3], arrays[3], from_x, False)
+    frames = framed(WIDTHS, arrays[:3], from_x, sends[0])
+    second = own_part(1, sends[0])
+    from_y = links.y(*sends)
+    from_y = lax.optimization_barrier((*from_y, *second))[:2]
+    wide, *sends = send_z(WIDTHS, frames, from_y, arrays[3], False)
+    fields = call(fields_kernel, [shaped(*frame.main)] * 4 + [shaped(frame.tall, nz)], limit=24)(wide, sends[0])
+    own_tile, inner_diag = own_part(2, sends[0])
+    halo = (wide, *links.z(*sends))
     outs = [shaped(*frame.main)] * 2 + [shaped(*frame.ends)] * 6 + [shaped(nx, ny, nz)]
     outs += [shaped(6, SUB, LANES)] * 2 + [shaped(SUB, AGG)] * 2
     scratch = [pltpu.VMEM(frame.main, F32), pltpu.VMEM(frame.ends, F32), pltpu.VMEM((nx, frame.rows, LANES), F32)]
@@ -851,14 +880,30 @@
         pair * 2,
     )(own_tile, face_label, face_near, face_weight)
     coarse = scaled_rhs
-    for _ in range(KC - 1):
-        coarse = call(turn_kernel, shaped(SUB, AGG))(tiles, scaled_rhs, scale, coarse, *links.near(coarse))
-    x_sends = call(functools.partial(send_kernel, n_x), [shaped(HALO, ny, nz)] * n_send)(pre, lift, coarse)
-    from_x = links.x(x_sends)
-    corrected = call(correct_kernel, shaped(nx, ny, nz))(pre, lift, coarse)
-    halo, _ = widened(links, (HALO,), (corrected,), from_x)
+
+    def turn(**more):
+        near = links.near(coarse, **more)
+        return call(turn_kernel, shaped(SUB, AGG))(tiles, scaled_rhs, scale, coarse, *near), near
+
+    widths, both = (HALO, HALO), (pre, fine_label)
+    rides = call(functools.partial(ride_kernel, n_x), [shaped(2 * HALO + 1, ny, nz)] * n_send)(*both, coarse)
+    coarse, near = turn(x=rides)
+    from_x = near[2:-2]
+    rides = send_y(widths, both, coarse, from_x, True)
+    frames = framed(widths, both, from_x, rides[0])
+    coarse, near = turn(y=rides)
+    wide, *rides = send_z(widths, frames, near[-2:], coarse, True)
+    coarse, near = turn(z=rides)
+    halo = (wide, *near[:2])
+    outs = [jax.ShapeDtypeStruct((frame.wide // 2, frame.tall, nz), jnp.int32)]
+    outs += [jax.ShapeDtypeStruct((2, frame.tall, nz), jnp.int32)]
+    lifts = call(lift_kernel, outs)(*halo)
+    for _ in range(KC - 4):
+        coarse, _ = turn()
+    table = links.all(coarse[:1])
     scratch = [pltpu.VMEM(frame.main, F32)] * 2 + [pltpu.VMEM(frame.ends, F32)] * 2
-    return call(post_kernel, shaped(nx, ny, nz), scratch, limit=24)(*halo, *fields)
+    kernel = functools.partial(post_kernel, links.sizes)
+    return call(kernel, shaped(nx, ny, nz), scratch, limit=24)(table, *lifts, *halo, *fields)
 
 
 def solution(mesh):

time: 89.5 us -> 93.2 us (1.041)
  local copies, waits for them, and re-layouts: 0 us -> 6.75 us
  waiting for transfers between devices: 21.8 us -> 18.3 us
    ppermute x22 -> x18, waiting for transfers between devices: 13.8 us -> 5.12 us  [send(): return lax.ppermute(values, ('gx', 'gy', 'gz'), pairs)]
    all_to_all x0 -> x1, waiting for transfers between devices: none -> 6.51 us  [all(): return lax.all_to_all(copies, ('gx', 'gy', 'gz'), 0, 0, tiled=True)]
    unnamed x0 -> x20, local copies, waits for them, and re-layouts: none -> 6.12 us
    all_to_all x0 -> x1, starting transfers between devices: none -> 4.92 us  [all(): return lax.all_to_all(copies, ('gx', 'gy', 'gz'), 0, 0, tiled=True)]
    ppermute x9 -> x8, waiting for transfers between devices: 6.67 us -> 3.24 us  [x(): return (lax.ppermute(sends[0], 'gx', self.ring_x),)]
    ppermute x22 -> x18, starting transfers between devices: 21 us -> 17.7 us  [send(): return lax.ppermute(values, ('gx', 'gy', 'gz'), pairs)]
    ppermute x14, waiting for transfers between devices: 1.42 us -> 3.39 us  [the longest x7 3.25 us: near(): lax.ppermute(to_high, 'gy', ring)]
    ppermute x14, starting transfers between devices: 8.14 us -> 6.65 us  [the longest x7 5.97 us: near(): lax.ppermute(to_low, 'gy', self.back(ring))]
  transfers between devices with their start and end apart: 45 -> 41, of which waited for: 19 -> 17; matrix products, arithmetic and copies ran while one was open for 0% -> 0% of each run, Pallas kernels for 15% -> 15%
where the time goes in v7:
time: 93.2 us; the launch traced here: 92.7 us
  starting transfers between devices  40.2 us (43%)
  Pallas kernels  27.1 us (29%)
  waiting for transfers between devices  18.3 us (20%)
  local copies, waits for them, and re-layouts  6.75 us (7%)
    pallas_call x25, Pallas kernels, run(): pl.pallas_call(placed, out_shape=outs, in_specs=in_specs or [VMEM] * len(...  27.1 us
    ppermute x18, starting transfers between devices, send(): return lax.ppermute(values, ('gx', 'gy', 'gz'), pairs)  17.7 us
    ppermute x8, starting transfers between devices, x(): return (lax.ppermute(sends[0], 'gx', self.ring_x),)  10.9 us
    all_to_all x1, waiting for transfers between devices, all(): return lax.all_to_all(copies, ('gx', 'gy', 'gz'), 0, 0, tiled=True)  6.51 us
    unnamed x20, local copies, waits for them, and re-layouts  6.12 us
    ppermute x7, starting transfers between devices, near(): lax.ppermute(to_low, 'gy', self.back(ring))  5.97 us
    ppermute x18, waiting for transfers between devices, send(): return lax.ppermute(values, ('gx', 'gy', 'gz'), pairs)  5.12 us
    all_to_all x1, starting transfers between devices, all(): return lax.all_to_all(copies, ('gx', 'gy', 'gz'), 0, 0, tiled=True)  4.92 us
  transfers between devices with their start and end apart: 41, of which 17 were waited for; matrix products, arithmetic and copies ran while one was open for 0% of the time, Pallas kernels for 15%

profile of v7, /device:TPU:0, one launch (start us, length us, event | category | flops | bytes accessed | tf_op | source)
XLA Modules:
  0.0 92.7 jit_solution(680042416181475074)
XLA Ops:
  0.9 3.0 %collective-permute-start = (f32[11,32,128]{2,1,0:T(8,128)S(1)}, f32[11,32,128]{2,1,0:T(8,128)S(1)}, u32[]{:S(2)}, u32[]{:S(2)}) collective-permute-start(f32[11,32,128]{2,1,0:T(8,128)S(1)} %shard_map.46.refs_4_.refs_3_), channel_id=1, source_target_pairs={{0,16},{16,0},{1,17},{17,1},{2,18},{18,2},{3,19},{19,3},{4,20},{20... | collective-permute-start | bytes 540680 | tf_op jit(solution)/shard_map/ppermute | solution.py:280
  3.9 1.3 %shard_map.47 = (f32[24,32,128]{2,1,0:T(8,128)S(1)}, f32[24,32,128]{2,1,0:T(8,128)S(1)}, f32[24,32,128]{2,1,0:T(8,128)S(1)}, s32[12,16,64]{2,1,0:T(8,128)S(1)}) custom-call(f32[24,32,128]{2,1,0:T(8,128)} %refs_0_.3, f32[24,32,128]{2,1,0:T(8,128)} %refs_1_.3, f32[24,32,128]{2,1,0:T(8,128)} %refs_2_.3, s32[12,16,64]{2,1,0:T(8,128)} %refs_3_.3, ...), custom_call_target="tpu_custom_call" | custom-call | flops 1000000 | bytes 100000 | tf_op jit(solution)/shard_map/pallas_call | solution.py:37
  5.2 1.6 %shard_map.48 = (f32[12,8,128]{2,1,0:T(8,128)S(1)}, f32[3,12,8,128]{3,2,1,0:T(8,128)S(1)}, f32[3,12,8,128]{3,2,1,0:T(8,128)S(1)}, f32[12,8,128]{2,1,0:T(8,128)S(...) custom-call(f32[24,32,128]{2,1,0:T(8,128)S(1)} %get-tuple-element.56.refs_0_, ...), custom_call_target="tpu_custom_call" | custom-call | flops 1000000 | bytes 100000 | tf_op jit(solution)/shard_map/pallas_call | solution.py:37
  6.8 1.4 %shard_map.49.refs_4_ = f32[128,256]{1,0:T(8,128)S(1)} custom-call(f32[12,8,128]{2,1,0:T(8,128)S(1)} %get-tuple-element.59.refs_0_.refs_12_, f32[3,12,8,128]{3,2,1,0:T(8,128)S(1)} %get-tuple-element.60.refs_1_, f32[3,12,8,128]{3,2,1,0:T(8,128)S(1)} %get-tuple-element.61.refs_2_, f32[12,8,128]{2,1,0:T(8,128)S(1)} %get-tuple-element.62.refs_3_, ...), custom_call_target="tpu_custom_call" | custom-call | flops 1000000 | bytes 100000 | tf_op jit(solution)/shard_map/pallas_call | solution.py:37
  8.6 1.8 %collective-permute-start.2 = (f32[400,128]{1,0:T(8,128)S(1)}, f32[400,128]{1,0:T(8,128)S(1)}, u32[]{:S(2)}, u32[]{:S(2)}) collective-permute-start(f32[400,128]{1,0:T(8,128)S(1)} %get-tuple-element.69), channel_id=1, source_target_pairs={{0,16},{1,17},{2,18},{3,19},{4,8},{5,9},{6,10},{7,11},{8,4},{9,5},... | collective-permute-start | bytes 614408 | tf_op jit(solution)/shard_map/ppermute | solution.py:276
  10.5 3.3 %shard_map.51.refs_4_ = f32[128,256]{1,0:T(8,128)S(1)} custom-call(f32[12,8,128]{2,1,0:T(8,128)S(1)} %get-tuple-element.59.refs_0_.refs_12_, f32[3,12,8,128]{3,2,1,0:T(8,128)S(1)} %get-tuple-element.60.refs_1_, f32[3,12,8,128]{3,2,1,0:T(8,128)S(1)} %get-tuple-element.61.refs_2_, f32[12,8,128]{2,1,0:T(8,128)S(1)} %get-tuple-element.62.refs_3_, ...), custom_call_target="tpu_custom_call" | custom-call | flops 1000000 | bytes 100000 | tf_op jit(solution)/shard_map/pallas_call | solution.py:37
  15.4 1.7 %collective-permute-start.3 = (f32[136,128]{1,0:T(8,128)S(1)}, f32[136,128]{1,0:T(8,128)S(1)}, u32[]{:S(2)}, u32[]{:S(2)}) collective-permute-start(f32[136,128]{1,0:T(8,128)S(1)} %get-tuple-element.72.refs_5_.refs_1_), channel_id=1, source_target_pairs={{0,1},{1,2},{2,3},{3,7},{7,6},{6,5},{5,4},{4,0},{8,9},{9,10},{10,1... | collective-permute-start | bytes 208904 | tf_op jit(solution)/shard_map/ppermute | solution.py:276
  17.1 1.8 %shard_map.54 = (bf16[128,256]{1,0:T(8,128)(2,1)S(1)}, f32[8,128]{1,0:T(8,128)S(1)}) custom-call(f32[12,8,128]{2,1,0:T(8,128)S(1)} %get-tuple-element.59.refs_0_.refs_12_, f32[3,12,8,128]{3,2,1,0:T(8,128)S(1)} %get-tuple-element.60.refs_1_, f32[3,12,8,128]{3,2,1,0:T(8,128)S(1)} %get-tuple-element.61.refs_2_, f32[12,8,128]{2,1,0:T(8,128)S(1)} %get-tuple-element.62.refs_3_, ...), custom_call_target="tpu_custom_call" | custom-call | flops 1000000 | bytes 100000 | tf_op jit(solution)/shard_map/pallas_call | solution.py:37
  18.9 1.4 %shard_map.55 = (f32[32,56,128]{2,1,0:T(8,128)S(1)}, f32[32,56,128]{2,1,0:T(8,128)S(1)}, f32[32,56,128]{2,1,0:T(8,128)S(1)}, f32[32,56,128]{2,1,0:T(8,128)S(1)}, f32[40,128]{1,0:T(8,128)S(1)}) custom-call(f32[3,32,56,128]{3,2,1,0:T(8,128)S(1)} %get-tuple-element.75.refs_0_, f32[136,128]{1,0:T(8,128)S(1)} %get-tuple-element.72.refs_5_.refs_1_), custom_call_target="tpu_custom_call" | custom-call | flops 1000000 | bytes 100000 | tf_op jit(solution)/shard_map/pallas_call | solution.py:37
  20.3 5.1 %shard_map.56 = (f32[32,56,128]{2,1,0:T(8,128)S(1)}, f32[32,56,128]{2,1,0:T(8,128)S(1)}, f32[2,56,128]{2,1,0:T(8,128)S(1)}, f32[2,56,128]{2,1,0:T(8,128)S(1)}, f...) custom-call(f32[3,32,56,128]{3,2,1,0:T(8,128)S(1)} %get-tuple-elemen, ...), custom_call_target="tpu_custom_call" | custom-call | flops 1000000 | bytes 100000 | tf_op jit(solution)/shard_map/pallas_call | solution.py:37
  25.4 1.8 %collective-permute-start.7 = (f32[9,32,128]{2,1,0:T(8,128)S(1)}, f32[9,32,128]{2,1,0:T(8,128)S(1)}, u32[]{:S(2)}, u32[]{:S(2)}) collective-permute-start(f32[9,32,128]{2,1,0:T(8,128)S(1)} %shard_map.58), channel_id=1, source_target_pairs={{0,16},{16,0},{1,17},{17,1},{2,18},{18,2},{3,19},{19,3},{4,20},{20... | collective-permute-start | bytes 442376 | tf_op jit(solution)/shard_map/ppermute | solution.py:280
  28.5 1.3 %collective-permute-start.5 = (f32[8,128]{1,0:T(8,128)S(1)}, f32[8,128]{1,0:T(8,128)S(1)}, u32[]{:S(2)}, u32[]{:S(2)}) collective-permute-start(f32[8,128]{1,0:T(8,128)S(1)} %get-tuple-element.85.refs_2_.refs_1_.refs_3_), channel_id=1, source_target_pairs={{0,1},{1,2},{2,3},{3,7},{7,6},{6,5},{5,4},{4,0},{8,9},{9,10},{10,1... | collective-permute-start | bytes 12296 | tf_op jit(solution)/shard_map/ppermute | solution.py:276
  29.7 1.7 %shard_map.57.refs_0_ = bf16[768,256]{1,0:T(8,128)(2,1)S(1)} custom-call(bf16[128,256]{1,0:T(8,128)(2,1)S(1)} %get-tuple-element.73.refs_0_, f32[6,8,128]{2,1,0:T(8,128)S(1)} %get-tuple-element.74.refs_13_.refs_1_, f32[6,8,128]{2,1,0:T(8,128)S(1)} %get-tuple-element.83.refs_2_, f32[6,8,128]{2,1,0:T(8,128)S(1)} %get-tuple-element.84.refs_3_), custom_call_target="tpu_custom_call" | custom-call | flops 1000000 | bytes 100000 | tf_op jit(solution)/shard_map/pallas_call | solution.py:37
  37.2 1.4 %collective-permute-done.13.refs_7_.refs_3_ = f32[264,128]{1,0:T(8,128)S(1)} collective-permute-done((f32[264,128]{1,0:T(8,128)S(1)}, f32[264,128]{1,0:T(8,128)S(1)}, u32[]{:S(2)}, u32[]{:S(2)}) %collective-permute-start.13) | collective-permute-done | bytes 135200 | tf_op jit(solution)/shard_map/ppermute | solution.py:288
  39.1 1.6 %collective-permute-start.15 = (f32[88,128]{1,0:T(8,128)S(1)}, f32[88,128]{1,0:T(8,128)S(1)}, u32[]{:S(2)}, u32[]{:S(2)}) collective-permute-start(f32[88,128]{1,0:T(8,128)S(1)} %get-tuple-element.94), channel_id=1, source_target_pairs={{0,1},{1,2},{2,3},{3,7},{7,6},{6,5},{5,4},{4,0},{8,9},{9,10},{10,1... | collective-permute-start | bytes 135176 | tf_op jit(solution)/shard_map/ppermute | solution.py:276
  42.4 1.7 %collective-permute-done.18.refs_7_ = f32[8,128]{1,0:T(8,128)S(1)} collective-permute-done((f32[8,128]{1,0:T(8,128)S(1)}, f32[8,128]{1,0:T(8,128)S(1)}, u32[]{:S(2)}, u32[]{:S(2)}) %collective-permute-start.18) | collective-permute-done | bytes 4128 | tf_op jit(solution)/shard_map/ppermute | solution.py:288
  45.5 1.4 %collective-permute-start.22 = (f32[8,128]{1,0:T(8,128)S(1)}, f32[8,128]{1,0:T(8,128)S(1)}, u32[]{:S(2)}, u32[]{:S(2)}) collective-permute-start(f32[8,128]{1,0:T(8,128)S(1)} %shard_map.64.refs_3_), channel_id=1, source_target_pairs={{0,16},{16,0},{1,17},{17,1},{2,18},{18,2},{3,19},{19,3},{4,20},{20... | collective-permute-start | bytes 12296 | tf_op jit(solution)/shard_map/ppermute | solution.py:280
  47.7 1.3 %collective-permute-start.20 = (f32[8,128]{1,0:T(8,128)S(1)}, f32[8,128]{1,0:T(8,128)S(1)}, u32[]{:S(2)}, u32[]{:S(2)}) collective-permute-start(f32[8,128]{1,0:T(8,128)S(1)} %shard_map.64.refs_3_), channel_id=1, source_target_pairs={{0,1},{1,2},{2,3},{3,7},{7,6},{6,5},{5,4},{4,0},{8,9},{9,10},{10,1... | collective-permute-start | bytes 12296 | tf_op jit(solution)/shard_map/ppermute | solution.py:276
  49.1 1.4 %collective-permute-done.21.refs_5_ = f32[8,128]{1,0:T(8,128)S(1)} collective-permute-done((f32[8,128]{1,0:T(8,128)S(1)}, f32[8,128]{1,0:T(8,128)S(1)}, u32[]{:S(2)}, u32[]{:S(2)}) %collective-permute-start.21) | collective-permute-done | bytes 4128 | tf_op jit(solution)/shard_map/ppermute | solution.py:276
  56.8 1.4 %collective-permute-start.34 = (f32[8,128]{1,0:T(8,128)S(1)}, f32[8,128]{1,0:T(8,128)S(1)}, u32[]{:S(2)}, u32[]{:S(2)}) collective-permute-start(f32[8,128]{1,0:T(8,128)S(1)} %shard_map.66.refs_3_), channel_id=1, source_target_pairs={{4,0},{8,4},{12,8},{0,12},{5,1},{9,5},{13,9},{1,13},{6,2},{10,6},{... | collective-permute-start | bytes 12296 | tf_op jit(solution)/shard_map/ppermute | solution.py:288
  63.0 1.3 %collective-permute-start.39 = (f32[8,128]{1,0:T(8,128)S(1)}, f32[8,128]{1,0:T(8,128)S(1)}, u32[]{:S(2)}, u32[]{:S(2)}) collective-permute-start(f32[8,128]{1,0:T(8,128)S(1)} %shard_map.67.refs_3_), channel_id=1, source_target_pairs={{4,0},{8,4},{12,8},{0,12},{5,1},{9,5},{13,9},{1,13},{6,2},{10,6},{... | collective-permute-start | bytes 12296 | tf_op jit(solution)/shard_map/ppermute | solution.py:288
  69.7 4.9 %all-to-all-start = ((f32[32,1,128]{2,1,0:T(1,128)}), f32[32,1,128]{2,1,0:T(1,128)S(1)}, u32[]{:S(2)}, u32[]{:S(2)}) async-start(f32[32,1,128]{2,1,0:T(1,128)} %broadcast_in_dim.3), calls=%async_computation | async-start | bytes 32768 | tf_op jit(solution)/shard_map/all_to_all | solution.py:294
  75.2 6.5 %all-to-all-done.refs_0_ = f32[32,1,128]{2,1,0:T(1,128)S(1)} async-done(((f32[32,1,128]{2,1,0:T(1,128)}), f32[32,1,128]{2,1,0:T(1,128)S(1)}, u32[]{:S(2)}, u32[]{:S(2)}) %all-to-all-start) | async-done | bytes 16416 | tf_op jit(solution)/shard_map/all_to_all | solution.py:294
  87.3 5.5 %shard_map.70 = f32[24,32,128]{2,1,0:T(8,128)} custom-call(f32[32,1,128]{2,1,0:T(1,128)S(1)} %all-to-all-done.refs_0_, s32[16,40,128]{2,1,0:T(8,128)S(1)} %get-tuple-element.97.refs_1_, s32[2,40,128]{2,1,0:T(8,128)S(1)} %copy-done.9, f32[2,32,56,128]{3,2,1,0:T(8,128)S(1)} %get-tuple-element.96.refs_0_.refs_3_, ...), custom_call_target="tpu_custom_call" | custom-call | flops 1000000 | bytes 100000 | tf_op jit(solution)/shard_map/pallas_call | solution.py:37
  (105 shorter events, 36.8 us)
Async XLA Ops:
  0.9 7.6 %collective-permute-start = (f32[11,32,128]{2,1,0:T(8,128)S(1)}, f32[11,32,128]{2,1,0:T(8,128)S(1)}, u32[]{:S(2)}, u32[]{:S(2)}) collective-permute-start(f32[11,32,128]{2,1,0:T(8,128)S(1)} %shard_map.46.refs_4_.refs_3_), channel_id=1, source_target_pairs={{0,16},{16,0},{1,17},{17,1},{2,18},{18,2},{3,19},{19,3},{4,20},{20... | collective-permute-start | bytes 540680 | tf_op jit(solution)/shard_map/ppermute | solution.py:280
  8.6 5.9 %collective-permute-start.2 = (f32[400,128]{1,0:T(8,128)S(1)}, f32[400,128]{1,0:T(8,128)S(1)}, u32[]{:S(2)}, u32[]{:S(2)}) collective-permute-start(f32[400,128]{1,0:T(8,128)S(1)} %get-tuple-element.69), channel_id=1, source_target_pairs={{0,16},{1,17},{2,18},{3,19},{4,8},{5,9},{6,10},{7,11},{8,4},{9,5},... | collective-permute-start | bytes 614408 | tf_op jit(solution)/shard_map/ppermute | solution.py:276
  10.4 4.1 %collective-permute-start.1 = (f32[400,128]{1,0:T(8,128)S(1)}, f32[400,128]{1,0:T(8,128)S(1)}, u32[]{:S(2)}, u32[]{:S(2)}) collective-permute-start(f32[400,128]{1,0:T(8,128)S(1)} %get-tuple-element.65.refs_5_), channel_id=1, source_target_pairs={{0,4},{1,5},{2,6},{3,7},{4,0},{5,1},{6,2},{7,3},{8,12},{9,13},{10,... | collective-permute-start | bytes 614408 | tf_op jit(solution)/shard_map/ppermute | solution.py:276
  15.1 5.2 %collective-permute-start.4 = (f32[136,128]{1,0:T(8,128)S(1)}, f32[136,128]{1,0:T(8,128)S(1)}, u32[]{:S(2)}, u32[]{:S(2)}) collective-permute-start(f32[136,128]{1,0:T(8,128)S(1)} %get-tuple-element.76), channel_id=1, source_target_pairs={{1,0},{2,1},{3,2},{7,3},{6,7},{5,6},{4,5},{0,4},{9,8},{10,9},{11,1... | collective-permute-start | bytes 208904 | tf_op jit(solution)/shard_map/ppermute | solution.py:276
  15.4 4.9 %collective-permute-start.3 = (f32[136,128]{1,0:T(8,128)S(1)}, f32[136,128]{1,0:T(8,128)S(1)}, u32[]{:S(2)}, u32[]{:S(2)}) collective-permute-start(f32[136,128]{1,0:T(8,128)S(1)} %get-tuple-element.72.refs_5_.refs_1_), channel_id=1, source_target_pairs={{0,1},{1,2},{2,3},{3,7},{7,6},{6,5},{5,4},{4,0},{8,9},{9,10},{10,1... | collective-permute-start | bytes 208904 | tf_op jit(solution)/shard_map/ppermute | solution.py:276
  25.4 6.1 %collective-permute-start.7 = (f32[9,32,128]{2,1,0:T(8,128)S(1)}, f32[9,32,128]{2,1,0:T(8,128)S(1)}, u32[]{:S(2)}, u32[]{:S(2)}) collective-permute-start(f32[9,32,128]{2,1,0:T(8,128)S(1)} %shard_map.58), channel_id=1, source_target_pairs={{0,16},{16,0},{1,17},{17,1},{2,18},{18,2},{3,19},{19,3},{4,20},{20... | collective-permute-start | bytes 442376 | tf_op jit(solution)/shard_map/ppermute | solution.py:280
  27.2 4.3 %collective-permute-start.9 = (f32[8,128]{1,0:T(8,128)S(1)}, f32[8,128]{1,0:T(8,128)S(1)}, u32[]{:S(2)}, u32[]{:S(2)}) collective-permute-start(f32[8,128]{1,0:T(8,128)S(1)} %get-tuple-element.85.refs_2_.refs_1_.refs_3_), channel_id=1, source_target_pairs={{4,0},{8,4},{12,8},{0,12},{5,1},{9,5},{13,9},{1,13},{6,2},{10,6},{... | collective-permute-start | bytes 12296 | tf_op jit(solution)/shard_map/ppermute | solution.py:288
  27.2 4.3 %collective-permute-start.8 = (f32[8,128]{1,0:T(8,128)S(1)}, f32[8,128]{1,0:T(8,128)S(1)}, u32[]{:S(2)}, u32[]{:S(2)}) collective-permute-start(f32[8,128]{1,0:T(8,128)S(1)} %get-tuple-element.85.refs_2_.refs_1_.refs_3_), channel_id=1, source_target_pairs={{0,4},{4,8},{8,12},{12,0},{1,5},{5,9},{9,13},{13,1},{2,6},{6,10},{... | collective-permute-start | bytes 12296 | tf_op jit(solution)/shard_map/ppermute | solution.py:288
  27.7 3.8 %collective-permute-start.6 = (f32[8,128]{1,0:T(8,128)S(1)}, f32[8,128]{1,0:T(8,128)S(1)}, u32[]{:S(2)}, u32[]{:S(2)}) collective-permute-start(f32[8,128]{1,0:T(8,128)S(1)} %get-tuple-element.85.refs_2_.refs_1_.refs_3_), channel_id=1, source_target_pairs={{1,0},{2,1},{3,2},{7,3},{6,7},{5,6},{4,5},{0,4},{9,8},{10,9},{11,1... | collective-permute-start | bytes 12296 | tf_op jit(solution)/shard_map/ppermute | solution.py:276
  31.8 5.4 %collective-permute-start.14 = (f32[264,128]{1,0:T(8,128)S(1)}, f32[264,128]{1,0:T(8,128)S(1)}, u32[]{:S(2)}, u32[]{:S(2)}) collective-permute-start(f32[264,128]{1,0:T(8,128)S(1)} %get-tuple-element.90), channel_id=1, source_target_pairs={{4,0},{8,4},{12,8},{0,12},{5,1},{9,5},{13,9},{1,13},{6,2},{10,6},{... | collective-permute-start | bytes 405512 | tf_op jit(solution)/shard_map/ppermute | solution.py:288
  33.0 5.6 %collective-permute-start.13 = (f32[264,128]{1,0:T(8,128)S(1)}, f32[264,128]{1,0:T(8,128)S(1)}, u32[]{:S(2)}, u32[]{:S(2)}) collective-permute-start(f32[264,128]{1,0:T(8,128)S(1)} %get-tuple-element.89.refs_4_), channel_id=1, source_target_pairs={{0,4},{4,8},{8,12},{12,0},{1,5},{5,9},{9,13},{13,1},{2,6},{6,10},{... | collective-permute-start | bytes 405512 | tf_op jit(solution)/shard_map/ppermute | solution.py:288
  33.0 3.6 %collective-permute-start.12 = (f32[8,128]{1,0:T(8,128)S(1)}, f32[8,128]{1,0:T(8,128)S(1)}, u32[]{:S(2)}, u32[]{:S(2)}) collective-permute-start(f32[8,128]{1,0:T(8,128)S(1)} %shard_map.59.refs_2_.refs_3_), channel_id=1, source_target_pairs={{0,16},{16,0},{1,17},{17,1},{2,18},{18,2},{3,19},{19,3},{4,20},{20... | collective-permute-start | bytes 12296 | tf_op jit(solution)/shard_map/ppermute | solution.py:280
  33.6 3.6 %collective-permute-start.11 = (f32[8,128]{1,0:T(8,128)S(1)}, f32[8,128]{1,0:T(8,128)S(1)}, u32[]{:S(2)}, u32[]{:S(2)}) collective-permute-start(f32[8,128]{1,0:T(8,128)S(1)} %shard_map.59.refs_2_.refs_3_), channel_id=1, source_target_pairs={{1,0},{2,1},{3,2},{7,3},{6,7},{5,6},{4,5},{0,4},{9,8},{10,9},{11,1... | collective-permute-start | bytes 12296 | tf_op jit(solution)/shard_map/ppermute | solution.py:276
  39.1 5.7 %collective-permute-start.15 = (f32[88,128]{1,0:T(8,128)S(1)}, f32[88,128]{1,0:T(8,128)S(1)}, u32[]{:S(2)}, u32[]{:S(2)}) collective-permute-start(f32[88,128]{1,0:T(8,128)S(1)} %get-tuple-element.94), channel_id=1, source_target_pairs={{0,1},{1,2},{2,3},{3,7},{7,6},{6,5},{5,4},{4,0},{8,9},{9,10},{10,1... | collective-permute-start | bytes 135176 | tf_op jit(solution)/shard_map/ppermute | solution.py:276
  40.7 4.1 %collective-permute-start.16 = (f32[88,128]{1,0:T(8,128)S(1)}, f32[88,128]{1,0:T(8,128)S(1)}, u32[]{:S(2)}, u32[]{:S(2)}) collective-permute-start(f32[88,128]{1,0:T(8,128)S(1)} %get-tuple-element.95), channel_id=1, source_target_pairs={{1,0},{2,1},{3,2},{7,3},{6,7},{5,6},{4,5},{0,4},{9,8},{10,9},{11,1... | collective-permute-start | bytes 135176 | tf_op jit(solution)/shard_map/ppermute | solution.py:276
  45.0 4.0 %collective-permute-start.24 = (f32[8,128]{1,0:T(8,128)S(1)}, f32[8,128]{1,0:T(8,128)S(1)}, u32[]{:S(2)}, u32[]{:S(2)}) collective-permute-start(f32[8,128]{1,0:T(8,128)S(1)} %shard_map.64.refs_3_), channel_id=1, source_target_pairs={{4,0},{8,4},{12,8},{0,12},{5,1},{9,5},{13,9},{1,13},{6,2},{10,6},{... | collective-permute-start | bytes 12296 | tf_op jit(solution)/shard_map/ppermute | solution.py:288
  47.0 3.6 %collective-permute-start.21 = (f32[8,128]{1,0:T(8,128)S(1)}, f32[8,128]{1,0:T(8,128)S(1)}, u32[]{:S(2)}, u32[]{:S(2)}) collective-permute-start(f32[8,128]{1,0:T(8,128)S(1)} %shard_map.64.refs_3_), channel_id=1, source_target_pairs={{1,0},{2,1},{3,2},{7,3},{6,7},{5,6},{4,5},{0,4},{9,8},{10,9},{11,1... | collective-permute-start | bytes 12296 | tf_op jit(solution)/shard_map/ppermute | solution.py:276
  50.7 4.3 %collective-permute-start.29 = (f32[8,128]{1,0:T(8,128)S(1)}, f32[8,128]{1,0:T(8,128)S(1)}, u32[]{:S(2)}, u32[]{:S(2)}) collective-permute-start(f32[8,128]{1,0:T(8,128)S(1)} %shard_map.65.refs_3_), channel_id=1, source_target_pairs={{4,0},{8,4},{12,8},{0,12},{5,1},{9,5},{13,9},{1,13},{6,2},{10,6},{... | collective-permute-start | bytes 12296 | tf_op jit(solution)/shard_map/ppermute | solution.py:288
  51.8 3.6 %collective-permute-start.27 = (f32[8,128]{1,0:T(8,128)S(1)}, f32[8,128]{1,0:T(8,128)S(1)}, u32[]{:S(2)}, u32[]{:S(2)}) collective-permute-start(f32[8,128]{1,0:T(8,128)S(1)} %shard_map.65.refs_3_), channel_id=1, source_target_pairs={{0,16},{16,0},{1,17},{17,1},{2,18},{18,2},{3,19},{19,3},{4,20},{20... | collective-permute-start | bytes 12296 | tf_op jit(solution)/shard_map/ppermute | solution.py:280
  56.8 4.5 %collective-permute-start.34 = (f32[8,128]{1,0:T(8,128)S(1)}, f32[8,128]{1,0:T(8,128)S(1)}, u32[]{:S(2)}, u32[]{:S(2)}) collective-permute-start(f32[8,128]{1,0:T(8,128)S(1)} %shard_map.66.refs_3_), channel_id=1, source_target_pairs={{4,0},{8,4},{12,8},{0,12},{5,1},{9,5},{13,9},{1,13},{6,2},{10,6},{... | collective-permute-start | bytes 12296 | tf_op jit(solution)/shard_map/ppermute | solution.py:288
  58.2 3.6 %collective-permute-start.32 = (f32[8,128]{1,0:T(8,128)S(1)}, f32[8,128]{1,0:T(8,128)S(1)}, u32[]{:S(2)}, u32[]{:S(2)}) collective-permute-start(f32[8,128]{1,0:T(8,128)S(1)} %shard_map.66.refs_3_), channel_id=1, source_target_pairs={{0,16},{16,0},{1,17},{17,1},{2,18},{18,2},{3,19},{19,3},{4,20},{20... | collective-permute-start | bytes 12296 | tf_op jit(solution)/shard_map/ppermute | solution.py:280
  63.0 4.2 %collective-permute-start.39 = (f32[8,128]{1,0:T(8,128)S(1)}, f32[8,128]{1,0:T(8,128)S(1)}, u32[]{:S(2)}, u32[]{:S(2)}) collective-permute-start(f32[8,128]{1,0:T(8,128)S(1)} %shard_map.67.refs_3_), channel_id=1, source_target_pairs={{4,0},{8,4},{12,8},{0,12},{5,1},{9,5},{13,9},{1,13},{6,2},{10,6},{... | collective-permute-start | bytes 12296 | tf_op jit(solution)/shard_map/ppermute | solution.py:288
  65.2 3.6 %collective-permute-start.36 = (f32[8,128]{1,0:T(8,128)S(1)}, f32[8,128]{1,0:T(8,128)S(1)}, u32[]{:S(2)}, u32[]{:S(2)}) collective-permute-start(f32[8,128]{1,0:T(8,128)S(1)} %shard_map.67.refs_3_), channel_id=1, source_target_pairs={{1,0},{2,1},{3,2},{7,3},{6,7},{5,6},{4,5},{0,4},{9,8},{10,9},{11,1... | collective-permute-start | bytes 12296 | tf_op jit(solution)/shard_map/ppermute | solution.py:276
  69.7 12.1 %all-to-all-start = ((f32[32,1,128]{2,1,0:T(1,128)}), f32[32,1,128]{2,1,0:T(1,128)S(1)}, u32[]{:S(2)}, u32[]{:S(2)}) async-start(f32[32,1,128]{2,1,0:T(1,128)} %broadcast_in_dim.3), calls=%async_computation | async-start | bytes 32768 | tf_op jit(solution)/shard_map/all_to_all | solution.py:294
  (27 other events, 95.5 us)

commit v8 on v7

--- a/solution.py
+++ b/solution.py
@@ -1,5 +1,4 @@
 import functools
-import math
 
 import jax
 import jax.numpy as jnp
@@ -281,17 +280,13 @@
         return lax.ppermute(sends[0], "gx", self.ring_x), lax.ppermute(sends[1], "gx", self.back(self.ring_x))
 
     def near(self, values, x=None, y=None, z=None):
-        ring = [(j, (j + 1) % self.sizes[1]) for j in range(self.sizes[1])]
         forth, back = self.z(*(z or (values, values)))
         from_x = self.x(x or (values, values))
-        to_high, to_low = y or (values, values)
-        low, high = lax.ppermute(to_high, "gy", ring), lax.ppermute(to_low, "gy", self.back(ring))
-        return (forth, back, *from_x, low, high)
-
-    def all(self, values):
-        total = math.prod(self.sizes)
-        copies = jnp.broadcast_to(values, (total, *values.shape))
-        return lax.all_to_all(copies, ("gx", "gy", "gz"), 0, 0, tiled=True)
+        return (forth, back, *from_x, *self.ring_y(*(y or (values, values))))
+
+    def ring_y(self, to_high, to_low):
+        ring = [(j, (j + 1) % self.sizes[1]) for j in range(self.sizes[1])]
+        return lax.ppermute(to_high, "gy", ring), lax.ppermute(to_low, "gy", self.back(ring))
 
     def y(self, inner, outer):
         return self.send(inner, self.inner), self.send(outer, self.outer)
@@ -735,6 +730,17 @@
         out[2 * HALO, :SUB] = coarse[...]
 
 
+def three_kernel(flags, low, mid, high, out):
+    row = row_no(out.shape)
+    out[...] = jnp.where(row == 0, low[...], jnp.where(row == 1, mid[...], high[...]))
+
+
+def nine_kernel(flags, low, mid, high, out):
+    out[...] = jnp.zeros(out.shape, F32)
+    for n, ref in enumerate((low, mid, high)):
+        out[3 * n : 3 * n + 3] = ref[:3]
+
+
 def lift_kernel(flags, wide_ref, forth, back, main, ends):
     frame = Frame(wide_ref.shape[1] - 2 * HALO, wide_ref.shape[2] - 2 * (SUB + HALO))
     tall = frame.tall
@@ -745,7 +751,7 @@
         ends[s] = values.astype(jnp.int32)
 
 
-def post_kernel(sizes, flags, table, labels, end_labels, wide_ref, forth, back, *refs):
+def post_kernel(flags, table, table_forth, table_back, labels, end_labels, wide_ref, forth, back, *refs):
     (wx, wy, wz, inv_diag, start), ends = refs[:5], refs[5:11]
     out, one, two, one_ends, two_ends = refs[11:]
     nx, ny = out.shape[0], out.shape[1]
@@ -754,15 +760,13 @@
     ex, ey, ez_up, ez_low, inv_ends, start_ends = ends
     for ref in (one, two, one_ends, two_ends):
         clear_spares(ref, frame)
-    place = [lax.axis_index(a) for a in ("gx", "gy", "gz")]
     row, lane = row_no((tall, LANES)), lane_no((tall, LANES))
+    under, over = sides(flags, table_forth[...], table_back[...])
+    tables = {-1: under, 0: table[...], 1: over}
 
     def table_at(dx, dz):
-        tables = []
-        for dy in (-1, 0, 1):
-            at = [jnp.clip(p + d, 0, n - 1) for p, d, n in zip(place, (dx, dy, dz), sizes)]
-            tables.append(table[(at[0] * sizes[1] + at[1]) * sizes[2] + at[2]])
-        return jnp.where(row < HALO, tables[0], jnp.where(row < HALO + ny, tables[1], tables[2]))
+        low, mid, high = (tables[dz][3 * n + dx + 1 : 3 * n + dx + 2] for n in range(3))
+        return jnp.where(row < HALO, low, jnp.where(row < HALO + ny, mid, high))
 
     for x_from, x_to, dx in ((0, HALO, -1), (HALO, HALO + nx, 0), (HALO + nx, wide, 1)):
         values = table_at(dx, 0)
@@ -900,10 +904,13 @@
     lifts = call(lift_kernel, outs)(*halo)
     for _ in range(KC - 4):
         coarse, _ = turn()
-    table = links.all(coarse[:1])
+    from_x = links.x([coarse] * n_send)
+    three = call(three_kernel, shaped(SUB, AGG))(from_x[0], coarse, from_x[-1])
+    low, high = links.ring_y(three, three)
+    nine = call(nine_kernel, shaped(2 * SUB, AGG))(low, three, high)
+    tables = (nine, *links.z(nine, nine))
     scratch = [pltpu.VMEM(frame.main, F32)] * 2 + [pltpu.VMEM(frame.ends, F32)] * 2
-    kernel = functools.partial(post_kernel, links.sizes)
-    return call(kernel, shaped(nx, ny, nz), scratch, limit=24)(table, *lifts, *halo, *fields)
+    return call(post_kernel, shaped(nx, ny, nz), scratch, limit=24)(*tables, *lifts, *halo, *fields)
 
 
 def solution(mesh):

time: 93.2 us -> 85.3 us (0.915)
  local copies, waits for them, and re-layouts: 6.75 us -> 0 us
  starting transfers between devices: 40.2 us -> 39 us
    all_to_all x1 -> x0, waiting for transfers between devices: 6.51 us -> none  [all(): return lax.all_to_all(copies, ('gx', 'gy', 'gz'), 0, 0, tiled=True)]
    unnamed x20 -> x0, local copies, waits for them, and re-layouts: 6.12 us -> none
    all_to_all x1 -> x0, starting transfers between devices: 4.92 us -> none  [all(): return lax.all_to_all(copies, ('gx', 'gy', 'gz'), 0, 0, tiled=True)]
    ppermute x14 -> x16, waiting for transfers between devices: 3.39 us -> 6.17 us  [the longest x8 4.94 us: ring_y(): lax.ppermute(to_high, 'gy', ring)]
    ppermute x8 -> x9, waiting for transfers between devices: 3.24 us -> 5.68 us  [x(): return (lax.ppermute(sends[0], 'gx', self.ring_x),)]
    ppermute x18 -> x20, starting transfers between devices: 17.7 us -> 19.8 us  [send(): return lax.ppermute(values, ('gx', 'gy', 'gz'), pairs)]
    ppermute x18 -> x20, waiting for transfers between devices: 5.12 us -> 6.8 us  [send(): return lax.ppermute(values, ('gx', 'gy', 'gz'), pairs)]
    ppermute x8 -> x9, starting transfers between devices: 10.9 us -> 12.2 us  [x(): return (lax.ppermute(sends[0], 'gx', self.ring_x),)]
  transfers between devices with their start and end apart: 41 -> 45, of which waited for: 17 -> 20; matrix products, arithmetic and copies ran while one was open for 0% -> 0% of each run, Pallas kernels for 15% -> 16%
where the time goes in v8:
time: 85.3 us; the launch traced here: 85.1 us
  starting transfers between devices  39 us (46%)
  Pallas kernels  27.2 us (32%)
  waiting for transfers between devices  18.6 us (22%)
    pallas_call x27, Pallas kernels, run(): pl.pallas_call(placed, out_shape=outs, in_specs=in_specs or [VMEM] * len(...  27.2 us
    ppermute x20, starting transfers between devices, send(): return lax.ppermute(values, ('gx', 'gy', 'gz'), pairs)  19.8 us
    ppermute x9, starting transfers between devices, x(): return (lax.ppermute(sends[0], 'gx', self.ring_x),)  12.2 us
    ppermute x20, waiting for transfers between devices, send(): return lax.ppermute(values, ('gx', 'gy', 'gz'), pairs)  6.8 us
    ppermute x8, starting transfers between devices, ring_y(): lax.ppermute(to_low, 'gy', self.back(ring))  6.17 us
    ppermute x9, waiting for transfers between devices, x(): return (lax.ppermute(sends[0], 'gx', self.ring_x),)  5.68 us
    ppermute x8, waiting for transfers between devices, ring_y(): lax.ppermute(to_high, 'gy', ring)  4.94 us
  transfers between devices with their start and end apart: 45, of which 20 were waited for; matrix products, arithmetic and copies ran while one was open for 0% of the time, Pallas kernels for 16%

profile of v8, /device:TPU:0, one launch (start us, length us, event | category | flops | bytes accessed | tf_op | source)
XLA Modules:
  0.0 85.1 jit_solution(17461150017116545570)
XLA Ops:
  0.9 3.0 %collective-permute-start = (f32[11,32,128]{2,1,0:T(8,128)S(1)}, f32[11,32,128]{2,1,0:T(8,128)S(1)}, u32[]{:S(2)}, u32[]{:S(2)}) collective-permute-start(f32[11,32,128]{2,1,0:T(8,128)S(1)} %shard_map.46.refs_4_.refs_3_), channel_id=1, source_target_pairs={{0,16},{16,0},{1,17},{17,1},{2,18},{18,2},{3,19},{19,3},{4,20},{20... | collective-permute-start | bytes 540680 | tf_op jit(solution)/shard_map/ppermute | solution.py:279
  5.2 1.6 %shard_map.48 = (f32[12,8,128]{2,1,0:T(8,128)S(1)}, f32[3,12,8,128]{3,2,1,0:T(8,128)S(1)}, f32[3,12,8,128]{3,2,1,0:T(8,128)S(1)}, f32[12,8,128]{2,1,0:T(8,128)S(...) custom-call(f32[24,32,128]{2,1,0:T(8,128)S(1)} %get-tuple-element.56.refs_0_, ...), custom_call_target="tpu_custom_call" | custom-call | flops 1000000 | bytes 100000 | tf_op jit(solution)/shard_map/pallas_call | solution.py:36
  6.8 1.4 %shard_map.49.refs_4_ = f32[128,256]{1,0:T(8,128)S(1)} custom-call(f32[12,8,128]{2,1,0:T(8,128)S(1)} %get-tuple-element.59.refs_0_.refs_12_, f32[3,12,8,128]{3,2,1,0:T(8,128)S(1)} %get-tuple-element.60.refs_1_, f32[3,12,8,128]{3,2,1,0:T(8,128)S(1)} %get-tuple-element.61.refs_2_, f32[12,8,128]{2,1,0:T(8,128)S(1)} %get-tuple-element.62.refs_3_, ...), custom_call_target="tpu_custom_call" | custom-call | flops 1000000 | bytes 100000 | tf_op jit(solution)/shard_map/pallas_call | solution.py:36
  8.6 1.8 %collective-permute-start.2 = (f32[400,128]{1,0:T(8,128)S(1)}, f32[400,128]{1,0:T(8,128)S(1)}, u32[]{:S(2)}, u32[]{:S(2)}) collective-permute-start(f32[400,128]{1,0:T(8,128)S(1)} %get-tuple-element.69), channel_id=1, source_target_pairs={{0,16},{1,17},{2,18},{3,19},{4,8},{5,9},{6,10},{7,11},{8,4},{9,5},... | collective-permute-start | bytes 614408 | tf_op jit(solution)/shard_map/ppermute | solution.py:275
  10.5 3.3 %shard_map.51.refs_4_ = f32[128,256]{1,0:T(8,128)S(1)} custom-call(f32[12,8,128]{2,1,0:T(8,128)S(1)} %get-tuple-element.59.refs_0_.refs_12_, f32[3,12,8,128]{3,2,1,0:T(8,128)S(1)} %get-tuple-element.60.refs_1_, f32[3,12,8,128]{3,2,1,0:T(8,128)S(1)} %get-tuple-element.61.refs_2_, f32[12,8,128]{2,1,0:T(8,128)S(1)} %get-tuple-element.62.refs_3_, ...), custom_call_target="tpu_custom_call" | custom-call | flops 1000000 | bytes 100000 | tf_op jit(solution)/shard_map/pallas_call | solution.py:36
  15.4 1.7 %collective-permute-start.3 = (f32[136,128]{1,0:T(8,128)S(1)}, f32[136,128]{1,0:T(8,128)S(1)}, u32[]{:S(2)}, u32[]{:S(2)}) collective-permute-start(f32[136,128]{1,0:T(8,128)S(1)} %get-tuple-element.72.refs_5_.refs_1_), channel_id=1, source_target_pairs={{0,1},{1,2},{2,3},{3,7},{7,6},{6,5},{5,4},{4,0},{8,9},{9,10},{10,1... | collective-permute-start | bytes 208904 | tf_op jit(solution)/shard_map/ppermute | solution.py:275
  17.1 1.8 %shard_map.54 = (bf16[128,256]{1,0:T(8,128)(2,1)S(1)}, f32[8,128]{1,0:T(8,128)S(1)}) custom-call(f32[12,8,128]{2,1,0:T(8,128)S(1)} %get-tuple-element.59.refs_0_.refs_12_, f32[3,12,8,128]{3,2,1,0:T(8,128)S(1)} %get-tuple-element.60.refs_1_, f32[3,12,8,128]{3,2,1,0:T(8,128)S(1)} %get-tuple-element.61.refs_2_, f32[12,8,128]{2,1,0:T(8,128)S(1)} %get-tuple-element.62.refs_3_, ...), custom_call_target="tpu_custom_call" | custom-call | flops 1000000 | bytes 100000 | tf_op jit(solution)/shard_map/pallas_call | solution.py:36
  18.9 1.4 %shard_map.55 = (f32[32,56,128]{2,1,0:T(8,128)S(1)}, f32[32,56,128]{2,1,0:T(8,128)S(1)}, f32[32,56,128]{2,1,0:T(8,128)S(1)}, f32[32,56,128]{2,1,0:T(8,128)S(1)}, f32[40,128]{1,0:T(8,128)S(1)}) custom-call(f32[3,32,56,128]{3,2,1,0:T(8,128)S(1)} %get-tuple-element.75.refs_0_, f32[136,128]{1,0:T(8,128)S(1)} %get-tuple-element.72.refs_5_.refs_1_), custom_call_target="tpu_custom_call" | custom-call | flops 1000000 | bytes 100000 | tf_op jit(solution)/shard_map/pallas_call | solution.py:36
  20.3 5.0 %shard_map.56 = (f32[32,56,128]{2,1,0:T(8,128)S(1)}, f32[32,56,128]{2,1,0:T(8,128)S(1)}, f32[2,56,128]{2,1,0:T(8,128)S(1)}, f32[2,56,128]{2,1,0:T(8,128)S(1)}, f...) custom-call(f32[3,32,56,128]{3,2,1,0:T(8,128)S(1)} %get-tuple-elemen, ...), custom_call_target="tpu_custom_call" | custom-call | flops 1000000 | bytes 100000 | tf_op jit(solution)/shard_map/pallas_call | solution.py:36
  25.3 1.8 %collective-permute-start.7 = (f32[9,32,128]{2,1,0:T(8,128)S(1)}, f32[9,32,128]{2,1,0:T(8,128)S(1)}, u32[]{:S(2)}, u32[]{:S(2)}) collective-permute-start(f32[9,32,128]{2,1,0:T(8,128)S(1)} %shard_map.58), channel_id=1, source_target_pairs={{0,16},{16,0},{1,17},{17,1},{2,18},{18,2},{3,19},{19,3},{4,20},{20... | collective-permute-start | bytes 442376 | tf_op jit(solution)/shard_map/ppermute | solution.py:279
  29.6 1.7 %shard_map.57.refs_0_ = bf16[768,256]{1,0:T(8,128)(2,1)S(1)} custom-call(bf16[128,256]{1,0:T(8,128)(2,1)S(1)} %get-tuple-element.73.refs_0_, f32[6,8,128]{2,1,0:T(8,128)S(1)} %get-tuple-element.74.refs_13_.refs_1_, f32[6,8,128]{2,1,0:T(8,128)S(1)} %get-tuple-element.83.refs_2_, f32[6,8,128]{2,1,0:T(8,128)S(1)} %get-tuple-element.84.refs_3_), custom_call_target="tpu_custom_call" | custom-call | flops 1000000 | bytes 100000 | tf_op jit(solution)/shard_map/pallas_call | solution.py:36
  37.1 1.4 %collective-permute-done.13.refs_7_.refs_3_ = f32[264,128]{1,0:T(8,128)S(1)} collective-permute-done((f32[264,128]{1,0:T(8,128)S(1)}, f32[264,128]{1,0:T(8,128)S(1)}, u32[]{:S(2)}, u32[]{:S(2)}) %collective-permute-start.13) | collective-permute-done | bytes 135200 | tf_op jit(solution)/shard_map/ppermute | solution.py:289
  39.0 1.6 %collective-permute-start.15 = (f32[88,128]{1,0:T(8,128)S(1)}, f32[88,128]{1,0:T(8,128)S(1)}, u32[]{:S(2)}, u32[]{:S(2)}) collective-permute-start(f32[88,128]{1,0:T(8,128)S(1)} %get-tuple-element.94), channel_id=1, source_target_pairs={{0,1},{1,2},{2,3},{3,7},{7,6},{6,5},{5,4},{4,0},{8,9},{9,10},{10,1... | collective-permute-start | bytes 135176 | tf_op jit(solution)/shard_map/ppermute | solution.py:275
  42.2 1.7 %collective-permute-done.18.refs_7_ = f32[8,128]{1,0:T(8,128)S(1)} collective-permute-done((f32[8,128]{1,0:T(8,128)S(1)}, f32[8,128]{1,0:T(8,128)S(1)}, u32[]{:S(2)}, u32[]{:S(2)}) %collective-permute-start.18) | collective-permute-done | bytes 4128 | tf_op jit(solution)/shard_map/ppermute | solution.py:289
  45.4 1.4 %collective-permute-start.22 = (f32[8,128]{1,0:T(8,128)S(1)}, f32[8,128]{1,0:T(8,128)S(1)}, u32[]{:S(2)}, u32[]{:S(2)}) collective-permute-start(f32[8,128]{1,0:T(8,128)S(1)} %shard_map.64.refs_3_), channel_id=1, source_target_pairs={{0,16},{16,0},{1,17},{17,1},{2,18},{18,2},{3,19},{19,3},{4,20},{20... | collective-permute-start | bytes 12296 | tf_op jit(solution)/shard_map/ppermute | solution.py:279
  47.5 1.3 %collective-permute-start.20 = (f32[8,128]{1,0:T(8,128)S(1)}, f32[8,128]{1,0:T(8,128)S(1)}, u32[]{:S(2)}, u32[]{:S(2)}) collective-permute-start(f32[8,128]{1,0:T(8,128)S(1)} %shard_map.64.refs_3_), channel_id=1, source_target_pairs={{0,1},{1,2},{2,3},{3,7},{7,6},{6,5},{5,4},{4,0},{8,9},{9,10},{10,1... | collective-permute-start | bytes 12296 | tf_op jit(solution)/shard_map/ppermute | solution.py:275
  49.0 1.4 %collective-permute-done.21.refs_5_ = f32[8,128]{1,0:T(8,128)S(1)} collective-permute-done((f32[8,128]{1,0:T(8,128)S(1)}, f32[8,128]{1,0:T(8,128)S(1)}, u32[]{:S(2)}, u32[]{:S(2)}) %collective-permute-start.21) | collective-permute-done | bytes 4128 | tf_op jit(solution)/shard_map/ppermute | solution.py:275
  56.7 1.4 %collective-permute-start.34 = (f32[8,128]{1,0:T(8,128)S(1)}, f32[8,128]{1,0:T(8,128)S(1)}, u32[]{:S(2)}, u32[]{:S(2)}) collective-permute-start(f32[8,128]{1,0:T(8,128)S(1)} %shard_map.66.refs_3_), channel_id=1, source_target_pairs={{4,0},{8,4},{12,8},{0,12},{5,1},{9,5},{13,9},{1,13},{6,2},{10,6},{... | collective-permute-start | bytes 12296 | tf_op jit(solution)/shard_map/ppermute | solution.py:289
  62.9 1.3 %collective-permute-start.39 = (f32[8,128]{1,0:T(8,128)S(1)}, f32[8,128]{1,0:T(8,128)S(1)}, u32[]{:S(2)}, u32[]{:S(2)}) collective-permute-start(f32[8,128]{1,0:T(8,128)S(1)} %shard_map.67.refs_3_), channel_id=1, source_target_pairs={{4,0},{8,4},{12,8},{0,12},{5,1},{9,5},{13,9},{1,13},{6,2},{10,6},{... | collective-permute-start | bytes 12296 | tf_op jit(solution)/shard_map/ppermute | solution.py:289
  70.1 2.5 %collective-permute-done.40.refs_0_.refs_2_ = f32[8,128]{1,0:T(8,128)S(1)} collective-permute-done((f32[8,128]{1,0:T(8,128)S(1)}, f32[8,128]{1,0:T(8,128)S(1)}, u32[]{:S(2)}, u32[]{:S(2)}) %collective-permute-start.40) | collective-permute-done | bytes 4128 | tf_op jit(solution)/shard_map/ppermute | solution.py:279
  74.2 1.7 %collective-permute-done.41.refs_0_ = f32[8,128]{1,0:T(8,128)S(1)} collective-permute-done((f32[8,128]{1,0:T(8,128)S(1)}, f32[8,128]{1,0:T(8,128)S(1)}, u32[]{:S(2)}, u32[]{:S(2)}) %collective-permute-start.41) | collective-permute-done | bytes 4128 | tf_op jit(solution)/shard_map/ppermute | solution.py:289
  75.9 2.0 %collective-permute-start.43 = (f32[16,128]{1,0:T(8,128)S(1)}, f32[16,128]{1,0:T(8,128)S(1)}, u32[]{:S(2)}, u32[]{:S(2)}) collective-permute-start(f32[16,128]{1,0:T(8,128)S(1)} %shard_map.70.refs_0_), channel_id=1, source_target_pairs={{0,1},{1,2},{2,3},{3,7},{7,6},{6,5},{5,4},{4,0},{8,9},{9,10},{10,1... | collective-permute-start | bytes 24584 | tf_op jit(solution)/shard_map/ppermute | solution.py:275
  77.9 1.6 %collective-permute-done.44.refs_2_ = f32[16,128]{1,0:T(8,128)S(1)} collective-permute-done((f32[16,128]{1,0:T(8,128)S(1)}, f32[16,128]{1,0:T(8,128)S(1)}, u32[]{:S(2)}, u32[]{:S(2)}) %collective-permute-start.44) | collective-permute-done | bytes 8224 | tf_op jit(solution)/shard_map/ppermute | solution.py:275
  79.5 5.6 %shard_map.72 = f32[24,32,128]{2,1,0:T(8,128)} custom-call(f32[16,128]{1,0:T(8,128)S(1)} %shard_map.70.refs_0_, f32[16,128]{1,0:T(8,128)S(1)} %collective-permute-done.43.refs_1_, f32[16,128]{1,0:T(8,128)S(1)} %collective-permute-done.44.refs_2_, s32[16,40,128]{2,1,0:T(8,128)S(1)} %get-tuple-element.97.refs_3_, s32[2,40,128]{2,1,0:T(8,128)S(1)} %get-tuple-element.98.refs_4_, ...), custom_call_target="tpu_custom_call" | custom-call | flops 1000000 | bytes 100000 | tf_op jit(solution)/shard_map/pallas_call | solution.py:36
  (93 shorter events, 35.4 us)
Async XLA Ops:
  0.9 7.6 %collective-permute-start = (f32[11,32,128]{2,1,0:T(8,128)S(1)}, f32[11,32,128]{2,1,0:T(8,128)S(1)}, u32[]{:S(2)}, u32[]{:S(2)}) collective-permute-start(f32[11,32,128]{2,1,0:T(8,128)S(1)} %shard_map.46.refs_4_.refs_3_), channel_id=1, source_target_pairs={{0,16},{16,0},{1,17},{17,1},{2,18},{18,2},{3,19},{19,3},{4,20},{20... | collective-permute-start | bytes 540680 | tf_op jit(solution)/shard_map/ppermute | solution.py:279
  8.6 5.9 %collective-permute-start.2 = (f32[400,128]{1,0:T(8,128)S(1)}, f32[400,128]{1,0:T(8,128)S(1)}, u32[]{:S(2)}, u32[]{:S(2)}) collective-permute-start(f32[400,128]{1,0:T(8,128)S(1)} %get-tuple-element.69), channel_id=1, source_target_pairs={{0,16},{1,17},{2,18},{3,19},{4,8},{5,9},{6,10},{7,11},{8,4},{9,5},... | collective-permute-start | bytes 614408 | tf_op jit(solution)/shard_map/ppermute | solution.py:275
  10.4 4.1 %collective-permute-start.1 = (f32[400,128]{1,0:T(8,128)S(1)}, f32[400,128]{1,0:T(8,128)S(1)}, u32[]{:S(2)}, u32[]{:S(2)}) collective-permute-start(f32[400,128]{1,0:T(8,128)S(1)} %get-tuple-element.65.refs_5_), channel_id=1, source_target_pairs={{0,4},{1,5},{2,6},{3,7},{4,0},{5,1},{6,2},{7,3},{8,12},{9,13},{10,... | collective-permute-start | bytes 614408 | tf_op jit(solution)/shard_map/ppermute | solution.py:275
  15.1 5.2 %collective-permute-start.4 = (f32[136,128]{1,0:T(8,128)S(1)}, f32[136,128]{1,0:T(8,128)S(1)}, u32[]{:S(2)}, u32[]{:S(2)}) collective-permute-start(f32[136,128]{1,0:T(8,128)S(1)} %get-tuple-element.76), channel_id=1, source_target_pairs={{1,0},{2,1},{3,2},{7,3},{6,7},{5,6},{4,5},{0,4},{9,8},{10,9},{11,1... | collective-permute-start | bytes 208904 | tf_op jit(solution)/shard_map/ppermute | solution.py:275
  15.4 4.8 %collective-permute-start.3 = (f32[136,128]{1,0:T(8,128)S(1)}, f32[136,128]{1,0:T(8,128)S(1)}, u32[]{:S(2)}, u32[]{:S(2)}) collective-permute-start(f32[136,128]{1,0:T(8,128)S(1)} %get-tuple-element.72.refs_5_.refs_1_), channel_id=1, source_target_pairs={{0,1},{1,2},{2,3},{3,7},{7,6},{6,5},{5,4},{4,0},{8,9},{9,10},{10,1... | collective-permute-start | bytes 208904 | tf_op jit(solution)/shard_map/ppermute | solution.py:275
  25.3 6.1 %collective-permute-start.7 = (f32[9,32,128]{2,1,0:T(8,128)S(1)}, f32[9,32,128]{2,1,0:T(8,128)S(1)}, u32[]{:S(2)}, u32[]{:S(2)}) collective-permute-start(f32[9,32,128]{2,1,0:T(8,128)S(1)} %shard_map.58), channel_id=1, source_target_pairs={{0,16},{16,0},{1,17},{17,1},{2,18},{18,2},{3,19},{19,3},{4,20},{20... | collective-permute-start | bytes 442376 | tf_op jit(solution)/shard_map/ppermute | solution.py:279
  27.1 4.3 %collective-permute-start.9 = (f32[8,128]{1,0:T(8,128)S(1)}, f32[8,128]{1,0:T(8,128)S(1)}, u32[]{:S(2)}, u32[]{:S(2)}) collective-permute-start(f32[8,128]{1,0:T(8,128)S(1)} %get-tuple-element.85.refs_2_.refs_1_.refs_3_), channel_id=1, source_target_pairs={{4,0},{8,4},{12,8},{0,12},{5,1},{9,5},{13,9},{1,13},{6,2},{10,6},{... | collective-permute-start | bytes 12296 | tf_op jit(solution)/shard_map/ppermute | solution.py:289
  27.1 4.3 %collective-permute-start.8 = (f32[8,128]{1,0:T(8,128)S(1)}, f32[8,128]{1,0:T(8,128)S(1)}, u32[]{:S(2)}, u32[]{:S(2)}) collective-permute-start(f32[8,128]{1,0:T(8,128)S(1)} %get-tuple-element.85.refs_2_.refs_1_.refs_3_), channel_id=1, source_target_pairs={{0,4},{4,8},{8,12},{12,0},{1,5},{5,9},{9,13},{13,1},{2,6},{6,10},{... | collective-permute-start | bytes 12296 | tf_op jit(solution)/shard_map/ppermute | solution.py:289
  27.6 3.8 %collective-permute-start.6 = (f32[8,128]{1,0:T(8,128)S(1)}, f32[8,128]{1,0:T(8,128)S(1)}, u32[]{:S(2)}, u32[]{:S(2)}) collective-permute-start(f32[8,128]{1,0:T(8,128)S(1)} %get-tuple-element.85.refs_2_.refs_1_.refs_3_), channel_id=1, source_target_pairs={{1,0},{2,1},{3,2},{7,3},{6,7},{5,6},{4,5},{0,4},{9,8},{10,9},{11,1... | collective-permute-start | bytes 12296 | tf_op jit(solution)/shard_map/ppermute | solution.py:275
  31.7 5.4 %collective-permute-start.14 = (f32[264,128]{1,0:T(8,128)S(1)}, f32[264,128]{1,0:T(8,128)S(1)}, u32[]{:S(2)}, u32[]{:S(2)}) collective-permute-start(f32[264,128]{1,0:T(8,128)S(1)} %get-tuple-element.90), channel_id=1, source_target_pairs={{4,0},{8,4},{12,8},{0,12},{5,1},{9,5},{13,9},{1,13},{6,2},{10,6},{... | collective-permute-start | bytes 405512 | tf_op jit(solution)/shard_map/ppermute | solution.py:289
  32.9 5.6 %collective-permute-start.13 = (f32[264,128]{1,0:T(8,128)S(1)}, f32[264,128]{1,0:T(8,128)S(1)}, u32[]{:S(2)}, u32[]{:S(2)}) collective-permute-start(f32[264,128]{1,0:T(8,128)S(1)} %get-tuple-element.89.refs_4_), channel_id=1, source_target_pairs={{0,4},{4,8},{8,12},{12,0},{1,5},{5,9},{9,13},{13,1},{2,6},{6,10},{... | collective-permute-start | bytes 405512 | tf_op jit(solution)/shard_map/ppermute | solution.py:289
  32.9 3.6 %collective-permute-start.12 = (f32[8,128]{1,0:T(8,128)S(1)}, f32[8,128]{1,0:T(8,128)S(1)}, u32[]{:S(2)}, u32[]{:S(2)}) collective-permute-start(f32[8,128]{1,0:T(8,128)S(1)} %shard_map.59.refs_2_.refs_3_), channel_id=1, source_target_pairs={{0,16},{16,0},{1,17},{17,1},{2,18},{18,2},{3,19},{19,3},{4,20},{20... | collective-permute-start | bytes 12296 | tf_op jit(solution)/shard_map/ppermute | solution.py:279
  39.0 5.7 %collective-permute-start.15 = (f32[88,128]{1,0:T(8,128)S(1)}, f32[88,128]{1,0:T(8,128)S(1)}, u32[]{:S(2)}, u32[]{:S(2)}) collective-permute-start(f32[88,128]{1,0:T(8,128)S(1)} %get-tuple-element.94), channel_id=1, source_target_pairs={{0,1},{1,2},{2,3},{3,7},{7,6},{6,5},{5,4},{4,0},{8,9},{9,10},{10,1... | collective-permute-start | bytes 135176 | tf_op jit(solution)/shard_map/ppermute | solution.py:275
  40.6 4.1 %collective-permute-start.16 = (f32[88,128]{1,0:T(8,128)S(1)}, f32[88,128]{1,0:T(8,128)S(1)}, u32[]{:S(2)}, u32[]{:S(2)}) collective-permute-start(f32[88,128]{1,0:T(8,128)S(1)} %get-tuple-element.95), channel_id=1, source_target_pairs={{1,0},{2,1},{3,2},{7,3},{6,7},{5,6},{4,5},{0,4},{9,8},{10,9},{11,1... | collective-permute-start | bytes 135176 | tf_op jit(solution)/shard_map/ppermute | solution.py:275
  41.1 3.6 %collective-permute-start.17 = (f32[8,128]{1,0:T(8,128)S(1)}, f32[8,128]{1,0:T(8,128)S(1)}, u32[]{:S(2)}, u32[]{:S(2)}) collective-permute-start(f32[8,128]{1,0:T(8,128)S(1)} %shard_map.61.refs_5_.refs_3_), channel_id=1, source_target_pairs={{0,16},{16,0},{1,17},{17,1},{2,18},{18,2},{3,19},{19,3},{4,20},{20... | collective-permute-start | bytes 12296 | tf_op jit(solution)/shard_map/ppermute | solution.py:279
  44.9 4.0 %collective-permute-start.24 = (f32[8,128]{1,0:T(8,128)S(1)}, f32[8,128]{1,0:T(8,128)S(1)}, u32[]{:S(2)}, u32[]{:S(2)}) collective-permute-start(f32[8,128]{1,0:T(8,128)S(1)} %shard_map.64.refs_3_), channel_id=1, source_target_pairs={{4,0},{8,4},{12,8},{0,12},{5,1},{9,5},{13,9},{1,13},{6,2},{10,6},{... | collective-permute-start | bytes 12296 | tf_op jit(solution)/shard_map/ppermute | solution.py:289
  45.4 3.6 %collective-permute-start.22 = (f32[8,128]{1,0:T(8,128)S(1)}, f32[8,128]{1,0:T(8,128)S(1)}, u32[]{:S(2)}, u32[]{:S(2)}) collective-permute-start(f32[8,128]{1,0:T(8,128)S(1)} %shard_map.64.refs_3_), channel_id=1, source_target_pairs={{0,16},{16,0},{1,17},{17,1},{2,18},{18,2},{3,19},{19,3},{4,20},{20... | collective-permute-start | bytes 12296 | tf_op jit(solution)/shard_map/ppermute | solution.py:279
  46.9 3.6 %collective-permute-start.21 = (f32[8,128]{1,0:T(8,128)S(1)}, f32[8,128]{1,0:T(8,128)S(1)}, u32[]{:S(2)}, u32[]{:S(2)}) collective-permute-start(f32[8,128]{1,0:T(8,128)S(1)} %shard_map.64.refs_3_), channel_id=1, source_target_pairs={{1,0},{2,1},{3,2},{7,3},{6,7},{5,6},{4,5},{0,4},{9,8},{10,9},{11,1... | collective-permute-start | bytes 12296 | tf_op jit(solution)/shard_map/ppermute | solution.py:275
  50.6 4.3 %collective-permute-start.29 = (f32[8,128]{1,0:T(8,128)S(1)}, f32[8,128]{1,0:T(8,128)S(1)}, u32[]{:S(2)}, u32[]{:S(2)}) collective-permute-start(f32[8,128]{1,0:T(8,128)S(1)} %shard_map.65.refs_3_), channel_id=1, source_target_pairs={{4,0},{8,4},{12,8},{0,12},{5,1},{9,5},{13,9},{1,13},{6,2},{10,6},{... | collective-permute-start | bytes 12296 | tf_op jit(solution)/shard_map/ppermute | solution.py:289
  56.7 4.5 %collective-permute-start.34 = (f32[8,128]{1,0:T(8,128)S(1)}, f32[8,128]{1,0:T(8,128)S(1)}, u32[]{:S(2)}, u32[]{:S(2)}) collective-permute-start(f32[8,128]{1,0:T(8,128)S(1)} %shard_map.66.refs_3_), channel_id=1, source_target_pairs={{4,0},{8,4},{12,8},{0,12},{5,1},{9,5},{13,9},{1,13},{6,2},{10,6},{... | collective-permute-start | bytes 12296 | tf_op jit(solution)/shard_map/ppermute | solution.py:289
  62.9 4.2 %collective-permute-start.39 = (f32[8,128]{1,0:T(8,128)S(1)}, f32[8,128]{1,0:T(8,128)S(1)}, u32[]{:S(2)}, u32[]{:S(2)}) collective-permute-start(f32[8,128]{1,0:T(8,128)S(1)} %shard_map.67.refs_3_), channel_id=1, source_target_pairs={{4,0},{8,4},{12,8},{0,12},{5,1},{9,5},{13,9},{1,13},{6,2},{10,6},{... | collective-permute-start | bytes 12296 | tf_op jit(solution)/shard_map/ppermute | solution.py:289
  68.9 3.7 %collective-permute-start.40 = (f32[8,128]{1,0:T(8,128)S(1)}, f32[8,128]{1,0:T(8,128)S(1)}, u32[]{:S(2)}, u32[]{:S(2)}) collective-permute-start(f32[8,128]{1,0:T(8,128)S(1)} %shard_map.68.refs_1_), channel_id=1, source_target_pairs={{0,16},{16,0},{1,17},{17,1},{2,18},{18,2},{3,19},{19,3},{4,20},{20... | collective-permute-start | bytes 12296 | tf_op jit(solution)/shard_map/ppermute | solution.py:279
  75.9 3.7 %collective-permute-start.44 = (f32[16,128]{1,0:T(8,128)S(1)}, f32[16,128]{1,0:T(8,128)S(1)}, u32[]{:S(2)}, u32[]{:S(2)}) collective-permute-start(f32[16,128]{1,0:T(8,128)S(1)} %shard_map.70.refs_0_), channel_id=1, source_target_pairs={{1,0},{2,1},{3,2},{7,3},{6,7},{5,6},{4,5},{0,4},{9,8},{10,9},{11,1... | collective-permute-start | bytes 24584 | tf_op jit(solution)/shard_map/ppermute | solution.py:275
  75.9 3.7 %collective-permute-start.43 = (f32[16,128]{1,0:T(8,128)S(1)}, f32[16,128]{1,0:T(8,128)S(1)}, u32[]{:S(2)}, u32[]{:S(2)}) collective-permute-start(f32[16,128]{1,0:T(8,128)S(1)} %shard_map.70.refs_0_), channel_id=1, source_target_pairs={{0,1},{1,2},{2,3},{3,7},{7,6},{6,5},{5,4},{4,0},{8,9},{9,10},{10,1... | collective-permute-start | bytes 24584 | tf_op jit(solution)/shard_map/ppermute | solution.py:275
  (21 other events, 64.0 us)

commit v9 on v8

--- a/solution.py
+++ b/solution.py
@@ -28,7 +28,7 @@
     return [jnp.asarray(flag, jnp.int32) for flag in flags]
 
 
-def call(kernel, outs, scratch=(), limit=16, flops=10**6, in_specs=None, aliases=None):
+def call(kernel, outs, scratch=(), limit=16, flops=10**6, in_specs=None, aliases=None, out_specs=None):
     def placed(*refs):
         kernel(places(), *refs)
 
@@ -37,7 +37,7 @@
             placed,
             out_shape=outs,
             in_specs=in_specs or [VMEM] * len(arrays),
-            out_specs=jax.tree.map(lambda _: VMEM, outs),
+            out_specs=out_specs or jax.tree.map(lambda _: VMEM, outs),
             scratch_shapes=list(scratch),
             input_output_aliases=aliases or {},
             compiler_params=pltpu.CompilerParams(vmem_limit_bytes=limit * 2**20),
@@ -357,13 +357,18 @@
     )
 
 
-def main_sum(frame, field, x, join, wx, wy, wz):
-    span, down = frame.span, pl.ds(SUB - 1, frame.tall)
-    here, face_z = field[x, span], wz[x, span]
-    total = wx[x, span] * field[x + 1, span] + wx[x - 1, span] * field[x - 1, span]
-    total = total + wy[x, span] * field[x, pl.ds(SUB + 1, frame.tall)] + wy[x, down] * field[x, down]
-    total = total + face_z * turned(here, -1, 1) + turned(face_z * here, 1, 1)
-    return total + at_edges(join, x)
+def main_sums(frame, field, xs, join, wx, wy, wz):
+    span = frame.span
+    slabs = [field[xs[0] - 1 + k, span] for k in range(len(xs) + 2)]
+    faces = [wx[xs[0] - 1 + k, span] for k in range(len(xs) + 1)]
+    totals = []
+    for k, x in enumerate(xs):
+        here, face_y, face_z = slabs[k + 1], wy[x, span], wz[x, span]
+        total = faces[k + 1] * slabs[k + 2] + faces[k] * slabs[k]
+        total = total + face_y * turned(here, -1, 0) + turned(face_y * here, 1, 0)
+        total = total + face_z * turned(here, -1, 1) + turned(face_z * here, 1, 1)
+        totals.append(total + at_edges(join, x))
+    return slabs[1:-1], totals
 
 
 def ends_sum(frame, ends, s, upper, lower, wx, wy, wz_up, wz_low):
@@ -401,13 +406,33 @@
     return jnp.where(at_low, flags[Y_LOW], jnp.where(at_high, flags[Y_HIGH], 1)).astype(F32)
 
 
-def fields_kernel(flags, wide_ref, _, wx, wy, wz, partial, cond_edges):
+def face_rows(count, flags, nb):
+    x = [(jnp.where(flags[IX] == 0, 1, 0), SUB)] if count == 2 else [(0, SUB), (1, SUB)]
+    return x + [(2, nb // 2), (3, nb // 2), (4, 2), (5, 2)]
+
+
+def add_rows(total, labels, b, values, c, rows=SUB):
+    iota = row_no((AGG, LANES)).astype(F32)
+    for r in range(rows):
+        row = pl.ds(r, 1)
+        total = total + jnp.where(labels[b, row] == iota, values[c, row], 0.0)
+    return total
+
+
+def pack_lanes(values):
+    lane = lane_no((2, LANES))
+    packed = values[:2]
+    for g in range(1, SUB):
+        packed = jnp.where(lane // 16 == g, turned(values[2 * g : 2 * g + 2], 16 * g, 1), packed)
+    return packed
+
+
+def fields_kernel(count, flags, wide_ref, face_label, inner_diag, wx, wy, wz, partial, cond_edges, face_weight, diag):
     frame = Frame(wx.shape[0] - 2 * HALO, wx.shape[1] - 2 * (SUB + HALO))
     wide, tall, span = frame.wide, frame.tall, frame.span
     last = HALO + frame.nx
     keep_y = faces_y_kept(flags, frame)
     inside = jnp.where(lane_no((1, LANES)) == LANES - 1, 0.0, 1.0)
-    clear_spares(wy, frame)
 
     def fields(xs, carry):
         before, edges = carry
@@ -430,13 +455,24 @@
 
     nothing = jnp.zeros((tall, LANES), F32)
     cond_edges[...] = batched(0, wide, fields, (nothing, nothing + 1.0), 4)[1]
-
-
-def fine_kernel(flags, wide_ref, forth, back, from_x_low, from_x_high, inner, outer, wx, wy, wz, partial, cond_edges,
-                block_label, face_label, inner_diag, *refs):
+    nb, ny = frame.nx // 2, frame.ny
+    for s, x in enumerate((HALO - 1, last - 1)):
+        rows = [wx[x, pl.ds(frame.own + c, ny // 2, stride=2)] for c in range(2)]
+        face_weight[s] = pack_rows(paired(rows[0] + rows[1]))
+    for s, at in ((2, frame.own - 1), (3, frame.own + ny - 1)):
+        lines = [wy[HALO + 2 * b, at : at + 1] + wy[HALO + 2 * b + 1, at : at + 1] for b in range(nb)]
+        face_weight[s, : nb // 2] = pack_rows(paired(jnp.concatenate(lines, axis=0)))
+    around = jnp.zeros((AGG, LANES), F32)
+    for s, rows in face_rows(count, flags, nb)[:-2]:
+        around = add_rows(around, face_label, s, face_weight, s, rows)
+    diag[...] = inner_diag[...] + lane_total(around)
+
+
+def fine_kernel(flags, wide_ref, forth, back, wx, wy, wz, partial, cond_edges, block_label, face_label, some_diag,
+                *refs):
     inv_diag, start = refs[:2]
     ends = refs[2:8]
-    pre, face_near, face_weight, scaled_rhs, scale, once, once_ends, res, diag, block_res = refs[8:]
+    pre, face_weight, scaled_rhs, scale, once, once_ends, res, diag, block_res = refs[8:]
     ex, ey, ez_up, ez_low, inv_ends, start_ends = ends
     nx, ny = pre.shape[0], pre.shape[1]
     frame = Frame(nx, ny)
@@ -444,7 +480,7 @@
     last = HALO + nx
     got = [sides(flags, forth[f * tall : (f + 1) * tall], back[f * tall : (f + 1) * tall]) for f in range(3)]
     (cond_below, cond_above), rhs_ends, absorb_ends = got
-    for ref in (start, once, ey, start_ends, once_ends):
+    for ref in (ey, start_ends, once_ends):
         clear_spares(ref, frame)
 
     lane = lane_no((1, LANES))
@@ -496,39 +532,31 @@
 
     def second(xs, carry):
         news = []
-        for x in xs:
-            total = main_sum(frame, start, x, join, wx, wy, wz)
-            news.append((2.0 - OMEGA_FINE) * start[x, span] + inv_diag[x, span] * total)
+        for x, here, total in zip(xs, *main_sums(frame, start, xs, join, wx, wy, wz)):
+            news.append((2.0 - OMEGA_FINE) * here + inv_diag[x, span] * total)
         for x, new in zip(xs, news):
             once[x, span] = new
         return carry
 
-    batched(HALO - 1, last + 1, second, 0)
+    batched(HALO - 1, last + 1, second, 0, 13 if (nx + 2) % 13 == 0 else 6)
     join2 = joined(end_low * once_ends[0, span], end_high * once_ends[1, span])
 
     def remainder(xs, carry):
         news = []
-        for x in xs:
-            total = main_sum(frame, once, x, join2, wx, wy, wz)
-            news.append(wide_ref[1, x, span] - diag[x, span] * once[x, span] + total)
+        for x, here, total in zip(xs, *main_sums(frame, once, xs, join2, wx, wy, wz)):
+            news.append(wide_ref[1, x, span] - diag[x, span] * here + total)
         for x, new in zip(xs, news):
             res[x - HALO, span] = new
         for x in xs:
             pre[x - HALO] = once[x, pl.ds(frame.own, ny)]
         return carry
 
-    batched(HALO, last, remainder, 0)
-
-    nb, half, width = nx // 2, ny // 2, LANES // 2
-    iota = row_no((AGG, LANES)).astype(F32)
+    batched(HALO, last, remainder, 0, 8)
+
+    nb, half = nx // 2, ny // 2
 
     def rows_at(ref, x, off):
         return ref[x, pl.ds(frame.own + off, half, stride=2)]
-
-    def add_rows(total, labels, b, values, c):
-        for r in range(SUB):
-            total = total + jnp.where(labels[b, r : r + 1] == iota, values[c, r : r + 1], 0.0)
-        return total
 
     def to_blocks(bs, carry):
         for b in bs:
@@ -538,56 +566,33 @@
 
     batched(0, nb, to_blocks, 0)
     zeros = jnp.zeros((AGG, LANES), F32)
-
-    def restrict(b, total):
-        return add_rows(total, block_label, b, block_res, b)
-
-    sums = lax.fori_loop(0, nb, restrict, zeros)
-
-    blank = jnp.zeros((half - nb, LANES), F32)
-    low_at, high_at = pl.ds(frame.own - 1, 1), pl.ds(frame.own + ny - 1, 1)
-    face_weight[0] = pack_rows(paired(rows_at(wx, HALO - 1, 0) + rows_at(wx, HALO - 1, 1)))
-    face_weight[1] = pack_rows(paired(rows_at(wx, last - 1, 0) + rows_at(wx, last - 1, 1)))
-    for s, at in ((2, low_at), (3, high_at)):
-        lines = [wy[HALO + 2 * b, at] + wy[HALO + 2 * b + 1, at] for b in range(nb)]
-        face_weight[s] = pack_rows(paired(jnp.concatenate(lines + [blank], axis=0)))
+    sums = lax.fori_loop(0, nb, lambda b, total: add_rows(total, block_label, b, block_res, b), zeros)
+
     lane = lane_no((half, LANES))
-    for s, (ref, side, layer_at) in ((4, (ez_up, 0, HALO - 1)), (5, (ez_low, 1, 0))):
+    around = zeros
+    for s, (ref, side, layer_at) in enumerate(((ez_up, 0, HALO - 1), (ez_low, 1, 0))):
         values = rows_at(ref, side, 0) + rows_at(ref, side, 1)
         values = values + turned(values, -HALO, 1)
         spot = jnp.minimum(2 * HALO * lane + HALO * HALO + layer_at, LANES - 1)
-        face_weight[s] = pack_rows(jnp.where(lane < nb, picked(values, spot), 0.0))
-    around = zeros
-    for s in range(6):
-        around = add_rows(around, face_label, s, face_weight, s)
-    scale[...] = OMEGA_COARSE / (inner_diag[...] + lane_total(around))
+        face_weight[s, :2] = pack_lanes(jnp.where(lane < nb, picked(values, spot), 0.0))
+        around = add_rows(around, face_label, 4 + s, face_weight, s, 2)
+    scale[...] = OMEGA_COARSE / (some_diag[...] + lane_total(around))
     scaled_rhs[...] = scale[...] * lane_total(sums)
 
-    at = sum(WIDTHS)
-    face_near[0] = pack_rows(from_x_low[at, :half])
-    face_near[1] = pack_rows(from_x_high[at, :half])
-    at = 3 * wide * HALO
-    for s, values in enumerate(sides(flags, outer[at : at + half], inner[at : at + half])):
-        face_near[2 + s] = pack_rows(values)
-    below, above = sides(flags, forth[3 * tall : 3 * tall + half], back[3 * tall : 3 * tall + half])
-    face_near[4] = pack_rows(below)
-    face_near[5] = pack_rows(above)
-
-
-def fill(left, right, labels, b, pairs):
+
+def tile_sum(tile, rows, label_at, pairs_at, group=4):
     iota = row_no((AGG, LANES)).astype(F32)
-    for r in range(SUB):
-        lanes = pl.ds(r * LANES, LANES)
-        row = pl.ds(r, 1)
-        left[:, lanes] = jnp.where(labels[b, row] == iota, 1.0, 0.0).astype(BF16)
-        held = sum(jnp.where(near[row] == iota, w[row], 0.0) for near, w in pairs)
-        high = held.astype(BF16)
-        right[:AGG, lanes] = high
-        right[AGG:, lanes] = (held - high.astype(F32)).astype(BF16)
-
-
-def product(left, right):
-    return lax.dot_general(left[...], right[...], (((1,), (1,)), ((), ())), preferred_element_type=F32)
+    for first in range(0, rows, group):
+        places, highs, lows = [], [], []
+        for r in range(first, min(first + group, rows)):
+            places.append(jnp.where(label_at(r) == iota, 1.0, 0.0).astype(BF16))
+            held = sum(jnp.where(near == iota, w, 0.0) for near, w in pairs_at(r))
+            highs.append(held.astype(BF16))
+            lows.append((held - highs[-1].astype(F32)).astype(BF16))
+        left = jnp.concatenate(places, axis=1)
+        right = jnp.concatenate([jnp.concatenate(highs, axis=1), jnp.concatenate(lows, axis=1)], axis=0)
+        tile = tile + lax.dot_general(left, right, (((1,), (1,)), ((), ())), preferred_element_type=F32)
+    return tile
 
 
 def both_halves(tile):
@@ -662,47 +667,54 @@
         low = jnp.where(lane == b, own[:, :1], low)
         high = jnp.where(lane == b, own[:, width - 1 : width], high)
     face_label[0], face_label[1] = block_label[0], block_label[nb - 1]
-    for s, values in enumerate((line[0], line[1], low, high)):
-        face_label[2 + s] = pack_rows(values)
+    for s in range(2):
+        face_label[2 + s, : nb // 2] = pack_rows(line[s, :nb])
+        face_label[4 + s, :2] = pack_lanes((low, high)[s])
 
 
 def own_kernel(first, last, total, flags, block_label, near, weights, inner, *refs):
     so_far, refs = (refs[0], refs[1:]) if first else (None, refs)
     refs = refs[1:]
-    iota = row_no((AGG, LANES)).astype(F32)
-
-    def step(bs, tile):
-        for k, b in enumerate(bs):
-            left, right = refs[-4 + 2 * (k % 2) :][:2]
-            fill(left, right, block_label, b, [(near.at[d, b], weights.at[d, b]) for d in range(3)])
-            tile = tile + product(left, right)
-        return tile
+
+    def step(b, tile):
+        def pairs_at(r):
+            return [(near[d, b, pl.ds(r, 1)], weights[d, b, pl.ds(r, 1)]) for d in range(3)]
+
+        return tile_sum(tile, SUB, lambda r: block_label[b, pl.ds(r, 1)], pairs_at)
 
     tile = so_far[...] if first else jnp.zeros((AGG, 2 * AGG), F32)
-    tile = batched(first, last, step, tile, 2)
+    tile = lax.fori_loop(first, last, step, tile)
     if last < total:
         refs[0][...] = tile
         return
-    out, inner_diag = refs[:2]
+    out, inner_diag = refs
     tile = both_halves(tile)
     keep_tile(out, 0, jnp.where(row_no((AGG, AGG)) == lane_no((AGG, AGG)), 0.0, tile + tile.T))
-
-    def gather(b, around):
-        for r in range(SUB):
-            around = around + jnp.where(block_label[b, r : r + 1] == iota, inner[b, r : r + 1], 0.0)
-        return around
-
-    inner_diag[...] = lane_total(lax.fori_loop(0, total, gather, jnp.zeros((AGG, LANES), F32)))
-
-
-def faces_kernel(count, flags, own, face_label, face_near, face_weight, out, *factors):
+    around = jnp.zeros((AGG, LANES), F32)
+    around = lax.fori_loop(0, total, lambda b, around: add_rows(around, block_label, b, inner, b), around)
+    inner_diag[...] = lane_total(around)
+
+
+def faces_kernel(count, nb, flags, own, face_label, weight_xy, weight_z, x_low, x_high, inner, outer, forth, back, out,
+                 near, weights):
     out[:AGG] = own[...]
-    s = jnp.where(flags[IX] == 0, 1, 0)
-    faces = ([s] if count == 2 else [0, 1]) + [2, 3, 4, 5]
-    for t, s in enumerate(faces):
-        left, right = factors[2 * (t % 2) :][:2]
-        fill(left, right, face_near, s, [(face_label.at[s], face_weight.at[s])])
-        keep_tile(out, t + 1, both_halves(product(left, right)))
+    at, half = x_low.shape[0] - 1, x_low.shape[1] // 2
+    near[0], near[1] = pack_rows(x_low[at, :half]), pack_rows(x_high[at, :half])
+    at = inner.shape[0] - half
+    for s, values in enumerate(sides(flags, outer[at:], inner[at:])):
+        near[2 + s, : nb // 2] = pack_rows(values[:nb])
+    at = forth.shape[0] - half
+    for s, values in enumerate(sides(flags, forth[at:], back[at:])):
+        near[4 + s, :2] = pack_lanes(values)
+    weights[:4], weights[4:] = weight_xy[...], weight_z[...]
+    for t, (s, rows) in enumerate(face_rows(count, flags, nb)):
+        tile = tile_sum(
+            jnp.zeros((AGG, 2 * AGG), F32),
+            rows,
+            lambda r, s=s: near[s, pl.ds(r, 1)],
+            lambda r, s=s: [(face_label[s, pl.ds(r, 1)], weights[s, pl.ds(r, 1)])],
+        )
+        keep_tile(out, t + 1, both_halves(tile))
 
 
 def turn_kernel(flags, tiles, scaled_rhs, scale, own, *refs):
@@ -753,12 +765,12 @@
 
 def post_kernel(flags, table, table_forth, table_back, labels, end_labels, wide_ref, forth, back, *refs):
     (wx, wy, wz, inv_diag, start), ends = refs[:5], refs[5:11]
-    out, one, two, one_ends, two_ends = refs[11:]
+    out, one, two, one_ends, two_ends, kept_out, sems = refs[11:]
     nx, ny = out.shape[0], out.shape[1]
     frame = Frame(nx, ny)
     wide, tall, span = frame.wide, frame.tall, frame.span
     ex, ey, ez_up, ez_low, inv_ends, start_ends = ends
-    for ref in (one, two, one_ends, two_ends):
+    for ref in (one_ends, two_ends):
         clear_spares(ref, frame)
     row, lane = row_no((tall, LANES)), lane_no((tall, LANES))
     under, over = sides(flags, table_forth[...], table_back[...])
@@ -785,6 +797,11 @@
         lifted = jnp.where(spot < HALO, below, jnp.where(spot < HALO + nx, inside, above))
         two_ends[s, span] = base + lifted
     kept = 1.0 - OMEGA_FINE
+
+    def result(at, count):
+        rows = pl.ds(at, count)
+        return pltpu.make_async_copy(kept_out.at[rows], out.at[rows], sems.at[at // count])
+
     buffers = ((two, two_ends), (one, one_ends), (two, two_ends), (one, one_ends))
     for s in range(POST):
         src, src_ends = buffers[s]
@@ -794,20 +811,21 @@
 
         def step(xs, edges, src=src, join=join, dst=dst, final=final):
             news = []
-            for x in xs:
-                here = src[x, span]
-                total = main_sum(frame, src, x, join, wx, wy, wz)
+            for x, here, total in zip(xs, *main_sums(frame, src, xs, join, wx, wy, wz)):
                 news.append(kept * here + start[x, span] + inv_diag[x, span] * total)
                 if not final:
                     edges = edge_step(here, x, edges)
             for x, new in zip(xs, news):
                 if final:
-                    out[x - HALO] = new[HALO : HALO + ny]
+                    kept_out[x - HALO] = new[HALO : HALO + ny]
                 else:
                     dst[x, span] = new
+            if final:
+                result(xs[0] - HALO, len(xs)).start()
             return edges
 
-        edges = batched(s + 1, wide - s - 1, step, jnp.zeros((tall, LANES), F32))
+        size = 8 if final else 10
+        edges = batched(s + 1, wide - s - 1, step, jnp.zeros((tall, LANES), F32), size)
         if not final:
             near = ends_near(src_ends[0, span], src_ends[1, span], edges)
             news = []
@@ -815,6 +833,8 @@
                 total = ends_sum(frame, src_ends, e, near[2 * e], near[2 * e + 1], ex, ey, ez_up, ez_low)
                 news.append(kept * src_ends[e, span] + start_ends[e, span] + inv_ends[e, span] * total)
             dst_ends[0, span], dst_ends[1, span] = news
+    for n in range(nx // 8):
+        result(8 * n, 8).wait()
 
 
 def body(links, right_side, conductance, absorption, block_agg):
@@ -842,18 +862,17 @@
     outs = [shaped(*blocks), shaped(3, *blocks), shaped(3, *blocks), shaped(*blocks), shaped(6, SUB, LANES)]
     outs += [shaped(nx, ny, nz)]
     scratch = [pltpu.VMEM((17, ny, LANES), F32), pltpu.VMEM((2, ny // 2, LANES), F32)]
-    pair = [pltpu.VMEM((AGG, SUB * LANES), BF16), pltpu.VMEM((2 * AGG, SUB * LANES), BF16)]
     *rows, face_label, fine_label = call(blocks_kernel, outs, scratch)(arrays[0], arrays[2], arrays[3], x_sends[0])
     block_label = rows[0]
-    bounds = (0, nb // 4, nb * 5 // 6, nb)
+    bounds = (0, nb * 5 // 12, nb)
     parts = []
 
     def own_part(p, sent):
         outs = [shaped(AGG, 2 * AGG)]
-        if p == 2:
+        if p == 1:
             outs = [jax.ShapeDtypeStruct((AGG, 2 * AGG), BF16), shaped(SUB, AGG)]
         kernel = functools.partial(own_kernel, bounds[p], bounds[p + 1], nb)
-        parts.append(call(kernel, outs, pair * 2)(*rows, *(parts[-1] if p else ()), sent))
+        parts.append(call(kernel, outs)(*rows, *(parts[-1] if p else ()), sent))
         return parts[-1]
 
     first = own_part(0, x_sends[0])
@@ -862,27 +881,29 @@
 
     sends = send_y(WIDTHS, arrays[:3], arrays[3], from_x, False)
     frames = framed(WIDTHS, arrays[:3], from_x, sends[0])
-    second = own_part(1, sends[0])
+    own_tile, inner_diag = own_part(1, sends[0])
     from_y = links.y(*sends)
-    from_y = lax.optimization_barrier((*from_y, *second))[:2]
+    *from_y, own_tile, inner_diag = lax.optimization_barrier((*from_y, own_tile, inner_diag))
     wide, *sends = send_z(WIDTHS, frames, from_y, arrays[3], False)
-    fields = call(fields_kernel, [shaped(*frame.main)] * 4 + [shaped(frame.tall, nz)], limit=24)(wide, sends[0])
-    own_tile, inner_diag = own_part(2, sends[0])
+    outs = [shaped(*frame.main)] * 4 + [shaped(frame.tall, nz), shaped(4, SUB, LANES), shaped(SUB, AGG)]
+    *fields, weight_xy, some_diag = call(functools.partial(fields_kernel, n_x), outs, limit=24)(
+        wide, face_label, inner_diag
+    )
     halo = (wide, *links.z(*sends))
     outs = [shaped(*frame.main)] * 2 + [shaped(*frame.ends)] * 6 + [shaped(nx, ny, nz)]
-    outs += [shaped(6, SUB, LANES)] * 2 + [shaped(SUB, AGG)] * 2
+    outs += [shaped(2, SUB, LANES)] + [shaped(SUB, AGG)] * 2
     scratch = [pltpu.VMEM(frame.main, F32), pltpu.VMEM(frame.ends, F32), pltpu.VMEM((nx, frame.rows, LANES), F32)]
     scratch += [pltpu.VMEM(frame.main, F32), pltpu.VMEM(blocks, F32)]
     got = call(fine_kernel, outs, scratch, limit=28)(
-        *halo, from_x[0], from_x[-1], *from_y, *fields, block_label, face_label, inner_diag
+        *halo, *fields, block_label, face_label, some_diag
     )
     fields, pre = (*fields[:3], *got[:8]), got[8]
-    face_near, face_weight, scaled_rhs, scale = got[9:]
+    weight_z, scaled_rhs, scale = got[9:]
     tiles = call(
-        functools.partial(faces_kernel, n_x),
+        functools.partial(faces_kernel, n_x, nb),
         jax.ShapeDtypeStruct(((n_send + 5) * AGG, 2 * AGG), BF16),
-        pair * 2,
-    )(own_tile, face_label, face_near, face_weight)
+        [pltpu.VMEM((6, SUB, LANES), F32)] * 2,
+    )(own_tile, face_label, weight_xy, weight_z, from_x[0], from_x[-1], *from_y, *halo[1:])
     coarse = scaled_rhs
 
     def turn(**more):
@@ -910,7 +931,10 @@
     nine = call(nine_kernel, shaped(2 * SUB, AGG))(low, three, high)
     tables = (nine, *links.z(nine, nine))
     scratch = [pltpu.VMEM(frame.main, F32)] * 2 + [pltpu.VMEM(frame.ends, F32)] * 2
-    return call(post_kernel, shaped(nx, ny, nz), scratch, limit=24)(*tables, *lifts, *halo, *fields)
+    scratch += [pltpu.VMEM((nx, ny, nz), F32), pltpu.SemaphoreType.DMA((nx // 8,))]
+    return call(post_kernel, shaped(nx, ny, nz), scratch, limit=24, out_specs=pl.BlockSpec(memory_space=pl.ANY))(
+        *tables, *lifts, *halo, *fields
+    )
 
 
 def solution(mesh):

time: 85.3 us -> 84.6 us (level)
  Pallas kernels: 27.2 us -> 24.5 us
  waiting for transfers between devices: 18.6 us -> 21.3 us
    ppermute x20, waiting for transfers between devices: 6.8 us -> 10.1 us  [send(): return lax.ppermute(values, ('gx', 'gy', 'gz'), pairs)]
    pallas_call x27 -> x26, Pallas kernels: 27.2 us -> 24.5 us  [run(): pl.pallas_call(placed, out_shape=outs, in_specs=in_specs or [VMEM] * len(...]
  transfers between devices with their start and end apart: 45 -> 45, of which waited for: 20 -> 22; matrix products, arithmetic and copies ran while one was open for 0% -> 0% of each run, Pallas kernels for 16% -> 14%
where the time goes in v9:
time: 84.6 us; the launch traced here: 84.4 us
  starting transfers between devices  38.4 us (45%)
  Pallas kernels  24.5 us (29%)
  waiting for transfers between devices  21.3 us (25%)
    pallas_call x26, Pallas kernels, run(): pl.pallas_call(placed, out_shape=outs, in_specs=in_specs or [VMEM] * len(...  24.5 us
    ppermute x20, starting transfers between devices, send(): return lax.ppermute(values, ('gx', 'gy', 'gz'), pairs)  19.1 us
    ppermute x9, starting transfers between devices, x(): return (lax.ppermute(sends[0], 'gx', self.ring_x),)  12 us
    ppermute x20, waiting for transfers between devices, send(): return lax.ppermute(values, ('gx', 'gy', 'gz'), pairs)  10.1 us
    ppermute x8, starting transfers between devices, ring_y(): lax.ppermute(to_low, 'gy', self.back(ring))  6.61 us
    ppermute x9, waiting for transfers between devices, x(): return (lax.ppermute(sends[0], 'gx', self.ring_x),)  5.3 us
    ppermute x8, waiting for transfers between devices, ring_y(): lax.ppermute(to_high, 'gy', ring)  4.63 us
  transfers between devices with their start and end apart: 45, of which 22 were waited for; matrix products, arithmetic and copies ran while one was open for 0% of the time, Pallas kernels for 14%

profile of v9, /device:TPU:0, one launch (start us, length us, event | category | flops | bytes accessed | tf_op | source)
XLA Modules:
  0.0 84.4 jit_solution(4981197726093134617)
XLA Ops:
  0.9 3.0 %collective-permute-start = (f32[11,32,128]{2,1,0:T(8,128)S(1)}, f32[11,32,128]{2,1,0:T(8,128)S(1)}, u32[]{:S(2)}, u32[]{:S(2)}) collective-permute-start(f32[11,32,128]{2,1,0:T(8,128)S(1)} %shard_map.46.refs_4_.refs_3_), channel_id=1, source_target_pairs={{0,16},{16,0},{1,17},{17,1},{2,18},{18,2},{3,19},{19,3},{4,20},{20... | collective-permute-start | bytes 540680 | tf_op jit(solution)/shard_map/ppermute | solution.py:279
  5.2 1.6 %shard_map.48 = (f32[12,8,128]{2,1,0:T(8,128)S(1)}, f32[3,12,8,128]{3,2,1,0:T(8,128)S(1)}, f32[3,12,8,128]{3,2,1,0:T(8,128)S(1)}, f32[12,8,128]{2,1,0:T(8,128)S(...) custom-call(f32[24,32,128]{2,1,0:T(8,128)S(1)} %get-tuple-element.59.refs_0_, ...), custom_call_target="tpu_custom_call" | custom-call | flops 1000000 | bytes 100000 | tf_op jit(solution)/shard_map/pallas_call | solution.py:36
  6.8 1.9 %shard_map.49.refs_4_ = f32[128,256]{1,0:T(8,128)S(1)} custom-call(f32[12,8,128]{2,1,0:T(8,128)S(1)} %get-tuple-element.63.refs_0_.refs_8_, f32[3,12,8,128]{3,2,1,0:T(8,128)S(1)} %get-tuple-element.64.refs_1_, f32[3,12,8,128]{3,2,1,0:T(8,128)S(1)} %get-tuple-element.65.refs_2_, f32[12,8,128]{2,1,0:T(8,128)S(1)} %get-tuple-element.66.refs_3_, ...), custom_call_target="tpu_custom_call" | custom-call | flops 1000000 | bytes 100000 | tf_op jit(solution)/shard_map/pallas_call | solution.py:36
  8.9 1.5 %collective-permute-start.2 = (f32[400,128]{1,0:T(8,128)S(1)}, f32[400,128]{1,0:T(8,128)S(1)}, u32[]{:S(2)}, u32[]{:S(2)}) collective-permute-start(f32[400,128]{1,0:T(8,128)S(1)} %get-tuple-element.69), channel_id=1, source_target_pairs={{0,16},{1,17},{2,18},{3,19},{4,8},{5,9},{6,10},{7,11},{8,4},{9,5},... | collective-permute-start | bytes 614408 | tf_op jit(solution)/shard_map/ppermute | solution.py:275
  10.6 3.6 %shard_map.51 = (bf16[128,256]{1,0:T(8,128)(2,1)S(1)}, f32[8,128]{1,0:T(8,128)S(1)}) custom-call(f32[12,8,128]{2,1,0:T(8,128)S(1)} %get-tuple-element.63.refs_0_.refs_8_, f32[3,12,8,128]{3,2,1,0:T(8,128)S(1)} %get-tuple-element.64.refs_1_, f32[3,12,8,128]{3,2,1,0:T(8,128)S(1)} %get-tuple-element.65.refs_2_, f32[12,8,128]{2,1,0:T(8,128)S(1)} %get-tuple-element.66.refs_3_, ...), custom_call_target="tpu_custom_call" | custom-call | flops 1000000 | bytes 100000 | tf_op jit(solution)/shard_map/pallas_call | solution.py:36
  15.4 1.6 %collective-permute-start.3 = (f32[136,128]{1,0:T(8,128)S(1)}, f32[136,128]{1,0:T(8,128)S(1)}, u32[]{:S(2)}, u32[]{:S(2)}) collective-permute-start(f32[136,128]{1,0:T(8,128)S(1)} %get-tuple-element.82), channel_id=1, source_target_pairs={{0,1},{1,2},{2,3},{3,7},{7,6},{6,5},{5,4},{4,0},{8,9},{9,10},{10,1... | collective-permute-start | bytes 208904 | tf_op jit(solution)/shard_map/ppermute | solution.py:275
  17.0 1.8 %shard_map.54 = (f32[32,56,128]{2,1,0:T(8,128)S(1)}, f32[32,56,128]{2,1,0:T(8,128)S(1)}, f32[32,56,128]{2,1,0:T(8,128)S(1)}, f32[32,56,128]{2,1,0:T(8,128)S(1)},...) custom-call(f32[3,32,56,128]{3,2,1,0:T(8,128)S(1)} %get-tuple-element.79.refs_0_, ...), custom_call_target="tpu_custom_call" | custom-call | flops 1000000 | bytes 100000 | tf_op jit(solution)/shard_map/pallas_call | solution.py:36
  19.1 2.2 %collective-permute-done.4.refs_2_.refs_9_ = f32[136,128]{1,0:T(8,128)S(1)} collective-permute-done((f32[136,128]{1,0:T(8,128)S(1)}, f32[136,128]{1,0:T(8,128)S(1)}, u32[]{:S(2)}, u32[]{:S(2)}) %collective-permute-start.4) | collective-permute-done | bytes 69664 | tf_op jit(solution)/shard_map/ppermute | solution.py:275
  21.3 4.5 %shard_map.55 = (f32[32,56,128]{2,1,0:T(8,128)S(1)}, f32[32,56,128]{2,1,0:T(8,128)S(1)}, f32[2,56,128]{2,1,0:T(8,128)S(1)}, f32[2,56,128]{2,1,0:T(8,128)S(1)}, f...) custom-call(f32[3,32,56,128]{3,2,1,0:T(8,128)S(1)} %get-tuple-elemen, ...), custom_call_target="tpu_custom_call" | custom-call | flops 1000000 | bytes 100000 | tf_op jit(solution)/shard_map/pallas_call | solution.py:36
  25.8 1.5 %collective-permute-start.7 = (f32[9,32,128]{2,1,0:T(8,128)S(1)}, f32[9,32,128]{2,1,0:T(8,128)S(1)}, u32[]{:S(2)}, u32[]{:S(2)}) collective-permute-start(f32[9,32,128]{2,1,0:T(8,128)S(1)} %shard_map.57), channel_id=1, source_target_pairs={{0,16},{16,0},{1,17},{17,1},{2,18},{18,2},{3,19},{19,3},{4,20},{20... | collective-permute-start | bytes 442376 | tf_op jit(solution)/shard_map/ppermute | solution.py:279
  28.3 1.6 %collective-permute-start.5 = (f32[8,128]{1,0:T(8,128)S(1)}, f32[8,128]{1,0:T(8,128)S(1)}, u32[]{:S(2)}, u32[]{:S(2)}) collective-permute-start(f32[8,128]{1,0:T(8,128)S(1)} %get-tuple-element.91.refs_2_.refs_1_.refs_3_), channel_id=1, source_target_pairs={{0,1},{1,2},{2,3},{3,7},{7,6},{6,5},{5,4},{4,0},{8,9},{9,10},{10,1... | collective-permute-start | bytes 12296 | tf_op jit(solution)/shard_map/ppermute | solution.py:275
  31.7 1.4 %collective-permute-start.14 = (f32[264,128]{1,0:T(8,128)S(1)}, f32[264,128]{1,0:T(8,128)S(1)}, u32[]{:S(2)}, u32[]{:S(2)}) collective-permute-start(f32[264,128]{1,0:T(8,128)S(1)} %get-tuple-element.96), channel_id=1, source_target_pairs={{4,0},{8,4},{12,8},{0,12},{5,1},{9,5},{13,9},{1,13},{6,2},{10,6},{... | collective-permute-start | bytes 405512 | tf_op jit(solution)/shard_map/ppermute | solution.py:289
  34.4 1.3 %collective-permute-start.10 = (f32[8,128]{1,0:T(8,128)S(1)}, f32[8,128]{1,0:T(8,128)S(1)}, u32[]{:S(2)}, u32[]{:S(2)}) collective-permute-start(f32[8,128]{1,0:T(8,128)S(1)} %shard_map.58.refs_2_.refs_3_), channel_id=1, source_target_pairs={{0,1},{1,2},{2,3},{3,7},{7,6},{6,5},{5,4},{4,0},{8,9},{9,10},{10,1... | collective-permute-start | bytes 12296 | tf_op jit(solution)/shard_map/ppermute | solution.py:275
  38.9 1.6 %collective-permute-start.15 = (f32[88,128]{1,0:T(8,128)S(1)}, f32[88,128]{1,0:T(8,128)S(1)}, u32[]{:S(2)}, u32[]{:S(2)}) collective-permute-start(f32[88,128]{1,0:T(8,128)S(1)} %get-tuple-element.100), channel_id=1, source_target_pairs={{0,1},{1,2},{2,3},{3,7},{7,6},{6,5},{5,4},{4,0},{8,9},{9,10},{10,1... | collective-permute-start | bytes 135176 | tf_op jit(solution)/shard_map/ppermute | solution.py:275
  42.5 1.7 %collective-permute-done.18.refs_7_ = f32[8,128]{1,0:T(8,128)S(1)} collective-permute-done((f32[8,128]{1,0:T(8,128)S(1)}, f32[8,128]{1,0:T(8,128)S(1)}, u32[]{:S(2)}, u32[]{:S(2)}) %collective-permute-start.18) | collective-permute-done | bytes 4128 | tf_op jit(solution)/shard_map/ppermute | solution.py:289
  56.6 1.3 %collective-permute-start.34 = (f32[8,128]{1,0:T(8,128)S(1)}, f32[8,128]{1,0:T(8,128)S(1)}, u32[]{:S(2)}, u32[]{:S(2)}) collective-permute-start(f32[8,128]{1,0:T(8,128)S(1)} %shard_map.65.refs_3_), channel_id=1, source_target_pairs={{4,0},{8,4},{12,8},{0,12},{5,1},{9,5},{13,9},{1,13},{6,2},{10,6},{... | collective-permute-start | bytes 12296 | tf_op jit(solution)/shard_map/ppermute | solution.py:289
  58.0 1.4 %collective-permute-start.32 = (f32[8,128]{1,0:T(8,128)S(1)}, f32[8,128]{1,0:T(8,128)S(1)}, u32[]{:S(2)}, u32[]{:S(2)}) collective-permute-start(f32[8,128]{1,0:T(8,128)S(1)} %shard_map.65.refs_3_), channel_id=1, source_target_pairs={{0,16},{16,0},{1,17},{17,1},{2,18},{18,2},{3,19},{19,3},{4,20},{20... | collective-permute-start | bytes 12296 | tf_op jit(solution)/shard_map/ppermute | solution.py:279
  60.0 1.4 %collective-permute-start.30 = (f32[8,128]{1,0:T(8,128)S(1)}, f32[8,128]{1,0:T(8,128)S(1)}, u32[]{:S(2)}, u32[]{:S(2)}) collective-permute-start(f32[8,128]{1,0:T(8,128)S(1)} %shard_map.65.refs_3_), channel_id=1, source_target_pairs={{0,1},{1,2},{2,3},{3,7},{7,6},{6,5},{5,4},{4,0},{8,9},{9,10},{10,1... | collective-permute-start | bytes 12296 | tf_op jit(solution)/shard_map/ppermute | solution.py:275
  61.6 1.3 %collective-permute-done.31.refs_5_ = f32[8,128]{1,0:T(8,128)S(1)} collective-permute-done((f32[8,128]{1,0:T(8,128)S(1)}, f32[8,128]{1,0:T(8,128)S(1)}, u32[]{:S(2)}, u32[]{:S(2)}) %collective-permute-start.31) | collective-permute-done | bytes 4128 | tf_op jit(solution)/shard_map/ppermute | solution.py:275
  70.0 2.4 %collective-permute-done.40.refs_0_.refs_2_ = f32[8,128]{1,0:T(8,128)S(1)} collective-permute-done((f32[8,128]{1,0:T(8,128)S(1)}, f32[8,128]{1,0:T(8,128)S(1)}, u32[]{:S(2)}, u32[]{:S(2)}) %collective-permute-start.40) | collective-permute-done | bytes 4128 | tf_op jit(solution)/shard_map/ppermute | solution.py:279
  74.1 1.7 %collective-permute-done.41.refs_0_ = f32[8,128]{1,0:T(8,128)S(1)} collective-permute-done((f32[8,128]{1,0:T(8,128)S(1)}, f32[8,128]{1,0:T(8,128)S(1)}, u32[]{:S(2)}, u32[]{:S(2)}) %collective-permute-start.41) | collective-permute-done | bytes 4128 | tf_op jit(solution)/shard_map/ppermute | solution.py:289
  75.8 2.0 %collective-permute-start.43 = (f32[16,128]{1,0:T(8,128)S(1)}, f32[16,128]{1,0:T(8,128)S(1)}, u32[]{:S(2)}, u32[]{:S(2)}) collective-permute-start(f32[16,128]{1,0:T(8,128)S(1)} %shard_map.69.refs_0_), channel_id=1, source_target_pairs={{0,1},{1,2},{2,3},{3,7},{7,6},{6,5},{5,4},{4,0},{8,9},{9,10},{10,1... | collective-permute-start | bytes 24584 | tf_op jit(solution)/shard_map/ppermute | solution.py:275
  77.8 1.6 %collective-permute-done.44.refs_2_ = f32[16,128]{1,0:T(8,128)S(1)} collective-permute-done((f32[16,128]{1,0:T(8,128)S(1)}, f32[16,128]{1,0:T(8,128)S(1)}, u32[]{:S(2)}, u32[]{:S(2)}) %collective-permute-start.44) | collective-permute-done | bytes 8224 | tf_op jit(solution)/shard_map/ppermute | solution.py:275
  79.4 5.0 %shard_map.71 = f32[24,32,128]{2,1,0:T(8,128)} custom-call(f32[16,128]{1,0:T(8,128)S(1)} %shard_map.69.refs_0_, f32[16,128]{1,0:T(8,128)S(1)} %collective-permute-done.43.refs_1_, f32[16,128]{1,0:T(8,128)S(1)} %collective-permute-done.44.refs_2_, s32[16,40,128]{2,1,0:T(8,128)S(1)} %get-tuple-element.103.refs_3_, ...), custom_call_target="tpu_custom_call" | custom-call | flops 1000000 | bytes 100000 | tf_op jit(solution)/shard_map/pallas_call | solution.py:36
  (92 shorter events, 35.3 us)
Async XLA Ops:
  0.9 7.9 %collective-permute-start = (f32[11,32,128]{2,1,0:T(8,128)S(1)}, f32[11,32,128]{2,1,0:T(8,128)S(1)}, u32[]{:S(2)}, u32[]{:S(2)}) collective-permute-start(f32[11,32,128]{2,1,0:T(8,128)S(1)} %shard_map.46.refs_4_.refs_3_), channel_id=1, source_target_pairs={{0,16},{16,0},{1,17},{17,1},{2,18},{18,2},{3,19},{19,3},{4,20},{20... | collective-permute-start | bytes 540680 | tf_op jit(solution)/shard_map/ppermute | solution.py:279
  8.9 5.9 %collective-permute-start.2 = (f32[400,128]{1,0:T(8,128)S(1)}, f32[400,128]{1,0:T(8,128)S(1)}, u32[]{:S(2)}, u32[]{:S(2)}) collective-permute-start(f32[400,128]{1,0:T(8,128)S(1)} %get-tuple-element.69), channel_id=1, source_target_pairs={{0,16},{1,17},{2,18},{3,19},{4,8},{5,9},{6,10},{7,11},{8,4},{9,5},... | collective-permute-start | bytes 614408 | tf_op jit(solution)/shard_map/ppermute | solution.py:275
  10.4 4.4 %collective-permute-start.1 = (f32[400,128]{1,0:T(8,128)S(1)}, f32[400,128]{1,0:T(8,128)S(1)}, u32[]{:S(2)}, u32[]{:S(2)}) collective-permute-start(f32[400,128]{1,0:T(8,128)S(1)} %get-tuple-element.68.refs_5_), channel_id=1, source_target_pairs={{0,4},{1,5},{2,6},{3,7},{4,0},{5,1},{6,2},{7,3},{8,12},{9,13},{10,... | collective-permute-start | bytes 614408 | tf_op jit(solution)/shard_map/ppermute | solution.py:275
  15.4 3.7 %collective-permute-start.3 = (f32[136,128]{1,0:T(8,128)S(1)}, f32[136,128]{1,0:T(8,128)S(1)}, u32[]{:S(2)}, u32[]{:S(2)}) collective-permute-start(f32[136,128]{1,0:T(8,128)S(1)} %get-tuple-element.82), channel_id=1, source_target_pairs={{0,1},{1,2},{2,3},{3,7},{7,6},{6,5},{5,4},{4,0},{8,9},{9,10},{10,1... | collective-permute-start | bytes 208904 | tf_op jit(solution)/shard_map/ppermute | solution.py:275
  17.0 4.3 %collective-permute-start.4 = (f32[136,128]{1,0:T(8,128)S(1)}, f32[136,128]{1,0:T(8,128)S(1)}, u32[]{:S(2)}, u32[]{:S(2)}) collective-permute-start(f32[136,128]{1,0:T(8,128)S(1)} %get-tuple-element.83), channel_id=1, source_target_pairs={{1,0},{2,1},{3,2},{7,3},{6,7},{5,6},{4,5},{0,4},{9,8},{10,9},{11,1... | collective-permute-start | bytes 208904 | tf_op jit(solution)/shard_map/ppermute | solution.py:275
  25.8 5.6 %collective-permute-start.7 = (f32[9,32,128]{2,1,0:T(8,128)S(1)}, f32[9,32,128]{2,1,0:T(8,128)S(1)}, u32[]{:S(2)}, u32[]{:S(2)}) collective-permute-start(f32[9,32,128]{2,1,0:T(8,128)S(1)} %shard_map.57), channel_id=1, source_target_pairs={{0,16},{16,0},{1,17},{17,1},{2,18},{18,2},{3,19},{19,3},{4,20},{20... | collective-permute-start | bytes 442376 | tf_op jit(solution)/shard_map/ppermute | solution.py:279
  27.8 3.6 %collective-permute-start.6 = (f32[8,128]{1,0:T(8,128)S(1)}, f32[8,128]{1,0:T(8,128)S(1)}, u32[]{:S(2)}, u32[]{:S(2)}) collective-permute-start(f32[8,128]{1,0:T(8,128)S(1)} %get-tuple-element.91.refs_2_.refs_1_.refs_3_), channel_id=1, source_target_pairs={{1,0},{2,1},{3,2},{7,3},{6,7},{5,6},{4,5},{0,4},{9,8},{10,9},{11,1... | collective-permute-start | bytes 12296 | tf_op jit(solution)/shard_map/ppermute | solution.py:275
  31.7 5.7 %collective-permute-start.14 = (f32[264,128]{1,0:T(8,128)S(1)}, f32[264,128]{1,0:T(8,128)S(1)}, u32[]{:S(2)}, u32[]{:S(2)}) collective-permute-start(f32[264,128]{1,0:T(8,128)S(1)} %get-tuple-element.96), channel_id=1, source_target_pairs={{4,0},{8,4},{12,8},{0,12},{5,1},{9,5},{13,9},{1,13},{6,2},{10,6},{... | collective-permute-start | bytes 405512 | tf_op jit(solution)/shard_map/ppermute | solution.py:289
  33.1 5.3 %collective-permute-start.13 = (f32[264,128]{1,0:T(8,128)S(1)}, f32[264,128]{1,0:T(8,128)S(1)}, u32[]{:S(2)}, u32[]{:S(2)}) collective-permute-start(f32[264,128]{1,0:T(8,128)S(1)} %get-tuple-element.95.refs_4_), channel_id=1, source_target_pairs={{0,4},{4,8},{8,12},{12,0},{1,5},{5,9},{9,13},{13,1},{2,6},{6,10},{... | collective-permute-start | bytes 405512 | tf_op jit(solution)/shard_map/ppermute | solution.py:289
  33.1 3.6 %collective-permute-start.12 = (f32[8,128]{1,0:T(8,128)S(1)}, f32[8,128]{1,0:T(8,128)S(1)}, u32[]{:S(2)}, u32[]{:S(2)}) collective-permute-start(f32[8,128]{1,0:T(8,128)S(1)} %shard_map.58.refs_2_.refs_3_), channel_id=1, source_target_pairs={{0,16},{16,0},{1,17},{17,1},{2,18},{18,2},{3,19},{19,3},{4,20},{20... | collective-permute-start | bytes 12296 | tf_op jit(solution)/shard_map/ppermute | solution.py:279
  33.7 3.6 %collective-permute-start.11 = (f32[8,128]{1,0:T(8,128)S(1)}, f32[8,128]{1,0:T(8,128)S(1)}, u32[]{:S(2)}, u32[]{:S(2)}) collective-permute-start(f32[8,128]{1,0:T(8,128)S(1)} %shard_map.58.refs_2_.refs_3_), channel_id=1, source_target_pairs={{1,0},{2,1},{3,2},{7,3},{6,7},{5,6},{4,5},{0,4},{9,8},{10,9},{11,1... | collective-permute-start | bytes 12296 | tf_op jit(solution)/shard_map/ppermute | solution.py:275
  38.9 6.0 %collective-permute-start.15 = (f32[88,128]{1,0:T(8,128)S(1)}, f32[88,128]{1,0:T(8,128)S(1)}, u32[]{:S(2)}, u32[]{:S(2)}) collective-permute-start(f32[88,128]{1,0:T(8,128)S(1)} %get-tuple-element.100), channel_id=1, source_target_pairs={{0,1},{1,2},{2,3},{3,7},{7,6},{6,5},{5,4},{4,0},{8,9},{9,10},{10,1... | collective-permute-start | bytes 135176 | tf_op jit(solution)/shard_map/ppermute | solution.py:275
  40.5 4.4 %collective-permute-start.16 = (f32[88,128]{1,0:T(8,128)S(1)}, f32[88,128]{1,0:T(8,128)S(1)}, u32[]{:S(2)}, u32[]{:S(2)}) collective-permute-start(f32[88,128]{1,0:T(8,128)S(1)} %get-tuple-element.101), channel_id=1, source_target_pairs={{1,0},{2,1},{3,2},{7,3},{6,7},{5,6},{4,5},{0,4},{9,8},{10,9},{11,1... | collective-permute-start | bytes 135176 | tf_op jit(solution)/shard_map/ppermute | solution.py:275
  41.2 3.6 %collective-permute-start.17 = (f32[8,128]{1,0:T(8,128)S(1)}, f32[8,128]{1,0:T(8,128)S(1)}, u32[]{:S(2)}, u32[]{:S(2)}) collective-permute-start(f32[8,128]{1,0:T(8,128)S(1)} %shard_map.60.refs_5_.refs_3_), channel_id=1, source_target_pairs={{0,16},{16,0},{1,17},{17,1},{2,18},{18,2},{3,19},{19,3},{4,20},{20... | collective-permute-start | bytes 12296 | tf_op jit(solution)/shard_map/ppermute | solution.py:279
  45.0 3.8 %collective-permute-start.24 = (f32[8,128]{1,0:T(8,128)S(1)}, f32[8,128]{1,0:T(8,128)S(1)}, u32[]{:S(2)}, u32[]{:S(2)}) collective-permute-start(f32[8,128]{1,0:T(8,128)S(1)} %shard_map.63.refs_3_), channel_id=1, source_target_pairs={{4,0},{8,4},{12,8},{0,12},{5,1},{9,5},{13,9},{1,13},{6,2},{10,6},{... | collective-permute-start | bytes 12296 | tf_op jit(solution)/shard_map/ppermute | solution.py:289
  50.5 4.4 %collective-permute-start.29 = (f32[8,128]{1,0:T(8,128)S(1)}, f32[8,128]{1,0:T(8,128)S(1)}, u32[]{:S(2)}, u32[]{:S(2)}) collective-permute-start(f32[8,128]{1,0:T(8,128)S(1)} %shard_map.64.refs_3_), channel_id=1, source_target_pairs={{4,0},{8,4},{12,8},{0,12},{5,1},{9,5},{13,9},{1,13},{6,2},{10,6},{... | collective-permute-start | bytes 12296 | tf_op jit(solution)/shard_map/ppermute | solution.py:289
  56.6 4.7 %collective-permute-start.34 = (f32[8,128]{1,0:T(8,128)S(1)}, f32[8,128]{1,0:T(8,128)S(1)}, u32[]{:S(2)}, u32[]{:S(2)}) collective-permute-start(f32[8,128]{1,0:T(8,128)S(1)} %shard_map.65.refs_3_), channel_id=1, source_target_pairs={{4,0},{8,4},{12,8},{0,12},{5,1},{9,5},{13,9},{1,13},{6,2},{10,6},{... | collective-permute-start | bytes 12296 | tf_op jit(solution)/shard_map/ppermute | solution.py:289
  58.0 3.6 %collective-permute-start.32 = (f32[8,128]{1,0:T(8,128)S(1)}, f32[8,128]{1,0:T(8,128)S(1)}, u32[]{:S(2)}, u32[]{:S(2)}) collective-permute-start(f32[8,128]{1,0:T(8,128)S(1)} %shard_map.65.refs_3_), channel_id=1, source_target_pairs={{0,16},{16,0},{1,17},{17,1},{2,18},{18,2},{3,19},{19,3},{4,20},{20... | collective-permute-start | bytes 12296 | tf_op jit(solution)/shard_map/ppermute | solution.py:279
  63.1 3.9 %collective-permute-start.39 = (f32[8,128]{1,0:T(8,128)S(1)}, f32[8,128]{1,0:T(8,128)S(1)}, u32[]{:S(2)}, u32[]{:S(2)}) collective-permute-start(f32[8,128]{1,0:T(8,128)S(1)} %shard_map.66.refs_3_), channel_id=1, source_target_pairs={{4,0},{8,4},{12,8},{0,12},{5,1},{9,5},{13,9},{1,13},{6,2},{10,6},{... | collective-permute-start | bytes 12296 | tf_op jit(solution)/shard_map/ppermute | solution.py:289
  64.2 3.6 %collective-permute-start.37 = (f32[8,128]{1,0:T(8,128)S(1)}, f32[8,128]{1,0:T(8,128)S(1)}, u32[]{:S(2)}, u32[]{:S(2)}) collective-permute-start(f32[8,128]{1,0:T(8,128)S(1)} %shard_map.66.refs_3_), channel_id=1, source_target_pairs={{0,16},{16,0},{1,17},{17,1},{2,18},{18,2},{3,19},{19,3},{4,20},{20... | collective-permute-start | bytes 12296 | tf_op jit(solution)/shard_map/ppermute | solution.py:279
  65.0 3.6 %collective-permute-start.36 = (f32[8,128]{1,0:T(8,128)S(1)}, f32[8,128]{1,0:T(8,128)S(1)}, u32[]{:S(2)}, u32[]{:S(2)}) collective-permute-start(f32[8,128]{1,0:T(8,128)S(1)} %shard_map.66.refs_3_), channel_id=1, source_target_pairs={{1,0},{2,1},{3,2},{7,3},{6,7},{5,6},{4,5},{0,4},{9,8},{10,9},{11,1... | collective-permute-start | bytes 12296 | tf_op jit(solution)/shard_map/ppermute | solution.py:275
  68.8 3.7 %collective-permute-start.40 = (f32[8,128]{1,0:T(8,128)S(1)}, f32[8,128]{1,0:T(8,128)S(1)}, u32[]{:S(2)}, u32[]{:S(2)}) collective-permute-start(f32[8,128]{1,0:T(8,128)S(1)} %shard_map.67.refs_1_), channel_id=1, source_target_pairs={{0,16},{16,0},{1,17},{17,1},{2,18},{18,2},{3,19},{19,3},{4,20},{20... | collective-permute-start | bytes 12296 | tf_op jit(solution)/shard_map/ppermute | solution.py:279
  75.8 3.7 %collective-permute-start.44 = (f32[16,128]{1,0:T(8,128)S(1)}, f32[16,128]{1,0:T(8,128)S(1)}, u32[]{:S(2)}, u32[]{:S(2)}) collective-permute-start(f32[16,128]{1,0:T(8,128)S(1)} %shard_map.69.refs_0_), channel_id=1, source_target_pairs={{1,0},{2,1},{3,2},{7,3},{6,7},{5,6},{4,5},{0,4},{9,8},{10,9},{11,1... | collective-permute-start | bytes 24584 | tf_op jit(solution)/shard_map/ppermute | solution.py:275
  75.8 3.7 %collective-permute-start.43 = (f32[16,128]{1,0:T(8,128)S(1)}, f32[16,128]{1,0:T(8,128)S(1)}, u32[]{:S(2)}, u32[]{:S(2)}) collective-permute-start(f32[16,128]{1,0:T(8,128)S(1)} %shard_map.69.refs_0_), channel_id=1, source_target_pairs={{0,1},{1,2},{2,3},{3,7},{7,6},{6,5},{5,4},{4,0},{8,9},{9,10},{10,1... | collective-permute-start | bytes 24584 | tf_op jit(solution)/shard_map/ppermute | solution.py:275
  (21 other events, 63.7 us)

commit v10 on v9

--- a/solution.py
+++ b/solution.py
@@ -102,36 +102,54 @@
     return copies
 
 
-def pack_x_kernel(count, widths, flags, *refs):
+def pack_kernel(count, widths, flags, *refs):
     fields = len(widths)
-    ins, outs = refs[: fields + 1], refs[fields + 1 : -2]
-    near, sems = refs[-2:]
+    n_x = 1 if count == 2 else 2
+    ins, kept = refs[: fields + 1], refs[fields + 1 : 2 * fields + 2]
+    outs, sems = refs[2 * fields + 2 : -1], refs[-1]
+    x_outs, y_outs, corner_outs = outs[:n_x], outs[n_x : n_x + 2], outs[n_x + 2 :]
     nx, ny = ins[0].shape[0], ins[0].shape[1]
-    base = bases(widths)
-    pairs = []
-    for s, out in enumerate(outs):
-
-        def place(size, width, s=s):
-            if count == 2:
-                return jnp.where(flags[IX] == 0, size - width, 0)
-            return (size - width, 0)[s]
-
-        for f, (ref, width) in enumerate(zip(ins, widths)):
-            pairs.append((ref.at[pl.ds(place(nx, width), width)], out.at[pl.ds(base[f], width)]))
-        pairs.append((ins[-1].at[place(nx // 2, 1)], near.at[s]))
-    copies = copied(pairs, sems)
-    for out in outs:
-        out[base[-1]] = jnp.zeros(out.shape[1:], F32)
+    nb, half, width = ins[-1].shape
+    thirds = 3
+    copies = []
+    for ref, out in zip(ins, kept):
+        for t in range(thirds):
+            size = ref.shape[0] // thirds
+            rows = pl.ds(t * size, size)
+            copies.append(pltpu.make_async_copy(ref.at[rows], out.at[rows], sems.at[len(copies)]))
+    for copy in copies:
+        copy.start()
+    for out in (*x_outs, *y_outs):
+        out[...] = jnp.zeros(out.shape, F32)
     for copy in copies:
         copy.wait()
-    for s, out in enumerate(outs):
-        out[base[-1], : ny // 2, : near.shape[2]] = near[s].astype(F32)
-
-
-def load_kernel(flags, *refs):
-    count = (len(refs) - 2) // 2
-    for copy in copied(list(zip(refs[:count], refs[count + 1 : -1])), refs[-1]):
-        copy.wait()
+    base = bases(widths)
+    labels = kept[-1]
+    for s, out in enumerate(x_outs):
+
+        def place(size, thick, s=s):
+            if count == 2:
+                return jnp.where(flags[IX] == 0, size - thick, 0)
+            return (size - thick, 0)[s]
+
+        for f, thick in enumerate(widths):
+            at = place(nx, thick)
+            for k in range(thick):
+                slab = kept[f][at + k]
+                out[base[f] + k] = slab
+                row = (sum(w * w for w in widths[:f])) + k * thick
+                corner_outs[2 * s][row : row + thick] = slab[ny - thick :]
+                corner_outs[2 * s + 1][row : row + thick] = slab[:thick]
+        out[base[-1], :half, :width] = labels[place(nb, 1)].astype(F32)
+    for out, high in zip(y_outs, (True, False)):
+        for f, thick in enumerate(widths):
+            for x in range(nx):
+                row = base[f] * nx + x * thick
+                out[row : row + thick] = kept[f][x, ny - thick :] if high else kept[f][x, :thick]
+        row = base[-1] * nx
+        for b in range(nb):
+            line = labels[b, half - 1 :] if high else labels[b, :1]
+            out[row + b : row + b + 1, :width] = line.astype(F32)
 
 
 def slab_of(own, low, high, base, width, x):
@@ -145,38 +163,19 @@
     return high[base + at] if at < width else None
 
 
-def pack_y_kernel(widths, labels, ring, flags, *refs):
-    fields = len(widths)
-    ins = refs[:fields]
-    low, high = refs[fields + 1 : fields + 3]
-    one, two = refs[fields + 3 :]
+def pack_y_kernel(fields, flags, *refs):
+    ins, rider = refs[:fields], refs[fields]
+    low, high, to_high, to_low = refs[fields + 1 :]
     nx, ny = ins[0].shape[0], ins[0].shape[1]
-    frame = Frame(nx, ny)
-    base = bases(widths)
-    even = flags[PARITY] == 0
-
-    def send(at, count, to_high, to_low):
-        one[at : at + count] = to_high if ring else jnp.where(even, to_high, to_low)
-        two[at : at + count] = to_low if ring else jnp.where(even, to_low, to_high)
-
+    wide = nx + 2 * HALO
     for f in range(fields):
-        for x in range(frame.wide):
-            slab = slab_of(ins[f], low, high, base[f], widths[f], x)
-            at = (f * frame.wide + x) * HALO
-            if slab is None:
-                slab = jnp.ones((ny, LANES), F32)
-            send(at, HALO, slab[ny - HALO :], slab[:HALO])
-    at = fields * frame.wide * HALO
-    if ring:
-        one[at:], two[at:] = refs[fields][...], refs[fields][...]
-    if labels:
-        nb, rows, width = refs[fields].shape
-        for out in (one, two):
-            out[at:] = jnp.zeros((out.shape[0] - at, LANES), F32)
-        for b in range(nb):
-            top, bottom = (refs[fields][b, row : row + 1].astype(F32) for row in (rows - 1, 0))
-            one[at + b : at + b + 1, :width] = jnp.where(even, top, bottom)
-            two[at + b : at + b + 1, :width] = jnp.where(even, bottom, top)
+        for x in range(wide):
+            slab = slab_of(ins[f], low, high, HALO * f, HALO, x)
+            at = (f * wide + x) * HALO
+            to_high[at : at + HALO] = slab[ny - HALO :]
+            to_low[at : at + HALO] = slab[:HALO]
+    at = fields * wide * HALO
+    to_high[at:], to_low[at:] = rider[...], rider[...]
 
 
 def packed_lanes(wide_ref, f, frame, rows, to_high, to_low):
@@ -192,27 +191,67 @@
     to_low[at] = turned(low, -HALO, 1)
 
 
-def frame_kernel(widths, flags, *refs):
+def first_frame_kernel(count, widths, flags, *refs):
     fields = len(widths)
+    ins, labels, refs = refs[:fields], refs[fields], refs[fields + 1 :]
+    x_low, x_high, y_low, y_high = refs[:4]
+    corners = refs[4:6] * 2 if count == 2 else refs[4:8]
+    wide_ref, send_forth, send_back, to_high, to_low = refs[-5:]
+    nx, ny = ins[0].shape[0], ins[0].shape[1]
+    frame = Frame(nx, ny)
+    base = bases(widths)
+    tall, own = frame.tall, frame.own
+    even = flags[PARITY] == 0
+    ones = jnp.ones((frame.rows, LANES), F32)
+    for f, thick in enumerate(widths):
+        for x in range(frame.wide):
+            slab = slab_of(ins[f], x_low, x_high, base[f], thick, x)
+            if slab is None:
+                wide_ref[f, x] = ones
+                continue
+            edge = ones[: SUB + HALO]
+            wide_ref[f, x, :own] = edge
+            wide_ref[f, x, own + ny :] = edge
+            wide_ref[f, x, own : own + ny] = slab
+            if HALO <= x < HALO + nx:
+                low, high, row = y_low, y_high, base[f] * nx + (x - HALO) * thick
+            else:
+                above = x >= HALO
+                low, high = corners[2 * above : 2 * above + 2]
+                at = x - HALO - nx if above else x - (HALO - thick)
+                row = sum(w * w for w in widths[:f]) + at * thick
+            wide_ref[f, x, own - thick : own] = low[row : row + thick]
+            wide_ref[f, x, own + ny : own + ny + thick] = high[row : row + thick]
+        packed_lanes(wide_ref, f, frame, pl.ds(SUB, tall), to_high, to_low)
+    high, low = to_high[...], to_low[...]
+    size = fields * tall
+    send_forth[:size], send_back[:size] = jnp.where(even, high, low), jnp.where(even, low, high)
+    nb, rows, width = labels.shape
+    lane = lane_no((rows, LANES))
+    high = low = jnp.zeros((rows, LANES), F32)
+    for b in range(nb):
+        slab = labels[b].astype(F32)
+        high = jnp.where(lane == b, slab[:, width - 1 :], high)
+        low = jnp.where(lane == b, slab[:, :1], low)
+    send_forth[size:], send_back[size:] = jnp.where(even, high, low), jnp.where(even, low, high)
+
+
+def frame_kernel(fields, flags, *refs):
     ins = refs[:fields]
     x_low, x_high, _ = refs[fields : fields + 3]
     wide_ref, to_high, to_low = refs[fields + 3 :]
     nx, ny = ins[0].shape[0], ins[0].shape[1]
     frame = Frame(nx, ny)
-    base = bases(widths)
-    tall, own = frame.tall, frame.own
     spare = jnp.ones((SUB, LANES), F32)
     for f in range(fields):
         for x in range(frame.wide):
-            slab = slab_of(ins[f], x_low, x_high, base[f], widths[f], x)
-            wide_ref[f, x, own : own + ny] = jnp.ones((ny, LANES), F32) if slab is None else slab
+            wide_ref[f, x, frame.own : frame.own + ny] = slab_of(ins[f], x_low, x_high, HALO * f, HALO, x)
             wide_ref[f, x, :SUB] = spare
-            wide_ref[f, x, SUB + tall :] = spare
-        packed_lanes(wide_ref, f, frame, pl.ds(2 * SUB, tall - 2 * SUB), to_high, to_low)
-
-
-def pack_z_kernel(widths, labels, ring, flags, wide_in, high_in, low_in, from_low, from_high, rider, *refs):
-    fields = len(widths)
+            wide_ref[f, x, SUB + frame.tall :] = spare
+        packed_lanes(wide_ref, f, frame, pl.ds(2 * SUB, frame.tall - 2 * SUB), to_high, to_low)
+
+
+def pack_z_kernel(fields, flags, wide_in, high_in, low_in, from_low, from_high, rider, *refs):
     wide_ref, send_forth, send_back, to_high, to_low = refs
     frame = Frame(wide_ref.shape[1] - 2 * HALO, wide_ref.shape[2] - 2 * (SUB + HALO))
     ny, tall, own = frame.ny, frame.tall, frame.own
@@ -220,11 +259,8 @@
     for f in range(fields):
         for x in range(frame.wide):
             at = (f * frame.wide + x) * HALO
-            low, high = from_low[at : at + HALO], from_high[at : at + HALO]
-            if not ring:
-                low, high = jnp.where(even, high, low), jnp.where(even, low, high)
-            wide_ref[f, x, SUB:own] = low
-            wide_ref[f, x, own + ny : own + ny + HALO] = high
+            wide_ref[f, x, SUB:own] = from_low[at : at + HALO]
+            wide_ref[f, x, own + ny : own + ny + HALO] = from_high[at : at + HALO]
     size = fields * tall
     to_high[...], to_low[...] = high_in[...], low_in[...]
     for f in range(fields):
@@ -232,17 +268,7 @@
             packed_lanes(wide_ref, f, frame, pl.ds(start, SUB), to_high, to_low)
     high, low = to_high[...], to_low[...]
     send_forth[:size], send_back[:size] = jnp.where(even, high, low), jnp.where(even, low, high)
-    if ring:
-        send_forth[size:], send_back[size:] = rider[...], rider[...]
-    if labels:
-        nb, rows, width = rider.shape
-        lane = lane_no((rows, LANES))
-        high = low = jnp.zeros((rows, LANES), F32)
-        for b in range(nb):
-            slab = rider[b].astype(F32)
-            high = jnp.where(lane == b, slab[:, width - 1 :], high)
-            low = jnp.where(lane == b, slab[:, :1], low)
-        send_forth[size:], send_back[size:] = jnp.where(even, high, low), jnp.where(even, low, high)
+    send_forth[size:], send_back[size:] = rider[...], rider[...]
 
 
 class Links:
@@ -251,17 +277,13 @@
         n_x, n_y, n_z = self.sizes
 
         def at(i, j, k):
-            return (i * n_y + j) * n_z + k
-
+            return (i % n_x * n_y + j % n_y) * n_z + k
+
+        every = [(i, j, k) for i in range(n_x) for j in range(n_y) for k in range(n_z)]
         self.ring_x = [(i, (i + 1) % n_x) for i in range(n_x)]
-        self.inner, self.outer, self.snake = [], [], []
+        self.corner = {d: [(at(i, j, k), at(i + d, j + 1, k)) for i, j, k in every] for d in (1, -1)}
+        self.snake = []
         for i in range(n_x):
-            for j in range(n_y):
-                for k in range(n_z):
-                    self.inner.append((at(i, j, k), at(i, j ^ 1, k)))
-                    over = (i, j + 1) if j % 2 else (i, j - 1)
-                    over = over if 0 <= over[1] < n_y else (i ^ 1, j)
-                    self.outer.append((at(i, j, k), at(*over, k)))
             for j in range(0, n_y, 2):
                 nodes = [at(i, j, k) for k in range(n_z)] + [at(i, j + 1, k) for k in reversed(range(n_z))]
                 self.snake += [(nodes[m], nodes[(m + 1) % len(nodes)]) for m in range(len(nodes))]
@@ -288,33 +310,39 @@
         ring = [(j, (j + 1) % self.sizes[1]) for j in range(self.sizes[1])]
         return lax.ppermute(to_high, "gy", ring), lax.ppermute(to_low, "gy", self.back(ring))
 
-    def y(self, inner, outer):
-        return self.send(inner, self.inner), self.send(outer, self.outer)
+    def corners(self, sends):
+        if self.sizes[0] == 2:
+            return self.send(sends[0], self.corner[1]), self.send(sends[1], self.back(self.corner[1]))
+        return (
+            self.send(sends[0], self.corner[1]),
+            self.send(sends[1], self.back(self.corner[-1])),
+            self.send(sends[2], self.corner[-1]),
+            self.send(sends[3], self.back(self.corner[1])),
+        )
 
     def z(self, forth, back):
         return self.send(forth, self.snake), self.send(back, self.back(self.snake))
 
 
-def send_y(widths, arrays, rider, from_x, ring):
+def send_y(arrays, rider, from_x):
     nx, ny, nz = arrays[0].shape
-    rows = len(widths) * Frame(nx, ny).wide * HALO + (SUB if ring else ny // 2)
-    kernel = functools.partial(pack_y_kernel, widths, not ring, ring)
+    rows = len(arrays) * Frame(nx, ny).wide * HALO + SUB
+    kernel = functools.partial(pack_y_kernel, len(arrays))
     return call(kernel, [shaped(rows, nz)] * 2)(*arrays, rider, from_x[0], from_x[-1])
 
 
-def framed(widths, arrays, from_x, sent):
+def framed(arrays, from_x, sent):
     nx, ny, nz = arrays[0].shape
-    frame, fields = Frame(nx, ny), len(widths)
+    frame, fields = Frame(nx, ny), len(arrays)
     outs = [shaped(fields, *frame.main)] + [shaped(fields * frame.tall, nz)] * 2
-    return call(functools.partial(frame_kernel, widths), outs)(*arrays, from_x[0], from_x[-1], sent)
-
-
-def send_z(widths, frames, from_y, rider, ring):
+    return call(functools.partial(frame_kernel, fields), outs)(*arrays, from_x[0], from_x[-1], sent)
+
+
+def send_z(frames, from_y, rider):
     wide, high, _ = frames
-    rows = high.shape[0] + (SUB if ring else rider.shape[1])
     return call(
-        functools.partial(pack_z_kernel, widths, not ring, ring),
-        [shaped(*wide.shape)] + [shaped(rows, LANES)] * 2,
+        functools.partial(pack_z_kernel, wide.shape[0]),
+        [shaped(*wide.shape)] + [shaped(high.shape[0] + SUB, LANES)] * 2,
         [pltpu.VMEM(high.shape, F32)] * 2,
         aliases={0: 0},
     )(*frames, *from_y, rider)
@@ -427,7 +455,7 @@
     return packed
 
 
-def fields_kernel(count, flags, wide_ref, face_label, inner_diag, wx, wy, wz, partial, cond_edges, face_weight, diag):
+def fields_kernel(count, flags, wide_ref, block_label, inner, face_label, wx, wy, wz, partial, cond_edges, face_weight, diag):
     frame = Frame(wx.shape[0] - 2 * HALO, wx.shape[1] - 2 * (SUB + HALO))
     wide, tall, span = frame.wide, frame.tall, frame.span
     last = HALO + frame.nx
@@ -463,9 +491,10 @@
         lines = [wy[HALO + 2 * b, at : at + 1] + wy[HALO + 2 * b + 1, at : at + 1] for b in range(nb)]
         face_weight[s, : nb // 2] = pack_rows(paired(jnp.concatenate(lines, axis=0)))
     around = jnp.zeros((AGG, LANES), F32)
+    around = lax.fori_loop(0, nb, lambda b, around: add_rows(around, block_label, b, inner, b), around)
     for s, rows in face_rows(count, flags, nb)[:-2]:
         around = add_rows(around, face_label, s, face_weight, s, rows)
-    diag[...] = inner_diag[...] + lane_total(around)
+    diag[...] = lane_total(around)
 
 
 def fine_kernel(flags, wide_ref, forth, back, wx, wy, wz, partial, cond_edges, block_label, face_label, some_diag,
@@ -606,7 +635,7 @@
     out[rows, AGG:] = (tile - high.astype(F32)).astype(BF16)
 
 
-def blocks_kernel(flags, cond, absorb, block_agg, _, block_label, near, weights, inner, face_label, fine_label,
+def blocks_kernel(flags, cond, absorb, block_agg, block_label, near, weights, inner, face_label, fine_label,
                   part, line):
     nx, ny = cond.shape[0], cond.shape[1]
     nb, half, width = nx // 2, ny // 2, LANES // 2
@@ -672,7 +701,7 @@
         face_label[4 + s, :2] = pack_lanes((low, high)[s])
 
 
-def own_kernel(first, last, total, flags, block_label, near, weights, inner, *refs):
+def own_kernel(first, last, total, flags, block_label, near, weights, *refs):
     so_far, refs = (refs[0], refs[1:]) if first else (None, refs)
     refs = refs[1:]
 
@@ -687,22 +716,18 @@
     if last < total:
         refs[0][...] = tile
         return
-    out, inner_diag = refs
     tile = both_halves(tile)
-    keep_tile(out, 0, jnp.where(row_no((AGG, AGG)) == lane_no((AGG, AGG)), 0.0, tile + tile.T))
-    around = jnp.zeros((AGG, LANES), F32)
-    around = lax.fori_loop(0, total, lambda b, around: add_rows(around, block_label, b, inner, b), around)
-    inner_diag[...] = lane_total(around)
-
-
-def faces_kernel(count, nb, flags, own, face_label, weight_xy, weight_z, x_low, x_high, inner, outer, forth, back, out,
+    keep_tile(refs[0], 0, jnp.where(row_no((AGG, AGG)) == lane_no((AGG, AGG)), 0.0, tile + tile.T))
+
+
+def faces_kernel(count, nb, flags, own, face_label, weight_xy, weight_z, x_low, x_high, y_low, y_high, forth, back, out,
                  near, weights):
     out[:AGG] = own[...]
     at, half = x_low.shape[0] - 1, x_low.shape[1] // 2
     near[0], near[1] = pack_rows(x_low[at, :half]), pack_rows(x_high[at, :half])
-    at = inner.shape[0] - half
-    for s, values in enumerate(sides(flags, outer[at:], inner[at:])):
-        near[2 + s, : nb // 2] = pack_rows(values[:nb])
+    at = sum(WIDTHS) * 2 * nb
+    for s, ref in enumerate((y_low, y_high)):
+        near[2 + s, : nb // 2] = pack_rows(ref[at : at + nb])
     at = forth.shape[0] - half
     for s, values in enumerate(sides(flags, forth[at:], back[at:])):
         near[4 + s, :2] = pack_lanes(values)
@@ -845,51 +870,47 @@
     arrays = (conductance, right_side, absorption, block_agg)
     n_send = 1 if n_x == 2 else 2
     pinned = [pltpu.with_memory_space_constraint(a, pltpu.HBM) for a in arrays]
-    hbm = pl.BlockSpec(memory_space=pltpu.HBM)
-    x_sends = call(
-        functools.partial(pack_x_kernel, n_x, WIDTHS),
-        [shaped(sum(WIDTHS) + 1, ny, nz)] * n_send,
-        [pltpu.VMEM((n_send, ny // 2, nz // 2), jnp.int32), pltpu.SemaphoreType.DMA((n_send * 4,))],
-        in_specs=[hbm] * 4,
+    outs = [jax.ShapeDtypeStruct(a.shape, a.dtype) for a in arrays]
+    outs += [shaped(sum(WIDTHS) + 1, ny, nz)] * n_send + [shaped(sum(WIDTHS) * nx + 16, nz)] * 2
+    outs += [shaped(-(-sum(w * w for w in WIDTHS) // SUB) * SUB, nz)] * (2 * n_send)
+    got = call(
+        functools.partial(pack_kernel, n_x, WIDTHS),
+        outs,
+        [pltpu.SemaphoreType.DMA((3 * 4,))],
+        in_specs=[pl.BlockSpec(memory_space=pltpu.HBM)] * 4,
     )(*pinned)
-    arrays = call(
-        load_kernel,
-        [jax.ShapeDtypeStruct(a.shape, a.dtype) for a in arrays],
-        [pltpu.SemaphoreType.DMA((4,))],
-        in_specs=[hbm] * 4 + [VMEM],
-    )(*pinned, x_sends[0])
+    arrays, sends = got[:4], got[4:]
+    from_x = links.x(sends[:n_send])
+    from_y = links.ring_y(*sends[n_send : n_send + 2])
+    from_corners = links.corners(sends[n_send + 2 :])
     blocks = (nb, SUB, LANES)
     outs = [shaped(*blocks), shaped(3, *blocks), shaped(3, *blocks), shaped(*blocks), shaped(6, SUB, LANES)]
     outs += [shaped(nx, ny, nz)]
     scratch = [pltpu.VMEM((17, ny, LANES), F32), pltpu.VMEM((2, ny // 2, LANES), F32)]
-    *rows, face_label, fine_label = call(blocks_kernel, outs, scratch)(arrays[0], arrays[2], arrays[3], x_sends[0])
+    *rows, inner, face_label, fine_label = call(blocks_kernel, outs, scratch)(arrays[0], arrays[2], arrays[3])
     block_label = rows[0]
-    bounds = (0, nb * 5 // 12, nb)
-    parts = []
-
-    def own_part(p, sent):
-        outs = [shaped(AGG, 2 * AGG)]
-        if p == 1:
-            outs = [jax.ShapeDtypeStruct((AGG, 2 * AGG), BF16), shaped(SUB, AGG)]
-        kernel = functools.partial(own_kernel, bounds[p], bounds[p + 1], nb)
-        parts.append(call(kernel, outs)(*rows, *(parts[-1] if p else ()), sent))
-        return parts[-1]
-
-    first = own_part(0, x_sends[0])
-    from_x = links.x(x_sends)
-    from_x = lax.optimization_barrier((*from_x, *first))[:-1]
-
-    sends = send_y(WIDTHS, arrays[:3], arrays[3], from_x, False)
-    frames = framed(WIDTHS, arrays[:3], from_x, sends[0])
-    own_tile, inner_diag = own_part(1, sends[0])
-    from_y = links.y(*sends)
-    *from_y, own_tile, inner_diag = lax.optimization_barrier((*from_y, own_tile, inner_diag))
-    wide, *sends = send_z(WIDTHS, frames, from_y, arrays[3], False)
+    bounds = (0, nb * 5 // 12, nb * 10 // 12, nb)
+
+    def own_part(p, *more):
+        out = jax.ShapeDtypeStruct((AGG, 2 * AGG), BF16) if p == 2 else shaped(AGG, 2 * AGG)
+        return call(functools.partial(own_kernel, bounds[p], bounds[p + 1], nb), [out])(*rows, *more)[0]
+
+    own_tile = own_part(0, sends[0])
+    got = lax.optimization_barrier((*from_x, *from_y, *from_corners, own_tile))
+    from_x, from_y, from_corners = got[:n_send], got[n_send : n_send + 2], got[n_send + 2 : -1]
+    size = len(WIDTHS) * frame.tall
+    wide, *sends = call(
+        functools.partial(first_frame_kernel, n_x, WIDTHS),
+        [shaped(len(WIDTHS), *frame.main)] + [shaped(size + ny // 2, nz)] * 2,
+        [pltpu.VMEM((size, nz), F32)] * 2,
+    )(*arrays, from_x[0], from_x[-1], *from_y, *from_corners)
     outs = [shaped(*frame.main)] * 4 + [shaped(frame.tall, nz), shaped(4, SUB, LANES), shaped(SUB, AGG)]
     *fields, weight_xy, some_diag = call(functools.partial(fields_kernel, n_x), outs, limit=24)(
-        wide, face_label, inner_diag
+        wide, block_label, inner, face_label
     )
+    own_tile = own_part(1, own_tile, sends[0])
     halo = (wide, *links.z(*sends))
+    *halo, own_tile = lax.optimization_barrier((*halo, own_tile))
     outs = [shaped(*frame.main)] * 2 + [shaped(*frame.ends)] * 6 + [shaped(nx, ny, nz)]
     outs += [shaped(2, SUB, LANES)] + [shaped(SUB, AGG)] * 2
     scratch = [pltpu.VMEM(frame.main, F32), pltpu.VMEM(frame.ends, F32), pltpu.VMEM((nx, frame.rows, LANES), F32)]
@@ -899,6 +920,7 @@
     )
     fields, pre = (*fields[:3], *got[:8]), got[8]
     weight_z, scaled_rhs, scale = got[9:]
+    own_tile = own_part(2, own_tile, scaled_rhs)
     tiles = call(
         functools.partial(faces_kernel, n_x, nb),
         jax.ShapeDtypeStruct(((n_send + 5) * AGG, 2 * AGG), BF16),
@@ -910,14 +932,14 @@
         near = links.near(coarse, **more)
         return call(turn_kernel, shaped(SUB, AGG))(tiles, scaled_rhs, scale, coarse, *near), near
 
-    widths, both = (HALO, HALO), (pre, fine_label)
+    both = (pre, fine_label)
     rides = call(functools.partial(ride_kernel, n_x), [shaped(2 * HALO + 1, ny, nz)] * n_send)(*both, coarse)
     coarse, near = turn(x=rides)
     from_x = near[2:-2]
-    rides = send_y(widths, both, coarse, from_x, True)
-    frames = framed(widths, both, from_x, rides[0])
+    rides = send_y(both, coarse, from_x)
+    frames = framed(both, from_x, rides[0])
     coarse, near = turn(y=rides)
-    wide, *rides = send_z(widths, frames, near[-2:], coarse, True)
+    wide, *rides = send_z(frames, near[-2:], coarse)
     coarse, near = turn(z=rides)
     halo = (wide, *near[:2])
     outs = [jax.ShapeDtypeStruct((frame.wide // 2, frame.tall, nz), jnp.int32)]

time: 84.6 us -> 83.3 us (0.985)
  waiting for transfers between devices: 21.3 us -> 18.2 us
  starting transfers between devices: 38.4 us -> 41.1 us
  Pallas kernels: 24.5 us -> 23.6 us
    ppermute x20, waiting for transfers between devices: 10.1 us -> 5.87 us  [send(): return lax.ppermute(values, ('gx', 'gy', 'gz'), pairs)]
    ppermute x8 -> x9, starting transfers between devices: 6.61 us -> 9.75 us  [ring_y(): lax.ppermute(to_low, 'gy', self.back(ring))]
    ppermute x9, starting transfers between devices: 12 us -> 10.2 us  [x(): return (lax.ppermute(sends[0], 'gx', self.ring_x),)]
    ppermute x20, starting transfers between devices: 19.1 us -> 20.5 us  [send(): return lax.ppermute(values, ('gx', 'gy', 'gz'), pairs)]
    pallas_call x26 -> x24, Pallas kernels: 24.5 us -> 23.6 us  [run(): pl.pallas_call(placed, out_shape=outs, in_specs=in_specs or [VMEM] * len(...]
    ppermute x8 -> x9, waiting for transfers between devices: 4.63 us -> 5.19 us  [ring_y(): lax.ppermute(to_high, 'gy', ring)]
  transfers between devices with their start and end apart: 45 -> 47, of which waited for: 22 -> 21; matrix products, arithmetic and copies ran while one was open for 0% -> 0% of each run, Pallas kernels for 14% -> 12%
where the time goes in v10:
time: 83.3 us; the launch traced here: 83.2 us
  starting transfers between devices  41.1 us (49%)
  Pallas kernels  23.6 us (28%)
  waiting for transfers between devices  18.2 us (22%)
    pallas_call x24, Pallas kernels, run(): pl.pallas_call(placed, out_shape=outs, in_specs=in_specs or [VMEM] * len(...  23.6 us
    ppermute x20, starting transfers between devices, send(): return lax.ppermute(values, ('gx', 'gy', 'gz'), pairs)  20.5 us
    ppermute x9, starting transfers between devices, x(): return (lax.ppermute(sends[0], 'gx', self.ring_x),)  10.2 us
    ppermute x9, starting transfers between devices, ring_y(): lax.ppermute(to_low, 'gy', self.back(ring))  9.75 us
    ppermute x20, waiting for transfers between devices, send(): return lax.ppermute(values, ('gx', 'gy', 'gz'), pairs)  5.87 us
    ppermute x9, waiting for transfers between devices, x(): return (lax.ppermute(sends[0], 'gx', self.ring_x),)  5.77 us
    ppermute x9, waiting for transfers between devices, ring_y(): lax.ppermute(to_high, 'gy', ring)  5.19 us
  transfers between devices with their start and end apart: 47, of which 21 were waited for; matrix products, arithmetic and copies ran while one was open for 0% of the time, Pallas kernels for 12%

profile of v10, /device:TPU:0, one launch (start us, length us, event | category | flops | bytes accessed | tf_op | source)
XLA Modules:
  0.0 83.2 jit_solution(17172784487361559379)
XLA Ops:
  0.0 1.5 %shard_map.46 = (f32[24,32,128]{2,1,0:T(8,128)S(1)}, f32[24,32,128]{2,1,0:T(8,128)S(1)}, f32[24,32,128]{2,1,0:T(8,128)S(1)}, s32[12,16,64]{2,1,0:T(8,128)S(1)}, ...) custom-call(f32[24,32,128]{2,1,0:T(8,128)} %refs_0_.1, ...), custom_call_target="tpu_custom_call" | custom-call | flops 1000000 | bytes 100000 | tf_op jit(solution)/shard_map/pallas_call | solution.py:36
  1.5 3.0 %collective-permute-start = (f32[11,32,128]{2,1,0:T(8,128)S(1)}, f32[11,32,128]{2,1,0:T(8,128)S(1)}, u32[]{:S(2)}, u32[]{:S(2)}) collective-permute-start(f32[11,32,128]{2,1,0:T(8,128)S(1)} %get-tuple-element.68.refs_3_), channel_id=1, source_target_pairs={{0,16},{16,0},{1,17},{17,1},{2,18},{18,2},{3,19},{19,3},{4,20},{20... | collective-permute-start | bytes 540680 | tf_op jit(solution)/shard_map/ppermute | solution.py:301
  4.5 1.7 %collective-permute-start.2 = (f32[256,128]{1,0:T(8,128)S(1)}, f32[256,128]{1,0:T(8,128)S(1)}, u32[]{:S(2)}, u32[]{:S(2)}) collective-permute-start(f32[256,128]{1,0:T(8,128)S(1)} %get-tuple-element.70), channel_id=1, source_target_pairs={{4,0},{8,4},{12,8},{0,12},{5,1},{9,5},{13,9},{1,13},{6,2},{10,6},{... | collective-permute-start | bytes 393224 | tf_op jit(solution)/shard_map/ppermute | solution.py:311
  6.3 2.6 %collective-permute-start.4 = (f32[40,128]{1,0:T(8,128)S(1)}, f32[40,128]{1,0:T(8,128)S(1)}, u32[]{:S(2)}, u32[]{:S(2)}) collective-permute-start(f32[40,128]{1,0:T(8,128)S(1)} %get-tuple-element.72), channel_id=1, source_target_pairs={{20,0},{21,1},{22,2},{23,3},{24,4},{25,5},{26,6},{27,7},{28,8},{29... | collective-permute-start | bytes 61448 | tf_op jit(solution)/shard_map/ppermute | solution.py:297
  8.9 1.6 %shard_map.47 = (f32[12,8,128]{2,1,0:T(8,128)S(1)}, f32[3,12,8,128]{3,2,1,0:T(8,128)S(1)}, f32[3,12,8,128]{3,2,1,0:T(8,128)S(1)}, f32[12,8,128]{2,1,0:T(8,128)S(...) custom-call(f32[24,32,128]{2,1,0:T(8,128)S(1)} %get-tuple-element.61.refs_0_, ...), custom_call_target="tpu_custom_call" | custom-call | flops 1000000 | bytes 100000 | tf_op jit(solution)/shard_map/pallas_call | solution.py:36
  10.6 1.9 %shard_map.48.refs_3_ = f32[128,256]{1,0:T(8,128)S(1)} custom-call(f32[12,8,128]{2,1,0:T(8,128)S(1)} %get-tuple-element.64.refs_0_.refs_1_.refs_8_, f32[3,12,8,128]{3,2,1,0:T(8,128)S(1)} %get-tuple-element.65.refs_1_, f32[3,12,8,128]{3,2,1,0:T(8,128)S(1)} %get-tuple-element.66.refs_2_, f32[11,32,128]{2,1,0:T(8,128)S(1)} %get-tuple-element.68.refs_3_), custom_call_target="tpu_custom_call" | custom-call | flops 1000000 | bytes 100000 | tf_op jit(solution)/shard_map/pallas_call | solution.py:36
  13.6 2.0 %collective-permute-start.5 = (f32[136,128]{1,0:T(8,128)S(1)}, f32[136,128]{1,0:T(8,128)S(1)}, u32[]{:S(2)}, u32[]{:S(2)}) collective-permute-start(f32[136,128]{1,0:T(8,128)S(1)} %get-tuple-element.79.refs_4_), channel_id=1, source_target_pairs={{0,1},{1,2},{2,3},{3,7},{7,6},{6,5},{5,4},{4,0},{8,9},{9,10},{10,1... | collective-permute-start | bytes 208904 | tf_op jit(solution)/shard_map/ppermute | solution.py:297
  15.7 1.9 %shard_map.50.refs_3_ = f32[128,256]{1,0:T(8,128)S(1)} custom-call(f32[12,8,128]{2,1,0:T(8,128)S(1)} %get-tuple-element.64.refs_0_.refs_1_.refs_8_, f32[3,12,8,128]{3,2,1,0:T(8,128)S(1)} %get-tuple-element.65.refs_1_, f32[3,12,8,128]{3,2,1,0:T(8,128)S(1)} %get-tuple-element.66.refs_2_, f32[128,256]{1,0:T(8,128)S(1)} %shard_map.48.refs_3_, ...), custom_call_target="tpu_custom_call" | custom-call | flops 1000000 | bytes 100000 | tf_op jit(solution)/shard_map/pallas_call | solution.py:36
  17.6 2.5 %shard_map.51 = (f32[32,56,128]{2,1,0:T(8,128)S(1)}, f32[32,56,128]{2,1,0:T(8,128)S(1)}, f32[32,56,128]{2,1,0:T(8,128)S(1)}, f32[32,56,128]{2,1,0:T(8,128)S(1)},...) custom-call(f32[3,32,56,128]{3,2,1,0:T(8,128)S(1)} %get-tuple-element.82.refs_0_, ...), custom_call_target="tpu_custom_call" | custom-call | flops 1000000 | bytes 100000 | tf_op jit(solution)/shard_map/pallas_call | solution.py:36
  20.1 4.5 %shard_map.52 = (f32[32,56,128]{2,1,0:T(8,128)S(1)}, f32[32,56,128]{2,1,0:T(8,128)S(1)}, f32[2,56,128]{2,1,0:T(8,128)S(1)}, f32[2,56,128]{2,1,0:T(8,128)S(1)}, f...) custom-call(f32[3,32,56,128]{3,2,1,0:T(8,128)S(1)} %get-tuple-elemen, ...), custom_call_target="tpu_custom_call" | custom-call | flops 1000000 | bytes 100000 | tf_op jit(solution)/shard_map/pallas_call | solution.py:36
  25.4 1.5 %collective-permute-start.8 = (f32[8,128]{1,0:T(8,128)S(1)}, f32[8,128]{1,0:T(8,128)S(1)}, u32[]{:S(2)}, u32[]{:S(2)}) collective-permute-start(f32[8,128]{1,0:T(8,128)S(1)} %get-tuple-element.93.refs_4_.refs_2_.refs_1_.refs_3_), channel_id=1, source_target_pairs={{1,0},{2,1},{3,2},{7,3},{6,7},{5,6},{4,5},{0,4},{9,8},{10,9},{11,1... | collective-permute-start | bytes 12296 | tf_op jit(solution)/shard_map/ppermute | solution.py:297
  32.5 1.4 %collective-permute-start.13 = (f32[8,128]{1,0:T(8,128)S(1)}, f32[8,128]{1,0:T(8,128)S(1)}, u32[]{:S(2)}, u32[]{:S(2)}) collective-permute-start(f32[8,128]{1,0:T(8,128)S(1)} %shard_map.56.refs_2_.refs_3_), channel_id=1, source_target_pairs={{1,0},{2,1},{3,2},{7,3},{6,7},{5,6},{4,5},{0,4},{9,8},{10,9},{11,1... | collective-permute-start | bytes 12296 | tf_op jit(solution)/shard_map/ppermute | solution.py:297
  37.5 1.6 %collective-permute-start.17 = (f32[88,128]{1,0:T(8,128)S(1)}, f32[88,128]{1,0:T(8,128)S(1)}, u32[]{:S(2)}, u32[]{:S(2)}) collective-permute-start(f32[88,128]{1,0:T(8,128)S(1)} %get-tuple-element.104), channel_id=1, source_target_pairs={{0,1},{1,2},{2,3},{3,7},{7,6},{6,5},{5,4},{4,0},{8,9},{9,10},{10,1... | collective-permute-start | bytes 135176 | tf_op jit(solution)/shard_map/ppermute | solution.py:297
  41.3 1.7 %collective-permute-done.20.refs_7_ = f32[8,128]{1,0:T(8,128)S(1)} collective-permute-done((f32[8,128]{1,0:T(8,128)S(1)}, f32[8,128]{1,0:T(8,128)S(1)}, u32[]{:S(2)}, u32[]{:S(2)}) %collective-permute-start.20) | collective-permute-done | bytes 4128 | tf_op jit(solution)/shard_map/ppermute | solution.py:311
  49.2 1.7 %collective-permute-start.31 = (f32[8,128]{1,0:T(8,128)S(1)}, f32[8,128]{1,0:T(8,128)S(1)}, u32[]{:S(2)}, u32[]{:S(2)}) collective-permute-start(f32[8,128]{1,0:T(8,128)S(1)} %shard_map.62.refs_3_), channel_id=1, source_target_pairs={{4,0},{8,4},{12,8},{0,12},{5,1},{9,5},{13,9},{1,13},{6,2},{10,6},{... | collective-permute-start | bytes 12296 | tf_op jit(solution)/shard_map/ppermute | solution.py:311
  55.4 1.4 %collective-permute-start.36 = (f32[8,128]{1,0:T(8,128)S(1)}, f32[8,128]{1,0:T(8,128)S(1)}, u32[]{:S(2)}, u32[]{:S(2)}) collective-permute-start(f32[8,128]{1,0:T(8,128)S(1)} %shard_map.63.refs_3_), channel_id=1, source_target_pairs={{4,0},{8,4},{12,8},{0,12},{5,1},{9,5},{13,9},{1,13},{6,2},{10,6},{... | collective-permute-start | bytes 12296 | tf_op jit(solution)/shard_map/ppermute | solution.py:311
  61.4 1.8 %collective-permute-start.41 = (f32[8,128]{1,0:T(8,128)S(1)}, f32[8,128]{1,0:T(8,128)S(1)}, u32[]{:S(2)}, u32[]{:S(2)}) collective-permute-start(f32[8,128]{1,0:T(8,128)S(1)} %shard_map.64.refs_3_), channel_id=1, source_target_pairs={{4,0},{8,4},{12,8},{0,12},{5,1},{9,5},{13,9},{1,13},{6,2},{10,6},{... | collective-permute-start | bytes 12296 | tf_op jit(solution)/shard_map/ppermute | solution.py:311
  63.7 1.4 %collective-permute-start.38 = (f32[8,128]{1,0:T(8,128)S(1)}, f32[8,128]{1,0:T(8,128)S(1)}, u32[]{:S(2)}, u32[]{:S(2)}) collective-permute-start(f32[8,128]{1,0:T(8,128)S(1)} %shard_map.64.refs_3_), channel_id=1, source_target_pairs={{1,0},{2,1},{3,2},{7,3},{6,7},{5,6},{4,5},{0,4},{9,8},{10,9},{11,1... | collective-permute-start | bytes 12296 | tf_op jit(solution)/shard_map/ppermute | solution.py:297
  67.5 1.6 %collective-permute-start.42 = (f32[8,128]{1,0:T(8,128)S(1)}, f32[8,128]{1,0:T(8,128)S(1)}, u32[]{:S(2)}, u32[]{:S(2)}) collective-permute-start(f32[8,128]{1,0:T(8,128)S(1)} %shard_map.65.refs_1_), channel_id=1, source_target_pairs={{0,16},{16,0},{1,17},{17,1},{2,18},{18,2},{3,19},{19,3},{4,20},{20... | collective-permute-start | bytes 12296 | tf_op jit(solution)/shard_map/ppermute | solution.py:301
  69.1 2.0 %collective-permute-done.42.refs_0_.refs_2_ = f32[8,128]{1,0:T(8,128)S(1)} collective-permute-done((f32[8,128]{1,0:T(8,128)S(1)}, f32[8,128]{1,0:T(8,128)S(1)}, u32[]{:S(2)}, u32[]{:S(2)}) %collective-permute-start.42) | collective-permute-done | bytes 4128 | tf_op jit(solution)/shard_map/ppermute | solution.py:301
  72.8 1.7 %collective-permute-done.43.refs_0_ = f32[8,128]{1,0:T(8,128)S(1)} collective-permute-done((f32[8,128]{1,0:T(8,128)S(1)}, f32[8,128]{1,0:T(8,128)S(1)}, u32[]{:S(2)}, u32[]{:S(2)}) %collective-permute-start.43) | collective-permute-done | bytes 4128 | tf_op jit(solution)/shard_map/ppermute | solution.py:311
  74.6 1.9 %collective-permute-start.45 = (f32[16,128]{1,0:T(8,128)S(1)}, f32[16,128]{1,0:T(8,128)S(1)}, u32[]{:S(2)}, u32[]{:S(2)}) collective-permute-start(f32[16,128]{1,0:T(8,128)S(1)} %shard_map.67.refs_0_), channel_id=1, source_target_pairs={{0,1},{1,2},{2,3},{3,7},{7,6},{6,5},{5,4},{4,0},{8,9},{9,10},{10,1... | collective-permute-start | bytes 24584 | tf_op jit(solution)/shard_map/ppermute | solution.py:297
  76.6 1.6 %collective-permute-done.46.refs_2_ = f32[16,128]{1,0:T(8,128)S(1)} collective-permute-done((f32[16,128]{1,0:T(8,128)S(1)}, f32[16,128]{1,0:T(8,128)S(1)}, u32[]{:S(2)}, u32[]{:S(2)}) %collective-permute-start.46) | collective-permute-done | bytes 8224 | tf_op jit(solution)/shard_map/ppermute | solution.py:297
  78.2 5.0 %shard_map.69 = f32[24,32,128]{2,1,0:T(8,128)} custom-call(f32[16,128]{1,0:T(8,128)S(1)} %shard_map.67.refs_0_, f32[16,128]{1,0:T(8,128)S(1)} %collective-permute-done.45.refs_1_, f32[16,128]{1,0:T(8,128)S(1)} %collective-permute-done.46.refs_2_, s32[16,40,128]{2,1,0:T(8,128)S(1)} %get-tuple-element.107.refs_3_, ...), custom_call_target="tpu_custom_call" | custom-call | flops 1000000 | bytes 100000 | tf_op jit(solution)/shard_map/pallas_call | solution.py:36
  (94 shorter events, 33.2 us)
Async XLA Ops:
  1.5 11.0 %collective-permute-start = (f32[11,32,128]{2,1,0:T(8,128)S(1)}, f32[11,32,128]{2,1,0:T(8,128)S(1)}, u32[]{:S(2)}, u32[]{:S(2)}) collective-permute-start(f32[11,32,128]{2,1,0:T(8,128)S(1)} %get-tuple-element.68.refs_3_), channel_id=1, source_target_pairs={{0,16},{16,0},{1,17},{17,1},{2,18},{18,2},{3,19},{19,3},{4,20},{20... | collective-permute-start | bytes 540680 | tf_op jit(solution)/shard_map/ppermute | solution.py:301
  4.5 8.0 %collective-permute-start.1 = (f32[256,128]{1,0:T(8,128)S(1)}, f32[256,128]{1,0:T(8,128)S(1)}, u32[]{:S(2)}, u32[]{:S(2)}) collective-permute-start(f32[256,128]{1,0:T(8,128)S(1)} %get-tuple-element.69), channel_id=1, source_target_pairs={{0,4},{4,8},{8,12},{12,0},{1,5},{5,9},{9,13},{13,1},{2,6},{6,10},{... | collective-permute-start | bytes 393224 | tf_op jit(solution)/shard_map/ppermute | solution.py:311
  4.5 8.0 %collective-permute-start.2 = (f32[256,128]{1,0:T(8,128)S(1)}, f32[256,128]{1,0:T(8,128)S(1)}, u32[]{:S(2)}, u32[]{:S(2)}) collective-permute-start(f32[256,128]{1,0:T(8,128)S(1)} %get-tuple-element.70), channel_id=1, source_target_pairs={{4,0},{8,4},{12,8},{0,12},{5,1},{9,5},{13,9},{1,13},{6,2},{10,6},{... | collective-permute-start | bytes 393224 | tf_op jit(solution)/shard_map/ppermute | solution.py:311
  6.3 6.2 %collective-permute-start.3 = (f32[40,128]{1,0:T(8,128)S(1)}, f32[40,128]{1,0:T(8,128)S(1)}, u32[]{:S(2)}, u32[]{:S(2)}) collective-permute-start(f32[40,128]{1,0:T(8,128)S(1)} %get-tuple-element.71), channel_id=1, source_target_pairs={{0,20},{1,21},{2,22},{3,23},{4,24},{5,25},{6,26},{7,27},{8,28},{9,... | collective-permute-start | bytes 61448 | tf_op jit(solution)/shard_map/ppermute | solution.py:297
  6.3 6.2 %collective-permute-start.4 = (f32[40,128]{1,0:T(8,128)S(1)}, f32[40,128]{1,0:T(8,128)S(1)}, u32[]{:S(2)}, u32[]{:S(2)}) collective-permute-start(f32[40,128]{1,0:T(8,128)S(1)} %get-tuple-element.72), channel_id=1, source_target_pairs={{20,0},{21,1},{22,2},{23,3},{24,4},{25,5},{26,6},{27,7},{28,8},{29... | collective-permute-start | bytes 61448 | tf_op jit(solution)/shard_map/ppermute | solution.py:297
  13.6 6.5 %collective-permute-start.6 = (f32[136,128]{1,0:T(8,128)S(1)}, f32[136,128]{1,0:T(8,128)S(1)}, u32[]{:S(2)}, u32[]{:S(2)}) collective-permute-start(f32[136,128]{1,0:T(8,128)S(1)} %get-tuple-element.80), channel_id=1, source_target_pairs={{1,0},{2,1},{3,2},{7,3},{6,7},{5,6},{4,5},{0,4},{9,8},{10,9},{11,1... | collective-permute-start | bytes 208904 | tf_op jit(solution)/shard_map/ppermute | solution.py:297
  13.6 6.5 %collective-permute-start.5 = (f32[136,128]{1,0:T(8,128)S(1)}, f32[136,128]{1,0:T(8,128)S(1)}, u32[]{:S(2)}, u32[]{:S(2)}) collective-permute-start(f32[136,128]{1,0:T(8,128)S(1)} %get-tuple-element.79.refs_4_), channel_id=1, source_target_pairs={{0,1},{1,2},{2,3},{3,7},{7,6},{6,5},{5,4},{4,0},{8,9},{9,10},{10,1... | collective-permute-start | bytes 208904 | tf_op jit(solution)/shard_map/ppermute | solution.py:297
  24.6 5.2 %collective-permute-start.9 = (f32[9,32,128]{2,1,0:T(8,128)S(1)}, f32[9,32,128]{2,1,0:T(8,128)S(1)}, u32[]{:S(2)}, u32[]{:S(2)}) collective-permute-start(f32[9,32,128]{2,1,0:T(8,128)S(1)} %shard_map.55), channel_id=1, source_target_pairs={{0,16},{16,0},{1,17},{17,1},{2,18},{18,2},{3,19},{19,3},{4,20},{20... | collective-permute-start | bytes 442376 | tf_op jit(solution)/shard_map/ppermute | solution.py:301
  24.8 4.1 %collective-permute-start.11 = (f32[8,128]{1,0:T(8,128)S(1)}, f32[8,128]{1,0:T(8,128)S(1)}, u32[]{:S(2)}, u32[]{:S(2)}) collective-permute-start(f32[8,128]{1,0:T(8,128)S(1)} %get-tuple-element.93.refs_4_.refs_2_.refs_1_.refs_3_), channel_id=1, source_target_pairs={{4,0},{8,4},{12,8},{0,12},{5,1},{9,5},{13,9},{1,13},{6,2},{10,6},{... | collective-permute-start | bytes 12296 | tf_op jit(solution)/shard_map/ppermute | solution.py:311
  24.8 4.1 %collective-permute-start.10 = (f32[8,128]{1,0:T(8,128)S(1)}, f32[8,128]{1,0:T(8,128)S(1)}, u32[]{:S(2)}, u32[]{:S(2)}) collective-permute-start(f32[8,128]{1,0:T(8,128)S(1)} %get-tuple-element.93.refs_4_.refs_2_.refs_1_.refs_3_), channel_id=1, source_target_pairs={{0,4},{4,8},{8,12},{12,0},{1,5},{5,9},{9,13},{13,1},{2,6},{6,10},{... | collective-permute-start | bytes 12296 | tf_op jit(solution)/shard_map/ppermute | solution.py:311
  25.4 3.6 %collective-permute-start.8 = (f32[8,128]{1,0:T(8,128)S(1)}, f32[8,128]{1,0:T(8,128)S(1)}, u32[]{:S(2)}, u32[]{:S(2)}) collective-permute-start(f32[8,128]{1,0:T(8,128)S(1)} %get-tuple-element.93.refs_4_.refs_2_.refs_1_.refs_3_), channel_id=1, source_target_pairs={{1,0},{2,1},{3,2},{7,3},{6,7},{5,6},{4,5},{0,4},{9,8},{10,9},{11,1... | collective-permute-start | bytes 12296 | tf_op jit(solution)/shard_map/ppermute | solution.py:297
  30.1 6.1 %collective-permute-start.16 = (f32[264,128]{1,0:T(8,128)S(1)}, f32[264,128]{1,0:T(8,128)S(1)}, u32[]{:S(2)}, u32[]{:S(2)}) collective-permute-start(f32[264,128]{1,0:T(8,128)S(1)} %get-tuple-element.100), channel_id=1, source_target_pairs={{4,0},{8,4},{12,8},{0,12},{5,1},{9,5},{13,9},{1,13},{6,2},{10,6},{... | collective-permute-start | bytes 405512 | tf_op jit(solution)/shard_map/ppermute | solution.py:311
  31.3 5.7 %collective-permute-start.15 = (f32[264,128]{1,0:T(8,128)S(1)}, f32[264,128]{1,0:T(8,128)S(1)}, u32[]{:S(2)}, u32[]{:S(2)}) collective-permute-start(f32[264,128]{1,0:T(8,128)S(1)} %get-tuple-element.99.refs_4_), channel_id=1, source_target_pairs={{0,4},{4,8},{8,12},{12,0},{1,5},{5,9},{9,13},{13,1},{2,6},{6,10},{... | collective-permute-start | bytes 405512 | tf_op jit(solution)/shard_map/ppermute | solution.py:311
  31.3 3.6 %collective-permute-start.14 = (f32[8,128]{1,0:T(8,128)S(1)}, f32[8,128]{1,0:T(8,128)S(1)}, u32[]{:S(2)}, u32[]{:S(2)}) collective-permute-start(f32[8,128]{1,0:T(8,128)S(1)} %shard_map.56.refs_2_.refs_3_), channel_id=1, source_target_pairs={{0,16},{16,0},{1,17},{17,1},{2,18},{18,2},{3,19},{19,3},{4,20},{20... | collective-permute-start | bytes 12296 | tf_op jit(solution)/shard_map/ppermute | solution.py:301
  32.5 3.6 %collective-permute-start.13 = (f32[8,128]{1,0:T(8,128)S(1)}, f32[8,128]{1,0:T(8,128)S(1)}, u32[]{:S(2)}, u32[]{:S(2)}) collective-permute-start(f32[8,128]{1,0:T(8,128)S(1)} %shard_map.56.refs_2_.refs_3_), channel_id=1, source_target_pairs={{1,0},{2,1},{3,2},{7,3},{6,7},{5,6},{4,5},{0,4},{9,8},{10,9},{11,1... | collective-permute-start | bytes 12296 | tf_op jit(solution)/shard_map/ppermute | solution.py:297
  37.5 6.1 %collective-permute-start.17 = (f32[88,128]{1,0:T(8,128)S(1)}, f32[88,128]{1,0:T(8,128)S(1)}, u32[]{:S(2)}, u32[]{:S(2)}) collective-permute-start(f32[88,128]{1,0:T(8,128)S(1)} %get-tuple-element.104), channel_id=1, source_target_pairs={{0,1},{1,2},{2,3},{3,7},{7,6},{6,5},{5,4},{4,0},{8,9},{9,10},{10,1... | collective-permute-start | bytes 135176 | tf_op jit(solution)/shard_map/ppermute | solution.py:297
  39.1 4.6 %collective-permute-start.18 = (f32[88,128]{1,0:T(8,128)S(1)}, f32[88,128]{1,0:T(8,128)S(1)}, u32[]{:S(2)}, u32[]{:S(2)}) collective-permute-start(f32[88,128]{1,0:T(8,128)S(1)} %get-tuple-element.105), channel_id=1, source_target_pairs={{1,0},{2,1},{3,2},{7,3},{6,7},{5,6},{4,5},{0,4},{9,8},{10,9},{11,1... | collective-permute-start | bytes 135176 | tf_op jit(solution)/shard_map/ppermute | solution.py:297
  43.8 3.7 %collective-permute-start.26 = (f32[8,128]{1,0:T(8,128)S(1)}, f32[8,128]{1,0:T(8,128)S(1)}, u32[]{:S(2)}, u32[]{:S(2)}) collective-permute-start(f32[8,128]{1,0:T(8,128)S(1)} %shard_map.61.refs_3_), channel_id=1, source_target_pairs={{4,0},{8,4},{12,8},{0,12},{5,1},{9,5},{13,9},{1,13},{6,2},{10,6},{... | collective-permute-start | bytes 12296 | tf_op jit(solution)/shard_map/ppermute | solution.py:311
  49.2 4.5 %collective-permute-start.31 = (f32[8,128]{1,0:T(8,128)S(1)}, f32[8,128]{1,0:T(8,128)S(1)}, u32[]{:S(2)}, u32[]{:S(2)}) collective-permute-start(f32[8,128]{1,0:T(8,128)S(1)} %shard_map.62.refs_3_), channel_id=1, source_target_pairs={{4,0},{8,4},{12,8},{0,12},{5,1},{9,5},{13,9},{1,13},{6,2},{10,6},{... | collective-permute-start | bytes 12296 | tf_op jit(solution)/shard_map/ppermute | solution.py:311
  55.4 4.3 %collective-permute-start.36 = (f32[8,128]{1,0:T(8,128)S(1)}, f32[8,128]{1,0:T(8,128)S(1)}, u32[]{:S(2)}, u32[]{:S(2)}) collective-permute-start(f32[8,128]{1,0:T(8,128)S(1)} %shard_map.63.refs_3_), channel_id=1, source_target_pairs={{4,0},{8,4},{12,8},{0,12},{5,1},{9,5},{13,9},{1,13},{6,2},{10,6},{... | collective-permute-start | bytes 12296 | tf_op jit(solution)/shard_map/ppermute | solution.py:311
  57.6 3.6 %collective-permute-start.33 = (f32[8,128]{1,0:T(8,128)S(1)}, f32[8,128]{1,0:T(8,128)S(1)}, u32[]{:S(2)}, u32[]{:S(2)}) collective-permute-start(f32[8,128]{1,0:T(8,128)S(1)} %shard_map.63.refs_3_), channel_id=1, source_target_pairs={{1,0},{2,1},{3,2},{7,3},{6,7},{5,6},{4,5},{0,4},{9,8},{10,9},{11,1... | collective-permute-start | bytes 12296 | tf_op jit(solution)/shard_map/ppermute | solution.py:297
  61.4 4.3 %collective-permute-start.41 = (f32[8,128]{1,0:T(8,128)S(1)}, f32[8,128]{1,0:T(8,128)S(1)}, u32[]{:S(2)}, u32[]{:S(2)}) collective-permute-start(f32[8,128]{1,0:T(8,128)S(1)} %shard_map.64.refs_3_), channel_id=1, source_target_pairs={{4,0},{8,4},{12,8},{0,12},{5,1},{9,5},{13,9},{1,13},{6,2},{10,6},{... | collective-permute-start | bytes 12296 | tf_op jit(solution)/shard_map/ppermute | solution.py:311
  67.5 3.7 %collective-permute-start.42 = (f32[8,128]{1,0:T(8,128)S(1)}, f32[8,128]{1,0:T(8,128)S(1)}, u32[]{:S(2)}, u32[]{:S(2)}) collective-permute-start(f32[8,128]{1,0:T(8,128)S(1)} %shard_map.65.refs_1_), channel_id=1, source_target_pairs={{0,16},{16,0},{1,17},{17,1},{2,18},{18,2},{3,19},{19,3},{4,20},{20... | collective-permute-start | bytes 12296 | tf_op jit(solution)/shard_map/ppermute | solution.py:301
  74.5 3.7 %collective-permute-start.46 = (f32[16,128]{1,0:T(8,128)S(1)}, f32[16,128]{1,0:T(8,128)S(1)}, u32[]{:S(2)}, u32[]{:S(2)}) collective-permute-start(f32[16,128]{1,0:T(8,128)S(1)} %shard_map.67.refs_0_), channel_id=1, source_target_pairs={{1,0},{2,1},{3,2},{7,3},{6,7},{5,6},{4,5},{0,4},{9,8},{10,9},{11,1... | collective-permute-start | bytes 24584 | tf_op jit(solution)/shard_map/ppermute | solution.py:297
  (23 other events, 69.0 us)

commit v11 on v10

--- a/solution.py
+++ b/solution.py
@@ -882,14 +882,15 @@
     arrays, sends = got[:4], got[4:]
     from_x = links.x(sends[:n_send])
     from_y = links.ring_y(*sends[n_send : n_send + 2])
-    from_corners = links.corners(sends[n_send + 2 :])
     blocks = (nb, SUB, LANES)
     outs = [shaped(*blocks), shaped(3, *blocks), shaped(3, *blocks), shaped(*blocks), shaped(6, SUB, LANES)]
     outs += [shaped(nx, ny, nz)]
     scratch = [pltpu.VMEM((17, ny, LANES), F32), pltpu.VMEM((2, ny // 2, LANES), F32)]
     *rows, inner, face_label, fine_label = call(blocks_kernel, outs, scratch)(arrays[0], arrays[2], arrays[3])
     block_label = rows[0]
-    bounds = (0, nb * 5 // 12, nb * 10 // 12, nb)
+    *corner_sends, inner = lax.optimization_barrier((*sends[n_send + 2 :], inner))
+    from_corners = links.corners(corner_sends)
+    bounds = (0, nb * 5 // 12, nb * 8 // 12, nb)
 
     def own_part(p, *more):
         out = jax.ShapeDtypeStruct((AGG, 2 * AGG), BF16) if p == 2 else shaped(AGG, 2 * AGG)

time: 83.3 us -> 84.5 us (1.014)
  waiting for transfers between devices: 18.2 us -> 19.5 us
    ppermute x20, waiting for transfers between devices: 5.87 us -> 6.73 us  [send(): return lax.ppermute(values, ('gx', 'gy', 'gz'), pairs)]
  transfers between devices with their start and end apart: 47 -> 47, of which waited for: 21 -> 18; matrix products, arithmetic and copies ran while one was open for 0% -> 0% of each run, Pallas kernels for 12% -> 12%
where the time goes in v11:
time: 84.5 us; the launch traced here: 84.4 us
  starting transfers between devices  41.1 us (49%)
  Pallas kernels  23.6 us (28%)
  waiting for transfers between devices  19.5 us (23%)
    pallas_call x24, Pallas kernels, run(): pl.pallas_call(placed, out_shape=outs, in_specs=in_specs or [VMEM] * len(...  23.6 us
    ppermute x20, starting transfers between devices, send(): return lax.ppermute(values, ('gx', 'gy', 'gz'), pairs)  20.6 us
    ppermute x9, starting transfers between devices, x(): return (lax.ppermute(sends[0], 'gx', self.ring_x),)  10.1 us
    ppermute x9, starting transfers between devices, ring_y(): lax.ppermute(to_low, 'gy', self.back(ring))  9.22 us
    ppermute x20, waiting for transfers between devices, send(): return lax.ppermute(values, ('gx', 'gy', 'gz'), pairs)  6.73 us
    ppermute x9, waiting for transfers between devices, x(): return (lax.ppermute(sends[0], 'gx', self.ring_x),)  6.3 us
    ppermute x9, waiting for transfers between devices, ring_y(): lax.ppermute(to_high, 'gy', ring)  5.49 us
  transfers between devices with their start and end apart: 47, of which 18 were waited for; matrix products, arithmetic and copies ran while one was open for 0% of the time, Pallas kernels for 12%

profile of v11, /device:TPU:0, one launch (start us, length us, event | category | flops | bytes accessed | tf_op | source)
XLA Modules:
  0.0 84.4 jit_solution(16297451313979734195)
XLA Ops:
  0.0 1.5 %shard_map.46 = (f32[24,32,128]{2,1,0:T(8,128)S(1)}, f32[24,32,128]{2,1,0:T(8,128)S(1)}, f32[24,32,128]{2,1,0:T(8,128)S(1)}, s32[12,16,64]{2,1,0:T(8,128)S(1)}, ...) custom-call(f32[24,32,128]{2,1,0:T(8,128)} %refs_0_.1, ...), custom_call_target="tpu_custom_call" | custom-call | flops 1000000 | bytes 100000 | tf_op jit(solution)/shard_map/pallas_call | solution.py:36
  1.5 3.0 %collective-permute-start = (f32[11,32,128]{2,1,0:T(8,128)S(1)}, f32[11,32,128]{2,1,0:T(8,128)S(1)}, u32[]{:S(2)}, u32[]{:S(2)}) collective-permute-start(f32[11,32,128]{2,1,0:T(8,128)S(1)} %get-tuple-element.71.refs_3_), channel_id=1, source_target_pairs={{0,16},{16,0},{1,17},{17,1},{2,18},{18,2},{3,19},{19,3},{4,20},{20... | collective-permute-start | bytes 540680 | tf_op jit(solution)/shard_map/ppermute | solution.py:301
  4.5 1.7 %collective-permute-start.2 = (f32[256,128]{1,0:T(8,128)S(1)}, f32[256,128]{1,0:T(8,128)S(1)}, u32[]{:S(2)}, u32[]{:S(2)}) collective-permute-start(f32[256,128]{1,0:T(8,128)S(1)} %get-tuple-element.73), channel_id=1, source_target_pairs={{4,0},{8,4},{12,8},{0,12},{5,1},{9,5},{13,9},{1,13},{6,2},{10,6},{... | collective-permute-start | bytes 393224 | tf_op jit(solution)/shard_map/ppermute | solution.py:311
  6.3 1.6 %shard_map.47 = (f32[12,8,128]{2,1,0:T(8,128)S(1)}, f32[3,12,8,128]{3,2,1,0:T(8,128)S(1)}, f32[3,12,8,128]{3,2,1,0:T(8,128)S(1)}, f32[12,8,128]{2,1,0:T(8,128)S(...) custom-call(f32[24,32,128]{2,1,0:T(8,128)S(1)} %get-tuple-element.64.refs_0_, ...), custom_call_target="tpu_custom_call" | custom-call | flops 1000000 | bytes 100000 | tf_op jit(solution)/shard_map/pallas_call | solution.py:36
  8.0 2.6 %collective-permute-start.4 = (f32[40,128]{1,0:T(8,128)S(1)}, f32[40,128]{1,0:T(8,128)S(1)}, u32[]{:S(2)}, u32[]{:S(2)}) collective-permute-start(f32[40,128]{1,0:T(8,128)S(1)} %get-tuple-element.78), channel_id=1, source_target_pairs={{20,0},{21,1},{22,2},{23,3},{24,4},{25,5},{26,6},{27,7},{28,8},{29... | collective-permute-start | bytes 61448 | tf_op jit(solution)/shard_map/ppermute | solution.py:297
  10.6 1.9 %shard_map.48.refs_3_ = f32[128,256]{1,0:T(8,128)S(1)} custom-call(f32[12,8,128]{2,1,0:T(8,128)S(1)} %get-tuple-element.67.refs_0_.refs_1_.refs_8_, f32[3,12,8,128]{3,2,1,0:T(8,128)S(1)} %get-tuple-element.68.refs_1_, f32[3,12,8,128]{3,2,1,0:T(8,128)S(1)} %get-tuple-element.69.refs_2_, f32[11,32,128]{2,1,0:T(8,128)S(1)} %get-tuple-element.71.refs_3_), custom_call_target="tpu_custom_call" | custom-call | flops 1000000 | bytes 100000 | tf_op jit(solution)/shard_map/pallas_call | solution.py:36
  16.9 2.5 %shard_map.51 = (f32[32,56,128]{2,1,0:T(8,128)S(1)}, f32[32,56,128]{2,1,0:T(8,128)S(1)}, f32[32,56,128]{2,1,0:T(8,128)S(1)}, f32[32,56,128]{2,1,0:T(8,128)S(1)},...) custom-call(f32[3,32,56,128]{3,2,1,0:T(8,128)S(1)} %get-tuple-element.88.refs_0_, ...), custom_call_target="tpu_custom_call" | custom-call | flops 1000000 | bytes 100000 | tf_op jit(solution)/shard_map/pallas_call | solution.py:36
  19.4 4.5 %shard_map.52 = (f32[32,56,128]{2,1,0:T(8,128)S(1)}, f32[32,56,128]{2,1,0:T(8,128)S(1)}, f32[2,56,128]{2,1,0:T(8,128)S(1)}, f32[2,56,128]{2,1,0:T(8,128)S(1)}, f...) custom-call(f32[3,32,56,128]{3,2,1,0:T(8,128)S(1)} %get-tuple-elemen, ...), custom_call_target="tpu_custom_call" | custom-call | flops 1000000 | bytes 100000 | tf_op jit(solution)/shard_map/pallas_call | solution.py:36
  25.7 1.6 %collective-permute-start.8 = (f32[8,128]{1,0:T(8,128)S(1)}, f32[8,128]{1,0:T(8,128)S(1)}, u32[]{:S(2)}, u32[]{:S(2)}) collective-permute-start(f32[8,128]{1,0:T(8,128)S(1)} %get-tuple-element.99.refs_4_.refs_2_.refs_1_.refs_3_), channel_id=1, source_target_pairs={{1,0},{2,1},{3,2},{7,3},{6,7},{5,6},{4,5},{0,4},{9,8},{10,9},{11,1... | collective-permute-start | bytes 12296 | tf_op jit(solution)/shard_map/ppermute | solution.py:297
  27.7 1.7 %shard_map.53.refs_0_ = bf16[128,256]{1,0:T(8,128)(2,1)S(1)} custom-call(f32[12,8,128]{2,1,0:T(8,128)S(1)} %get-tuple-element.67.refs_0_.refs_1_.refs_8_, f32[3,12,8,128]{3,2,1,0:T(8,128)S(1)} %get-tuple-element.68.refs_1_, f32[3,12,8,128]{3,2,1,0:T(8,128)S(1)} %get-tuple-element.69.refs_2_, f32[128,256]{1,0:T(8,128)S(1)} %shard_map.50.refs_3_, ...), custom_call_target="tpu_custom_call" | custom-call | flops 1000000 | bytes 100000 | tf_op jit(solution)/shard_map/pallas_call | solution.py:36
  35.8 1.7 %collective-permute-done.15.refs_7_.refs_3_ = f32[264,128]{1,0:T(8,128)S(1)} collective-permute-done((f32[264,128]{1,0:T(8,128)S(1)}, f32[264,128]{1,0:T(8,128)S(1)}, u32[]{:S(2)}, u32[]{:S(2)}) %collective-permute-start.15) | collective-permute-done | bytes 135200 | tf_op jit(solution)/shard_map/ppermute | solution.py:311
  37.9 1.7 %collective-permute-start.17 = (f32[88,128]{1,0:T(8,128)S(1)}, f32[88,128]{1,0:T(8,128)S(1)}, u32[]{:S(2)}, u32[]{:S(2)}) collective-permute-start(f32[88,128]{1,0:T(8,128)S(1)} %get-tuple-element.110), channel_id=1, source_target_pairs={{0,1},{1,2},{2,3},{3,7},{7,6},{6,5},{5,4},{4,0},{8,9},{9,10},{10,1... | collective-permute-start | bytes 135176 | tf_op jit(solution)/shard_map/ppermute | solution.py:297
  41.1 1.7 %collective-permute-done.20.refs_7_ = f32[8,128]{1,0:T(8,128)S(1)} collective-permute-done((f32[8,128]{1,0:T(8,128)S(1)}, f32[8,128]{1,0:T(8,128)S(1)}, u32[]{:S(2)}, u32[]{:S(2)}) %collective-permute-start.20) | collective-permute-done | bytes 4128 | tf_op jit(solution)/shard_map/ppermute | solution.py:311
  49.2 1.7 %collective-permute-start.31 = (f32[8,128]{1,0:T(8,128)S(1)}, f32[8,128]{1,0:T(8,128)S(1)}, u32[]{:S(2)}, u32[]{:S(2)}) collective-permute-start(f32[8,128]{1,0:T(8,128)S(1)} %shard_map.62.refs_3_), channel_id=1, source_target_pairs={{4,0},{8,4},{12,8},{0,12},{5,1},{9,5},{13,9},{1,13},{6,2},{10,6},{... | collective-permute-start | bytes 12296 | tf_op jit(solution)/shard_map/ppermute | solution.py:311
  50.9 1.4 %collective-permute-start.29 = (f32[8,128]{1,0:T(8,128)S(1)}, f32[8,128]{1,0:T(8,128)S(1)}, u32[]{:S(2)}, u32[]{:S(2)}) collective-permute-start(f32[8,128]{1,0:T(8,128)S(1)} %shard_map.62.refs_3_), channel_id=1, source_target_pairs={{0,16},{16,0},{1,17},{17,1},{2,18},{18,2},{3,19},{19,3},{4,20},{20... | collective-permute-start | bytes 12296 | tf_op jit(solution)/shard_map/ppermute | solution.py:301
  56.1 1.7 %collective-permute-start.36 = (f32[8,128]{1,0:T(8,128)S(1)}, f32[8,128]{1,0:T(8,128)S(1)}, u32[]{:S(2)}, u32[]{:S(2)}) collective-permute-start(f32[8,128]{1,0:T(8,128)S(1)} %shard_map.63.refs_3_), channel_id=1, source_target_pairs={{4,0},{8,4},{12,8},{0,12},{5,1},{9,5},{13,9},{1,13},{6,2},{10,6},{... | collective-permute-start | bytes 12296 | tf_op jit(solution)/shard_map/ppermute | solution.py:311
  63.4 1.7 %collective-permute-start.39 = (f32[8,128]{1,0:T(8,128)S(1)}, f32[8,128]{1,0:T(8,128)S(1)}, u32[]{:S(2)}, u32[]{:S(2)}) collective-permute-start(f32[8,128]{1,0:T(8,128)S(1)} %shard_map.64.refs_3_), channel_id=1, source_target_pairs={{0,16},{16,0},{1,17},{17,1},{2,18},{18,2},{3,19},{19,3},{4,20},{20... | collective-permute-start | bytes 12296 | tf_op jit(solution)/shard_map/ppermute | solution.py:301
  65.6 1.6 %collective-permute-start.37 = (f32[8,128]{1,0:T(8,128)S(1)}, f32[8,128]{1,0:T(8,128)S(1)}, u32[]{:S(2)}, u32[]{:S(2)}) collective-permute-start(f32[8,128]{1,0:T(8,128)S(1)} %shard_map.64.refs_3_), channel_id=1, source_target_pairs={{0,1},{1,2},{2,3},{3,7},{7,6},{6,5},{5,4},{4,0},{8,9},{9,10},{10,1... | collective-permute-start | bytes 12296 | tf_op jit(solution)/shard_map/ppermute | solution.py:297
  67.2 1.6 %collective-permute-done.38.refs_5_ = f32[8,128]{1,0:T(8,128)S(1)} collective-permute-done((f32[8,128]{1,0:T(8,128)S(1)}, f32[8,128]{1,0:T(8,128)S(1)}, u32[]{:S(2)}, u32[]{:S(2)}) %collective-permute-start.38) | collective-permute-done | bytes 4128 | tf_op jit(solution)/shard_map/ppermute | solution.py:297
  69.3 3.3 %collective-permute-done.42.refs_0_.refs_2_ = f32[8,128]{1,0:T(8,128)S(1)} collective-permute-done((f32[8,128]{1,0:T(8,128)S(1)}, f32[8,128]{1,0:T(8,128)S(1)}, u32[]{:S(2)}, u32[]{:S(2)}) %collective-permute-start.42) | collective-permute-done | bytes 4128 | tf_op jit(solution)/shard_map/ppermute | solution.py:301
  73.9 1.8 %collective-permute-done.43.refs_0_ = f32[8,128]{1,0:T(8,128)S(1)} collective-permute-done((f32[8,128]{1,0:T(8,128)S(1)}, f32[8,128]{1,0:T(8,128)S(1)}, u32[]{:S(2)}, u32[]{:S(2)}) %collective-permute-start.43) | collective-permute-done | bytes 4128 | tf_op jit(solution)/shard_map/ppermute | solution.py:311
  75.7 2.0 %collective-permute-start.45 = (f32[16,128]{1,0:T(8,128)S(1)}, f32[16,128]{1,0:T(8,128)S(1)}, u32[]{:S(2)}, u32[]{:S(2)}) collective-permute-start(f32[16,128]{1,0:T(8,128)S(1)} %shard_map.67.refs_0_), channel_id=1, source_target_pairs={{0,1},{1,2},{2,3},{3,7},{7,6},{6,5},{5,4},{4,0},{8,9},{9,10},{10,1... | collective-permute-start | bytes 24584 | tf_op jit(solution)/shard_map/ppermute | solution.py:297
  77.8 1.6 %collective-permute-done.46.refs_2_ = f32[16,128]{1,0:T(8,128)S(1)} collective-permute-done((f32[16,128]{1,0:T(8,128)S(1)}, f32[16,128]{1,0:T(8,128)S(1)}, u32[]{:S(2)}, u32[]{:S(2)}) %collective-permute-start.46) | collective-permute-done | bytes 8224 | tf_op jit(solution)/shard_map/ppermute | solution.py:297
  79.4 5.0 %shard_map.69 = f32[24,32,128]{2,1,0:T(8,128)} custom-call(f32[16,128]{1,0:T(8,128)S(1)} %shard_map.67.refs_0_, f32[16,128]{1,0:T(8,128)S(1)} %collective-permute-done.45.refs_1_, f32[16,128]{1,0:T(8,128)S(1)} %collective-permute-done.46.refs_2_, s32[16,40,128]{2,1,0:T(8,128)S(1)} %get-tuple-element.113.refs_3_, ...), custom_call_target="tpu_custom_call" | custom-call | flops 1000000 | bytes 100000 | tf_op jit(solution)/shard_map/pallas_call | solution.py:36
  (94 shorter events, 33.0 us)
Async XLA Ops:
  1.5 11.1 %collective-permute-start = (f32[11,32,128]{2,1,0:T(8,128)S(1)}, f32[11,32,128]{2,1,0:T(8,128)S(1)}, u32[]{:S(2)}, u32[]{:S(2)}) collective-permute-start(f32[11,32,128]{2,1,0:T(8,128)S(1)} %get-tuple-element.71.refs_3_), channel_id=1, source_target_pairs={{0,16},{16,0},{1,17},{17,1},{2,18},{18,2},{3,19},{19,3},{4,20},{20... | collective-permute-start | bytes 540680 | tf_op jit(solution)/shard_map/ppermute | solution.py:301
  4.5 8.0 %collective-permute-start.1 = (f32[256,128]{1,0:T(8,128)S(1)}, f32[256,128]{1,0:T(8,128)S(1)}, u32[]{:S(2)}, u32[]{:S(2)}) collective-permute-start(f32[256,128]{1,0:T(8,128)S(1)} %get-tuple-element.72), channel_id=1, source_target_pairs={{0,4},{4,8},{8,12},{12,0},{1,5},{5,9},{9,13},{13,1},{2,6},{6,10},{... | collective-permute-start | bytes 393224 | tf_op jit(solution)/shard_map/ppermute | solution.py:311
  4.5 8.0 %collective-permute-start.2 = (f32[256,128]{1,0:T(8,128)S(1)}, f32[256,128]{1,0:T(8,128)S(1)}, u32[]{:S(2)}, u32[]{:S(2)}) collective-permute-start(f32[256,128]{1,0:T(8,128)S(1)} %get-tuple-element.73), channel_id=1, source_target_pairs={{4,0},{8,4},{12,8},{0,12},{5,1},{9,5},{13,9},{1,13},{6,2},{10,6},{... | collective-permute-start | bytes 393224 | tf_op jit(solution)/shard_map/ppermute | solution.py:311
  7.9 4.6 %collective-permute-start.3 = (f32[40,128]{1,0:T(8,128)S(1)}, f32[40,128]{1,0:T(8,128)S(1)}, u32[]{:S(2)}, u32[]{:S(2)}) collective-permute-start(f32[40,128]{1,0:T(8,128)S(1)} %get-tuple-element.77), channel_id=1, source_target_pairs={{0,20},{1,21},{2,22},{3,23},{4,24},{5,25},{6,26},{7,27},{8,28},{9,... | collective-permute-start | bytes 61448 | tf_op jit(solution)/shard_map/ppermute | solution.py:297
  8.0 4.6 %collective-permute-start.4 = (f32[40,128]{1,0:T(8,128)S(1)}, f32[40,128]{1,0:T(8,128)S(1)}, u32[]{:S(2)}, u32[]{:S(2)}) collective-permute-start(f32[40,128]{1,0:T(8,128)S(1)} %get-tuple-element.78), channel_id=1, source_target_pairs={{20,0},{21,1},{22,2},{23,3},{24,4},{25,5},{26,6},{27,7},{28,8},{29... | collective-permute-start | bytes 61448 | tf_op jit(solution)/shard_map/ppermute | solution.py:297
  13.7 5.7 %collective-permute-start.6 = (f32[136,128]{1,0:T(8,128)S(1)}, f32[136,128]{1,0:T(8,128)S(1)}, u32[]{:S(2)}, u32[]{:S(2)}) collective-permute-start(f32[136,128]{1,0:T(8,128)S(1)} %get-tuple-element.86), channel_id=1, source_target_pairs={{1,0},{2,1},{3,2},{7,3},{6,7},{5,6},{4,5},{0,4},{9,8},{10,9},{11,1... | collective-permute-start | bytes 208904 | tf_op jit(solution)/shard_map/ppermute | solution.py:297
  14.8 4.6 %collective-permute-start.5 = (f32[136,128]{1,0:T(8,128)S(1)}, f32[136,128]{1,0:T(8,128)S(1)}, u32[]{:S(2)}, u32[]{:S(2)}) collective-permute-start(f32[136,128]{1,0:T(8,128)S(1)} %get-tuple-element.85.refs_4_), channel_id=1, source_target_pairs={{0,1},{1,2},{2,3},{3,7},{7,6},{6,5},{5,4},{4,0},{8,9},{9,10},{10,1... | collective-permute-start | bytes 208904 | tf_op jit(solution)/shard_map/ppermute | solution.py:297
  23.9 6.2 %collective-permute-start.9 = (f32[9,32,128]{2,1,0:T(8,128)S(1)}, f32[9,32,128]{2,1,0:T(8,128)S(1)}, u32[]{:S(2)}, u32[]{:S(2)}) collective-permute-start(f32[9,32,128]{2,1,0:T(8,128)S(1)} %shard_map.55), channel_id=1, source_target_pairs={{0,16},{16,0},{1,17},{17,1},{2,18},{18,2},{3,19},{19,3},{4,20},{20... | collective-permute-start | bytes 442376 | tf_op jit(solution)/shard_map/ppermute | solution.py:301
  24.5 5.5 %collective-permute-start.11 = (f32[8,128]{1,0:T(8,128)S(1)}, f32[8,128]{1,0:T(8,128)S(1)}, u32[]{:S(2)}, u32[]{:S(2)}) collective-permute-start(f32[8,128]{1,0:T(8,128)S(1)} %get-tuple-element.99.refs_4_.refs_2_.refs_1_.refs_3_), channel_id=1, source_target_pairs={{4,0},{8,4},{12,8},{0,12},{5,1},{9,5},{13,9},{1,13},{6,2},{10,6},{... | collective-permute-start | bytes 12296 | tf_op jit(solution)/shard_map/ppermute | solution.py:311
  25.7 4.4 %collective-permute-start.10 = (f32[8,128]{1,0:T(8,128)S(1)}, f32[8,128]{1,0:T(8,128)S(1)}, u32[]{:S(2)}, u32[]{:S(2)}) collective-permute-start(f32[8,128]{1,0:T(8,128)S(1)} %get-tuple-element.99.refs_4_.refs_2_.refs_1_.refs_3_), channel_id=1, source_target_pairs={{0,4},{4,8},{8,12},{12,0},{1,5},{5,9},{9,13},{13,1},{2,6},{6,10},{... | collective-permute-start | bytes 12296 | tf_op jit(solution)/shard_map/ppermute | solution.py:311
  25.7 4.4 %collective-permute-start.8 = (f32[8,128]{1,0:T(8,128)S(1)}, f32[8,128]{1,0:T(8,128)S(1)}, u32[]{:S(2)}, u32[]{:S(2)}) collective-permute-start(f32[8,128]{1,0:T(8,128)S(1)} %get-tuple-element.99.refs_4_.refs_2_.refs_1_.refs_3_), channel_id=1, source_target_pairs={{1,0},{2,1},{3,2},{7,3},{6,7},{5,6},{4,5},{0,4},{9,8},{10,9},{11,1... | collective-permute-start | bytes 12296 | tf_op jit(solution)/shard_map/ppermute | solution.py:297
  30.4 5.4 %collective-permute-start.16 = (f32[264,128]{1,0:T(8,128)S(1)}, f32[264,128]{1,0:T(8,128)S(1)}, u32[]{:S(2)}, u32[]{:S(2)}) collective-permute-start(f32[264,128]{1,0:T(8,128)S(1)} %get-tuple-element.106), channel_id=1, source_target_pairs={{4,0},{8,4},{12,8},{0,12},{5,1},{9,5},{13,9},{1,13},{6,2},{10,6},{... | collective-permute-start | bytes 405512 | tf_op jit(solution)/shard_map/ppermute | solution.py:311
  31.6 5.8 %collective-permute-start.15 = (f32[264,128]{1,0:T(8,128)S(1)}, f32[264,128]{1,0:T(8,128)S(1)}, u32[]{:S(2)}, u32[]{:S(2)}) collective-permute-start(f32[264,128]{1,0:T(8,128)S(1)} %get-tuple-element.105.refs_4_), channel_id=1, source_target_pairs={{0,4},{4,8},{8,12},{12,0},{1,5},{5,9},{9,13},{13,1},{2,6},{6,10},{... | collective-permute-start | bytes 405512 | tf_op jit(solution)/shard_map/ppermute | solution.py:311
  37.9 5.8 %collective-permute-start.17 = (f32[88,128]{1,0:T(8,128)S(1)}, f32[88,128]{1,0:T(8,128)S(1)}, u32[]{:S(2)}, u32[]{:S(2)}) collective-permute-start(f32[88,128]{1,0:T(8,128)S(1)} %get-tuple-element.110), channel_id=1, source_target_pairs={{0,1},{1,2},{2,3},{3,7},{7,6},{6,5},{5,4},{4,0},{8,9},{9,10},{10,1... | collective-permute-start | bytes 135176 | tf_op jit(solution)/shard_map/ppermute | solution.py:297
  39.6 4.1 %collective-permute-start.18 = (f32[88,128]{1,0:T(8,128)S(1)}, f32[88,128]{1,0:T(8,128)S(1)}, u32[]{:S(2)}, u32[]{:S(2)}) collective-permute-start(f32[88,128]{1,0:T(8,128)S(1)} %get-tuple-element.111), channel_id=1, source_target_pairs={{1,0},{2,1},{3,2},{7,3},{6,7},{5,6},{4,5},{0,4},{9,8},{10,9},{11,1... | collective-permute-start | bytes 135176 | tf_op jit(solution)/shard_map/ppermute | solution.py:297
  49.2 5.1 %collective-permute-start.31 = (f32[8,128]{1,0:T(8,128)S(1)}, f32[8,128]{1,0:T(8,128)S(1)}, u32[]{:S(2)}, u32[]{:S(2)}) collective-permute-start(f32[8,128]{1,0:T(8,128)S(1)} %shard_map.62.refs_3_), channel_id=1, source_target_pairs={{4,0},{8,4},{12,8},{0,12},{5,1},{9,5},{13,9},{1,13},{6,2},{10,6},{... | collective-permute-start | bytes 12296 | tf_op jit(solution)/shard_map/ppermute | solution.py:311
  56.1 4.3 %collective-permute-start.36 = (f32[8,128]{1,0:T(8,128)S(1)}, f32[8,128]{1,0:T(8,128)S(1)}, u32[]{:S(2)}, u32[]{:S(2)}) collective-permute-start(f32[8,128]{1,0:T(8,128)S(1)} %shard_map.63.refs_3_), channel_id=1, source_target_pairs={{4,0},{8,4},{12,8},{0,12},{5,1},{9,5},{13,9},{1,13},{6,2},{10,6},{... | collective-permute-start | bytes 12296 | tf_op jit(solution)/shard_map/ppermute | solution.py:311
  57.7 3.6 %collective-permute-start.34 = (f32[8,128]{1,0:T(8,128)S(1)}, f32[8,128]{1,0:T(8,128)S(1)}, u32[]{:S(2)}, u32[]{:S(2)}) collective-permute-start(f32[8,128]{1,0:T(8,128)S(1)} %shard_map.63.refs_3_), channel_id=1, source_target_pairs={{0,16},{16,0},{1,17},{17,1},{2,18},{18,2},{3,19},{19,3},{4,20},{20... | collective-permute-start | bytes 12296 | tf_op jit(solution)/shard_map/ppermute | solution.py:301
  62.1 5.1 %collective-permute-start.41 = (f32[8,128]{1,0:T(8,128)S(1)}, f32[8,128]{1,0:T(8,128)S(1)}, u32[]{:S(2)}, u32[]{:S(2)}) collective-permute-start(f32[8,128]{1,0:T(8,128)S(1)} %shard_map.64.refs_3_), channel_id=1, source_target_pairs={{4,0},{8,4},{12,8},{0,12},{5,1},{9,5},{13,9},{1,13},{6,2},{10,6},{... | collective-permute-start | bytes 12296 | tf_op jit(solution)/shard_map/ppermute | solution.py:311
  63.4 3.8 %collective-permute-start.40 = (f32[8,128]{1,0:T(8,128)S(1)}, f32[8,128]{1,0:T(8,128)S(1)}, u32[]{:S(2)}, u32[]{:S(2)}) collective-permute-start(f32[8,128]{1,0:T(8,128)S(1)} %shard_map.64.refs_3_), channel_id=1, source_target_pairs={{0,4},{4,8},{8,12},{12,0},{1,5},{5,9},{9,13},{13,1},{2,6},{6,10},{... | collective-permute-start | bytes 12296 | tf_op jit(solution)/shard_map/ppermute | solution.py:311
  63.4 3.8 %collective-permute-start.39 = (f32[8,128]{1,0:T(8,128)S(1)}, f32[8,128]{1,0:T(8,128)S(1)}, u32[]{:S(2)}, u32[]{:S(2)}) collective-permute-start(f32[8,128]{1,0:T(8,128)S(1)} %shard_map.64.refs_3_), channel_id=1, source_target_pairs={{0,16},{16,0},{1,17},{17,1},{2,18},{18,2},{3,19},{19,3},{4,20},{20... | collective-permute-start | bytes 12296 | tf_op jit(solution)/shard_map/ppermute | solution.py:301
  68.9 3.7 %collective-permute-start.42 = (f32[8,128]{1,0:T(8,128)S(1)}, f32[8,128]{1,0:T(8,128)S(1)}, u32[]{:S(2)}, u32[]{:S(2)}) collective-permute-start(f32[8,128]{1,0:T(8,128)S(1)} %shard_map.65.refs_1_), channel_id=1, source_target_pairs={{0,16},{16,0},{1,17},{17,1},{2,18},{18,2},{3,19},{19,3},{4,20},{20... | collective-permute-start | bytes 12296 | tf_op jit(solution)/shard_map/ppermute | solution.py:301
  75.7 3.7 %collective-permute-start.46 = (f32[16,128]{1,0:T(8,128)S(1)}, f32[16,128]{1,0:T(8,128)S(1)}, u32[]{:S(2)}, u32[]{:S(2)}) collective-permute-start(f32[16,128]{1,0:T(8,128)S(1)} %shard_map.67.refs_0_), channel_id=1, source_target_pairs={{1,0},{2,1},{3,2},{7,3},{6,7},{5,6},{4,5},{0,4},{9,8},{10,9},{11,1... | collective-permute-start | bytes 24584 | tf_op jit(solution)/shard_map/ppermute | solution.py:297
  75.7 3.7 %collective-permute-start.45 = (f32[16,128]{1,0:T(8,128)S(1)}, f32[16,128]{1,0:T(8,128)S(1)}, u32[]{:S(2)}, u32[]{:S(2)}) collective-permute-start(f32[16,128]{1,0:T(8,128)S(1)} %shard_map.67.refs_0_), channel_id=1, source_target_pairs={{0,1},{1,2},{2,3},{3,7},{7,6},{6,5},{5,4},{4,0},{8,9},{9,10},{10,1... | collective-permute-start | bytes 24584 | tf_op jit(solution)/shard_map/ppermute | solution.py:297
  (23 other events, 70.4 us)

commit v12 on v10

--- a/solution.py
+++ b/solution.py
@@ -756,15 +756,14 @@
     out[...] = (1.0 - OMEGA_COARSE) * own[...] + scaled_rhs[...] + scale[...] * applied
 
 
-def ride_kernel(count, flags, pre, fine_label, coarse, *outs):
-    nx = pre.shape[0]
+def ride_kernel(count, flags, field, coarse, *outs):
+    nx = field.shape[0]
     for s, out in enumerate(outs):
         at = jnp.where(flags[IX] == 0, nx - HALO, 0) if count == 2 else (nx - HALO, 0)[s]
-        for f, field in enumerate((pre, fine_label)):
-            for x in range(HALO):
-                out[HALO * f + x] = field[at + x]
-        out[2 * HALO] = jnp.zeros(out.shape[1:], F32)
-        out[2 * HALO, :SUB] = coarse[...]
+        for x in range(HALO):
+            out[x] = field[at + x]
+        out[HALO] = jnp.zeros(out.shape[1:], F32)
+        out[HALO, :SUB] = coarse[...]
 
 
 def three_kernel(flags, low, mid, high, out):
@@ -782,8 +781,8 @@
     frame = Frame(wide_ref.shape[1] - 2 * HALO, wide_ref.shape[2] - 2 * (SUB + HALO))
     tall = frame.tall
     for b in range(frame.wide // 2):
-        main[b] = wide_ref[1, 2 * b, frame.span].astype(jnp.int32)
-    rows = pl.ds(tall, tall)
+        main[b] = wide_ref[0, 2 * b, frame.span].astype(jnp.int32)
+    rows = pl.ds(0, tall)
     for s, values in enumerate(sides(flags, forth[rows], back[rows])):
         ends[s] = values.astype(jnp.int32)
 
@@ -882,22 +881,24 @@
     arrays, sends = got[:4], got[4:]
     from_x = links.x(sends[:n_send])
     from_y = links.ring_y(*sends[n_send : n_send + 2])
-    from_corners = links.corners(sends[n_send + 2 :])
     blocks = (nb, SUB, LANES)
     outs = [shaped(*blocks), shaped(3, *blocks), shaped(3, *blocks), shaped(*blocks), shaped(6, SUB, LANES)]
     outs += [shaped(nx, ny, nz)]
     scratch = [pltpu.VMEM((17, ny, LANES), F32), pltpu.VMEM((2, ny // 2, LANES), F32)]
     *rows, inner, face_label, fine_label = call(blocks_kernel, outs, scratch)(arrays[0], arrays[2], arrays[3])
     block_label = rows[0]
-    bounds = (0, nb * 5 // 12, nb * 10 // 12, nb)
+    bounds = [nb * n // 12 for n in (0, 5, 8, 11, 12)]
 
     def own_part(p, *more):
-        out = jax.ShapeDtypeStruct((AGG, 2 * AGG), BF16) if p == 2 else shaped(AGG, 2 * AGG)
+        out = jax.ShapeDtypeStruct((AGG, 2 * AGG), BF16) if p == 3 else shaped(AGG, 2 * AGG)
         return call(functools.partial(own_kernel, bounds[p], bounds[p + 1], nb), [out])(*rows, *more)[0]
 
     own_tile = own_part(0, sends[0])
+    *corner_sends, own_tile = lax.optimization_barrier((*sends[n_send + 2 :], own_tile))
+    from_corners = links.corners(corner_sends)
+    own_tile = own_part(1, own_tile, sends[0])
     got = lax.optimization_barrier((*from_x, *from_y, *from_corners, own_tile))
-    from_x, from_y, from_corners = got[:n_send], got[n_send : n_send + 2], got[n_send + 2 : -1]
+    from_x, from_y, from_corners, own_tile = got[:n_send], got[n_send : n_send + 2], got[n_send + 2 : -1], got[-1]
     size = len(WIDTHS) * frame.tall
     wide, *sends = call(
         functools.partial(first_frame_kernel, n_x, WIDTHS),
@@ -908,7 +909,7 @@
     *fields, weight_xy, some_diag = call(functools.partial(fields_kernel, n_x), outs, limit=24)(
         wide, block_label, inner, face_label
     )
-    own_tile = own_part(1, own_tile, sends[0])
+    own_tile = own_part(2, own_tile, sends[0])
     halo = (wide, *links.z(*sends))
     *halo, own_tile = lax.optimization_barrier((*halo, own_tile))
     outs = [shaped(*frame.main)] * 2 + [shaped(*frame.ends)] * 6 + [shaped(nx, ny, nz)]
@@ -920,7 +921,7 @@
     )
     fields, pre = (*fields[:3], *got[:8]), got[8]
     weight_z, scaled_rhs, scale = got[9:]
-    own_tile = own_part(2, own_tile, scaled_rhs)
+    own_tile = own_part(3, own_tile, scaled_rhs)
     tiles = call(
         functools.partial(faces_kernel, n_x, nb),
         jax.ShapeDtypeStruct(((n_send + 5) * AGG, 2 * AGG), BF16),
@@ -928,25 +929,29 @@
     )(own_tile, face_label, weight_xy, weight_z, from_x[0], from_x[-1], *from_y, *halo[1:])
     coarse = scaled_rhs
 
-    def turn(**more):
+    def turn(coarse, **more):
         near = links.near(coarse, **more)
         return call(turn_kernel, shaped(SUB, AGG))(tiles, scaled_rhs, scale, coarse, *near), near
 
-    both = (pre, fine_label)
-    rides = call(functools.partial(ride_kernel, n_x), [shaped(2 * HALO + 1, ny, nz)] * n_send)(*both, coarse)
-    coarse, near = turn(x=rides)
-    from_x = near[2:-2]
-    rides = send_y(both, coarse, from_x)
-    frames = framed(both, from_x, rides[0])
-    coarse, near = turn(y=rides)
-    wide, *rides = send_z(frames, near[-2:], coarse)
-    coarse, near = turn(z=rides)
-    halo = (wide, *near[:2])
+    def ridden(field, coarse):
+        kernel = functools.partial(ride_kernel, n_x)
+        rides = call(kernel, [shaped(HALO + 1, ny, nz)] * n_send)(field, coarse)
+        coarse, near = turn(coarse, x=rides)
+        from_x = near[2:-2]
+        rides = send_y((field,), coarse, from_x)
+        frames = framed((field,), from_x, rides[0])
+        coarse, near = turn(coarse, y=rides)
+        wide, *rides = send_z(frames, near[-2:], coarse)
+        coarse, near = turn(coarse, z=rides)
+        return coarse, (wide, *near[:2])
+
+    coarse, halo = ridden(pre, coarse)
+    coarse, label_halo = ridden(fine_label, coarse)
     outs = [jax.ShapeDtypeStruct((frame.wide // 2, frame.tall, nz), jnp.int32)]
     outs += [jax.ShapeDtypeStruct((2, frame.tall, nz), jnp.int32)]
-    lifts = call(lift_kernel, outs)(*halo)
-    for _ in range(KC - 4):
-        coarse, _ = turn()
+    lifts = call(lift_kernel, outs)(*label_halo)
+    for _ in range(KC - 7):
+        coarse, _ = turn(coarse)
     from_x = links.x([coarse] * n_send)
     three = call(three_kernel, shaped(SUB, AGG))(from_x[0], coarse, from_x[-1])
     low, high = links.ring_y(three, three)

time: 83.3 us -> 85.8 us (1.030)
  starting transfers between devices: 41.1 us -> 42.5 us
  waiting for transfers between devices: 18.2 us -> 19.2 us
    ppermute x9, starting transfers between devices: 10.2 us -> 11.4 us  [x(): return (lax.ppermute(sends[0], 'gx', self.ring_x),)]
    ppermute x9, waiting for transfers between devices: 5.19 us -> 6.32 us  [ring_y(): lax.ppermute(to_high, 'gy', ring)]
    pallas_call x24 -> x29, Pallas kernels: 23.6 us -> 23.8 us  [run(): pl.pallas_call(placed, out_shape=outs, in_specs=in_specs or [VMEM] * len(...]
  transfers between devices with their start and end apart: 47 -> 47, of which waited for: 21 -> 22; matrix products, arithmetic and copies ran while one was open for 0% -> 0% of each run, Pallas kernels for 12% -> 12%
where the time goes in v12:
time: 85.8 us; the launch traced here: 85.7 us
  starting transfers between devices  42.5 us (50%)
  Pallas kernels  23.8 us (28%)
  waiting for transfers between devices  19.2 us (22%)
    pallas_call x29, Pallas kernels, run(): pl.pallas_call(placed, out_shape=outs, in_specs=in_specs or [VMEM] * len(...  23.8 us
    ppermute x20, starting transfers between devices, send(): return lax.ppermute(values, ('gx', 'gy', 'gz'), pairs)  20.4 us
    ppermute x9, starting transfers between devices, x(): return (lax.ppermute(sends[0], 'gx', self.ring_x),)  11.4 us
    ppermute x9, starting transfers between devices, ring_y(): lax.ppermute(to_low, 'gy', self.back(ring))  9.97 us
    ppermute x9, waiting for transfers between devices, ring_y(): lax.ppermute(to_high, 'gy', ring)  6.32 us
    ppermute x20, waiting for transfers between devices, send(): return lax.ppermute(values, ('gx', 'gy', 'gz'), pairs)  6.12 us
    ppermute x9, waiting for transfers between devices, x(): return (lax.ppermute(sends[0], 'gx', self.ring_x),)  5.94 us
  transfers between devices with their start and end apart: 47, of which 22 were waited for; matrix products, arithmetic and copies ran while one was open for 0% of the time, Pallas kernels for 12%

profile of v12, /device:TPU:0, one launch (start us, length us, event | category | flops | bytes accessed | tf_op | source)
XLA Modules:
  0.0 85.7 jit_solution(7759189087771452418)
XLA Ops:
  0.0 1.5 %shard_map.46 = (f32[24,32,128]{2,1,0:T(8,128)S(1)}, f32[24,32,128]{2,1,0:T(8,128)S(1)}, f32[24,32,128]{2,1,0:T(8,128)S(1)}, s32[12,16,64]{2,1,0:T(8,128)S(1)}, ...) custom-call(f32[24,32,128]{2,1,0:T(8,128)} %refs_0_.1, ...), custom_call_target="tpu_custom_call" | custom-call | flops 1000000 | bytes 100000 | tf_op jit(solution)/shard_map/pallas_call | solution.py:36
  1.5 3.0 %collective-permute-start = (f32[11,32,128]{2,1,0:T(8,128)S(1)}, f32[11,32,128]{2,1,0:T(8,128)S(1)}, u32[]{:S(2)}, u32[]{:S(2)}) collective-permute-start(f32[11,32,128]{2,1,0:T(8,128)S(1)} %get-tuple-element.80.refs_3_.refs_4_), channel_id=1, source_target_pairs={{0,16},{16,0},{1,17},{17,1},{2,18},{18,2},{3,19},{19,3},{4,20},{20... | collective-permute-start | bytes 540680 | tf_op jit(solution)/shard_map/ppermute | solution.py:301
  4.5 1.7 %collective-permute-start.2 = (f32[256,128]{1,0:T(8,128)S(1)}, f32[256,128]{1,0:T(8,128)S(1)}, u32[]{:S(2)}, u32[]{:S(2)}) collective-permute-start(f32[256,128]{1,0:T(8,128)S(1)} %get-tuple-element.82), channel_id=1, source_target_pairs={{4,0},{8,4},{12,8},{0,12},{5,1},{9,5},{13,9},{1,13},{6,2},{10,6},{... | collective-permute-start | bytes 393224 | tf_op jit(solution)/shard_map/ppermute | solution.py:311
  6.3 1.6 %shard_map.47 = (f32[12,8,128]{2,1,0:T(8,128)S(1)}, f32[3,12,8,128]{3,2,1,0:T(8,128)S(1)}, f32[3,12,8,128]{3,2,1,0:T(8,128)S(1)}, f32[12,8,128]{2,1,0:T(8,128)S(...) custom-call(f32[24,32,128]{2,1,0:T(8,128)S(1)} %get-tuple-element.73.refs_0_, ...), custom_call_target="tpu_custom_call" | custom-call | flops 1000000 | bytes 100000 | tf_op jit(solution)/shard_map/pallas_call | solution.py:36
  7.9 1.9 %shard_map.48.refs_3_ = f32[128,256]{1,0:T(8,128)S(1)} custom-call(f32[12,8,128]{2,1,0:T(8,128)S(1)} %get-tuple-element.76.refs_0_.refs_1_.refs_8_, f32[3,12,8,128]{3,2,1,0:T(8,128)S(1)} %get-tuple-element.77.refs_1_, f32[3,12,8,128]{3,2,1,0:T(8,128)S(1)} %get-tuple-element.78.refs_2_, f32[11,32,128]{2,1,0:T(8,128)S(1)} %get-tuple-element.80.refs_3_.refs_4_), custom_call_target="tpu_custom_call" | custom-call | flops 1000000 | bytes 100000 | tf_op jit(solution)/shard_map/pallas_call | solution.py:36
  9.9 2.6 %collective-permute-start.4 = (f32[40,128]{1,0:T(8,128)S(1)}, f32[40,128]{1,0:T(8,128)S(1)}, u32[]{:S(2)}, u32[]{:S(2)}) collective-permute-start(f32[40,128]{1,0:T(8,128)S(1)} %get-tuple-element.86), channel_id=1, source_target_pairs={{20,0},{21,1},{22,2},{23,3},{24,4},{25,5},{26,6},{27,7},{28,8},{29... | collective-permute-start | bytes 61448 | tf_op jit(solution)/shard_map/ppermute | solution.py:297
  18.7 2.5 %shard_map.52 = (f32[32,56,128]{2,1,0:T(8,128)S(1)}, f32[32,56,128]{2,1,0:T(8,128)S(1)}, f32[32,56,128]{2,1,0:T(8,128)S(1)}, f32[32,56,128]{2,1,0:T(8,128)S(1)},...) custom-call(f32[3,32,56,128]{3,2,1,0:T(8,128)S(1)} %get-tuple-element.98.refs_0_, ...), custom_call_target="tpu_custom_call" | custom-call | flops 1000000 | bytes 100000 | tf_op jit(solution)/shard_map/pallas_call | solution.py:36
  21.3 4.5 %shard_map.53 = (f32[32,56,128]{2,1,0:T(8,128)S(1)}, f32[32,56,128]{2,1,0:T(8,128)S(1)}, f32[2,56,128]{2,1,0:T(8,128)S(1)}, f32[2,56,128]{2,1,0:T(8,128)S(1)}, f...) custom-call(f32[3,32,56,128]{3,2,1,0:T(8,128)S(1)} %get-tuple-elemen, ...), custom_call_target="tpu_custom_call" | custom-call | flops 1000000 | bytes 100000 | tf_op jit(solution)/shard_map/pallas_call | solution.py:36
  27.6 1.6 %collective-permute-start.8 = (f32[8,128]{1,0:T(8,128)S(1)}, f32[8,128]{1,0:T(8,128)S(1)}, u32[]{:S(2)}, u32[]{:S(2)}) collective-permute-start(f32[8,128]{1,0:T(8,128)S(1)} %get-tuple-element.109.refs_4_.refs_1_.refs_3_), channel_id=1, source_target_pairs={{1,0},{2,1},{3,2},{7,3},{6,7},{5,6},{4,5},{0,4},{9,8},{10,9},{11,1... | collective-permute-start | bytes 12296 | tf_op jit(solution)/shard_map/ppermute | solution.py:297
  31.6 2.0 %collective-permute-start.16 = (f32[136,128]{1,0:T(8,128)S(1)}, f32[136,128]{1,0:T(8,128)S(1)}, u32[]{:S(2)}, u32[]{:S(2)}) collective-permute-start(f32[136,128]{1,0:T(8,128)S(1)} %get-tuple-element.115), channel_id=1, source_target_pairs={{4,0},{8,4},{12,8},{0,12},{5,1},{9,5},{13,9},{1,13},{6,2},{10,6},{... | collective-permute-start | bytes 208904 | tf_op jit(solution)/shard_map/ppermute | solution.py:311
  38.3 1.8 %collective-permute-start.17 = (f32[48,128]{1,0:T(8,128)S(1)}, f32[48,128]{1,0:T(8,128)S(1)}, u32[]{:S(2)}, u32[]{:S(2)}) collective-permute-start(f32[48,128]{1,0:T(8,128)S(1)} %get-tuple-element.119), channel_id=1, source_target_pairs={{0,1},{1,2},{2,3},{3,7},{7,6},{6,5},{5,4},{4,0},{8,9},{9,10},{10,1... | collective-permute-start | bytes 73736 | tf_op jit(solution)/shard_map/ppermute | solution.py:297
  41.2 1.5 %collective-permute-start.19 = (f32[8,128]{1,0:T(8,128)S(1)}, f32[8,128]{1,0:T(8,128)S(1)}, u32[]{:S(2)}, u32[]{:S(2)}) collective-permute-start(f32[8,128]{1,0:T(8,128)S(1)} %shard_map.59.refs_5_.refs_3_), channel_id=1, source_target_pairs={{0,16},{16,0},{1,17},{17,1},{2,18},{18,2},{3,19},{19,3},{4,20},{20... | collective-permute-start | bytes 12296 | tf_op jit(solution)/shard_map/ppermute | solution.py:301
  42.7 1.5 %collective-permute-done.20.refs_7_ = f32[8,128]{1,0:T(8,128)S(1)} collective-permute-done((f32[8,128]{1,0:T(8,128)S(1)}, f32[8,128]{1,0:T(8,128)S(1)}, u32[]{:S(2)}, u32[]{:S(2)}) %collective-permute-start.20) | collective-permute-done | bytes 4128 | tf_op jit(solution)/shard_map/ppermute | solution.py:311
  45.0 1.6 %collective-permute-start.24 = (f32[5,32,128]{2,1,0:T(8,128)S(1)}, f32[5,32,128]{2,1,0:T(8,128)S(1)}, u32[]{:S(2)}, u32[]{:S(2)}) collective-permute-start(f32[5,32,128]{2,1,0:T(8,128)S(1)} %shard_map.63), channel_id=1, source_target_pairs={{0,16},{16,0},{1,17},{17,1},{2,18},{18,2},{3,19},{19,3},{4,20},{20... | collective-permute-start | bytes 245768 | tf_op jit(solution)/shard_map/ppermute | solution.py:301
  50.9 1.8 %collective-permute-start.31 = (f32[136,128]{1,0:T(8,128)S(1)}, f32[136,128]{1,0:T(8,128)S(1)}, u32[]{:S(2)}, u32[]{:S(2)}) collective-permute-start(f32[136,128]{1,0:T(8,128)S(1)} %get-tuple-element.123), channel_id=1, source_target_pairs={{4,0},{8,4},{12,8},{0,12},{5,1},{9,5},{13,9},{1,13},{6,2},{10,6},{... | collective-permute-start | bytes 208904 | tf_op jit(solution)/shard_map/ppermute | solution.py:311
  57.6 1.7 %collective-permute-start.32 = (f32[48,128]{1,0:T(8,128)S(1)}, f32[48,128]{1,0:T(8,128)S(1)}, u32[]{:S(2)}, u32[]{:S(2)}) collective-permute-start(f32[48,128]{1,0:T(8,128)S(1)} %get-tuple-element.127), channel_id=1, source_target_pairs={{0,1},{1,2},{2,3},{3,7},{7,6},{6,5},{5,4},{4,0},{8,9},{9,10},{10,1... | collective-permute-start | bytes 73736 | tf_op jit(solution)/shard_map/ppermute | solution.py:297
  60.3 1.5 %collective-permute-start.34 = (f32[8,128]{1,0:T(8,128)S(1)}, f32[8,128]{1,0:T(8,128)S(1)}, u32[]{:S(2)}, u32[]{:S(2)}) collective-permute-start(f32[8,128]{1,0:T(8,128)S(1)} %shard_map.66.refs_5_.refs_3_), channel_id=1, source_target_pairs={{0,16},{16,0},{1,17},{17,1},{2,18},{18,2},{3,19},{19,3},{4,20},{20... | collective-permute-start | bytes 12296 | tf_op jit(solution)/shard_map/ppermute | solution.py:301
  61.8 1.5 %collective-permute-done.35.refs_7_ = f32[8,128]{1,0:T(8,128)S(1)} collective-permute-done((f32[8,128]{1,0:T(8,128)S(1)}, f32[8,128]{1,0:T(8,128)S(1)}, u32[]{:S(2)}, u32[]{:S(2)}) %collective-permute-start.35) | collective-permute-done | bytes 4128 | tf_op jit(solution)/shard_map/ppermute | solution.py:311
  65.0 1.5 %collective-permute-start.39 = (f32[8,128]{1,0:T(8,128)S(1)}, f32[8,128]{1,0:T(8,128)S(1)}, u32[]{:S(2)}, u32[]{:S(2)}) collective-permute-start(f32[8,128]{1,0:T(8,128)S(1)} %shard_map.69.refs_3_), channel_id=1, source_target_pairs={{0,16},{16,0},{1,17},{17,1},{2,18},{18,2},{3,19},{19,3},{4,20},{20... | collective-permute-start | bytes 12296 | tf_op jit(solution)/shard_map/ppermute | solution.py:301
  70.9 3.1 %collective-permute-done.42.refs_0_.refs_2_ = f32[8,128]{1,0:T(8,128)S(1)} collective-permute-done((f32[8,128]{1,0:T(8,128)S(1)}, f32[8,128]{1,0:T(8,128)S(1)}, u32[]{:S(2)}, u32[]{:S(2)}) %collective-permute-start.42) | collective-permute-done | bytes 4128 | tf_op jit(solution)/shard_map/ppermute | solution.py:301
  75.3 1.8 %collective-permute-done.43.refs_0_ = f32[8,128]{1,0:T(8,128)S(1)} collective-permute-done((f32[8,128]{1,0:T(8,128)S(1)}, f32[8,128]{1,0:T(8,128)S(1)}, u32[]{:S(2)}, u32[]{:S(2)}) %collective-permute-start.43) | collective-permute-done | bytes 4128 | tf_op jit(solution)/shard_map/ppermute | solution.py:311
  77.0 2.0 %collective-permute-start.45 = (f32[16,128]{1,0:T(8,128)S(1)}, f32[16,128]{1,0:T(8,128)S(1)}, u32[]{:S(2)}, u32[]{:S(2)}) collective-permute-start(f32[16,128]{1,0:T(8,128)S(1)} %shard_map.72.refs_0_), channel_id=1, source_target_pairs={{0,1},{1,2},{2,3},{3,7},{7,6},{6,5},{5,4},{4,0},{8,9},{9,10},{10,1... | collective-permute-start | bytes 24584 | tf_op jit(solution)/shard_map/ppermute | solution.py:297
  79.1 1.7 %collective-permute-done.46.refs_2_ = f32[16,128]{1,0:T(8,128)S(1)} collective-permute-done((f32[16,128]{1,0:T(8,128)S(1)}, f32[16,128]{1,0:T(8,128)S(1)}, u32[]{:S(2)}, u32[]{:S(2)}) %collective-permute-start.46) | collective-permute-done | bytes 8224 | tf_op jit(solution)/shard_map/ppermute | solution.py:297
  80.7 4.9 %shard_map.74 = f32[24,32,128]{2,1,0:T(8,128)} custom-call(f32[16,128]{1,0:T(8,128)S(1)} %shard_map.72.refs_0_, f32[16,128]{1,0:T(8,128)S(1)} %collective-permute-done.45.refs_1_, f32[16,128]{1,0:T(8,128)S(1)} %collective-permute-done.46.refs_2_, s32[16,40,128]{2,1,0:T(8,128)S(1)} %get-tuple-element.130.refs_3_, ...), custom_call_target="tpu_custom_call" | custom-call | flops 1000000 | bytes 100000 | tf_op jit(solution)/shard_map/pallas_call | solution.py:36
  (99 shorter events, 34.6 us)
Async XLA Ops:
  1.5 12.9 %collective-permute-start = (f32[11,32,128]{2,1,0:T(8,128)S(1)}, f32[11,32,128]{2,1,0:T(8,128)S(1)}, u32[]{:S(2)}, u32[]{:S(2)}) collective-permute-start(f32[11,32,128]{2,1,0:T(8,128)S(1)} %get-tuple-element.80.refs_3_.refs_4_), channel_id=1, source_target_pairs={{0,16},{16,0},{1,17},{17,1},{2,18},{18,2},{3,19},{19,3},{4,20},{20... | collective-permute-start | bytes 540680 | tf_op jit(solution)/shard_map/ppermute | solution.py:301
  4.5 9.9 %collective-permute-start.1 = (f32[256,128]{1,0:T(8,128)S(1)}, f32[256,128]{1,0:T(8,128)S(1)}, u32[]{:S(2)}, u32[]{:S(2)}) collective-permute-start(f32[256,128]{1,0:T(8,128)S(1)} %get-tuple-element.81), channel_id=1, source_target_pairs={{0,4},{4,8},{8,12},{12,0},{1,5},{5,9},{9,13},{13,1},{2,6},{6,10},{... | collective-permute-start | bytes 393224 | tf_op jit(solution)/shard_map/ppermute | solution.py:311
  4.5 9.9 %collective-permute-start.2 = (f32[256,128]{1,0:T(8,128)S(1)}, f32[256,128]{1,0:T(8,128)S(1)}, u32[]{:S(2)}, u32[]{:S(2)}) collective-permute-start(f32[256,128]{1,0:T(8,128)S(1)} %get-tuple-element.82), channel_id=1, source_target_pairs={{4,0},{8,4},{12,8},{0,12},{5,1},{9,5},{13,9},{1,13},{6,2},{10,6},{... | collective-permute-start | bytes 393224 | tf_op jit(solution)/shard_map/ppermute | solution.py:311
  9.9 4.2 %collective-permute-start.3 = (f32[40,128]{1,0:T(8,128)S(1)}, f32[40,128]{1,0:T(8,128)S(1)}, u32[]{:S(2)}, u32[]{:S(2)}) collective-permute-start(f32[40,128]{1,0:T(8,128)S(1)} %get-tuple-element.85), channel_id=1, source_target_pairs={{0,20},{1,21},{2,22},{3,23},{4,24},{5,25},{6,26},{7,27},{8,28},{9,... | collective-permute-start | bytes 61448 | tf_op jit(solution)/shard_map/ppermute | solution.py:297
  9.9 4.5 %collective-permute-start.4 = (f32[40,128]{1,0:T(8,128)S(1)}, f32[40,128]{1,0:T(8,128)S(1)}, u32[]{:S(2)}, u32[]{:S(2)}) collective-permute-start(f32[40,128]{1,0:T(8,128)S(1)} %get-tuple-element.86), channel_id=1, source_target_pairs={{20,0},{21,1},{22,2},{23,3},{24,4},{25,5},{26,6},{27,7},{28,8},{29... | collective-permute-start | bytes 61448 | tf_op jit(solution)/shard_map/ppermute | solution.py:297
  15.5 5.7 %collective-permute-start.6 = (f32[136,128]{1,0:T(8,128)S(1)}, f32[136,128]{1,0:T(8,128)S(1)}, u32[]{:S(2)}, u32[]{:S(2)}) collective-permute-start(f32[136,128]{1,0:T(8,128)S(1)} %get-tuple-element.95), channel_id=1, source_target_pairs={{1,0},{2,1},{3,2},{7,3},{6,7},{5,6},{4,5},{0,4},{9,8},{10,9},{11,1... | collective-permute-start | bytes 208904 | tf_op jit(solution)/shard_map/ppermute | solution.py:297
  16.7 4.5 %collective-permute-start.5 = (f32[136,128]{1,0:T(8,128)S(1)}, f32[136,128]{1,0:T(8,128)S(1)}, u32[]{:S(2)}, u32[]{:S(2)}) collective-permute-start(f32[136,128]{1,0:T(8,128)S(1)} %get-tuple-element.94.refs_4_), channel_id=1, source_target_pairs={{0,1},{1,2},{2,3},{3,7},{7,6},{6,5},{5,4},{4,0},{8,9},{9,10},{10,1... | collective-permute-start | bytes 208904 | tf_op jit(solution)/shard_map/ppermute | solution.py:297
  25.7 5.6 %collective-permute-start.9 = (f32[5,32,128]{2,1,0:T(8,128)S(1)}, f32[5,32,128]{2,1,0:T(8,128)S(1)}, u32[]{:S(2)}, u32[]{:S(2)}) collective-permute-start(f32[5,32,128]{2,1,0:T(8,128)S(1)} %shard_map.56), channel_id=1, source_target_pairs={{0,16},{16,0},{1,17},{17,1},{2,18},{18,2},{3,19},{19,3},{4,20},{20... | collective-permute-start | bytes 245768 | tf_op jit(solution)/shard_map/ppermute | solution.py:301
  26.5 4.3 %collective-permute-start.11 = (f32[8,128]{1,0:T(8,128)S(1)}, f32[8,128]{1,0:T(8,128)S(1)}, u32[]{:S(2)}, u32[]{:S(2)}) collective-permute-start(f32[8,128]{1,0:T(8,128)S(1)} %get-tuple-element.109.refs_4_.refs_1_.refs_3_), channel_id=1, source_target_pairs={{4,0},{8,4},{12,8},{0,12},{5,1},{9,5},{13,9},{1,13},{6,2},{10,6},{... | collective-permute-start | bytes 12296 | tf_op jit(solution)/shard_map/ppermute | solution.py:311
  27.6 3.6 %collective-permute-start.8 = (f32[8,128]{1,0:T(8,128)S(1)}, f32[8,128]{1,0:T(8,128)S(1)}, u32[]{:S(2)}, u32[]{:S(2)}) collective-permute-start(f32[8,128]{1,0:T(8,128)S(1)} %get-tuple-element.109.refs_4_.refs_1_.refs_3_), channel_id=1, source_target_pairs={{1,0},{2,1},{3,2},{7,3},{6,7},{5,6},{4,5},{0,4},{9,8},{10,9},{11,1... | collective-permute-start | bytes 12296 | tf_op jit(solution)/shard_map/ppermute | solution.py:297
  31.6 6.1 %collective-permute-start.16 = (f32[136,128]{1,0:T(8,128)S(1)}, f32[136,128]{1,0:T(8,128)S(1)}, u32[]{:S(2)}, u32[]{:S(2)}) collective-permute-start(f32[136,128]{1,0:T(8,128)S(1)} %get-tuple-element.115), channel_id=1, source_target_pairs={{4,0},{8,4},{12,8},{0,12},{5,1},{9,5},{13,9},{1,13},{6,2},{10,6},{... | collective-permute-start | bytes 208904 | tf_op jit(solution)/shard_map/ppermute | solution.py:311
  33.5 4.4 %collective-permute-start.15 = (f32[136,128]{1,0:T(8,128)S(1)}, f32[136,128]{1,0:T(8,128)S(1)}, u32[]{:S(2)}, u32[]{:S(2)}) collective-permute-start(f32[136,128]{1,0:T(8,128)S(1)} %get-tuple-element.114.refs_3_), channel_id=1, source_target_pairs={{0,4},{4,8},{8,12},{12,0},{1,5},{5,9},{9,13},{13,1},{2,6},{6,10},{... | collective-permute-start | bytes 208904 | tf_op jit(solution)/shard_map/ppermute | solution.py:311
  38.3 6.5 %collective-permute-start.17 = (f32[48,128]{1,0:T(8,128)S(1)}, f32[48,128]{1,0:T(8,128)S(1)}, u32[]{:S(2)}, u32[]{:S(2)}) collective-permute-start(f32[48,128]{1,0:T(8,128)S(1)} %get-tuple-element.119), channel_id=1, source_target_pairs={{0,1},{1,2},{2,3},{3,7},{7,6},{6,5},{5,4},{4,0},{8,9},{9,10},{10,1... | collective-permute-start | bytes 73736 | tf_op jit(solution)/shard_map/ppermute | solution.py:297
  40.1 4.7 %collective-permute-start.18 = (f32[48,128]{1,0:T(8,128)S(1)}, f32[48,128]{1,0:T(8,128)S(1)}, u32[]{:S(2)}, u32[]{:S(2)}) collective-permute-start(f32[48,128]{1,0:T(8,128)S(1)} %get-tuple-element.120), channel_id=1, source_target_pairs={{1,0},{2,1},{3,2},{7,3},{6,7},{5,6},{4,5},{0,4},{9,8},{10,9},{11,1... | collective-permute-start | bytes 73736 | tf_op jit(solution)/shard_map/ppermute | solution.py:297
  45.0 5.7 %collective-permute-start.24 = (f32[5,32,128]{2,1,0:T(8,128)S(1)}, f32[5,32,128]{2,1,0:T(8,128)S(1)}, u32[]{:S(2)}, u32[]{:S(2)}) collective-permute-start(f32[5,32,128]{2,1,0:T(8,128)S(1)} %shard_map.63), channel_id=1, source_target_pairs={{0,16},{16,0},{1,17},{17,1},{2,18},{18,2},{3,19},{19,3},{4,20},{20... | collective-permute-start | bytes 245768 | tf_op jit(solution)/shard_map/ppermute | solution.py:301
  50.9 6.0 %collective-permute-start.31 = (f32[136,128]{1,0:T(8,128)S(1)}, f32[136,128]{1,0:T(8,128)S(1)}, u32[]{:S(2)}, u32[]{:S(2)}) collective-permute-start(f32[136,128]{1,0:T(8,128)S(1)} %get-tuple-element.123), channel_id=1, source_target_pairs={{4,0},{8,4},{12,8},{0,12},{5,1},{9,5},{13,9},{1,13},{6,2},{10,6},{... | collective-permute-start | bytes 208904 | tf_op jit(solution)/shard_map/ppermute | solution.py:311
  52.7 4.5 %collective-permute-start.30 = (f32[136,128]{1,0:T(8,128)S(1)}, f32[136,128]{1,0:T(8,128)S(1)}, u32[]{:S(2)}, u32[]{:S(2)}) collective-permute-start(f32[136,128]{1,0:T(8,128)S(1)} %get-tuple-element.122.refs_3_), channel_id=1, source_target_pairs={{0,4},{4,8},{8,12},{12,0},{1,5},{5,9},{9,13},{13,1},{2,6},{6,10},{... | collective-permute-start | bytes 208904 | tf_op jit(solution)/shard_map/ppermute | solution.py:311
  57.6 6.3 %collective-permute-start.32 = (f32[48,128]{1,0:T(8,128)S(1)}, f32[48,128]{1,0:T(8,128)S(1)}, u32[]{:S(2)}, u32[]{:S(2)}) collective-permute-start(f32[48,128]{1,0:T(8,128)S(1)} %get-tuple-element.127), channel_id=1, source_target_pairs={{0,1},{1,2},{2,3},{3,7},{7,6},{6,5},{5,4},{4,0},{8,9},{9,10},{10,1... | collective-permute-start | bytes 73736 | tf_op jit(solution)/shard_map/ppermute | solution.py:297
  59.3 4.6 %collective-permute-start.33 = (f32[48,128]{1,0:T(8,128)S(1)}, f32[48,128]{1,0:T(8,128)S(1)}, u32[]{:S(2)}, u32[]{:S(2)}) collective-permute-start(f32[48,128]{1,0:T(8,128)S(1)} %get-tuple-element.128), channel_id=1, source_target_pairs={{1,0},{2,1},{3,2},{7,3},{6,7},{5,6},{4,5},{0,4},{9,8},{10,9},{11,1... | collective-permute-start | bytes 73736 | tf_op jit(solution)/shard_map/ppermute | solution.py:297
  64.1 4.4 %collective-permute-start.41 = (f32[8,128]{1,0:T(8,128)S(1)}, f32[8,128]{1,0:T(8,128)S(1)}, u32[]{:S(2)}, u32[]{:S(2)}) collective-permute-start(f32[8,128]{1,0:T(8,128)S(1)} %shard_map.69.refs_3_), channel_id=1, source_target_pairs={{4,0},{8,4},{12,8},{0,12},{5,1},{9,5},{13,9},{1,13},{6,2},{10,6},{... | collective-permute-start | bytes 12296 | tf_op jit(solution)/shard_map/ppermute | solution.py:311
  65.0 3.6 %collective-permute-start.39 = (f32[8,128]{1,0:T(8,128)S(1)}, f32[8,128]{1,0:T(8,128)S(1)}, u32[]{:S(2)}, u32[]{:S(2)}) collective-permute-start(f32[8,128]{1,0:T(8,128)S(1)} %shard_map.69.refs_3_), channel_id=1, source_target_pairs={{0,16},{16,0},{1,17},{17,1},{2,18},{18,2},{3,19},{19,3},{4,20},{20... | collective-permute-start | bytes 12296 | tf_op jit(solution)/shard_map/ppermute | solution.py:301
  70.3 3.7 %collective-permute-start.42 = (f32[8,128]{1,0:T(8,128)S(1)}, f32[8,128]{1,0:T(8,128)S(1)}, u32[]{:S(2)}, u32[]{:S(2)}) collective-permute-start(f32[8,128]{1,0:T(8,128)S(1)} %shard_map.70.refs_1_), channel_id=1, source_target_pairs={{0,16},{16,0},{1,17},{17,1},{2,18},{18,2},{3,19},{19,3},{4,20},{20... | collective-permute-start | bytes 12296 | tf_op jit(solution)/shard_map/ppermute | solution.py:301
  77.0 3.7 %collective-permute-start.46 = (f32[16,128]{1,0:T(8,128)S(1)}, f32[16,128]{1,0:T(8,128)S(1)}, u32[]{:S(2)}, u32[]{:S(2)}) collective-permute-start(f32[16,128]{1,0:T(8,128)S(1)} %shard_map.72.refs_0_), channel_id=1, source_target_pairs={{1,0},{2,1},{3,2},{7,3},{6,7},{5,6},{4,5},{0,4},{9,8},{10,9},{11,1... | collective-permute-start | bytes 24584 | tf_op jit(solution)/shard_map/ppermute | solution.py:297
  77.0 3.7 %collective-permute-start.45 = (f32[16,128]{1,0:T(8,128)S(1)}, f32[16,128]{1,0:T(8,128)S(1)}, u32[]{:S(2)}, u32[]{:S(2)}) collective-permute-start(f32[16,128]{1,0:T(8,128)S(1)} %shard_map.72.refs_0_), channel_id=1, source_target_pairs={{0,1},{1,2},{2,3},{3,7},{7,6},{6,5},{5,4},{4,0},{8,9},{9,10},{10,1... | collective-permute-start | bytes 24584 | tf_op jit(solution)/shard_map/ppermute | solution.py:297
  (23 other events, 68.5 us)

commit v13 on v10

--- a/solution.py
+++ b/solution.py
@@ -635,7 +635,7 @@
     out[rows, AGG:] = (tile - high.astype(F32)).astype(BF16)
 
 
-def blocks_kernel(flags, cond, absorb, block_agg, block_label, near, weights, inner, face_label, fine_label,
+def blocks_kernel(flags, cond, absorb, block_agg, _, block_label, near, weights, inner, face_label, fine_label,
                   part, line):
     nx, ny = cond.shape[0], cond.shape[1]
     nb, half, width = nx // 2, ny // 2, LANES // 2
@@ -672,14 +672,14 @@
             near_y, past_y = turned(own, -1, 0), turned(own, 1, 0)
             near_z, past_z = turned(own, -1, 1), turned(own, 1, 1)
             total = paired(sum(halves(absorb[x] + absorb[x + 1], slot + 3)))
-            for beside, values in (
+            for d, (beside, values) in enumerate((
                 (near_x, high_x), (past_x, low_x), (near_y, high_y), (past_y, low_y), (near_z, high_z), (past_z, low_z)
-            ):
-                total = total + jnp.where(beside != own, values, 0.0)
+            )):
+                leaving = jnp.where(beside != own, values, 0.0)
+                total = total + leaving
+                near[d, b], weights[d, b] = pack_rows(beside).astype(jnp.int32), pack_rows(leaving)
             block_label[b] = pack_rows(own)
             inner[b] = pack_rows(total)
-            for d, (beside, values) in enumerate(((near_x, high_x), (near_y, high_y), (near_z, high_z))):
-                near[d, b], weights[d, b] = pack_rows(beside), pack_rows(values)
             spread = picked(own, lane // 2)
             for a in range(2):
                 for c in range(2):
@@ -701,28 +701,24 @@
         face_label[4 + s, :2] = pack_lanes((low, high)[s])
 
 
-def own_kernel(first, last, total, flags, block_label, near, weights, *refs):
-    so_far, refs = (refs[0], refs[1:]) if first else (None, refs)
-    refs = refs[1:]
-
-    def step(b, tile):
-        def pairs_at(r):
-            return [(near[d, b, pl.ds(r, 1)], weights[d, b, pl.ds(r, 1)]) for d in range(3)]
-
-        return tile_sum(tile, SUB, lambda r: block_label[b, pl.ds(r, 1)], pairs_at)
-
-    tile = so_far[...] if first else jnp.zeros((AGG, 2 * AGG), F32)
-    tile = lax.fori_loop(first, last, step, tile)
-    if last < total:
-        refs[0][...] = tile
-        return
-    tile = both_halves(tile)
-    keep_tile(refs[0], 0, jnp.where(row_no((AGG, AGG)) == lane_no((AGG, AGG)), 0.0, tile + tile.T))
-
-
-def faces_kernel(count, nb, flags, own, face_label, weight_xy, weight_z, x_low, x_high, y_low, y_high, forth, back, out,
+def own_turn_kernel(flags, block_label, near, weights, coarse, out, values):
+    table = jnp.broadcast_to(coarse[:1], (SUB, LANES))
+    nb = block_label.shape[0]
+
+    def sums(bs, carry):
+        news = [sum(weights[d, b] * picked(table, near[d, b]) for d in range(6)) for b in bs]
+        for b, new in zip(bs, news):
+            values[b] = new
+        return carry
+
+    batched(0, nb, sums, 0)
+    total = jnp.zeros((AGG, LANES), F32)
+    total = lax.fori_loop(0, nb, lambda b, total: add_rows(total, block_label, b, values, b), total)
+    out[...] = lane_total(total)
+
+
+def faces_kernel(count, nb, flags, face_label, weight_xy, weight_z, x_low, x_high, y_low, y_high, forth, back, out,
                  near, weights):
-    out[:AGG] = own[...]
     at, half = x_low.shape[0] - 1, x_low.shape[1] // 2
     near[0], near[1] = pack_rows(x_low[at, :half]), pack_rows(x_high[at, :half])
     at = sum(WIDTHS) * 2 * nb
@@ -739,13 +735,13 @@
             lambda r, s=s: near[s, pl.ds(r, 1)],
             lambda r, s=s: [(face_label[s, pl.ds(r, 1)], weights[s, pl.ds(r, 1)])],
         )
-        keep_tile(out, t + 1, both_halves(tile))
-
-
-def turn_kernel(flags, tiles, scaled_rhs, scale, own, *refs):
+        keep_tile(out, t, both_halves(tile))
+
+
+def turn_kernel(flags, tiles, scaled_rhs, scale, own, inside, *refs):
     forth, back, *others, out = refs
     got = [ref[ref.shape[0] - 1, :SUB] if len(ref.shape) == 3 else ref[ref.shape[0] - SUB :] for ref in (*others, forth, back)]
-    vectors = [own[...], *got[:-2], *sides(flags, *got[-2:])]
+    vectors = [*got[:-2], *sides(flags, *got[-2:])]
     row = row_no((SUB, AGG))
     parts = []
     for v in vectors:
@@ -753,7 +749,7 @@
         parts.append(jnp.where(row == 0, high, jnp.where(row == 1, v - high, 0.0)).astype(BF16))
     got = jnp.dot(jnp.concatenate(parts, axis=1), tiles[...], preferred_element_type=F32)
     applied = jnp.sum(got[:, :AGG] + got[:, AGG:], axis=0, keepdims=True)
-    out[...] = (1.0 - OMEGA_COARSE) * own[...] + scaled_rhs[...] + scale[...] * applied
+    out[...] = (1.0 - OMEGA_COARSE) * own[...] + scaled_rhs[...] + scale[...] * (inside[...] + applied)
 
 
 def ride_kernel(count, flags, pre, fine_label, coarse, *outs):
@@ -883,34 +879,25 @@
     from_x = links.x(sends[:n_send])
     from_y = links.ring_y(*sends[n_send : n_send + 2])
     from_corners = links.corners(sends[n_send + 2 :])
-    blocks = (nb, SUB, LANES)
-    outs = [shaped(*blocks), shaped(3, *blocks), shaped(3, *blocks), shaped(*blocks), shaped(6, SUB, LANES)]
-    outs += [shaped(nx, ny, nz)]
-    scratch = [pltpu.VMEM((17, ny, LANES), F32), pltpu.VMEM((2, ny // 2, LANES), F32)]
-    *rows, inner, face_label, fine_label = call(blocks_kernel, outs, scratch)(arrays[0], arrays[2], arrays[3])
-    block_label = rows[0]
-    bounds = (0, nb * 5 // 12, nb * 10 // 12, nb)
-
-    def own_part(p, *more):
-        out = jax.ShapeDtypeStruct((AGG, 2 * AGG), BF16) if p == 2 else shaped(AGG, 2 * AGG)
-        return call(functools.partial(own_kernel, bounds[p], bounds[p + 1], nb), [out])(*rows, *more)[0]
-
-    own_tile = own_part(0, sends[0])
-    got = lax.optimization_barrier((*from_x, *from_y, *from_corners, own_tile))
-    from_x, from_y, from_corners = got[:n_send], got[n_send : n_send + 2], got[n_send + 2 : -1]
     size = len(WIDTHS) * frame.tall
     wide, *sends = call(
         functools.partial(first_frame_kernel, n_x, WIDTHS),
         [shaped(len(WIDTHS), *frame.main)] + [shaped(size + ny // 2, nz)] * 2,
         [pltpu.VMEM((size, nz), F32)] * 2,
     )(*arrays, from_x[0], from_x[-1], *from_y, *from_corners)
+    blocks = (nb, SUB, LANES)
+    outs = [shaped(*blocks), jax.ShapeDtypeStruct((6, *blocks), jnp.int32), shaped(6, *blocks), shaped(*blocks)]
+    outs += [shaped(6, SUB, LANES), shaped(nx, ny, nz)]
+    scratch = [pltpu.VMEM((17, ny, LANES), F32), pltpu.VMEM((2, ny // 2, LANES), F32)]
+    *rows, inner, face_label, fine_label = call(blocks_kernel, outs, scratch)(
+        arrays[0], arrays[2], arrays[3], sends[0]
+    )
+    block_label = rows[0]
     outs = [shaped(*frame.main)] * 4 + [shaped(frame.tall, nz), shaped(4, SUB, LANES), shaped(SUB, AGG)]
     *fields, weight_xy, some_diag = call(functools.partial(fields_kernel, n_x), outs, limit=24)(
         wide, block_label, inner, face_label
     )
-    own_tile = own_part(1, own_tile, sends[0])
     halo = (wide, *links.z(*sends))
-    *halo, own_tile = lax.optimization_barrier((*halo, own_tile))
     outs = [shaped(*frame.main)] * 2 + [shaped(*frame.ends)] * 6 + [shaped(nx, ny, nz)]
     outs += [shaped(2, SUB, LANES)] + [shaped(SUB, AGG)] * 2
     scratch = [pltpu.VMEM(frame.main, F32), pltpu.VMEM(frame.ends, F32), pltpu.VMEM((nx, frame.rows, LANES), F32)]
@@ -920,17 +907,17 @@
     )
     fields, pre = (*fields[:3], *got[:8]), got[8]
     weight_z, scaled_rhs, scale = got[9:]
-    own_tile = own_part(2, own_tile, scaled_rhs)
     tiles = call(
         functools.partial(faces_kernel, n_x, nb),
-        jax.ShapeDtypeStruct(((n_send + 5) * AGG, 2 * AGG), BF16),
+        jax.ShapeDtypeStruct(((n_send + 4) * AGG, 2 * AGG), BF16),
         [pltpu.VMEM((6, SUB, LANES), F32)] * 2,
-    )(own_tile, face_label, weight_xy, weight_z, from_x[0], from_x[-1], *from_y, *halo[1:])
+    )(face_label, weight_xy, weight_z, from_x[0], from_x[-1], *from_y, *halo[1:])
     coarse = scaled_rhs
 
     def turn(**more):
         near = links.near(coarse, **more)
-        return call(turn_kernel, shaped(SUB, AGG))(tiles, scaled_rhs, scale, coarse, *near), near
+        inside = call(own_turn_kernel, shaped(SUB, AGG), [pltpu.VMEM(blocks, F32)])(*rows, coarse)
+        return call(turn_kernel, shaped(SUB, AGG))(tiles, scaled_rhs, scale, coarse, inside, *near), near
 
     both = (pre, fine_label)
     rides = call(functools.partial(ride_kernel, n_x), [shaped(2 * HALO + 1, ny, nz)] * n_send)(*both, coarse)

time: 83.3 us -> 83.1 us (level)
  waiting for transfers between devices: 18.2 us -> 14.7 us
  Pallas kernels: 23.6 us -> 27 us
    pallas_call x24 -> x28, Pallas kernels: 23.6 us -> 27 us  [run(): pl.pallas_call(placed, out_shape=outs, in_specs=in_specs or [VMEM] * len(...]
    ppermute x9, waiting for transfers between devices: 5.77 us -> 4.45 us  [x(): return (lax.ppermute(sends[0], 'gx', self.ring_x),)]
    ppermute x9, waiting for transfers between devices: 5.19 us -> 4.23 us  [ring_y(): lax.ppermute(to_high, 'gy', ring)]
  transfers between devices with their start and end apart: 47 -> 47, of which waited for: 21 -> 14; matrix products, arithmetic and copies ran while one was open for 0% -> 0% of each run, Pallas kernels for 12% -> 16%
where the time goes in v13:
time: 83.1 us; the launch traced here: 82.9 us
  starting transfers between devices  40.9 us (49%)
  Pallas kernels  27 us (32%)
  waiting for transfers between devices  14.7 us (18%)
    pallas_call x28, Pallas kernels, run(): pl.pallas_call(placed, out_shape=outs, in_specs=in_specs or [VMEM] * len(...  27 us
    ppermute x20, starting transfers between devices, send(): return lax.ppermute(values, ('gx', 'gy', 'gz'), pairs)  20.5 us
    ppermute x9, starting transfers between devices, x(): return (lax.ppermute(sends[0], 'gx', self.ring_x),)  10.2 us
    ppermute x9, starting transfers between devices, ring_y(): lax.ppermute(to_low, 'gy', self.back(ring))  9.25 us
    ppermute x20, waiting for transfers between devices, send(): return lax.ppermute(values, ('gx', 'gy', 'gz'), pairs)  5.14 us
    ppermute x9, waiting for transfers between devices, x(): return (lax.ppermute(sends[0], 'gx', self.ring_x),)  4.45 us
    ppermute x9, waiting for transfers between devices, ring_y(): lax.ppermute(to_high, 'gy', ring)  4.23 us
  transfers between devices with their start and end apart: 47, of which 14 were waited for; matrix products, arithmetic and copies ran while one was open for 0% of the time, Pallas kernels for 16%

profile of v13, /device:TPU:0, one launch (start us, length us, event | category | flops | bytes accessed | tf_op | source)
XLA Modules:
  0.0 82.9 jit_solution(8860410569195486951)
XLA Ops:
  0.0 1.5 %shard_map.46 = (f32[24,32,128]{2,1,0:T(8,128)S(1)}, f32[24,32,128]{2,1,0:T(8,128)S(1)}, f32[24,32,128]{2,1,0:T(8,128)S(1)}, s32[12,16,64]{2,1,0:T(8,128)S(1)}, ...) custom-call(f32[24,32,128]{2,1,0:T(8,128)} %refs_0_.1, ...), custom_call_target="tpu_custom_call" | custom-call | flops 1000000 | bytes 100000 | tf_op jit(solution)/shard_map/pallas_call | solution.py:36
  1.5 3.0 %collective-permute-start = (f32[11,32,128]{2,1,0:T(8,128)S(1)}, f32[11,32,128]{2,1,0:T(8,128)S(1)}, u32[]{:S(2)}, u32[]{:S(2)}) collective-permute-start(f32[11,32,128]{2,1,0:T(8,128)S(1)} %get-tuple-element.56), channel_id=1, source_target_pairs={{0,16},{16,0},{1,17},{17,1},{2,18},{18,2},{3,19},{19,3},{4,20},{20... | collective-permute-start | bytes 540680 | tf_op jit(solution)/shard_map/ppermute | solution.py:301
  4.5 1.7 %collective-permute-start.2 = (f32[256,128]{1,0:T(8,128)S(1)}, f32[256,128]{1,0:T(8,128)S(1)}, u32[]{:S(2)}, u32[]{:S(2)}) collective-permute-start(f32[256,128]{1,0:T(8,128)S(1)} %get-tuple-element.58), channel_id=1, source_target_pairs={{4,0},{8,4},{12,8},{0,12},{5,1},{9,5},{13,9},{1,13},{6,2},{10,6},{... | collective-permute-start | bytes 393224 | tf_op jit(solution)/shard_map/ppermute | solution.py:311
  6.3 2.6 %collective-permute-start.4 = (f32[40,128]{1,0:T(8,128)S(1)}, f32[40,128]{1,0:T(8,128)S(1)}, u32[]{:S(2)}, u32[]{:S(2)}) collective-permute-start(f32[40,128]{1,0:T(8,128)S(1)} %get-tuple-element.60), channel_id=1, source_target_pairs={{20,0},{21,1},{22,2},{23,3},{24,4},{25,5},{26,6},{27,7},{28,8},{29... | collective-permute-start | bytes 61448 | tf_op jit(solution)/shard_map/ppermute | solution.py:297
  8.9 1.7 %collective-permute-done.3.refs_8_ = f32[40,128]{1,0:T(8,128)S(1)} collective-permute-done((f32[40,128]{1,0:T(8,128)S(1)}, f32[40,128]{1,0:T(8,128)S(1)}, u32[]{:S(2)}, u32[]{:S(2)}) %collective-permute-start.3) | collective-permute-done | bytes 20512 | tf_op jit(solution)/shard_map/ppermute | solution.py:297
  13.9 1.9 %shard_map.48 = (f32[12,8,128]{2,1,0:T(8,128)S(1)}, s32[6,12,8,128]{3,2,1,0:T(8,128)S(1)}, f32[6,12,8,128]{3,2,1,0:T(8,128)S(1)}, f32[12,8,128]{2,1,0:T(8,128)S(...) custom-call(f32[24,32,128]{2,1,0:T(8,128)S(1)} %get-tuple-element.52.refs_0_, ...), custom_call_target="tpu_custom_call" | custom-call | flops 1000000 | bytes 100000 | tf_op jit(solution)/shard_map/pallas_call | solution.py:36
  15.8 2.5 %shard_map.49 = (f32[32,56,128]{2,1,0:T(8,128)S(1)}, f32[32,56,128]{2,1,0:T(8,128)S(1)}, f32[32,56,128]{2,1,0:T(8,128)S(1)}, f32[32,56,128]{2,1,0:T(8,128)S(1)},...) custom-call(f32[3,32,56,128]{3,2,1,0:T(8,128)S(1)} %get-tuple-element.63.refs_0_, ...), custom_call_target="tpu_custom_call" | custom-call | flops 1000000 | bytes 100000 | tf_op jit(solution)/shard_map/pallas_call | solution.py:36
  18.4 4.5 %shard_map.50 = (f32[32,56,128]{2,1,0:T(8,128)S(1)}, f32[32,56,128]{2,1,0:T(8,128)S(1)}, f32[2,56,128]{2,1,0:T(8,128)S(1)}, f32[2,56,128]{2,1,0:T(8,128)S(1)}, f...) custom-call(f32[3,32,56,128]{3,2,1,0:T(8,128)S(1)} %get-tuple-elemen, ...), custom_call_target="tpu_custom_call" | custom-call | flops 1000000 | bytes 100000 | tf_op jit(solution)/shard_map/pallas_call | solution.py:36
  24.8 1.6 %collective-permute-start.8 = (f32[8,128]{1,0:T(8,128)S(1)}, f32[8,128]{1,0:T(8,128)S(1)}, u32[]{:S(2)}, u32[]{:S(2)}) collective-permute-start(f32[8,128]{1,0:T(8,128)S(1)} %get-tuple-element.75.refs_3_.refs_2_.refs_1_), channel_id=1, source_target_pairs={{1,0},{2,1},{3,2},{7,3},{6,7},{5,6},{4,5},{0,4},{9,8},{10,9},{11,1... | collective-permute-start | bytes 12296 | tf_op jit(solution)/shard_map/ppermute | solution.py:297
  29.4 1.3 %collective-permute-start.16 = (f32[264,128]{1,0:T(8,128)S(1)}, f32[264,128]{1,0:T(8,128)S(1)}, u32[]{:S(2)}, u32[]{:S(2)}) collective-permute-start(f32[264,128]{1,0:T(8,128)S(1)} %get-tuple-element.82), channel_id=1, source_target_pairs={{4,0},{8,4},{12,8},{0,12},{5,1},{9,5},{13,9},{1,13},{6,2},{10,6},{... | collective-permute-start | bytes 405512 | tf_op jit(solution)/shard_map/ppermute | solution.py:311
  31.2 1.4 %collective-permute-start.13 = (f32[8,128]{1,0:T(8,128)S(1)}, f32[8,128]{1,0:T(8,128)S(1)}, u32[]{:S(2)}, u32[]{:S(2)}) collective-permute-start(f32[8,128]{1,0:T(8,128)S(1)} %shard_map.54.refs_3_.refs_2_), channel_id=1, source_target_pairs={{1,0},{2,1},{3,2},{7,3},{6,7},{5,6},{4,5},{0,4},{9,8},{10,9},{11,1... | collective-permute-start | bytes 12296 | tf_op jit(solution)/shard_map/ppermute | solution.py:297
  34.9 1.7 %collective-permute-done.15.refs_8_.refs_3_ = f32[264,128]{1,0:T(8,128)S(1)} collective-permute-done((f32[264,128]{1,0:T(8,128)S(1)}, f32[264,128]{1,0:T(8,128)S(1)}, u32[]{:S(2)}, u32[]{:S(2)}) %collective-permute-start.15) | collective-permute-done | bytes 135200 | tf_op jit(solution)/shard_map/ppermute | solution.py:311
  37.0 1.6 %collective-permute-start.17 = (f32[88,128]{1,0:T(8,128)S(1)}, f32[88,128]{1,0:T(8,128)S(1)}, u32[]{:S(2)}, u32[]{:S(2)}) collective-permute-start(f32[88,128]{1,0:T(8,128)S(1)} %get-tuple-element.86), channel_id=1, source_target_pairs={{0,1},{1,2},{2,3},{3,7},{7,6},{6,5},{5,4},{4,0},{8,9},{9,10},{10,1... | collective-permute-start | bytes 135176 | tf_op jit(solution)/shard_map/ppermute | solution.py:297
  48.2 1.7 %collective-permute-start.31 = (f32[8,128]{1,0:T(8,128)S(1)}, f32[8,128]{1,0:T(8,128)S(1)}, u32[]{:S(2)}, u32[]{:S(2)}) collective-permute-start(f32[8,128]{1,0:T(8,128)S(1)} %shard_map.63.refs_3_), channel_id=1, source_target_pairs={{4,0},{8,4},{12,8},{0,12},{5,1},{9,5},{13,9},{1,13},{6,2},{10,6},{... | collective-permute-start | bytes 12296 | tf_op jit(solution)/shard_map/ppermute | solution.py:311
  49.8 1.4 %collective-permute-start.29 = (f32[8,128]{1,0:T(8,128)S(1)}, f32[8,128]{1,0:T(8,128)S(1)}, u32[]{:S(2)}, u32[]{:S(2)}) collective-permute-start(f32[8,128]{1,0:T(8,128)S(1)} %shard_map.63.refs_3_), channel_id=1, source_target_pairs={{0,16},{16,0},{1,17},{17,1},{2,18},{18,2},{3,19},{19,3},{4,20},{20... | collective-permute-start | bytes 12296 | tf_op jit(solution)/shard_map/ppermute | solution.py:301
  51.9 1.3 %collective-permute-start.27 = (f32[8,128]{1,0:T(8,128)S(1)}, f32[8,128]{1,0:T(8,128)S(1)}, u32[]{:S(2)}, u32[]{:S(2)}) collective-permute-start(f32[8,128]{1,0:T(8,128)S(1)} %shard_map.63.refs_3_), channel_id=1, source_target_pairs={{0,1},{1,2},{2,3},{3,7},{7,6},{6,5},{5,4},{4,0},{8,9},{9,10},{10,1... | collective-permute-start | bytes 12296 | tf_op jit(solution)/shard_map/ppermute | solution.py:297
  55.0 1.7 %collective-permute-start.36 = (f32[8,128]{1,0:T(8,128)S(1)}, f32[8,128]{1,0:T(8,128)S(1)}, u32[]{:S(2)}, u32[]{:S(2)}) collective-permute-start(f32[8,128]{1,0:T(8,128)S(1)} %shard_map.65.refs_3_), channel_id=1, source_target_pairs={{4,0},{8,4},{12,8},{0,12},{5,1},{9,5},{13,9},{1,13},{6,2},{10,6},{... | collective-permute-start | bytes 12296 | tf_op jit(solution)/shard_map/ppermute | solution.py:311
  62.2 1.5 %collective-permute-start.39 = (f32[8,128]{1,0:T(8,128)S(1)}, f32[8,128]{1,0:T(8,128)S(1)}, u32[]{:S(2)}, u32[]{:S(2)}) collective-permute-start(f32[8,128]{1,0:T(8,128)S(1)} %shard_map.67.refs_3_), channel_id=1, source_target_pairs={{0,16},{16,0},{1,17},{17,1},{2,18},{18,2},{3,19},{19,3},{4,20},{20... | collective-permute-start | bytes 12296 | tf_op jit(solution)/shard_map/ppermute | solution.py:301
  64.2 1.5 %collective-permute-start.37 = (f32[8,128]{1,0:T(8,128)S(1)}, f32[8,128]{1,0:T(8,128)S(1)}, u32[]{:S(2)}, u32[]{:S(2)}) collective-permute-start(f32[8,128]{1,0:T(8,128)S(1)} %shard_map.67.refs_3_), channel_id=1, source_target_pairs={{0,1},{1,2},{2,3},{3,7},{7,6},{6,5},{5,4},{4,0},{8,9},{9,10},{10,1... | collective-permute-start | bytes 12296 | tf_op jit(solution)/shard_map/ppermute | solution.py:297
  68.1 3.1 %collective-permute-done.42.refs_0_.refs_2_ = f32[8,128]{1,0:T(8,128)S(1)} collective-permute-done((f32[8,128]{1,0:T(8,128)S(1)}, f32[8,128]{1,0:T(8,128)S(1)}, u32[]{:S(2)}, u32[]{:S(2)}) %collective-permute-start.42) | collective-permute-done | bytes 4128 | tf_op jit(solution)/shard_map/ppermute | solution.py:301
  72.5 1.8 %collective-permute-done.43.refs_0_ = f32[8,128]{1,0:T(8,128)S(1)} collective-permute-done((f32[8,128]{1,0:T(8,128)S(1)}, f32[8,128]{1,0:T(8,128)S(1)}, u32[]{:S(2)}, u32[]{:S(2)}) %collective-permute-start.43) | collective-permute-done | bytes 4128 | tf_op jit(solution)/shard_map/ppermute | solution.py:311
  74.3 2.0 %collective-permute-start.45 = (f32[16,128]{1,0:T(8,128)S(1)}, f32[16,128]{1,0:T(8,128)S(1)}, u32[]{:S(2)}, u32[]{:S(2)}) collective-permute-start(f32[16,128]{1,0:T(8,128)S(1)} %shard_map.71.refs_0_), channel_id=1, source_target_pairs={{0,1},{1,2},{2,3},{3,7},{7,6},{6,5},{5,4},{4,0},{8,9},{9,10},{10,1... | collective-permute-start | bytes 24584 | tf_op jit(solution)/shard_map/ppermute | solution.py:297
  76.3 1.6 %collective-permute-done.46.refs_2_ = f32[16,128]{1,0:T(8,128)S(1)} collective-permute-done((f32[16,128]{1,0:T(8,128)S(1)}, f32[16,128]{1,0:T(8,128)S(1)}, u32[]{:S(2)}, u32[]{:S(2)}) %collective-permute-start.46) | collective-permute-done | bytes 8224 | tf_op jit(solution)/shard_map/ppermute | solution.py:297
  77.9 5.0 %shard_map.73 = f32[24,32,128]{2,1,0:T(8,128)} custom-call(f32[16,128]{1,0:T(8,128)S(1)} %shard_map.71.refs_0_, f32[16,128]{1,0:T(8,128)S(1)} %collective-permute-done.45.refs_1_, f32[16,128]{1,0:T(8,128)S(1)} %collective-permute-done.46.refs_2_, s32[16,40,128]{2,1,0:T(8,128)S(1)} %get-tuple-element.89.refs_3_, s32[2,40,128]{2,1,0:T(8,128)S(1)} %get-tuple-element.90.refs_4_, ...), custom_call_target="tpu_custom_call" | custom-call | flops 1000000 | bytes 100000 | tf_op jit(solution)/shard_map/pallas_call | solution.py:36
  (98 shorter events, 33.0 us)
Async XLA Ops:
  1.5 9.3 %collective-permute-start = (f32[11,32,128]{2,1,0:T(8,128)S(1)}, f32[11,32,128]{2,1,0:T(8,128)S(1)}, u32[]{:S(2)}, u32[]{:S(2)}) collective-permute-start(f32[11,32,128]{2,1,0:T(8,128)S(1)} %get-tuple-element.56), channel_id=1, source_target_pairs={{0,16},{16,0},{1,17},{17,1},{2,18},{18,2},{3,19},{19,3},{4,20},{20... | collective-permute-start | bytes 540680 | tf_op jit(solution)/shard_map/ppermute | solution.py:301
  4.5 6.3 %collective-permute-start.1 = (f32[256,128]{1,0:T(8,128)S(1)}, f32[256,128]{1,0:T(8,128)S(1)}, u32[]{:S(2)}, u32[]{:S(2)}) collective-permute-start(f32[256,128]{1,0:T(8,128)S(1)} %get-tuple-element.57), channel_id=1, source_target_pairs={{0,4},{4,8},{8,12},{12,0},{1,5},{5,9},{9,13},{13,1},{2,6},{6,10},{... | collective-permute-start | bytes 393224 | tf_op jit(solution)/shard_map/ppermute | solution.py:311
  4.5 6.3 %collective-permute-start.2 = (f32[256,128]{1,0:T(8,128)S(1)}, f32[256,128]{1,0:T(8,128)S(1)}, u32[]{:S(2)}, u32[]{:S(2)}) collective-permute-start(f32[256,128]{1,0:T(8,128)S(1)} %get-tuple-element.58), channel_id=1, source_target_pairs={{4,0},{8,4},{12,8},{0,12},{5,1},{9,5},{13,9},{1,13},{6,2},{10,6},{... | collective-permute-start | bytes 393224 | tf_op jit(solution)/shard_map/ppermute | solution.py:311
  6.3 4.4 %collective-permute-start.3 = (f32[40,128]{1,0:T(8,128)S(1)}, f32[40,128]{1,0:T(8,128)S(1)}, u32[]{:S(2)}, u32[]{:S(2)}) collective-permute-start(f32[40,128]{1,0:T(8,128)S(1)} %get-tuple-element.59), channel_id=1, source_target_pairs={{0,20},{1,21},{2,22},{3,23},{4,24},{5,25},{6,26},{7,27},{8,28},{9,... | collective-permute-start | bytes 61448 | tf_op jit(solution)/shard_map/ppermute | solution.py:297
  6.3 4.5 %collective-permute-start.4 = (f32[40,128]{1,0:T(8,128)S(1)}, f32[40,128]{1,0:T(8,128)S(1)}, u32[]{:S(2)}, u32[]{:S(2)}) collective-permute-start(f32[40,128]{1,0:T(8,128)S(1)} %get-tuple-element.60), channel_id=1, source_target_pairs={{20,0},{21,1},{22,2},{23,3},{24,4},{25,5},{26,6},{27,7},{28,8},{29... | collective-permute-start | bytes 61448 | tf_op jit(solution)/shard_map/ppermute | solution.py:297
  11.9 6.5 %collective-permute-start.6 = (f32[136,128]{1,0:T(8,128)S(1)}, f32[136,128]{1,0:T(8,128)S(1)}, u32[]{:S(2)}, u32[]{:S(2)}) collective-permute-start(f32[136,128]{1,0:T(8,128)S(1)} %get-tuple-element.67), channel_id=1, source_target_pairs={{1,0},{2,1},{3,2},{7,3},{6,7},{5,6},{4,5},{0,4},{9,8},{10,9},{11,1... | collective-permute-start | bytes 208904 | tf_op jit(solution)/shard_map/ppermute | solution.py:297
  13.1 5.3 %collective-permute-start.5 = (f32[136,128]{1,0:T(8,128)S(1)}, f32[136,128]{1,0:T(8,128)S(1)}, u32[]{:S(2)}, u32[]{:S(2)}) collective-permute-start(f32[136,128]{1,0:T(8,128)S(1)} %get-tuple-element.61.refs_3_), channel_id=1, source_target_pairs={{0,1},{1,2},{2,3},{3,7},{7,6},{6,5},{5,4},{4,0},{8,9},{9,10},{10,1... | collective-permute-start | bytes 208904 | tf_op jit(solution)/shard_map/ppermute | solution.py:297
  22.9 6.3 %collective-permute-start.9 = (f32[9,32,128]{2,1,0:T(8,128)S(1)}, f32[9,32,128]{2,1,0:T(8,128)S(1)}, u32[]{:S(2)}, u32[]{:S(2)}) collective-permute-start(f32[9,32,128]{2,1,0:T(8,128)S(1)} %shard_map.53), channel_id=1, source_target_pairs={{0,16},{16,0},{1,17},{17,1},{2,18},{18,2},{3,19},{19,3},{4,20},{20... | collective-permute-start | bytes 442376 | tf_op jit(solution)/shard_map/ppermute | solution.py:301
  23.6 5.0 %collective-permute-start.11 = (f32[8,128]{1,0:T(8,128)S(1)}, f32[8,128]{1,0:T(8,128)S(1)}, u32[]{:S(2)}, u32[]{:S(2)}) collective-permute-start(f32[8,128]{1,0:T(8,128)S(1)} %get-tuple-element.75.refs_3_.refs_2_.refs_1_), channel_id=1, source_target_pairs={{4,0},{8,4},{12,8},{0,12},{5,1},{9,5},{13,9},{1,13},{6,2},{10,6},{... | collective-permute-start | bytes 12296 | tf_op jit(solution)/shard_map/ppermute | solution.py:311
  29.4 5.4 %collective-permute-start.16 = (f32[264,128]{1,0:T(8,128)S(1)}, f32[264,128]{1,0:T(8,128)S(1)}, u32[]{:S(2)}, u32[]{:S(2)}) collective-permute-start(f32[264,128]{1,0:T(8,128)S(1)} %get-tuple-element.82), channel_id=1, source_target_pairs={{4,0},{8,4},{12,8},{0,12},{5,1},{9,5},{13,9},{1,13},{6,2},{10,6},{... | collective-permute-start | bytes 405512 | tf_op jit(solution)/shard_map/ppermute | solution.py:311
  30.7 5.8 %collective-permute-start.15 = (f32[264,128]{1,0:T(8,128)S(1)}, f32[264,128]{1,0:T(8,128)S(1)}, u32[]{:S(2)}, u32[]{:S(2)}) collective-permute-start(f32[264,128]{1,0:T(8,128)S(1)} %get-tuple-element.81.refs_4_), channel_id=1, source_target_pairs={{0,4},{4,8},{8,12},{12,0},{1,5},{5,9},{9,13},{13,1},{2,6},{6,10},{... | collective-permute-start | bytes 405512 | tf_op jit(solution)/shard_map/ppermute | solution.py:311
  30.7 4.1 %collective-permute-start.14 = (f32[8,128]{1,0:T(8,128)S(1)}, f32[8,128]{1,0:T(8,128)S(1)}, u32[]{:S(2)}, u32[]{:S(2)}) collective-permute-start(f32[8,128]{1,0:T(8,128)S(1)} %shard_map.54.refs_3_.refs_2_), channel_id=1, source_target_pairs={{0,16},{16,0},{1,17},{17,1},{2,18},{18,2},{3,19},{19,3},{4,20},{20... | collective-permute-start | bytes 12296 | tf_op jit(solution)/shard_map/ppermute | solution.py:301
  37.0 5.7 %collective-permute-start.17 = (f32[88,128]{1,0:T(8,128)S(1)}, f32[88,128]{1,0:T(8,128)S(1)}, u32[]{:S(2)}, u32[]{:S(2)}) collective-permute-start(f32[88,128]{1,0:T(8,128)S(1)} %get-tuple-element.86), channel_id=1, source_target_pairs={{0,1},{1,2},{2,3},{3,7},{7,6},{6,5},{5,4},{4,0},{8,9},{9,10},{10,1... | collective-permute-start | bytes 135176 | tf_op jit(solution)/shard_map/ppermute | solution.py:297
  38.6 4.1 %collective-permute-start.18 = (f32[88,128]{1,0:T(8,128)S(1)}, f32[88,128]{1,0:T(8,128)S(1)}, u32[]{:S(2)}, u32[]{:S(2)}) collective-permute-start(f32[88,128]{1,0:T(8,128)S(1)} %get-tuple-element.87), channel_id=1, source_target_pairs={{1,0},{2,1},{3,2},{7,3},{6,7},{5,6},{4,5},{0,4},{9,8},{10,9},{11,1... | collective-permute-start | bytes 135176 | tf_op jit(solution)/shard_map/ppermute | solution.py:297
  42.9 4.7 %collective-permute-start.26 = (f32[8,128]{1,0:T(8,128)S(1)}, f32[8,128]{1,0:T(8,128)S(1)}, u32[]{:S(2)}, u32[]{:S(2)}) collective-permute-start(f32[8,128]{1,0:T(8,128)S(1)} %shard_map.61.refs_3_), channel_id=1, source_target_pairs={{4,0},{8,4},{12,8},{0,12},{5,1},{9,5},{13,9},{1,13},{6,2},{10,6},{... | collective-permute-start | bytes 12296 | tf_op jit(solution)/shard_map/ppermute | solution.py:311
  43.2 4.3 %collective-permute-start.25 = (f32[8,128]{1,0:T(8,128)S(1)}, f32[8,128]{1,0:T(8,128)S(1)}, u32[]{:S(2)}, u32[]{:S(2)}) collective-permute-start(f32[8,128]{1,0:T(8,128)S(1)} %shard_map.61.refs_3_), channel_id=1, source_target_pairs={{0,4},{4,8},{8,12},{12,0},{1,5},{5,9},{9,13},{13,1},{2,6},{6,10},{... | collective-permute-start | bytes 12296 | tf_op jit(solution)/shard_map/ppermute | solution.py:311
  43.4 4.2 %collective-permute-start.24 = (f32[8,128]{1,0:T(8,128)S(1)}, f32[8,128]{1,0:T(8,128)S(1)}, u32[]{:S(2)}, u32[]{:S(2)}) collective-permute-start(f32[8,128]{1,0:T(8,128)S(1)} %shard_map.61.refs_3_), channel_id=1, source_target_pairs={{0,16},{16,0},{1,17},{17,1},{2,18},{18,2},{3,19},{19,3},{4,20},{20... | collective-permute-start | bytes 12296 | tf_op jit(solution)/shard_map/ppermute | solution.py:301
  48.2 6.2 %collective-permute-start.31 = (f32[8,128]{1,0:T(8,128)S(1)}, f32[8,128]{1,0:T(8,128)S(1)}, u32[]{:S(2)}, u32[]{:S(2)}) collective-permute-start(f32[8,128]{1,0:T(8,128)S(1)} %shard_map.63.refs_3_), channel_id=1, source_target_pairs={{4,0},{8,4},{12,8},{0,12},{5,1},{9,5},{13,9},{1,13},{6,2},{10,6},{... | collective-permute-start | bytes 12296 | tf_op jit(solution)/shard_map/ppermute | solution.py:311
  49.8 4.6 %collective-permute-start.30 = (f32[8,128]{1,0:T(8,128)S(1)}, f32[8,128]{1,0:T(8,128)S(1)}, u32[]{:S(2)}, u32[]{:S(2)}) collective-permute-start(f32[8,128]{1,0:T(8,128)S(1)} %shard_map.63.refs_3_), channel_id=1, source_target_pairs={{0,4},{4,8},{8,12},{12,0},{1,5},{5,9},{9,13},{13,1},{2,6},{6,10},{... | collective-permute-start | bytes 12296 | tf_op jit(solution)/shard_map/ppermute | solution.py:311
  49.8 4.6 %collective-permute-start.29 = (f32[8,128]{1,0:T(8,128)S(1)}, f32[8,128]{1,0:T(8,128)S(1)}, u32[]{:S(2)}, u32[]{:S(2)}) collective-permute-start(f32[8,128]{1,0:T(8,128)S(1)} %shard_map.63.refs_3_), channel_id=1, source_target_pairs={{0,16},{16,0},{1,17},{17,1},{2,18},{18,2},{3,19},{19,3},{4,20},{20... | collective-permute-start | bytes 12296 | tf_op jit(solution)/shard_map/ppermute | solution.py:301
  55.0 5.5 %collective-permute-start.36 = (f32[8,128]{1,0:T(8,128)S(1)}, f32[8,128]{1,0:T(8,128)S(1)}, u32[]{:S(2)}, u32[]{:S(2)}) collective-permute-start(f32[8,128]{1,0:T(8,128)S(1)} %shard_map.65.refs_3_), channel_id=1, source_target_pairs={{4,0},{8,4},{12,8},{0,12},{5,1},{9,5},{13,9},{1,13},{6,2},{10,6},{... | collective-permute-start | bytes 12296 | tf_op jit(solution)/shard_map/ppermute | solution.py:311
  61.1 5.8 %collective-permute-start.41 = (f32[8,128]{1,0:T(8,128)S(1)}, f32[8,128]{1,0:T(8,128)S(1)}, u32[]{:S(2)}, u32[]{:S(2)}) collective-permute-start(f32[8,128]{1,0:T(8,128)S(1)} %shard_map.67.refs_3_), channel_id=1, source_target_pairs={{4,0},{8,4},{12,8},{0,12},{5,1},{9,5},{13,9},{1,13},{6,2},{10,6},{... | collective-permute-start | bytes 12296 | tf_op jit(solution)/shard_map/ppermute | solution.py:311
  62.2 4.7 %collective-permute-start.40 = (f32[8,128]{1,0:T(8,128)S(1)}, f32[8,128]{1,0:T(8,128)S(1)}, u32[]{:S(2)}, u32[]{:S(2)}) collective-permute-start(f32[8,128]{1,0:T(8,128)S(1)} %shard_map.67.refs_3_), channel_id=1, source_target_pairs={{0,4},{4,8},{8,12},{12,0},{1,5},{5,9},{9,13},{13,1},{2,6},{6,10},{... | collective-permute-start | bytes 12296 | tf_op jit(solution)/shard_map/ppermute | solution.py:311
  62.2 4.7 %collective-permute-start.39 = (f32[8,128]{1,0:T(8,128)S(1)}, f32[8,128]{1,0:T(8,128)S(1)}, u32[]{:S(2)}, u32[]{:S(2)}) collective-permute-start(f32[8,128]{1,0:T(8,128)S(1)} %shard_map.67.refs_3_), channel_id=1, source_target_pairs={{0,16},{16,0},{1,17},{17,1},{2,18},{18,2},{3,19},{19,3},{4,20},{20... | collective-permute-start | bytes 12296 | tf_op jit(solution)/shard_map/ppermute | solution.py:301
  (23 other events, 73.3 us)

commit v14 on v13

--- a/solution.py
+++ b/solution.py
@@ -784,9 +784,23 @@
         ends[s] = values.astype(jnp.int32)
 
 
-def post_kernel(flags, table, table_forth, table_back, labels, end_labels, wide_ref, forth, back, *refs):
+def own_lift_kernel(flags, wide_ref, labels, coarse, lifted):
+    frame = Frame(wide_ref.shape[1] - 2 * HALO, wide_ref.shape[2] - 2 * (SUB + HALO))
+    table = jnp.broadcast_to(coarse[:1], (frame.tall, LANES))
+
+    def lift(bs, carry):
+        news = [picked(table, labels[b]) for b in bs]
+        for b, new in zip(bs, news):
+            for a in range(2):
+                lifted[2 * b + a, frame.span] = wide_ref[0, 2 * b + a, frame.span] + new
+        return carry
+
+    batched(HALO // 2, (HALO + frame.nx) // 2, lift, 0, 4)
+
+
+def post_kernel(flags, own_lifted, table, table_forth, table_back, labels, end_labels, wide_ref, forth, back, *refs):
     (wx, wy, wz, inv_diag, start), ends = refs[:5], refs[5:11]
-    out, one, two, one_ends, two_ends, kept_out, sems = refs[11:]
+    out, lifted, one, two, one_ends, two_ends, kept_out, sems = refs[11:]
     nx, ny = out.shape[0], out.shape[1]
     frame = Frame(nx, ny)
     wide, tall, span = frame.wide, frame.tall, frame.span
@@ -801,29 +815,34 @@
         low, mid, high = (tables[dz][3 * n + dx + 1 : 3 * n + dx + 2] for n in range(3))
         return jnp.where(row < HALO, low, jnp.where(row < HALO + ny, mid, high))
 
-    for x_from, x_to, dx in ((0, HALO, -1), (HALO, HALO + nx, 0), (HALO + nx, wide, 1)):
-        values = table_at(dx, 0)
-
-        def lift(bs, carry, values=values):
-            news = [picked(values, labels[b]) for b in bs]
-            for b, new in zip(bs, news):
-                for a in range(2):
-                    two[2 * b + a, span] = wide_ref[0, 2 * b + a, span] + new
-            return carry
-
-        batched(x_from // 2, x_to // 2, lift, 0, 4)
+    def lift(x, values, at):
+        rows = pl.ds(SUB + at.start, at.size)
+        lifted[x, rows] = wide_ref[0, x, rows] + picked(values[at.start : at.start + at.size], labels[x // 2, at])
+
+    for x in range(wide):
+        if HALO <= x < HALO + nx:
+            continue
+        lift(x, table_at(-1 if x < HALO else 1, 0), pl.ds(0, tall))
+    mid = table_at(0, 0)
+
+    def ends_of_rows(xs, carry):
+        for x in xs:
+            for at in (pl.ds(0, SUB), pl.ds(tall - SUB, SUB)):
+                lift(x, mid, at)
+        return carry
+
+    batched(HALO, HALO + nx, ends_of_rows, 0, 6)
     for s, (dz, base) in enumerate(zip((-1, 1), sides(flags, forth[:tall], back[:tall]))):
         below, inside, above = (picked(table_at(dx, dz), end_labels[s]) for dx in (-1, 0, 1))
         spot = lane // HALO
-        lifted = jnp.where(spot < HALO, below, jnp.where(spot < HALO + nx, inside, above))
-        two_ends[s, span] = base + lifted
+        two_ends[s, span] = base + jnp.where(spot < HALO, below, jnp.where(spot < HALO + nx, inside, above))
     kept = 1.0 - OMEGA_FINE
 
     def result(at, count):
         rows = pl.ds(at, count)
         return pltpu.make_async_copy(kept_out.at[rows], out.at[rows], sems.at[at // count])
 
-    buffers = ((two, two_ends), (one, one_ends), (two, two_ends), (one, one_ends))
+    buffers = ((lifted, two_ends), (one, one_ends), (two, two_ends), (one, one_ends))
     for s in range(POST):
         src, src_ends = buffers[s]
         join = joined(ez_up[0, span] * src_ends[0, span], ez_low[1, span] * src_ends[1, span])
@@ -879,12 +898,6 @@
     from_x = links.x(sends[:n_send])
     from_y = links.ring_y(*sends[n_send : n_send + 2])
     from_corners = links.corners(sends[n_send + 2 :])
-    size = len(WIDTHS) * frame.tall
-    wide, *sends = call(
-        functools.partial(first_frame_kernel, n_x, WIDTHS),
-        [shaped(len(WIDTHS), *frame.main)] + [shaped(size + ny // 2, nz)] * 2,
-        [pltpu.VMEM((size, nz), F32)] * 2,
-    )(*arrays, from_x[0], from_x[-1], *from_y, *from_corners)
     blocks = (nb, SUB, LANES)
     outs = [shaped(*blocks), jax.ShapeDtypeStruct((6, *blocks), jnp.int32), shaped(6, *blocks), shaped(*blocks)]
     outs += [shaped(6, SUB, LANES), shaped(nx, ny, nz)]
@@ -892,7 +905,15 @@
     *rows, inner, face_label, fine_label = call(blocks_kernel, outs, scratch)(
         arrays[0], arrays[2], arrays[3], sends[0]
     )
+    got = lax.optimization_barrier((*from_x, *from_y, *from_corners, inner))
+    from_x, from_y, from_corners, inner = got[:n_send], got[n_send : n_send + 2], got[n_send + 2 : -1], got[-1]
     block_label = rows[0]
+    size = len(WIDTHS) * frame.tall
+    wide, *sends = call(
+        functools.partial(first_frame_kernel, n_x, WIDTHS),
+        [shaped(len(WIDTHS), *frame.main)] + [shaped(size + ny // 2, nz)] * 2,
+        [pltpu.VMEM((size, nz), F32)] * 2,
+    )(*arrays, from_x[0], from_x[-1], *from_y, *from_corners)
     outs = [shaped(*frame.main)] * 4 + [shaped(frame.tall, nz), shaped(4, SUB, LANES), shaped(SUB, AGG)]
     *fields, weight_xy, some_diag = call(functools.partial(fields_kernel, n_x), outs, limit=24)(
         wide, block_label, inner, face_label
@@ -935,15 +956,17 @@
     for _ in range(KC - 4):
         coarse, _ = turn()
     from_x = links.x([coarse] * n_send)
+    own_lifted = call(own_lift_kernel, shaped(*frame.main))(halo[0], lifts[0], coarse)
     three = call(three_kernel, shaped(SUB, AGG))(from_x[0], coarse, from_x[-1])
     low, high = links.ring_y(three, three)
     nine = call(nine_kernel, shaped(2 * SUB, AGG))(low, three, high)
     tables = (nine, *links.z(nine, nine))
     scratch = [pltpu.VMEM(frame.main, F32)] * 2 + [pltpu.VMEM(frame.ends, F32)] * 2
     scratch += [pltpu.VMEM((nx, ny, nz), F32), pltpu.SemaphoreType.DMA((nx // 8,))]
-    return call(post_kernel, shaped(nx, ny, nz), scratch, limit=24, out_specs=pl.BlockSpec(memory_space=pl.ANY))(
-        *tables, *lifts, *halo, *fields
-    )
+    outs, out_specs = [shaped(nx, ny, nz), shaped(*frame.main)], [pl.BlockSpec(memory_space=pl.ANY), VMEM]
+    return call(post_kernel, outs, scratch, limit=24, out_specs=out_specs, aliases={0: 1})(
+        own_lifted, *tables, *lifts, *halo, *fields
+    )[0]
 
 
 def solution(mesh):

time: 83.1 us -> 81.2 us (0.977)
  waiting for transfers between devices: 14.7 us -> 11.8 us
    ppermute x9, waiting for transfers between devices: 4.45 us -> 2.66 us  [x(): return (lax.ppermute(sends[0], 'gx', self.ring_x),)]
    ppermute x9, starting transfers between devices: 10.2 us -> 11.2 us  [x(): return (lax.ppermute(sends[0], 'gx', self.ring_x),)]
    pallas_call x28 -> x29, Pallas kernels: 27 us -> 27.5 us  [run(): pl.pallas_call(placed, out_shape=outs, in_specs=in_specs or [VMEM] * len(...]
  transfers between devices with their start and end apart: 47 -> 47, of which waited for: 14 -> 12; matrix products, arithmetic and copies ran while one was open for 0% -> 0% of each run, Pallas kernels for 16% -> 17%
where the time goes in v14:
time: 81.2 us; the launch traced here: 80.9 us
  starting transfers between devices  41.2 us (51%)
  Pallas kernels  27.5 us (34%)
  waiting for transfers between devices  11.8 us (15%)
    pallas_call x29, Pallas kernels, run(): pl.pallas_call(placed, out_shape=outs, in_specs=in_specs or [VMEM] * len(...  27.5 us
    ppermute x20, starting transfers between devices, send(): return lax.ppermute(values, ('gx', 'gy', 'gz'), pairs)  20 us
    ppermute x9, starting transfers between devices, x(): return (lax.ppermute(sends[0], 'gx', self.ring_x),)  11.2 us
    ppermute x9, starting transfers between devices, ring_y(): lax.ppermute(to_low, 'gy', self.back(ring))  9.18 us
    ppermute x20, waiting for transfers between devices, send(): return lax.ppermute(values, ('gx', 'gy', 'gz'), pairs)  4.69 us
    ppermute x9, waiting for transfers between devices, ring_y(): lax.ppermute(to_high, 'gy', ring)  3.42 us
    ppermute x9, waiting for transfers between devices, x(): return (lax.ppermute(sends[0], 'gx', self.ring_x),)  2.66 us
  transfers between devices with their start and end apart: 47, of which 12 were waited for; matrix products, arithmetic and copies ran while one was open for 0% of the time, Pallas kernels for 17%

profile of v14, /device:TPU:0, one launch (start us, length us, event | category | flops | bytes accessed | tf_op | source)
XLA Modules:
  0.0 80.9 jit_solution(14538539299381176162)
XLA Ops:
  0.0 1.5 %shard_map.46 = (f32[24,32,128]{2,1,0:T(8,128)S(1)}, f32[24,32,128]{2,1,0:T(8,128)S(1)}, f32[24,32,128]{2,1,0:T(8,128)S(1)}, s32[12,16,64]{2,1,0:T(8,128)S(1)}, ...) custom-call(f32[24,32,128]{2,1,0:T(8,128)} %refs_0_.1, ...), custom_call_target="tpu_custom_call" | custom-call | flops 1000000 | bytes 100000 | tf_op jit(solution)/shard_map/pallas_call | solution.py:36
  1.5 3.0 %collective-permute-start = (f32[11,32,128]{2,1,0:T(8,128)S(1)}, f32[11,32,128]{2,1,0:T(8,128)S(1)}, u32[]{:S(2)}, u32[]{:S(2)}) collective-permute-start(f32[11,32,128]{2,1,0:T(8,128)S(1)} %get-tuple-element.63.refs_3_), channel_id=1, source_target_pairs={{0,16},{16,0},{1,17},{17,1},{2,18},{18,2},{3,19},{19,3},{4,20},{20... | collective-permute-start | bytes 540680 | tf_op jit(solution)/shard_map/ppermute | solution.py:301
  4.5 1.7 %collective-permute-start.2 = (f32[256,128]{1,0:T(8,128)S(1)}, f32[256,128]{1,0:T(8,128)S(1)}, u32[]{:S(2)}, u32[]{:S(2)}) collective-permute-start(f32[256,128]{1,0:T(8,128)S(1)} %get-tuple-element.65), channel_id=1, source_target_pairs={{4,0},{8,4},{12,8},{0,12},{5,1},{9,5},{13,9},{1,13},{6,2},{10,6},{... | collective-permute-start | bytes 393224 | tf_op jit(solution)/shard_map/ppermute | solution.py:311
  6.3 2.6 %collective-permute-start.4 = (f32[40,128]{1,0:T(8,128)S(1)}, f32[40,128]{1,0:T(8,128)S(1)}, u32[]{:S(2)}, u32[]{:S(2)}) collective-permute-start(f32[40,128]{1,0:T(8,128)S(1)} %get-tuple-element.67), channel_id=1, source_target_pairs={{20,0},{21,1},{22,2},{23,3},{24,4},{25,5},{26,6},{27,7},{28,8},{29... | collective-permute-start | bytes 61448 | tf_op jit(solution)/shard_map/ppermute | solution.py:297
  8.9 1.9 %shard_map.47 = (f32[12,8,128]{2,1,0:T(8,128)S(1)}, s32[6,12,8,128]{3,2,1,0:T(8,128)S(1)}, f32[6,12,8,128]{3,2,1,0:T(8,128)S(1)}, f32[12,8,128]{2,1,0:T(8,128)S(...) custom-call(f32[24,32,128]{2,1,0:T(8,128)S(1)} %get-tuple-element.59.refs_0_, ...), custom_call_target="tpu_custom_call" | custom-call | flops 1000000 | bytes 100000 | tf_op jit(solution)/shard_map/pallas_call | solution.py:36
  12.0 1.6 %collective-permute-start.5 = (f32[136,128]{1,0:T(8,128)S(1)}, f32[136,128]{1,0:T(8,128)S(1)}, u32[]{:S(2)}, u32[]{:S(2)}) collective-permute-start(f32[136,128]{1,0:T(8,128)S(1)} %get-tuple-element.75), channel_id=1, source_target_pairs={{0,1},{1,2},{2,3},{3,7},{7,6},{6,5},{5,4},{4,0},{8,9},{9,10},{10,1... | collective-permute-start | bytes 208904 | tf_op jit(solution)/shard_map/ppermute | solution.py:297
  13.6 2.5 %shard_map.49 = (f32[32,56,128]{2,1,0:T(8,128)S(1)}, f32[32,56,128]{2,1,0:T(8,128)S(1)}, f32[32,56,128]{2,1,0:T(8,128)S(1)}, f32[32,56,128]{2,1,0:T(8,128)S(1)},...) custom-call(f32[3,32,56,128]{3,2,1,0:T(8,128)S(1)} %get-tuple-element.74.refs_0_, ...), custom_call_target="tpu_custom_call" | custom-call | flops 1000000 | bytes 100000 | tf_op jit(solution)/shard_map/pallas_call | solution.py:36
  16.1 1.8 %collective-permute-done.6.refs_2_.refs_8_ = f32[136,128]{1,0:T(8,128)S(1)} collective-permute-done((f32[136,128]{1,0:T(8,128)S(1)}, f32[136,128]{1,0:T(8,128)S(1)}, u32[]{:S(2)}, u32[]{:S(2)}) %collective-permute-start.6) | collective-permute-done | bytes 69664 | tf_op jit(solution)/shard_map/ppermute | solution.py:297
  17.9 4.5 %shard_map.50 = (f32[32,56,128]{2,1,0:T(8,128)S(1)}, f32[32,56,128]{2,1,0:T(8,128)S(1)}, f32[2,56,128]{2,1,0:T(8,128)S(1)}, f32[2,56,128]{2,1,0:T(8,128)S(1)}, f...) custom-call(f32[3,32,56,128]{3,2,1,0:T(8,128)S(1)} %get-tuple-elemen, ...), custom_call_target="tpu_custom_call" | custom-call | flops 1000000 | bytes 100000 | tf_op jit(solution)/shard_map/pallas_call | solution.py:36
  27.9 1.2 %collective-permute-start.13 = (f32[264,128]{1,0:T(8,128)S(1)}, f32[264,128]{1,0:T(8,128)S(1)}, u32[]{:S(2)}, u32[]{:S(2)}) collective-permute-start(f32[264,128]{1,0:T(8,128)S(1)} %get-tuple-element.98), channel_id=1, source_target_pairs={{4,0},{8,4},{12,8},{0,12},{5,1},{9,5},{13,9},{1,13},{6,2},{10,6},{... | collective-permute-start | bytes 405512 | tf_op jit(solution)/shard_map/ppermute | solution.py:311
  30.3 1.4 %collective-permute-start.15 = (f32[8,128]{1,0:T(8,128)S(1)}, f32[8,128]{1,0:T(8,128)S(1)}, u32[]{:S(2)}, u32[]{:S(2)}) collective-permute-start(f32[8,128]{1,0:T(8,128)S(1)} %shard_map.54.refs_2_.refs_3_), channel_id=1, source_target_pairs={{1,0},{2,1},{3,2},{7,3},{6,7},{5,6},{4,5},{0,4},{9,8},{10,9},{11,1... | collective-permute-start | bytes 12296 | tf_op jit(solution)/shard_map/ppermute | solution.py:297
  35.2 1.6 %collective-permute-start.17 = (f32[88,128]{1,0:T(8,128)S(1)}, f32[88,128]{1,0:T(8,128)S(1)}, u32[]{:S(2)}, u32[]{:S(2)}) collective-permute-start(f32[88,128]{1,0:T(8,128)S(1)} %get-tuple-element.100), channel_id=1, source_target_pairs={{0,1},{1,2},{2,3},{3,7},{7,6},{6,5},{5,4},{4,0},{8,9},{9,10},{10,1... | collective-permute-start | bytes 135176 | tf_op jit(solution)/shard_map/ppermute | solution.py:297
  46.9 1.7 %collective-permute-start.31 = (f32[8,128]{1,0:T(8,128)S(1)}, f32[8,128]{1,0:T(8,128)S(1)}, u32[]{:S(2)}, u32[]{:S(2)}) collective-permute-start(f32[8,128]{1,0:T(8,128)S(1)} %shard_map.64.refs_3_), channel_id=1, source_target_pairs={{4,0},{8,4},{12,8},{0,12},{5,1},{9,5},{13,9},{1,13},{6,2},{10,6},{... | collective-permute-start | bytes 12296 | tf_op jit(solution)/shard_map/ppermute | solution.py:311
  53.1 1.3 %collective-permute-start.36 = (f32[8,128]{1,0:T(8,128)S(1)}, f32[8,128]{1,0:T(8,128)S(1)}, u32[]{:S(2)}, u32[]{:S(2)}) collective-permute-start(f32[8,128]{1,0:T(8,128)S(1)} %shard_map.66.refs_3_), channel_id=1, source_target_pairs={{4,0},{8,4},{12,8},{0,12},{5,1},{9,5},{13,9},{1,13},{6,2},{10,6},{... | collective-permute-start | bytes 12296 | tf_op jit(solution)/shard_map/ppermute | solution.py:311
  54.5 1.3 %collective-permute-start.34 = (f32[8,128]{1,0:T(8,128)S(1)}, f32[8,128]{1,0:T(8,128)S(1)}, u32[]{:S(2)}, u32[]{:S(2)}) collective-permute-start(f32[8,128]{1,0:T(8,128)S(1)} %shard_map.66.refs_3_), channel_id=1, source_target_pairs={{0,16},{16,0},{1,17},{17,1},{2,18},{18,2},{3,19},{19,3},{4,20},{20... | collective-permute-start | bytes 12296 | tf_op jit(solution)/shard_map/ppermute | solution.py:301
  56.5 1.3 %collective-permute-start.32 = (f32[8,128]{1,0:T(8,128)S(1)}, f32[8,128]{1,0:T(8,128)S(1)}, u32[]{:S(2)}, u32[]{:S(2)}) collective-permute-start(f32[8,128]{1,0:T(8,128)S(1)} %shard_map.66.refs_3_), channel_id=1, source_target_pairs={{0,1},{1,2},{2,3},{3,7},{7,6},{6,5},{5,4},{4,0},{8,9},{9,10},{10,1... | collective-permute-start | bytes 12296 | tf_op jit(solution)/shard_map/ppermute | solution.py:297
  59.6 1.4 %collective-permute-start.41 = (f32[8,128]{1,0:T(8,128)S(1)}, f32[8,128]{1,0:T(8,128)S(1)}, u32[]{:S(2)}, u32[]{:S(2)}) collective-permute-start(f32[8,128]{1,0:T(8,128)S(1)} %shard_map.68.refs_3_), channel_id=1, source_target_pairs={{4,0},{8,4},{12,8},{0,12},{5,1},{9,5},{13,9},{1,13},{6,2},{10,6},{... | collective-permute-start | bytes 12296 | tf_op jit(solution)/shard_map/ppermute | solution.py:311
  61.5 1.4 %collective-permute-start.38 = (f32[8,128]{1,0:T(8,128)S(1)}, f32[8,128]{1,0:T(8,128)S(1)}, u32[]{:S(2)}, u32[]{:S(2)}) collective-permute-start(f32[8,128]{1,0:T(8,128)S(1)} %shard_map.68.refs_3_), channel_id=1, source_target_pairs={{1,0},{2,1},{3,2},{7,3},{6,7},{5,6},{4,5},{0,4},{9,8},{10,9},{11,1... | collective-permute-start | bytes 12296 | tf_op jit(solution)/shard_map/ppermute | solution.py:297
  65.3 1.6 %collective-permute-start.42 = (f32[8,128]{1,0:T(8,128)S(1)}, f32[8,128]{1,0:T(8,128)S(1)}, u32[]{:S(2)}, u32[]{:S(2)}) collective-permute-start(f32[8,128]{1,0:T(8,128)S(1)} %shard_map.70.refs_2_.refs_1_), channel_id=1, source_target_pairs={{0,16},{16,0},{1,17},{17,1},{2,18},{18,2},{3,19},{19,3},{4,20},{20... | collective-permute-start | bytes 12296 | tf_op jit(solution)/shard_map/ppermute | solution.py:301
  66.9 2.1 %collective-permute-done.42.refs_0_.refs_2_ = f32[8,128]{1,0:T(8,128)S(1)} collective-permute-done((f32[8,128]{1,0:T(8,128)S(1)}, f32[8,128]{1,0:T(8,128)S(1)}, u32[]{:S(2)}, u32[]{:S(2)}) %collective-permute-start.42) | collective-permute-done | bytes 4128 | tf_op jit(solution)/shard_map/ppermute | solution.py:301
  70.5 1.7 %collective-permute-done.43.refs_0_ = f32[8,128]{1,0:T(8,128)S(1)} collective-permute-done((f32[8,128]{1,0:T(8,128)S(1)}, f32[8,128]{1,0:T(8,128)S(1)}, u32[]{:S(2)}, u32[]{:S(2)}) %collective-permute-start.43) | collective-permute-done | bytes 4128 | tf_op jit(solution)/shard_map/ppermute | solution.py:311
  72.3 1.9 %collective-permute-start.45 = (f32[16,128]{1,0:T(8,128)S(1)}, f32[16,128]{1,0:T(8,128)S(1)}, u32[]{:S(2)}, u32[]{:S(2)}) collective-permute-start(f32[16,128]{1,0:T(8,128)S(1)} %shard_map.73.refs_1_), channel_id=1, source_target_pairs={{0,1},{1,2},{2,3},{3,7},{7,6},{6,5},{5,4},{4,0},{8,9},{9,10},{10,1... | collective-permute-start | bytes 24584 | tf_op jit(solution)/shard_map/ppermute | solution.py:297
  74.6 1.2 %collective-permute-done.46.refs_3_ = f32[16,128]{1,0:T(8,128)S(1)} collective-permute-done((f32[16,128]{1,0:T(8,128)S(1)}, f32[16,128]{1,0:T(8,128)S(1)}, u32[]{:S(2)}, u32[]{:S(2)}) %collective-permute-start.46) | collective-permute-done | bytes 8224 | tf_op jit(solution)/shard_map/ppermute | solution.py:297
  75.8 5.1 %shard_map.74 = (f32[24,32,128]{2,1,0:T(8,128)}, f32[32,56,128]{2,1,0:T(8,128)S(1)}) custom-call(f32[32,56,128]{2,1,0:T(8,128)S(1)} %shard_map.71.refs_0_, f32[16,128]{1,0:T(8,128)S(1)} %shard_map.73.refs_1_, f32[16,128]{1,0:T(8,128)S(1)} %collective-permute-done.45.refs_2_, ...), custom_call_target="tpu_custom_call", output_to_operand_aliasing={{1}: (0, {})} | custom-call | flops 1000000 | bytes 100000 | tf_op jit(solution)/shard_map/pallas_call | solution.py:36
  (99 shorter events, 33.2 us)
Async XLA Ops:
  1.5 9.4 %collective-permute-start = (f32[11,32,128]{2,1,0:T(8,128)S(1)}, f32[11,32,128]{2,1,0:T(8,128)S(1)}, u32[]{:S(2)}, u32[]{:S(2)}) collective-permute-start(f32[11,32,128]{2,1,0:T(8,128)S(1)} %get-tuple-element.63.refs_3_), channel_id=1, source_target_pairs={{0,16},{16,0},{1,17},{17,1},{2,18},{18,2},{3,19},{19,3},{4,20},{20... | collective-permute-start | bytes 540680 | tf_op jit(solution)/shard_map/ppermute | solution.py:301
  4.5 6.4 %collective-permute-start.1 = (f32[256,128]{1,0:T(8,128)S(1)}, f32[256,128]{1,0:T(8,128)S(1)}, u32[]{:S(2)}, u32[]{:S(2)}) collective-permute-start(f32[256,128]{1,0:T(8,128)S(1)} %get-tuple-element.64), channel_id=1, source_target_pairs={{0,4},{4,8},{8,12},{12,0},{1,5},{5,9},{9,13},{13,1},{2,6},{6,10},{... | collective-permute-start | bytes 393224 | tf_op jit(solution)/shard_map/ppermute | solution.py:311
  4.5 6.4 %collective-permute-start.2 = (f32[256,128]{1,0:T(8,128)S(1)}, f32[256,128]{1,0:T(8,128)S(1)}, u32[]{:S(2)}, u32[]{:S(2)}) collective-permute-start(f32[256,128]{1,0:T(8,128)S(1)} %get-tuple-element.65), channel_id=1, source_target_pairs={{4,0},{8,4},{12,8},{0,12},{5,1},{9,5},{13,9},{1,13},{6,2},{10,6},{... | collective-permute-start | bytes 393224 | tf_op jit(solution)/shard_map/ppermute | solution.py:311
  6.3 4.6 %collective-permute-start.3 = (f32[40,128]{1,0:T(8,128)S(1)}, f32[40,128]{1,0:T(8,128)S(1)}, u32[]{:S(2)}, u32[]{:S(2)}) collective-permute-start(f32[40,128]{1,0:T(8,128)S(1)} %get-tuple-element.66), channel_id=1, source_target_pairs={{0,20},{1,21},{2,22},{3,23},{4,24},{5,25},{6,26},{7,27},{8,28},{9,... | collective-permute-start | bytes 61448 | tf_op jit(solution)/shard_map/ppermute | solution.py:297
  6.3 4.6 %collective-permute-start.4 = (f32[40,128]{1,0:T(8,128)S(1)}, f32[40,128]{1,0:T(8,128)S(1)}, u32[]{:S(2)}, u32[]{:S(2)}) collective-permute-start(f32[40,128]{1,0:T(8,128)S(1)} %get-tuple-element.67), channel_id=1, source_target_pairs={{20,0},{21,1},{22,2},{23,3},{24,4},{25,5},{26,6},{27,7},{28,8},{29... | collective-permute-start | bytes 61448 | tf_op jit(solution)/shard_map/ppermute | solution.py:297
  12.0 4.1 %collective-permute-start.5 = (f32[136,128]{1,0:T(8,128)S(1)}, f32[136,128]{1,0:T(8,128)S(1)}, u32[]{:S(2)}, u32[]{:S(2)}) collective-permute-start(f32[136,128]{1,0:T(8,128)S(1)} %get-tuple-element.75), channel_id=1, source_target_pairs={{0,1},{1,2},{2,3},{3,7},{7,6},{6,5},{5,4},{4,0},{8,9},{9,10},{10,1... | collective-permute-start | bytes 208904 | tf_op jit(solution)/shard_map/ppermute | solution.py:297
  13.6 4.3 %collective-permute-start.6 = (f32[136,128]{1,0:T(8,128)S(1)}, f32[136,128]{1,0:T(8,128)S(1)}, u32[]{:S(2)}, u32[]{:S(2)}) collective-permute-start(f32[136,128]{1,0:T(8,128)S(1)} %get-tuple-element.76), channel_id=1, source_target_pairs={{1,0},{2,1},{3,2},{7,3},{6,7},{5,6},{4,5},{0,4},{9,8},{10,9},{11,1... | collective-permute-start | bytes 208904 | tf_op jit(solution)/shard_map/ppermute | solution.py:297
  22.4 5.3 %collective-permute-start.7 = (f32[9,32,128]{2,1,0:T(8,128)S(1)}, f32[9,32,128]{2,1,0:T(8,128)S(1)}, u32[]{:S(2)}, u32[]{:S(2)}) collective-permute-start(f32[9,32,128]{2,1,0:T(8,128)S(1)} %shard_map.51), channel_id=1, source_target_pairs={{0,16},{16,0},{1,17},{17,1},{2,18},{18,2},{3,19},{19,3},{4,20},{20... | collective-permute-start | bytes 442376 | tf_op jit(solution)/shard_map/ppermute | solution.py:301
  23.2 4.4 %collective-permute-start.11 = (f32[8,128]{1,0:T(8,128)S(1)}, f32[8,128]{1,0:T(8,128)S(1)}, u32[]{:S(2)}, u32[]{:S(2)}) collective-permute-start(f32[8,128]{1,0:T(8,128)S(1)} %get-tuple-element.88.refs_2_.refs_3_.refs_1_), channel_id=1, source_target_pairs={{4,0},{8,4},{12,8},{0,12},{5,1},{9,5},{13,9},{1,13},{6,2},{10,6},{... | collective-permute-start | bytes 12296 | tf_op jit(solution)/shard_map/ppermute | solution.py:311
  23.2 4.4 %collective-permute-start.10 = (f32[8,128]{1,0:T(8,128)S(1)}, f32[8,128]{1,0:T(8,128)S(1)}, u32[]{:S(2)}, u32[]{:S(2)}) collective-permute-start(f32[8,128]{1,0:T(8,128)S(1)} %get-tuple-element.88.refs_2_.refs_3_.refs_1_), channel_id=1, source_target_pairs={{0,4},{4,8},{8,12},{12,0},{1,5},{5,9},{9,13},{13,1},{2,6},{6,10},{... | collective-permute-start | bytes 12296 | tf_op jit(solution)/shard_map/ppermute | solution.py:311
  27.9 6.0 %collective-permute-start.13 = (f32[264,128]{1,0:T(8,128)S(1)}, f32[264,128]{1,0:T(8,128)S(1)}, u32[]{:S(2)}, u32[]{:S(2)}) collective-permute-start(f32[264,128]{1,0:T(8,128)S(1)} %get-tuple-element.98), channel_id=1, source_target_pairs={{4,0},{8,4},{12,8},{0,12},{5,1},{9,5},{13,9},{1,13},{6,2},{10,6},{... | collective-permute-start | bytes 405512 | tf_op jit(solution)/shard_map/ppermute | solution.py:311
  29.1 5.6 %collective-permute-start.12 = (f32[264,128]{1,0:T(8,128)S(1)}, f32[264,128]{1,0:T(8,128)S(1)}, u32[]{:S(2)}, u32[]{:S(2)}) collective-permute-start(f32[264,128]{1,0:T(8,128)S(1)} %get-tuple-element.94.refs_4_), channel_id=1, source_target_pairs={{0,4},{4,8},{8,12},{12,0},{1,5},{5,9},{9,13},{13,1},{2,6},{6,10},{... | collective-permute-start | bytes 405512 | tf_op jit(solution)/shard_map/ppermute | solution.py:311
  29.1 4.7 %collective-permute-start.16 = (f32[8,128]{1,0:T(8,128)S(1)}, f32[8,128]{1,0:T(8,128)S(1)}, u32[]{:S(2)}, u32[]{:S(2)}) collective-permute-start(f32[8,128]{1,0:T(8,128)S(1)} %shard_map.54.refs_2_.refs_3_), channel_id=1, source_target_pairs={{0,16},{16,0},{1,17},{17,1},{2,18},{18,2},{3,19},{19,3},{4,20},{20... | collective-permute-start | bytes 12296 | tf_op jit(solution)/shard_map/ppermute | solution.py:301
  35.2 6.1 %collective-permute-start.17 = (f32[88,128]{1,0:T(8,128)S(1)}, f32[88,128]{1,0:T(8,128)S(1)}, u32[]{:S(2)}, u32[]{:S(2)}) collective-permute-start(f32[88,128]{1,0:T(8,128)S(1)} %get-tuple-element.100), channel_id=1, source_target_pairs={{0,1},{1,2},{2,3},{3,7},{7,6},{6,5},{5,4},{4,0},{8,9},{9,10},{10,1... | collective-permute-start | bytes 135176 | tf_op jit(solution)/shard_map/ppermute | solution.py:297
  36.8 4.5 %collective-permute-start.18 = (f32[88,128]{1,0:T(8,128)S(1)}, f32[88,128]{1,0:T(8,128)S(1)}, u32[]{:S(2)}, u32[]{:S(2)}) collective-permute-start(f32[88,128]{1,0:T(8,128)S(1)} %get-tuple-element.101), channel_id=1, source_target_pairs={{1,0},{2,1},{3,2},{7,3},{6,7},{5,6},{4,5},{0,4},{9,8},{10,9},{11,1... | collective-permute-start | bytes 135176 | tf_op jit(solution)/shard_map/ppermute | solution.py:297
  41.5 4.8 %collective-permute-start.26 = (f32[8,128]{1,0:T(8,128)S(1)}, f32[8,128]{1,0:T(8,128)S(1)}, u32[]{:S(2)}, u32[]{:S(2)}) collective-permute-start(f32[8,128]{1,0:T(8,128)S(1)} %shard_map.62.refs_3_), channel_id=1, source_target_pairs={{4,0},{8,4},{12,8},{0,12},{5,1},{9,5},{13,9},{1,13},{6,2},{10,6},{... | collective-permute-start | bytes 12296 | tf_op jit(solution)/shard_map/ppermute | solution.py:311
  42.1 4.2 %collective-permute-start.25 = (f32[8,128]{1,0:T(8,128)S(1)}, f32[8,128]{1,0:T(8,128)S(1)}, u32[]{:S(2)}, u32[]{:S(2)}) collective-permute-start(f32[8,128]{1,0:T(8,128)S(1)} %shard_map.62.refs_3_), channel_id=1, source_target_pairs={{0,4},{4,8},{8,12},{12,0},{1,5},{5,9},{9,13},{13,1},{2,6},{6,10},{... | collective-permute-start | bytes 12296 | tf_op jit(solution)/shard_map/ppermute | solution.py:311
  42.2 4.2 %collective-permute-start.24 = (f32[8,128]{1,0:T(8,128)S(1)}, f32[8,128]{1,0:T(8,128)S(1)}, u32[]{:S(2)}, u32[]{:S(2)}) collective-permute-start(f32[8,128]{1,0:T(8,128)S(1)} %shard_map.62.refs_3_), channel_id=1, source_target_pairs={{0,16},{16,0},{1,17},{17,1},{2,18},{18,2},{3,19},{19,3},{4,20},{20... | collective-permute-start | bytes 12296 | tf_op jit(solution)/shard_map/ppermute | solution.py:301
  46.9 5.6 %collective-permute-start.31 = (f32[8,128]{1,0:T(8,128)S(1)}, f32[8,128]{1,0:T(8,128)S(1)}, u32[]{:S(2)}, u32[]{:S(2)}) collective-permute-start(f32[8,128]{1,0:T(8,128)S(1)} %shard_map.64.refs_3_), channel_id=1, source_target_pairs={{4,0},{8,4},{12,8},{0,12},{5,1},{9,5},{13,9},{1,13},{6,2},{10,6},{... | collective-permute-start | bytes 12296 | tf_op jit(solution)/shard_map/ppermute | solution.py:311
  48.6 4.0 %collective-permute-start.29 = (f32[8,128]{1,0:T(8,128)S(1)}, f32[8,128]{1,0:T(8,128)S(1)}, u32[]{:S(2)}, u32[]{:S(2)}) collective-permute-start(f32[8,128]{1,0:T(8,128)S(1)} %shard_map.64.refs_3_), channel_id=1, source_target_pairs={{0,16},{16,0},{1,17},{17,1},{2,18},{18,2},{3,19},{19,3},{4,20},{20... | collective-permute-start | bytes 12296 | tf_op jit(solution)/shard_map/ppermute | solution.py:301
  53.1 5.9 %collective-permute-start.36 = (f32[8,128]{1,0:T(8,128)S(1)}, f32[8,128]{1,0:T(8,128)S(1)}, u32[]{:S(2)}, u32[]{:S(2)}) collective-permute-start(f32[8,128]{1,0:T(8,128)S(1)} %shard_map.66.refs_3_), channel_id=1, source_target_pairs={{4,0},{8,4},{12,8},{0,12},{5,1},{9,5},{13,9},{1,13},{6,2},{10,6},{... | collective-permute-start | bytes 12296 | tf_op jit(solution)/shard_map/ppermute | solution.py:311
  54.5 4.5 %collective-permute-start.35 = (f32[8,128]{1,0:T(8,128)S(1)}, f32[8,128]{1,0:T(8,128)S(1)}, u32[]{:S(2)}, u32[]{:S(2)}) collective-permute-start(f32[8,128]{1,0:T(8,128)S(1)} %shard_map.66.refs_3_), channel_id=1, source_target_pairs={{0,4},{4,8},{8,12},{12,0},{1,5},{5,9},{9,13},{13,1},{2,6},{6,10},{... | collective-permute-start | bytes 12296 | tf_op jit(solution)/shard_map/ppermute | solution.py:311
  54.5 4.5 %collective-permute-start.34 = (f32[8,128]{1,0:T(8,128)S(1)}, f32[8,128]{1,0:T(8,128)S(1)}, u32[]{:S(2)}, u32[]{:S(2)}) collective-permute-start(f32[8,128]{1,0:T(8,128)S(1)} %shard_map.66.refs_3_), channel_id=1, source_target_pairs={{0,16},{16,0},{1,17},{17,1},{2,18},{18,2},{3,19},{19,3},{4,20},{20... | collective-permute-start | bytes 12296 | tf_op jit(solution)/shard_map/ppermute | solution.py:301
  59.6 5.1 %collective-permute-start.41 = (f32[8,128]{1,0:T(8,128)S(1)}, f32[8,128]{1,0:T(8,128)S(1)}, u32[]{:S(2)}, u32[]{:S(2)}) collective-permute-start(f32[8,128]{1,0:T(8,128)S(1)} %shard_map.68.refs_3_), channel_id=1, source_target_pairs={{4,0},{8,4},{12,8},{0,12},{5,1},{9,5},{13,9},{1,13},{6,2},{10,6},{... | collective-permute-start | bytes 12296 | tf_op jit(solution)/shard_map/ppermute | solution.py:311
  (23 other events, 74.0 us)

commit v15 on v13

--- a/solution.py
+++ b/solution.py
@@ -551,7 +551,7 @@
                 ref[x, span] = value
         return edges
 
-    edges = batched(0, wide, first_sweep, jnp.zeros((tall, LANES), F32), 4)
+    edges = batched(0, wide, first_sweep, jnp.zeros((tall, LANES), F32), 8)
 
     join = joined(end_low * start_ends[0, span], end_high * start_ends[1, span])
     near = ends_near(start_ends[0, span], start_ends[1, span], edges)
@@ -784,7 +784,29 @@
         ends[s] = values.astype(jnp.int32)
 
 
-def post_kernel(flags, table, table_forth, table_back, labels, end_labels, wide_ref, forth, back, *refs):
+def rows_of(frame, table, dx):
+    row = row_no((frame.tall, LANES))
+    low, mid, high = (table[3 * n + dx + 1 : 3 * n + dx + 2] for n in range(3))
+    return jnp.where(row < HALO, low, jnp.where(row < HALO + frame.ny, mid, high))
+
+
+def lift_main_kernel(flags, table, labels, wide_ref, lifted):
+    frame = Frame(wide_ref.shape[1] - 2 * HALO, wide_ref.shape[2] - 2 * (SUB + HALO))
+    last = HALO + frame.nx
+    for first, stop, dx in ((0, HALO, -1), (HALO, last, 0), (last, frame.wide, 1)):
+        values = rows_of(frame, table[...], dx)
+
+        def lift(bs, carry, values=values):
+            news = [picked(values, labels[b]) for b in bs]
+            for b, new in zip(bs, news):
+                for a in range(2):
+                    lifted[2 * b + a, frame.span] = wide_ref[0, 2 * b + a, frame.span] + new
+            return carry
+
+        batched(first // 2, stop // 2, lift, 0, 6)
+
+
+def post_kernel(flags, lifted, table_forth, table_back, end_labels, forth, back, *refs):
     (wx, wy, wz, inv_diag, start), ends = refs[:5], refs[5:11]
     out, one, two, one_ends, two_ends, kept_out, sems = refs[11:]
     nx, ny = out.shape[0], out.shape[1]
@@ -793,37 +815,19 @@
     ex, ey, ez_up, ez_low, inv_ends, start_ends = ends
     for ref in (one_ends, two_ends):
         clear_spares(ref, frame)
-    row, lane = row_no((tall, LANES)), lane_no((tall, LANES))
-    under, over = sides(flags, table_forth[...], table_back[...])
-    tables = {-1: under, 0: table[...], 1: over}
-
-    def table_at(dx, dz):
-        low, mid, high = (tables[dz][3 * n + dx + 1 : 3 * n + dx + 2] for n in range(3))
-        return jnp.where(row < HALO, low, jnp.where(row < HALO + ny, mid, high))
-
-    for x_from, x_to, dx in ((0, HALO, -1), (HALO, HALO + nx, 0), (HALO + nx, wide, 1)):
-        values = table_at(dx, 0)
-
-        def lift(bs, carry, values=values):
-            news = [picked(values, labels[b]) for b in bs]
-            for b, new in zip(bs, news):
-                for a in range(2):
-                    two[2 * b + a, span] = wide_ref[0, 2 * b + a, span] + new
-            return carry
-
-        batched(x_from // 2, x_to // 2, lift, 0, 4)
-    for s, (dz, base) in enumerate(zip((-1, 1), sides(flags, forth[:tall], back[:tall]))):
-        below, inside, above = (picked(table_at(dx, dz), end_labels[s]) for dx in (-1, 0, 1))
+    lane = lane_no((tall, LANES))
+    tables = sides(flags, table_forth[...], table_back[...])
+    for s, (table, base) in enumerate(zip(tables, sides(flags, forth[:tall], back[:tall]))):
+        below, inside, above = (picked(rows_of(frame, table, dx), end_labels[s]) for dx in (-1, 0, 1))
         spot = lane // HALO
-        lifted = jnp.where(spot < HALO, below, jnp.where(spot < HALO + nx, inside, above))
-        two_ends[s, span] = base + lifted
+        two_ends[s, span] = base + jnp.where(spot < HALO, below, jnp.where(spot < HALO + nx, inside, above))
     kept = 1.0 - OMEGA_FINE
 
     def result(at, count):
         rows = pl.ds(at, count)
         return pltpu.make_async_copy(kept_out.at[rows], out.at[rows], sems.at[at // count])
 
-    buffers = ((two, two_ends), (one, one_ends), (two, two_ends), (one, one_ends))
+    buffers = ((lifted, two_ends), (one, one_ends), (two, two_ends), (one, one_ends))
     for s in range(POST):
         src, src_ends = buffers[s]
         join = joined(ez_up[0, span] * src_ends[0, span], ez_low[1, span] * src_ends[1, span])
@@ -879,12 +883,6 @@
     from_x = links.x(sends[:n_send])
     from_y = links.ring_y(*sends[n_send : n_send + 2])
     from_corners = links.corners(sends[n_send + 2 :])
-    size = len(WIDTHS) * frame.tall
-    wide, *sends = call(
-        functools.partial(first_frame_kernel, n_x, WIDTHS),
-        [shaped(len(WIDTHS), *frame.main)] + [shaped(size + ny // 2, nz)] * 2,
-        [pltpu.VMEM((size, nz), F32)] * 2,
-    )(*arrays, from_x[0], from_x[-1], *from_y, *from_corners)
     blocks = (nb, SUB, LANES)
     outs = [shaped(*blocks), jax.ShapeDtypeStruct((6, *blocks), jnp.int32), shaped(6, *blocks), shaped(*blocks)]
     outs += [shaped(6, SUB, LANES), shaped(nx, ny, nz)]
@@ -892,7 +890,15 @@
     *rows, inner, face_label, fine_label = call(blocks_kernel, outs, scratch)(
         arrays[0], arrays[2], arrays[3], sends[0]
     )
+    got = lax.optimization_barrier((*from_x, *from_y, *from_corners, inner))
+    from_x, from_y, from_corners, inner = got[:n_send], got[n_send : n_send + 2], got[n_send + 2 : -1], got[-1]
     block_label = rows[0]
+    size = len(WIDTHS) * frame.tall
+    wide, *sends = call(
+        functools.partial(first_frame_kernel, n_x, WIDTHS),
+        [shaped(len(WIDTHS), *frame.main)] + [shaped(size + ny // 2, nz)] * 2,
+        [pltpu.VMEM((size, nz), F32)] * 2,
+    )(*arrays, from_x[0], from_x[-1], *from_y, *from_corners)
     outs = [shaped(*frame.main)] * 4 + [shaped(frame.tall, nz), shaped(4, SUB, LANES), shaped(SUB, AGG)]
     *fields, weight_xy, some_diag = call(functools.partial(fields_kernel, n_x), outs, limit=24)(
         wide, block_label, inner, face_label
@@ -938,11 +944,12 @@
     three = call(three_kernel, shaped(SUB, AGG))(from_x[0], coarse, from_x[-1])
     low, high = links.ring_y(three, three)
     nine = call(nine_kernel, shaped(2 * SUB, AGG))(low, three, high)
-    tables = (nine, *links.z(nine, nine))
+    tables = links.z(nine, nine)
+    lifted = call(lift_main_kernel, shaped(*frame.main))(nine, lifts[0], halo[0])
     scratch = [pltpu.VMEM(frame.main, F32)] * 2 + [pltpu.VMEM(frame.ends, F32)] * 2
     scratch += [pltpu.VMEM((nx, ny, nz), F32), pltpu.SemaphoreType.DMA((nx // 8,))]
     return call(post_kernel, shaped(nx, ny, nz), scratch, limit=24, out_specs=pl.BlockSpec(memory_space=pl.ANY))(
-        *tables, *lifts, *halo, *fields
+        lifted, *tables, lifts[1], *halo[1:], *fields
     )
 
 

time: 83.1 us -> 80 us (0.963)
  waiting for transfers between devices: 14.7 us -> 11.7 us
    ppermute x9, waiting for transfers between devices: 4.45 us -> 2.66 us  [x(): return (lax.ppermute(sends[0], 'gx', self.ring_x),)]
    ppermute x9, starting transfers between devices: 10.2 us -> 11.2 us  [x(): return (lax.ppermute(sends[0], 'gx', self.ring_x),)]
    pallas_call x28 -> x29, Pallas kernels: 27 us -> 26.4 us  [run(): pl.pallas_call(placed, out_shape=outs, in_specs=in_specs or [VMEM] * len(...]
  transfers between devices with their start and end apart: 47 -> 47, of which waited for: 14 -> 12; matrix products, arithmetic and copies ran while one was open for 0% -> 0% of each run, Pallas kernels for 16% -> 17%
where the time goes in v15:
time: 80 us; the launch traced here: 79.8 us
  starting transfers between devices  41.2 us (52%)
  Pallas kernels  26.4 us (33%)
  waiting for transfers between devices  11.7 us (15%)
    pallas_call x29, Pallas kernels, run(): pl.pallas_call(placed, out_shape=outs, in_specs=in_specs or [VMEM] * len(...  26.4 us
    ppermute x20, starting transfers between devices, send(): return lax.ppermute(values, ('gx', 'gy', 'gz'), pairs)  20 us
    ppermute x9, starting transfers between devices, x(): return (lax.ppermute(sends[0], 'gx', self.ring_x),)  11.2 us
    ppermute x9, starting transfers between devices, ring_y(): lax.ppermute(to_low, 'gy', self.back(ring))  9.18 us
    ppermute x20, waiting for transfers between devices, send(): return lax.ppermute(values, ('gx', 'gy', 'gz'), pairs)  4.6 us
    ppermute x9, waiting for transfers between devices, ring_y(): lax.ppermute(to_high, 'gy', ring)  3.41 us
    ppermute x9, waiting for transfers between devices, x(): return (lax.ppermute(sends[0], 'gx', self.ring_x),)  2.66 us
  transfers between devices with their start and end apart: 47, of which 12 were waited for; matrix products, arithmetic and copies ran while one was open for 0% of the time, Pallas kernels for 17%

profile of v15, /device:TPU:0, one launch (start us, length us, event | category | flops | bytes accessed | tf_op | source)
XLA Modules:
  0.0 79.8 jit_solution(1421901021078145069)
XLA Ops:
  0.0 1.5 %shard_map.46 = (f32[24,32,128]{2,1,0:T(8,128)S(1)}, f32[24,32,128]{2,1,0:T(8,128)S(1)}, f32[24,32,128]{2,1,0:T(8,128)S(1)}, s32[12,16,64]{2,1,0:T(8,128)S(1)}, ...) custom-call(f32[24,32,128]{2,1,0:T(8,128)} %refs_0_.1, ...), custom_call_target="tpu_custom_call" | custom-call | flops 1000000 | bytes 100000 | tf_op jit(solution)/shard_map/pallas_call | solution.py:36
  1.5 3.0 %collective-permute-start = (f32[11,32,128]{2,1,0:T(8,128)S(1)}, f32[11,32,128]{2,1,0:T(8,128)S(1)}, u32[]{:S(2)}, u32[]{:S(2)}) collective-permute-start(f32[11,32,128]{2,1,0:T(8,128)S(1)} %get-tuple-element.61.refs_3_), channel_id=1, source_target_pairs={{0,16},{16,0},{1,17},{17,1},{2,18},{18,2},{3,19},{19,3},{4,20},{20... | collective-permute-start | bytes 540680 | tf_op jit(solution)/shard_map/ppermute | solution.py:301
  4.5 1.7 %collective-permute-start.2 = (f32[256,128]{1,0:T(8,128)S(1)}, f32[256,128]{1,0:T(8,128)S(1)}, u32[]{:S(2)}, u32[]{:S(2)}) collective-permute-start(f32[256,128]{1,0:T(8,128)S(1)} %get-tuple-element.65), channel_id=1, source_target_pairs={{4,0},{8,4},{12,8},{0,12},{5,1},{9,5},{13,9},{1,13},{6,2},{10,6},{... | collective-permute-start | bytes 393224 | tf_op jit(solution)/shard_map/ppermute | solution.py:311
  6.3 2.6 %collective-permute-start.4 = (f32[40,128]{1,0:T(8,128)S(1)}, f32[40,128]{1,0:T(8,128)S(1)}, u32[]{:S(2)}, u32[]{:S(2)}) collective-permute-start(f32[40,128]{1,0:T(8,128)S(1)} %get-tuple-element.67), channel_id=1, source_target_pairs={{20,0},{21,1},{22,2},{23,3},{24,4},{25,5},{26,6},{27,7},{28,8},{29... | collective-permute-start | bytes 61448 | tf_op jit(solution)/shard_map/ppermute | solution.py:297
  8.9 1.9 %shard_map.47 = (f32[12,8,128]{2,1,0:T(8,128)S(1)}, s32[6,12,8,128]{3,2,1,0:T(8,128)S(1)}, f32[6,12,8,128]{3,2,1,0:T(8,128)S(1)}, f32[12,8,128]{2,1,0:T(8,128)S(...) custom-call(f32[24,32,128]{2,1,0:T(8,128)S(1)} %get-tuple-element.58.refs_0_, ...), custom_call_target="tpu_custom_call" | custom-call | flops 1000000 | bytes 100000 | tf_op jit(solution)/shard_map/pallas_call | solution.py:36
  12.0 1.6 %collective-permute-start.5 = (f32[136,128]{1,0:T(8,128)S(1)}, f32[136,128]{1,0:T(8,128)S(1)}, u32[]{:S(2)}, u32[]{:S(2)}) collective-permute-start(f32[136,128]{1,0:T(8,128)S(1)} %get-tuple-element.78), channel_id=1, source_target_pairs={{0,1},{1,2},{2,3},{3,7},{7,6},{6,5},{5,4},{4,0},{8,9},{9,10},{10,1... | collective-permute-start | bytes 208904 | tf_op jit(solution)/shard_map/ppermute | solution.py:297
  13.6 2.5 %shard_map.49 = (f32[32,56,128]{2,1,0:T(8,128)S(1)}, f32[32,56,128]{2,1,0:T(8,128)S(1)}, f32[32,56,128]{2,1,0:T(8,128)S(1)}, f32[32,56,128]{2,1,0:T(8,128)S(1)},...) custom-call(f32[3,32,56,128]{3,2,1,0:T(8,128)S(1)} %get-tuple-element.74.refs_0_, ...), custom_call_target="tpu_custom_call" | custom-call | flops 1000000 | bytes 100000 | tf_op jit(solution)/shard_map/pallas_call | solution.py:36
  16.1 1.8 %collective-permute-done.6.refs_2_.refs_8_ = f32[136,128]{1,0:T(8,128)S(1)} collective-permute-done((f32[136,128]{1,0:T(8,128)S(1)}, f32[136,128]{1,0:T(8,128)S(1)}, u32[]{:S(2)}, u32[]{:S(2)}) %collective-permute-start.6) | collective-permute-done | bytes 69664 | tf_op jit(solution)/shard_map/ppermute | solution.py:297
  17.9 3.9 %shard_map.50 = (f32[32,56,128]{2,1,0:T(8,128)S(1)}, f32[32,56,128]{2,1,0:T(8,128)S(1)}, f32[2,56,128]{2,1,0:T(8,128)S(1)}, f32[2,56,128]{2,1,0:T(8,128)S(1)}, f...) custom-call(f32[3,32,56,128]{3,2,1,0:T(8,128)S(1)} %get-tuple-elemen, ...), custom_call_target="tpu_custom_call" | custom-call | flops 1000000 | bytes 100000 | tf_op jit(solution)/shard_map/pallas_call | solution.py:36
  24.0 1.1 %collective-permute-start.7 = (f32[8,128]{1,0:T(8,128)S(1)}, f32[8,128]{1,0:T(8,128)S(1)}, u32[]{:S(2)}, u32[]{:S(2)}) collective-permute-start(f32[8,128]{1,0:T(8,128)S(1)} %get-tuple-element.87.refs_3_.refs_2_.refs_1_), channel_id=1, source_target_pairs={{0,1},{1,2},{2,3},{3,7},{7,6},{6,5},{5,4},{4,0},{8,9},{9,10},{10,1... | collective-permute-start | bytes 12296 | tf_op jit(solution)/shard_map/ppermute | solution.py:297
  27.3 1.2 %collective-permute-start.16 = (f32[264,128]{1,0:T(8,128)S(1)}, f32[264,128]{1,0:T(8,128)S(1)}, u32[]{:S(2)}, u32[]{:S(2)}) collective-permute-start(f32[264,128]{1,0:T(8,128)S(1)} %get-tuple-element.94), channel_id=1, source_target_pairs={{4,0},{8,4},{12,8},{0,12},{5,1},{9,5},{13,9},{1,13},{6,2},{10,6},{... | collective-permute-start | bytes 405512 | tf_op jit(solution)/shard_map/ppermute | solution.py:311
  29.7 1.4 %collective-permute-start.13 = (f32[8,128]{1,0:T(8,128)S(1)}, f32[8,128]{1,0:T(8,128)S(1)}, u32[]{:S(2)}, u32[]{:S(2)}) collective-permute-start(f32[8,128]{1,0:T(8,128)S(1)} %shard_map.54.refs_3_.refs_2_), channel_id=1, source_target_pairs={{1,0},{2,1},{3,2},{7,3},{6,7},{5,6},{4,5},{0,4},{9,8},{10,9},{11,1... | collective-permute-start | bytes 12296 | tf_op jit(solution)/shard_map/ppermute | solution.py:297
  34.6 1.6 %collective-permute-start.17 = (f32[88,128]{1,0:T(8,128)S(1)}, f32[88,128]{1,0:T(8,128)S(1)}, u32[]{:S(2)}, u32[]{:S(2)}) collective-permute-start(f32[88,128]{1,0:T(8,128)S(1)} %get-tuple-element.98), channel_id=1, source_target_pairs={{0,1},{1,2},{2,3},{3,7},{7,6},{6,5},{5,4},{4,0},{8,9},{9,10},{10,1... | collective-permute-start | bytes 135176 | tf_op jit(solution)/shard_map/ppermute | solution.py:297
  46.3 1.7 %collective-permute-start.31 = (f32[8,128]{1,0:T(8,128)S(1)}, f32[8,128]{1,0:T(8,128)S(1)}, u32[]{:S(2)}, u32[]{:S(2)}) collective-permute-start(f32[8,128]{1,0:T(8,128)S(1)} %shard_map.63.refs_3_), channel_id=1, source_target_pairs={{4,0},{8,4},{12,8},{0,12},{5,1},{9,5},{13,9},{1,13},{6,2},{10,6},{... | collective-permute-start | bytes 12296 | tf_op jit(solution)/shard_map/ppermute | solution.py:311
  52.5 1.3 %collective-permute-start.36 = (f32[8,128]{1,0:T(8,128)S(1)}, f32[8,128]{1,0:T(8,128)S(1)}, u32[]{:S(2)}, u32[]{:S(2)}) collective-permute-start(f32[8,128]{1,0:T(8,128)S(1)} %shard_map.65.refs_3_), channel_id=1, source_target_pairs={{4,0},{8,4},{12,8},{0,12},{5,1},{9,5},{13,9},{1,13},{6,2},{10,6},{... | collective-permute-start | bytes 12296 | tf_op jit(solution)/shard_map/ppermute | solution.py:311
  53.9 1.3 %collective-permute-start.34 = (f32[8,128]{1,0:T(8,128)S(1)}, f32[8,128]{1,0:T(8,128)S(1)}, u32[]{:S(2)}, u32[]{:S(2)}) collective-permute-start(f32[8,128]{1,0:T(8,128)S(1)} %shard_map.65.refs_3_), channel_id=1, source_target_pairs={{0,16},{16,0},{1,17},{17,1},{2,18},{18,2},{3,19},{19,3},{4,20},{20... | collective-permute-start | bytes 12296 | tf_op jit(solution)/shard_map/ppermute | solution.py:301
  55.9 1.3 %collective-permute-start.32 = (f32[8,128]{1,0:T(8,128)S(1)}, f32[8,128]{1,0:T(8,128)S(1)}, u32[]{:S(2)}, u32[]{:S(2)}) collective-permute-start(f32[8,128]{1,0:T(8,128)S(1)} %shard_map.65.refs_3_), channel_id=1, source_target_pairs={{0,1},{1,2},{2,3},{3,7},{7,6},{6,5},{5,4},{4,0},{8,9},{9,10},{10,1... | collective-permute-start | bytes 12296 | tf_op jit(solution)/shard_map/ppermute | solution.py:297
  59.0 1.4 %collective-permute-start.41 = (f32[8,128]{1,0:T(8,128)S(1)}, f32[8,128]{1,0:T(8,128)S(1)}, u32[]{:S(2)}, u32[]{:S(2)}) collective-permute-start(f32[8,128]{1,0:T(8,128)S(1)} %shard_map.67.refs_3_), channel_id=1, source_target_pairs={{4,0},{8,4},{12,8},{0,12},{5,1},{9,5},{13,9},{1,13},{6,2},{10,6},{... | collective-permute-start | bytes 12296 | tf_op jit(solution)/shard_map/ppermute | solution.py:311
  60.9 1.4 %collective-permute-start.38 = (f32[8,128]{1,0:T(8,128)S(1)}, f32[8,128]{1,0:T(8,128)S(1)}, u32[]{:S(2)}, u32[]{:S(2)}) collective-permute-start(f32[8,128]{1,0:T(8,128)S(1)} %shard_map.67.refs_3_), channel_id=1, source_target_pairs={{1,0},{2,1},{3,2},{7,3},{6,7},{5,6},{4,5},{0,4},{9,8},{10,9},{11,1... | collective-permute-start | bytes 12296 | tf_op jit(solution)/shard_map/ppermute | solution.py:297
  64.7 1.6 %collective-permute-start.42 = (f32[8,128]{1,0:T(8,128)S(1)}, f32[8,128]{1,0:T(8,128)S(1)}, u32[]{:S(2)}, u32[]{:S(2)}) collective-permute-start(f32[8,128]{1,0:T(8,128)S(1)} %shard_map.69.refs_1_), channel_id=1, source_target_pairs={{0,16},{16,0},{1,17},{17,1},{2,18},{18,2},{3,19},{19,3},{4,20},{20... | collective-permute-start | bytes 12296 | tf_op jit(solution)/shard_map/ppermute | solution.py:301
  66.3 2.1 %collective-permute-done.42.refs_0_.refs_2_ = f32[8,128]{1,0:T(8,128)S(1)} collective-permute-done((f32[8,128]{1,0:T(8,128)S(1)}, f32[8,128]{1,0:T(8,128)S(1)}, u32[]{:S(2)}, u32[]{:S(2)}) %collective-permute-start.42) | collective-permute-done | bytes 4128 | tf_op jit(solution)/shard_map/ppermute | solution.py:301
  69.9 1.7 %collective-permute-done.43.refs_0_ = f32[8,128]{1,0:T(8,128)S(1)} collective-permute-done((f32[8,128]{1,0:T(8,128)S(1)}, f32[8,128]{1,0:T(8,128)S(1)}, u32[]{:S(2)}, u32[]{:S(2)}) %collective-permute-start.43) | collective-permute-done | bytes 4128 | tf_op jit(solution)/shard_map/ppermute | solution.py:311
  71.7 1.9 %collective-permute-start.45 = (f32[16,128]{1,0:T(8,128)S(1)}, f32[16,128]{1,0:T(8,128)S(1)}, u32[]{:S(2)}, u32[]{:S(2)}) collective-permute-start(f32[16,128]{1,0:T(8,128)S(1)} %shard_map.71.refs_0_), channel_id=1, source_target_pairs={{0,1},{1,2},{2,3},{3,7},{7,6},{6,5},{5,4},{4,0},{8,9},{9,10},{10,1... | collective-permute-start | bytes 24584 | tf_op jit(solution)/shard_map/ppermute | solution.py:297
  75.2 4.5 %shard_map.74 = f32[24,32,128]{2,1,0:T(8,128)} custom-call(f32[32,56,128]{2,1,0:T(8,128)S(1)} %shard_map.73.refs_0_, f32[16,128]{1,0:T(8,128)S(1)} %collective-permute-done.45.refs_1_, f32[16,128]{1,0:T(8,128)S(1)} %collective-permute-done.46.refs_2_, s32[2,40,128]{2,1,0:T(8,128)S(1)} %get-tuple-element.102.refs_3_, ...), custom_call_target="tpu_custom_call" | custom-call | flops 1000000 | bytes 100000 | tf_op jit(solution)/shard_map/pallas_call | solution.py:36
  (99 shorter events, 33.2 us)
Async XLA Ops:
  1.5 9.4 %collective-permute-start = (f32[11,32,128]{2,1,0:T(8,128)S(1)}, f32[11,32,128]{2,1,0:T(8,128)S(1)}, u32[]{:S(2)}, u32[]{:S(2)}) collective-permute-start(f32[11,32,128]{2,1,0:T(8,128)S(1)} %get-tuple-element.61.refs_3_), channel_id=1, source_target_pairs={{0,16},{16,0},{1,17},{17,1},{2,18},{18,2},{3,19},{19,3},{4,20},{20... | collective-permute-start | bytes 540680 | tf_op jit(solution)/shard_map/ppermute | solution.py:301
  4.5 6.4 %collective-permute-start.1 = (f32[256,128]{1,0:T(8,128)S(1)}, f32[256,128]{1,0:T(8,128)S(1)}, u32[]{:S(2)}, u32[]{:S(2)}) collective-permute-start(f32[256,128]{1,0:T(8,128)S(1)} %get-tuple-element.64), channel_id=1, source_target_pairs={{0,4},{4,8},{8,12},{12,0},{1,5},{5,9},{9,13},{13,1},{2,6},{6,10},{... | collective-permute-start | bytes 393224 | tf_op jit(solution)/shard_map/ppermute | solution.py:311
  4.5 6.4 %collective-permute-start.2 = (f32[256,128]{1,0:T(8,128)S(1)}, f32[256,128]{1,0:T(8,128)S(1)}, u32[]{:S(2)}, u32[]{:S(2)}) collective-permute-start(f32[256,128]{1,0:T(8,128)S(1)} %get-tuple-element.65), channel_id=1, source_target_pairs={{4,0},{8,4},{12,8},{0,12},{5,1},{9,5},{13,9},{1,13},{6,2},{10,6},{... | collective-permute-start | bytes 393224 | tf_op jit(solution)/shard_map/ppermute | solution.py:311
  6.3 4.6 %collective-permute-start.3 = (f32[40,128]{1,0:T(8,128)S(1)}, f32[40,128]{1,0:T(8,128)S(1)}, u32[]{:S(2)}, u32[]{:S(2)}) collective-permute-start(f32[40,128]{1,0:T(8,128)S(1)} %get-tuple-element.66), channel_id=1, source_target_pairs={{0,20},{1,21},{2,22},{3,23},{4,24},{5,25},{6,26},{7,27},{8,28},{9,... | collective-permute-start | bytes 61448 | tf_op jit(solution)/shard_map/ppermute | solution.py:297
  6.3 4.6 %collective-permute-start.4 = (f32[40,128]{1,0:T(8,128)S(1)}, f32[40,128]{1,0:T(8,128)S(1)}, u32[]{:S(2)}, u32[]{:S(2)}) collective-permute-start(f32[40,128]{1,0:T(8,128)S(1)} %get-tuple-element.67), channel_id=1, source_target_pairs={{20,0},{21,1},{22,2},{23,3},{24,4},{25,5},{26,6},{27,7},{28,8},{29... | collective-permute-start | bytes 61448 | tf_op jit(solution)/shard_map/ppermute | solution.py:297
  12.0 4.1 %collective-permute-start.5 = (f32[136,128]{1,0:T(8,128)S(1)}, f32[136,128]{1,0:T(8,128)S(1)}, u32[]{:S(2)}, u32[]{:S(2)}) collective-permute-start(f32[136,128]{1,0:T(8,128)S(1)} %get-tuple-element.78), channel_id=1, source_target_pairs={{0,1},{1,2},{2,3},{3,7},{7,6},{6,5},{5,4},{4,0},{8,9},{9,10},{10,1... | collective-permute-start | bytes 208904 | tf_op jit(solution)/shard_map/ppermute | solution.py:297
  13.6 4.3 %collective-permute-start.6 = (f32[136,128]{1,0:T(8,128)S(1)}, f32[136,128]{1,0:T(8,128)S(1)}, u32[]{:S(2)}, u32[]{:S(2)}) collective-permute-start(f32[136,128]{1,0:T(8,128)S(1)} %get-tuple-element.79), channel_id=1, source_target_pairs={{1,0},{2,1},{3,2},{7,3},{6,7},{5,6},{4,5},{0,4},{9,8},{10,9},{11,1... | collective-permute-start | bytes 208904 | tf_op jit(solution)/shard_map/ppermute | solution.py:297
  21.8 5.3 %collective-permute-start.9 = (f32[9,32,128]{2,1,0:T(8,128)S(1)}, f32[9,32,128]{2,1,0:T(8,128)S(1)}, u32[]{:S(2)}, u32[]{:S(2)}) collective-permute-start(f32[9,32,128]{2,1,0:T(8,128)S(1)} %shard_map.53), channel_id=1, source_target_pairs={{0,16},{16,0},{1,17},{17,1},{2,18},{18,2},{3,19},{19,3},{4,20},{20... | collective-permute-start | bytes 442376 | tf_op jit(solution)/shard_map/ppermute | solution.py:301
  22.6 4.4 %collective-permute-start.11 = (f32[8,128]{1,0:T(8,128)S(1)}, f32[8,128]{1,0:T(8,128)S(1)}, u32[]{:S(2)}, u32[]{:S(2)}) collective-permute-start(f32[8,128]{1,0:T(8,128)S(1)} %get-tuple-element.87.refs_3_.refs_2_.refs_1_), channel_id=1, source_target_pairs={{4,0},{8,4},{12,8},{0,12},{5,1},{9,5},{13,9},{1,13},{6,2},{10,6},{... | collective-permute-start | bytes 12296 | tf_op jit(solution)/shard_map/ppermute | solution.py:311
  22.6 4.4 %collective-permute-start.10 = (f32[8,128]{1,0:T(8,128)S(1)}, f32[8,128]{1,0:T(8,128)S(1)}, u32[]{:S(2)}, u32[]{:S(2)}) collective-permute-start(f32[8,128]{1,0:T(8,128)S(1)} %get-tuple-element.87.refs_3_.refs_2_.refs_1_), channel_id=1, source_target_pairs={{0,4},{4,8},{8,12},{12,0},{1,5},{5,9},{9,13},{13,1},{2,6},{6,10},{... | collective-permute-start | bytes 12296 | tf_op jit(solution)/shard_map/ppermute | solution.py:311
  27.3 6.0 %collective-permute-start.16 = (f32[264,128]{1,0:T(8,128)S(1)}, f32[264,128]{1,0:T(8,128)S(1)}, u32[]{:S(2)}, u32[]{:S(2)}) collective-permute-start(f32[264,128]{1,0:T(8,128)S(1)} %get-tuple-element.94), channel_id=1, source_target_pairs={{4,0},{8,4},{12,8},{0,12},{5,1},{9,5},{13,9},{1,13},{6,2},{10,6},{... | collective-permute-start | bytes 405512 | tf_op jit(solution)/shard_map/ppermute | solution.py:311
  28.5 5.6 %collective-permute-start.15 = (f32[264,128]{1,0:T(8,128)S(1)}, f32[264,128]{1,0:T(8,128)S(1)}, u32[]{:S(2)}, u32[]{:S(2)}) collective-permute-start(f32[264,128]{1,0:T(8,128)S(1)} %get-tuple-element.93.refs_4_), channel_id=1, source_target_pairs={{0,4},{4,8},{8,12},{12,0},{1,5},{5,9},{9,13},{13,1},{2,6},{6,10},{... | collective-permute-start | bytes 405512 | tf_op jit(solution)/shard_map/ppermute | solution.py:311
  28.5 4.7 %collective-permute-start.14 = (f32[8,128]{1,0:T(8,128)S(1)}, f32[8,128]{1,0:T(8,128)S(1)}, u32[]{:S(2)}, u32[]{:S(2)}) collective-permute-start(f32[8,128]{1,0:T(8,128)S(1)} %shard_map.54.refs_3_.refs_2_), channel_id=1, source_target_pairs={{0,16},{16,0},{1,17},{17,1},{2,18},{18,2},{3,19},{19,3},{4,20},{20... | collective-permute-start | bytes 12296 | tf_op jit(solution)/shard_map/ppermute | solution.py:301
  34.6 6.1 %collective-permute-start.17 = (f32[88,128]{1,0:T(8,128)S(1)}, f32[88,128]{1,0:T(8,128)S(1)}, u32[]{:S(2)}, u32[]{:S(2)}) collective-permute-start(f32[88,128]{1,0:T(8,128)S(1)} %get-tuple-element.98), channel_id=1, source_target_pairs={{0,1},{1,2},{2,3},{3,7},{7,6},{6,5},{5,4},{4,0},{8,9},{9,10},{10,1... | collective-permute-start | bytes 135176 | tf_op jit(solution)/shard_map/ppermute | solution.py:297
  36.2 4.5 %collective-permute-start.18 = (f32[88,128]{1,0:T(8,128)S(1)}, f32[88,128]{1,0:T(8,128)S(1)}, u32[]{:S(2)}, u32[]{:S(2)}) collective-permute-start(f32[88,128]{1,0:T(8,128)S(1)} %get-tuple-element.99), channel_id=1, source_target_pairs={{1,0},{2,1},{3,2},{7,3},{6,7},{5,6},{4,5},{0,4},{9,8},{10,9},{11,1... | collective-permute-start | bytes 135176 | tf_op jit(solution)/shard_map/ppermute | solution.py:297
  40.9 4.8 %collective-permute-start.26 = (f32[8,128]{1,0:T(8,128)S(1)}, f32[8,128]{1,0:T(8,128)S(1)}, u32[]{:S(2)}, u32[]{:S(2)}) collective-permute-start(f32[8,128]{1,0:T(8,128)S(1)} %shard_map.61.refs_3_), channel_id=1, source_target_pairs={{4,0},{8,4},{12,8},{0,12},{5,1},{9,5},{13,9},{1,13},{6,2},{10,6},{... | collective-permute-start | bytes 12296 | tf_op jit(solution)/shard_map/ppermute | solution.py:311
  41.5 4.2 %collective-permute-start.25 = (f32[8,128]{1,0:T(8,128)S(1)}, f32[8,128]{1,0:T(8,128)S(1)}, u32[]{:S(2)}, u32[]{:S(2)}) collective-permute-start(f32[8,128]{1,0:T(8,128)S(1)} %shard_map.61.refs_3_), channel_id=1, source_target_pairs={{0,4},{4,8},{8,12},{12,0},{1,5},{5,9},{9,13},{13,1},{2,6},{6,10},{... | collective-permute-start | bytes 12296 | tf_op jit(solution)/shard_map/ppermute | solution.py:311
  41.5 4.2 %collective-permute-start.24 = (f32[8,128]{1,0:T(8,128)S(1)}, f32[8,128]{1,0:T(8,128)S(1)}, u32[]{:S(2)}, u32[]{:S(2)}) collective-permute-start(f32[8,128]{1,0:T(8,128)S(1)} %shard_map.61.refs_3_), channel_id=1, source_target_pairs={{0,16},{16,0},{1,17},{17,1},{2,18},{18,2},{3,19},{19,3},{4,20},{20... | collective-permute-start | bytes 12296 | tf_op jit(solution)/shard_map/ppermute | solution.py:301
  46.3 5.6 %collective-permute-start.31 = (f32[8,128]{1,0:T(8,128)S(1)}, f32[8,128]{1,0:T(8,128)S(1)}, u32[]{:S(2)}, u32[]{:S(2)}) collective-permute-start(f32[8,128]{1,0:T(8,128)S(1)} %shard_map.63.refs_3_), channel_id=1, source_target_pairs={{4,0},{8,4},{12,8},{0,12},{5,1},{9,5},{13,9},{1,13},{6,2},{10,6},{... | collective-permute-start | bytes 12296 | tf_op jit(solution)/shard_map/ppermute | solution.py:311
  48.0 4.0 %collective-permute-start.29 = (f32[8,128]{1,0:T(8,128)S(1)}, f32[8,128]{1,0:T(8,128)S(1)}, u32[]{:S(2)}, u32[]{:S(2)}) collective-permute-start(f32[8,128]{1,0:T(8,128)S(1)} %shard_map.63.refs_3_), channel_id=1, source_target_pairs={{0,16},{16,0},{1,17},{17,1},{2,18},{18,2},{3,19},{19,3},{4,20},{20... | collective-permute-start | bytes 12296 | tf_op jit(solution)/shard_map/ppermute | solution.py:301
  52.5 5.9 %collective-permute-start.36 = (f32[8,128]{1,0:T(8,128)S(1)}, f32[8,128]{1,0:T(8,128)S(1)}, u32[]{:S(2)}, u32[]{:S(2)}) collective-permute-start(f32[8,128]{1,0:T(8,128)S(1)} %shard_map.65.refs_3_), channel_id=1, source_target_pairs={{4,0},{8,4},{12,8},{0,12},{5,1},{9,5},{13,9},{1,13},{6,2},{10,6},{... | collective-permute-start | bytes 12296 | tf_op jit(solution)/shard_map/ppermute | solution.py:311
  53.9 4.5 %collective-permute-start.35 = (f32[8,128]{1,0:T(8,128)S(1)}, f32[8,128]{1,0:T(8,128)S(1)}, u32[]{:S(2)}, u32[]{:S(2)}) collective-permute-start(f32[8,128]{1,0:T(8,128)S(1)} %shard_map.65.refs_3_), channel_id=1, source_target_pairs={{0,4},{4,8},{8,12},{12,0},{1,5},{5,9},{9,13},{13,1},{2,6},{6,10},{... | collective-permute-start | bytes 12296 | tf_op jit(solution)/shard_map/ppermute | solution.py:311
  53.9 4.5 %collective-permute-start.34 = (f32[8,128]{1,0:T(8,128)S(1)}, f32[8,128]{1,0:T(8,128)S(1)}, u32[]{:S(2)}, u32[]{:S(2)}) collective-permute-start(f32[8,128]{1,0:T(8,128)S(1)} %shard_map.65.refs_3_), channel_id=1, source_target_pairs={{0,16},{16,0},{1,17},{17,1},{2,18},{18,2},{3,19},{19,3},{4,20},{20... | collective-permute-start | bytes 12296 | tf_op jit(solution)/shard_map/ppermute | solution.py:301
  59.0 5.1 %collective-permute-start.41 = (f32[8,128]{1,0:T(8,128)S(1)}, f32[8,128]{1,0:T(8,128)S(1)}, u32[]{:S(2)}, u32[]{:S(2)}) collective-permute-start(f32[8,128]{1,0:T(8,128)S(1)} %shard_map.67.refs_3_), channel_id=1, source_target_pairs={{4,0},{8,4},{12,8},{0,12},{5,1},{9,5},{13,9},{1,13},{6,2},{10,6},{... | collective-permute-start | bytes 12296 | tf_op jit(solution)/shard_map/ppermute | solution.py:311
  (23 other events, 74.0 us)

commit v16 on v15

--- a/solution.py
+++ b/solution.py
@@ -635,8 +635,7 @@
     out[rows, AGG:] = (tile - high.astype(F32)).astype(BF16)
 
 
-def blocks_kernel(flags, cond, absorb, block_agg, _, block_label, near, weights, inner, face_label, fine_label,
-                  part, line):
+def blocks_kernel(flags, cond, absorb, block_agg, _, block_label, near, weights, inner, part):
     nx, ny = cond.shape[0], cond.shape[1]
     nb, half, width = nx // 2, ny // 2, LANES // 2
     lane, row = lane_no((half, LANES)), row_no((half, LANES))
@@ -680,21 +679,27 @@
                 near[d, b], weights[d, b] = pack_rows(beside).astype(jnp.int32), pack_rows(leaving)
             block_label[b] = pack_rows(own)
             inner[b] = pack_rows(total)
-            spread = picked(own, lane // 2)
-            for a in range(2):
-                for c in range(2):
-                    fine_label[x + a, pl.ds(c, half, stride=2)] = spread
             low_x = high_x
         return carry
 
     batched(0, nb, step, 0, 4)
+
+
+def labels_kernel(flags, block_agg, block_label, _, face_label, fine_label, line):
+    nb, half, width = block_agg.shape
+    lane = lane_no((half, LANES))
     line[...] = jnp.zeros(line.shape, F32)
     low, high = jnp.zeros((half, LANES), F32), jnp.zeros((half, LANES), F32)
     for b in range(nb):
-        own = label_at(b)
+        own = block_agg[b].astype(F32)
+        own = jnp.concatenate([own, own], axis=1)
         line[0, b : b + 1], line[1, b : b + 1] = own[:1], own[half - 1 :]
         low = jnp.where(lane == b, own[:, :1], low)
         high = jnp.where(lane == b, own[:, width - 1 : width], high)
+        spread = picked(own, lane // 2)
+        for a in range(2):
+            for c in range(2):
+                fine_label[2 * b + a, pl.ds(c, half, stride=2)] = spread
     face_label[0], face_label[1] = block_label[0], block_label[nb - 1]
     for s in range(2):
         face_label[2 + s, : nb // 2] = pack_rows(line[s, :nb])
@@ -885,9 +890,7 @@
     from_corners = links.corners(sends[n_send + 2 :])
     blocks = (nb, SUB, LANES)
     outs = [shaped(*blocks), jax.ShapeDtypeStruct((6, *blocks), jnp.int32), shaped(6, *blocks), shaped(*blocks)]
-    outs += [shaped(6, SUB, LANES), shaped(nx, ny, nz)]
-    scratch = [pltpu.VMEM((17, ny, LANES), F32), pltpu.VMEM((2, ny // 2, LANES), F32)]
-    *rows, inner, face_label, fine_label = call(blocks_kernel, outs, scratch)(
+    *rows, inner = call(blocks_kernel, outs, [pltpu.VMEM((17, ny, LANES), F32)])(
         arrays[0], arrays[2], arrays[3], sends[0]
     )
     got = lax.optimization_barrier((*from_x, *from_y, *from_corners, inner))
@@ -899,6 +902,10 @@
         [shaped(len(WIDTHS), *frame.main)] + [shaped(size + ny // 2, nz)] * 2,
         [pltpu.VMEM((size, nz), F32)] * 2,
     )(*arrays, from_x[0], from_x[-1], *from_y, *from_corners)
+    outs = [shaped(6, SUB, LANES), shaped(nx, ny, nz)]
+    face_label, fine_label = call(labels_kernel, outs, [pltpu.VMEM((2, ny // 2, LANES), F32)])(
+        arrays[3], block_label, sends[0]
+    )
     outs = [shaped(*frame.main)] * 4 + [shaped(frame.tall, nz), shaped(4, SUB, LANES), shaped(SUB, AGG)]
     *fields, weight_xy, some_diag = call(functools.partial(fields_kernel, n_x), outs, limit=24)(
         wide, block_label, inner, face_label

time: 80 us -> 80.4 us (level)
  waiting for transfers between devices: 11.7 us -> 12.7 us
    ppermute x9, waiting for transfers between devices: 2.66 us -> 4.45 us  [x(): return (lax.ppermute(sends[0], 'gx', self.ring_x),)]
    ppermute x20, waiting for transfers between devices: 4.6 us -> 3.27 us  [send(): return lax.ppermute(values, ('gx', 'gy', 'gz'), pairs)]
    ppermute x9, starting transfers between devices: 11.2 us -> 10.4 us  [x(): return (lax.ppermute(sends[0], 'gx', self.ring_x),)]
    pallas_call x29 -> x30, Pallas kernels: 26.4 us -> 26.3 us  [run(): pl.pallas_call(placed, out_shape=outs, in_specs=in_specs or [VMEM] * len(...]
  transfers between devices with their start and end apart: 47 -> 47, of which waited for: 12 -> 14; matrix products, arithmetic and copies ran while one was open for 0% -> 0% of each run, Pallas kernels for 17% -> 17%
where the time goes in v16:
time: 80.4 us; the launch traced here: 80.3 us
  starting transfers between devices  41 us (51%)
  Pallas kernels  26.3 us (33%)
  waiting for transfers between devices  12.7 us (16%)
    pallas_call x30, Pallas kernels, run(): pl.pallas_call(placed, out_shape=outs, in_specs=in_specs or [VMEM] * len(...  26.3 us
    ppermute x20, starting transfers between devices, send(): return lax.ppermute(values, ('gx', 'gy', 'gz'), pairs)  20.5 us
    ppermute x9, starting transfers between devices, x(): return (lax.ppermute(sends[0], 'gx', self.ring_x),)  10.4 us
    ppermute x9, starting transfers between devices, ring_y(): lax.ppermute(to_low, 'gy', self.back(ring))  9.19 us
    ppermute x9, waiting for transfers between devices, x(): return (lax.ppermute(sends[0], 'gx', self.ring_x),)  4.45 us
    ppermute x9, waiting for transfers between devices, ring_y(): lax.ppermute(to_high, 'gy', ring)  4.11 us
    ppermute x20, waiting for transfers between devices, send(): return lax.ppermute(values, ('gx', 'gy', 'gz'), pairs)  3.27 us
  transfers between devices with their start and end apart: 47, of which 14 were waited for; matrix products, arithmetic and copies ran while one was open for 0% of the time, Pallas kernels for 17%

profile of v16, /device:TPU:0, one launch (start us, length us, event | category | flops | bytes accessed | tf_op | source)
XLA Modules:
  0.0 80.3 jit_solution(8475469722051859060)
XLA Ops:
  0.0 1.5 %shard_map.46 = (f32[24,32,128]{2,1,0:T(8,128)S(1)}, f32[24,32,128]{2,1,0:T(8,128)S(1)}, f32[24,32,128]{2,1,0:T(8,128)S(1)}, s32[12,16,64]{2,1,0:T(8,128)S(1)}, ...) custom-call(f32[24,32,128]{2,1,0:T(8,128)} %refs_0_.1, ...), custom_call_target="tpu_custom_call" | custom-call | flops 1000000 | bytes 100000 | tf_op jit(solution)/shard_map/pallas_call | solution.py:36
  1.5 3.0 %collective-permute-start = (f32[11,32,128]{2,1,0:T(8,128)S(1)}, f32[11,32,128]{2,1,0:T(8,128)S(1)}, u32[]{:S(2)}, u32[]{:S(2)}) collective-permute-start(f32[11,32,128]{2,1,0:T(8,128)S(1)} %get-tuple-element.61.refs_3_), channel_id=1, source_target_pairs={{0,16},{16,0},{1,17},{17,1},{2,18},{18,2},{3,19},{19,3},{4,20},{20... | collective-permute-start | bytes 540680 | tf_op jit(solution)/shard_map/ppermute | solution.py:301
  4.5 1.7 %collective-permute-start.2 = (f32[256,128]{1,0:T(8,128)S(1)}, f32[256,128]{1,0:T(8,128)S(1)}, u32[]{:S(2)}, u32[]{:S(2)}) collective-permute-start(f32[256,128]{1,0:T(8,128)S(1)} %get-tuple-element.65), channel_id=1, source_target_pairs={{4,0},{8,4},{12,8},{0,12},{5,1},{9,5},{13,9},{1,13},{6,2},{10,6},{... | collective-permute-start | bytes 393224 | tf_op jit(solution)/shard_map/ppermute | solution.py:311
  6.3 2.6 %collective-permute-start.4 = (f32[40,128]{1,0:T(8,128)S(1)}, f32[40,128]{1,0:T(8,128)S(1)}, u32[]{:S(2)}, u32[]{:S(2)}) collective-permute-start(f32[40,128]{1,0:T(8,128)S(1)} %get-tuple-element.67), channel_id=1, source_target_pairs={{20,0},{21,1},{22,2},{23,3},{24,4},{25,5},{26,6},{27,7},{28,8},{29... | collective-permute-start | bytes 61448 | tf_op jit(solution)/shard_map/ppermute | solution.py:297
  8.9 1.4 %shard_map.47 = (f32[12,8,128]{2,1,0:T(8,128)S(1)}, s32[6,12,8,128]{3,2,1,0:T(8,128)S(1)}, f32[6,12,8,128]{3,2,1,0:T(8,128)S(1)}, f32[12,8,128]{2,1,0:T(8,128)S(1)}) custom-call(f32[24,32,128]{2,1,0:T(8,128)S(1)} %get-tuple-element.59.refs_0_, f32[24,32,128]{2,1,0:T(8,128)S(1)} %get-tuple-element.60.refs_1_.refs_2_, ...), custom_call_target="tpu_custom_call" | custom-call | flops 1000000 | bytes 100000 | tf_op jit(solution)/shard_map/pallas_call | solution.py:36
  11.9 1.2 %collective-permute-start.6 = (f32[136,128]{1,0:T(8,128)S(1)}, f32[136,128]{1,0:T(8,128)S(1)}, u32[]{:S(2)}, u32[]{:S(2)}) collective-permute-start(f32[136,128]{1,0:T(8,128)S(1)} %get-tuple-element.79), channel_id=1, source_target_pairs={{1,0},{2,1},{3,2},{7,3},{6,7},{5,6},{4,5},{0,4},{9,8},{10,9},{11,1... | collective-permute-start | bytes 208904 | tf_op jit(solution)/shard_map/ppermute | solution.py:297
  14.3 2.5 %shard_map.50 = (f32[32,56,128]{2,1,0:T(8,128)S(1)}, f32[32,56,128]{2,1,0:T(8,128)S(1)}, f32[32,56,128]{2,1,0:T(8,128)S(1)}, f32[32,56,128]{2,1,0:T(8,128)S(1)},...) custom-call(f32[3,32,56,128]{3,2,1,0:T(8,128)S(1)} %get-tuple-element.76.refs_0_, ...), custom_call_target="tpu_custom_call" | custom-call | flops 1000000 | bytes 100000 | tf_op jit(solution)/shard_map/pallas_call | solution.py:36
  16.8 3.9 %shard_map.51 = (f32[32,56,128]{2,1,0:T(8,128)S(1)}, f32[32,56,128]{2,1,0:T(8,128)S(1)}, f32[2,56,128]{2,1,0:T(8,128)S(1)}, f32[2,56,128]{2,1,0:T(8,128)S(1)}, f...) custom-call(f32[3,32,56,128]{3,2,1,0:T(8,128)S(1)} %get-tuple-elemen, ...), custom_call_target="tpu_custom_call" | custom-call | flops 1000000 | bytes 100000 | tf_op jit(solution)/shard_map/pallas_call | solution.py:36
  21.5 1.4 %collective-permute-start.11 = (f32[8,128]{1,0:T(8,128)S(1)}, f32[8,128]{1,0:T(8,128)S(1)}, u32[]{:S(2)}, u32[]{:S(2)}) collective-permute-start(f32[8,128]{1,0:T(8,128)S(1)} %get-tuple-element.87.refs_3_.refs_2_.refs_1_), channel_id=1, source_target_pairs={{4,0},{8,4},{12,8},{0,12},{5,1},{9,5},{13,9},{1,13},{6,2},{10,6},{... | collective-permute-start | bytes 12296 | tf_op jit(solution)/shard_map/ppermute | solution.py:311
  22.8 1.6 %collective-permute-start.8 = (f32[8,128]{1,0:T(8,128)S(1)}, f32[8,128]{1,0:T(8,128)S(1)}, u32[]{:S(2)}, u32[]{:S(2)}) collective-permute-start(f32[8,128]{1,0:T(8,128)S(1)} %get-tuple-element.87.refs_3_.refs_2_.refs_1_), channel_id=1, source_target_pairs={{1,0},{2,1},{3,2},{7,3},{6,7},{5,6},{4,5},{0,4},{9,8},{10,9},{11,1... | collective-permute-start | bytes 12296 | tf_op jit(solution)/shard_map/ppermute | solution.py:297
  29.3 1.2 %collective-permute-start.13 = (f32[8,128]{1,0:T(8,128)S(1)}, f32[8,128]{1,0:T(8,128)S(1)}, u32[]{:S(2)}, u32[]{:S(2)}) collective-permute-start(f32[8,128]{1,0:T(8,128)S(1)} %shard_map.55.refs_3_.refs_2_), channel_id=1, source_target_pairs={{1,0},{2,1},{3,2},{7,3},{6,7},{5,6},{4,5},{0,4},{9,8},{10,9},{11,1... | collective-permute-start | bytes 12296 | tf_op jit(solution)/shard_map/ppermute | solution.py:297
  32.9 1.5 %collective-permute-done.15.refs_8_.refs_3_ = f32[264,128]{1,0:T(8,128)S(1)} collective-permute-done((f32[264,128]{1,0:T(8,128)S(1)}, f32[264,128]{1,0:T(8,128)S(1)}, u32[]{:S(2)}, u32[]{:S(2)}) %collective-permute-start.15) | collective-permute-done | bytes 135200 | tf_op jit(solution)/shard_map/ppermute | solution.py:311
  34.9 1.6 %collective-permute-start.17 = (f32[88,128]{1,0:T(8,128)S(1)}, f32[88,128]{1,0:T(8,128)S(1)}, u32[]{:S(2)}, u32[]{:S(2)}) collective-permute-start(f32[88,128]{1,0:T(8,128)S(1)} %get-tuple-element.98), channel_id=1, source_target_pairs={{0,1},{1,2},{2,3},{3,7},{7,6},{6,5},{5,4},{4,0},{8,9},{9,10},{10,1... | collective-permute-start | bytes 135176 | tf_op jit(solution)/shard_map/ppermute | solution.py:297
  42.3 1.3 %collective-permute-start.23 = (f32[8,128]{1,0:T(8,128)S(1)}, f32[8,128]{1,0:T(8,128)S(1)}, u32[]{:S(2)}, u32[]{:S(2)}) collective-permute-start(f32[8,128]{1,0:T(8,128)S(1)} %shard_map.62.refs_3_), channel_id=1, source_target_pairs={{1,0},{2,1},{3,2},{7,3},{6,7},{5,6},{4,5},{0,4},{9,8},{10,9},{11,1... | collective-permute-start | bytes 12296 | tf_op jit(solution)/shard_map/ppermute | solution.py:297
  46.1 1.7 %collective-permute-start.31 = (f32[8,128]{1,0:T(8,128)S(1)}, f32[8,128]{1,0:T(8,128)S(1)}, u32[]{:S(2)}, u32[]{:S(2)}) collective-permute-start(f32[8,128]{1,0:T(8,128)S(1)} %shard_map.64.refs_3_), channel_id=1, source_target_pairs={{4,0},{8,4},{12,8},{0,12},{5,1},{9,5},{13,9},{1,13},{6,2},{10,6},{... | collective-permute-start | bytes 12296 | tf_op jit(solution)/shard_map/ppermute | solution.py:311
  47.7 1.4 %collective-permute-start.29 = (f32[8,128]{1,0:T(8,128)S(1)}, f32[8,128]{1,0:T(8,128)S(1)}, u32[]{:S(2)}, u32[]{:S(2)}) collective-permute-start(f32[8,128]{1,0:T(8,128)S(1)} %shard_map.64.refs_3_), channel_id=1, source_target_pairs={{0,16},{16,0},{1,17},{17,1},{2,18},{18,2},{3,19},{19,3},{4,20},{20... | collective-permute-start | bytes 12296 | tf_op jit(solution)/shard_map/ppermute | solution.py:301
  49.8 1.3 %collective-permute-start.27 = (f32[8,128]{1,0:T(8,128)S(1)}, f32[8,128]{1,0:T(8,128)S(1)}, u32[]{:S(2)}, u32[]{:S(2)}) collective-permute-start(f32[8,128]{1,0:T(8,128)S(1)} %shard_map.64.refs_3_), channel_id=1, source_target_pairs={{0,1},{1,2},{2,3},{3,7},{7,6},{6,5},{5,4},{4,0},{8,9},{9,10},{10,1... | collective-permute-start | bytes 12296 | tf_op jit(solution)/shard_map/ppermute | solution.py:297
  52.9 1.6 %collective-permute-start.36 = (f32[8,128]{1,0:T(8,128)S(1)}, f32[8,128]{1,0:T(8,128)S(1)}, u32[]{:S(2)}, u32[]{:S(2)}) collective-permute-start(f32[8,128]{1,0:T(8,128)S(1)} %shard_map.66.refs_3_), channel_id=1, source_target_pairs={{4,0},{8,4},{12,8},{0,12},{5,1},{9,5},{13,9},{1,13},{6,2},{10,6},{... | collective-permute-start | bytes 12296 | tf_op jit(solution)/shard_map/ppermute | solution.py:311
  60.0 1.5 %collective-permute-start.39 = (f32[8,128]{1,0:T(8,128)S(1)}, f32[8,128]{1,0:T(8,128)S(1)}, u32[]{:S(2)}, u32[]{:S(2)}) collective-permute-start(f32[8,128]{1,0:T(8,128)S(1)} %shard_map.68.refs_3_), channel_id=1, source_target_pairs={{0,16},{16,0},{1,17},{17,1},{2,18},{18,2},{3,19},{19,3},{4,20},{20... | collective-permute-start | bytes 12296 | tf_op jit(solution)/shard_map/ppermute | solution.py:301
  62.0 1.5 %collective-permute-start.37 = (f32[8,128]{1,0:T(8,128)S(1)}, f32[8,128]{1,0:T(8,128)S(1)}, u32[]{:S(2)}, u32[]{:S(2)}) collective-permute-start(f32[8,128]{1,0:T(8,128)S(1)} %shard_map.68.refs_3_), channel_id=1, source_target_pairs={{0,1},{1,2},{2,3},{3,7},{7,6},{6,5},{5,4},{4,0},{8,9},{9,10},{10,1... | collective-permute-start | bytes 12296 | tf_op jit(solution)/shard_map/ppermute | solution.py:297
  65.9 3.1 %collective-permute-done.42.refs_0_.refs_2_ = f32[8,128]{1,0:T(8,128)S(1)} collective-permute-done((f32[8,128]{1,0:T(8,128)S(1)}, f32[8,128]{1,0:T(8,128)S(1)}, u32[]{:S(2)}, u32[]{:S(2)}) %collective-permute-start.42) | collective-permute-done | bytes 4128 | tf_op jit(solution)/shard_map/ppermute | solution.py:301
  70.3 1.8 %collective-permute-done.43.refs_0_ = f32[8,128]{1,0:T(8,128)S(1)} collective-permute-done((f32[8,128]{1,0:T(8,128)S(1)}, f32[8,128]{1,0:T(8,128)S(1)}, u32[]{:S(2)}, u32[]{:S(2)}) %collective-permute-start.43) | collective-permute-done | bytes 4128 | tf_op jit(solution)/shard_map/ppermute | solution.py:311
  72.1 2.0 %collective-permute-start.45 = (f32[16,128]{1,0:T(8,128)S(1)}, f32[16,128]{1,0:T(8,128)S(1)}, u32[]{:S(2)}, u32[]{:S(2)}) collective-permute-start(f32[16,128]{1,0:T(8,128)S(1)} %shard_map.72.refs_0_), channel_id=1, source_target_pairs={{0,1},{1,2},{2,3},{3,7},{7,6},{6,5},{5,4},{4,0},{8,9},{9,10},{10,1... | collective-permute-start | bytes 24584 | tf_op jit(solution)/shard_map/ppermute | solution.py:297
  75.7 4.5 %shard_map.75 = f32[24,32,128]{2,1,0:T(8,128)} custom-call(f32[32,56,128]{2,1,0:T(8,128)S(1)} %shard_map.74.refs_0_, f32[16,128]{1,0:T(8,128)S(1)} %collective-permute-done.45.refs_1_, f32[16,128]{1,0:T(8,128)S(1)} %collective-permute-done.46.refs_2_, s32[2,40,128]{2,1,0:T(8,128)S(1)} %get-tuple-element.102.refs_3_, ...), custom_call_target="tpu_custom_call" | custom-call | flops 1000000 | bytes 100000 | tf_op jit(solution)/shard_map/pallas_call | solution.py:36
  (100 shorter events, 32.9 us)
Async XLA Ops:
  1.5 9.3 %collective-permute-start = (f32[11,32,128]{2,1,0:T(8,128)S(1)}, f32[11,32,128]{2,1,0:T(8,128)S(1)}, u32[]{:S(2)}, u32[]{:S(2)}) collective-permute-start(f32[11,32,128]{2,1,0:T(8,128)S(1)} %get-tuple-element.61.refs_3_), channel_id=1, source_target_pairs={{0,16},{16,0},{1,17},{17,1},{2,18},{18,2},{3,19},{19,3},{4,20},{20... | collective-permute-start | bytes 540680 | tf_op jit(solution)/shard_map/ppermute | solution.py:301
  4.5 6.3 %collective-permute-start.1 = (f32[256,128]{1,0:T(8,128)S(1)}, f32[256,128]{1,0:T(8,128)S(1)}, u32[]{:S(2)}, u32[]{:S(2)}) collective-permute-start(f32[256,128]{1,0:T(8,128)S(1)} %get-tuple-element.64), channel_id=1, source_target_pairs={{0,4},{4,8},{8,12},{12,0},{1,5},{5,9},{9,13},{13,1},{2,6},{6,10},{... | collective-permute-start | bytes 393224 | tf_op jit(solution)/shard_map/ppermute | solution.py:311
  4.5 6.3 %collective-permute-start.2 = (f32[256,128]{1,0:T(8,128)S(1)}, f32[256,128]{1,0:T(8,128)S(1)}, u32[]{:S(2)}, u32[]{:S(2)}) collective-permute-start(f32[256,128]{1,0:T(8,128)S(1)} %get-tuple-element.65), channel_id=1, source_target_pairs={{4,0},{8,4},{12,8},{0,12},{5,1},{9,5},{13,9},{1,13},{6,2},{10,6},{... | collective-permute-start | bytes 393224 | tf_op jit(solution)/shard_map/ppermute | solution.py:311
  6.3 4.4 %collective-permute-start.3 = (f32[40,128]{1,0:T(8,128)S(1)}, f32[40,128]{1,0:T(8,128)S(1)}, u32[]{:S(2)}, u32[]{:S(2)}) collective-permute-start(f32[40,128]{1,0:T(8,128)S(1)} %get-tuple-element.66), channel_id=1, source_target_pairs={{0,20},{1,21},{2,22},{3,23},{4,24},{5,25},{6,26},{7,27},{8,28},{9,... | collective-permute-start | bytes 61448 | tf_op jit(solution)/shard_map/ppermute | solution.py:297
  6.3 4.5 %collective-permute-start.4 = (f32[40,128]{1,0:T(8,128)S(1)}, f32[40,128]{1,0:T(8,128)S(1)}, u32[]{:S(2)}, u32[]{:S(2)}) collective-permute-start(f32[40,128]{1,0:T(8,128)S(1)} %get-tuple-element.67), channel_id=1, source_target_pairs={{20,0},{21,1},{22,2},{23,3},{24,4},{25,5},{26,6},{27,7},{28,8},{29... | collective-permute-start | bytes 61448 | tf_op jit(solution)/shard_map/ppermute | solution.py:297
  11.9 4.9 %collective-permute-start.6 = (f32[136,128]{1,0:T(8,128)S(1)}, f32[136,128]{1,0:T(8,128)S(1)}, u32[]{:S(2)}, u32[]{:S(2)}) collective-permute-start(f32[136,128]{1,0:T(8,128)S(1)} %get-tuple-element.79), channel_id=1, source_target_pairs={{1,0},{2,1},{3,2},{7,3},{6,7},{5,6},{4,5},{0,4},{9,8},{10,9},{11,1... | collective-permute-start | bytes 208904 | tf_op jit(solution)/shard_map/ppermute | solution.py:297
  20.7 6.5 %collective-permute-start.9 = (f32[9,32,128]{2,1,0:T(8,128)S(1)}, f32[9,32,128]{2,1,0:T(8,128)S(1)}, u32[]{:S(2)}, u32[]{:S(2)}) collective-permute-start(f32[9,32,128]{2,1,0:T(8,128)S(1)} %shard_map.54), channel_id=1, source_target_pairs={{0,16},{16,0},{1,17},{17,1},{2,18},{18,2},{3,19},{19,3},{4,20},{20... | collective-permute-start | bytes 442376 | tf_op jit(solution)/shard_map/ppermute | solution.py:301
  21.5 5.2 %collective-permute-start.11 = (f32[8,128]{1,0:T(8,128)S(1)}, f32[8,128]{1,0:T(8,128)S(1)}, u32[]{:S(2)}, u32[]{:S(2)}) collective-permute-start(f32[8,128]{1,0:T(8,128)S(1)} %get-tuple-element.87.refs_3_.refs_2_.refs_1_), channel_id=1, source_target_pairs={{4,0},{8,4},{12,8},{0,12},{5,1},{9,5},{13,9},{1,13},{6,2},{10,6},{... | collective-permute-start | bytes 12296 | tf_op jit(solution)/shard_map/ppermute | solution.py:311
  22.8 3.9 %collective-permute-start.8 = (f32[8,128]{1,0:T(8,128)S(1)}, f32[8,128]{1,0:T(8,128)S(1)}, u32[]{:S(2)}, u32[]{:S(2)}) collective-permute-start(f32[8,128]{1,0:T(8,128)S(1)} %get-tuple-element.87.refs_3_.refs_2_.refs_1_), channel_id=1, source_target_pairs={{1,0},{2,1},{3,2},{7,3},{6,7},{5,6},{4,5},{0,4},{9,8},{10,9},{11,1... | collective-permute-start | bytes 12296 | tf_op jit(solution)/shard_map/ppermute | solution.py:297
  27.5 5.4 %collective-permute-start.16 = (f32[264,128]{1,0:T(8,128)S(1)}, f32[264,128]{1,0:T(8,128)S(1)}, u32[]{:S(2)}, u32[]{:S(2)}) collective-permute-start(f32[264,128]{1,0:T(8,128)S(1)} %get-tuple-element.94), channel_id=1, source_target_pairs={{4,0},{8,4},{12,8},{0,12},{5,1},{9,5},{13,9},{1,13},{6,2},{10,6},{... | collective-permute-start | bytes 405512 | tf_op jit(solution)/shard_map/ppermute | solution.py:311
  28.6 5.8 %collective-permute-start.15 = (f32[264,128]{1,0:T(8,128)S(1)}, f32[264,128]{1,0:T(8,128)S(1)}, u32[]{:S(2)}, u32[]{:S(2)}) collective-permute-start(f32[264,128]{1,0:T(8,128)S(1)} %get-tuple-element.93.refs_4_), channel_id=1, source_target_pairs={{0,4},{4,8},{8,12},{12,0},{1,5},{5,9},{9,13},{13,1},{2,6},{6,10},{... | collective-permute-start | bytes 405512 | tf_op jit(solution)/shard_map/ppermute | solution.py:311
  28.6 4.2 %collective-permute-start.14 = (f32[8,128]{1,0:T(8,128)S(1)}, f32[8,128]{1,0:T(8,128)S(1)}, u32[]{:S(2)}, u32[]{:S(2)}) collective-permute-start(f32[8,128]{1,0:T(8,128)S(1)} %shard_map.55.refs_3_.refs_2_), channel_id=1, source_target_pairs={{0,16},{16,0},{1,17},{17,1},{2,18},{18,2},{3,19},{19,3},{4,20},{20... | collective-permute-start | bytes 12296 | tf_op jit(solution)/shard_map/ppermute | solution.py:301
  34.9 5.7 %collective-permute-start.17 = (f32[88,128]{1,0:T(8,128)S(1)}, f32[88,128]{1,0:T(8,128)S(1)}, u32[]{:S(2)}, u32[]{:S(2)}) collective-permute-start(f32[88,128]{1,0:T(8,128)S(1)} %get-tuple-element.98), channel_id=1, source_target_pairs={{0,1},{1,2},{2,3},{3,7},{7,6},{6,5},{5,4},{4,0},{8,9},{9,10},{10,1... | collective-permute-start | bytes 135176 | tf_op jit(solution)/shard_map/ppermute | solution.py:297
  36.5 4.1 %collective-permute-start.18 = (f32[88,128]{1,0:T(8,128)S(1)}, f32[88,128]{1,0:T(8,128)S(1)}, u32[]{:S(2)}, u32[]{:S(2)}) collective-permute-start(f32[88,128]{1,0:T(8,128)S(1)} %get-tuple-element.99), channel_id=1, source_target_pairs={{1,0},{2,1},{3,2},{7,3},{6,7},{5,6},{4,5},{0,4},{9,8},{10,9},{11,1... | collective-permute-start | bytes 135176 | tf_op jit(solution)/shard_map/ppermute | solution.py:297
  40.8 4.7 %collective-permute-start.26 = (f32[8,128]{1,0:T(8,128)S(1)}, f32[8,128]{1,0:T(8,128)S(1)}, u32[]{:S(2)}, u32[]{:S(2)}) collective-permute-start(f32[8,128]{1,0:T(8,128)S(1)} %shard_map.62.refs_3_), channel_id=1, source_target_pairs={{4,0},{8,4},{12,8},{0,12},{5,1},{9,5},{13,9},{1,13},{6,2},{10,6},{... | collective-permute-start | bytes 12296 | tf_op jit(solution)/shard_map/ppermute | solution.py:311
  41.1 4.3 %collective-permute-start.25 = (f32[8,128]{1,0:T(8,128)S(1)}, f32[8,128]{1,0:T(8,128)S(1)}, u32[]{:S(2)}, u32[]{:S(2)}) collective-permute-start(f32[8,128]{1,0:T(8,128)S(1)} %shard_map.62.refs_3_), channel_id=1, source_target_pairs={{0,4},{4,8},{8,12},{12,0},{1,5},{5,9},{9,13},{13,1},{2,6},{6,10},{... | collective-permute-start | bytes 12296 | tf_op jit(solution)/shard_map/ppermute | solution.py:311
  41.3 4.2 %collective-permute-start.24 = (f32[8,128]{1,0:T(8,128)S(1)}, f32[8,128]{1,0:T(8,128)S(1)}, u32[]{:S(2)}, u32[]{:S(2)}) collective-permute-start(f32[8,128]{1,0:T(8,128)S(1)} %shard_map.62.refs_3_), channel_id=1, source_target_pairs={{0,16},{16,0},{1,17},{17,1},{2,18},{18,2},{3,19},{19,3},{4,20},{20... | collective-permute-start | bytes 12296 | tf_op jit(solution)/shard_map/ppermute | solution.py:301
  46.1 6.2 %collective-permute-start.31 = (f32[8,128]{1,0:T(8,128)S(1)}, f32[8,128]{1,0:T(8,128)S(1)}, u32[]{:S(2)}, u32[]{:S(2)}) collective-permute-start(f32[8,128]{1,0:T(8,128)S(1)} %shard_map.64.refs_3_), channel_id=1, source_target_pairs={{4,0},{8,4},{12,8},{0,12},{5,1},{9,5},{13,9},{1,13},{6,2},{10,6},{... | collective-permute-start | bytes 12296 | tf_op jit(solution)/shard_map/ppermute | solution.py:311
  47.7 4.6 %collective-permute-start.30 = (f32[8,128]{1,0:T(8,128)S(1)}, f32[8,128]{1,0:T(8,128)S(1)}, u32[]{:S(2)}, u32[]{:S(2)}) collective-permute-start(f32[8,128]{1,0:T(8,128)S(1)} %shard_map.64.refs_3_), channel_id=1, source_target_pairs={{0,4},{4,8},{8,12},{12,0},{1,5},{5,9},{9,13},{13,1},{2,6},{6,10},{... | collective-permute-start | bytes 12296 | tf_op jit(solution)/shard_map/ppermute | solution.py:311
  47.7 4.6 %collective-permute-start.29 = (f32[8,128]{1,0:T(8,128)S(1)}, f32[8,128]{1,0:T(8,128)S(1)}, u32[]{:S(2)}, u32[]{:S(2)}) collective-permute-start(f32[8,128]{1,0:T(8,128)S(1)} %shard_map.64.refs_3_), channel_id=1, source_target_pairs={{0,16},{16,0},{1,17},{17,1},{2,18},{18,2},{3,19},{19,3},{4,20},{20... | collective-permute-start | bytes 12296 | tf_op jit(solution)/shard_map/ppermute | solution.py:301
  52.9 5.5 %collective-permute-start.36 = (f32[8,128]{1,0:T(8,128)S(1)}, f32[8,128]{1,0:T(8,128)S(1)}, u32[]{:S(2)}, u32[]{:S(2)}) collective-permute-start(f32[8,128]{1,0:T(8,128)S(1)} %shard_map.66.refs_3_), channel_id=1, source_target_pairs={{4,0},{8,4},{12,8},{0,12},{5,1},{9,5},{13,9},{1,13},{6,2},{10,6},{... | collective-permute-start | bytes 12296 | tf_op jit(solution)/shard_map/ppermute | solution.py:311
  59.0 5.7 %collective-permute-start.41 = (f32[8,128]{1,0:T(8,128)S(1)}, f32[8,128]{1,0:T(8,128)S(1)}, u32[]{:S(2)}, u32[]{:S(2)}) collective-permute-start(f32[8,128]{1,0:T(8,128)S(1)} %shard_map.68.refs_3_), channel_id=1, source_target_pairs={{4,0},{8,4},{12,8},{0,12},{5,1},{9,5},{13,9},{1,13},{6,2},{10,6},{... | collective-permute-start | bytes 12296 | tf_op jit(solution)/shard_map/ppermute | solution.py:311
  60.0 4.7 %collective-permute-start.40 = (f32[8,128]{1,0:T(8,128)S(1)}, f32[8,128]{1,0:T(8,128)S(1)}, u32[]{:S(2)}, u32[]{:S(2)}) collective-permute-start(f32[8,128]{1,0:T(8,128)S(1)} %shard_map.68.refs_3_), channel_id=1, source_target_pairs={{0,4},{4,8},{8,12},{12,0},{1,5},{5,9},{9,13},{13,1},{2,6},{6,10},{... | collective-permute-start | bytes 12296 | tf_op jit(solution)/shard_map/ppermute | solution.py:311
  60.0 4.7 %collective-permute-start.39 = (f32[8,128]{1,0:T(8,128)S(1)}, f32[8,128]{1,0:T(8,128)S(1)}, u32[]{:S(2)}, u32[]{:S(2)}) collective-permute-start(f32[8,128]{1,0:T(8,128)S(1)} %shard_map.68.refs_3_), channel_id=1, source_target_pairs={{0,16},{16,0},{1,17},{17,1},{2,18},{18,2},{3,19},{19,3},{4,20},{20... | collective-permute-start | bytes 12296 | tf_op jit(solution)/shard_map/ppermute | solution.py:301
  (23 other events, 73.4 us)

commit v17 on v16

--- a/solution.py
+++ b/solution.py
@@ -482,7 +482,7 @@
         return before, edges
 
     nothing = jnp.zeros((tall, LANES), F32)
-    cond_edges[...] = batched(0, wide, fields, (nothing, nothing + 1.0), 4)[1]
+    cond_edges[...] = batched(0, wide, fields, (nothing, nothing + 1.0), 8)[1]
     nb, ny = frame.nx // 2, frame.ny
     for s, x in enumerate((HALO - 1, last - 1)):
         rows = [wx[x, pl.ds(frame.own + c, ny // 2, stride=2)] for c in range(2)]

time: 80.4 us -> 80.5 us (level)
    ppermute x9, starting transfers between devices: 9.19 us -> 10.7 us  [ring_y(): lax.ppermute(to_low, 'gy', self.back(ring))]
where the time goes in v17:
time: 80.5 us; the launch traced here: 80.4 us
  starting transfers between devices  41.6 us (52%)
  Pallas kernels  25.9 us (32%)
  waiting for transfers between devices  12.5 us (16%)
    pallas_call x30, Pallas kernels, run(): pl.pallas_call(placed, out_shape=outs, in_specs=in_specs or [VMEM] * len(...  25.9 us
    ppermute x20, starting transfers between devices, send(): return lax.ppermute(values, ('gx', 'gy', 'gz'), pairs)  20.5 us
    ppermute x9, starting transfers between devices, ring_y(): lax.ppermute(to_low, 'gy', self.back(ring))  10.7 us
    ppermute x9, starting transfers between devices, x(): return (lax.ppermute(sends[0], 'gx', self.ring_x),)  10 us
    ppermute x9, waiting for transfers between devices, ring_y(): lax.ppermute(to_high, 'gy', ring)  4.17 us
    ppermute x9, waiting for transfers between devices, x(): return (lax.ppermute(sends[0], 'gx', self.ring_x),)  3.73 us
    ppermute x20, waiting for transfers between devices, send(): return lax.ppermute(values, ('gx', 'gy', 'gz'), pairs)  3.27 us
  transfers between devices with their start and end apart: 47, of which 14 were waited for; matrix products, arithmetic and copies ran while one was open for 0% of the time, Pallas kernels for 17%

profile of v17, /device:TPU:0, one launch (start us, length us, event | category | flops | bytes accessed | tf_op | source)
XLA Modules:
  0.0 80.4 jit_solution(1754958858064083352)
XLA Ops:
  0.0 1.5 %shard_map.46 = (f32[24,32,128]{2,1,0:T(8,128)S(1)}, f32[24,32,128]{2,1,0:T(8,128)S(1)}, f32[24,32,128]{2,1,0:T(8,128)S(1)}, s32[12,16,64]{2,1,0:T(8,128)S(1)}, ...) custom-call(f32[24,32,128]{2,1,0:T(8,128)} %refs_0_.1, ...), custom_call_target="tpu_custom_call" | custom-call | flops 1000000 | bytes 100000 | tf_op jit(solution)/shard_map/pallas_call | solution.py:36
  1.5 3.0 %collective-permute-start = (f32[11,32,128]{2,1,0:T(8,128)S(1)}, f32[11,32,128]{2,1,0:T(8,128)S(1)}, u32[]{:S(2)}, u32[]{:S(2)}) collective-permute-start(f32[11,32,128]{2,1,0:T(8,128)S(1)} %get-tuple-element.61.refs_3_), channel_id=1, source_target_pairs={{0,16},{16,0},{1,17},{17,1},{2,18},{18,2},{3,19},{19,3},{4,20},{20... | collective-permute-start | bytes 540680 | tf_op jit(solution)/shard_map/ppermute | solution.py:301
  4.5 1.7 %collective-permute-start.2 = (f32[256,128]{1,0:T(8,128)S(1)}, f32[256,128]{1,0:T(8,128)S(1)}, u32[]{:S(2)}, u32[]{:S(2)}) collective-permute-start(f32[256,128]{1,0:T(8,128)S(1)} %get-tuple-element.65), channel_id=1, source_target_pairs={{4,0},{8,4},{12,8},{0,12},{5,1},{9,5},{13,9},{1,13},{6,2},{10,6},{... | collective-permute-start | bytes 393224 | tf_op jit(solution)/shard_map/ppermute | solution.py:311
  6.3 2.6 %collective-permute-start.4 = (f32[40,128]{1,0:T(8,128)S(1)}, f32[40,128]{1,0:T(8,128)S(1)}, u32[]{:S(2)}, u32[]{:S(2)}) collective-permute-start(f32[40,128]{1,0:T(8,128)S(1)} %get-tuple-element.67), channel_id=1, source_target_pairs={{20,0},{21,1},{22,2},{23,3},{24,4},{25,5},{26,6},{27,7},{28,8},{29... | collective-permute-start | bytes 61448 | tf_op jit(solution)/shard_map/ppermute | solution.py:297
  8.9 1.4 %shard_map.47 = (f32[12,8,128]{2,1,0:T(8,128)S(1)}, s32[6,12,8,128]{3,2,1,0:T(8,128)S(1)}, f32[6,12,8,128]{3,2,1,0:T(8,128)S(1)}, f32[12,8,128]{2,1,0:T(8,128)S(1)}) custom-call(f32[24,32,128]{2,1,0:T(8,128)S(1)} %get-tuple-element.59.refs_0_, f32[24,32,128]{2,1,0:T(8,128)S(1)} %get-tuple-element.60.refs_1_.refs_2_, ...), custom_call_target="tpu_custom_call" | custom-call | flops 1000000 | bytes 100000 | tf_op jit(solution)/shard_map/pallas_call | solution.py:36
  14.3 2.2 %shard_map.50 = (f32[32,56,128]{2,1,0:T(8,128)S(1)}, f32[32,56,128]{2,1,0:T(8,128)S(1)}, f32[32,56,128]{2,1,0:T(8,128)S(1)}, f32[32,56,128]{2,1,0:T(8,128)S(1)},...) custom-call(f32[3,32,56,128]{3,2,1,0:T(8,128)S(1)} %get-tuple-element.76.refs_0_, ...), custom_call_target="tpu_custom_call" | custom-call | flops 1000000 | bytes 100000 | tf_op jit(solution)/shard_map/pallas_call | solution.py:36
  16.4 3.9 %shard_map.51 = (f32[32,56,128]{2,1,0:T(8,128)S(1)}, f32[32,56,128]{2,1,0:T(8,128)S(1)}, f32[2,56,128]{2,1,0:T(8,128)S(1)}, f32[2,56,128]{2,1,0:T(8,128)S(1)}, f...) custom-call(f32[3,32,56,128]{3,2,1,0:T(8,128)S(1)} %get-tuple-elemen, ...), custom_call_target="tpu_custom_call" | custom-call | flops 1000000 | bytes 100000 | tf_op jit(solution)/shard_map/pallas_call | solution.py:36
  21.1 1.7 %collective-permute-start.11 = (f32[8,128]{1,0:T(8,128)S(1)}, f32[8,128]{1,0:T(8,128)S(1)}, u32[]{:S(2)}, u32[]{:S(2)}) collective-permute-start(f32[8,128]{1,0:T(8,128)S(1)} %get-tuple-element.87.refs_3_.refs_2_.refs_1_), channel_id=1, source_target_pairs={{4,0},{8,4},{12,8},{0,12},{5,1},{9,5},{13,9},{1,13},{6,2},{10,6},{... | collective-permute-start | bytes 12296 | tf_op jit(solution)/shard_map/ppermute | solution.py:311
  22.8 1.6 %collective-permute-start.8 = (f32[8,128]{1,0:T(8,128)S(1)}, f32[8,128]{1,0:T(8,128)S(1)}, u32[]{:S(2)}, u32[]{:S(2)}) collective-permute-start(f32[8,128]{1,0:T(8,128)S(1)} %get-tuple-element.87.refs_3_.refs_2_.refs_1_), channel_id=1, source_target_pairs={{1,0},{2,1},{3,2},{7,3},{6,7},{5,6},{4,5},{0,4},{9,8},{10,9},{11,1... | collective-permute-start | bytes 12296 | tf_op jit(solution)/shard_map/ppermute | solution.py:297
  27.2 1.4 %collective-permute-start.16 = (f32[264,128]{1,0:T(8,128)S(1)}, f32[264,128]{1,0:T(8,128)S(1)}, u32[]{:S(2)}, u32[]{:S(2)}) collective-permute-start(f32[264,128]{1,0:T(8,128)S(1)} %get-tuple-element.94), channel_id=1, source_target_pairs={{4,0},{8,4},{12,8},{0,12},{5,1},{9,5},{13,9},{1,13},{6,2},{10,6},{... | collective-permute-start | bytes 405512 | tf_op jit(solution)/shard_map/ppermute | solution.py:311
  29.1 1.4 %collective-permute-start.13 = (f32[8,128]{1,0:T(8,128)S(1)}, f32[8,128]{1,0:T(8,128)S(1)}, u32[]{:S(2)}, u32[]{:S(2)}) collective-permute-start(f32[8,128]{1,0:T(8,128)S(1)} %shard_map.55.refs_3_.refs_2_), channel_id=1, source_target_pairs={{1,0},{2,1},{3,2},{7,3},{6,7},{5,6},{4,5},{0,4},{9,8},{10,9},{11,1... | collective-permute-start | bytes 12296 | tf_op jit(solution)/shard_map/ppermute | solution.py:297
  32.8 1.7 %collective-permute-done.15.refs_8_.refs_3_ = f32[264,128]{1,0:T(8,128)S(1)} collective-permute-done((f32[264,128]{1,0:T(8,128)S(1)}, f32[264,128]{1,0:T(8,128)S(1)}, u32[]{:S(2)}, u32[]{:S(2)}) %collective-permute-start.15) | collective-permute-done | bytes 135200 | tf_op jit(solution)/shard_map/ppermute | solution.py:311
  34.9 1.6 %collective-permute-start.17 = (f32[88,128]{1,0:T(8,128)S(1)}, f32[88,128]{1,0:T(8,128)S(1)}, u32[]{:S(2)}, u32[]{:S(2)}) collective-permute-start(f32[88,128]{1,0:T(8,128)S(1)} %get-tuple-element.98), channel_id=1, source_target_pairs={{0,1},{1,2},{2,3},{3,7},{7,6},{6,5},{5,4},{4,0},{8,9},{9,10},{10,1... | collective-permute-start | bytes 135176 | tf_op jit(solution)/shard_map/ppermute | solution.py:297
  42.3 1.3 %collective-permute-start.23 = (f32[8,128]{1,0:T(8,128)S(1)}, f32[8,128]{1,0:T(8,128)S(1)}, u32[]{:S(2)}, u32[]{:S(2)}) collective-permute-start(f32[8,128]{1,0:T(8,128)S(1)} %shard_map.62.refs_3_), channel_id=1, source_target_pairs={{1,0},{2,1},{3,2},{7,3},{6,7},{5,6},{4,5},{0,4},{9,8},{10,9},{11,1... | collective-permute-start | bytes 12296 | tf_op jit(solution)/shard_map/ppermute | solution.py:297
  46.1 1.7 %collective-permute-start.31 = (f32[8,128]{1,0:T(8,128)S(1)}, f32[8,128]{1,0:T(8,128)S(1)}, u32[]{:S(2)}, u32[]{:S(2)}) collective-permute-start(f32[8,128]{1,0:T(8,128)S(1)} %shard_map.64.refs_3_), channel_id=1, source_target_pairs={{4,0},{8,4},{12,8},{0,12},{5,1},{9,5},{13,9},{1,13},{6,2},{10,6},{... | collective-permute-start | bytes 12296 | tf_op jit(solution)/shard_map/ppermute | solution.py:311
  47.7 1.4 %collective-permute-start.29 = (f32[8,128]{1,0:T(8,128)S(1)}, f32[8,128]{1,0:T(8,128)S(1)}, u32[]{:S(2)}, u32[]{:S(2)}) collective-permute-start(f32[8,128]{1,0:T(8,128)S(1)} %shard_map.64.refs_3_), channel_id=1, source_target_pairs={{0,16},{16,0},{1,17},{17,1},{2,18},{18,2},{3,19},{19,3},{4,20},{20... | collective-permute-start | bytes 12296 | tf_op jit(solution)/shard_map/ppermute | solution.py:301
  49.8 1.3 %collective-permute-start.27 = (f32[8,128]{1,0:T(8,128)S(1)}, f32[8,128]{1,0:T(8,128)S(1)}, u32[]{:S(2)}, u32[]{:S(2)}) collective-permute-start(f32[8,128]{1,0:T(8,128)S(1)} %shard_map.64.refs_3_), channel_id=1, source_target_pairs={{0,1},{1,2},{2,3},{3,7},{7,6},{6,5},{5,4},{4,0},{8,9},{9,10},{10,1... | collective-permute-start | bytes 12296 | tf_op jit(solution)/shard_map/ppermute | solution.py:297
  52.9 1.4 %collective-permute-start.36 = (f32[8,128]{1,0:T(8,128)S(1)}, f32[8,128]{1,0:T(8,128)S(1)}, u32[]{:S(2)}, u32[]{:S(2)}) collective-permute-start(f32[8,128]{1,0:T(8,128)S(1)} %shard_map.66.refs_3_), channel_id=1, source_target_pairs={{4,0},{8,4},{12,8},{0,12},{5,1},{9,5},{13,9},{1,13},{6,2},{10,6},{... | collective-permute-start | bytes 12296 | tf_op jit(solution)/shard_map/ppermute | solution.py:311
  58.5 1.5 %collective-permute-start.41 = (f32[8,128]{1,0:T(8,128)S(1)}, f32[8,128]{1,0:T(8,128)S(1)}, u32[]{:S(2)}, u32[]{:S(2)}) collective-permute-start(f32[8,128]{1,0:T(8,128)S(1)} %shard_map.68.refs_3_), channel_id=1, source_target_pairs={{4,0},{8,4},{12,8},{0,12},{5,1},{9,5},{13,9},{1,13},{6,2},{10,6},{... | collective-permute-start | bytes 12296 | tf_op jit(solution)/shard_map/ppermute | solution.py:311
  65.9 2.6 %collective-permute-done.42.refs_0_.refs_2_ = f32[8,128]{1,0:T(8,128)S(1)} collective-permute-done((f32[8,128]{1,0:T(8,128)S(1)}, f32[8,128]{1,0:T(8,128)S(1)}, u32[]{:S(2)}, u32[]{:S(2)}) %collective-permute-start.42) | collective-permute-done | bytes 4128 | tf_op jit(solution)/shard_map/ppermute | solution.py:301
  69.2 1.3 %collective-permute-done.44.refs_2_ = f32[8,128]{1,0:T(8,128)S(1)} collective-permute-done((f32[8,128]{1,0:T(8,128)S(1)}, f32[8,128]{1,0:T(8,128)S(1)}, u32[]{:S(2)}, u32[]{:S(2)}) %collective-permute-start.44) | collective-permute-done | bytes 4128 | tf_op jit(solution)/shard_map/ppermute | solution.py:311
  70.5 1.7 %collective-permute-done.43.refs_0_ = f32[8,128]{1,0:T(8,128)S(1)} collective-permute-done((f32[8,128]{1,0:T(8,128)S(1)}, f32[8,128]{1,0:T(8,128)S(1)}, u32[]{:S(2)}, u32[]{:S(2)}) %collective-permute-start.43) | collective-permute-done | bytes 4128 | tf_op jit(solution)/shard_map/ppermute | solution.py:311
  72.2 2.0 %collective-permute-start.45 = (f32[16,128]{1,0:T(8,128)S(1)}, f32[16,128]{1,0:T(8,128)S(1)}, u32[]{:S(2)}, u32[]{:S(2)}) collective-permute-start(f32[16,128]{1,0:T(8,128)S(1)} %shard_map.72.refs_0_), channel_id=1, source_target_pairs={{0,1},{1,2},{2,3},{3,7},{7,6},{6,5},{5,4},{4,0},{8,9},{9,10},{10,1... | collective-permute-start | bytes 24584 | tf_op jit(solution)/shard_map/ppermute | solution.py:297
  75.9 4.5 %shard_map.75 = f32[24,32,128]{2,1,0:T(8,128)} custom-call(f32[32,56,128]{2,1,0:T(8,128)S(1)} %shard_map.74.refs_0_, f32[16,128]{1,0:T(8,128)S(1)} %collective-permute-done.45.refs_1_, f32[16,128]{1,0:T(8,128)S(1)} %collective-permute-done.46.refs_2_, s32[2,40,128]{2,1,0:T(8,128)S(1)} %get-tuple-element.102.refs_3_, ...), custom_call_target="tpu_custom_call" | custom-call | flops 1000000 | bytes 100000 | tf_op jit(solution)/shard_map/pallas_call | solution.py:36
  (100 shorter events, 33.7 us)
Async XLA Ops:
  1.5 9.3 %collective-permute-start = (f32[11,32,128]{2,1,0:T(8,128)S(1)}, f32[11,32,128]{2,1,0:T(8,128)S(1)}, u32[]{:S(2)}, u32[]{:S(2)}) collective-permute-start(f32[11,32,128]{2,1,0:T(8,128)S(1)} %get-tuple-element.61.refs_3_), channel_id=1, source_target_pairs={{0,16},{16,0},{1,17},{17,1},{2,18},{18,2},{3,19},{19,3},{4,20},{20... | collective-permute-start | bytes 540680 | tf_op jit(solution)/shard_map/ppermute | solution.py:301
  4.5 6.3 %collective-permute-start.1 = (f32[256,128]{1,0:T(8,128)S(1)}, f32[256,128]{1,0:T(8,128)S(1)}, u32[]{:S(2)}, u32[]{:S(2)}) collective-permute-start(f32[256,128]{1,0:T(8,128)S(1)} %get-tuple-element.64), channel_id=1, source_target_pairs={{0,4},{4,8},{8,12},{12,0},{1,5},{5,9},{9,13},{13,1},{2,6},{6,10},{... | collective-permute-start | bytes 393224 | tf_op jit(solution)/shard_map/ppermute | solution.py:311
  4.5 6.3 %collective-permute-start.2 = (f32[256,128]{1,0:T(8,128)S(1)}, f32[256,128]{1,0:T(8,128)S(1)}, u32[]{:S(2)}, u32[]{:S(2)}) collective-permute-start(f32[256,128]{1,0:T(8,128)S(1)} %get-tuple-element.65), channel_id=1, source_target_pairs={{4,0},{8,4},{12,8},{0,12},{5,1},{9,5},{13,9},{1,13},{6,2},{10,6},{... | collective-permute-start | bytes 393224 | tf_op jit(solution)/shard_map/ppermute | solution.py:311
  6.3 4.4 %collective-permute-start.3 = (f32[40,128]{1,0:T(8,128)S(1)}, f32[40,128]{1,0:T(8,128)S(1)}, u32[]{:S(2)}, u32[]{:S(2)}) collective-permute-start(f32[40,128]{1,0:T(8,128)S(1)} %get-tuple-element.66), channel_id=1, source_target_pairs={{0,20},{1,21},{2,22},{3,23},{4,24},{5,25},{6,26},{7,27},{8,28},{9,... | collective-permute-start | bytes 61448 | tf_op jit(solution)/shard_map/ppermute | solution.py:297
  6.3 4.5 %collective-permute-start.4 = (f32[40,128]{1,0:T(8,128)S(1)}, f32[40,128]{1,0:T(8,128)S(1)}, u32[]{:S(2)}, u32[]{:S(2)}) collective-permute-start(f32[40,128]{1,0:T(8,128)S(1)} %get-tuple-element.67), channel_id=1, source_target_pairs={{20,0},{21,1},{22,2},{23,3},{24,4},{25,5},{26,6},{27,7},{28,8},{29... | collective-permute-start | bytes 61448 | tf_op jit(solution)/shard_map/ppermute | solution.py:297
  11.9 4.6 %collective-permute-start.6 = (f32[136,128]{1,0:T(8,128)S(1)}, f32[136,128]{1,0:T(8,128)S(1)}, u32[]{:S(2)}, u32[]{:S(2)}) collective-permute-start(f32[136,128]{1,0:T(8,128)S(1)} %get-tuple-element.79), channel_id=1, source_target_pairs={{1,0},{2,1},{3,2},{7,3},{6,7},{5,6},{4,5},{0,4},{9,8},{10,9},{11,1... | collective-permute-start | bytes 208904 | tf_op jit(solution)/shard_map/ppermute | solution.py:297
  20.3 6.7 %collective-permute-start.9 = (f32[9,32,128]{2,1,0:T(8,128)S(1)}, f32[9,32,128]{2,1,0:T(8,128)S(1)}, u32[]{:S(2)}, u32[]{:S(2)}) collective-permute-start(f32[9,32,128]{2,1,0:T(8,128)S(1)} %shard_map.54), channel_id=1, source_target_pairs={{0,16},{16,0},{1,17},{17,1},{2,18},{18,2},{3,19},{19,3},{4,20},{20... | collective-permute-start | bytes 442376 | tf_op jit(solution)/shard_map/ppermute | solution.py:301
  21.1 5.6 %collective-permute-start.11 = (f32[8,128]{1,0:T(8,128)S(1)}, f32[8,128]{1,0:T(8,128)S(1)}, u32[]{:S(2)}, u32[]{:S(2)}) collective-permute-start(f32[8,128]{1,0:T(8,128)S(1)} %get-tuple-element.87.refs_3_.refs_2_.refs_1_), channel_id=1, source_target_pairs={{4,0},{8,4},{12,8},{0,12},{5,1},{9,5},{13,9},{1,13},{6,2},{10,6},{... | collective-permute-start | bytes 12296 | tf_op jit(solution)/shard_map/ppermute | solution.py:311
  22.8 3.9 %collective-permute-start.8 = (f32[8,128]{1,0:T(8,128)S(1)}, f32[8,128]{1,0:T(8,128)S(1)}, u32[]{:S(2)}, u32[]{:S(2)}) collective-permute-start(f32[8,128]{1,0:T(8,128)S(1)} %get-tuple-element.87.refs_3_.refs_2_.refs_1_), channel_id=1, source_target_pairs={{1,0},{2,1},{3,2},{7,3},{6,7},{5,6},{4,5},{0,4},{9,8},{10,9},{11,1... | collective-permute-start | bytes 12296 | tf_op jit(solution)/shard_map/ppermute | solution.py:297
  27.2 5.5 %collective-permute-start.16 = (f32[264,128]{1,0:T(8,128)S(1)}, f32[264,128]{1,0:T(8,128)S(1)}, u32[]{:S(2)}, u32[]{:S(2)}) collective-permute-start(f32[264,128]{1,0:T(8,128)S(1)} %get-tuple-element.94), channel_id=1, source_target_pairs={{4,0},{8,4},{12,8},{0,12},{5,1},{9,5},{13,9},{1,13},{6,2},{10,6},{... | collective-permute-start | bytes 405512 | tf_op jit(solution)/shard_map/ppermute | solution.py:311
  28.6 5.8 %collective-permute-start.15 = (f32[264,128]{1,0:T(8,128)S(1)}, f32[264,128]{1,0:T(8,128)S(1)}, u32[]{:S(2)}, u32[]{:S(2)}) collective-permute-start(f32[264,128]{1,0:T(8,128)S(1)} %get-tuple-element.93.refs_4_), channel_id=1, source_target_pairs={{0,4},{4,8},{8,12},{12,0},{1,5},{5,9},{9,13},{13,1},{2,6},{6,10},{... | collective-permute-start | bytes 405512 | tf_op jit(solution)/shard_map/ppermute | solution.py:311
  28.6 4.1 %collective-permute-start.14 = (f32[8,128]{1,0:T(8,128)S(1)}, f32[8,128]{1,0:T(8,128)S(1)}, u32[]{:S(2)}, u32[]{:S(2)}) collective-permute-start(f32[8,128]{1,0:T(8,128)S(1)} %shard_map.55.refs_3_.refs_2_), channel_id=1, source_target_pairs={{0,16},{16,0},{1,17},{17,1},{2,18},{18,2},{3,19},{19,3},{4,20},{20... | collective-permute-start | bytes 12296 | tf_op jit(solution)/shard_map/ppermute | solution.py:301
  34.9 5.7 %collective-permute-start.17 = (f32[88,128]{1,0:T(8,128)S(1)}, f32[88,128]{1,0:T(8,128)S(1)}, u32[]{:S(2)}, u32[]{:S(2)}) collective-permute-start(f32[88,128]{1,0:T(8,128)S(1)} %get-tuple-element.98), channel_id=1, source_target_pairs={{0,1},{1,2},{2,3},{3,7},{7,6},{6,5},{5,4},{4,0},{8,9},{9,10},{10,1... | collective-permute-start | bytes 135176 | tf_op jit(solution)/shard_map/ppermute | solution.py:297
  36.5 4.1 %collective-permute-start.18 = (f32[88,128]{1,0:T(8,128)S(1)}, f32[88,128]{1,0:T(8,128)S(1)}, u32[]{:S(2)}, u32[]{:S(2)}) collective-permute-start(f32[88,128]{1,0:T(8,128)S(1)} %get-tuple-element.99), channel_id=1, source_target_pairs={{1,0},{2,1},{3,2},{7,3},{6,7},{5,6},{4,5},{0,4},{9,8},{10,9},{11,1... | collective-permute-start | bytes 135176 | tf_op jit(solution)/shard_map/ppermute | solution.py:297
  40.8 4.7 %collective-permute-start.26 = (f32[8,128]{1,0:T(8,128)S(1)}, f32[8,128]{1,0:T(8,128)S(1)}, u32[]{:S(2)}, u32[]{:S(2)}) collective-permute-start(f32[8,128]{1,0:T(8,128)S(1)} %shard_map.62.refs_3_), channel_id=1, source_target_pairs={{4,0},{8,4},{12,8},{0,12},{5,1},{9,5},{13,9},{1,13},{6,2},{10,6},{... | collective-permute-start | bytes 12296 | tf_op jit(solution)/shard_map/ppermute | solution.py:311
  41.1 4.3 %collective-permute-start.25 = (f32[8,128]{1,0:T(8,128)S(1)}, f32[8,128]{1,0:T(8,128)S(1)}, u32[]{:S(2)}, u32[]{:S(2)}) collective-permute-start(f32[8,128]{1,0:T(8,128)S(1)} %shard_map.62.refs_3_), channel_id=1, source_target_pairs={{0,4},{4,8},{8,12},{12,0},{1,5},{5,9},{9,13},{13,1},{2,6},{6,10},{... | collective-permute-start | bytes 12296 | tf_op jit(solution)/shard_map/ppermute | solution.py:311
  41.3 4.2 %collective-permute-start.24 = (f32[8,128]{1,0:T(8,128)S(1)}, f32[8,128]{1,0:T(8,128)S(1)}, u32[]{:S(2)}, u32[]{:S(2)}) collective-permute-start(f32[8,128]{1,0:T(8,128)S(1)} %shard_map.62.refs_3_), channel_id=1, source_target_pairs={{0,16},{16,0},{1,17},{17,1},{2,18},{18,2},{3,19},{19,3},{4,20},{20... | collective-permute-start | bytes 12296 | tf_op jit(solution)/shard_map/ppermute | solution.py:301
  46.1 6.2 %collective-permute-start.31 = (f32[8,128]{1,0:T(8,128)S(1)}, f32[8,128]{1,0:T(8,128)S(1)}, u32[]{:S(2)}, u32[]{:S(2)}) collective-permute-start(f32[8,128]{1,0:T(8,128)S(1)} %shard_map.64.refs_3_), channel_id=1, source_target_pairs={{4,0},{8,4},{12,8},{0,12},{5,1},{9,5},{13,9},{1,13},{6,2},{10,6},{... | collective-permute-start | bytes 12296 | tf_op jit(solution)/shard_map/ppermute | solution.py:311
  47.7 4.6 %collective-permute-start.30 = (f32[8,128]{1,0:T(8,128)S(1)}, f32[8,128]{1,0:T(8,128)S(1)}, u32[]{:S(2)}, u32[]{:S(2)}) collective-permute-start(f32[8,128]{1,0:T(8,128)S(1)} %shard_map.64.refs_3_), channel_id=1, source_target_pairs={{0,4},{4,8},{8,12},{12,0},{1,5},{5,9},{9,13},{13,1},{2,6},{6,10},{... | collective-permute-start | bytes 12296 | tf_op jit(solution)/shard_map/ppermute | solution.py:311
  47.7 4.6 %collective-permute-start.29 = (f32[8,128]{1,0:T(8,128)S(1)}, f32[8,128]{1,0:T(8,128)S(1)}, u32[]{:S(2)}, u32[]{:S(2)}) collective-permute-start(f32[8,128]{1,0:T(8,128)S(1)} %shard_map.64.refs_3_), channel_id=1, source_target_pairs={{0,16},{16,0},{1,17},{17,1},{2,18},{18,2},{3,19},{19,3},{4,20},{20... | collective-permute-start | bytes 12296 | tf_op jit(solution)/shard_map/ppermute | solution.py:301
  52.9 5.0 %collective-permute-start.36 = (f32[8,128]{1,0:T(8,128)S(1)}, f32[8,128]{1,0:T(8,128)S(1)}, u32[]{:S(2)}, u32[]{:S(2)}) collective-permute-start(f32[8,128]{1,0:T(8,128)S(1)} %shard_map.66.refs_3_), channel_id=1, source_target_pairs={{4,0},{8,4},{12,8},{0,12},{5,1},{9,5},{13,9},{1,13},{6,2},{10,6},{... | collective-permute-start | bytes 12296 | tf_op jit(solution)/shard_map/ppermute | solution.py:311
  58.5 5.7 %collective-permute-start.41 = (f32[8,128]{1,0:T(8,128)S(1)}, f32[8,128]{1,0:T(8,128)S(1)}, u32[]{:S(2)}, u32[]{:S(2)}) collective-permute-start(f32[8,128]{1,0:T(8,128)S(1)} %shard_map.68.refs_3_), channel_id=1, source_target_pairs={{4,0},{8,4},{12,8},{0,12},{5,1},{9,5},{13,9},{1,13},{6,2},{10,6},{... | collective-permute-start | bytes 12296 | tf_op jit(solution)/shard_map/ppermute | solution.py:311
  60.0 4.2 %collective-permute-start.40 = (f32[8,128]{1,0:T(8,128)S(1)}, f32[8,128]{1,0:T(8,128)S(1)}, u32[]{:S(2)}, u32[]{:S(2)}) collective-permute-start(f32[8,128]{1,0:T(8,128)S(1)} %shard_map.68.refs_3_), channel_id=1, source_target_pairs={{0,4},{4,8},{8,12},{12,0},{1,5},{5,9},{9,13},{13,1},{2,6},{6,10},{... | collective-permute-start | bytes 12296 | tf_op jit(solution)/shard_map/ppermute | solution.py:311
  60.0 4.2 %collective-permute-start.39 = (f32[8,128]{1,0:T(8,128)S(1)}, f32[8,128]{1,0:T(8,128)S(1)}, u32[]{:S(2)}, u32[]{:S(2)}) collective-permute-start(f32[8,128]{1,0:T(8,128)S(1)} %shard_map.68.refs_3_), channel_id=1, source_target_pairs={{0,16},{16,0},{1,17},{17,1},{2,18},{18,2},{3,19},{19,3},{4,20},{20... | collective-permute-start | bytes 12296 | tf_op jit(solution)/shard_map/ppermute | solution.py:301
  (23 other events, 72.6 us)

commit v18 on v15

--- a/solution.py
+++ b/solution.py
@@ -849,7 +849,7 @@
                 result(xs[0] - HALO, len(xs)).start()
             return edges
 
-        size = 8 if final else 10
+        size = 8 if final else 15
         edges = batched(s + 1, wide - s - 1, step, jnp.zeros((tall, LANES), F32), size)
         if not final:
             near = ends_near(src_ends[0, span], src_ends[1, span], edges)

time: 80 us -> 79.8 us (level)
  transfers between devices with their start and end apart: 47 -> 47, of which waited for: 12 -> 12; matrix products, arithmetic and copies ran while one was open for 0% -> 0% of each run, Pallas kernels for 17% -> 18%
where the time goes in v18:
time: 79.8 us; the launch traced here: 79.5 us
  starting transfers between devices  41.2 us (52%)
  Pallas kernels  26.2 us (33%)
  waiting for transfers between devices  11.7 us (15%)
    pallas_call x29, Pallas kernels, run(): pl.pallas_call(placed, out_shape=outs, in_specs=in_specs or [VMEM] * len(...  26.2 us
    ppermute x20, starting transfers between devices, send(): return lax.ppermute(values, ('gx', 'gy', 'gz'), pairs)  20 us
    ppermute x9, starting transfers between devices, x(): return (lax.ppermute(sends[0], 'gx', self.ring_x),)  11.2 us
    ppermute x9, starting transfers between devices, ring_y(): lax.ppermute(to_low, 'gy', self.back(ring))  9.18 us
    ppermute x20, waiting for transfers between devices, send(): return lax.ppermute(values, ('gx', 'gy', 'gz'), pairs)  4.6 us
    ppermute x9, waiting for transfers between devices, ring_y(): lax.ppermute(to_high, 'gy', ring)  3.41 us
    ppermute x9, waiting for transfers between devices, x(): return (lax.ppermute(sends[0], 'gx', self.ring_x),)  2.66 us
  transfers between devices with their start and end apart: 47, of which 12 were waited for; matrix products, arithmetic and copies ran while one was open for 0% of the time, Pallas kernels for 18%

profile of v18, /device:TPU:0, one launch (start us, length us, event | category | flops | bytes accessed | tf_op | source)
XLA Modules:
  0.0 79.5 jit_solution(4016112270001404545)
XLA Ops:
  0.0 1.5 %shard_map.46 = (f32[24,32,128]{2,1,0:T(8,128)S(1)}, f32[24,32,128]{2,1,0:T(8,128)S(1)}, f32[24,32,128]{2,1,0:T(8,128)S(1)}, s32[12,16,64]{2,1,0:T(8,128)S(1)}, ...) custom-call(f32[24,32,128]{2,1,0:T(8,128)} %refs_0_.1, ...), custom_call_target="tpu_custom_call" | custom-call | flops 1000000 | bytes 100000 | tf_op jit(solution)/shard_map/pallas_call | solution.py:36
  1.5 3.0 %collective-permute-start = (f32[11,32,128]{2,1,0:T(8,128)S(1)}, f32[11,32,128]{2,1,0:T(8,128)S(1)}, u32[]{:S(2)}, u32[]{:S(2)}) collective-permute-start(f32[11,32,128]{2,1,0:T(8,128)S(1)} %get-tuple-element.61.refs_3_), channel_id=1, source_target_pairs={{0,16},{16,0},{1,17},{17,1},{2,18},{18,2},{3,19},{19,3},{4,20},{20... | collective-permute-start | bytes 540680 | tf_op jit(solution)/shard_map/ppermute | solution.py:301
  4.5 1.7 %collective-permute-start.2 = (f32[256,128]{1,0:T(8,128)S(1)}, f32[256,128]{1,0:T(8,128)S(1)}, u32[]{:S(2)}, u32[]{:S(2)}) collective-permute-start(f32[256,128]{1,0:T(8,128)S(1)} %get-tuple-element.65), channel_id=1, source_target_pairs={{4,0},{8,4},{12,8},{0,12},{5,1},{9,5},{13,9},{1,13},{6,2},{10,6},{... | collective-permute-start | bytes 393224 | tf_op jit(solution)/shard_map/ppermute | solution.py:311
  6.3 2.6 %collective-permute-start.4 = (f32[40,128]{1,0:T(8,128)S(1)}, f32[40,128]{1,0:T(8,128)S(1)}, u32[]{:S(2)}, u32[]{:S(2)}) collective-permute-start(f32[40,128]{1,0:T(8,128)S(1)} %get-tuple-element.67), channel_id=1, source_target_pairs={{20,0},{21,1},{22,2},{23,3},{24,4},{25,5},{26,6},{27,7},{28,8},{29... | collective-permute-start | bytes 61448 | tf_op jit(solution)/shard_map/ppermute | solution.py:297
  8.9 1.9 %shard_map.47 = (f32[12,8,128]{2,1,0:T(8,128)S(1)}, s32[6,12,8,128]{3,2,1,0:T(8,128)S(1)}, f32[6,12,8,128]{3,2,1,0:T(8,128)S(1)}, f32[12,8,128]{2,1,0:T(8,128)S(...) custom-call(f32[24,32,128]{2,1,0:T(8,128)S(1)} %get-tuple-element.58.refs_0_, ...), custom_call_target="tpu_custom_call" | custom-call | flops 1000000 | bytes 100000 | tf_op jit(solution)/shard_map/pallas_call | solution.py:36
  12.0 1.6 %collective-permute-start.5 = (f32[136,128]{1,0:T(8,128)S(1)}, f32[136,128]{1,0:T(8,128)S(1)}, u32[]{:S(2)}, u32[]{:S(2)}) collective-permute-start(f32[136,128]{1,0:T(8,128)S(1)} %get-tuple-element.78), channel_id=1, source_target_pairs={{0,1},{1,2},{2,3},{3,7},{7,6},{6,5},{5,4},{4,0},{8,9},{9,10},{10,1... | collective-permute-start | bytes 208904 | tf_op jit(solution)/shard_map/ppermute | solution.py:297
  13.6 2.5 %shard_map.49 = (f32[32,56,128]{2,1,0:T(8,128)S(1)}, f32[32,56,128]{2,1,0:T(8,128)S(1)}, f32[32,56,128]{2,1,0:T(8,128)S(1)}, f32[32,56,128]{2,1,0:T(8,128)S(1)},...) custom-call(f32[3,32,56,128]{3,2,1,0:T(8,128)S(1)} %get-tuple-element.74.refs_0_, ...), custom_call_target="tpu_custom_call" | custom-call | flops 1000000 | bytes 100000 | tf_op jit(solution)/shard_map/pallas_call | solution.py:36
  16.1 1.8 %collective-permute-done.6.refs_2_.refs_8_ = f32[136,128]{1,0:T(8,128)S(1)} collective-permute-done((f32[136,128]{1,0:T(8,128)S(1)}, f32[136,128]{1,0:T(8,128)S(1)}, u32[]{:S(2)}, u32[]{:S(2)}) %collective-permute-start.6) | collective-permute-done | bytes 69664 | tf_op jit(solution)/shard_map/ppermute | solution.py:297
  17.9 3.9 %shard_map.50 = (f32[32,56,128]{2,1,0:T(8,128)S(1)}, f32[32,56,128]{2,1,0:T(8,128)S(1)}, f32[2,56,128]{2,1,0:T(8,128)S(1)}, f32[2,56,128]{2,1,0:T(8,128)S(1)}, f...) custom-call(f32[3,32,56,128]{3,2,1,0:T(8,128)S(1)} %get-tuple-elemen, ...), custom_call_target="tpu_custom_call" | custom-call | flops 1000000 | bytes 100000 | tf_op jit(solution)/shard_map/pallas_call | solution.py:36
  24.0 1.1 %collective-permute-start.7 = (f32[8,128]{1,0:T(8,128)S(1)}, f32[8,128]{1,0:T(8,128)S(1)}, u32[]{:S(2)}, u32[]{:S(2)}) collective-permute-start(f32[8,128]{1,0:T(8,128)S(1)} %get-tuple-element.87.refs_3_.refs_2_.refs_1_), channel_id=1, source_target_pairs={{0,1},{1,2},{2,3},{3,7},{7,6},{6,5},{5,4},{4,0},{8,9},{9,10},{10,1... | collective-permute-start | bytes 12296 | tf_op jit(solution)/shard_map/ppermute | solution.py:297
  27.3 1.2 %collective-permute-start.16 = (f32[264,128]{1,0:T(8,128)S(1)}, f32[264,128]{1,0:T(8,128)S(1)}, u32[]{:S(2)}, u32[]{:S(2)}) collective-permute-start(f32[264,128]{1,0:T(8,128)S(1)} %get-tuple-element.94), channel_id=1, source_target_pairs={{4,0},{8,4},{12,8},{0,12},{5,1},{9,5},{13,9},{1,13},{6,2},{10,6},{... | collective-permute-start | bytes 405512 | tf_op jit(solution)/shard_map/ppermute | solution.py:311
  29.7 1.4 %collective-permute-start.13 = (f32[8,128]{1,0:T(8,128)S(1)}, f32[8,128]{1,0:T(8,128)S(1)}, u32[]{:S(2)}, u32[]{:S(2)}) collective-permute-start(f32[8,128]{1,0:T(8,128)S(1)} %shard_map.54.refs_3_.refs_2_), channel_id=1, source_target_pairs={{1,0},{2,1},{3,2},{7,3},{6,7},{5,6},{4,5},{0,4},{9,8},{10,9},{11,1... | collective-permute-start | bytes 12296 | tf_op jit(solution)/shard_map/ppermute | solution.py:297
  34.6 1.6 %collective-permute-start.17 = (f32[88,128]{1,0:T(8,128)S(1)}, f32[88,128]{1,0:T(8,128)S(1)}, u32[]{:S(2)}, u32[]{:S(2)}) collective-permute-start(f32[88,128]{1,0:T(8,128)S(1)} %get-tuple-element.98), channel_id=1, source_target_pairs={{0,1},{1,2},{2,3},{3,7},{7,6},{6,5},{5,4},{4,0},{8,9},{9,10},{10,1... | collective-permute-start | bytes 135176 | tf_op jit(solution)/shard_map/ppermute | solution.py:297
  46.3 1.7 %collective-permute-start.31 = (f32[8,128]{1,0:T(8,128)S(1)}, f32[8,128]{1,0:T(8,128)S(1)}, u32[]{:S(2)}, u32[]{:S(2)}) collective-permute-start(f32[8,128]{1,0:T(8,128)S(1)} %shard_map.63.refs_3_), channel_id=1, source_target_pairs={{4,0},{8,4},{12,8},{0,12},{5,1},{9,5},{13,9},{1,13},{6,2},{10,6},{... | collective-permute-start | bytes 12296 | tf_op jit(solution)/shard_map/ppermute | solution.py:311
  52.5 1.3 %collective-permute-start.36 = (f32[8,128]{1,0:T(8,128)S(1)}, f32[8,128]{1,0:T(8,128)S(1)}, u32[]{:S(2)}, u32[]{:S(2)}) collective-permute-start(f32[8,128]{1,0:T(8,128)S(1)} %shard_map.65.refs_3_), channel_id=1, source_target_pairs={{4,0},{8,4},{12,8},{0,12},{5,1},{9,5},{13,9},{1,13},{6,2},{10,6},{... | collective-permute-start | bytes 12296 | tf_op jit(solution)/shard_map/ppermute | solution.py:311
  53.9 1.3 %collective-permute-start.34 = (f32[8,128]{1,0:T(8,128)S(1)}, f32[8,128]{1,0:T(8,128)S(1)}, u32[]{:S(2)}, u32[]{:S(2)}) collective-permute-start(f32[8,128]{1,0:T(8,128)S(1)} %shard_map.65.refs_3_), channel_id=1, source_target_pairs={{0,16},{16,0},{1,17},{17,1},{2,18},{18,2},{3,19},{19,3},{4,20},{20... | collective-permute-start | bytes 12296 | tf_op jit(solution)/shard_map/ppermute | solution.py:301
  55.9 1.3 %collective-permute-start.32 = (f32[8,128]{1,0:T(8,128)S(1)}, f32[8,128]{1,0:T(8,128)S(1)}, u32[]{:S(2)}, u32[]{:S(2)}) collective-permute-start(f32[8,128]{1,0:T(8,128)S(1)} %shard_map.65.refs_3_), channel_id=1, source_target_pairs={{0,1},{1,2},{2,3},{3,7},{7,6},{6,5},{5,4},{4,0},{8,9},{9,10},{10,1... | collective-permute-start | bytes 12296 | tf_op jit(solution)/shard_map/ppermute | solution.py:297
  59.0 1.4 %collective-permute-start.41 = (f32[8,128]{1,0:T(8,128)S(1)}, f32[8,128]{1,0:T(8,128)S(1)}, u32[]{:S(2)}, u32[]{:S(2)}) collective-permute-start(f32[8,128]{1,0:T(8,128)S(1)} %shard_map.67.refs_3_), channel_id=1, source_target_pairs={{4,0},{8,4},{12,8},{0,12},{5,1},{9,5},{13,9},{1,13},{6,2},{10,6},{... | collective-permute-start | bytes 12296 | tf_op jit(solution)/shard_map/ppermute | solution.py:311
  60.9 1.4 %collective-permute-start.38 = (f32[8,128]{1,0:T(8,128)S(1)}, f32[8,128]{1,0:T(8,128)S(1)}, u32[]{:S(2)}, u32[]{:S(2)}) collective-permute-start(f32[8,128]{1,0:T(8,128)S(1)} %shard_map.67.refs_3_), channel_id=1, source_target_pairs={{1,0},{2,1},{3,2},{7,3},{6,7},{5,6},{4,5},{0,4},{9,8},{10,9},{11,1... | collective-permute-start | bytes 12296 | tf_op jit(solution)/shard_map/ppermute | solution.py:297
  64.7 1.6 %collective-permute-start.42 = (f32[8,128]{1,0:T(8,128)S(1)}, f32[8,128]{1,0:T(8,128)S(1)}, u32[]{:S(2)}, u32[]{:S(2)}) collective-permute-start(f32[8,128]{1,0:T(8,128)S(1)} %shard_map.69.refs_1_), channel_id=1, source_target_pairs={{0,16},{16,0},{1,17},{17,1},{2,18},{18,2},{3,19},{19,3},{4,20},{20... | collective-permute-start | bytes 12296 | tf_op jit(solution)/shard_map/ppermute | solution.py:301
  66.3 2.1 %collective-permute-done.42.refs_0_.refs_2_ = f32[8,128]{1,0:T(8,128)S(1)} collective-permute-done((f32[8,128]{1,0:T(8,128)S(1)}, f32[8,128]{1,0:T(8,128)S(1)}, u32[]{:S(2)}, u32[]{:S(2)}) %collective-permute-start.42) | collective-permute-done | bytes 4128 | tf_op jit(solution)/shard_map/ppermute | solution.py:301
  69.9 1.7 %collective-permute-done.43.refs_0_ = f32[8,128]{1,0:T(8,128)S(1)} collective-permute-done((f32[8,128]{1,0:T(8,128)S(1)}, f32[8,128]{1,0:T(8,128)S(1)}, u32[]{:S(2)}, u32[]{:S(2)}) %collective-permute-start.43) | collective-permute-done | bytes 4128 | tf_op jit(solution)/shard_map/ppermute | solution.py:311
  71.7 1.9 %collective-permute-start.45 = (f32[16,128]{1,0:T(8,128)S(1)}, f32[16,128]{1,0:T(8,128)S(1)}, u32[]{:S(2)}, u32[]{:S(2)}) collective-permute-start(f32[16,128]{1,0:T(8,128)S(1)} %shard_map.71.refs_0_), channel_id=1, source_target_pairs={{0,1},{1,2},{2,3},{3,7},{7,6},{6,5},{5,4},{4,0},{8,9},{9,10},{10,1... | collective-permute-start | bytes 24584 | tf_op jit(solution)/shard_map/ppermute | solution.py:297
  75.2 4.3 %shard_map.74 = f32[24,32,128]{2,1,0:T(8,128)} custom-call(f32[32,56,128]{2,1,0:T(8,128)S(1)} %shard_map.73.refs_0_, f32[16,128]{1,0:T(8,128)S(1)} %collective-permute-done.45.refs_1_, f32[16,128]{1,0:T(8,128)S(1)} %collective-permute-done.46.refs_2_, s32[2,40,128]{2,1,0:T(8,128)S(1)} %get-tuple-element.102.refs_3_, ...), custom_call_target="tpu_custom_call" | custom-call | flops 1000000 | bytes 100000 | tf_op jit(solution)/shard_map/pallas_call | solution.py:36
  (99 shorter events, 33.2 us)
Async XLA Ops:
  1.5 9.4 %collective-permute-start = (f32[11,32,128]{2,1,0:T(8,128)S(1)}, f32[11,32,128]{2,1,0:T(8,128)S(1)}, u32[]{:S(2)}, u32[]{:S(2)}) collective-permute-start(f32[11,32,128]{2,1,0:T(8,128)S(1)} %get-tuple-element.61.refs_3_), channel_id=1, source_target_pairs={{0,16},{16,0},{1,17},{17,1},{2,18},{18,2},{3,19},{19,3},{4,20},{20... | collective-permute-start | bytes 540680 | tf_op jit(solution)/shard_map/ppermute | solution.py:301
  4.5 6.4 %collective-permute-start.1 = (f32[256,128]{1,0:T(8,128)S(1)}, f32[256,128]{1,0:T(8,128)S(1)}, u32[]{:S(2)}, u32[]{:S(2)}) collective-permute-start(f32[256,128]{1,0:T(8,128)S(1)} %get-tuple-element.64), channel_id=1, source_target_pairs={{0,4},{4,8},{8,12},{12,0},{1,5},{5,9},{9,13},{13,1},{2,6},{6,10},{... | collective-permute-start | bytes 393224 | tf_op jit(solution)/shard_map/ppermute | solution.py:311
  4.5 6.4 %collective-permute-start.2 = (f32[256,128]{1,0:T(8,128)S(1)}, f32[256,128]{1,0:T(8,128)S(1)}, u32[]{:S(2)}, u32[]{:S(2)}) collective-permute-start(f32[256,128]{1,0:T(8,128)S(1)} %get-tuple-element.65), channel_id=1, source_target_pairs={{4,0},{8,4},{12,8},{0,12},{5,1},{9,5},{13,9},{1,13},{6,2},{10,6},{... | collective-permute-start | bytes 393224 | tf_op jit(solution)/shard_map/ppermute | solution.py:311
  6.3 4.6 %collective-permute-start.3 = (f32[40,128]{1,0:T(8,128)S(1)}, f32[40,128]{1,0:T(8,128)S(1)}, u32[]{:S(2)}, u32[]{:S(2)}) collective-permute-start(f32[40,128]{1,0:T(8,128)S(1)} %get-tuple-element.66), channel_id=1, source_target_pairs={{0,20},{1,21},{2,22},{3,23},{4,24},{5,25},{6,26},{7,27},{8,28},{9,... | collective-permute-start | bytes 61448 | tf_op jit(solution)/shard_map/ppermute | solution.py:297
  6.3 4.6 %collective-permute-start.4 = (f32[40,128]{1,0:T(8,128)S(1)}, f32[40,128]{1,0:T(8,128)S(1)}, u32[]{:S(2)}, u32[]{:S(2)}) collective-permute-start(f32[40,128]{1,0:T(8,128)S(1)} %get-tuple-element.67), channel_id=1, source_target_pairs={{20,0},{21,1},{22,2},{23,3},{24,4},{25,5},{26,6},{27,7},{28,8},{29... | collective-permute-start | bytes 61448 | tf_op jit(solution)/shard_map/ppermute | solution.py:297
  12.0 4.1 %collective-permute-start.5 = (f32[136,128]{1,0:T(8,128)S(1)}, f32[136,128]{1,0:T(8,128)S(1)}, u32[]{:S(2)}, u32[]{:S(2)}) collective-permute-start(f32[136,128]{1,0:T(8,128)S(1)} %get-tuple-element.78), channel_id=1, source_target_pairs={{0,1},{1,2},{2,3},{3,7},{7,6},{6,5},{5,4},{4,0},{8,9},{9,10},{10,1... | collective-permute-start | bytes 208904 | tf_op jit(solution)/shard_map/ppermute | solution.py:297
  13.6 4.3 %collective-permute-start.6 = (f32[136,128]{1,0:T(8,128)S(1)}, f32[136,128]{1,0:T(8,128)S(1)}, u32[]{:S(2)}, u32[]{:S(2)}) collective-permute-start(f32[136,128]{1,0:T(8,128)S(1)} %get-tuple-element.79), channel_id=1, source_target_pairs={{1,0},{2,1},{3,2},{7,3},{6,7},{5,6},{4,5},{0,4},{9,8},{10,9},{11,1... | collective-permute-start | bytes 208904 | tf_op jit(solution)/shard_map/ppermute | solution.py:297
  21.8 5.3 %collective-permute-start.9 = (f32[9,32,128]{2,1,0:T(8,128)S(1)}, f32[9,32,128]{2,1,0:T(8,128)S(1)}, u32[]{:S(2)}, u32[]{:S(2)}) collective-permute-start(f32[9,32,128]{2,1,0:T(8,128)S(1)} %shard_map.53), channel_id=1, source_target_pairs={{0,16},{16,0},{1,17},{17,1},{2,18},{18,2},{3,19},{19,3},{4,20},{20... | collective-permute-start | bytes 442376 | tf_op jit(solution)/shard_map/ppermute | solution.py:301
  22.6 4.4 %collective-permute-start.11 = (f32[8,128]{1,0:T(8,128)S(1)}, f32[8,128]{1,0:T(8,128)S(1)}, u32[]{:S(2)}, u32[]{:S(2)}) collective-permute-start(f32[8,128]{1,0:T(8,128)S(1)} %get-tuple-element.87.refs_3_.refs_2_.refs_1_), channel_id=1, source_target_pairs={{4,0},{8,4},{12,8},{0,12},{5,1},{9,5},{13,9},{1,13},{6,2},{10,6},{... | collective-permute-start | bytes 12296 | tf_op jit(solution)/shard_map/ppermute | solution.py:311
  22.6 4.4 %collective-permute-start.10 = (f32[8,128]{1,0:T(8,128)S(1)}, f32[8,128]{1,0:T(8,128)S(1)}, u32[]{:S(2)}, u32[]{:S(2)}) collective-permute-start(f32[8,128]{1,0:T(8,128)S(1)} %get-tuple-element.87.refs_3_.refs_2_.refs_1_), channel_id=1, source_target_pairs={{0,4},{4,8},{8,12},{12,0},{1,5},{5,9},{9,13},{13,1},{2,6},{6,10},{... | collective-permute-start | bytes 12296 | tf_op jit(solution)/shard_map/ppermute | solution.py:311
  27.3 6.0 %collective-permute-start.16 = (f32[264,128]{1,0:T(8,128)S(1)}, f32[264,128]{1,0:T(8,128)S(1)}, u32[]{:S(2)}, u32[]{:S(2)}) collective-permute-start(f32[264,128]{1,0:T(8,128)S(1)} %get-tuple-element.94), channel_id=1, source_target_pairs={{4,0},{8,4},{12,8},{0,12},{5,1},{9,5},{13,9},{1,13},{6,2},{10,6},{... | collective-permute-start | bytes 405512 | tf_op jit(solution)/shard_map/ppermute | solution.py:311
  28.5 5.6 %collective-permute-start.15 = (f32[264,128]{1,0:T(8,128)S(1)}, f32[264,128]{1,0:T(8,128)S(1)}, u32[]{:S(2)}, u32[]{:S(2)}) collective-permute-start(f32[264,128]{1,0:T(8,128)S(1)} %get-tuple-element.93.refs_4_), channel_id=1, source_target_pairs={{0,4},{4,8},{8,12},{12,0},{1,5},{5,9},{9,13},{13,1},{2,6},{6,10},{... | collective-permute-start | bytes 405512 | tf_op jit(solution)/shard_map/ppermute | solution.py:311
  28.5 4.7 %collective-permute-start.14 = (f32[8,128]{1,0:T(8,128)S(1)}, f32[8,128]{1,0:T(8,128)S(1)}, u32[]{:S(2)}, u32[]{:S(2)}) collective-permute-start(f32[8,128]{1,0:T(8,128)S(1)} %shard_map.54.refs_3_.refs_2_), channel_id=1, source_target_pairs={{0,16},{16,0},{1,17},{17,1},{2,18},{18,2},{3,19},{19,3},{4,20},{20... | collective-permute-start | bytes 12296 | tf_op jit(solution)/shard_map/ppermute | solution.py:301
  34.6 6.1 %collective-permute-start.17 = (f32[88,128]{1,0:T(8,128)S(1)}, f32[88,128]{1,0:T(8,128)S(1)}, u32[]{:S(2)}, u32[]{:S(2)}) collective-permute-start(f32[88,128]{1,0:T(8,128)S(1)} %get-tuple-element.98), channel_id=1, source_target_pairs={{0,1},{1,2},{2,3},{3,7},{7,6},{6,5},{5,4},{4,0},{8,9},{9,10},{10,1... | collective-permute-start | bytes 135176 | tf_op jit(solution)/shard_map/ppermute | solution.py:297
  36.2 4.5 %collective-permute-start.18 = (f32[88,128]{1,0:T(8,128)S(1)}, f32[88,128]{1,0:T(8,128)S(1)}, u32[]{:S(2)}, u32[]{:S(2)}) collective-permute-start(f32[88,128]{1,0:T(8,128)S(1)} %get-tuple-element.99), channel_id=1, source_target_pairs={{1,0},{2,1},{3,2},{7,3},{6,7},{5,6},{4,5},{0,4},{9,8},{10,9},{11,1... | collective-permute-start | bytes 135176 | tf_op jit(solution)/shard_map/ppermute | solution.py:297
  40.9 4.8 %collective-permute-start.26 = (f32[8,128]{1,0:T(8,128)S(1)}, f32[8,128]{1,0:T(8,128)S(1)}, u32[]{:S(2)}, u32[]{:S(2)}) collective-permute-start(f32[8,128]{1,0:T(8,128)S(1)} %shard_map.61.refs_3_), channel_id=1, source_target_pairs={{4,0},{8,4},{12,8},{0,12},{5,1},{9,5},{13,9},{1,13},{6,2},{10,6},{... | collective-permute-start | bytes 12296 | tf_op jit(solution)/shard_map/ppermute | solution.py:311
  41.5 4.2 %collective-permute-start.25 = (f32[8,128]{1,0:T(8,128)S(1)}, f32[8,128]{1,0:T(8,128)S(1)}, u32[]{:S(2)}, u32[]{:S(2)}) collective-permute-start(f32[8,128]{1,0:T(8,128)S(1)} %shard_map.61.refs_3_), channel_id=1, source_target_pairs={{0,4},{4,8},{8,12},{12,0},{1,5},{5,9},{9,13},{13,1},{2,6},{6,10},{... | collective-permute-start | bytes 12296 | tf_op jit(solution)/shard_map/ppermute | solution.py:311
  41.5 4.2 %collective-permute-start.24 = (f32[8,128]{1,0:T(8,128)S(1)}, f32[8,128]{1,0:T(8,128)S(1)}, u32[]{:S(2)}, u32[]{:S(2)}) collective-permute-start(f32[8,128]{1,0:T(8,128)S(1)} %shard_map.61.refs_3_), channel_id=1, source_target_pairs={{0,16},{16,0},{1,17},{17,1},{2,18},{18,2},{3,19},{19,3},{4,20},{20... | collective-permute-start | bytes 12296 | tf_op jit(solution)/shard_map/ppermute | solution.py:301
  46.3 5.6 %collective-permute-start.31 = (f32[8,128]{1,0:T(8,128)S(1)}, f32[8,128]{1,0:T(8,128)S(1)}, u32[]{:S(2)}, u32[]{:S(2)}) collective-permute-start(f32[8,128]{1,0:T(8,128)S(1)} %shard_map.63.refs_3_), channel_id=1, source_target_pairs={{4,0},{8,4},{12,8},{0,12},{5,1},{9,5},{13,9},{1,13},{6,2},{10,6},{... | collective-permute-start | bytes 12296 | tf_op jit(solution)/shard_map/ppermute | solution.py:311
  48.0 4.0 %collective-permute-start.29 = (f32[8,128]{1,0:T(8,128)S(1)}, f32[8,128]{1,0:T(8,128)S(1)}, u32[]{:S(2)}, u32[]{:S(2)}) collective-permute-start(f32[8,128]{1,0:T(8,128)S(1)} %shard_map.63.refs_3_), channel_id=1, source_target_pairs={{0,16},{16,0},{1,17},{17,1},{2,18},{18,2},{3,19},{19,3},{4,20},{20... | collective-permute-start | bytes 12296 | tf_op jit(solution)/shard_map/ppermute | solution.py:301
  52.5 5.9 %collective-permute-start.36 = (f32[8,128]{1,0:T(8,128)S(1)}, f32[8,128]{1,0:T(8,128)S(1)}, u32[]{:S(2)}, u32[]{:S(2)}) collective-permute-start(f32[8,128]{1,0:T(8,128)S(1)} %shard_map.65.refs_3_), channel_id=1, source_target_pairs={{4,0},{8,4},{12,8},{0,12},{5,1},{9,5},{13,9},{1,13},{6,2},{10,6},{... | collective-permute-start | bytes 12296 | tf_op jit(solution)/shard_map/ppermute | solution.py:311
  53.9 4.5 %collective-permute-start.35 = (f32[8,128]{1,0:T(8,128)S(1)}, f32[8,128]{1,0:T(8,128)S(1)}, u32[]{:S(2)}, u32[]{:S(2)}) collective-permute-start(f32[8,128]{1,0:T(8,128)S(1)} %shard_map.65.refs_3_), channel_id=1, source_target_pairs={{0,4},{4,8},{8,12},{12,0},{1,5},{5,9},{9,13},{13,1},{2,6},{6,10},{... | collective-permute-start | bytes 12296 | tf_op jit(solution)/shard_map/ppermute | solution.py:311
  53.9 4.5 %collective-permute-start.34 = (f32[8,128]{1,0:T(8,128)S(1)}, f32[8,128]{1,0:T(8,128)S(1)}, u32[]{:S(2)}, u32[]{:S(2)}) collective-permute-start(f32[8,128]{1,0:T(8,128)S(1)} %shard_map.65.refs_3_), channel_id=1, source_target_pairs={{0,16},{16,0},{1,17},{17,1},{2,18},{18,2},{3,19},{19,3},{4,20},{20... | collective-permute-start | bytes 12296 | tf_op jit(solution)/shard_map/ppermute | solution.py:301
  59.0 5.1 %collective-permute-start.41 = (f32[8,128]{1,0:T(8,128)S(1)}, f32[8,128]{1,0:T(8,128)S(1)}, u32[]{:S(2)}, u32[]{:S(2)}) collective-permute-start(f32[8,128]{1,0:T(8,128)S(1)} %shard_map.67.refs_3_), channel_id=1, source_target_pairs={{4,0},{8,4},{12,8},{0,12},{5,1},{9,5},{13,9},{1,13},{6,2},{10,6},{... | collective-permute-start | bytes 12296 | tf_op jit(solution)/shard_map/ppermute | solution.py:311
  (23 other events, 74.0 us)
